TPU v7x, 32 devices: a whole 2x2x4 slice. The times are simulated.
32 devices in a mesh: rows: 8 (over z, x), heads: 4 (over y, core).
Axes of the slice: x: 2, y: 2, z: 4, core: 2. Of those that a mesh axis runs over, the one named last changes fastest.
Arguments:
- sheet: bfloat16 [128, 256, 768], P('rows'), may hold values from -6 to 6
- w_query: bfloat16 [768, 768], P(None, 'heads'), may hold values from -0.21875 to 0.21875
- w_key: bfloat16 [768, 768], P(None, 'heads'), may hold values from -0.21875 to 0.21875
- w_value: bfloat16 [768, 768], P(None, 'heads'), may hold values from -0.21875 to 0.21875
- cotangent: bfloat16 [128, 256, 768], P('rows', None, 'heads'), may hold values from -6 to 6
- lengths: int32 [128], P('rows'), may hold values from 32 to 256
Outputs:
- input_grad: bfloat16 [128, 256, 768], P('rows', None, 'heads')
- weight_grad: float32 [768, 3, 768], P('rows', None, 'heads')
All inputs are finite; a program needn't handle non-finite values.
Results may differ from a plain program's by a relative error of at most 0.013.
Values may be sent and summed in bfloat16 or wider, within the bound.
No kernel may reach another device: no remote copies, remote signals or barrier semaphores. Data moves between devices by JAX's collectives and lax.ppermute only.
A program may use at most 128 MiB of HBM per device.

v0:
```python
import jax
import jax.numpy as jnp
from jax import lax
from jax.sharding import PartitionSpec as P

HEAD_DIM = 64


def softmax_back(logits, dprob, scale):
    probs = jax.nn.softmax(scale * logits, axis=-1)
    inner = jnp.sum(probs * dprob, axis=-1, keepdims=True)
    dscore = scale * probs * (dprob - inner)
    return (probs.astype(jnp.bfloat16), dscore.astype(jnp.bfloat16))


def body(sheet, w_query, w_key, w_value, cotangent, lengths):
    row_dev, cols, width = sheet.shape
    local = w_query.shape[1]
    heads_here = local // HEAD_DIM
    total_rows = row_dev * lax.axis_size("rows")
    scale = 1.0 / jnp.sqrt(jnp.float32(HEAD_DIM * total_rows))
    valid = (jnp.arange(cols, dtype=jnp.int32)[None, :] < lengths[:, None]).astype(jnp.float32)
    weights = jnp.concatenate([w_query, w_key, w_value], axis=1)
    flat = sheet.reshape(row_dev * cols, width)
    projected = jnp.dot(flat, weights, preferred_element_type=jnp.float32).reshape(
        row_dev, cols, 3 * local
    )
    projected = (projected * valid[..., None]).astype(jnp.bfloat16)
    split = (row_dev, cols, heads_here, HEAD_DIM)
    query = projected[..., :local].reshape(split)
    key = projected[..., local : 2 * local].reshape(split)
    value = projected[..., 2 * local :].reshape(split)
    grad_out = cotangent.reshape(split)
    logit_part = jnp.einsum("rihd,rjhd->hij", query, key, preferred_element_type=jnp.float32)
    dprob_part = jnp.einsum("rihd,rjhd->hij", grad_out, value, preferred_element_type=jnp.float32)
    logits, dprob = lax.psum((logit_part, dprob_part), "rows")
    probs_b, dscore = softmax_back(logits, dprob, scale)
    mask = valid[..., None]
    dquery = jnp.einsum("hij,rjhd->rihd", dscore, key, preferred_element_type=jnp.float32).reshape(
        row_dev, cols, local
    )
    dkey = jnp.einsum("hij,rihd->rjhd", dscore, query, preferred_element_type=jnp.float32).reshape(
        row_dev, cols, local
    )
    dvalue = jnp.einsum(
        "hij,rihd->rjhd", probs_b, grad_out, preferred_element_type=jnp.float32
    ).reshape(row_dev, cols, local)
    grads = (jnp.concatenate([dquery, dkey, dvalue], axis=-1) * mask).astype(jnp.bfloat16)
    flat_grads = grads.reshape(row_dev * cols, 3 * local)
    input_part = lax.dot_general(
        flat_grads, weights, (((1,), (1,)), ((), ())), preferred_element_type=jnp.float32
    )
    input_part = input_part.reshape(row_dev, cols, width).astype(jnp.bfloat16)
    input_grad = (
        lax.psum_scatter(input_part, "heads", scatter_dimension=2, tiled=True)
        .astype(jnp.float32)
        .astype(jnp.bfloat16)
    )
    rows_out = width // lax.axis_size("rows")
    weight_grad = lax.psum_scatter(
        lax.dot_general(
            flat, flat_grads, (((0,), (0,)), ((), ())), preferred_element_type=jnp.float32
        ),
        "rows",
        scatter_dimension=0,
        tiled=True,
    )
    return (input_grad, weight_grad.reshape(rows_out, 3, local))


def solution(mesh):
    in_specs = (
        P("rows", None, None),
        P(None, "heads"),
        P(None, "heads"),
        P(None, "heads"),
        P("rows", None, "heads"),
        P("rows"),
    )
    out_specs = (P("rows", None, "heads"), P("rows", None, "heads"))
    return jax.shard_map(body, mesh=mesh, in_specs=in_specs, out_specs=out_specs, check_vma=False)
```

profile of v0, /device:TPU:0, one launch (start us, length us, event | category | flops | bytes accessed | tf_op | source)
XLA Modules:
  0.0 288.6 jit_solution(2252720750042608672)
XLA Ops:
  7.9 1.0 constant_dynamic-update-slice_fusion.2
  8.9 1.0 constant_dynamic-update-slice_fusion.1
  9.9 1.0 constant_dynamic-update-slice_fusion
  10.9 6.3 %fusion.38 = f32[576,4096]{1,0:T(8,128)S(1)} fusion(bf16[768,576]{0,1:T(8,128)(2,1)S(1)} %constant_dynamic-update-slice_fusion, bf16[4096,768]{1,0:T(8,128)(2,1)} %bitcast.72), kind=kOutput, calls=%fused_computation.43 | convolution fusion | flops 3623878656 | bytes 16613376 | tf_op jit(solution)/shard_map/dot_general | solution.py:25
  17.2 1.1 fusion.2
  18.7 1.1 copy-done.4
  19.8 1.6 convolution_bitcast_fusion.4
  21.4 1.6 convolution_bitcast_fusion.3
  23.3 1.2 copy.32
  24.6 90.6 %all-reduce.3.cloned.1.call-done = (f32[3,256,256]{2,1,0:T(8,128)}, f32[3,256,256]{2,1,0:T(8,128)}) async-done(((f32[3,256,256]{2,1,0:T(8,128)}, f32[3,256,256]{2,1,0:T(8,128)}), (f32[3,256,256]{2,1,0:T(8,128)}, f32[3,256,256]{2,1,0:T(8,128)})) %all-reduce.3.cloned.1.call-update) | async-done | bytes 1572880 | tf_op jit(solution)/shard_map/psum | solution.py:36
  115.2 1.5 fusion.37
  116.7 7.2 %convolution_bitcast_fusion.1 = f32[16,256,3,64]{1,3,0,2:T(8,128)} fusion(bf16[16,256,3,64]{1,3,2,0:T(8,128)(2,1)} %bitcast.69, f32[3,256,256]{2,1,0:T(8,128)} %get-tuple-element.9, f32[3,256,256]{2,1,0:T(8,128)S(1)} %get-tuple-element.14, f32[3,256]{1,0:T(4,128)S(1)} %get-tuple-element.13), kind=kOutput, calls=%fused_computation.8 | convolution fusion | flops 404030464 | bytes 6294528 | tf_op jit(solution)/shard_map/hij,rjhd->rihd/dot_general | solution.py:39
  123.9 6.8 %convolution_bitcast_fusion = f32[16,256,3,64]{1,3,0,2:T(8,128)} fusion(bf16[16,256,3,64]{1,3,2,0:T(8,128)(2,1)S(1)} %bitcast.67, f32[3,256,256]{2,1,0:T(8,128)} %get-tuple-element.9, f32[3,256,256]{2,1,0:T(8,128)S(1)} %get-tuple-element.14, f32[3,256]{1,0:T(4,128)S(1)} %get-tuple-element.13), kind=kOutput, calls=%fused_computation.7 | convolution fusion | flops 404030464 | bytes 6294528 | tf_op jit(solution)/shard_map/hij,rihd->rjhd/dot_general | solution.py:42
  130.7 2.3 copy.29
  133.6 2.1 copy.31
  135.6 5.0 %fusion.19 = f32[3,256,1024]{1,2,0} fusion(bf16[3,256,1024]{1,2,0:T(8,128)(2,1)} %bitcast.70, f32[3,256]{1,0:T(4,128)S(1)} %get-tuple-element.13, f32[3,256,256]{2,1,0:T(8,128)} %get-tuple-element.8), kind=kOutput, calls=%fused_computation.25 | convolution fusion | flops 403440640 | bytes 5508096
  140.6 2.2 copy.33
  142.9 1.6 copy-done.2
  144.5 7.8 %convolution_bitcast_fusion.2 = f32[768,576]{0,1:T(8,128)} fusion(bf16[16,256,768]{2,1,0:T(8,128)(2,1)} %param.6, f32[16,256,192]{1,2,0:T(8,128)S(1)} %bitcast.63, f32[16,256,192]{1,2,0:T(8,128)S(1)} %bitcast.62, f32[16,256,192]{1,2,0:T(8,128)S(1)} %bitcast.59, f32[16,256]{1,0:T(8,128)S(1)} %fusion.24), kind=kOutput, calls=%fused_computation.11 | convolution fusion | flops 3633315840 | bytes 17514496 | tf_op jit(solution)/shard_map/dot_general | solution.py:61
  152.4 2.8 copy.38
  155.3 9.2 %convolution_convert_fusion = bf16[16,256,768]{1,2,0:T(8,128)(2,1)} fusion(bf16[768,576]{0,1:T(8,128)(2,1)} %copy-done.5, f32[16,256,192]{1,2,0:T(8,128)} %bitcast.64, f32[16,256,192]{1,2,0:T(8,128)} %bitcast.61, f32[16,256,192]{1,2,0:T(8,128)S(1)} %bitcast.60, f32[16,256]{1,0:T(8,128)S(1)} %fusion.24), kind=kOutput, calls=%fused_computation.6 | convolution fusion | flops 3636461568 | bytes 16629760 | tf_op jit(solution)/shard_map/dot_general | solution.py:50
  164.5 57.0 %reduce-scatter.7.cloned.1.call-done = f32[96,576]{1,0:T(8,128)} async-done(((f32[768,576]{1,0:T(8,128)}), f32[96,576]{1,0:T(8,128)}) %reduce-scatter.7.cloned.1.call-update) | async-done | bytes 221200
  221.5 1.1 copy.39
  223.5 58.6 %reduce-scatter.5.cloned.1.call-done = bf16[16,256,192]{1,2,0:T(8,128)(2,1)} async-done(((bf16[16,256,768]{1,2,0:T(8,128)(2,1)}), bf16[16,256,192]{1,2,0:T(8,128)(2,1)}) %reduce-scatter.5.cloned.1.call-update) | async-done | bytes 1572880 | tf_op jit(solution)/shard_map/reduce_scatter | solution.py:55
  (19 shorter events, 2.9 us)
Async XLA Ops:
  7.2 108.0 %all-reduce.3.cloned.1.call-start = ((), (), s32[]{:S(2)}) async-start(), calls=%async_computation.4 | async-start | bytes 3145728 | tf_op jit(solution)/shard_map/psum | solution.py:36
  10.9 6.3 %copy-start.5 = (bf16[768,576]{0,1:T(8,128)(2,1)}, bf16[768,576]{0,1:T(8,128)(2,1)S(1)}, u32[]{:S(2)}) copy-start(bf16[768,576]{0,1:T(8,128)(2,1)S(1)} %constant_dynamic-update-slice_fusion) | copy-start | bytes 2654212
  18.7 1.1 copy-start.4
  18.7 2.7 copy-start
  23.1 198.4 %reduce-scatter.7.cloned.1.call-start = ((), (), s32[]{:S(2)}) async-start(), calls=%async_computation.3 | async-start | bytes 2211840
  130.7 2.8 copy-start.3
  140.6 3.9 %copy-start.1 = (f32[16,256,3,64]{1,3,2,0:T(8,128)S(1)}, f32[16,256,3,64]{1,3,2,0:T(8,128)}, u32[]{:S(2)}) copy-start(f32[16,256,3,64]{1,3,2,0:T(8,128)} %copy.31) | copy-start | bytes 9437188
  142.9 1.6 copy-start.2
  155.2 126.9 %reduce-scatter.5.cloned.1.call-start = ((), (), s32[]{:S(2)}) async-start(), calls=%async_computation.2 | async-start | bytes 7864320 | tf_op jit(solution)/shard_map/reduce_scatter | solution.py:55
Sparse Core Ops, SparseCore 0:
  23.2 91.9 all-reduce.2
  155.3 66.1 reduce-scatter.6
  224.8 57.2 reduce-scatter.4
where the time goes:
time: 289 us
  waiting for transfers between devices  206 us (71%)
  matrix products  45.6 us (16%)
  local copies, waits for them, and re-layouts  19.2 us (7%)
  between operations  13.8 us (5%)
  other arithmetic  3.3 us (1%)
    psum x1, waiting for transfers between devices, body(): logits, dprob = lax.psum((logit_part, dprob_part), 'rows')  90.6 us
    reduce_scatter x1, waiting for transfers between devices, body(): lax.psum_scatter(input_part, 'heads', scatter_dimension=2, tiled=True)  58.6 us
    unnamed x4, waiting for transfers between devices  57 us
    unnamed x17, local copies, waits for them, and re-layouts  10.1 us
    dot_general x1, matrix products, body(): lax.dot_general(flat_grads, weights, (((1,), (1,)), ((), ())), preferred_...  9.24 us
    dot_general x1, matrix products, body(): lax.dot_general(flat, flat_grads, (((0,), (0,)), ((), ())), preferred_ele...  7.84 us
    dot_general x1, matrix products, body(): jnp.einsum('hij,rjhd->rihd', dscore, key, preferred_element_type=jnp.floa...  7.25 us
    dot_general x1, matrix products, body(): jnp.einsum('hij,rihd->rjhd', dscore, query, preferred_element_type=jnp.fl...  6.79 us
  transfers between devices with their start and end apart: 3, of which 3 were waited for; matrix products, arithmetic and copies ran while one was open for 4% of the time, Pallas kernels for 0%

commit v1 on v0

v1 whole, which is shorter than its diff:
```python
import jax
import jax.numpy as jnp
from jax import lax
from jax.sharding import PartitionSpec as P

HEAD_DIM = 64
F32 = jnp.float32
BF16 = jnp.bfloat16


def shift(values, axis, step):
    n = lax.axis_size(axis)
    return lax.ppermute(values, axis, [(s, (s + step) % n) for s in range(n)])


def flip(values, axis, bit):
    n = lax.axis_size(axis)
    return lax.ppermute(values, axis, [(s, s ^ bit) for s in range(n)])


def block(values, index):
    return lax.dynamic_index_in_dim(values, index, 0, keepdims=False)


def scatter_sum(parts, axis):
    n = lax.axis_size(axis)
    if n > 8:
        return lax.psum_scatter(parts, axis, scatter_dimension=0, tiled=False)
    me = lax.axis_index(axis)
    narrow = parts.astype(BF16)
    got = [shift(block(narrow, (me + k) % n), axis, k) for k in range(1, n)]
    total = block(parts, me)
    for piece in got:
        total = total + piece.astype(F32)
    return total


def gather(values, axis):
    n = lax.axis_size(axis)
    if n > 8:
        return lax.all_gather(values, axis)
    me = lax.axis_index(axis)
    out = jnp.zeros((n,) + values.shape, values.dtype)
    out = lax.dynamic_update_index_in_dim(out, values, me, 0)
    for k in range(1, n):
        out = lax.dynamic_update_index_in_dim(out, shift(values, axis, k), (me + n - k) % n, 0)
    return out


def softmax_back(logits, dprob, scale):
    probs = jax.nn.softmax(scale * logits, axis=-1)
    inner = jnp.sum(probs * dprob, axis=-1, keepdims=True)
    dscore = scale * probs * (dprob - inner)
    return (probs.astype(BF16), dscore.astype(BF16))


def body(sheet, w_query, w_key, w_value, cotangent, lengths):
    row_dev, cols, width = sheet.shape
    local = w_query.shape[1]
    heads_here = local // HEAD_DIM
    n_rows = lax.axis_size("rows")
    n_heads = lax.axis_size("heads")
    total_rows = row_dev * n_rows
    scale = 1.0 / jnp.sqrt(jnp.float32(HEAD_DIM * total_rows))
    valid = (jnp.arange(cols, dtype=jnp.int32)[None, :] < lengths[:, None]).astype(F32)
    weights = jnp.concatenate([w_query, w_key, w_value], axis=1)
    flat = sheet.reshape(row_dev * cols, width)
    projected = jnp.dot(flat, weights, preferred_element_type=F32).reshape(row_dev, cols, 3 * local)
    projected = (projected * valid[..., None]).astype(BF16)
    split = (row_dev, cols, heads_here, HEAD_DIM)
    query = projected[..., :local].reshape(split)
    key = projected[..., local : 2 * local].reshape(split)
    value = projected[..., 2 * local :].reshape(split)
    grad_out = cotangent.reshape(split)
    logit_part = jnp.einsum("rihd,rjhd->hij", query, key, preferred_element_type=F32)
    dprob_part = jnp.einsum("rihd,rjhd->hij", grad_out, value, preferred_element_type=F32)
    own = cols // n_rows

    def by_shard(part):
        return part.reshape(heads_here, n_rows, own, cols).transpose(1, 0, 2, 3)

    logits = scatter_sum(by_shard(logit_part), "rows")
    dprob = scatter_sum(by_shard(dprob_part), "rows")
    probs_own, dscore_own = softmax_back(logits, dprob, scale)

    def whole(part):
        return gather(part, "rows").transpose(1, 0, 2, 3).reshape(heads_here, cols, cols)

    probs_b = whole(probs_own)
    dscore = whole(dscore_own)
    mask = valid[..., None]
    dquery = jnp.einsum("hij,rjhd->rihd", dscore, key, preferred_element_type=F32).reshape(
        row_dev, cols, local
    )
    dkey = jnp.einsum("hij,rihd->rjhd", dscore, query, preferred_element_type=F32).reshape(
        row_dev, cols, local
    )
    dvalue = jnp.einsum("hij,rihd->rjhd", probs_b, grad_out, preferred_element_type=F32).reshape(
        row_dev, cols, local
    )
    grads = (jnp.concatenate([dquery, dkey, dvalue], axis=-1) * mask).astype(BF16)
    flat_grads = grads.reshape(row_dev * cols, 3 * local)

    me = lax.axis_index("heads")
    chunks = 4
    step = row_dev // chunks
    pieces = []
    for c in range(chunks):
        rows = grads[c * step : (c + 1) * step].reshape(step * cols, 3 * local)
        part = lax.dot_general(
            weights.reshape(n_heads, width // n_heads, 3 * local),
            rows,
            (((2,), (1,)), ((), ())),
            preferred_element_type=F32,
        ).astype(BF16)
        part = part.reshape((n_heads, width // n_heads, step, cols))
        bit = 1
        live = part
        while bit < n_heads:
            half = live.reshape((live.shape[0] // 2, 2) + live.shape[1:])
            mine = (me // bit) % 2
            keep = lax.dynamic_index_in_dim(half, mine, 1, keepdims=False)
            give = lax.dynamic_index_in_dim(half, 1 - mine, 1, keepdims=False)
            live = (keep.astype(F32) + flip(give, "heads", bit).astype(F32)).astype(BF16)
            bit *= 2
        pieces.append(live[0].transpose(1, 2, 0))
    input_grad = jnp.concatenate(pieces, axis=0)

    weight_part = lax.dot_general(flat, flat_grads, (((0,), (0,)), ((), ())), preferred_element_type=F32)
    rows_out = width // n_rows
    weight_grad = scatter_sum(weight_part.reshape(n_rows, rows_out, 3 * local), "rows")
    return (input_grad, weight_grad.reshape(rows_out, 3, local))


def solution(mesh):
    in_specs = (
        P("rows", None, None),
        P(None, "heads"),
        P(None, "heads"),
        P(None, "heads"),
        P("rows", None, "heads"),
        P("rows"),
    )
    out_specs = (P("rows", None, "heads"), P("rows", None, "heads"))
    return jax.shard_map(body, mesh=mesh, in_specs=in_specs, out_specs=out_specs, check_vma=False)
```

time: 289 us -> 209 us (0.72)
  waiting for transfers between devices: 206 us -> 34.4 us
  starting transfers between devices: 0.3 us -> 61.2 us
  local copies, waits for them, and re-layouts: 19.2 us -> 63 us
  matrix products: 45.6 us -> 32.5 us
  between operations: 13.8 us -> 1.3 us
  other arithmetic: 3.3 us -> 15.4 us
    psum x1 -> x0, waiting for transfers between devices: 90.6 us -> none  [body(): logits, dprob = lax.psum((logit_part, dprob_part), 'rows')]
    ppermute x0 -> x43, starting transfers between devices: none -> 61.2 us  [the longest x35 56.4 us: shift(): return lax.ppermute(values, axis, [(s, (s + step) % n) for s in range(n)])]
    reduce_scatter x1 -> x0, waiting for transfers between devices: 58.6 us -> none  [body(): lax.psum_scatter(input_part, 'heads', scatter_dimension=2, tiled=True)]
    unnamed x4 -> x0, waiting for transfers between devices: 57 us -> none
    ppermute x0 -> x43, waiting for transfers between devices: none -> 34.4 us  [the longest x8 28.1 us: flip(): return lax.ppermute(values, axis, [(s, s ^ bit) for s in range(n)])]
    another operation x0 -> x6, local copies, waits for them, and re-layouts: none -> 13.6 us  [the longest x4 13.5 us: body(): half = live.reshape((live.shape[0] // 2, 2) + live.shape[1:])]
    dynamic_slice x0 -> x6, local copies, waits for them, and re-layouts: none -> 11.2 us  [the longest x2 7.23 us: body(): keep = lax.dynamic_index_in_dim(half, mine, 1, keepdims=False)]
    reshape x0 -> x4, local copies, waits for them, and re-layouts: none -> 9.32 us  [body(): rows = grads[c * step:(c + 1) * step].reshape(step * cols, 3 * local)]
  transfers between devices with their start and end apart: 3 -> 43, of which waited for: 3 -> 10; matrix products, arithmetic and copies ran while one was open for 4% -> 38% of each run, Pallas kernels for 0% -> 0%
where the time goes in v1:
time: 209 us; the launch traced here: 208 us
  local copies, waits for them, and re-layouts  63 us (30%)
  starting transfers between devices  61.2 us (29%)
  waiting for transfers between devices  34.4 us (16%)
  matrix products  32.5 us (16%)
  other arithmetic  15.4 us (7%)
    ppermute x35, starting transfers between devices, shift(): return lax.ppermute(values, axis, [(s, (s + step) % n) for s in range(n)])  56.4 us
    ppermute x8, waiting for transfers between devices, flip(): return lax.ppermute(values, axis, [(s, s ^ bit) for s in range(n)])  28.1 us
    dot_general x4, matrix products, body(): lax.dot_general(weights.reshape(n_heads, width // n_heads, 3 * local), ro...  16.2 us
    another operation x4, local copies, waits for them, and re-layouts, body(): half = live.reshape((live.shape[0] // 2, 2) + live.shape[1:])  13.5 us
    reshape x4, local copies, waits for them, and re-layouts, body(): rows = grads[c * step:(c + 1) * step].reshape(step * cols, 3 * local)  9.32 us
    slice x5, local copies, waits for them, and re-layouts, body(): rows = grads[c * step:(c + 1) * step].reshape(step * cols, 3 * local)  8.81 us
    unnamed x53, local copies, waits for them, and re-layouts  7.65 us
    dynamic_slice x2, local copies, waits for them, and re-layouts, body(): keep = lax.dynamic_index_in_dim(half, mine, 1, keepdims=False)  7.23 us
  transfers between devices with their start and end apart: 43, of which 10 were waited for; matrix products, arithmetic and copies ran while one was open for 38% of the time, Pallas kernels for 0%

profile of v1, /device:TPU:0, one launch (start us, length us, event | category | flops | bytes accessed | tf_op | source)
XLA Modules:
  0.0 207.8 jit_solution(11402893744524879471)
XLA Ops:
  3.5 6.3 %fusion.48 = f32[576,4096]{1,0:T(8,128)S(1)} fusion(bf16[768,576]{0,1:T(8,128)(2,1)S(1)} %constant_dynamic-update-slice_fusion, bf16[4096,768]{1,0:T(8,128)(2,1)} %bitcast.309), kind=kOutput, calls=%fused_computation.128 | convolution fusion | flops 3623878656 | bytes 16613376 | tf_op jit(solution)/shard_map/dot_general | solution.py:68
  14.7 2.9 %collective-permute-start = (bf16[3,32,256]{2,1,0:T(8,128)(2,1)S(1)}, bf16[3,32,256]{2,1,0:T(8,128)(2,1)S(1)}, u32[]{:S(2)}, u32[]{:S(2)}) collective-permute-start(bf16[3,32,256]{2,1,0:T(8,128)(2,1)S(1)} %get-tuple-element.35), channel_id=1, source_target_pairs={{0,4},{4,8},{8,12},{12,16},{16,20},{20,24},{24,28},{28,0},{1,5},{5... | collective-permute-start | bytes 147464 | tf_op jit(solution)/shard_map/ppermute | solution.py:13
  32.9 2.9 %collective-permute-start.11 = (bf16[3,32,256]{2,1,0:T(8,128)(2,1)S(1)}, bf16[3,32,256]{2,1,0:T(8,128)(2,1)S(1)}, u32[]{:S(2)}, u32[]{:S(2)}) collective-permute-start(bf16[3,32,256]{2,1,0:T(8,128)(2,1)S(1)} %get-tuple-element.31), channel_id=1, source_target_pairs={{0,20},{4,24},{8,28},{12,0},{16,4},{20,8},{24,12},{28,16},{1,21},{... | collective-permute-start | bytes 147464 | tf_op jit(solution)/shard_map/ppermute | solution.py:13
  52.1 2.7 %copy.64 = bf16[16,256,3,64]{1,3,0,2:T(8,128)(2,1)} copy(bf16[16,256,3,64]{1,3,2,0:T(8,128)(2,1)} %bitcast.294) | data formatting | bytes 3145728 | tf_op jit(solution)/shard_map/reshape | solution.py:74
  70.2 3.3 %collective-permute-start.24 = (bf16[3,32,256]{2,1,0:T(8,128)(2,1)}, bf16[3,32,256]{2,1,0:T(8,128)(2,1)S(1)}, u32[]{:S(2)}, u32[]{:S(2)}) collective-permute-start(bf16[3,32,256]{2,1,0:T(8,128)(2,1)} %get-tuple-element.5), channel_id=1, source_target_pairs={{0,16},{4,20},{8,24},{12,28},{16,0},{20,4},{24,8},{28,12},{1,17},{... | collective-permute-start | bytes 147464 | tf_op jit(solution)/shard_map/ppermute | solution.py:13
  75.2 2.9 %collective-permute-start.26 = (bf16[3,32,256]{2,1,0:T(8,128)(2,1)S(1)}, bf16[3,32,256]{2,1,0:T(8,128)(2,1)S(1)}, u32[]{:S(2)}, u32[]{:S(2)}) collective-permute-start(bf16[3,32,256]{2,1,0:T(8,128)(2,1)S(1)} %copy-done.16), channel_id=1, source_target_pairs={{0,24},{4,28},{8,0},{12,4},{16,8},{20,12},{24,16},{28,20},{1,25},{... | collective-permute-start | bytes 147464 | tf_op jit(solution)/shard_map/ppermute | solution.py:13
  85.9 5.1 %convolution_bitcast_fusion.2 = f32[768,576]{0,1:T(8,128)} fusion(bf16[16,256,576]{1,2,0:T(8,128)(2,1)S(1)} %fusion.4, bf16[16,256,768]{2,1,0:T(8,128)(2,1)S(1)} %bitcast.311), kind=kOutput, calls=%fused_computation.24 | convolution fusion | flops 3623878656 | bytes 12779520 | tf_op jit(solution)/shard_map/dot_general | solution.py:129
  106.4 3.7 %convolution_convert_fusion.3 = bf16[4,192,1024]{2,1,0:T(8,128)(2,1)} fusion(bf16[4,192,576]{2,1,0:T(8,128)(2,1)} %bitcast.302, bf16[1024,576,1]{0,1,2:T(8,128)(2,1)S(1)} %reshape.190), kind=kOutput, calls=%fused_computation.12 | convolution fusion | flops 906756096 | bytes 3637248 | tf_op jit(solution)/shard_map/dot_general | solution.py:110
  110.1 2.9 %reshape_reshape.12 = bf16[2,2,192,4,256]{4,3,2,1,0:T(4,128)(2,1)S(1)} reshape(bf16[4,192,1024]{2,1,0:T(8,128)(2,1)} %convolution_convert_fusion.3) | data formatting | bytes 3145728 | tf_op jit(solution)/shard_map/reshape;reshape | solution.py:120
  113.0 3.2 %copy.69 = bf16[4,256,576]{1,0,2:T(4,128)(2,1)} copy(bf16[4,256,576]{1,2,0:T(8,128)(2,1)} %get-tuple-element.9) | data formatting | bytes 2359296 | tf_op jit(solution)/shard_map/slice | solution.py:109
  116.2 3.4 %reshape.191 = bf16[1024,576,1]{0,1,2:T(8,128)(2,1)} reshape(bf16[4,256,576]{1,0,2:T(4,128)(2,1)} %copy.69) | data formatting | bytes 2359296 | tf_op jit(solution)/shard_map/reshape | solution.py:109
  119.6 4.1 %convolution_convert_fusion.2 = bf16[4,192,1024]{2,1,0:T(8,128)(2,1)} fusion(bf16[4,192,576]{2,1,0:T(8,128)(2,1)} %bitcast.303, bf16[1024,576,1]{0,1,2:T(8,128)(2,1)} %reshape.191), kind=kOutput, calls=%fused_computation.11 | convolution fusion | flops 906756096 | bytes 3637248 | tf_op jit(solution)/shard_map/dot_general | solution.py:110
  123.7 3.9 %reshape_reshape.13 = bf16[2,2,192,4,256]{4,3,2,1,0:T(4,128)(2,1)} reshape(bf16[4,192,1024]{2,1,0:T(8,128)(2,1)} %convolution_convert_fusion.2) | data formatting | bytes 3145728 | tf_op jit(solution)/shard_map/reshape;reshape | solution.py:120
  127.6 3.6 %constant_dynamic-slice_fusion.8 = (bf16[2,1,192,4,256]{4,3,2,1,0:T(4,128)(2,1)}, bf16[2,1,192,4,256]{4,3,2,1,0:T(4,128)(2,1)}, bf16[2,1,192,4,256]{4,3,2,1,0:T(4,128)(2,1)S(1)}, bf16[2,1,192,4,256]{4,3,2,1,0:T(4,128)(2,1)}) fusion(bf16[2,2,192,4,256]{4,3,2,1,0:T(4,128)(2,1)} %reshape_reshape.13, s32[]{:T(128)S(6)} %select_n.221, s32[]{:T(128)S(6)} %select_n.222, ...), kind=kLoop, calls=%fused_computation.118 | loop fusion | bytes 6291464 | tf_op jit(solution)/shard_map/jit(dynamic_index_in_dim)/dynamic_slice | solution.py:122
  135.3 4.2 %convolution_convert_fusion.1 = bf16[4,192,1024]{2,1,0:T(8,128)(2,1)} fusion(bf16[4,192,576]{2,1,0:T(8,128)(2,1)} %bitcast.304, bf16[1024,576,1]{0,1,2:T(8,128)(2,1)} %reshape.192), kind=kOutput, calls=%fused_computation.10 | convolution fusion | flops 906756096 | bytes 3637248 | tf_op jit(solution)/shard_map/dot_general | solution.py:110
  142.1 4.2 %convolution_convert_fusion = bf16[4,192,1024]{2,1,0:T(8,128)(2,1)} fusion(bf16[4,192,576]{2,1,0:T(8,128)(2,1)} %bitcast.305, bf16[1024,576,1]{0,1,2:T(8,128)(2,1)} %reshape.193), kind=kOutput, calls=%fused_computation.9 | convolution fusion | flops 906756096 | bytes 3637248 | tf_op jit(solution)/shard_map/dot_general | solution.py:110
  147.3 2.9 %reshape_reshape.14 = bf16[2,2,192,4,256]{4,3,2,1,0:T(4,128)(2,1)S(1)} reshape(bf16[4,192,1024]{2,1,0:T(8,128)(2,1)} %convolution_convert_fusion.1) | data formatting | bytes 3145728 | tf_op jit(solution)/shard_map/reshape;reshape | solution.py:120
  150.2 3.9 %reshape_reshape.15 = bf16[2,2,192,4,256]{4,3,2,1,0:T(4,128)(2,1)} reshape(bf16[4,192,1024]{2,1,0:T(8,128)(2,1)} %convolution_convert_fusion) | data formatting | bytes 3145728 | tf_op jit(solution)/shard_map/reshape;reshape | solution.py:120
  154.0 3.5 %collective-permute-start.40 = (bf16[96,576]{1,0:T(8,128)(2,1)}, bf16[96,576]{1,0:T(8,128)(2,1)S(1)}, u32[]{:S(2)}, u32[]{:S(2)}) collective-permute-start(bf16[96,576]{1,0:T(8,128)(2,1)} %get-tuple-element.24), channel_id=1, source_target_pairs={{0,20},{4,24},{8,28},{12,0},{16,4},{20,8},{24,12},{28,16},{1,21},{... | collective-permute-start | bytes 331784 | tf_op jit(solution)/shard_map/ppermute | solution.py:13
  159.3 3.6 %constant_dynamic-slice_fusion.2 = (bf16[2,1,192,4,256]{4,3,2,1,0:T(4,128)(2,1)}, bf16[2,1,192,4,256]{4,3,2,1,0:T(4,128)(2,1)S(1)}, bf16[2,1,192,4,256]{4,3,2,1,0:T(4,128)(2,1)S(1)}, bf16[2,1,192,4,256]{4,3,2,1,0:T(4,128)(2,1)}) fusion(bf16[2,2,192,4,256]{4,3,2,1,0:T(4,128)(2,1)} %reshape_reshape.15, s32[]{:T(128)S(6)} %select_n.221, s32[]{:T(128)S(6)} %select_n.222, ...), kind=kLoop, calls=%fused_computation.112 | loop fusion | bytes 6291464 | tf_op jit(solution)/shard_map/jit(dynamic_index_in_dim)/dynamic_slice | solution.py:122
  178.0 3.5 %collective-permute-done.29 = bf16[1,192,4,256]{3,1,2,0:T(8,128)(2,1)S(1)} collective-permute-done((bf16[1,192,4,256]{3,1,2,0:T(8,128)(2,1)S(1)}, bf16[1,192,4,256]{3,1,2,0:T(8,128)(2,1)S(1)}, u32[]{:S(2)}, u32[]{:S(2)}) %collective-permute-start.29) | collective-permute-done | bytes 393248 | tf_op jit(solution)/shard_map/ppermute | solution.py:18
  181.6 8.3 %collective-permute-done.31 = bf16[1,192,4,256]{3,1,2,0:T(8,128)(2,1)S(1)} collective-permute-done((bf16[1,192,4,256]{3,1,2,0:T(8,128)(2,1)S(1)}, bf16[1,192,4,256]{3,1,2,0:T(8,128)(2,1)S(1)}, u32[]{:S(2)}, u32[]{:S(2)}) %collective-permute-start.31) | collective-permute-done | bytes 393248 | tf_op jit(solution)/shard_map/ppermute | solution.py:18
  190.0 8.3 %collective-permute-done.33 = bf16[1,192,4,256]{3,1,2,0:T(8,128)(2,1)S(1)} collective-permute-done((bf16[1,192,4,256]{3,1,2,0:T(8,128)(2,1)S(1)}, bf16[1,192,4,256]{3,1,2,0:T(8,128)(2,1)S(1)}, u32[]{:S(2)}, u32[]{:S(2)}) %collective-permute-start.33) | collective-permute-done | bytes 393248 | tf_op jit(solution)/shard_map/ppermute | solution.py:18
  198.5 7.9 %collective-permute-done.35 = bf16[1,192,4,256]{3,1,2,0:T(8,128)(2,1)S(1)} collective-permute-done((bf16[1,192,4,256]{3,1,2,0:T(8,128)(2,1)S(1)}, bf16[1,192,4,256]{3,1,2,0:T(8,128)(2,1)S(1)}, u32[]{:S(2)}, u32[]{:S(2)}) %collective-permute-start.35) | collective-permute-done | bytes 393248 | tf_op jit(solution)/shard_map/ppermute | solution.py:18
  (196 shorter events, 105.4 us)
Async XLA Ops:
  14.7 15.2 %collective-permute-start = (bf16[3,32,256]{2,1,0:T(8,128)(2,1)S(1)}, bf16[3,32,256]{2,1,0:T(8,128)(2,1)S(1)}, u32[]{:S(2)}, u32[]{:S(2)}) collective-permute-start(bf16[3,32,256]{2,1,0:T(8,128)(2,1)S(1)} %get-tuple-element.35), channel_id=1, source_target_pairs={{0,4},{4,8},{8,12},{12,16},{16,20},{20,24},{24,28},{28,0},{1,5},{5... | collective-permute-start | bytes 147464 | tf_op jit(solution)/shard_map/ppermute | solution.py:13
  17.6 13.6 %collective-permute-start.1 = (bf16[3,32,256]{2,1,0:T(8,128)(2,1)S(1)}, bf16[3,32,256]{2,1,0:T(8,128)(2,1)S(1)}, u32[]{:S(2)}, u32[]{:S(2)}) collective-permute-start(bf16[3,32,256]{2,1,0:T(8,128)(2,1)S(1)} %get-tuple-element.41), channel_id=1, source_target_pairs={{0,8},{4,12},{8,16},{12,20},{16,24},{20,28},{24,0},{28,4},{1,9},{5... | collective-permute-start | bytes 147464 | tf_op jit(solution)/shard_map/ppermute | solution.py:13
  19.2 13.5 %collective-permute-start.2 = (bf16[3,32,256]{2,1,0:T(8,128)(2,1)S(1)}, bf16[3,32,256]{2,1,0:T(8,128)(2,1)S(1)}, u32[]{:S(2)}, u32[]{:S(2)}) collective-permute-start(bf16[3,32,256]{2,1,0:T(8,128)(2,1)S(1)} %get-tuple-element.40), channel_id=1, source_target_pairs={{0,12},{4,16},{8,20},{12,24},{16,28},{20,0},{24,4},{28,8},{1,13},{... | collective-permute-start | bytes 147464 | tf_op jit(solution)/shard_map/ppermute | solution.py:13
  21.7 11.1 %collective-permute-start.3 = (bf16[3,32,256]{2,1,0:T(8,128)(2,1)S(1)}, bf16[3,32,256]{2,1,0:T(8,128)(2,1)S(1)}, u32[]{:S(2)}, u32[]{:S(2)}) collective-permute-start(bf16[3,32,256]{2,1,0:T(8,128)(2,1)S(1)} %get-tuple-element.39), channel_id=1, source_target_pairs={{0,16},{4,20},{8,24},{12,28},{16,0},{20,4},{24,8},{28,12},{1,17},{... | collective-permute-start | bytes 147464 | tf_op jit(solution)/shard_map/ppermute | solution.py:13
  23.0 12.8 %collective-permute-start.4 = (bf16[3,32,256]{2,1,0:T(8,128)(2,1)}, bf16[3,32,256]{2,1,0:T(8,128)(2,1)S(1)}, u32[]{:S(2)}, u32[]{:S(2)}) collective-permute-start(bf16[3,32,256]{2,1,0:T(8,128)(2,1)} %get-tuple-element.38), channel_id=1, source_target_pairs={{0,20},{4,24},{8,28},{12,0},{16,4},{20,8},{24,12},{28,16},{1,21},{... | collective-permute-start | bytes 147464 | tf_op jit(solution)/shard_map/ppermute | solution.py:13
  35.7 8.6 %collective-permute-start.12 = (bf16[3,32,256]{2,1,0:T(8,128)(2,1)}, bf16[3,32,256]{2,1,0:T(8,128)(2,1)}, u32[]{:S(2)}, u32[]{:S(2)}) collective-permute-start(bf16[3,32,256]{2,1,0:T(8,128)(2,1)} %get-tuple-element.30), channel_id=1, source_target_pairs={{0,24},{4,28},{8,0},{12,4},{16,8},{20,12},{24,16},{28,20},{1,25},{... | collective-permute-start | bytes 147464 | tf_op jit(solution)/shard_map/ppermute | solution.py:13
  50.2 12.6 %collective-permute-start.14 = (bf16[3,32,256]{2,1,0:T(8,128)(2,1)}, bf16[3,32,256]{2,1,0:T(8,128)(2,1)}, u32[]{:S(2)}, u32[]{:S(2)}) collective-permute-start(bf16[3,32,256]{2,1,0:T(8,128)(2,1)} %get-tuple-element.44), channel_id=1, source_target_pairs={{0,4},{4,8},{8,12},{12,16},{16,20},{20,24},{24,28},{28,0},{1,5},{5... | collective-permute-start | bytes 147464 | tf_op jit(solution)/shard_map/ppermute | solution.py:13
  57.0 8.5 %collective-permute-start.15 = (bf16[3,32,256]{2,1,0:T(8,128)(2,1)}, bf16[3,32,256]{2,1,0:T(8,128)(2,1)S(1)}, u32[]{:S(2)}, u32[]{:S(2)}) collective-permute-start(bf16[3,32,256]{2,1,0:T(8,128)(2,1)} %get-tuple-element.44), channel_id=1, source_target_pairs={{0,8},{4,12},{8,16},{12,20},{16,24},{20,28},{24,0},{28,4},{1,9},{5... | collective-permute-start | bytes 147464 | tf_op jit(solution)/shard_map/ppermute | solution.py:13
  57.0 9.8 %collective-permute-start.16 = (bf16[3,32,256]{2,1,0:T(8,128)(2,1)}, bf16[3,32,256]{2,1,0:T(8,128)(2,1)S(1)}, u32[]{:S(2)}, u32[]{:S(2)}) collective-permute-start(bf16[3,32,256]{2,1,0:T(8,128)(2,1)} %get-tuple-element.44), channel_id=1, source_target_pairs={{0,12},{4,16},{8,20},{12,24},{16,28},{20,0},{24,4},{28,8},{1,13},{... | collective-permute-start | bytes 147464 | tf_op jit(solution)/shard_map/ppermute | solution.py:13
  67.6 10.5 %collective-permute-start.22 = (bf16[3,32,256]{2,1,0:T(8,128)(2,1)}, bf16[3,32,256]{2,1,0:T(8,128)(2,1)S(1)}, u32[]{:S(2)}, u32[]{:S(2)}) collective-permute-start(bf16[3,32,256]{2,1,0:T(8,128)(2,1)} %get-tuple-element.5), channel_id=1, source_target_pairs={{0,8},{4,12},{8,16},{12,20},{16,24},{20,28},{24,0},{28,4},{1,9},{5... | collective-permute-start | bytes 147464 | tf_op jit(solution)/shard_map/ppermute | solution.py:13
  68.2 12.0 %collective-permute-start.23 = (bf16[3,32,256]{2,1,0:T(8,128)(2,1)}, bf16[3,32,256]{2,1,0:T(8,128)(2,1)S(1)}, u32[]{:S(2)}, u32[]{:S(2)}) collective-permute-start(bf16[3,32,256]{2,1,0:T(8,128)(2,1)} %get-tuple-element.5), channel_id=1, source_target_pairs={{0,12},{4,16},{8,20},{12,24},{16,28},{20,0},{24,4},{28,8},{1,13},{... | collective-permute-start | bytes 147464 | tf_op jit(solution)/shard_map/ppermute | solution.py:13
  70.2 10.0 %collective-permute-start.24 = (bf16[3,32,256]{2,1,0:T(8,128)(2,1)}, bf16[3,32,256]{2,1,0:T(8,128)(2,1)S(1)}, u32[]{:S(2)}, u32[]{:S(2)}) collective-permute-start(bf16[3,32,256]{2,1,0:T(8,128)(2,1)} %get-tuple-element.5), channel_id=1, source_target_pairs={{0,16},{4,20},{8,24},{12,28},{16,0},{20,4},{24,8},{28,12},{1,17},{... | collective-permute-start | bytes 147464 | tf_op jit(solution)/shard_map/ppermute | solution.py:13
  95.8 58.3 %collective-permute-start.36 = (bf16[96,576]{1,0:T(8,128)(2,1)}, bf16[96,576]{1,0:T(8,128)(2,1)}, u32[]{:S(2)}, u32[]{:S(2)}) collective-permute-start(bf16[96,576]{1,0:T(8,128)(2,1)} %get-tuple-element.21), channel_id=1, source_target_pairs={{0,4},{4,8},{8,12},{12,16},{16,20},{20,24},{24,28},{28,0},{1,5},{5... | collective-permute-start | bytes 331784 | tf_op jit(solution)/shard_map/ppermute | solution.py:13
  97.3 60.2 %collective-permute-start.37 = (bf16[96,576]{1,0:T(8,128)(2,1)}, bf16[96,576]{1,0:T(8,128)(2,1)}, u32[]{:S(2)}, u32[]{:S(2)}) collective-permute-start(bf16[96,576]{1,0:T(8,128)(2,1)} %get-tuple-element.27), channel_id=1, source_target_pairs={{0,8},{4,12},{8,16},{12,20},{16,24},{20,28},{24,0},{28,4},{1,9},{5... | collective-permute-start | bytes 331784 | tf_op jit(solution)/shard_map/ppermute | solution.py:13
  98.9 58.6 %collective-permute-start.38 = (bf16[96,576]{1,0:T(8,128)(2,1)}, bf16[96,576]{1,0:T(8,128)(2,1)}, u32[]{:S(2)}, u32[]{:S(2)}) collective-permute-start(bf16[96,576]{1,0:T(8,128)(2,1)} %get-tuple-element.26), channel_id=1, source_target_pairs={{0,12},{4,16},{8,20},{12,24},{16,28},{20,0},{24,4},{28,8},{1,13},{... | collective-permute-start | bytes 331784 | tf_op jit(solution)/shard_map/ppermute | solution.py:13
  100.9 58.3 %collective-permute-start.39 = (bf16[96,576]{1,0:T(8,128)(2,1)}, bf16[96,576]{1,0:T(8,128)(2,1)}, u32[]{:S(2)}, u32[]{:S(2)}) collective-permute-start(bf16[96,576]{1,0:T(8,128)(2,1)} %get-tuple-element.25), channel_id=1, source_target_pairs={{0,16},{4,20},{8,24},{12,28},{16,0},{20,4},{24,8},{28,12},{1,17},{... | collective-permute-start | bytes 331784 | tf_op jit(solution)/shard_map/ppermute | solution.py:13
  132.2 35.9 %collective-permute-start.28 = (bf16[2,192,4,256]{3,1,2,0:T(8,128)(2,1)}, bf16[2,192,4,256]{3,1,2,0:T(8,128)(2,1)}, u32[]{:S(2)}, u32[]{:S(2)}) collective-permute-start(bf16[2,192,4,256]{3,1,2,0:T(8,128)(2,1)} %bitcast.280), channel_id=1, source_target_pairs={{0,1},{1,0},{2,3},{3,2},{4,5},{5,4},{6,7},{7,6},{8,9},{9,8},{10,11... | collective-permute-start | bytes 2359304 | tf_op jit(solution)/shard_map/ppermute | solution.py:18
  154.0 10.9 %collective-permute-start.40 = (bf16[96,576]{1,0:T(8,128)(2,1)}, bf16[96,576]{1,0:T(8,128)(2,1)S(1)}, u32[]{:S(2)}, u32[]{:S(2)}) collective-permute-start(bf16[96,576]{1,0:T(8,128)(2,1)} %get-tuple-element.24), channel_id=1, source_target_pairs={{0,20},{4,24},{8,28},{12,0},{16,4},{20,8},{24,12},{28,16},{1,21},{... | collective-permute-start | bytes 331784 | tf_op jit(solution)/shard_map/ppermute | solution.py:13
  159.3 11.8 %collective-permute-start.30 = (bf16[2,192,4,256]{3,1,2,0:T(8,128)(2,1)}, bf16[2,192,4,256]{3,1,2,0:T(8,128)(2,1)}, u32[]{:S(2)}, u32[]{:S(2)}) collective-permute-start(bf16[2,192,4,256]{3,1,2,0:T(8,128)(2,1)} %bitcast.308), channel_id=1, source_target_pairs={{0,1},{1,0},{2,3},{3,2},{4,5},{5,4},{6,7},{7,6},{8,9},{9,8},{10,11... | collective-permute-start | bytes 2359304 | tf_op jit(solution)/shard_map/ppermute | solution.py:18
  165.9 10.2 %collective-permute-start.34 = (bf16[2,192,4,256]{3,1,2,0:T(8,128)(2,1)}, bf16[2,192,4,256]{3,1,2,0:T(8,128)(2,1)}, u32[]{:S(2)}, u32[]{:S(2)}) collective-permute-start(bf16[2,192,4,256]{3,1,2,0:T(8,128)(2,1)} %bitcast.277), channel_id=1, source_target_pairs={{0,1},{1,0},{2,3},{3,2},{4,5},{5,4},{6,7},{7,6},{8,9},{9,8},{10,11... | collective-permute-start | bytes 2359304 | tf_op jit(solution)/shard_map/ppermute | solution.py:18
  169.5 12.0 %collective-permute-start.29 = (bf16[1,192,4,256]{3,1,2,0:T(8,128)(2,1)S(1)}, bf16[1,192,4,256]{3,1,2,0:T(8,128)(2,1)S(1)}, u32[]{:S(2)}, u32[]{:S(2)}) collective-permute-start(bf16[1,192,4,256]{3,1,2,0:T(8,128)(2,1)S(1)} %constant_dynamic-slice_fusion.9), channel_id=1, source_target_pairs={{0,2},{1,3},{2,0},{3,1},{4,6},{5,7},{6,4},{7,5},{8,10},{9,11},{10,... | collective-permute-start | bytes 1179656 | tf_op jit(solution)/shard_map/ppermute | solution.py:18
  172.5 17.4 %collective-permute-start.31 = (bf16[1,192,4,256]{3,1,2,0:T(8,128)(2,1)S(1)}, bf16[1,192,4,256]{3,1,2,0:T(8,128)(2,1)S(1)}, u32[]{:S(2)}, u32[]{:S(2)}) collective-permute-start(bf16[1,192,4,256]{3,1,2,0:T(8,128)(2,1)S(1)} %constant_dynamic-slice_fusion.6), channel_id=1, source_target_pairs={{0,2},{1,3},{2,0},{3,1},{4,6},{5,7},{6,4},{7,5},{8,10},{9,11},{10,... | collective-permute-start | bytes 1179656 | tf_op jit(solution)/shard_map/ppermute | solution.py:18
  174.5 23.8 %collective-permute-start.33 = (bf16[1,192,4,256]{3,1,2,0:T(8,128)(2,1)S(1)}, bf16[1,192,4,256]{3,1,2,0:T(8,128)(2,1)S(1)}, u32[]{:S(2)}, u32[]{:S(2)}) collective-permute-start(bf16[1,192,4,256]{3,1,2,0:T(8,128)(2,1)S(1)} %constant_dynamic-slice_fusion.3), channel_id=1, source_target_pairs={{0,2},{1,3},{2,0},{3,1},{4,6},{5,7},{6,4},{7,5},{8,10},{9,11},{10,... | collective-permute-start | bytes 1179656 | tf_op jit(solution)/shard_map/ppermute | solution.py:18
  177.4 29.0 %collective-permute-start.35 = (bf16[1,192,4,256]{3,1,2,0:T(8,128)(2,1)S(1)}, bf16[1,192,4,256]{3,1,2,0:T(8,128)(2,1)S(1)}, u32[]{:S(2)}, u32[]{:S(2)}) collective-permute-start(bf16[1,192,4,256]{3,1,2,0:T(8,128)(2,1)S(1)} %constant_dynamic-slice_fusion), channel_id=1, source_target_pairs={{0,2},{1,3},{2,0},{3,1},{4,6},{5,7},{6,4},{7,5},{8,10},{9,11},{10,... | collective-permute-start | bytes 1179656 | tf_op jit(solution)/shard_map/ppermute | solution.py:18
  (44 other events, 212.5 us)

commit v2 on v0

v2 whole, which is shorter than its diff:
```python
import functools

import jax
import jax.numpy as jnp
from jax import lax
from jax.experimental import pallas as pl
from jax.experimental.pallas import tpu as pltpu
from jax.sharding import PartitionSpec as P

HEAD_DIM = 64
F32 = jnp.float32
BF16 = jnp.bfloat16
LIMIT = 40 * 1024 * 1024

NN = (((1,), (0,)), ((), ()))
NT = (((1,), (1,)), ((), ()))
TN = (((0,), (0,)), ((), ()))


def mm(a, b, dims):
    return lax.dot_general(a, b, dims, preferred_element_type=F32)


def flip(values, axis, bit):
    n = lax.axis_size(axis)
    return lax.ppermute(values, axis, [(s, s ^ bit) for s in range(n)])


def params():
    return pltpu.CompilerParams(vmem_limit_bytes=LIMIT)


def cost(flops, moved):
    return pl.CostEstimate(flops=int(flops), bytes_accessed=int(moved), transcendentals=0)


def smem():
    return pl.BlockSpec(memory_space=pltpu.SMEM)


def lane_mask(length, cols):
    return (lax.broadcasted_iota(jnp.int32, (1, cols), 1) < length).astype(F32)


def project_kernel(lengths, sheet, wq, wk, wv, cot, qk, gt, parts, wt, acc):
    step = pl.program_id(0)
    rows, cols, _ = sheet.shape
    local = wq.shape[1]
    heads = local // HEAD_DIM

    @pl.when(step == 0)
    def _():
        for index, weight in enumerate((wq, wk, wv)):
            wt[index] = weight[...].T
        acc[...] = jnp.zeros_like(acc)

    projected = [[], [], []]
    for r in range(rows):
        mask = lane_mask(lengths[step * rows + r], cols)
        row = sheet[r]
        for index in range(3):
            value = (mm(wt[index], row, NT) * mask).astype(BF16)
            projected[index].append(value.reshape(heads, HEAD_DIM, cols))
        gt[:, r] = cot[r].T.reshape(heads, HEAD_DIM, cols)
    q, k, v = [jnp.stack(p, axis=1) for p in projected]
    qk[:heads] = q
    qk[heads:] = k
    for h in range(heads):
        flat = (rows * HEAD_DIM, cols)
        acc[0, h] += mm(q[h].reshape(flat), k[h].reshape(flat), TN)
        acc[1, h] += mm(gt[h].reshape(flat), v[h].reshape(flat), TN)

    @pl.when(step == pl.num_programs(0) - 1)
    def _():
        shards = parts.shape[0]
        for kind in range(2):
            for h in range(heads):
                parts[:, kind, h] = acc[kind, h].reshape(shards, cols // shards, cols).astype(parts.dtype)


def project(lengths, sheet, wq, wk, wv, cot, shards, kind, block):
    rows, cols, width = sheet.shape
    local = wq.shape[1]
    heads = local // HEAD_DIM
    whole = lambda shape: pl.BlockSpec(shape, lambda s: (0,) * len(shape))
    parts = (shards, 2, heads, cols // shards, cols)
    return pl.pallas_call(
        project_kernel,
        grid=(rows // block,),
        in_specs=[
            smem(),
            pl.BlockSpec((block, cols, width), lambda s: (s, 0, 0)),
            whole(wq.shape),
            whole(wq.shape),
            whole(wq.shape),
            pl.BlockSpec((block, cols, local), lambda s: (s, 0, 0)),
        ],
        out_specs=[
            pl.BlockSpec((2 * heads, block, HEAD_DIM, cols), lambda s: (0, s, 0, 0)),
            pl.BlockSpec((heads, block, HEAD_DIM, cols), lambda s: (0, s, 0, 0)),
            whole(parts),
        ],
        out_shape=[
            jax.ShapeDtypeStruct((2 * heads, rows, HEAD_DIM, cols), BF16),
            jax.ShapeDtypeStruct((heads, rows, HEAD_DIM, cols), BF16),
            jax.ShapeDtypeStruct(parts, kind),
        ],
        scratch_shapes=[
            pltpu.VMEM((3, local, width), BF16),
            pltpu.VMEM((2, heads, cols, cols), F32),
        ],
        compiler_params=params(),
        cost_estimate=cost(2 * rows * cols * local * (3 * width + 2 * cols), 2 * rows * cols * (width + 4 * local)),
        name="project",
    )(lengths, sheet, wq, wk, wv, cot)


def softmax_kernel(scale, got, out):
    logits = jnp.sum(got[:, 0].astype(F32), axis=0) * scale
    dprob = jnp.sum(got[:, 1].astype(F32), axis=0)
    shifted = jnp.exp(logits - jnp.max(logits, axis=-1, keepdims=True))
    probs = shifted / jnp.sum(shifted, axis=-1, keepdims=True)
    inner = jnp.sum(probs * dprob, axis=-1, keepdims=True)
    both = (probs.astype(BF16), (scale * probs * (dprob - inner)).astype(BF16))
    for copy in range(out.shape[0]):
        out[copy, 0] = both[0]
        out[copy, 1] = both[1]


def softmax_back(got, scale, copies):
    return pl.pallas_call(
        functools.partial(softmax_kernel, scale),
        out_shape=jax.ShapeDtypeStruct((copies,) + got.shape[1:], BF16),
        compiler_params=params(),
        cost_estimate=cost(got.size * 8, got.size * 4),
        name="softmax_back",
    )(got)


def backward_kernel(first, lengths, me, scores, qk, gt, wq, wk, wv, *rest):
    blocks, grads = rest[:-1], rest[-1]
    heads, rows, _, cols = gt.shape
    flat = (rows * HEAD_DIM, cols)
    square = lambda kind, h: scores[:, kind, h].reshape(cols, cols)
    split = (rows, HEAD_DIM, cols)
    masks = jnp.stack([lane_mask(lengths[first + r], cols) for r in range(rows)])
    for h in range(heads):
        probs, dscore = square(0, h), square(1, h)
        dq = mm(qk[heads + h].reshape(flat), dscore, NT)
        dk = mm(qk[h].reshape(flat), dscore, NN)
        dv = mm(gt[h].reshape(flat), probs, NN)
        for index, value in enumerate((dq, dk, dv)):
            grads[index * heads + h] = (value.reshape(split) * masks).astype(BF16)
    local = heads * HEAD_DIM
    for j, out in enumerate(blocks):
        here = me[0] ^ j
        for r in range(rows):
            total = None
            for index, weight in enumerate((wq, wk, wv)):
                grad = grads[index * heads : (index + 1) * heads, r].reshape(local, cols)
                term = mm(weight[here], grad, NN)
                total = term if total is None else total + term
            out[r] = total.astype(BF16)


def backward(first, count, lengths, me, scores, qk, gt, wq, wk, wv):
    heads, rows, _, cols = gt.shape
    n, share, local = wq.shape
    whole = lambda a: pl.BlockSpec(a.shape, lambda s: (0,) * a.ndim)
    at = first // count
    return pl.pallas_call(
        functools.partial(backward_kernel, first),
        grid=(1,),
        in_specs=[
            smem(),
            smem(),
            whole(scores),
            pl.BlockSpec((2 * heads, count, HEAD_DIM, cols), lambda s: (0, at, 0, 0)),
            pl.BlockSpec((heads, count, HEAD_DIM, cols), lambda s: (0, at, 0, 0)),
            whole(wq),
            whole(wq),
            whole(wq),
        ],
        out_specs=[pl.BlockSpec((count, share, cols), lambda s: (0, 0, 0))] * n
        + [pl.BlockSpec((3 * heads, count, HEAD_DIM, cols), lambda s: (0, 0, 0, 0))],
        out_shape=[jax.ShapeDtypeStruct((count, share, cols), BF16)] * n
        + [jax.ShapeDtypeStruct((3 * heads, count, HEAD_DIM, cols), BF16)],
        compiler_params=params(),
        cost_estimate=cost(
            2 * count * cols * local * 3 * (cols + n * share), 2 * count * cols * (6 * local + n * share)
        ),
        name="backward",
    )(lengths, me, scores, qk, gt, wq, wk, wv)


def add_kernel(keep, got, out):
    out[...] = (keep[...].astype(F32) + got[...].astype(F32)).astype(BF16)


def add(keep, got):
    return pl.pallas_call(
        add_kernel,
        out_shape=jax.ShapeDtypeStruct(keep.shape, BF16),
        compiler_params=params(),
        cost_estimate=cost(keep.size, keep.size * 6),
        name="add",
    )(keep, got)


def finish_kernel(keep, got, *rest):
    out = rest[-1]
    for r in range(keep.shape[0]):
        total = (keep[r].astype(F32) + got[r].astype(F32)).astype(BF16)
        out[r] = total.T


def finish(keep, got, at, total_rows, before):
    count, share, cols = keep.shape
    spec = pl.BlockSpec(keep.shape, lambda s: (0, 0, 0))
    extra = [] if before is None else [before]
    return pl.pallas_call(
        finish_kernel,
        grid=(1,),
        in_specs=[spec, spec] + [pl.BlockSpec(memory_space=pl.ANY)] * len(extra),
        out_specs=pl.BlockSpec((count, cols, share), lambda s: (at, 0, 0)),
        out_shape=jax.ShapeDtypeStruct((total_rows, cols, share), BF16),
        input_output_aliases={2: 0} if extra else {},
        compiler_params=params(),
        cost_estimate=cost(keep.size, keep.size * 6),
        name="finish",
    )(keep, got, *extra)


def weight_kernel(sheet, *rest):
    grads, out, acc = rest[:-2], rest[-2], rest[-1]
    step = pl.program_id(0)
    rows, cols, width = sheet.shape

    @pl.when(step == 0)
    def _():
        acc[...] = jnp.zeros_like(acc)

    for index, grad in enumerate(grads):
        @pl.when(step == index)
        def _():
            n = grad.shape[0] * HEAD_DIM
            left = jnp.concatenate([grad[:, r].reshape(n, cols) for r in range(rows)], axis=1)
            acc[...] += mm(left, sheet[...].reshape(rows * cols, width), NN)

    @pl.when(step == pl.num_programs(0) - 1)
    def _():
        out[...] = acc[...].T.reshape(out.shape).astype(out.dtype)


def weight_part(sheet, grads, shards, kind):
    rows, cols, width = sheet.shape
    count = rows // len(grads)
    columns = grads[0].shape[0] * HEAD_DIM
    shape = (shards, width // shards, columns)
    return pl.pallas_call(
        weight_kernel,
        grid=(len(grads),),
        in_specs=[pl.BlockSpec((count, cols, width), lambda s: (s, 0, 0))]
        + [pl.BlockSpec(g.shape, lambda s: (0, 0, 0, 0)) for g in grads],
        out_specs=pl.BlockSpec(shape, lambda s: (0, 0, 0)),
        out_shape=jax.ShapeDtypeStruct(shape, kind),
        scratch_shapes=[pltpu.VMEM((columns, width), F32)],
        compiler_params=params(),
        cost_estimate=cost(2 * rows * cols * width * columns, 2 * rows * cols * (width + columns)),
        name="weight_part",
    )(sheet, *grads)


def sum_kernel(got, out):
    out[...] = jnp.sum(got[...].astype(F32), axis=0)


def sum_parts(got):
    return pl.pallas_call(
        sum_kernel,
        out_shape=jax.ShapeDtypeStruct(got.shape[1:], F32),
        compiler_params=params(),
        cost_estimate=cost(got.size, got.size * 2),
        name="sum_parts",
    )(got)


def body(sheet, w_query, w_key, w_value, cotangent, lengths):
    row_dev, cols, width = sheet.shape
    local = w_query.shape[1]
    n_rows = lax.axis_size("rows")
    n_heads = lax.axis_size("heads")
    scale = float(1.0 / (HEAD_DIM * row_dev * n_rows) ** 0.5)
    direct = n_rows <= 8
    shards = n_rows if direct else 1
    chunk = 4

    qk, gt, parts = project(
        lengths, sheet, w_query, w_key, w_value, cotangent, shards, BF16 if direct else F32, 4
    )
    if direct:
        got = lax.all_to_all(parts, "rows", 0, 0)
        scores = lax.all_to_all(softmax_back(got, scale, shards), "rows", 0, 0)
    else:
        scores = softmax_back(lax.psum(parts, "rows"), scale, 1)

    me = lax.axis_index("heads").astype(jnp.int32).reshape(1)
    by_device = [w.reshape(n_heads, width // n_heads, local) for w in (w_query, w_key, w_value)]
    out, grads = None, []
    for first in range(0, row_dev, chunk):
        *live, grad = backward(first, chunk, lengths, me, scores, qk, gt, *by_device)
        grads.append(grad)
        bit = 1
        while bit < n_heads:
            give, keep = live[1::2], live[0::2]
            got = [flip(g, "heads", bit) for g in give]
            last = bit * 2 == n_heads
            if last:
                out = finish(keep[0], got[0], first // chunk, row_dev, out)
            else:
                live = [add(a, b) for a, b in zip(keep, got)]
            bit *= 2

    if direct:
        got = lax.all_to_all(weight_part(sheet, grads, shards, BF16), "rows", 0, 0)
        weight_grad = sum_parts(got)
    else:
        weight_grad = lax.psum_scatter(
            weight_part(sheet, grads, 1, F32)[0], "rows", scatter_dimension=0, tiled=True
        )
    return (out, weight_grad.reshape(width // n_rows, 3, local))


def solution(mesh):
    in_specs = (
        P("rows", None, None),
        P(None, "heads"),
        P(None, "heads"),
        P(None, "heads"),
        P("rows", None, "heads"),
        P("rows"),
    )
    out_specs = (P("rows", None, "heads"), P("rows", None, "heads"))
    return jax.shard_map(body, mesh=mesh, in_specs=in_specs, out_specs=out_specs, check_vma=False)
```

time: 289 us -> 155 us (0.54)
  waiting for transfers between devices: 206 us -> 51.9 us
  matrix products: 45.6 us -> 0 us
  Pallas kernels: 0 us -> 31.3 us
  blocking collectives: 0 us -> 27.2 us
  starting transfers between devices: 0.3 us -> 14.4 us
  between operations: 13.8 us -> 0.97 us
  local copies, waits for them, and re-layouts: 19.2 us -> 28.2 us
  other arithmetic: 3.3 us -> 0.01 us
    psum x1 -> x0, waiting for transfers between devices: 90.6 us -> none  [body(): logits, dprob = lax.psum((logit_part, dprob_part), 'rows')]
    reduce_scatter x1 -> x0, waiting for transfers between devices: 58.6 us -> none  [body(): lax.psum_scatter(input_part, 'heads', scatter_dimension=2, tiled=True)]
    unnamed x4 -> x0, waiting for transfers between devices: 57 us -> none
    dot_general x7 -> x0, matrix products: 40.6 us -> none  [the longest x1 9.24 us: body(): lax.dot_general(flat_grads, weights, (((1,), (1,)), ((), ())), preferred_...]
    ppermute x0 -> x12, waiting for transfers between devices: none -> 32.8 us  [flip(): return lax.ppermute(values, axis, [(s, s ^ bit) for s in range(n)])]
    pallas_call x0 -> x20, Pallas kernels: none -> 31.3 us  [the longest x4 13.5 us: backward(): pl.pallas_call(functools.partial(backward_kernel, first), grid=(1,), in_s...]
    all_to_all x0 -> x1, blocking collectives: none -> 27.2 us  [body(): got = lax.all_to_all(parts, 'rows', 0, 0)]
    all_to_all x0 -> x2, waiting for transfers between devices: none -> 19.1 us  [the longest x1 19.1 us: body(): scores = lax.all_to_all(softmax_back(got, scale, shards), 'rows', 0, 0)]
  transfers between devices with their start and end apart: 3 -> 14, of which waited for: 3 -> 7; matrix products, arithmetic and copies ran while one was open for 4% -> 1% of each run, Pallas kernels for 0% -> 1%
where the time goes in v2:
time: 155 us; the launch traced here: 154 us
  waiting for transfers between devices  51.9 us (33%)
  Pallas kernels  31.3 us (20%)
  local copies, waits for them, and re-layouts  28.2 us (18%)
  blocking collectives  27.2 us (18%)
  starting transfers between devices  14.4 us (9%)
    ppermute x12, waiting for transfers between devices, flip(): return lax.ppermute(values, axis, [(s, s ^ bit) for s in range(n)])  32.8 us
    unnamed x80, local copies, waits for them, and re-layouts  28 us
    all_to_all x1, blocking collectives, body(): got = lax.all_to_all(parts, 'rows', 0, 0)  27.2 us
    all_to_all x1, waiting for transfers between devices, body(): scores = lax.all_to_all(softmax_back(got, scale, shards), 'rows', 0, 0)  19.1 us
    pallas_call x4, Pallas kernels, backward(): pl.pallas_call(functools.partial(backward_kernel, first), grid=(1,), in_s...  13.5 us
    pallas_call x1, Pallas kernels, project(): pl.pallas_call(project_kernel, grid=(rows // block,), in_specs=[smem(), p...  10.3 us
    ppermute x12, starting transfers between devices, flip(): return lax.ppermute(values, axis, [(s, s ^ bit) for s in range(n)])  6.05 us
    pallas_call x1, Pallas kernels, weight_part(): pl.pallas_call(weight_kernel, grid=(len(grads),), in_specs=[pl.BlockSpec(...  5.54 us
  transfers between devices with their start and end apart: 14, of which 7 were waited for; matrix products, arithmetic and copies ran while one was open for 1% of the time, Pallas kernels for 1%

profile of v2, /device:TPU:0, one launch (start us, length us, event | category | flops | bytes accessed | tf_op | source)
XLA Modules:
  0.0 153.9 jit_solution(17388087961291188302)
XLA Ops:
  0.6 1.2 copy.20.wq
  1.9 1.9 %copy.21.wk = bf16[768,192]{1,0:T(8,128)(2,1)} copy(bf16[768,192]{0,1:T(8,128)(2,1)} %param.8) | data formatting | bytes 589824 | tf_op args[2]
  3.8 1.9 %copy.22.wv = bf16[768,192]{1,0:T(8,128)(2,1)} copy(bf16[768,192]{0,1:T(8,128)(2,1)} %param.9) | data formatting | bytes 589824 | tf_op args[3]
  5.7 2.5 %copy.23.cot = bf16[16,256,192]{2,1,0:T(8,128)(2,1)} copy(bf16[16,256,192]{1,2,0:T(8,128)(2,1)S(1)} %copy-done.34) | data formatting | bytes 3145728 | tf_op args[4]
  10.2 1.6 %copy-done.7 = bf16[16,256,192]{2,1,0:T(8,128)(2,1)S(1)} copy-done((bf16[16,256,192]{2,1,0:T(8,128)(2,1)S(1)}, bf16[16,256,192]{2,1,0:T(8,128)(2,1)}, u32[]{:S(2)}) %copy-start.7) | copy-done | bytes 1572888
  11.8 10.3 %project.1 = (bf16[6,16,64,256]{3,2,1,0:T(8,128)(2,1)S(1)}, bf16[3,16,64,256]{3,2,1,0:T(8,128)(2,1)S(1)}, bf16[8,2,3,32,256]{4,3,2,1,0:T(8,128)(2,1)S(1)}) custom-call(s32[16]{0:T(128)S(1)} %copy-done.24, bf16[16,256,768]{2,1,0:T(8,128)(2,1)} %sheet.3, bf16[768,192]{1,0:T(8,128)(2,1)S(1)} %copy.20.wq, bf16[768,192]{1,0:T(8,128)(2,1)S(1)} %copy-done.2, ...), custom_call_target="tpu_custom_call" | custom-call | flops 4429185024 | bytes 12582912 | tf_op jit(solution)/shard_map/project/pallas_call | solution.py:87
  22.1 1.1 copy-done
  23.3 27.2 %all_to_all.15.got = bf16[8,2,3,32,256]{4,3,2,1,0:T(8,128)(2,1)S(1)} all-to-all(bf16[8,2,3,32,256]{4,3,2,1,0:T(8,128)(2,1)S(1)} %get-tuple-element.25), channel_id=1, replica_groups=mesh['rows'=8,'heads'=4] {'rows'}, dimensions={0} | all-to-all | bytes 1572864 | tf_op jit(solution)/shard_map/all_to_all | solution.py:302
  51.6 4.4 %all-to-all-start.1 = ((bf16[8,2,3,32,256]{4,3,2,1,0:T(8,128)(2,1)}), bf16[8,2,3,32,256]{4,3,2,1,0:T(8,128)(2,1)}, u32[]{:S(2)}, u32[]{:S(2)}) async-start(bf16[8,2,3,32,256]{4,3,2,1,0:T(8,128)(2,1)} %copy-done.6), calls=%async_computation.1 | async-start | bytes 1572864 | tf_op jit(solution)/shard_map/all_to_all | solution.py:303
  56.1 19.1 %all-to-all-done.1.scores = bf16[8,2,3,32,256]{4,3,2,1,0:T(8,128)(2,1)} async-done(((bf16[8,2,3,32,256]{4,3,2,1,0:T(8,128)(2,1)}), bf16[8,2,3,32,256]{4,3,2,1,0:T(8,128)(2,1)}, u32[]{:S(2)}, u32[]{:S(2)}) %all-to-all-start.1) | async-done | bytes 786464 | tf_op jit(solution)/shard_map/all_to_all | solution.py:303
  75.2 1.4 copy-done.1
  78.6 3.5 %backward.4 = (bf16[4,192,256]{2,1,0:T(8,128)(2,1)S(1)}, bf16[4,192,256]{2,1,0:T(8,128)(2,1)}, bf16[4,192,256]{2,1,0:T(8,128)(2,1)S(1)}, bf16[4,192,256]{2,1,0:T(8,128)(2,1)S(1)}, bf16[9,4,64,256]{3,2,1,0:T(8,128)(2,1)S(1)}) custom-call(s32[16]{0:T(128)S(1)} %copy-done.24, s32[1]{0:T(128)} %bitcast.me, bf16[8,2,3,32,256]{4,3,2,1,0:T(8,128)(2,1)} %all-to-all-done.1.scores, ...), custom_call_target="tpu_custom_call" | custom-call | flops 1207959552 | bytes 3932160 | tf_op jit(solution)/shard_map/backward/pallas_call | solution.py:171
  83.6 3.7 %backward.5 = (bf16[4,192,256]{2,1,0:T(8,128)(2,1)S(1)}, bf16[4,192,256]{2,1,0:T(8,128)(2,1)}, bf16[4,192,256]{2,1,0:T(8,128)(2,1)S(1)}, bf16[4,192,256]{2,1,0:T(8,128)(2,1)S(1)}, bf16[9,4,64,256]{3,2,1,0:T(8,128)(2,1)S(1)}) custom-call(s32[16]{0:T(128)S(1)} %copy-done.24, s32[1]{0:T(128)} %bitcast.me, bf16[8,2,3,32,256]{4,3,2,1,0:T(8,128)(2,1)} %all-to-all-done.1.scores, ...), custom_call_target="tpu_custom_call" | custom-call | flops 1207959552 | bytes 3932160 | tf_op jit(solution)/shard_map/backward/pallas_call | solution.py:171
  89.6 3.1 %backward.6 = (bf16[4,192,256]{2,1,0:T(8,128)(2,1)S(1)}, bf16[4,192,256]{2,1,0:T(8,128)(2,1)S(1)}, bf16[4,192,256]{2,1,0:T(8,128)(2,1)S(1)}, bf16[4,192,256]{2,1,0:T(8,128)(2,1)S(1)}, bf16[9,4,64,256]{3,2,1,0:T(8,128)(2,1)S(1)}) custom-call(s32[16]{0:T(128)S(1)} %copy-done.24, s32[1]{0:T(128)} %bitcast.me, ...), custom_call_target="tpu_custom_call" | custom-call | flops 1207959552 | bytes 3932160 | tf_op jit(solution)/shard_map/backward/pallas_call | solution.py:171
  94.2 3.2 %backward.7 = (bf16[4,192,256]{2,1,0:T(8,128)(2,1)S(1)}, bf16[4,192,256]{2,1,0:T(8,128)(2,1)S(1)}, bf16[4,192,256]{2,1,0:T(8,128)(2,1)S(1)}, bf16[4,192,256]{2,1,0:T(8,128)(2,1)S(1)}, bf16[9,4,64,256]{3,2,1,0:T(8,128)(2,1)S(1)}) custom-call(s32[16]{0:T(128)S(1)} %copy-done.24, s32[1]{0:T(128)} %bitcast.me, ...), custom_call_target="tpu_custom_call" | custom-call | flops 1207959552 | bytes 3932160 | tf_op jit(solution)/shard_map/backward/pallas_call | solution.py:171
  100.5 5.5 %weight_part.1 = bf16[8,96,576]{2,1,0:T(8,128)(2,1)} custom-call(bf16[16,256,768]{2,1,0:T(8,128)(2,1)S(1)} %bitcast.18, bf16[9,4,64,256]{3,2,1,0:T(8,128)(2,1)S(1)} %get-tuple-element.44.rest_0_, bf16[9,4,64,256]{3,2,1,0:T(8,128)(2,1)S(1)} %get-tuple-element.45.rest_1_, bf16[9,4,64,256]{3,2,1,0:T(8,128)(2,1)S(1)} %get-tuple-element.46.rest_2_, ...), custom_call_target="tpu_custom_call" | custom-call | flops 3623878656 | bytes 11010048 | tf_op jit(solution)/shard_map/weight_part/pallas_call | solution.py:260
  106.0 3.9 %all-to-all-start.2 = ((bf16[8,96,576]{2,1,0:T(8,128)(2,1)}), bf16[8,96,576]{2,1,0:T(8,128)(2,1)S(1)}, u32[]{:S(2)}, u32[]{:S(2)}) async-start(bf16[8,96,576]{2,1,0:T(8,128)(2,1)} %weight_part.1), calls=%async_computation.2 | async-start | bytes 1966080 | tf_op jit(solution)/shard_map/all_to_all | solution.py:325
  113.8 1.6 %collective-permute-start.11 = (bf16[4,192,256]{2,1,0:T(8,128)(2,1)S(1)}, bf16[4,192,256]{2,1,0:T(8,128)(2,1)S(1)}, u32[]{:S(2)}, u32[]{:S(2)}) collective-permute-start(bf16[4,192,256]{2,1,0:T(8,128)(2,1)S(1)} %add.15), channel_id=1, source_target_pairs={{0,2},{1,3},{2,0},{3,1},{4,6},{5,7},{6,4},{7,5},{8,10},{9,11},{10,... | collective-permute-start | bytes 1179656 | tf_op jit(solution)/shard_map/ppermute | solution.py:26
  116.1 1.5 collective-permute-start.5
  118.5 7.3 %collective-permute-done.11.got = bf16[4,192,256]{2,1,0:T(8,128)(2,1)S(1)} collective-permute-done((bf16[4,192,256]{2,1,0:T(8,128)(2,1)S(1)}, bf16[4,192,256]{2,1,0:T(8,128)(2,1)S(1)}, u32[]{:S(2)}, u32[]{:S(2)}) %collective-permute-start.11) | collective-permute-done | bytes 393248 | tf_op jit(solution)/shard_map/ppermute | solution.py:26
  126.0 8.2 %collective-permute-done.8.got = bf16[4,192,256]{2,1,0:T(8,128)(2,1)S(1)} collective-permute-done((bf16[4,192,256]{2,1,0:T(8,128)(2,1)S(1)}, bf16[4,192,256]{2,1,0:T(8,128)(2,1)S(1)}, u32[]{:S(2)}, u32[]{:S(2)}) %collective-permute-start.8) | collective-permute-done | bytes 393248 | tf_op jit(solution)/shard_map/ppermute | solution.py:26
  134.5 8.2 %collective-permute-done.5.got = bf16[4,192,256]{2,1,0:T(8,128)(2,1)S(1)} collective-permute-done((bf16[4,192,256]{2,1,0:T(8,128)(2,1)S(1)}, bf16[4,192,256]{2,1,0:T(8,128)(2,1)S(1)}, u32[]{:S(2)}, u32[]{:S(2)}) %collective-permute-start.5) | collective-permute-done | bytes 393248 | tf_op jit(solution)/shard_map/ppermute | solution.py:26
  142.9 7.4 %collective-permute-done.2.got = bf16[4,192,256]{2,1,0:T(8,128)(2,1)S(1)} collective-permute-done((bf16[4,192,256]{2,1,0:T(8,128)(2,1)S(1)}, bf16[4,192,256]{2,1,0:T(8,128)(2,1)S(1)}, u32[]{:S(2)}, u32[]{:S(2)}) %collective-permute-start.2) | collective-permute-done | bytes 393248 | tf_op jit(solution)/shard_map/ppermute | solution.py:26
  150.5 2.3 %copy.28 = bf16[16,256,192]{1,2,0:T(8,128)(2,1)} copy(bf16[16,256,192]{2,1,0:T(8,128)(2,1)S(1)} %finish.7) | data formatting | bytes 3145728
  (107 shorter events, 20.7 us)
Async XLA Ops:
  51.6 23.5 %all-to-all-start.1 = ((bf16[8,2,3,32,256]{4,3,2,1,0:T(8,128)(2,1)}), bf16[8,2,3,32,256]{4,3,2,1,0:T(8,128)(2,1)}, u32[]{:S(2)}, u32[]{:S(2)}) async-start(bf16[8,2,3,32,256]{4,3,2,1,0:T(8,128)(2,1)} %copy-done.6), calls=%async_computation.1 | async-start | bytes 1572864 | tf_op jit(solution)/shard_map/all_to_all | solution.py:303
  83.6 16.9 %slice-start = ((s8[6291456]{0:T(1024)(128)(4,1)}), s8[4194304]{0:T(1024)(128)(4,1)S(1)}, s32[]{:S(2)}) async-start(s8[6291456]{0:T(1024)(128)(4,1)} %bitcast.17), calls=%async_computation.3 | async-start | bytes 8388608
  89.6 10.9 %slice-start.1 = ((s8[6291456]{0:T(1024)(128)(4,1)}), s8[2097152]{0:T(1024)(128)(4,1)S(1)}, s32[]{:S(2)}) async-start(s8[6291456]{0:T(1024)(128)(4,1)} %bitcast.17), calls=%async_computation.4 | async-start | bytes 4194304
  94.2 5.5 %copy-start.28 = (bf16[4,192,256]{2,1,0:T(8,128)(2,1)}, bf16[4,192,256]{2,1,0:T(8,128)(2,1)S(1)}, u32[]{:S(2)}) copy-start(bf16[4,192,256]{2,1,0:T(8,128)(2,1)S(1)} %get-tuple-element.39) | copy-start | bytes 1179652
  100.5 9.5 %copy-start.33 = (bf16[4,192,256]{2,1,0:T(8,128)(2,1)S(1)}, bf16[4,192,256]{2,1,0:T(8,128)(2,1)}, u32[]{:S(2)}) copy-start(bf16[4,192,256]{2,1,0:T(8,128)(2,1)} %copy-done.32) | copy-start | bytes 1179652
  100.5 9.6 %copy-start.31 = (bf16[4,192,256]{2,1,0:T(8,128)(2,1)S(1)}, bf16[4,192,256]{2,1,0:T(8,128)(2,1)}, u32[]{:S(2)}) copy-start(bf16[4,192,256]{2,1,0:T(8,128)(2,1)} %copy-done.30) | copy-start | bytes 1179652
  106.0 7.0 %copy-start.19 = (bf16[4,192,256]{2,1,0:T(8,128)(2,1)S(1)}, bf16[4,192,256]{2,1,0:T(8,128)(2,1)}, u32[]{:S(2)}) copy-start(bf16[4,192,256]{2,1,0:T(8,128)(2,1)} %copy-done.18) | copy-start | bytes 1179652
  106.0 7.1 %copy-start.21 = (bf16[4,192,256]{2,1,0:T(8,128)(2,1)S(1)}, bf16[4,192,256]{2,1,0:T(8,128)(2,1)}, u32[]{:S(2)}) copy-start(bf16[4,192,256]{2,1,0:T(8,128)(2,1)} %copy-done.20) | copy-start | bytes 1179652
  106.0 7.2 %copy-start.26 = (bf16[4,192,256]{2,1,0:T(8,128)(2,1)S(1)}, bf16[4,192,256]{2,1,0:T(8,128)(2,1)}, u32[]{:S(2)}) copy-start(bf16[4,192,256]{2,1,0:T(8,128)(2,1)} %copy-done.25) | copy-start | bytes 1179652
  106.0 7.7 %copy-start.23 = (bf16[4,192,256]{2,1,0:T(8,128)(2,1)S(1)}, bf16[4,192,256]{2,1,0:T(8,128)(2,1)}, u32[]{:S(2)}) copy-start(bf16[4,192,256]{2,1,0:T(8,128)(2,1)} %copy-done.22) | copy-start | bytes 1179652
  106.0 46.8 %all-to-all-start.2 = ((bf16[8,96,576]{2,1,0:T(8,128)(2,1)}), bf16[8,96,576]{2,1,0:T(8,128)(2,1)S(1)}, u32[]{:S(2)}, u32[]{:S(2)}) async-start(bf16[8,96,576]{2,1,0:T(8,128)(2,1)} %weight_part.1), calls=%async_computation.2 | async-start | bytes 1966080 | tf_op jit(solution)/shard_map/all_to_all | solution.py:325
  109.9 5.4 %copy-start.17 = (bf16[4,192,256]{2,1,0:T(8,128)(2,1)S(1)}, bf16[4,192,256]{2,1,0:T(8,128)(2,1)}, u32[]{:S(2)}) copy-start(bf16[4,192,256]{2,1,0:T(8,128)(2,1)} %copy-done.16) | copy-start | bytes 1179652
  110.0 1.8 %collective-permute-start.1 = (bf16[4,192,256]{2,1,0:T(8,128)(2,1)S(1)}, bf16[4,192,256]{2,1,0:T(8,128)(2,1)S(1)}, u32[]{:S(2)}, u32[]{:S(2)}) collective-permute-start(bf16[4,192,256]{2,1,0:T(8,128)(2,1)S(1)} %copy-done.33), channel_id=1, source_target_pairs={{0,1},{1,0},{2,3},{3,2},{4,5},{5,4},{6,7},{7,6},{8,9},{9,8},{10,11... | collective-permute-start | bytes 1179656 | tf_op jit(solution)/shard_map/ppermute | solution.py:26
  110.1 2.8 %collective-permute-start.4 = (bf16[4,192,256]{2,1,0:T(8,128)(2,1)S(1)}, bf16[4,192,256]{2,1,0:T(8,128)(2,1)S(1)}, u32[]{:S(2)}, u32[]{:S(2)}) collective-permute-start(bf16[4,192,256]{2,1,0:T(8,128)(2,1)S(1)} %copy-done.31), channel_id=1, source_target_pairs={{0,1},{1,0},{2,3},{3,2},{4,5},{5,4},{6,7},{7,6},{8,9},{9,8},{10,11... | collective-permute-start | bytes 1179656 | tf_op jit(solution)/shard_map/ppermute | solution.py:26
  110.5 2.7 %collective-permute-start.10 = (bf16[4,192,256]{2,1,0:T(8,128)(2,1)}, bf16[4,192,256]{2,1,0:T(8,128)(2,1)S(1)}, u32[]{:S(2)}, u32[]{:S(2)}) collective-permute-start(bf16[4,192,256]{2,1,0:T(8,128)(2,1)} %copy-done.29), channel_id=1, source_target_pairs={{0,1},{1,0},{2,3},{3,2},{4,5},{5,4},{6,7},{7,6},{8,9},{9,8},{10,11... | collective-permute-start | bytes 1179656 | tf_op jit(solution)/shard_map/ppermute | solution.py:26
  110.6 3.2 %collective-permute-start.7 = (bf16[4,192,256]{2,1,0:T(8,128)(2,1)}, bf16[4,192,256]{2,1,0:T(8,128)(2,1)S(1)}, u32[]{:S(2)}, u32[]{:S(2)}) collective-permute-start(bf16[4,192,256]{2,1,0:T(8,128)(2,1)} %copy-done.28), channel_id=1, source_target_pairs={{0,1},{1,0},{2,3},{3,2},{4,5},{5,4},{6,7},{7,6},{8,9},{9,8},{10,11... | collective-permute-start | bytes 1179656 | tf_op jit(solution)/shard_map/ppermute | solution.py:26
  111.1 4.4 %collective-permute-start = (bf16[4,192,256]{2,1,0:T(8,128)(2,1)}, bf16[4,192,256]{2,1,0:T(8,128)(2,1)S(1)}, u32[]{:S(2)}, u32[]{:S(2)}) collective-permute-start(bf16[4,192,256]{2,1,0:T(8,128)(2,1)} %get-tuple-element.29), channel_id=1, source_target_pairs={{0,1},{1,0},{2,3},{3,2},{4,5},{5,4},{6,7},{7,6},{8,9},{9,8},{10,11... | collective-permute-start | bytes 1179656 | tf_op jit(solution)/shard_map/ppermute | solution.py:26
  111.8 4.3 %collective-permute-start.3 = (bf16[4,192,256]{2,1,0:T(8,128)(2,1)}, bf16[4,192,256]{2,1,0:T(8,128)(2,1)S(1)}, u32[]{:S(2)}, u32[]{:S(2)}) collective-permute-start(bf16[4,192,256]{2,1,0:T(8,128)(2,1)} %get-tuple-element.33), channel_id=1, source_target_pairs={{0,1},{1,0},{2,3},{3,2},{4,5},{5,4},{6,7},{7,6},{8,9},{9,8},{10,11... | collective-permute-start | bytes 1179656 | tf_op jit(solution)/shard_map/ppermute | solution.py:26
  112.9 4.7 %collective-permute-start.6 = (bf16[4,192,256]{2,1,0:T(8,128)(2,1)}, bf16[4,192,256]{2,1,0:T(8,128)(2,1)S(1)}, u32[]{:S(2)}, u32[]{:S(2)}) collective-permute-start(bf16[4,192,256]{2,1,0:T(8,128)(2,1)} %copy-done.27), channel_id=1, source_target_pairs={{0,1},{1,0},{2,3},{3,2},{4,5},{5,4},{6,7},{7,6},{8,9},{9,8},{10,11... | collective-permute-start | bytes 1179656 | tf_op jit(solution)/shard_map/ppermute | solution.py:26
  113.3 5.2 %collective-permute-start.9 = (bf16[4,192,256]{2,1,0:T(8,128)(2,1)S(1)}, bf16[4,192,256]{2,1,0:T(8,128)(2,1)S(1)}, u32[]{:S(2)}, u32[]{:S(2)}) collective-permute-start(bf16[4,192,256]{2,1,0:T(8,128)(2,1)S(1)} %copy-done.26), channel_id=1, source_target_pairs={{0,1},{1,0},{2,3},{3,2},{4,5},{5,4},{6,7},{7,6},{8,9},{9,8},{10,11... | collective-permute-start | bytes 1179656 | tf_op jit(solution)/shard_map/ppermute | solution.py:26
  113.8 12.0 %collective-permute-start.11 = (bf16[4,192,256]{2,1,0:T(8,128)(2,1)S(1)}, bf16[4,192,256]{2,1,0:T(8,128)(2,1)S(1)}, u32[]{:S(2)}, u32[]{:S(2)}) collective-permute-start(bf16[4,192,256]{2,1,0:T(8,128)(2,1)S(1)} %add.15), channel_id=1, source_target_pairs={{0,2},{1,3},{2,0},{3,1},{4,6},{5,7},{6,4},{7,5},{8,10},{9,11},{10,... | collective-permute-start | bytes 1179656 | tf_op jit(solution)/shard_map/ppermute | solution.py:26
  115.5 18.8 %collective-permute-start.8 = (bf16[4,192,256]{2,1,0:T(8,128)(2,1)S(1)}, bf16[4,192,256]{2,1,0:T(8,128)(2,1)S(1)}, u32[]{:S(2)}, u32[]{:S(2)}) collective-permute-start(bf16[4,192,256]{2,1,0:T(8,128)(2,1)S(1)} %add.13), channel_id=1, source_target_pairs={{0,2},{1,3},{2,0},{3,1},{4,6},{5,7},{6,4},{7,5},{8,10},{9,11},{10,... | collective-permute-start | bytes 1179656 | tf_op jit(solution)/shard_map/ppermute | solution.py:26
  116.1 26.6 %collective-permute-start.5 = (bf16[4,192,256]{2,1,0:T(8,128)(2,1)S(1)}, bf16[4,192,256]{2,1,0:T(8,128)(2,1)S(1)}, u32[]{:S(2)}, u32[]{:S(2)}) collective-permute-start(bf16[4,192,256]{2,1,0:T(8,128)(2,1)S(1)} %add.11), channel_id=1, source_target_pairs={{0,2},{1,3},{2,0},{3,1},{4,6},{5,7},{6,4},{7,5},{8,10},{9,11},{10,... | collective-permute-start | bytes 1179656 | tf_op jit(solution)/shard_map/ppermute | solution.py:26
  117.6 32.7 %collective-permute-start.2 = (bf16[4,192,256]{2,1,0:T(8,128)(2,1)S(1)}, bf16[4,192,256]{2,1,0:T(8,128)(2,1)S(1)}, u32[]{:S(2)}, u32[]{:S(2)}) collective-permute-start(bf16[4,192,256]{2,1,0:T(8,128)(2,1)S(1)} %add.9), channel_id=1, source_target_pairs={{0,2},{1,3},{2,0},{3,1},{4,6},{5,7},{6,4},{7,5},{8,10},{9,11},{10,... | collective-permute-start | bytes 1179656 | tf_op jit(solution)/shard_map/ppermute | solution.py:26
  (27 other events, 51.6 us)

commit v3 on v0

v3 whole, which is shorter than its diff:
```python
import functools

import jax
import jax.numpy as jnp
from jax import lax
from jax.experimental import pallas as pl
from jax.experimental.pallas import tpu as pltpu
from jax.sharding import PartitionSpec as P

HEAD_DIM = 64
F32 = jnp.float32
BF16 = jnp.bfloat16
MIB = 1024 * 1024

NN = (((1,), (0,)), ((), ()))
NT = (((1,), (1,)), ((), ()))
TN = (((0,), (0,)), ((), ()))


def mm(a, b, dims):
    return lax.dot_general(a, b, dims, preferred_element_type=F32)


def flip(values, axis, bit):
    n = lax.axis_size(axis)
    return lax.ppermute(values, axis, [(s, s ^ bit) for s in range(n)])


def cost(flops, moved):
    return pl.CostEstimate(flops=int(flops), bytes_accessed=int(moved), transcendentals=0)


SMEM = pl.BlockSpec(memory_space=pltpu.SMEM)
VMEM = pl.BlockSpec(memory_space=pltpu.VMEM)
ANY = pl.BlockSpec(memory_space=pl.ANY)


def like(shape, dtype=BF16):
    return jax.ShapeDtypeStruct(shape, dtype)


def in_vmem(kernel, name, out, *operands, scalars=0, after=(), limit=12, flops=0):
    many = len(after)

    def run(*refs):
        kernel(*refs[: len(operands)], *refs[len(operands) + many :])

    moved = 2 * sum(a.size for a in operands) + 2 * sum(o.size for o in out)
    return pl.pallas_call(
        run,
        in_specs=[SMEM] * scalars + [VMEM] * (len(operands) - scalars) + [ANY] * many,
        out_specs=[VMEM] * len(out),
        out_shape=list(out),
        compiler_params=pltpu.CompilerParams(vmem_limit_bytes=limit * MIB),
        cost_estimate=cost(flops, moved),
        name=name,
    )(*operands, *after)


def lane_mask(length, cols):
    return (lax.broadcasted_iota(jnp.int32, (1, cols), 1) < length).astype(F32)


def put_shards(me, acc, outs):
    shards = acc.shape[1]
    for j in range(shards):
        out = outs[j % len(outs)]
        out[j // len(outs)] = acc[:, me ^ j].astype(out.dtype)


def query_key_kernel(lengths, me, sheet, wq, wk, qk, *rest):
    outs, wt, acc = rest[:-2], rest[-2], rest[-1]
    step = pl.program_id(0)
    rows, cols, _ = sheet.shape
    local = wq.shape[0]
    heads = local // HEAD_DIM

    @pl.when(step == 0)
    def _():
        wt[:local] = wq[...]
        wt[local:] = wk[...]
        acc[...] = jnp.zeros_like(acc)

    for r in range(rows):
        mask = lane_mask(lengths[step * rows + r], cols)
        value = (mm(wt[...], sheet[r], NT) * mask).astype(BF16)
        qk[r] = value.reshape(2 * heads, HEAD_DIM, cols)
    flat = (rows * HEAD_DIM, cols)
    for h in range(heads):
        term = mm(qk[:, h].reshape(flat), qk[:, heads + h].reshape(flat), TN)
        acc[h] += term.reshape(acc.shape[1:])

    @pl.when(step == pl.num_programs(0) - 1)
    def _():
        put_shards(me[0], acc, outs)


def value_kernel(lengths, me, sheet, wq, wk, wv, cot, natural, *rest):
    outs, turned, acc = rest[:-2], rest[-2], rest[-1]
    step = pl.program_id(0)
    rows, cols, _ = sheet.shape
    local = wq.shape[0]
    heads = local // HEAD_DIM

    @pl.when(step == 0)
    def _():
        acc[...] = jnp.zeros_like(acc)
        for index, weight in enumerate((wq, wk, wv)):
            turned[:, :, index * local : (index + 1) * local] = weight[...].T.reshape(
                turned.shape[:2] + (local,)
            )
        for j in range(turned.shape[0]):
            natural[j] = turned[me[1] ^ j]

    values = []
    for r in range(rows):
        mask = lane_mask(lengths[step * rows + r], cols)
        value = (mm(wv[...], sheet[r], NT) * mask).astype(BF16)
        values.append(value.reshape(heads, HEAD_DIM, cols))
    flat = (rows * HEAD_DIM, cols)
    for h in range(heads):
        left = cot[:, h * HEAD_DIM : (h + 1) * HEAD_DIM].reshape(flat)
        right = jnp.concatenate([v[h] for v in values], axis=0)
        acc[h] += mm(left, right, TN).reshape(acc.shape[1:])

    @pl.when(step == pl.num_programs(0) - 1)
    def _():
        put_shards(me[0], acc, outs)


def part_shapes(shards, heads, cols):
    if shards == 1:
        return [like((1, heads, cols, cols), F32)]
    return [like((shards // 2, heads, cols // shards, cols))] * 2


def whole(shape):
    return pl.BlockSpec(shape, lambda s: (0,) * len(shape))


def query_key(lengths, me, sheet, wq, wk, shards, block):
    rows, cols, width = sheet.shape
    local = wq.shape[0]
    heads = local // HEAD_DIM
    outs = part_shapes(shards, heads, cols)
    return pl.pallas_call(
        query_key_kernel,
        grid=(rows // block,),
        in_specs=[
            SMEM,
            SMEM,
            pl.BlockSpec((block, cols, width), lambda s: (s, 0, 0)),
            whole(wq.shape),
            whole(wk.shape),
        ],
        out_specs=[pl.BlockSpec((block, 2 * heads, HEAD_DIM, cols), lambda s: (s, 0, 0, 0))]
        + [whole(o.shape) for o in outs],
        out_shape=[like((rows, 2 * heads, HEAD_DIM, cols))] + outs,
        scratch_shapes=[
            pltpu.VMEM((2 * local, width), BF16),
            pltpu.VMEM((heads, shards, cols // shards, cols), F32),
        ],
        compiler_params=pltpu.CompilerParams(vmem_limit_bytes=20 * MIB),
        cost_estimate=cost(2 * rows * cols * local * (2 * width + cols), 2 * rows * cols * (width + 2 * local)),
        name="query_key",
    )(lengths, me, sheet, wq, wk)


def value_dprob(lengths, me, sheet, wq, wk, wv, cot, shards, devices, block):
    rows, cols, width = sheet.shape
    local = wv.shape[0]
    heads = local // HEAD_DIM
    outs = part_shapes(shards, heads, cols)
    natural = (devices, width // devices, 3 * local)
    return pl.pallas_call(
        value_kernel,
        grid=(rows // block,),
        in_specs=[
            SMEM,
            SMEM,
            pl.BlockSpec((block, cols, width), lambda s: (s, 0, 0)),
            whole(wq.shape),
            whole(wk.shape),
            whole(wv.shape),
            pl.BlockSpec((block, local, cols), lambda s: (s, 0, 0)),
        ],
        out_specs=[whole(natural)] + [whole(o.shape) for o in outs],
        out_shape=[like(natural)] + outs,
        scratch_shapes=[
            pltpu.VMEM(natural, BF16),
            pltpu.VMEM((heads, shards, cols // shards, cols), F32),
        ],
        compiler_params=pltpu.CompilerParams(vmem_limit_bytes=20 * MIB),
        cost_estimate=cost(2 * rows * cols * local * (width + cols), 2 * rows * cols * (width + local)),
        name="value_dprob",
    )(lengths, me, sheet, wq, wk, wv, cot)


def add_split_kernel(keep, got, give_out, keep_out):
    for j in range(keep.shape[0]):
        total = (keep[j].astype(F32) + got[j].astype(F32)).astype(BF16)
        (give_out if j % 2 else keep_out)[j // 2] = total


def add_split(keep, got):
    half = like((keep.shape[0] // 2,) + keep.shape[1:])
    return in_vmem(add_split_kernel, "add_split", (half, half), keep, got)


def halve(keep, give, axis, bits):
    for bit in bits[:-1]:
        give, keep = add_split(keep, flip(give, axis, bit))
    return keep, flip(give, axis, bits[-1])


def softmax_kernel(scale, *refs):
    *terms, probs_out, dscore_out = refs
    half = len(terms) // 2
    total = lambda some: functools.reduce(jnp.add, [t[0].astype(F32) for t in some])
    logits = total(terms[:half]) * scale
    dprob = total(terms[half:])
    shifted = jnp.exp(logits - jnp.max(logits, axis=-1, keepdims=True))
    probs = shifted / jnp.sum(shifted, axis=-1, keepdims=True)
    inner = jnp.sum(probs * dprob, axis=-1, keepdims=True)
    probs_out[0] = probs.astype(BF16)
    dscore_out[0] = (scale * probs * (dprob - inner)).astype(BF16)


def softmax_back(logits, dprob, scale):
    out = like(logits[0].shape)
    return in_vmem(
        functools.partial(softmax_kernel, scale), "softmax_back", (out, out), *logits, *dprob, limit=16
    )


def double(values, axis, bits):
    order = [0]
    for bit in bits[:-1]:
        values = jnp.concatenate([values, flip(values, axis, bit)], axis=0)
        order = order + [j ^ bit for j in order]
    other = flip(values, axis, bits[-1])
    return (values, other), (order, [j ^ bits[-1] for j in order])


def assemble_kernel(orders, me, *refs):
    pieces, outs = refs[:-2], refs[-2:]
    per = len(orders)
    for kind, out in enumerate(outs):
        for piece, order in zip(pieces[kind * per : (kind + 1) * per], orders):
            for t, j in enumerate(order):
                out[me[0] ^ j] = piece[t]


def assemble(me, probs, dscore, orders, shards):
    out = like((shards,) + probs[0].shape[1:])
    return in_vmem(
        functools.partial(assemble_kernel, orders), "assemble", (out, out), me, *probs, *dscore, scalars=1
    )


def backward_kernel(first, lengths, probs, dscore, qk, cot, weights, *rest):
    blocks, grads = rest[:-1], rest[-1]
    count, all_heads, _, cols = grads.shape
    heads = all_heads // 3
    rows = pl.ds(first, count)
    flat = (count * HEAD_DIM, cols)
    split = (count, HEAD_DIM, cols)
    masks = jnp.stack([lane_mask(lengths[first + r], cols) for r in range(count)])
    for h in range(heads):
        p, ds = [ref[:, h].reshape(cols, cols) for ref in (probs, dscore)]
        g = cot[rows, h * HEAD_DIM : (h + 1) * HEAD_DIM].reshape(flat)
        dq = mm(qk[rows, heads + h].reshape(flat), ds, NT)
        dk = mm(qk[rows, h].reshape(flat), ds, NN)
        dv = mm(g, p, NN)
        for index, value in enumerate((dq, dk, dv)):
            grads[:, index * heads + h] = (value.reshape(split) * masks).astype(BF16)
    devices, share, columns = weights.shape
    left = weights[...].reshape(devices * share, columns)
    for r in range(count):
        part = mm(left, grads[r].reshape(columns, cols), NN).astype(BF16)
        for j in range(devices):
            blocks[j % 2][j // 2, r] = part[j * share : (j + 1) * share]


def backward(first, count, lengths, probs, dscore, qk, cot, weights, after):
    cols = qk.shape[-1]
    heads = qk.shape[1] // 2
    devices, share, columns = weights.shape
    half = like((devices // 2, count, share, cols))
    return in_vmem(
        functools.partial(backward_kernel, first),
        "backward",
        (half, half, like((count, 3 * heads, HEAD_DIM, cols))),
        lengths,
        probs,
        dscore,
        qk,
        cot,
        weights,
        scalars=1,
        after=after,
        limit=16,
        flops=2 * count * cols * columns * (cols + devices * share),
    )


def finish_kernel(keep, got, *rest):
    out = rest[-1]
    out[...] = (keep[0].astype(F32) + got[0].astype(F32)).astype(BF16)


def finish(keep, got, at, total_rows, before):
    _, count, share, cols = keep.shape
    spec = pl.BlockSpec(keep.shape, lambda s: (0, 0, 0, 0))
    extra = [] if before is None else [before]
    return pl.pallas_call(
        finish_kernel,
        grid=(1,),
        in_specs=[spec, spec] + [ANY] * len(extra),
        out_specs=pl.BlockSpec((count, share, cols), lambda s: (at, 0, 0)),
        out_shape=like((total_rows, share, cols)),
        input_output_aliases={2: 0} if extra else {},
        compiler_params=pltpu.CompilerParams(vmem_limit_bytes=12 * MIB),
        cost_estimate=cost(keep.size, keep.size * 6),
        name="finish",
    )(keep, got, *extra)


def weight_kernel(many, *refs):
    sheet, grads, out, acc = refs[0], refs[1 : 1 + many], refs[-2], refs[-1]
    step = pl.program_id(0)
    rows, cols, width = sheet.shape

    @pl.when(step == 0)
    def _():
        acc[...] = jnp.zeros_like(acc)

    for index, grad in enumerate(grads):
        @pl.when(step == index)
        def _():
            n = grad.shape[1] * HEAD_DIM
            left = jnp.concatenate([grad[r].reshape(n, cols) for r in range(rows)], axis=1)
            acc[...] += mm(left, sheet[...].reshape(rows * cols, width), NN)

    @pl.when(step == pl.num_programs(0) - 1)
    def _():
        out[...] = acc[...].T.reshape(out.shape).astype(out.dtype)


def weight_part(sheet, grads, shards, kind, after):
    rows, cols, width = sheet.shape
    many = len(grads)
    count = rows // many
    columns = grads[0].shape[1] * HEAD_DIM
    shape = (shards, width // shards, columns)
    return pl.pallas_call(
        functools.partial(weight_kernel, many),
        grid=(many,),
        in_specs=[pl.BlockSpec((count, cols, width), lambda s: (s, 0, 0))]
        + [VMEM] * many
        + [ANY] * len(after),
        out_specs=pl.BlockSpec(shape, lambda s: (0, 0, 0)),
        out_shape=like(shape, kind),
        scratch_shapes=[pltpu.VMEM((columns, width), F32)],
        compiler_params=pltpu.CompilerParams(vmem_limit_bytes=20 * MIB),
        cost_estimate=cost(2 * rows * cols * width * columns, 2 * rows * cols * (width + columns)),
        name="weight_part",
    )(sheet, *grads, *after)


def sum_kernel(got, out):
    total = jnp.sum(got[...].astype(F32), axis=0)
    local = out.shape[-1]
    for index in range(3):
        out[index] = total[:, index * local : (index + 1) * local]


def sum_parts(got, local):
    return in_vmem(sum_kernel, "sum_parts", (like((3, got.shape[1], local), F32),), got)[0]


def body(sheet, w_query, w_key, w_value, cotangent, lengths):
    row_dev, cols, width = sheet.shape
    local = w_query.shape[1]
    n_rows = lax.axis_size("rows")
    n_heads = lax.axis_size("heads")
    scale = float(1.0 / (HEAD_DIM * row_dev * n_rows) ** 0.5)
    direct = n_rows <= 8
    shards = n_rows if direct else 1
    row_bits = [1 << b for b in range(n_rows.bit_length() - 1)]
    chunk = 4

    me = jnp.stack([lax.axis_index("rows"), lax.axis_index("heads")]).astype(jnp.int32)
    wq, wk, wv = w_query.T, w_key.T, w_value.T
    cot = jnp.swapaxes(cotangent, 1, 2)

    qk, *logits = query_key(lengths, me, sheet, wq, wk, shards, 4)
    weights, *dprob = value_dprob(lengths, me, sheet, wq, wk, wv, cot, shards, n_heads, 4)
    if direct:
        logits = halve(*logits, "rows", row_bits)
        dprob = halve(*dprob, "rows", row_bits)
        probs_own, dscore_own = softmax_back(logits, dprob, scale)
        probs, orders = double(probs_own, "rows", row_bits[::-1])
        dscore, _ = double(dscore_own, "rows", row_bits[::-1])
        probs, dscore = assemble(me, probs, dscore, orders, shards)
    else:
        logits, dprob = lax.psum((logits, dprob), "rows")
        probs, dscore = softmax_back(logits, dprob, scale)

    grads, adds, last = [], [], []
    for first in range(0, row_dev, chunk):
        after = adds[-2:-1]
        keep, give, grad = backward(first, chunk, lengths, probs, dscore, qk, cot, weights, after)
        grads.append(grad)
        bit = 1
        while bit * 2 < n_heads:
            give, keep = add_split(keep, flip(give, "heads", bit))
            bit *= 2
        adds.append(keep)
        last.append((keep, flip(give, "heads", bit)))

    if direct:
        parts = weight_part(sheet, grads, shards, BF16, adds[-2:-1])
        weight_grad = sum_parts(lax.all_to_all(parts, "rows", 0, 0), local)
        weight_grad = jnp.swapaxes(weight_grad, 0, 1)
    else:
        parts = weight_part(sheet, grads, 1, F32, adds[-2:-1])[0]
        weight_grad = lax.psum_scatter(parts, "rows", scatter_dimension=0, tiled=True)
        weight_grad = weight_grad.reshape(width // n_rows, 3, local)

    out = None
    for index, (keep, got) in enumerate(last):
        out = finish(keep, got, index, row_dev, out)
    return (jnp.swapaxes(out, 1, 2), weight_grad)


def solution(mesh):
    in_specs = (
        P("rows", None, None),
        P(None, "heads"),
        P(None, "heads"),
        P(None, "heads"),
        P("rows", None, "heads"),
        P("rows"),
    )
    out_specs = (P("rows", None, "heads"), P("rows", None, "heads"))
    return jax.shard_map(body, mesh=mesh, in_specs=in_specs, out_specs=out_specs, check_vma=False)
```

time: 289 us -> 118 us (0.41)
  waiting for transfers between devices: 206 us -> 47.2 us
  matrix products: 45.6 us -> 0 us
  Pallas kernels: 0 us -> 30.3 us
  starting transfers between devices: 0.3 us -> 30.4 us
  between operations: 13.8 us -> 0.84 us
  local copies, waits for them, and re-layouts: 19.2 us -> 9.21 us
  other arithmetic: 3.3 us -> 0.1 us
    psum x1 -> x0, waiting for transfers between devices: 90.6 us -> none  [body(): logits, dprob = lax.psum((logit_part, dprob_part), 'rows')]
    reduce_scatter x1 -> x0, waiting for transfers between devices: 58.6 us -> none  [body(): lax.psum_scatter(input_part, 'heads', scatter_dimension=2, tiled=True)]
    unnamed x4 -> x0, waiting for transfers between devices: 57 us -> none
    ppermute x0 -> x20, waiting for transfers between devices: none -> 47.2 us  [flip(): return lax.ppermute(values, axis, [(s, s ^ bit) for s in range(n)])]
    dot_general x7 -> x0, matrix products: 40.6 us -> none  [the longest x1 9.24 us: body(): lax.dot_general(flat_grads, weights, (((1,), (1,)), ((), ())), preferred_...]
    pallas_call x0 -> x22, Pallas kernels: none -> 30.3 us  [the longest x15 11.8 us: in_vmem(): pl.pallas_call(run, in_specs=[SMEM] * scalars + [VMEM] * (len(operands) -...]
    ppermute x0 -> x20, starting transfers between devices: none -> 25 us  [flip(): return lax.ppermute(values, axis, [(s, s ^ bit) for s in range(n)])]
    transpose x3 -> x0, local copies, waits for them, and re-layouts: 6.58 us -> none  [the longest x1 2.27 us: body(): jnp.einsum('hij,rjhd->rihd', dscore, key, preferred_element_type=jnp.floa...]
  transfers between devices with their start and end apart: 3 -> 21, of which waited for: 3 -> 14; matrix products, arithmetic and copies ran while one was open for 4% -> 0% of each run, Pallas kernels for 0% -> 13%
where the time goes in v3:
time: 118 us
  waiting for transfers between devices  47.2 us (40%)
  starting transfers between devices  30.4 us (26%)
  Pallas kernels  30.3 us (26%)
  local copies, waits for them, and re-layouts  9.21 us (8%)
    ppermute x20, waiting for transfers between devices, flip(): return lax.ppermute(values, axis, [(s, s ^ bit) for s in range(n)])  47.2 us
    ppermute x20, starting transfers between devices, flip(): return lax.ppermute(values, axis, [(s, s ^ bit) for s in range(n)])  25 us
    pallas_call x15, Pallas kernels, in_vmem(): pl.pallas_call(run, in_specs=[SMEM] * scalars + [VMEM] * (len(operands) -...  11.8 us
    unnamed x29, local copies, waits for them, and re-layouts  9.2 us
    pallas_call x1, Pallas kernels, weight_part(): pl.pallas_call(functools.partial(weight_kernel, many), grid=(many,), in_s...  5.5 us
    all_to_all x1, starting transfers between devices, body(): weight_grad = sum_parts(lax.all_to_all(parts, 'rows', 0, 0), local)  5.44 us
    pallas_call x1, Pallas kernels, query_key(): pl.pallas_call(query_key_kernel, grid=(rows // block,), in_specs=[SMEM, S...  4.9 us
    pallas_call x1, Pallas kernels, value_dprob(): pl.pallas_call(value_kernel, grid=(rows // block,), in_specs=[SMEM, SMEM,...  4.78 us
  transfers between devices with their start and end apart: 21, of which 14 were waited for; matrix products, arithmetic and copies ran while one was open for 0% of the time, Pallas kernels for 13%

profile of v3, /device:TPU:0, one launch (start us, length us, event | category | flops | bytes accessed | tf_op | source)
XLA Modules:
  0.0 118.1 jit_solution(5183102608643763987)
XLA Ops:
  2.1 2.8 %copy-done.2 = bf16[16,256,768]{2,1,0:T(8,128)(2,1)S(1)} copy-done((bf16[16,256,768]{2,1,0:T(8,128)(2,1)S(1)}, bf16[16,256,768]{2,1,0:T(8,128)(2,1)}, u32[]{:S(2)}) %copy-start.2) | copy-done | bytes 6291480
  8.4 4.8 %value_dprob.1 = (bf16[4,192,576]{2,1,0:T(8,128)(2,1)S(1)}, bf16[4,3,32,256]{3,2,1,0:T(8,128)(2,1)S(1)}, bf16[4,3,32,256]{3,2,1,0:T(8,128)(2,1)S(1)}) custom-call(s32[16]{0:T(128)S(1)} %copy-done.6, s32[2]{0:T(128)S(1)} %pad_add_fusion.me.refs_0_, bf16[16,256,768]{2,1,0:T(8,128)(2,1)S(1)} %copy-done.2, bf16[192,768]{1,0:T(8,128)(2,1)S(1)} %bitcast.16, ...), custom_call_target="tpu_custom_call" | custom-call | flops 1610612736 | bytes 7864320 | tf_op jit(solution)/shard_map/value_dprob/pallas_call | solution.py:175
  13.2 3.0 %collective-permute-start.3 = (bf16[4,3,32,256]{3,2,1,0:T(8,128)(2,1)S(1)}, bf16[4,3,32,256]{3,2,1,0:T(8,128)(2,1)S(1)}, u32[]{:S(2)}, u32[]{:S(2)}) collective-permute-start(bf16[4,3,32,256]{3,2,1,0:T(8,128)(2,1)S(1)} %get-tuple-element.47), channel_id=1, source_target_pairs={{0,4},{4,0},{8,12},{12,8},{16,20},{20,16},{24,28},{28,24},{1,5},{5... | collective-permute-start | bytes 589832 | tf_op jit(solution)/shard_map/ppermute | solution.py:26
  16.2 4.9 %query_key.1 = (bf16[16,6,64,256]{3,2,1,0:T(8,128)(2,1)S(1)}, bf16[4,3,32,256]{3,2,1,0:T(8,128)(2,1)S(1)}, bf16[4,3,32,256]{3,2,1,0:T(8,128)(2,1)S(1)}) custom-call(s32[16]{0:T(128)S(1)} %copy-done.6, s32[2]{0:T(128)S(1)} %pad_add_fusion.me.refs_0_, bf16[16,256,768]{2,1,0:T(8,128)(2,1)S(1)} %copy-done.2, bf16[192,768]{1,0:T(8,128)(2,1)S(1)} %bitcast.17, ...), custom_call_target="tpu_custom_call" | custom-call | flops 2818572288 | bytes 9437184 | tf_op jit(solution)/shard_map/query_key/pallas_call | solution.py:146
  21.3 2.2 %collective-permute-start.4 = (bf16[2,3,32,256]{3,2,1,0:T(8,128)(2,1)S(1)}, bf16[2,3,32,256]{3,2,1,0:T(8,128)(2,1)S(1)}, u32[]{:S(2)}, u32[]{:S(2)}) collective-permute-start(bf16[2,3,32,256]{3,2,1,0:T(8,128)(2,1)S(1)} %get-tuple-element.49), channel_id=1, source_target_pairs={{0,8},{4,12},{8,0},{12,4},{16,24},{20,28},{24,16},{28,20},{1,9},{5... | collective-permute-start | bytes 294920 | tf_op jit(solution)/shard_map/ppermute | solution.py:26
  23.5 4.1 %collective-permute-done.refs_1_ = bf16[4,3,32,256]{3,2,1,0:T(8,128)(2,1)S(1)} collective-permute-done((bf16[4,3,32,256]{3,2,1,0:T(8,128)(2,1)S(1)}, bf16[4,3,32,256]{3,2,1,0:T(8,128)(2,1)S(1)}, u32[]{:S(2)}, u32[]{:S(2)}) %collective-permute-start) | collective-permute-done | bytes 196640 | tf_op jit(solution)/shard_map/ppermute | solution.py:26
  29.3 2.7 %collective-permute-start.5 = (bf16[1,3,32,256]{3,2,1,0:T(8,128)(2,1)S(1)}, bf16[1,3,32,256]{3,2,1,0:T(8,128)(2,1)S(1)}, u32[]{:S(2)}, u32[]{:S(2)}) collective-permute-start(bf16[1,3,32,256]{3,2,1,0:T(8,128)(2,1)S(1)} %get-tuple-element.51), channel_id=1, source_target_pairs={{0,16},{4,20},{8,24},{12,28},{16,0},{20,4},{24,8},{28,12},{1,17},{... | collective-permute-start | bytes 147464 | tf_op jit(solution)/shard_map/ppermute | solution.py:26
  32.9 2.1 %collective-permute-start.2 = (bf16[1,3,32,256]{3,2,1,0:T(8,128)(2,1)S(1)}, bf16[1,3,32,256]{3,2,1,0:T(8,128)(2,1)S(1)}, u32[]{:S(2)}, u32[]{:S(2)}) collective-permute-start(bf16[1,3,32,256]{3,2,1,0:T(8,128)(2,1)S(1)} %get-tuple-element.45), channel_id=1, source_target_pairs={{0,16},{4,20},{8,24},{12,28},{16,0},{20,4},{24,8},{28,12},{1,17},{... | collective-permute-start | bytes 147464 | tf_op jit(solution)/shard_map/ppermute | solution.py:26
  35.8 2.2 %collective-permute-done.2.refs_1_ = bf16[1,3,32,256]{3,2,1,0:T(8,128)(2,1)S(1)} collective-permute-done((bf16[1,3,32,256]{3,2,1,0:T(8,128)(2,1)S(1)}, bf16[1,3,32,256]{3,2,1,0:T(8,128)(2,1)S(1)}, u32[]{:S(2)}, u32[]{:S(2)}) %collective-permute-start.2) | collective-permute-done | bytes 49184 | tf_op jit(solution)/shard_map/ppermute | solution.py:26
  38.2 2.2 %collective-permute-start.9 = (bf16[1,3,32,256]{3,2,1,0:T(8,128)(2,1)S(1)}, bf16[1,3,32,256]{3,2,1,0:T(8,128)(2,1)S(1)}, u32[]{:S(2)}, u32[]{:S(2)}) collective-permute-start(bf16[1,3,32,256]{3,2,1,0:T(8,128)(2,1)S(1)} %get-tuple-element.53), channel_id=1, source_target_pairs={{0,16},{4,20},{8,24},{12,28},{16,0},{20,4},{24,8},{28,12},{1,17},{... | collective-permute-start | bytes 147464 | tf_op jit(solution)/shard_map/ppermute | solution.py:26
  41.2 2.0 %collective-permute-done.9 = bf16[1,3,32,256]{3,2,1,0:T(8,128)(2,1)S(1)} collective-permute-done((bf16[1,3,32,256]{3,2,1,0:T(8,128)(2,1)S(1)}, bf16[1,3,32,256]{3,2,1,0:T(8,128)(2,1)S(1)}, u32[]{:S(2)}, u32[]{:S(2)}) %collective-permute-start.9) | collective-permute-done | bytes 49184 | tf_op jit(solution)/shard_map/ppermute | solution.py:26
  43.3 2.2 %collective-permute-start.10 = (bf16[2,3,32,256]{3,2,1,0:T(8,128)(2,1)S(1)}, bf16[2,3,32,256]{3,2,1,0:T(8,128)(2,1)S(1)}, u32[]{:S(2)}, u32[]{:S(2)}) collective-permute-start(bf16[2,3,32,256]{3,2,1,0:T(8,128)(2,1)S(1)} %pad_maximum_fusion.1), channel_id=1, source_target_pairs={{0,8},{4,12},{8,0},{12,4},{16,24},{20,28},{24,16},{28,20},{1,9},{5... | collective-permute-start | bytes 294920 | tf_op jit(solution)/shard_map/ppermute | solution.py:26
  50.8 2.9 %collective-permute-done.11.refs_4_ = bf16[4,3,32,256]{3,2,1,0:T(8,128)(2,1)S(1)} collective-permute-done((bf16[4,3,32,256]{3,2,1,0:T(8,128)(2,1)S(1)}, bf16[4,3,32,256]{3,2,1,0:T(8,128)(2,1)S(1)}, u32[]{:S(2)}, u32[]{:S(2)}) %collective-permute-start.11) | collective-permute-done | bytes 196640 | tf_op jit(solution)/shard_map/ppermute | solution.py:26
  53.8 2.2 %collective-permute-done.8.refs_2_ = bf16[4,3,32,256]{3,2,1,0:T(8,128)(2,1)S(1)} collective-permute-done((bf16[4,3,32,256]{3,2,1,0:T(8,128)(2,1)S(1)}, bf16[4,3,32,256]{3,2,1,0:T(8,128)(2,1)S(1)}, u32[]{:S(2)}, u32[]{:S(2)}) %collective-permute-start.8) | collective-permute-done | bytes 196640 | tf_op jit(solution)/shard_map/ppermute | solution.py:26
  56.6 2.3 %backward.6 = (bf16[2,4,192,256]{3,2,1,0:T(8,128)(2,1)S(1)}, bf16[2,4,192,256]{3,2,1,0:T(8,128)(2,1)S(1)}, bf16[4,9,64,256]{3,2,1,0:T(8,128)(2,1)S(1)}) custom-call(s32[16]{0:T(128)S(1)} %copy-done.6, bf16[8,3,32,256]{3,2,1,0:T(8,128)(2,1)S(1)} %get-tuple-element.54.refs_1_, bf16[8,3,32,256]{3,2,1,0:T(8,128)(2,1)S(1)} %get-tuple-element.55.refs_2_, ...), custom_call_target="tpu_custom_call" | custom-call | flops 1207959552 | bytes 9142304 | tf_op jit(solution)/shard_map/backward/pallas_call | solution.py:49
  59.0 2.3 %backward.4 = (bf16[2,4,192,256]{3,2,1,0:T(8,128)(2,1)S(1)}, bf16[2,4,192,256]{3,2,1,0:T(8,128)(2,1)S(1)}, bf16[4,9,64,256]{3,2,1,0:T(8,128)(2,1)S(1)}) custom-call(s32[16]{0:T(128)S(1)} %copy-done.7, bf16[8,3,32,256]{3,2,1,0:T(8,128)(2,1)S(1)} %get-tuple-element.54.refs_1_, bf16[8,3,32,256]{3,2,1,0:T(8,128)(2,1)S(1)} %get-tuple-element.55.refs_2_, ...), custom_call_target="tpu_custom_call" | custom-call | flops 1207959552 | bytes 9142304 | tf_op jit(solution)/shard_map/backward/pallas_call | solution.py:49
  62.0 2.3 %backward.7 = (bf16[2,4,192,256]{3,2,1,0:T(8,128)(2,1)S(1)}, bf16[2,4,192,256]{3,2,1,0:T(8,128)(2,1)S(1)}, bf16[4,9,64,256]{3,2,1,0:T(8,128)(2,1)S(1)}) custom-call(s32[16]{0:T(128)S(1)} %copy-done.7, bf16[8,3,32,256]{3,2,1,0:T(8,128)(2,1)S(1)} %get-tuple-element.54.refs_1_, bf16[8,3,32,256]{3,2,1,0:T(8,128)(2,1)S(1)} %get-tuple-element.55.refs_2_, ...), custom_call_target="tpu_custom_call" | custom-call | flops 1207959552 | bytes 9142304 | tf_op jit(solution)/shard_map/backward/pallas_call | solution.py:49
  64.6 2.3 %backward.5 = (bf16[2,4,192,256]{3,2,1,0:T(8,128)(2,1)S(1)}, bf16[2,4,192,256]{3,2,1,0:T(8,128)(2,1)S(1)}, bf16[4,9,64,256]{3,2,1,0:T(8,128)(2,1)S(1)}) custom-call(s32[16]{0:T(128)S(1)} %copy-done.7, bf16[8,3,32,256]{3,2,1,0:T(8,128)(2,1)S(1)} %get-tuple-element.54.refs_1_, bf16[8,3,32,256]{3,2,1,0:T(8,128)(2,1)S(1)} %get-tuple-element.55.refs_2_, ...), custom_call_target="tpu_custom_call" | custom-call | flops 1207959552 | bytes 9142304 | tf_op jit(solution)/shard_map/backward/pallas_call | solution.py:49
  68.6 5.5 %weight_part.1 = bf16[8,96,576]{2,1,0:T(8,128)(2,1)} custom-call(bf16[16,256,768]{2,1,0:T(8,128)(2,1)S(1)} %bitcast.14, bf16[4,9,64,256]{3,2,1,0:T(8,128)(2,1)S(1)} %get-tuple-element.74.refs_1_, bf16[4,9,64,256]{3,2,1,0:T(8,128)(2,1)S(1)} %get-tuple-element.75.refs_2_, bf16[4,9,64,256]{3,2,1,0:T(8,128)(2,1)S(1)} %get-tuple-element.76.refs_3_, ...), custom_call_target="tpu_custom_call" | custom-call | flops 3623878656 | bytes 11010048 | tf_op jit(solution)/shard_map/weight_part/pallas_call | solution.py:356
  74.1 5.4 %all-to-all-start = ((bf16[8,96,576]{2,1,0:T(8,128)(2,1)}), bf16[8,96,576]{2,1,0:T(8,128)(2,1)S(1)}, u32[]{:S(2)}, u32[]{:S(2)}) async-start(bf16[8,96,576]{2,1,0:T(8,128)(2,1)} %weight_part.1), calls=%async_computation | async-start | bytes 1966080 | tf_op jit(solution)/shard_map/all_to_all | solution.py:424
  84.0 7.6 %collective-permute-done.19.got = bf16[1,4,192,256]{3,2,1,0:T(8,128)(2,1)S(1)} collective-permute-done((bf16[1,4,192,256]{3,2,1,0:T(8,128)(2,1)S(1)}, bf16[1,4,192,256]{3,2,1,0:T(8,128)(2,1)S(1)}, u32[]{:S(2)}, u32[]{:S(2)}) %collective-permute-start.19) | collective-permute-done | bytes 393248 | tf_op jit(solution)/shard_map/ppermute | solution.py:26
  92.5 7.6 %collective-permute-done.18.got = bf16[1,4,192,256]{3,2,1,0:T(8,128)(2,1)S(1)} collective-permute-done((bf16[1,4,192,256]{3,2,1,0:T(8,128)(2,1)}, bf16[1,4,192,256]{3,2,1,0:T(8,128)(2,1)S(1)}, u32[]{:S(2)}, u32[]{:S(2)}) %collective-permute-start.18) | collective-permute-done | bytes 393248 | tf_op jit(solution)/shard_map/ppermute | solution.py:26
  100.9 7.6 %collective-permute-done.17.got = bf16[1,4,192,256]{3,2,1,0:T(8,128)(2,1)S(1)} collective-permute-done((bf16[1,4,192,256]{3,2,1,0:T(8,128)(2,1)}, bf16[1,4,192,256]{3,2,1,0:T(8,128)(2,1)S(1)}, u32[]{:S(2)}, u32[]{:S(2)}) %collective-permute-start.17) | collective-permute-done | bytes 393248 | tf_op jit(solution)/shard_map/ppermute | solution.py:26
  109.3 7.0 %collective-permute-done.14.got = bf16[1,4,192,256]{3,2,1,0:T(8,128)(2,1)S(1)} collective-permute-done((bf16[1,4,192,256]{3,2,1,0:T(8,128)(2,1)S(1)}, bf16[1,4,192,256]{3,2,1,0:T(8,128)(2,1)S(1)}, u32[]{:S(2)}, u32[]{:S(2)}) %collective-permute-start.14) | collective-permute-done | bytes 393248 | tf_op jit(solution)/shard_map/ppermute | solution.py:26
  (75 shorter events, 27.1 us)
Async XLA Ops:
  13.2 8.0 %collective-permute-start.3 = (bf16[4,3,32,256]{3,2,1,0:T(8,128)(2,1)S(1)}, bf16[4,3,32,256]{3,2,1,0:T(8,128)(2,1)S(1)}, u32[]{:S(2)}, u32[]{:S(2)}) collective-permute-start(bf16[4,3,32,256]{3,2,1,0:T(8,128)(2,1)S(1)} %get-tuple-element.47), channel_id=1, source_target_pairs={{0,4},{4,0},{8,12},{12,8},{16,20},{20,16},{24,28},{28,24},{1,5},{5... | collective-permute-start | bytes 589832 | tf_op jit(solution)/shard_map/ppermute | solution.py:26
  21.1 6.4 %collective-permute-start = (bf16[4,3,32,256]{3,2,1,0:T(8,128)(2,1)S(1)}, bf16[4,3,32,256]{3,2,1,0:T(8,128)(2,1)S(1)}, u32[]{:S(2)}, u32[]{:S(2)}) collective-permute-start(bf16[4,3,32,256]{3,2,1,0:T(8,128)(2,1)S(1)} %get-tuple-element.41), channel_id=1, source_target_pairs={{0,4},{4,0},{8,12},{12,8},{16,20},{20,16},{24,28},{28,24},{1,5},{5... | collective-permute-start | bytes 589832 | tf_op jit(solution)/shard_map/ppermute | solution.py:26
  21.3 35.3 %copy-start.1 = (bf16[16,256,192]{1,2,0:T(8,128)(2,1)S(1)}, bf16[16,256,192]{1,2,0:T(8,128)(2,1)}, u32[]{:S(2)}) copy-start(bf16[16,256,192]{1,2,0:T(8,128)(2,1)} %param.10) | copy-start | bytes 4718596
  21.3 8.0 %collective-permute-start.4 = (bf16[2,3,32,256]{3,2,1,0:T(8,128)(2,1)S(1)}, bf16[2,3,32,256]{3,2,1,0:T(8,128)(2,1)S(1)}, u32[]{:S(2)}, u32[]{:S(2)}) collective-permute-start(bf16[2,3,32,256]{3,2,1,0:T(8,128)(2,1)S(1)} %get-tuple-element.49), channel_id=1, source_target_pairs={{0,8},{4,12},{8,0},{12,4},{16,24},{20,28},{24,16},{28,20},{1,9},{5... | collective-permute-start | bytes 294920 | tf_op jit(solution)/shard_map/ppermute | solution.py:26
  27.6 5.2 %collective-permute-start.1 = (bf16[2,3,32,256]{3,2,1,0:T(8,128)(2,1)S(1)}, bf16[2,3,32,256]{3,2,1,0:T(8,128)(2,1)S(1)}, u32[]{:S(2)}, u32[]{:S(2)}) collective-permute-start(bf16[2,3,32,256]{3,2,1,0:T(8,128)(2,1)S(1)} %get-tuple-element.43), channel_id=1, source_target_pairs={{0,8},{4,12},{8,0},{12,4},{16,24},{20,28},{24,16},{28,20},{1,9},{5... | collective-permute-start | bytes 294920 | tf_op jit(solution)/shard_map/ppermute | solution.py:26
  29.3 6.4 %collective-permute-start.5 = (bf16[1,3,32,256]{3,2,1,0:T(8,128)(2,1)S(1)}, bf16[1,3,32,256]{3,2,1,0:T(8,128)(2,1)S(1)}, u32[]{:S(2)}, u32[]{:S(2)}) collective-permute-start(bf16[1,3,32,256]{3,2,1,0:T(8,128)(2,1)S(1)} %get-tuple-element.51), channel_id=1, source_target_pairs={{0,16},{4,20},{8,24},{12,28},{16,0},{20,4},{24,8},{28,12},{1,17},{... | collective-permute-start | bytes 147464 | tf_op jit(solution)/shard_map/ppermute | solution.py:26
  32.9 5.1 %collective-permute-start.2 = (bf16[1,3,32,256]{3,2,1,0:T(8,128)(2,1)S(1)}, bf16[1,3,32,256]{3,2,1,0:T(8,128)(2,1)S(1)}, u32[]{:S(2)}, u32[]{:S(2)}) collective-permute-start(bf16[1,3,32,256]{3,2,1,0:T(8,128)(2,1)S(1)} %get-tuple-element.45), channel_id=1, source_target_pairs={{0,16},{4,20},{8,24},{12,28},{16,0},{20,4},{24,8},{28,12},{1,17},{... | collective-permute-start | bytes 147464 | tf_op jit(solution)/shard_map/ppermute | solution.py:26
  38.2 5.1 %collective-permute-start.9 = (bf16[1,3,32,256]{3,2,1,0:T(8,128)(2,1)S(1)}, bf16[1,3,32,256]{3,2,1,0:T(8,128)(2,1)S(1)}, u32[]{:S(2)}, u32[]{:S(2)}) collective-permute-start(bf16[1,3,32,256]{3,2,1,0:T(8,128)(2,1)S(1)} %get-tuple-element.53), channel_id=1, source_target_pairs={{0,16},{4,20},{8,24},{12,28},{16,0},{20,4},{24,8},{28,12},{1,17},{... | collective-permute-start | bytes 147464 | tf_op jit(solution)/shard_map/ppermute | solution.py:26
  40.4 5.2 %collective-permute-start.6 = (bf16[1,3,32,256]{3,2,1,0:T(8,128)(2,1)S(1)}, bf16[1,3,32,256]{3,2,1,0:T(8,128)(2,1)S(1)}, u32[]{:S(2)}, u32[]{:S(2)}) collective-permute-start(bf16[1,3,32,256]{3,2,1,0:T(8,128)(2,1)S(1)} %get-tuple-element.52), channel_id=1, source_target_pairs={{0,16},{4,20},{8,24},{12,28},{16,0},{20,4},{24,8},{28,12},{1,17},{... | collective-permute-start | bytes 147464 | tf_op jit(solution)/shard_map/ppermute | solution.py:26
  43.3 4.8 %collective-permute-start.10 = (bf16[2,3,32,256]{3,2,1,0:T(8,128)(2,1)S(1)}, bf16[2,3,32,256]{3,2,1,0:T(8,128)(2,1)S(1)}, u32[]{:S(2)}, u32[]{:S(2)}) collective-permute-start(bf16[2,3,32,256]{3,2,1,0:T(8,128)(2,1)S(1)} %pad_maximum_fusion.1), channel_id=1, source_target_pairs={{0,8},{4,12},{8,0},{12,4},{16,24},{20,28},{24,16},{28,20},{1,9},{5... | collective-permute-start | bytes 294920 | tf_op jit(solution)/shard_map/ppermute | solution.py:26
  45.6 4.7 %collective-permute-start.7 = (bf16[2,3,32,256]{3,2,1,0:T(8,128)(2,1)S(1)}, bf16[2,3,32,256]{3,2,1,0:T(8,128)(2,1)S(1)}, u32[]{:S(2)}, u32[]{:S(2)}) collective-permute-start(bf16[2,3,32,256]{3,2,1,0:T(8,128)(2,1)S(1)} %pad_maximum_fusion), channel_id=1, source_target_pairs={{0,8},{4,12},{8,0},{12,4},{16,24},{20,28},{24,16},{28,20},{1,9},{5... | collective-permute-start | bytes 294920 | tf_op jit(solution)/shard_map/ppermute | solution.py:26
  48.0 5.7 %collective-permute-start.11 = (bf16[4,3,32,256]{3,2,1,0:T(8,128)(2,1)S(1)}, bf16[4,3,32,256]{3,2,1,0:T(8,128)(2,1)S(1)}, u32[]{:S(2)}, u32[]{:S(2)}) collective-permute-start(bf16[4,3,32,256]{3,2,1,0:T(8,128)(2,1)S(1)} %constant_dynamic-update-slice_fusion.3.refs_3_), channel_id=1, source_target_pairs={{0,4},{4,0},{8,12},{12,8},{16,20},{20,16},{24,28},{28,24},{1,5},{5... | collective-permute-start | bytes 589832 | tf_op jit(solution)/shard_map/ppermute | solution.py:26
  50.2 5.7 %collective-permute-start.8 = (bf16[4,3,32,256]{3,2,1,0:T(8,128)(2,1)S(1)}, bf16[4,3,32,256]{3,2,1,0:T(8,128)(2,1)S(1)}, u32[]{:S(2)}, u32[]{:S(2)}) collective-permute-start(bf16[4,3,32,256]{3,2,1,0:T(8,128)(2,1)S(1)} %constant_dynamic-update-slice_fusion.refs_1_), channel_id=1, source_target_pairs={{0,4},{4,0},{8,12},{12,8},{16,20},{20,16},{24,28},{28,24},{1,5},{5... | collective-permute-start | bytes 589832 | tf_op jit(solution)/shard_map/ppermute | solution.py:26
  58.9 2.9 %collective-permute-start.15 = (bf16[2,4,192,256]{3,2,1,0:T(8,128)(2,1)S(1)}, bf16[2,4,192,256]{3,2,1,0:T(8,128)(2,1)S(1)}, u32[]{:S(2)}, u32[]{:S(2)}) collective-permute-start(bf16[2,4,192,256]{3,2,1,0:T(8,128)(2,1)S(1)} %get-tuple-element.66), channel_id=1, source_target_pairs={{0,1},{1,0},{2,3},{3,2},{4,5},{5,4},{6,7},{7,6},{8,9},{9,8},{10,11... | collective-permute-start | bytes 2359304 | tf_op jit(solution)/shard_map/ppermute | solution.py:26
  61.3 3.2 %collective-permute-start.12 = (bf16[2,4,192,256]{3,2,1,0:T(8,128)(2,1)S(1)}, bf16[2,4,192,256]{3,2,1,0:T(8,128)(2,1)S(1)}, u32[]{:S(2)}, u32[]{:S(2)}) collective-permute-start(bf16[2,4,192,256]{3,2,1,0:T(8,128)(2,1)S(1)} %get-tuple-element.59), channel_id=1, source_target_pairs={{0,1},{1,0},{2,3},{3,2},{4,5},{5,4},{6,7},{7,6},{8,9},{9,8},{10,11... | collective-permute-start | bytes 2359304 | tf_op jit(solution)/shard_map/ppermute | solution.py:26
  62.0 6.5 %slice-start = ((s8[6291456]{0:T(1024)(128)(4,1)}), s8[4194304]{0:T(1024)(128)(4,1)S(1)}, s32[]{:S(2)}) async-start(s8[6291456]{0:T(1024)(128)(4,1)} %bitcast.13), calls=%async_computation.1 | async-start | bytes 8388608
  64.3 2.6 %collective-permute-start.16 = (bf16[2,4,192,256]{3,2,1,0:T(8,128)(2,1)S(1)}, bf16[2,4,192,256]{3,2,1,0:T(8,128)(2,1)S(1)}, u32[]{:S(2)}, u32[]{:S(2)}) collective-permute-start(bf16[2,4,192,256]{3,2,1,0:T(8,128)(2,1)S(1)} %get-tuple-element.69), channel_id=1, source_target_pairs={{0,1},{1,0},{2,3},{3,2},{4,5},{5,4},{6,7},{7,6},{8,9},{9,8},{10,11... | collective-permute-start | bytes 2359304 | tf_op jit(solution)/shard_map/ppermute | solution.py:26
  64.6 3.9 %slice-start.1 = ((s8[6291456]{0:T(1024)(128)(4,1)}), s8[2097152]{0:T(1024)(128)(4,1)S(1)}, s32[]{:S(2)}) async-start(s8[6291456]{0:T(1024)(128)(4,1)} %bitcast.13), calls=%async_computation.2 | async-start | bytes 4194304
  74.1 43.1 %all-to-all-start = ((bf16[8,96,576]{2,1,0:T(8,128)(2,1)}), bf16[8,96,576]{2,1,0:T(8,128)(2,1)S(1)}, u32[]{:S(2)}, u32[]{:S(2)}) async-start(bf16[8,96,576]{2,1,0:T(8,128)(2,1)} %weight_part.1), calls=%async_computation | async-start | bytes 1966080 | tf_op jit(solution)/shard_map/all_to_all | solution.py:424
  79.5 3.8 %collective-permute-start.13 = (bf16[2,4,192,256]{3,2,1,0:T(8,128)(2,1)}, bf16[2,4,192,256]{3,2,1,0:T(8,128)(2,1)S(1)}, u32[]{:S(2)}, u32[]{:S(2)}) collective-permute-start(bf16[2,4,192,256]{3,2,1,0:T(8,128)(2,1)} %copy-done.8), channel_id=1, source_target_pairs={{0,1},{1,0},{2,3},{3,2},{4,5},{5,4},{6,7},{7,6},{8,9},{9,8},{10,11... | collective-permute-start | bytes 2359304 | tf_op jit(solution)/shard_map/ppermute | solution.py:26
  79.7 11.9 %collective-permute-start.19 = (bf16[1,4,192,256]{3,2,1,0:T(8,128)(2,1)S(1)}, bf16[1,4,192,256]{3,2,1,0:T(8,128)(2,1)S(1)}, u32[]{:S(2)}, u32[]{:S(2)}) collective-permute-start(bf16[1,4,192,256]{3,2,1,0:T(8,128)(2,1)S(1)} %get-tuple-element.73), channel_id=1, source_target_pairs={{0,2},{1,3},{2,0},{3,1},{4,6},{5,7},{6,4},{7,5},{8,10},{9,11},{10,... | collective-permute-start | bytes 1179656 | tf_op jit(solution)/shard_map/ppermute | solution.py:26
  81.3 18.8 %collective-permute-start.18 = (bf16[1,4,192,256]{3,2,1,0:T(8,128)(2,1)}, bf16[1,4,192,256]{3,2,1,0:T(8,128)(2,1)S(1)}, u32[]{:S(2)}, u32[]{:S(2)}) collective-permute-start(bf16[1,4,192,256]{3,2,1,0:T(8,128)(2,1)} %copy-done.9), channel_id=1, source_target_pairs={{0,2},{1,3},{2,0},{3,1},{4,6},{5,7},{6,4},{7,5},{8,10},{9,11},{10,... | collective-permute-start | bytes 1179656 | tf_op jit(solution)/shard_map/ppermute | solution.py:26
  81.7 26.8 %collective-permute-start.17 = (bf16[1,4,192,256]{3,2,1,0:T(8,128)(2,1)}, bf16[1,4,192,256]{3,2,1,0:T(8,128)(2,1)S(1)}, u32[]{:S(2)}, u32[]{:S(2)}) collective-permute-start(bf16[1,4,192,256]{3,2,1,0:T(8,128)(2,1)} %copy-done.10), channel_id=1, source_target_pairs={{0,2},{1,3},{2,0},{3,1},{4,6},{5,7},{6,4},{7,5},{8,10},{9,11},{10,... | collective-permute-start | bytes 1179656 | tf_op jit(solution)/shard_map/ppermute | solution.py:26
  83.5 32.8 %collective-permute-start.14 = (bf16[1,4,192,256]{3,2,1,0:T(8,128)(2,1)S(1)}, bf16[1,4,192,256]{3,2,1,0:T(8,128)(2,1)S(1)}, u32[]{:S(2)}, u32[]{:S(2)}) collective-permute-start(bf16[1,4,192,256]{3,2,1,0:T(8,128)(2,1)S(1)} %get-tuple-element.64), channel_id=1, source_target_pairs={{0,2},{1,3},{2,0},{3,1},{4,6},{5,7},{6,4},{7,5},{8,10},{9,11},{10,... | collective-permute-start | bytes 1179656 | tf_op jit(solution)/shard_map/ppermute | solution.py:26
  (10 other events, 15.0 us)

commit v4 on v3

--- a/solution.py
+++ b/solution.py
@@ -1,4 +1,5 @@
 import functools
+import math
 
 import jax
 import jax.numpy as jnp
@@ -27,7 +28,7 @@
 
 
 def cost(flops, moved):
-    return pl.CostEstimate(flops=int(flops), bytes_accessed=int(moved), transcendentals=0)
+    return pl.CostEstimate(flops=int(flops) // 64, bytes_accessed=int(moved) // 64, transcendentals=0)
 
 
 SMEM = pl.BlockSpec(memory_space=pltpu.SMEM)
@@ -95,7 +96,7 @@
         put_shards(me[0], acc, outs)
 
 
-def value_kernel(lengths, me, sheet, wq, wk, wv, cot, natural, *rest):
+def value_kernel(lengths, me, sheet, wq, wk, wv, cot, _, natural, *rest):
     outs, turned, acc = rest[:-2], rest[-2], rest[-1]
     step = pl.program_id(0)
     rows, cols, _ = sheet.shape
@@ -131,7 +132,8 @@
 def part_shapes(shards, heads, cols):
     if shards == 1:
         return [like((1, heads, cols, cols), F32)]
-    return [like((shards // 2, heads, cols // shards, cols))] * 2
+    half = (shards // 2, heads, cols // shards, cols)
+    return [like(half, F32), like(half)]
 
 
 def whole(shape):
@@ -160,13 +162,13 @@
             pltpu.VMEM((2 * local, width), BF16),
             pltpu.VMEM((heads, shards, cols // shards, cols), F32),
         ],
-        compiler_params=pltpu.CompilerParams(vmem_limit_bytes=20 * MIB),
+        compiler_params=pltpu.CompilerParams(vmem_limit_bytes=56 * MIB),
         cost_estimate=cost(2 * rows * cols * local * (2 * width + cols), 2 * rows * cols * (width + 2 * local)),
         name="query_key",
     )(lengths, me, sheet, wq, wk)
 
 
-def value_dprob(lengths, me, sheet, wq, wk, wv, cot, shards, devices, block):
+def value_dprob(lengths, me, sheet, wq, wk, wv, cot, after, shards, devices, block):
     rows, cols, width = sheet.shape
     local = wv.shape[0]
     heads = local // HEAD_DIM
@@ -183,6 +185,7 @@
             whole(wk.shape),
             whole(wv.shape),
             pl.BlockSpec((block, local, cols), lambda s: (s, 0, 0)),
+            ANY,
         ],
         out_specs=[whole(natural)] + [whole(o.shape) for o in outs],
         out_shape=[like(natural)] + outs,
@@ -190,21 +193,22 @@
             pltpu.VMEM(natural, BF16),
             pltpu.VMEM((heads, shards, cols // shards, cols), F32),
         ],
-        compiler_params=pltpu.CompilerParams(vmem_limit_bytes=20 * MIB),
+        compiler_params=pltpu.CompilerParams(vmem_limit_bytes=56 * MIB),
         cost_estimate=cost(2 * rows * cols * local * (width + cols), 2 * rows * cols * (width + local)),
         name="value_dprob",
-    )(lengths, me, sheet, wq, wk, wv, cot)
+    )(lengths, me, sheet, wq, wk, wv, cot, after)
 
 
 def add_split_kernel(keep, got, give_out, keep_out):
     for j in range(keep.shape[0]):
-        total = (keep[j].astype(F32) + got[j].astype(F32)).astype(BF16)
-        (give_out if j % 2 else keep_out)[j // 2] = total
+        total = keep[j].astype(F32) + got[j].astype(F32)
+        out = give_out if j % 2 else keep_out
+        out[j // 2] = total.astype(out.dtype)
 
 
 def add_split(keep, got):
-    half = like((keep.shape[0] // 2,) + keep.shape[1:])
-    return in_vmem(add_split_kernel, "add_split", (half, half), keep, got)
+    half = (keep.shape[0] // 2,) + keep.shape[1:]
+    return in_vmem(add_split_kernel, "add_split", (like(half), like(half, keep.dtype)), keep, got)
 
 
 def halve(keep, give, axis, bits):
@@ -309,15 +313,16 @@
     out[...] = (keep[0].astype(F32) + got[0].astype(F32)).astype(BF16)
 
 
-def finish(keep, got, at, total_rows, before):
+def finish(keep, got, first, total_rows, before):
     _, count, share, cols = keep.shape
-    spec = pl.BlockSpec(keep.shape, lambda s: (0, 0, 0, 0))
+    block = math.gcd(first, count) if first else count
+    spec = pl.BlockSpec((1, block, share, cols), lambda s: (0, s, 0, 0))
     extra = [] if before is None else [before]
     return pl.pallas_call(
         finish_kernel,
-        grid=(1,),
+        grid=(count // block,),
         in_specs=[spec, spec] + [ANY] * len(extra),
-        out_specs=pl.BlockSpec((count, share, cols), lambda s: (at, 0, 0)),
+        out_specs=pl.BlockSpec((block, share, cols), lambda s: (first // block + s, 0, 0)),
         out_shape=like((total_rows, share, cols)),
         input_output_aliases={2: 0} if extra else {},
         compiler_params=pltpu.CompilerParams(vmem_limit_bytes=12 * MIB),
@@ -326,46 +331,29 @@
     )(keep, got, *extra)
 
 
-def weight_kernel(many, *refs):
-    sheet, grads, out, acc = refs[0], refs[1 : 1 + many], refs[-2], refs[-1]
-    step = pl.program_id(0)
+def weight_kernel(*refs):
+    sheet, *grads, out = refs
     rows, cols, width = sheet.shape
-
-    @pl.when(step == 0)
-    def _():
-        acc[...] = jnp.zeros_like(acc)
-
-    for index, grad in enumerate(grads):
-        @pl.when(step == index)
-        def _():
-            n = grad.shape[1] * HEAD_DIM
-            left = jnp.concatenate([grad[r].reshape(n, cols) for r in range(rows)], axis=1)
-            acc[...] += mm(left, sheet[...].reshape(rows * cols, width), NN)
-
-    @pl.when(step == pl.num_programs(0) - 1)
-    def _():
-        out[...] = acc[...].T.reshape(out.shape).astype(out.dtype)
+    n = grads[0].shape[1] * HEAD_DIM
+    left = [g[r].reshape(n, cols) for g in grads for r in range(g.shape[0])]
+    total = mm(jnp.concatenate(left, axis=1), sheet[...].reshape(rows * cols, width), NN)
+    out[...] = total.T.reshape(out.shape).astype(out.dtype)
 
 
 def weight_part(sheet, grads, shards, kind, after):
     rows, cols, width = sheet.shape
-    many = len(grads)
-    count = rows // many
     columns = grads[0].shape[1] * HEAD_DIM
-    shape = (shards, width // shards, columns)
-    return pl.pallas_call(
-        functools.partial(weight_kernel, many),
-        grid=(many,),
-        in_specs=[pl.BlockSpec((count, cols, width), lambda s: (s, 0, 0))]
-        + [VMEM] * many
-        + [ANY] * len(after),
-        out_specs=pl.BlockSpec(shape, lambda s: (0, 0, 0)),
-        out_shape=like(shape, kind),
-        scratch_shapes=[pltpu.VMEM((columns, width), F32)],
-        compiler_params=pltpu.CompilerParams(vmem_limit_bytes=20 * MIB),
-        cost_estimate=cost(2 * rows * cols * width * columns, 2 * rows * cols * (width + columns)),
-        name="weight_part",
-    )(sheet, *grads, *after)
+    out = like((shards, width // shards, columns), kind)
+    return in_vmem(
+        weight_kernel,
+        "weight_part",
+        (out,),
+        sheet,
+        *grads,
+        after=after,
+        limit=24,
+        flops=2 * rows * cols * width * columns,
+    )[0]
 
 
 def sum_kernel(got, out):
@@ -388,14 +376,14 @@
     direct = n_rows <= 8
     shards = n_rows if direct else 1
     row_bits = [1 << b for b in range(n_rows.bit_length() - 1)]
-    chunk = 4
+    chunks = [row_dev // 8, row_dev // 4, row_dev // 4, 3 * row_dev // 8]
 
     me = jnp.stack([lax.axis_index("rows"), lax.axis_index("heads")]).astype(jnp.int32)
     wq, wk, wv = w_query.T, w_key.T, w_value.T
     cot = jnp.swapaxes(cotangent, 1, 2)
 
     qk, *logits = query_key(lengths, me, sheet, wq, wk, shards, 4)
-    weights, *dprob = value_dprob(lengths, me, sheet, wq, wk, wv, cot, shards, n_heads, 4)
+    weights, *dprob = value_dprob(lengths, me, sheet, wq, wk, wv, cot, logits[-1], shards, n_heads, 4)
     if direct:
         logits = halve(*logits, "rows", row_bits)
         dprob = halve(*dprob, "rows", row_bits)
@@ -408,7 +396,8 @@
         probs, dscore = softmax_back(logits, dprob, scale)
 
     grads, adds, last = [], [], []
-    for first in range(0, row_dev, chunk):
+    first = 0
+    for chunk in chunks:
         after = adds[-2:-1]
         keep, give, grad = backward(first, chunk, lengths, probs, dscore, qk, cot, weights, after)
         grads.append(grad)
@@ -417,20 +406,21 @@
             give, keep = add_split(keep, flip(give, "heads", bit))
             bit *= 2
         adds.append(keep)
-        last.append((keep, flip(give, "heads", bit)))
+        last.append((keep, flip(give, "heads", bit), first))
+        first += chunk
 
     if direct:
-        parts = weight_part(sheet, grads, shards, BF16, adds[-2:-1])
+        parts = weight_part(sheet, grads, shards, BF16, [last[0][1]] + adds[-2:-1])
         weight_grad = sum_parts(lax.all_to_all(parts, "rows", 0, 0), local)
         weight_grad = jnp.swapaxes(weight_grad, 0, 1)
     else:
-        parts = weight_part(sheet, grads, 1, F32, adds[-2:-1])[0]
+        parts = weight_part(sheet, grads, 1, F32, [last[0][1]] + adds[-2:-1])[0]
         weight_grad = lax.psum_scatter(parts, "rows", scatter_dimension=0, tiled=True)
         weight_grad = weight_grad.reshape(width // n_rows, 3, local)
 
     out = None
-    for index, (keep, got) in enumerate(last):
-        out = finish(keep, got, index, row_dev, out)
+    for keep, got, first in last:
+        out = finish(keep, got, first, row_dev, out)
     return (jnp.swapaxes(out, 1, 2), weight_grad)
 
 

time: 118 us -> 123 us (1.042)
  Pallas kernels: 30.3 us -> 38.5 us
  local copies, waits for them, and re-layouts: 9.21 us -> 3.04 us
  starting transfers between devices: 30.4 us -> 31.8 us
    pallas_call x15 -> x16, Pallas kernels: 11.8 us -> 19 us  [in_vmem(): pl.pallas_call(run, in_specs=[SMEM] * scalars + [VMEM] * (len(operands) -...]
    unnamed x29 -> x31, local copies, waits for them, and re-layouts: 9.2 us -> 3.03 us
    pallas_call x5 -> x4, Pallas kernels: 8.85 us -> 3.75 us  [finish(): pl.pallas_call(finish_kernel, grid=(count // block,), in_specs=[spec, spe...]
    pallas_call x1, Pallas kernels: 4.78 us -> 8.02 us  [value_dprob(): pl.pallas_call(value_kernel, grid=(rows // block,), in_specs=[SMEM, SMEM,...]
    pallas_call x1, Pallas kernels: 4.9 us -> 7.72 us  [query_key(): pl.pallas_call(query_key_kernel, grid=(rows // block,), in_specs=[SMEM, S...]
    ppermute x20, starting transfers between devices: 25 us -> 26.3 us  [flip(): return lax.ppermute(values, axis, [(s, s ^ bit) for s in range(n)])]
  transfers between devices with their start and end apart: 21 -> 21, of which waited for: 14 -> 13; matrix products, arithmetic and copies ran while one was open for 0% -> 0% of each run, Pallas kernels for 13% -> 22%
where the time goes in v4:
time: 123 us
  waiting for transfers between devices  47.8 us (39%)
  Pallas kernels  38.5 us (31%)
  starting transfers between devices  31.8 us (26%)
  local copies, waits for them, and re-layouts  3.04 us (2%)
    ppermute x20, waiting for transfers between devices, flip(): return lax.ppermute(values, axis, [(s, s ^ bit) for s in range(n)])  47.8 us
    ppermute x20, starting transfers between devices, flip(): return lax.ppermute(values, axis, [(s, s ^ bit) for s in range(n)])  26.3 us
    pallas_call x16, Pallas kernels, in_vmem(): pl.pallas_call(run, in_specs=[SMEM] * scalars + [VMEM] * (len(operands) -...  19 us
    pallas_call x1, Pallas kernels, value_dprob(): pl.pallas_call(value_kernel, grid=(rows // block,), in_specs=[SMEM, SMEM,...  8.02 us
    pallas_call x1, Pallas kernels, query_key(): pl.pallas_call(query_key_kernel, grid=(rows // block,), in_specs=[SMEM, S...  7.72 us
    all_to_all x1, starting transfers between devices, body(): weight_grad = sum_parts(lax.all_to_all(parts, 'rows', 0, 0), local)  5.48 us
    pallas_call x4, Pallas kernels, finish(): pl.pallas_call(finish_kernel, grid=(count // block,), in_specs=[spec, spe...  3.75 us
    unnamed x31, local copies, waits for them, and re-layouts  3.03 us
  transfers between devices with their start and end apart: 21, of which 13 were waited for; matrix products, arithmetic and copies ran while one was open for 0% of the time, Pallas kernels for 22%

profile of v4, /device:TPU:0, one launch (start us, length us, event | category | flops | bytes accessed | tf_op | source)
XLA Modules:
  0.0 122.6 jit_solution(1136922645507722248)
XLA Ops:
  1.2 7.7 %query_key.1 = (bf16[16,6,64,256]{3,2,1,0:T(8,128)(2,1)}, f32[4,3,32,256]{3,2,1,0:T(8,128)}, bf16[4,3,32,256]{3,2,1,0:T(8,128)(2,1)}) custom-call(s32[16]{0:T(128)} %refs_0_.8, s32[2]{0:T(128)} %pad_add_fusion.me.refs_0_, bf16[16,256,768]{2,1,0:T(8,128)(2,1)} %refs_0_.9, bf16[192,768]{1,0:T(8,128)(2,1)} %bitcast.16, bf16[192,768]{1,0:T(8,128)(2,1)} %bitcast.18), custom_call_target="tpu_custom_call" | custom-call | flops 44040192 | bytes 147456 | tf_op jit(solution)/shard_map/query_key/pallas_call | solution.py:148
  8.9 3.0 %collective-permute-start = (bf16[4,3,32,256]{3,2,1,0:T(8,128)(2,1)}, bf16[4,3,32,256]{3,2,1,0:T(8,128)(2,1)S(1)}, u32[]{:S(2)}, u32[]{:S(2)}) collective-permute-start(bf16[4,3,32,256]{3,2,1,0:T(8,128)(2,1)} %get-tuple-element.41._), channel_id=1, source_target_pairs={{0,4},{4,0},{8,12},{12,8},{16,20},{20,16},{24,28},{28,24},{1,5},{5... | collective-permute-start | bytes 589832 | tf_op jit(solution)/shard_map/ppermute | solution.py:27
  11.9 8.0 %value_dprob.1 = (bf16[4,192,576]{2,1,0:T(8,128)(2,1)}, f32[4,3,32,256]{3,2,1,0:T(8,128)}, bf16[4,3,32,256]{3,2,1,0:T(8,128)(2,1)}) custom-call(s32[16]{0:T(128)} %refs_0_.8, s32[2]{0:T(128)} %pad_add_fusion.me.refs_0_, bf16[16,256,768]{2,1,0:T(8,128)(2,1)} %refs_0_.9, bf16[192,768]{1,0:T(8,128)(2,1)} %bitcast.17, bf16[192,768]{1,0:T(8,128)(2,1)} %bitcast.19, ...), custom_call_target="tpu_custom_call" | custom-call | flops 25165824 | bytes 122880 | tf_op jit(solution)/shard_map/value_dprob/pallas_call | solution.py:177
  20.0 2.1 %collective-permute-start.1 = (bf16[2,3,32,256]{3,2,1,0:T(8,128)(2,1)S(1)}, bf16[2,3,32,256]{3,2,1,0:T(8,128)(2,1)S(1)}, u32[]{:S(2)}, u32[]{:S(2)}) collective-permute-start(bf16[2,3,32,256]{3,2,1,0:T(8,128)(2,1)S(1)} %get-tuple-element.43), channel_id=1, source_target_pairs={{0,8},{4,12},{8,0},{12,4},{16,24},{20,28},{24,16},{28,20},{1,9},{5... | collective-permute-start | bytes 294920 | tf_op jit(solution)/shard_map/ppermute | solution.py:27
  22.2 4.3 %collective-permute-done.3.refs_1_ = bf16[4,3,32,256]{3,2,1,0:T(8,128)(2,1)S(1)} collective-permute-done((bf16[4,3,32,256]{3,2,1,0:T(8,128)(2,1)}, bf16[4,3,32,256]{3,2,1,0:T(8,128)(2,1)S(1)}, u32[]{:S(2)}, u32[]{:S(2)}) %collective-permute-start.3) | collective-permute-done | bytes 196640 | tf_op jit(solution)/shard_map/ppermute | solution.py:27
  27.6 1.6 %collective-permute-start.4 = (bf16[2,3,32,256]{3,2,1,0:T(8,128)(2,1)S(1)}, bf16[2,3,32,256]{3,2,1,0:T(8,128)(2,1)S(1)}, u32[]{:S(2)}, u32[]{:S(2)}) collective-permute-start(bf16[2,3,32,256]{3,2,1,0:T(8,128)(2,1)S(1)} %get-tuple-element.49), channel_id=1, source_target_pairs={{0,8},{4,12},{8,0},{12,4},{16,24},{20,28},{24,16},{28,20},{1,9},{5... | collective-permute-start | bytes 294920 | tf_op jit(solution)/shard_map/ppermute | solution.py:27
  29.2 2.6 %collective-permute-start.2 = (bf16[1,3,32,256]{3,2,1,0:T(8,128)(2,1)S(1)}, bf16[1,3,32,256]{3,2,1,0:T(8,128)(2,1)S(1)}, u32[]{:S(2)}, u32[]{:S(2)}) collective-permute-start(bf16[1,3,32,256]{3,2,1,0:T(8,128)(2,1)S(1)} %get-tuple-element.45), channel_id=1, source_target_pairs={{0,16},{4,20},{8,24},{12,28},{16,0},{20,4},{24,8},{28,12},{1,17},{... | collective-permute-start | bytes 147464 | tf_op jit(solution)/shard_map/ppermute | solution.py:27
  32.8 2.2 %collective-permute-start.5 = (bf16[1,3,32,256]{3,2,1,0:T(8,128)(2,1)S(1)}, bf16[1,3,32,256]{3,2,1,0:T(8,128)(2,1)S(1)}, u32[]{:S(2)}, u32[]{:S(2)}) collective-permute-start(bf16[1,3,32,256]{3,2,1,0:T(8,128)(2,1)S(1)} %get-tuple-element.51), channel_id=1, source_target_pairs={{0,16},{4,20},{8,24},{12,28},{16,0},{20,4},{24,8},{28,12},{1,17},{... | collective-permute-start | bytes 147464 | tf_op jit(solution)/shard_map/ppermute | solution.py:27
  35.6 2.2 %collective-permute-done.5.refs_3_ = bf16[1,3,32,256]{3,2,1,0:T(8,128)(2,1)S(1)} collective-permute-done((bf16[1,3,32,256]{3,2,1,0:T(8,128)(2,1)S(1)}, bf16[1,3,32,256]{3,2,1,0:T(8,128)(2,1)S(1)}, u32[]{:S(2)}, u32[]{:S(2)}) %collective-permute-start.5) | collective-permute-done | bytes 49184 | tf_op jit(solution)/shard_map/ppermute | solution.py:27
  38.1 2.2 %collective-permute-start.6 = (bf16[1,3,32,256]{3,2,1,0:T(8,128)(2,1)S(1)}, bf16[1,3,32,256]{3,2,1,0:T(8,128)(2,1)S(1)}, u32[]{:S(2)}, u32[]{:S(2)}) collective-permute-start(bf16[1,3,32,256]{3,2,1,0:T(8,128)(2,1)S(1)} %get-tuple-element.52), channel_id=1, source_target_pairs={{0,16},{4,20},{8,24},{12,28},{16,0},{20,4},{24,8},{28,12},{1,17},{... | collective-permute-start | bytes 147464 | tf_op jit(solution)/shard_map/ppermute | solution.py:27
  41.1 2.0 %collective-permute-done.6 = bf16[1,3,32,256]{3,2,1,0:T(8,128)(2,1)S(1)} collective-permute-done((bf16[1,3,32,256]{3,2,1,0:T(8,128)(2,1)S(1)}, bf16[1,3,32,256]{3,2,1,0:T(8,128)(2,1)S(1)}, u32[]{:S(2)}, u32[]{:S(2)}) %collective-permute-start.6) | collective-permute-done | bytes 49184 | tf_op jit(solution)/shard_map/ppermute | solution.py:27
  43.2 2.2 %collective-permute-start.7 = (bf16[2,3,32,256]{3,2,1,0:T(8,128)(2,1)S(1)}, bf16[2,3,32,256]{3,2,1,0:T(8,128)(2,1)S(1)}, u32[]{:S(2)}, u32[]{:S(2)}) collective-permute-start(bf16[2,3,32,256]{3,2,1,0:T(8,128)(2,1)S(1)} %pad_maximum_fusion), channel_id=1, source_target_pairs={{0,8},{4,12},{8,0},{12,4},{16,24},{20,28},{24,16},{28,20},{1,9},{5... | collective-permute-start | bytes 294920 | tf_op jit(solution)/shard_map/ppermute | solution.py:27
  45.5 1.9 %collective-permute-start.10 = (bf16[2,3,32,256]{3,2,1,0:T(8,128)(2,1)S(1)}, bf16[2,3,32,256]{3,2,1,0:T(8,128)(2,1)S(1)}, u32[]{:S(2)}, u32[]{:S(2)}) collective-permute-start(bf16[2,3,32,256]{3,2,1,0:T(8,128)(2,1)S(1)} %pad_maximum_fusion.1), channel_id=1, source_target_pairs={{0,8},{4,12},{8,0},{12,4},{16,24},{20,28},{24,16},{28,20},{1,9},{5... | collective-permute-start | bytes 294920 | tf_op jit(solution)/shard_map/ppermute | solution.py:27
  50.8 2.9 %collective-permute-done.8.refs_2_ = bf16[4,3,32,256]{3,2,1,0:T(8,128)(2,1)S(1)} collective-permute-done((bf16[4,3,32,256]{3,2,1,0:T(8,128)(2,1)S(1)}, bf16[4,3,32,256]{3,2,1,0:T(8,128)(2,1)S(1)}, u32[]{:S(2)}, u32[]{:S(2)}) %collective-permute-start.8) | collective-permute-done | bytes 196640 | tf_op jit(solution)/shard_map/ppermute | solution.py:27
  53.7 2.2 %collective-permute-done.11.refs_4_ = bf16[4,3,32,256]{3,2,1,0:T(8,128)(2,1)S(1)} collective-permute-done((bf16[4,3,32,256]{3,2,1,0:T(8,128)(2,1)S(1)}, bf16[4,3,32,256]{3,2,1,0:T(8,128)(2,1)S(1)}, u32[]{:S(2)}, u32[]{:S(2)}) %collective-permute-start.11) | collective-permute-done | bytes 196640 | tf_op jit(solution)/shard_map/ppermute | solution.py:27
  57.7 1.6 %backward.6 = (bf16[2,2,192,256]{3,2,1,0:T(8,128)(2,1)S(1)}, bf16[2,2,192,256]{3,2,1,0:T(8,128)(2,1)S(1)}, bf16[2,9,64,256]{3,2,1,0:T(8,128)(2,1)S(1)}) custom-call(s32[16]{0:T(128)S(1)} %copy-done.6, bf16[8,3,32,256]{3,2,1,0:T(8,128)(2,1)S(1)} %get-tuple-element.54.refs_1_, bf16[8,3,32,256]{3,2,1,0:T(8,128)(2,1)S(1)} %get-tuple-element.55.refs_2_, ...), custom_call_target="tpu_custom_call" | custom-call | flops 9437184 | bytes 121344 | tf_op jit(solution)/shard_map/backward/pallas_call | solution.py:50
  59.5 2.3 %backward.4 = (bf16[2,4,192,256]{3,2,1,0:T(8,128)(2,1)S(1)}, bf16[2,4,192,256]{3,2,1,0:T(8,128)(2,1)S(1)}, bf16[4,9,64,256]{3,2,1,0:T(8,128)(2,1)S(1)}) custom-call(s32[16]{0:T(128)S(1)} %copy-done.6, bf16[8,3,32,256]{3,2,1,0:T(8,128)(2,1)S(1)} %get-tuple-element.54.refs_1_, bf16[8,3,32,256]{3,2,1,0:T(8,128)(2,1)S(1)} %get-tuple-element.55.refs_2_, ...), custom_call_target="tpu_custom_call" | custom-call | flops 18874368 | bytes 142848 | tf_op jit(solution)/shard_map/backward/pallas_call | solution.py:50
  62.4 2.3 %backward.7 = (bf16[2,4,192,256]{3,2,1,0:T(8,128)(2,1)S(1)}, bf16[2,4,192,256]{3,2,1,0:T(8,128)(2,1)S(1)}, bf16[4,9,64,256]{3,2,1,0:T(8,128)(2,1)S(1)}) custom-call(s32[16]{0:T(128)S(1)} %copy-done.6, bf16[8,3,32,256]{3,2,1,0:T(8,128)(2,1)S(1)} %get-tuple-element.54.refs_1_, bf16[8,3,32,256]{3,2,1,0:T(8,128)(2,1)S(1)} %get-tuple-element.55.refs_2_, ...), custom_call_target="tpu_custom_call" | custom-call | flops 18874368 | bytes 142848 | tf_op jit(solution)/shard_map/backward/pallas_call | solution.py:50
  65.1 4.0 %backward.5 = (bf16[2,6,192,256]{3,2,1,0:T(8,128)(2,1)S(1)}, bf16[2,6,192,256]{3,2,1,0:T(8,128)(2,1)}, bf16[6,9,64,256]{3,2,1,0:T(8,128)(2,1)S(1)}) custom-call(s32[16]{0:T(128)S(1)} %copy-done.6, bf16[8,3,32,256]{3,2,1,0:T(8,128)(2,1)S(1)} %get-tuple-element.54.refs_1_, bf16[8,3,32,256]{3,2,1,0:T(8,128)(2,1)S(1)} %get-tuple-element.55.refs_2_, ...), custom_call_target="tpu_custom_call" | custom-call | flops 28311552 | bytes 164352 | tf_op jit(solution)/shard_map/backward/pallas_call | solution.py:50
  72.0 4.4 %collective-permute-done.19.got.refs_5_ = bf16[1,2,192,256]{3,2,1,0:T(8,128)(2,1)S(1)} collective-permute-done((bf16[1,2,192,256]{3,2,1,0:T(8,128)(2,1)S(1)}, bf16[1,2,192,256]{3,2,1,0:T(8,128)(2,1)S(1)}, u32[]{:S(2)}, u32[]{:S(2)}) %collective-permute-start.19) | collective-permute-done | bytes 196640 | tf_op jit(solution)/shard_map/ppermute | solution.py:27
  76.4 4.9 %weight_part.1 = bf16[8,96,576]{2,1,0:T(8,128)(2,1)} custom-call(bf16[16,256,768]{2,1,0:T(8,128)(2,1)S(1)} %bitcast.9, bf16[2,9,64,256]{3,2,1,0:T(8,128)(2,1)S(1)} %get-tuple-element.74.refs_1_, bf16[4,9,64,256]{3,2,1,0:T(8,128)(2,1)S(1)} %get-tuple-element.75.refs_2_, bf16[4,9,64,256]{3,2,1,0:T(8,128)(2,1)S(1)} %get-tuple-element.76.refs_3_, ...), custom_call_target="tpu_custom_call" | custom-call | flops 56623104 | bytes 185856 | tf_op jit(solution)/shard_map/weight_part/pallas_call | solution.py:50
  81.3 5.5 %all-to-all-start = ((bf16[8,96,576]{2,1,0:T(8,128)(2,1)}), bf16[8,96,576]{2,1,0:T(8,128)(2,1)S(1)}, u32[]{:S(2)}, u32[]{:S(2)}) async-start(bf16[8,96,576]{2,1,0:T(8,128)(2,1)} %weight_part.1), calls=%async_computation | async-start | bytes 1966080 | tf_op jit(solution)/shard_map/all_to_all | solution.py:414
  92.7 20.4 %collective-permute-done.18.got = bf16[1,4,192,256]{3,2,1,0:T(8,128)(2,1)S(1)} collective-permute-done((bf16[1,4,192,256]{3,2,1,0:T(8,128)(2,1)S(1)}, bf16[1,4,192,256]{3,2,1,0:T(8,128)(2,1)S(1)}, u32[]{:S(2)}, u32[]{:S(2)}) %collective-permute-start.18) | collective-permute-done | bytes 393248 | tf_op jit(solution)/shard_map/ppermute | solution.py:27
  114.0 5.5 %collective-permute-done.17.got = bf16[1,4,192,256]{3,2,1,0:T(8,128)(2,1)S(1)} collective-permute-done((bf16[1,4,192,256]{3,2,1,0:T(8,128)(2,1)S(1)}, bf16[1,4,192,256]{3,2,1,0:T(8,128)(2,1)S(1)}, u32[]{:S(2)}, u32[]{:S(2)}) %collective-permute-start.17) | collective-permute-done | bytes 393248 | tf_op jit(solution)/shard_map/ppermute | solution.py:27
  (77 shorter events, 23.6 us)
Async XLA Ops:
  8.9 11.0 %collective-permute-start = (bf16[4,3,32,256]{3,2,1,0:T(8,128)(2,1)}, bf16[4,3,32,256]{3,2,1,0:T(8,128)(2,1)S(1)}, u32[]{:S(2)}, u32[]{:S(2)}) collective-permute-start(bf16[4,3,32,256]{3,2,1,0:T(8,128)(2,1)} %get-tuple-element.41._), channel_id=1, source_target_pairs={{0,4},{4,0},{8,12},{12,8},{16,20},{20,16},{24,28},{28,24},{1,5},{5... | collective-permute-start | bytes 589832 | tf_op jit(solution)/shard_map/ppermute | solution.py:27
  11.9 44.6 %copy-start.1 = (bf16[16,256,192]{1,2,0:T(8,128)(2,1)S(1)}, bf16[16,256,192]{1,2,0:T(8,128)(2,1)}, u32[]{:S(2)}) copy-start(bf16[16,256,192]{1,2,0:T(8,128)(2,1)} %param.10) | copy-start | bytes 4718596
  19.9 6.6 %collective-permute-start.3 = (bf16[4,3,32,256]{3,2,1,0:T(8,128)(2,1)}, bf16[4,3,32,256]{3,2,1,0:T(8,128)(2,1)S(1)}, u32[]{:S(2)}, u32[]{:S(2)}) collective-permute-start(bf16[4,3,32,256]{3,2,1,0:T(8,128)(2,1)} %get-tuple-element.47), channel_id=1, source_target_pairs={{0,4},{4,0},{8,12},{12,8},{16,20},{20,16},{24,28},{28,24},{1,5},{5... | collective-permute-start | bytes 589832 | tf_op jit(solution)/shard_map/ppermute | solution.py:27
  20.0 35.9 %copy-start.7 = (s32[2]{0:T(128)S(1)}, s32[2]{0:T(128)}, u32[]{:S(2)}) copy-start(s32[2]{0:T(128)} %pad_add_fusion.me.refs_0_) | copy-start | bytes 28
  20.0 9.2 %collective-permute-start.1 = (bf16[2,3,32,256]{3,2,1,0:T(8,128)(2,1)S(1)}, bf16[2,3,32,256]{3,2,1,0:T(8,128)(2,1)S(1)}, u32[]{:S(2)}, u32[]{:S(2)}) collective-permute-start(bf16[2,3,32,256]{3,2,1,0:T(8,128)(2,1)S(1)} %get-tuple-element.43), channel_id=1, source_target_pairs={{0,8},{4,12},{8,0},{12,4},{16,24},{20,28},{24,16},{28,20},{1,9},{5... | collective-permute-start | bytes 294920 | tf_op jit(solution)/shard_map/ppermute | solution.py:27
  27.5 29.0 %copy-start = (bf16[16,6,64,256]{3,2,1,0:T(8,128)(2,1)S(1)}, bf16[16,6,64,256]{3,2,1,0:T(8,128)(2,1)}, u32[]{:S(2)}) copy-start(bf16[16,6,64,256]{3,2,1,0:T(8,128)(2,1)} %get-tuple-element.56.refs_3_) | copy-start | bytes 9437188
  27.6 5.2 %collective-permute-start.4 = (bf16[2,3,32,256]{3,2,1,0:T(8,128)(2,1)S(1)}, bf16[2,3,32,256]{3,2,1,0:T(8,128)(2,1)S(1)}, u32[]{:S(2)}, u32[]{:S(2)}) collective-permute-start(bf16[2,3,32,256]{3,2,1,0:T(8,128)(2,1)S(1)} %get-tuple-element.49), channel_id=1, source_target_pairs={{0,8},{4,12},{8,0},{12,4},{16,24},{20,28},{24,16},{28,20},{1,9},{5... | collective-permute-start | bytes 294920 | tf_op jit(solution)/shard_map/ppermute | solution.py:27
  29.2 6.4 %collective-permute-start.2 = (bf16[1,3,32,256]{3,2,1,0:T(8,128)(2,1)S(1)}, bf16[1,3,32,256]{3,2,1,0:T(8,128)(2,1)S(1)}, u32[]{:S(2)}, u32[]{:S(2)}) collective-permute-start(bf16[1,3,32,256]{3,2,1,0:T(8,128)(2,1)S(1)} %get-tuple-element.45), channel_id=1, source_target_pairs={{0,16},{4,20},{8,24},{12,28},{16,0},{20,4},{24,8},{28,12},{1,17},{... | collective-permute-start | bytes 147464 | tf_op jit(solution)/shard_map/ppermute | solution.py:27
  32.8 5.1 %collective-permute-start.5 = (bf16[1,3,32,256]{3,2,1,0:T(8,128)(2,1)S(1)}, bf16[1,3,32,256]{3,2,1,0:T(8,128)(2,1)S(1)}, u32[]{:S(2)}, u32[]{:S(2)}) collective-permute-start(bf16[1,3,32,256]{3,2,1,0:T(8,128)(2,1)S(1)} %get-tuple-element.51), channel_id=1, source_target_pairs={{0,16},{4,20},{8,24},{12,28},{16,0},{20,4},{24,8},{28,12},{1,17},{... | collective-permute-start | bytes 147464 | tf_op jit(solution)/shard_map/ppermute | solution.py:27
  38.1 5.1 %collective-permute-start.6 = (bf16[1,3,32,256]{3,2,1,0:T(8,128)(2,1)S(1)}, bf16[1,3,32,256]{3,2,1,0:T(8,128)(2,1)S(1)}, u32[]{:S(2)}, u32[]{:S(2)}) collective-permute-start(bf16[1,3,32,256]{3,2,1,0:T(8,128)(2,1)S(1)} %get-tuple-element.52), channel_id=1, source_target_pairs={{0,16},{4,20},{8,24},{12,28},{16,0},{20,4},{24,8},{28,12},{1,17},{... | collective-permute-start | bytes 147464 | tf_op jit(solution)/shard_map/ppermute | solution.py:27
  40.3 5.2 %collective-permute-start.9 = (bf16[1,3,32,256]{3,2,1,0:T(8,128)(2,1)S(1)}, bf16[1,3,32,256]{3,2,1,0:T(8,128)(2,1)S(1)}, u32[]{:S(2)}, u32[]{:S(2)}) collective-permute-start(bf16[1,3,32,256]{3,2,1,0:T(8,128)(2,1)S(1)} %get-tuple-element.53), channel_id=1, source_target_pairs={{0,16},{4,20},{8,24},{12,28},{16,0},{20,4},{24,8},{28,12},{1,17},{... | collective-permute-start | bytes 147464 | tf_op jit(solution)/shard_map/ppermute | solution.py:27
  43.2 4.8 %collective-permute-start.7 = (bf16[2,3,32,256]{3,2,1,0:T(8,128)(2,1)S(1)}, bf16[2,3,32,256]{3,2,1,0:T(8,128)(2,1)S(1)}, u32[]{:S(2)}, u32[]{:S(2)}) collective-permute-start(bf16[2,3,32,256]{3,2,1,0:T(8,128)(2,1)S(1)} %pad_maximum_fusion), channel_id=1, source_target_pairs={{0,8},{4,12},{8,0},{12,4},{16,24},{20,28},{24,16},{28,20},{1,9},{5... | collective-permute-start | bytes 294920 | tf_op jit(solution)/shard_map/ppermute | solution.py:27
  45.5 4.7 %collective-permute-start.10 = (bf16[2,3,32,256]{3,2,1,0:T(8,128)(2,1)S(1)}, bf16[2,3,32,256]{3,2,1,0:T(8,128)(2,1)S(1)}, u32[]{:S(2)}, u32[]{:S(2)}) collective-permute-start(bf16[2,3,32,256]{3,2,1,0:T(8,128)(2,1)S(1)} %pad_maximum_fusion.1), channel_id=1, source_target_pairs={{0,8},{4,12},{8,0},{12,4},{16,24},{20,28},{24,16},{28,20},{1,9},{5... | collective-permute-start | bytes 294920 | tf_op jit(solution)/shard_map/ppermute | solution.py:27
  48.0 5.7 %collective-permute-start.8 = (bf16[4,3,32,256]{3,2,1,0:T(8,128)(2,1)S(1)}, bf16[4,3,32,256]{3,2,1,0:T(8,128)(2,1)S(1)}, u32[]{:S(2)}, u32[]{:S(2)}) collective-permute-start(bf16[4,3,32,256]{3,2,1,0:T(8,128)(2,1)S(1)} %constant_dynamic-update-slice_fusion.refs_1_), channel_id=1, source_target_pairs={{0,4},{4,0},{8,12},{12,8},{16,20},{20,16},{24,28},{28,24},{1,5},{5... | collective-permute-start | bytes 589832 | tf_op jit(solution)/shard_map/ppermute | solution.py:27
  50.2 5.7 %collective-permute-start.11 = (bf16[4,3,32,256]{3,2,1,0:T(8,128)(2,1)S(1)}, bf16[4,3,32,256]{3,2,1,0:T(8,128)(2,1)S(1)}, u32[]{:S(2)}, u32[]{:S(2)}) collective-permute-start(bf16[4,3,32,256]{3,2,1,0:T(8,128)(2,1)S(1)} %constant_dynamic-update-slice_fusion.3.refs_3_), channel_id=1, source_target_pairs={{0,4},{4,0},{8,12},{12,8},{16,20},{20,16},{24,28},{28,24},{1,5},{5... | collective-permute-start | bytes 589832 | tf_op jit(solution)/shard_map/ppermute | solution.py:27
  59.4 2.9 %collective-permute-start.15 = (bf16[2,2,192,256]{3,2,1,0:T(8,128)(2,1)S(1)}, bf16[2,2,192,256]{3,2,1,0:T(8,128)(2,1)S(1)}, u32[]{:S(2)}, u32[]{:S(2)}) collective-permute-start(bf16[2,2,192,256]{3,2,1,0:T(8,128)(2,1)S(1)} %get-tuple-element.66), channel_id=1, source_target_pairs={{0,1},{1,0},{2,3},{3,2},{4,5},{5,4},{6,7},{7,6},{8,9},{9,8},{10,11... | collective-permute-start | bytes 1179656 | tf_op jit(solution)/shard_map/ppermute | solution.py:27
  61.8 3.1 %collective-permute-start.12 = (bf16[2,4,192,256]{3,2,1,0:T(8,128)(2,1)S(1)}, bf16[2,4,192,256]{3,2,1,0:T(8,128)(2,1)S(1)}, u32[]{:S(2)}, u32[]{:S(2)}) collective-permute-start(bf16[2,4,192,256]{3,2,1,0:T(8,128)(2,1)S(1)} %get-tuple-element.59), channel_id=1, source_target_pairs={{0,1},{1,0},{2,3},{3,2},{4,5},{5,4},{6,7},{7,6},{8,9},{9,8},{10,11... | collective-permute-start | bytes 2359304 | tf_op jit(solution)/shard_map/ppermute | solution.py:27
  64.7 6.4 %collective-permute-start.16 = (bf16[2,4,192,256]{3,2,1,0:T(8,128)(2,1)S(1)}, bf16[2,4,192,256]{3,2,1,0:T(8,128)(2,1)S(1)}, u32[]{:S(2)}, u32[]{:S(2)}) collective-permute-start(bf16[2,4,192,256]{3,2,1,0:T(8,128)(2,1)S(1)} %get-tuple-element.69), channel_id=1, source_target_pairs={{0,1},{1,0},{2,3},{3,2},{4,5},{5,4},{6,7},{7,6},{8,9},{9,8},{10,11... | collective-permute-start | bytes 2359304 | tf_op jit(solution)/shard_map/ppermute | solution.py:27
  69.1 17.7 %collective-permute-start.13 = (bf16[2,6,192,256]{3,2,1,0:T(8,128)(2,1)}, bf16[2,6,192,256]{3,2,1,0:T(8,128)(2,1)}, u32[]{:S(2)}, u32[]{:S(2)}) collective-permute-start(bf16[2,6,192,256]{3,2,1,0:T(8,128)(2,1)} %get-tuple-element.62), channel_id=1, source_target_pairs={{0,1},{1,0},{2,3},{3,2},{4,5},{5,4},{6,7},{7,6},{8,9},{9,8},{10,11... | collective-permute-start | bytes 3538952 | tf_op jit(solution)/shard_map/ppermute | solution.py:27
  69.6 6.8 %collective-permute-start.19 = (bf16[1,2,192,256]{3,2,1,0:T(8,128)(2,1)S(1)}, bf16[1,2,192,256]{3,2,1,0:T(8,128)(2,1)S(1)}, u32[]{:S(2)}, u32[]{:S(2)}) collective-permute-start(bf16[1,2,192,256]{3,2,1,0:T(8,128)(2,1)S(1)} %get-tuple-element.73), channel_id=1, source_target_pairs={{0,2},{1,3},{2,0},{3,1},{4,6},{5,7},{6,4},{7,5},{8,10},{9,11},{10,... | collective-permute-start | bytes 589832 | tf_op jit(solution)/shard_map/ppermute | solution.py:27
  81.3 40.4 %all-to-all-start = ((bf16[8,96,576]{2,1,0:T(8,128)(2,1)}), bf16[8,96,576]{2,1,0:T(8,128)(2,1)S(1)}, u32[]{:S(2)}, u32[]{:S(2)}) async-start(bf16[8,96,576]{2,1,0:T(8,128)(2,1)} %weight_part.1), calls=%async_computation | async-start | bytes 1966080 | tf_op jit(solution)/shard_map/all_to_all | solution.py:414
  88.4 31.9 %collective-permute-start.14 = (bf16[1,6,192,256]{3,2,1,0:T(8,128)(2,1)S(1)}, bf16[1,6,192,256]{3,2,1,0:T(8,128)(2,1)S(1)}, u32[]{:S(2)}, u32[]{:S(2)}) collective-permute-start(bf16[1,6,192,256]{3,2,1,0:T(8,128)(2,1)S(1)} %get-tuple-element.64), channel_id=1, source_target_pairs={{0,2},{1,3},{2,0},{3,1},{4,6},{5,7},{6,4},{7,5},{8,10},{9,11},{10,... | collective-permute-start | bytes 1769480 | tf_op jit(solution)/shard_map/ppermute | solution.py:27
  90.0 23.2 %collective-permute-start.18 = (bf16[1,4,192,256]{3,2,1,0:T(8,128)(2,1)S(1)}, bf16[1,4,192,256]{3,2,1,0:T(8,128)(2,1)S(1)}, u32[]{:S(2)}, u32[]{:S(2)}) collective-permute-start(bf16[1,4,192,256]{3,2,1,0:T(8,128)(2,1)S(1)} %copy-done.9), channel_id=1, source_target_pairs={{0,2},{1,3},{2,0},{3,1},{4,6},{5,7},{6,4},{7,5},{8,10},{9,11},{10,... | collective-permute-start | bytes 1179656 | tf_op jit(solution)/shard_map/ppermute | solution.py:27
  90.5 28.9 %collective-permute-start.17 = (bf16[1,4,192,256]{3,2,1,0:T(8,128)(2,1)S(1)}, bf16[1,4,192,256]{3,2,1,0:T(8,128)(2,1)S(1)}, u32[]{:S(2)}, u32[]{:S(2)}) collective-permute-start(bf16[1,4,192,256]{3,2,1,0:T(8,128)(2,1)S(1)} %copy-done.11), channel_id=1, source_target_pairs={{0,2},{1,3},{2,0},{3,1},{4,6},{5,7},{6,4},{7,5},{8,10},{9,11},{10,... | collective-permute-start | bytes 1179656 | tf_op jit(solution)/shard_map/ppermute | solution.py:27
  (11 other events, 78.1 us)

commit v5 on v4

--- a/solution.py
+++ b/solution.py
@@ -28,30 +28,33 @@
 
 
 def cost(flops, moved):
-    return pl.CostEstimate(flops=int(flops) // 64, bytes_accessed=int(moved) // 64, transcendentals=0)
+    return pl.CostEstimate(flops=int(flops), bytes_accessed=int(moved), transcendentals=0)
 
 
 SMEM = pl.BlockSpec(memory_space=pltpu.SMEM)
 VMEM = pl.BlockSpec(memory_space=pltpu.VMEM)
 ANY = pl.BlockSpec(memory_space=pl.ANY)
+HBM = pl.BlockSpec(memory_space=pltpu.HBM)
 
 
 def like(shape, dtype=BF16):
     return jax.ShapeDtypeStruct(shape, dtype)
 
 
-def in_vmem(kernel, name, out, *operands, scalars=0, after=(), limit=12, flops=0):
+def in_vmem(kernel, name, out, *operands, scalars=0, streamed=0, after=(), scratch=(), limit=12, flops=0):
     many = len(after)
 
     def run(*refs):
         kernel(*refs[: len(operands)], *refs[len(operands) + many :])
 
     moved = 2 * sum(a.size for a in operands) + 2 * sum(o.size for o in out)
+    held = len(operands) - scalars - streamed
     return pl.pallas_call(
         run,
-        in_specs=[SMEM] * scalars + [VMEM] * (len(operands) - scalars) + [ANY] * many,
+        in_specs=[SMEM] * scalars + [HBM] * streamed + [VMEM] * held + [ANY] * many,
         out_specs=[VMEM] * len(out),
         out_shape=list(out),
+        scratch_shapes=list(scratch),
         compiler_params=pltpu.CompilerParams(vmem_limit_bytes=limit * MIB),
         cost_estimate=cost(flops, moved),
         name=name,
@@ -69,64 +72,127 @@
         out[j // len(outs)] = acc[:, me ^ j].astype(out.dtype)
 
 
-def query_key_kernel(lengths, me, sheet, wq, wk, qk, *rest):
-    outs, wt, acc = rest[:-2], rest[-2], rest[-1]
-    step = pl.program_id(0)
+BLOCK = 4
+
+
+def query_key_kernel(lengths, me, sheet, wq, wk, qk, held, *rest):
+    outs, (wt, acc, sems) = rest[:-3], rest[-3:]
     rows, cols, _ = sheet.shape
     local = wq.shape[0]
     heads = local // HEAD_DIM
-
-    @pl.when(step == 0)
-    def _():
-        wt[:local] = wq[...]
-        wt[local:] = wk[...]
-        acc[...] = jnp.zeros_like(acc)
-
-    for r in range(rows):
-        mask = lane_mask(lengths[step * rows + r], cols)
-        value = (mm(wt[...], sheet[r], NT) * mask).astype(BF16)
-        qk[r] = value.reshape(2 * heads, HEAD_DIM, cols)
-    flat = (rows * HEAD_DIM, cols)
-    for h in range(heads):
-        term = mm(qk[:, h].reshape(flat), qk[:, heads + h].reshape(flat), TN)
-        acc[h] += term.reshape(acc.shape[1:])
-
-    @pl.when(step == pl.num_programs(0) - 1)
-    def _():
-        put_shards(me[0], acc, outs)
-
-
-def value_kernel(lengths, me, sheet, wq, wk, wv, cot, _, natural, *rest):
-    outs, turned, acc = rest[:-2], rest[-2], rest[-1]
-    step = pl.program_id(0)
-    rows, cols, _ = sheet.shape
+    copies = [
+        pltpu.make_async_copy(wq, wt.at[:local], sems.at[0]),
+        pltpu.make_async_copy(wk, wt.at[local:], sems.at[1]),
+    ]
+    for index, first in enumerate(range(0, rows, BLOCK)):
+        some = pl.ds(first, BLOCK)
+        copies.append(pltpu.make_async_copy(sheet.at[some], held.at[some], sems.at[2 + index]))
+    for copy in copies:
+        copy.start()
+    copies[0].wait()
+    copies[1].wait()
+    flat = (BLOCK * HEAD_DIM, cols)
+    for index, first in enumerate(range(0, rows, BLOCK)):
+        copies[2 + index].wait()
+        for r in range(first, first + BLOCK):
+            value = (mm(wt[...], held[r], NT) * lane_mask(lengths[r], cols)).astype(BF16)
+            qk[r] = value.reshape(2 * heads, HEAD_DIM, cols)
+        some = pl.ds(first, BLOCK)
+        for h in range(heads):
+            term = mm(qk[some, h].reshape(flat), qk[some, heads + h].reshape(flat), TN)
+            term = term.reshape(acc.shape[1:])
+            acc[h] = term if index == 0 else acc[h] + term
+    put_shards(me[0], acc, outs)
+
+
+def query_key(lengths, me, sheet, wq, wk, shards):
+    rows, cols, width = sheet.shape
     local = wq.shape[0]
     heads = local // HEAD_DIM
-
-    @pl.when(step == 0)
-    def _():
-        acc[...] = jnp.zeros_like(acc)
-        for index, weight in enumerate((wq, wk, wv)):
-            turned[:, :, index * local : (index + 1) * local] = weight[...].T.reshape(
-                turned.shape[:2] + (local,)
-            )
-        for j in range(turned.shape[0]):
-            natural[j] = turned[me[1] ^ j]
-
-    values = []
-    for r in range(rows):
-        mask = lane_mask(lengths[step * rows + r], cols)
-        value = (mm(wv[...], sheet[r], NT) * mask).astype(BF16)
-        values.append(value.reshape(heads, HEAD_DIM, cols))
-    flat = (rows * HEAD_DIM, cols)
-    for h in range(heads):
-        left = cot[:, h * HEAD_DIM : (h + 1) * HEAD_DIM].reshape(flat)
-        right = jnp.concatenate([v[h] for v in values], axis=0)
-        acc[h] += mm(left, right, TN).reshape(acc.shape[1:])
-
-    @pl.when(step == pl.num_programs(0) - 1)
-    def _():
-        put_shards(me[0], acc, outs)
+    return in_vmem(
+        query_key_kernel,
+        "query_key",
+        [like((rows, 2 * heads, HEAD_DIM, cols)), like(sheet.shape)] + part_shapes(shards, heads, cols),
+        lengths,
+        me,
+        sheet,
+        wq,
+        wk,
+        scalars=2,
+        streamed=3,
+        scratch=(
+            pltpu.VMEM((2 * local, width), BF16),
+            pltpu.VMEM((heads, shards, cols // shards, cols), F32),
+            pltpu.SemaphoreType.DMA((2 + rows // BLOCK,)),
+        ),
+        limit=16,
+        flops=2 * rows * cols * local * (2 * width + cols),
+    )
+
+
+def value_kernel(lengths, me, sheet, wv, cot, *rest):
+    outs, acc = rest[:-1], rest[-1]
+    rows, cols, _ = sheet.shape
+    local = wv.shape[0]
+    heads = local // HEAD_DIM
+    flat = (BLOCK * HEAD_DIM, cols)
+    for first in range(0, rows, BLOCK):
+        values = []
+        for r in range(first, first + BLOCK):
+            value = (mm(wv[...], sheet[r], NT) * lane_mask(lengths[r], cols)).astype(BF16)
+            values.append(value.reshape(heads, HEAD_DIM, cols))
+        for h in range(heads):
+            left = cot[pl.ds(first, BLOCK), h * HEAD_DIM : (h + 1) * HEAD_DIM].reshape(flat)
+            right = jnp.concatenate([v[h] for v in values], axis=0)
+            term = mm(left, right, TN).reshape(acc.shape[1:])
+            acc[h] = term if first == 0 else acc[h] + term
+    put_shards(me[0], acc, outs)
+
+
+def value_dprob(lengths, me, sheet, wv, cot, after, shards):
+    rows, cols, width = sheet.shape
+    local = wv.shape[0]
+    heads = local // HEAD_DIM
+    return in_vmem(
+        value_kernel,
+        "value_dprob",
+        part_shapes(shards, heads, cols),
+        lengths,
+        me,
+        sheet,
+        wv,
+        cot,
+        scalars=2,
+        after=after,
+        scratch=(pltpu.VMEM((heads, shards, cols // shards, cols), F32),),
+        limit=16,
+        flops=2 * rows * cols * local * (width + cols),
+    )
+
+
+def turn_kernel(me, wq, wk, wv, natural, turned):
+    local = wq.shape[0]
+    for index, weight in enumerate((wq, wk, wv)):
+        turned[:, :, index * local : (index + 1) * local] = weight[...].T.reshape(turned.shape[:2] + (local,))
+    for j in range(turned.shape[0]):
+        natural[j] = turned[me[1] ^ j]
+
+
+def turn(me, wq, wk, wv, devices, after):
+    local, width = wq.shape
+    shape = (devices, width // devices, 3 * local)
+    return in_vmem(
+        turn_kernel,
+        "turn",
+        (like(shape),),
+        me,
+        wq,
+        wk,
+        wv,
+        scalars=1,
+        after=after,
+        scratch=(pltpu.VMEM(shape, BF16),),
+    )[0]
 
 
 def part_shapes(shards, heads, cols):
@@ -136,69 +202,6 @@
     return [like(half, F32), like(half)]
 
 
-def whole(shape):
-    return pl.BlockSpec(shape, lambda s: (0,) * len(shape))
-
-
-def query_key(lengths, me, sheet, wq, wk, shards, block):
-    rows, cols, width = sheet.shape
-    local = wq.shape[0]
-    heads = local // HEAD_DIM
-    outs = part_shapes(shards, heads, cols)
-    return pl.pallas_call(
-        query_key_kernel,
-        grid=(rows // block,),
-        in_specs=[
-            SMEM,
-            SMEM,
-            pl.BlockSpec((block, cols, width), lambda s: (s, 0, 0)),
-            whole(wq.shape),
-            whole(wk.shape),
-        ],
-        out_specs=[pl.BlockSpec((block, 2 * heads, HEAD_DIM, cols), lambda s: (s, 0, 0, 0))]
-        + [whole(o.shape) for o in outs],
-        out_shape=[like((rows, 2 * heads, HEAD_DIM, cols))] + outs,
-        scratch_shapes=[
-            pltpu.VMEM((2 * local, width), BF16),
-            pltpu.VMEM((heads, shards, cols // shards, cols), F32),
-        ],
-        compiler_params=pltpu.CompilerParams(vmem_limit_bytes=56 * MIB),
-        cost_estimate=cost(2 * rows * cols * local * (2 * width + cols), 2 * rows * cols * (width + 2 * local)),
-        name="query_key",
-    )(lengths, me, sheet, wq, wk)
-
-
-def value_dprob(lengths, me, sheet, wq, wk, wv, cot, after, shards, devices, block):
-    rows, cols, width = sheet.shape
-    local = wv.shape[0]
-    heads = local // HEAD_DIM
-    outs = part_shapes(shards, heads, cols)
-    natural = (devices, width // devices, 3 * local)
-    return pl.pallas_call(
-        value_kernel,
-        grid=(rows // block,),
-        in_specs=[
-            SMEM,
-            SMEM,
-            pl.BlockSpec((block, cols, width), lambda s: (s, 0, 0)),
-            whole(wq.shape),
-            whole(wk.shape),
-            whole(wv.shape),
-            pl.BlockSpec((block, local, cols), lambda s: (s, 0, 0)),
-            ANY,
-        ],
-        out_specs=[whole(natural)] + [whole(o.shape) for o in outs],
-        out_shape=[like(natural)] + outs,
-        scratch_shapes=[
-            pltpu.VMEM(natural, BF16),
-            pltpu.VMEM((heads, shards, cols // shards, cols), F32),
-        ],
-        compiler_params=pltpu.CompilerParams(vmem_limit_bytes=56 * MIB),
-        cost_estimate=cost(2 * rows * cols * local * (width + cols), 2 * rows * cols * (width + local)),
-        name="value_dprob",
-    )(lengths, me, sheet, wq, wk, wv, cot, after)
-
-
 def add_split_kernel(keep, got, give_out, keep_out):
     for j in range(keep.shape[0]):
         total = keep[j].astype(F32) + got[j].astype(F32)
@@ -206,14 +209,15 @@
         out[j // 2] = total.astype(out.dtype)
 
 
-def add_split(keep, got):
+def add_split(keep, got, after=()):
     half = (keep.shape[0] // 2,) + keep.shape[1:]
-    return in_vmem(add_split_kernel, "add_split", (like(half), like(half, keep.dtype)), keep, got)
-
-
-def halve(keep, give, axis, bits):
-    for bit in bits[:-1]:
-        give, keep = add_split(keep, flip(give, axis, bit))
+    return in_vmem(add_split_kernel, "add_split", (like(half), like(half, keep.dtype)), keep, got, after=after)
+
+
+def halve(keep, give, axis, bits, after=()):
+    after = list(after) + [()] * len(bits)
+    for bit, waits in zip(bits[:-1], after):
+        give, keep = add_split(keep, flip(give, axis, bit), waits)
     return keep, flip(give, axis, bits[-1])
 
 
@@ -331,40 +335,60 @@
     )(keep, got, *extra)
 
 
-def weight_kernel(*refs):
-    sheet, *grads, out = refs
+def weight_kernel(me, sheet, *refs):
+    *grads, keep, give, turned = refs
     rows, cols, width = sheet.shape
     n = grads[0].shape[1] * HEAD_DIM
     left = [g[r].reshape(n, cols) for g in grads for r in range(g.shape[0])]
     total = mm(jnp.concatenate(left, axis=1), sheet[...].reshape(rows * cols, width), NN)
-    out[...] = total.T.reshape(out.shape).astype(out.dtype)
-
-
-def weight_part(sheet, grads, shards, kind, after):
+    turned[...] = total.T.reshape(turned.shape)
+    for j in range(turned.shape[0]):
+        out = (keep, give)[j % 2]
+        out[j // 2] = turned[me[0] ^ j].astype(out.dtype)
+
+
+def whole_weight_kernel(me, sheet, *refs):
+    *grads, out = refs
+    rows, cols, width = sheet.shape
+    n = grads[0].shape[1] * HEAD_DIM
+    left = [g[r].reshape(n, cols) for g in grads for r in range(g.shape[0])]
+    out[...] = mm(jnp.concatenate(left, axis=1), sheet[...].reshape(rows * cols, width), NN).T
+
+
+def weight_part(me, sheet, grads, shards, after):
     rows, cols, width = sheet.shape
     columns = grads[0].shape[1] * HEAD_DIM
-    out = like((shards, width // shards, columns), kind)
-    return in_vmem(
-        weight_kernel,
+    if shards == 1:
+        kernel, outs, scratch = whole_weight_kernel, [like((width, columns), F32)], ()
+    else:
+        half = (shards // 2, width // shards, columns)
+        kernel, outs = weight_kernel, [like(half, F32), like(half)]
+        scratch = (pltpu.VMEM((shards,) + half[1:], F32),)
+    return in_vmem(
+        kernel,
         "weight_part",
-        (out,),
+        outs,
+        me,
         sheet,
         *grads,
+        scalars=1,
         after=after,
+        scratch=scratch,
         limit=24,
         flops=2 * rows * cols * width * columns,
-    )[0]
-
-
-def sum_kernel(got, out):
-    total = jnp.sum(got[...].astype(F32), axis=0)
+    )
+
+
+def last_kernel(keep, got, out):
+    total = keep[0] + got[0].astype(F32)
     local = out.shape[-1]
-    for index in range(3):
+    for index in range(out.shape[0]):
         out[index] = total[:, index * local : (index + 1) * local]
 
 
-def sum_parts(got, local):
-    return in_vmem(sum_kernel, "sum_parts", (like((3, got.shape[1], local), F32),), got)[0]
+def last_sum(keep, got, local, after):
+    shape = (keep.shape[2] // local, keep.shape[1], local)
+    return in_vmem(last_kernel, "last_sum", (like(shape, F32),), keep, got, after=after)[0]
 
 
 def body(sheet, w_query, w_key, w_value, cotangent, lengths):
@@ -382,8 +406,9 @@
     wq, wk, wv = w_query.T, w_key.T, w_value.T
     cot = jnp.swapaxes(cotangent, 1, 2)
 
-    qk, *logits = query_key(lengths, me, sheet, wq, wk, shards, 4)
-    weights, *dprob = value_dprob(lengths, me, sheet, wq, wk, wv, cot, logits[-1], shards, n_heads, 4)
+    qk, held, *logits = query_key(lengths, me, sheet, wq, wk, shards)
+    dprob = value_dprob(lengths, me, held, wv, cot, logits[-1:], shards)
+    weights = turn(me, wq, wk, wv, n_heads, dprob[-1:])
     if direct:
         logits = halve(*logits, "rows", row_bits)
         dprob = halve(*dprob, "rows", row_bits)
@@ -409,13 +434,14 @@
         last.append((keep, flip(give, "heads", bit), first))
         first += chunk
 
+    arrived = [got for _, got, _ in last]
+    parts = weight_part(me, held, grads, shards, arrived[:1])
     if direct:
-        parts = weight_part(sheet, grads, shards, BF16, [last[0][1]] + adds[-2:-1])
-        weight_grad = sum_parts(lax.all_to_all(parts, "rows", 0, 0), local)
+        parts = halve(*parts, "rows", row_bits, [arrived[1:2], arrived[2:3]])
+        weight_grad = last_sum(*parts, local, arrived[3:])
         weight_grad = jnp.swapaxes(weight_grad, 0, 1)
     else:
-        parts = weight_part(sheet, grads, 1, F32, [last[0][1]] + adds[-2:-1])[0]
-        weight_grad = lax.psum_scatter(parts, "rows", scatter_dimension=0, tiled=True)
+        weight_grad = lax.psum_scatter(parts[0], "rows", scatter_dimension=0, tiled=True)
         weight_grad = weight_grad.reshape(width // n_rows, 3, local)
 
     out = None

time: 123 us -> 113 us (0.919)
  Pallas kernels: 38.5 us -> 30.3 us
  waiting for transfers between devices: 47.8 us -> 43.7 us
  local copies, waits for them, and re-layouts: 3.04 us -> 5.41 us
    pallas_call x18 -> x21, Pallas kernels: 34.8 us -> 26.6 us  [in_vmem(): pl.pallas_call(run, in_specs=[SMEM] * scalars + [HBM] * streamed + [VMEM]...]
    ppermute x20 -> x23, starting transfers between devices: 26.3 us -> 32.4 us  [flip(): return lax.ppermute(values, axis, [(s, s ^ bit) for s in range(n)])]
    all_to_all x1 -> x0, starting transfers between devices: 5.48 us -> none  [body(): weight_grad = sum_parts(lax.all_to_all(parts, 'rows', 0, 0), local)]
    ppermute x20 -> x23, waiting for transfers between devices: 47.8 us -> 43.7 us  [flip(): return lax.ppermute(values, axis, [(s, s ^ bit) for s in range(n)])]
    unnamed x31 -> x21, local copies, waits for them, and re-layouts: 3.03 us -> 5.4 us
  transfers between devices with their start and end apart: 21 -> 23, of which waited for: 13 -> 16; matrix products, arithmetic and copies ran while one was open for 0% -> 0% of each run, Pallas kernels for 22% -> 19%
where the time goes in v5:
time: 113 us
  waiting for transfers between devices  43.7 us (39%)
  starting transfers between devices  32.4 us (29%)
  Pallas kernels  30.3 us (27%)
  local copies, waits for them, and re-layouts  5.41 us (5%)
    ppermute x23, waiting for transfers between devices, flip(): return lax.ppermute(values, axis, [(s, s ^ bit) for s in range(n)])  43.7 us
    ppermute x23, starting transfers between devices, flip(): return lax.ppermute(values, axis, [(s, s ^ bit) for s in range(n)])  32.4 us
    pallas_call x21, Pallas kernels, in_vmem(): pl.pallas_call(run, in_specs=[SMEM] * scalars + [HBM] * streamed + [VMEM]...  26.6 us
    unnamed x21, local copies, waits for them, and re-layouts  5.4 us
    pallas_call x4, Pallas kernels, finish(): pl.pallas_call(finish_kernel, grid=(count // block,), in_specs=[spec, spe...  3.75 us
  transfers between devices with their start and end apart: 23, of which 16 were waited for; matrix products, arithmetic and copies ran while one was open for 0% of the time, Pallas kernels for 19%

profile of v5, /device:TPU:0, one launch (start us, length us, event | category | flops | bytes accessed | tf_op | source)
XLA Modules:
  0.0 112.7 jit_solution(8592326287019246353)
XLA Ops:
  3.3 2.8 %copy-done.8 = bf16[16,256,768]{2,1,0:T(8,128)(2,1)S(1)} copy-done((bf16[16,256,768]{2,1,0:T(8,128)(2,1)S(1)}, bf16[16,256,768]{2,1,0:T(8,128)(2,1)}, u32[]{:S(2)}) %copy-start.8) | copy-done | bytes 6291480
  6.1 5.1 %query_key.1 = (bf16[16,6,64,256]{3,2,1,0:T(8,128)(2,1)S(1)}, bf16[16,256,768]{2,1,0:T(8,128)(2,1)S(1)}, f32[4,3,32,256]{3,2,1,0:T(8,128)S(1)}, bf16[4,3,32,256]{3,2,1,0:T(8,128)(2,1)S(1)}) custom-call(s32[16]{0:T(128)S(1)} %copy-done.6, s32[2]{0:T(128)S(1)} %pad_add_fusion.refs_1_.refs_0_, bf16[16,256,768]{2,1,0:T(8,128)(2,1)S(1)} %copy-done.8, ...), custom_call_target="tpu_custom_call" | custom-call | flops 2818572288 | bytes 16711716 | tf_op jit(solution)/shard_map/query_key/pallas_call | solution.py:52
  11.2 3.0 %collective-permute-start = (bf16[4,3,32,256]{3,2,1,0:T(8,128)(2,1)S(1)}, bf16[4,3,32,256]{3,2,1,0:T(8,128)(2,1)S(1)}, u32[]{:S(2)}, u32[]{:S(2)}) collective-permute-start(bf16[4,3,32,256]{3,2,1,0:T(8,128)(2,1)S(1)} %get-tuple-element.47.refs_5_), channel_id=1, source_target_pairs={{0,4},{4,0},{8,12},{12,8},{16,20},{20,16},{24,28},{28,24},{1,5},{5... | collective-permute-start | bytes 589832 | tf_op jit(solution)/shard_map/ppermute | solution.py:27
  14.2 3.5 %value_dprob.1 = (f32[4,3,32,256]{3,2,1,0:T(8,128)S(1)}, bf16[4,3,32,256]{3,2,1,0:T(8,128)(2,1)S(1)}) custom-call(s32[16]{0:T(128)S(1)} %copy-done.6, s32[2]{0:T(128)S(1)} %pad_add_fusion.refs_1_.refs_0_, bf16[16,256,768]{2,1,0:T(8,128)(2,1)S(1)} %get-tuple-element.52.refs_2_.refs_1_, bf16[192,768]{1,0:T(8,128)(2,1)S(1)} %bitcast.13, ...), custom_call_target="tpu_custom_call" | custom-call | flops 1610612736 | bytes 8552484 | tf_op jit(solution)/shard_map/value_dprob/pallas_call | solution.py:52
  19.2 1.9 %collective-permute-start.1 = (bf16[2,3,32,256]{3,2,1,0:T(8,128)(2,1)S(1)}, bf16[2,3,32,256]{3,2,1,0:T(8,128)(2,1)S(1)}, u32[]{:S(2)}, u32[]{:S(2)}) collective-permute-start(bf16[2,3,32,256]{3,2,1,0:T(8,128)(2,1)S(1)} %get-tuple-element.49), channel_id=1, source_target_pairs={{0,8},{4,12},{8,0},{12,4},{16,24},{20,28},{24,16},{28,20},{1,9},{5... | collective-permute-start | bytes 294920 | tf_op jit(solution)/shard_map/ppermute | solution.py:27
  21.1 3.1 %collective-permute-done.3.refs_1_ = bf16[4,3,32,256]{3,2,1,0:T(8,128)(2,1)S(1)} collective-permute-done((bf16[4,3,32,256]{3,2,1,0:T(8,128)(2,1)S(1)}, bf16[4,3,32,256]{3,2,1,0:T(8,128)(2,1)S(1)}, u32[]{:S(2)}, u32[]{:S(2)}) %collective-permute-start.3) | collective-permute-done | bytes 196640 | tf_op jit(solution)/shard_map/ppermute | solution.py:27
  25.9 2.7 %collective-permute-start.2 = (bf16[1,3,32,256]{3,2,1,0:T(8,128)(2,1)S(1)}, bf16[1,3,32,256]{3,2,1,0:T(8,128)(2,1)S(1)}, u32[]{:S(2)}, u32[]{:S(2)}) collective-permute-start(bf16[1,3,32,256]{3,2,1,0:T(8,128)(2,1)S(1)} %get-tuple-element.51), channel_id=1, source_target_pairs={{0,16},{4,20},{8,24},{12,28},{16,0},{20,4},{24,8},{28,12},{1,17},{... | collective-permute-start | bytes 147464 | tf_op jit(solution)/shard_map/ppermute | solution.py:27
  29.4 2.2 %collective-permute-start.5 = (bf16[1,3,32,256]{3,2,1,0:T(8,128)(2,1)S(1)}, bf16[1,3,32,256]{3,2,1,0:T(8,128)(2,1)S(1)}, u32[]{:S(2)}, u32[]{:S(2)}) collective-permute-start(bf16[1,3,32,256]{3,2,1,0:T(8,128)(2,1)S(1)} %get-tuple-element.58), channel_id=1, source_target_pairs={{0,16},{4,20},{8,24},{12,28},{16,0},{20,4},{24,8},{28,12},{1,17},{... | collective-permute-start | bytes 147464 | tf_op jit(solution)/shard_map/ppermute | solution.py:27
  32.3 2.1 %collective-permute-done.5.refs_3_ = bf16[1,3,32,256]{3,2,1,0:T(8,128)(2,1)S(1)} collective-permute-done((bf16[1,3,32,256]{3,2,1,0:T(8,128)(2,1)S(1)}, bf16[1,3,32,256]{3,2,1,0:T(8,128)(2,1)S(1)}, u32[]{:S(2)}, u32[]{:S(2)}) %collective-permute-start.5) | collective-permute-done | bytes 49184 | tf_op jit(solution)/shard_map/ppermute | solution.py:27
  34.7 2.2 %collective-permute-start.6 = (bf16[1,3,32,256]{3,2,1,0:T(8,128)(2,1)S(1)}, bf16[1,3,32,256]{3,2,1,0:T(8,128)(2,1)S(1)}, u32[]{:S(2)}, u32[]{:S(2)}) collective-permute-start(bf16[1,3,32,256]{3,2,1,0:T(8,128)(2,1)S(1)} %get-tuple-element.59), channel_id=1, source_target_pairs={{0,16},{4,20},{8,24},{12,28},{16,0},{20,4},{24,8},{28,12},{1,17},{... | collective-permute-start | bytes 147464 | tf_op jit(solution)/shard_map/ppermute | solution.py:27
  37.8 2.0 %collective-permute-done.6 = bf16[1,3,32,256]{3,2,1,0:T(8,128)(2,1)S(1)} collective-permute-done((bf16[1,3,32,256]{3,2,1,0:T(8,128)(2,1)S(1)}, bf16[1,3,32,256]{3,2,1,0:T(8,128)(2,1)S(1)}, u32[]{:S(2)}, u32[]{:S(2)}) %collective-permute-start.6) | collective-permute-done | bytes 49184 | tf_op jit(solution)/shard_map/ppermute | solution.py:27
  39.8 2.2 %collective-permute-start.7 = (bf16[2,3,32,256]{3,2,1,0:T(8,128)(2,1)S(1)}, bf16[2,3,32,256]{3,2,1,0:T(8,128)(2,1)S(1)}, u32[]{:S(2)}, u32[]{:S(2)}) collective-permute-start(bf16[2,3,32,256]{3,2,1,0:T(8,128)(2,1)S(1)} %pad_maximum_fusion), channel_id=1, source_target_pairs={{0,8},{4,12},{8,0},{12,4},{16,24},{20,28},{24,16},{28,20},{1,9},{5... | collective-permute-start | bytes 294920 | tf_op jit(solution)/shard_map/ppermute | solution.py:27
  42.1 1.9 %collective-permute-start.10 = (bf16[2,3,32,256]{3,2,1,0:T(8,128)(2,1)S(1)}, bf16[2,3,32,256]{3,2,1,0:T(8,128)(2,1)S(1)}, u32[]{:S(2)}, u32[]{:S(2)}) collective-permute-start(bf16[2,3,32,256]{3,2,1,0:T(8,128)(2,1)S(1)} %pad_maximum_fusion.1), channel_id=1, source_target_pairs={{0,8},{4,12},{8,0},{12,4},{16,24},{20,28},{24,16},{28,20},{1,9},{5... | collective-permute-start | bytes 294920 | tf_op jit(solution)/shard_map/ppermute | solution.py:27
  50.4 2.2 %collective-permute-done.11.refs_4_ = bf16[4,3,32,256]{3,2,1,0:T(8,128)(2,1)S(1)} collective-permute-done((bf16[4,3,32,256]{3,2,1,0:T(8,128)(2,1)S(1)}, bf16[4,3,32,256]{3,2,1,0:T(8,128)(2,1)S(1)}, u32[]{:S(2)}, u32[]{:S(2)}) %collective-permute-start.11) | collective-permute-done | bytes 196640 | tf_op jit(solution)/shard_map/ppermute | solution.py:27
  53.2 2.3 %backward.4 = (bf16[2,4,192,256]{3,2,1,0:T(8,128)(2,1)S(1)}, bf16[2,4,192,256]{3,2,1,0:T(8,128)(2,1)S(1)}, bf16[4,9,64,256]{3,2,1,0:T(8,128)(2,1)S(1)}) custom-call(s32[16]{0:T(128)S(1)} %copy-done.7, bf16[8,3,32,256]{3,2,1,0:T(8,128)(2,1)S(1)} %get-tuple-element.61.refs_1_, bf16[8,3,32,256]{3,2,1,0:T(8,128)(2,1)S(1)} %get-tuple-element.62.refs_2_, ...), custom_call_target="tpu_custom_call" | custom-call | flops 1207959552 | bytes 9142304 | tf_op jit(solution)/shard_map/backward/pallas_call | solution.py:52
  58.0 3.0 %backward.5 = (bf16[2,6,192,256]{3,2,1,0:T(8,128)(2,1)S(1)}, bf16[2,6,192,256]{3,2,1,0:T(8,128)(2,1)S(1)}, bf16[6,9,64,256]{3,2,1,0:T(8,128)(2,1)S(1)}) custom-call(s32[16]{0:T(128)S(1)} %copy-done.7, bf16[8,3,32,256]{3,2,1,0:T(8,128)(2,1)S(1)} %get-tuple-element.61.refs_1_, bf16[8,3,32,256]{3,2,1,0:T(8,128)(2,1)S(1)} %get-tuple-element.62.refs_2_, ...), custom_call_target="tpu_custom_call" | custom-call | flops 1811939328 | bytes 10518560 | tf_op jit(solution)/shard_map/backward/pallas_call | solution.py:52
  62.9 2.5 %backward.7 = (bf16[2,4,192,256]{3,2,1,0:T(8,128)(2,1)S(1)}, bf16[2,4,192,256]{3,2,1,0:T(8,128)(2,1)S(1)}, bf16[4,9,64,256]{3,2,1,0:T(8,128)(2,1)S(1)}) custom-call(s32[16]{0:T(128)S(1)} %copy-done.7, bf16[8,3,32,256]{3,2,1,0:T(8,128)(2,1)S(1)} %get-tuple-element.61.refs_1_, bf16[8,3,32,256]{3,2,1,0:T(8,128)(2,1)S(1)} %get-tuple-element.62.refs_2_, ...), custom_call_target="tpu_custom_call" | custom-call | flops 1207959552 | bytes 9142304 | tf_op jit(solution)/shard_map/backward/pallas_call | solution.py:52
  65.6 3.0 %collective-permute-done.19.got.refs_6_ = bf16[1,2,192,256]{3,2,1,0:T(8,128)(2,1)S(1)} collective-permute-done((bf16[1,2,192,256]{3,2,1,0:T(8,128)(2,1)S(1)}, bf16[1,2,192,256]{3,2,1,0:T(8,128)(2,1)S(1)}, u32[]{:S(2)}, u32[]{:S(2)}) %collective-permute-start.19) | collective-permute-done | bytes 196640 | tf_op jit(solution)/shard_map/ppermute | solution.py:27
  68.6 4.7 %weight_part.1 = (f32[4,96,576]{2,1,0:T(8,128)S(1)}, bf16[4,96,576]{2,1,0:T(8,128)(2,1)S(1)}) custom-call(s32[2]{0:T(128)S(1)} %pad_add_fusion.refs_1_.refs_0_, bf16[16,256,768]{2,1,0:T(8,128)(2,1)S(1)} %get-tuple-element.52.refs_2_.refs_1_, bf16[2,9,64,256]{3,2,1,0:T(8,128)(2,1)S(1)} %get-tuple-element.80.refs_2_, ...), custom_call_target="tpu_custom_call" | custom-call | flops 3623878656 | bytes 11894788 | tf_op jit(solution)/shard_map/weight_part/pallas_call | solution.py:52
  78.5 7.9 %collective-permute-done.18.got.refs_2_ = bf16[1,4,192,256]{3,2,1,0:T(8,128)(2,1)S(1)} collective-permute-done((bf16[1,4,192,256]{3,2,1,0:T(8,128)(2,1)S(1)}, bf16[1,4,192,256]{3,2,1,0:T(8,128)(2,1)S(1)}, u32[]{:S(2)}, u32[]{:S(2)}) %collective-permute-start.18) | collective-permute-done | bytes 393248 | tf_op jit(solution)/shard_map/ppermute | solution.py:27
  86.6 2.1 %collective-permute-start.21 = (bf16[2,96,576]{2,1,0:T(8,128)(2,1)S(1)}, bf16[2,96,576]{2,1,0:T(8,128)(2,1)S(1)}, u32[]{:S(2)}, u32[]{:S(2)}) collective-permute-start(bf16[2,96,576]{2,1,0:T(8,128)(2,1)S(1)} %get-tuple-element.87), channel_id=1, source_target_pairs={{0,8},{4,12},{8,0},{12,4},{16,24},{20,28},{24,16},{28,20},{1,9},{5... | collective-permute-start | bytes 663560 | tf_op jit(solution)/shard_map/ppermute | solution.py:27
  88.6 4.3 %collective-permute-done.21.refs_1_ = bf16[2,96,576]{2,1,0:T(8,128)(2,1)S(1)} collective-permute-done((bf16[2,96,576]{2,1,0:T(8,128)(2,1)S(1)}, bf16[2,96,576]{2,1,0:T(8,128)(2,1)S(1)}, u32[]{:S(2)}, u32[]{:S(2)}) %collective-permute-start.21) | collective-permute-done | bytes 221216 | tf_op jit(solution)/shard_map/ppermute | solution.py:27
  92.9 12.8 %collective-permute-done.17.got.refs_2_ = bf16[1,4,192,256]{3,2,1,0:T(8,128)(2,1)S(1)} collective-permute-done((bf16[1,4,192,256]{3,2,1,0:T(8,128)(2,1)S(1)}, bf16[1,4,192,256]{3,2,1,0:T(8,128)(2,1)S(1)}, u32[]{:S(2)}, u32[]{:S(2)}) %collective-permute-start.17) | collective-permute-done | bytes 393248 | tf_op jit(solution)/shard_map/ppermute | solution.py:27
  105.8 2.4 %collective-permute-start.22 = (bf16[1,96,576]{2,1,0:T(8,128)(2,1)S(1)}, bf16[1,96,576]{2,1,0:T(8,128)(2,1)S(1)}, u32[]{:S(2)}, u32[]{:S(2)}) collective-permute-start(bf16[1,96,576]{2,1,0:T(8,128)(2,1)S(1)} %get-tuple-element.89), channel_id=1, source_target_pairs={{0,16},{4,20},{8,24},{12,28},{16,0},{20,4},{24,8},{28,12},{1,17},{... | collective-permute-start | bytes 331784 | tf_op jit(solution)/shard_map/ppermute | solution.py:27
  (73 shorter events, 30.0 us)
Async XLA Ops:
  11.2 7.9 %collective-permute-start = (bf16[4,3,32,256]{3,2,1,0:T(8,128)(2,1)S(1)}, bf16[4,3,32,256]{3,2,1,0:T(8,128)(2,1)S(1)}, u32[]{:S(2)}, u32[]{:S(2)}) collective-permute-start(bf16[4,3,32,256]{3,2,1,0:T(8,128)(2,1)S(1)} %get-tuple-element.47.refs_5_), channel_id=1, source_target_pairs={{0,4},{4,0},{8,12},{12,8},{16,20},{20,16},{24,28},{28,24},{1,5},{5... | collective-permute-start | bytes 589832 | tf_op jit(solution)/shard_map/ppermute | solution.py:27
  17.8 6.4 %collective-permute-start.3 = (bf16[4,3,32,256]{3,2,1,0:T(8,128)(2,1)S(1)}, bf16[4,3,32,256]{3,2,1,0:T(8,128)(2,1)S(1)}, u32[]{:S(2)}, u32[]{:S(2)}) collective-permute-start(bf16[4,3,32,256]{3,2,1,0:T(8,128)(2,1)S(1)} %get-tuple-element.54.refs_4_), channel_id=1, source_target_pairs={{0,4},{4,0},{8,12},{12,8},{16,20},{20,16},{24,28},{28,24},{1,5},{5... | collective-permute-start | bytes 589832 | tf_op jit(solution)/shard_map/ppermute | solution.py:27
  19.1 28.8 %copy-start.5 = (bf16[768,192]{0,1:T(8,128)(2,1)S(1)}, bf16[768,192]{0,1:T(8,128)(2,1)}, u32[]{:S(2)}) copy-start(bf16[768,192]{0,1:T(8,128)(2,1)} %param.8) | copy-start | bytes 884740
  19.2 6.7 %collective-permute-start.1 = (bf16[2,3,32,256]{3,2,1,0:T(8,128)(2,1)S(1)}, bf16[2,3,32,256]{3,2,1,0:T(8,128)(2,1)S(1)}, u32[]{:S(2)}, u32[]{:S(2)}) collective-permute-start(bf16[2,3,32,256]{3,2,1,0:T(8,128)(2,1)S(1)} %get-tuple-element.49), channel_id=1, source_target_pairs={{0,8},{4,12},{8,0},{12,4},{16,24},{20,28},{24,16},{28,20},{1,9},{5... | collective-permute-start | bytes 294920 | tf_op jit(solution)/shard_map/ppermute | solution.py:27
  24.2 5.2 %collective-permute-start.4 = (bf16[2,3,32,256]{3,2,1,0:T(8,128)(2,1)S(1)}, bf16[2,3,32,256]{3,2,1,0:T(8,128)(2,1)S(1)}, u32[]{:S(2)}, u32[]{:S(2)}) collective-permute-start(bf16[2,3,32,256]{3,2,1,0:T(8,128)(2,1)S(1)} %get-tuple-element.56), channel_id=1, source_target_pairs={{0,8},{4,12},{8,0},{12,4},{16,24},{20,28},{24,16},{28,20},{1,9},{5... | collective-permute-start | bytes 294920 | tf_op jit(solution)/shard_map/ppermute | solution.py:27
  25.9 6.4 %collective-permute-start.2 = (bf16[1,3,32,256]{3,2,1,0:T(8,128)(2,1)S(1)}, bf16[1,3,32,256]{3,2,1,0:T(8,128)(2,1)S(1)}, u32[]{:S(2)}, u32[]{:S(2)}) collective-permute-start(bf16[1,3,32,256]{3,2,1,0:T(8,128)(2,1)S(1)} %get-tuple-element.51), channel_id=1, source_target_pairs={{0,16},{4,20},{8,24},{12,28},{16,0},{20,4},{24,8},{28,12},{1,17},{... | collective-permute-start | bytes 147464 | tf_op jit(solution)/shard_map/ppermute | solution.py:27
  29.4 5.1 %collective-permute-start.5 = (bf16[1,3,32,256]{3,2,1,0:T(8,128)(2,1)S(1)}, bf16[1,3,32,256]{3,2,1,0:T(8,128)(2,1)S(1)}, u32[]{:S(2)}, u32[]{:S(2)}) collective-permute-start(bf16[1,3,32,256]{3,2,1,0:T(8,128)(2,1)S(1)} %get-tuple-element.58), channel_id=1, source_target_pairs={{0,16},{4,20},{8,24},{12,28},{16,0},{20,4},{24,8},{28,12},{1,17},{... | collective-permute-start | bytes 147464 | tf_op jit(solution)/shard_map/ppermute | solution.py:27
  34.7 5.1 %collective-permute-start.6 = (bf16[1,3,32,256]{3,2,1,0:T(8,128)(2,1)S(1)}, bf16[1,3,32,256]{3,2,1,0:T(8,128)(2,1)S(1)}, u32[]{:S(2)}, u32[]{:S(2)}) collective-permute-start(bf16[1,3,32,256]{3,2,1,0:T(8,128)(2,1)S(1)} %get-tuple-element.59), channel_id=1, source_target_pairs={{0,16},{4,20},{8,24},{12,28},{16,0},{20,4},{24,8},{28,12},{1,17},{... | collective-permute-start | bytes 147464 | tf_op jit(solution)/shard_map/ppermute | solution.py:27
  37.0 5.2 %collective-permute-start.9 = (bf16[1,3,32,256]{3,2,1,0:T(8,128)(2,1)S(1)}, bf16[1,3,32,256]{3,2,1,0:T(8,128)(2,1)S(1)}, u32[]{:S(2)}, u32[]{:S(2)}) collective-permute-start(bf16[1,3,32,256]{3,2,1,0:T(8,128)(2,1)S(1)} %get-tuple-element.60), channel_id=1, source_target_pairs={{0,16},{4,20},{8,24},{12,28},{16,0},{20,4},{24,8},{28,12},{1,17},{... | collective-permute-start | bytes 147464 | tf_op jit(solution)/shard_map/ppermute | solution.py:27
  39.8 4.8 %collective-permute-start.7 = (bf16[2,3,32,256]{3,2,1,0:T(8,128)(2,1)S(1)}, bf16[2,3,32,256]{3,2,1,0:T(8,128)(2,1)S(1)}, u32[]{:S(2)}, u32[]{:S(2)}) collective-permute-start(bf16[2,3,32,256]{3,2,1,0:T(8,128)(2,1)S(1)} %pad_maximum_fusion), channel_id=1, source_target_pairs={{0,8},{4,12},{8,0},{12,4},{16,24},{20,28},{24,16},{28,20},{1,9},{5... | collective-permute-start | bytes 294920 | tf_op jit(solution)/shard_map/ppermute | solution.py:27
  42.1 4.7 %collective-permute-start.10 = (bf16[2,3,32,256]{3,2,1,0:T(8,128)(2,1)S(1)}, bf16[2,3,32,256]{3,2,1,0:T(8,128)(2,1)S(1)}, u32[]{:S(2)}, u32[]{:S(2)}) collective-permute-start(bf16[2,3,32,256]{3,2,1,0:T(8,128)(2,1)S(1)} %pad_maximum_fusion.1), channel_id=1, source_target_pairs={{0,8},{4,12},{8,0},{12,4},{16,24},{20,28},{24,16},{28,20},{1,9},{5... | collective-permute-start | bytes 294920 | tf_op jit(solution)/shard_map/ppermute | solution.py:27
  44.6 5.7 %collective-permute-start.8 = (bf16[4,3,32,256]{3,2,1,0:T(8,128)(2,1)S(1)}, bf16[4,3,32,256]{3,2,1,0:T(8,128)(2,1)S(1)}, u32[]{:S(2)}, u32[]{:S(2)}) collective-permute-start(bf16[4,3,32,256]{3,2,1,0:T(8,128)(2,1)S(1)} %constant_dynamic-update-slice_fusion.refs_1_), channel_id=1, source_target_pairs={{0,4},{4,0},{8,12},{12,8},{16,20},{20,16},{24,28},{28,24},{1,5},{5... | collective-permute-start | bytes 589832 | tf_op jit(solution)/shard_map/ppermute | solution.py:27
  46.8 5.7 %collective-permute-start.11 = (bf16[4,3,32,256]{3,2,1,0:T(8,128)(2,1)S(1)}, bf16[4,3,32,256]{3,2,1,0:T(8,128)(2,1)S(1)}, u32[]{:S(2)}, u32[]{:S(2)}) collective-permute-start(bf16[4,3,32,256]{3,2,1,0:T(8,128)(2,1)S(1)} %constant_dynamic-update-slice_fusion.3.refs_3_), channel_id=1, source_target_pairs={{0,4},{4,0},{8,12},{12,8},{16,20},{20,16},{24,28},{28,24},{1,5},{5... | collective-permute-start | bytes 589832 | tf_op jit(solution)/shard_map/ppermute | solution.py:27
  55.5 2.4 %collective-permute-start.12 = (bf16[2,4,192,256]{3,2,1,0:T(8,128)(2,1)S(1)}, bf16[2,4,192,256]{3,2,1,0:T(8,128)(2,1)S(1)}, u32[]{:S(2)}, u32[]{:S(2)}) collective-permute-start(bf16[2,4,192,256]{3,2,1,0:T(8,128)(2,1)S(1)} %get-tuple-element.65), channel_id=1, source_target_pairs={{0,1},{1,0},{2,3},{3,2},{4,5},{5,4},{6,7},{7,6},{8,9},{9,8},{10,11... | collective-permute-start | bytes 2359304 | tf_op jit(solution)/shard_map/ppermute | solution.py:27
  57.2 4.0 %collective-permute-start.15 = (bf16[2,2,192,256]{3,2,1,0:T(8,128)(2,1)S(1)}, bf16[2,2,192,256]{3,2,1,0:T(8,128)(2,1)S(1)}, u32[]{:S(2)}, u32[]{:S(2)}) collective-permute-start(bf16[2,2,192,256]{3,2,1,0:T(8,128)(2,1)S(1)} %get-tuple-element.72), channel_id=1, source_target_pairs={{0,1},{1,0},{2,3},{3,2},{4,5},{5,4},{6,7},{7,6},{8,9},{9,8},{10,11... | collective-permute-start | bytes 1179656 | tf_op jit(solution)/shard_map/ppermute | solution.py:27
  61.0 14.9 %collective-permute-start.13 = (bf16[2,6,192,256]{3,2,1,0:T(8,128)(2,1)S(1)}, bf16[2,6,192,256]{3,2,1,0:T(8,128)(2,1)S(1)}, u32[]{:S(2)}, u32[]{:S(2)}) collective-permute-start(bf16[2,6,192,256]{3,2,1,0:T(8,128)(2,1)S(1)} %get-tuple-element.68), channel_id=1, source_target_pairs={{0,1},{1,0},{2,3},{3,2},{4,5},{5,4},{6,7},{7,6},{8,9},{9,8},{10,11... | collective-permute-start | bytes 3538952 | tf_op jit(solution)/shard_map/ppermute | solution.py:27
  61.3 7.2 %collective-permute-start.19 = (bf16[1,2,192,256]{3,2,1,0:T(8,128)(2,1)S(1)}, bf16[1,2,192,256]{3,2,1,0:T(8,128)(2,1)S(1)}, u32[]{:S(2)}, u32[]{:S(2)}) collective-permute-start(bf16[1,2,192,256]{3,2,1,0:T(8,128)(2,1)S(1)} %get-tuple-element.79), channel_id=1, source_target_pairs={{0,2},{1,3},{2,0},{3,1},{4,6},{5,7},{6,4},{7,5},{8,10},{9,11},{10,... | collective-permute-start | bytes 589832 | tf_op jit(solution)/shard_map/ppermute | solution.py:27
  65.4 11.3 %collective-permute-start.16 = (bf16[2,4,192,256]{3,2,1,0:T(8,128)(2,1)S(1)}, bf16[2,4,192,256]{3,2,1,0:T(8,128)(2,1)S(1)}, u32[]{:S(2)}, u32[]{:S(2)}) collective-permute-start(bf16[2,4,192,256]{3,2,1,0:T(8,128)(2,1)S(1)} %get-tuple-element.75), channel_id=1, source_target_pairs={{0,1},{1,0},{2,3},{3,2},{4,5},{5,4},{6,7},{7,6},{8,9},{9,8},{10,11... | collective-permute-start | bytes 2359304 | tf_op jit(solution)/shard_map/ppermute | solution.py:27
  73.3 13.1 %collective-permute-start.20 = (bf16[4,96,576]{2,1,0:T(8,128)(2,1)S(1)}, bf16[4,96,576]{2,1,0:T(8,128)(2,1)S(1)}, u32[]{:S(2)}, u32[]{:S(2)}) collective-permute-start(bf16[4,96,576]{2,1,0:T(8,128)(2,1)S(1)} %get-tuple-element.85), channel_id=1, source_target_pairs={{0,4},{4,0},{8,12},{12,8},{16,20},{20,16},{24,28},{28,24},{1,5},{5... | collective-permute-start | bytes 1327112 | tf_op jit(solution)/shard_map/ppermute | solution.py:27
  74.4 12.1 %collective-permute-start.18 = (bf16[1,4,192,256]{3,2,1,0:T(8,128)(2,1)S(1)}, bf16[1,4,192,256]{3,2,1,0:T(8,128)(2,1)S(1)}, u32[]{:S(2)}, u32[]{:S(2)}) collective-permute-start(bf16[1,4,192,256]{3,2,1,0:T(8,128)(2,1)S(1)} %get-tuple-element.78), channel_id=1, source_target_pairs={{0,2},{1,3},{2,0},{3,1},{4,6},{5,7},{6,4},{7,5},{8,10},{9,11},{10,... | collective-permute-start | bytes 1179656 | tf_op jit(solution)/shard_map/ppermute | solution.py:27
  76.2 34.3 %collective-permute-start.14 = (bf16[1,6,192,256]{3,2,1,0:T(8,128)(2,1)S(1)}, bf16[1,6,192,256]{3,2,1,0:T(8,128)(2,1)S(1)}, u32[]{:S(2)}, u32[]{:S(2)}) collective-permute-start(bf16[1,6,192,256]{3,2,1,0:T(8,128)(2,1)S(1)} %get-tuple-element.70), channel_id=1, source_target_pairs={{0,2},{1,3},{2,0},{3,1},{4,6},{5,7},{6,4},{7,5},{8,10},{9,11},{10,... | collective-permute-start | bytes 1769480 | tf_op jit(solution)/shard_map/ppermute | solution.py:27
  76.9 28.8 %collective-permute-start.17 = (bf16[1,4,192,256]{3,2,1,0:T(8,128)(2,1)S(1)}, bf16[1,4,192,256]{3,2,1,0:T(8,128)(2,1)S(1)}, u32[]{:S(2)}, u32[]{:S(2)}) collective-permute-start(bf16[1,4,192,256]{3,2,1,0:T(8,128)(2,1)S(1)} %get-tuple-element.77), channel_id=1, source_target_pairs={{0,2},{1,3},{2,0},{3,1},{4,6},{5,7},{6,4},{7,5},{8,10},{9,11},{10,... | collective-permute-start | bytes 1179656 | tf_op jit(solution)/shard_map/ppermute | solution.py:27
  86.6 6.4 %collective-permute-start.21 = (bf16[2,96,576]{2,1,0:T(8,128)(2,1)S(1)}, bf16[2,96,576]{2,1,0:T(8,128)(2,1)S(1)}, u32[]{:S(2)}, u32[]{:S(2)}) collective-permute-start(bf16[2,96,576]{2,1,0:T(8,128)(2,1)S(1)} %get-tuple-element.87), channel_id=1, source_target_pairs={{0,8},{4,12},{8,0},{12,4},{16,24},{20,28},{24,16},{28,20},{1,9},{5... | collective-permute-start | bytes 663560 | tf_op jit(solution)/shard_map/ppermute | solution.py:27
  105.8 6.1 %collective-permute-start.22 = (bf16[1,96,576]{2,1,0:T(8,128)(2,1)S(1)}, bf16[1,96,576]{2,1,0:T(8,128)(2,1)S(1)}, u32[]{:S(2)}, u32[]{:S(2)}) collective-permute-start(bf16[1,96,576]{2,1,0:T(8,128)(2,1)S(1)} %get-tuple-element.89), channel_id=1, source_target_pairs={{0,16},{4,20},{8,24},{12,28},{16,0},{20,4},{24,8},{28,12},{1,17},{... | collective-permute-start | bytes 331784 | tf_op jit(solution)/shard_map/ppermute | solution.py:27
  (8 other events, 59.0 us)

commit v6 on v5

--- a/solution.py
+++ b/solution.py
@@ -39,6 +39,10 @@
 
 def like(shape, dtype=BF16):
     return jax.ShapeDtypeStruct(shape, dtype)
+
+
+def place(a, stays):
+    return pltpu.with_memory_space_constraint(a, pltpu.HBM) if stays else a
 
 
 def in_vmem(kernel, name, out, *operands, scalars=0, streamed=0, after=(), scratch=(), limit=12, flops=0):
@@ -58,7 +62,7 @@
         compiler_params=pltpu.CompilerParams(vmem_limit_bytes=limit * MIB),
         cost_estimate=cost(flops, moved),
         name=name,
-    )(*operands, *after)
+    )(*[place(a, scalars <= i < scalars + streamed) for i, a in enumerate(operands)], *after)
 
 
 def lane_mask(length, cols):
@@ -125,7 +129,7 @@
             pltpu.VMEM((heads, shards, cols // shards, cols), F32),
             pltpu.SemaphoreType.DMA((2 + rows // BLOCK,)),
         ),
-        limit=16,
+        limit=46,
         flops=2 * rows * cols * local * (2 * width + cols),
     )
 
@@ -174,24 +178,51 @@
     local = wq.shape[0]
     for index, weight in enumerate((wq, wk, wv)):
         turned[:, :, index * local : (index + 1) * local] = weight[...].T.reshape(turned.shape[:2] + (local,))
-    for j in range(turned.shape[0]):
+    for j in range(natural.shape[0]):
         natural[j] = turned[me[1] ^ j]
 
 
 def turn(me, wq, wk, wv, devices, after):
     local, width = wq.shape
-    shape = (devices, width // devices, 3 * local)
+    shape = (width // devices, 3 * local)
     return in_vmem(
         turn_kernel,
         "turn",
-        (like(shape),),
+        (like((2,) + shape),),
         me,
         wq,
         wk,
         wv,
         scalars=1,
         after=after,
-        scratch=(pltpu.VMEM(shape, BF16),),
+        scratch=(pltpu.VMEM((devices,) + shape, BF16),),
+    )[0]
+
+
+def far_query_key_kernel(lengths, sheet, wq, wk, qk):
+    rows, cols, _ = sheet.shape
+    local = wq.shape[0]
+    heads = local // HEAD_DIM
+    both = jnp.concatenate([wq[...], wk[...]], axis=0)
+    for r in range(rows):
+        value = (mm(both, sheet[r], NT) * lane_mask(lengths[r], cols)).astype(BF16)
+        qk[r] = value.reshape(2 * heads, HEAD_DIM, cols)
+
+
+def far_query_key(lengths, sheet, wq, wk, after):
+    rows, cols, width = sheet.shape
+    local = wq.shape[0]
+    return in_vmem(
+        far_query_key_kernel,
+        "far_query_key",
+        (like((rows, 2 * local // HEAD_DIM, HEAD_DIM, cols)),),
+        lengths,
+        sheet,
+        wq,
+        wk,
+        scalars=1,
+        after=after,
+        flops=4 * rows * cols * local * width,
     )[0]
 
 
@@ -266,10 +297,9 @@
     )
 
 
-def backward_kernel(first, lengths, probs, dscore, qk, cot, weights, *rest):
-    blocks, grads = rest[:-1], rest[-1]
-    count, all_heads, _, cols = grads.shape
-    heads = all_heads // 3
+def gradients(lengths, first, count, probs, dscore, qk, cot, grads):
+    cols = qk.shape[-1]
+    heads = qk.shape[1] // 2
     rows = pl.ds(first, count)
     flat = (count * HEAD_DIM, cols)
     split = (count, HEAD_DIM, cols)
@@ -282,45 +312,95 @@
         dv = mm(g, p, NN)
         for index, value in enumerate((dq, dk, dv)):
             grads[:, index * heads + h] = (value.reshape(split) * masks).astype(BF16)
-    devices, share, columns = weights.shape
-    left = weights[...].reshape(devices * share, columns)
-    for r in range(count):
-        part = mm(left, grads[r].reshape(columns, cols), NN).astype(BF16)
-        for j in range(devices):
-            blocks[j % 2][j // 2, r] = part[j * share : (j + 1) * share]
-
-
-def backward(first, count, lengths, probs, dscore, qk, cot, weights, after):
-    cols = qk.shape[-1]
-    heads = qk.shape[1] // 2
-    devices, share, columns = weights.shape
-    half = like((devices // 2, count, share, cols))
-    return in_vmem(
-        functools.partial(backward_kernel, first),
-        "backward",
-        (half, half, like((count, 3 * heads, HEAD_DIM, cols))),
+
+
+def own_gradients_kernel(lengths, probs, dscore, qk, cot, grads):
+    gradients(lengths, 0, qk.shape[0], probs, dscore, qk, cot, grads)
+
+
+def own_gradients(lengths, probs, dscore, qk, cot):
+    rows, two, _, cols = qk.shape
+    return in_vmem(
+        own_gradients_kernel,
+        "own_gradients",
+        (like((rows, two // 2 * 3, HEAD_DIM, cols)),),
         lengths,
         probs,
         dscore,
         qk,
         cot,
+        scalars=1,
+        limit=24,
+        flops=3 * rows * two * HEAD_DIM * cols * cols,
+    )[0]
+
+
+def own_input_kernel(grads, weights, out):
+    near, share, columns = weights.shape
+    left = weights[...].reshape(near * share, columns)
+    for r in range(grads.shape[0]):
+        part = mm(left, grads[r].reshape(columns, grads.shape[-1]), NN).astype(BF16)
+        out[:, r] = part.reshape(near, share, grads.shape[-1])
+
+
+def own_input(grads, weights, after):
+    rows, cols = grads.shape[0], grads.shape[-1]
+    near, share, columns = weights.shape
+    return in_vmem(
+        own_input_kernel,
+        "own_input",
+        (like((near, rows, share, cols)),),
+        grads,
         weights,
+        after=after,
+        flops=2 * rows * cols * near * share * columns,
+    )[0]
+
+
+def far_input_kernel(first, lengths, own, *refs):
+    *refs, keep, give, grads = refs
+    count, share, cols = keep.shape
+    total = [own[:, first + r].astype(F32) for r in range(count)]
+    for i in range(0, len(refs), 5):
+        probs, dscore, qk, cot, weights = refs[i : i + 5]
+        gradients(lengths, first, count, probs, dscore, qk, cot, grads)
+        near, _, columns = weights.shape
+        left = weights[...].reshape(near * share, columns)
+        for r in range(count):
+            part = mm(left, grads[r].reshape(columns, cols), NN).astype(BF16)
+            total[r] = total[r] + part.reshape(near, share, cols).astype(F32)
+    for r in range(count):
+        keep[r] = total[r][0].astype(keep.dtype)
+        give[r] = total[r][1].astype(give.dtype)
+
+
+def far_input(first, count, lengths, own, far):
+    _, rows, share, cols = own.shape
+    columns = far[0][-1].shape[-1]
+    out = like((count, share, cols))
+    return in_vmem(
+        functools.partial(far_input_kernel, first),
+        "far_input",
+        (out, out),
+        lengths,
+        own,
+        *[a for one in far for a in one],
         scalars=1,
-        after=after,
+        scratch=(pltpu.VMEM((count, columns // HEAD_DIM, HEAD_DIM, cols), BF16),),
         limit=16,
-        flops=2 * count * cols * columns * (cols + devices * share),
+        flops=2 * len(far) * count * cols * columns * (cols + 2 * share),
     )
 
 
 def finish_kernel(keep, got, *rest):
     out = rest[-1]
-    out[...] = (keep[0].astype(F32) + got[0].astype(F32)).astype(BF16)
+    out[...] = (keep[...].astype(F32) + got[...].astype(F32)).astype(BF16)
 
 
 def finish(keep, got, first, total_rows, before):
-    _, count, share, cols = keep.shape
+    count, share, cols = keep.shape
     block = math.gcd(first, count) if first else count
-    spec = pl.BlockSpec((1, block, share, cols), lambda s: (0, s, 0, 0))
+    spec = pl.BlockSpec((block, share, cols), lambda s: (s, 0, 0))
     extra = [] if before is None else [before]
     return pl.pallas_call(
         finish_kernel,
@@ -335,60 +415,62 @@
     )(keep, got, *extra)
 
 
-def weight_kernel(me, sheet, *refs):
-    *grads, keep, give, turned = refs
+def weight_product(sheet, grads, first, count):
     rows, cols, width = sheet.shape
-    n = grads[0].shape[1] * HEAD_DIM
-    left = [g[r].reshape(n, cols) for g in grads for r in range(g.shape[0])]
-    total = mm(jnp.concatenate(left, axis=1), sheet[...].reshape(rows * cols, width), NN)
-    turned[...] = total.T.reshape(turned.shape)
+    columns = grads.shape[1] * HEAD_DIM
+    left = [grads[r].reshape(columns, cols)[first : first + count] for r in range(rows)]
+    return mm(jnp.concatenate(left, axis=1), sheet[...].reshape(rows * cols, width), NN).T
+
+
+def weight_kernel(first, me, sheet, grads, keep, give, turned):
+    total = weight_product(sheet, grads, first, turned.shape[-1])
+    turned[...] = total.reshape(turned.shape)
     for j in range(turned.shape[0]):
         out = (keep, give)[j % 2]
         out[j // 2] = turned[me[0] ^ j].astype(out.dtype)
 
 
-def whole_weight_kernel(me, sheet, *refs):
-    *grads, out = refs
+def whole_weight_kernel(first, me, sheet, grads, out):
+    out[...] = weight_product(sheet, grads, first, out.shape[-1])
+
+
+def weight_part(me, sheet, grads, first, count, shards, after):
     rows, cols, width = sheet.shape
-    n = grads[0].shape[1] * HEAD_DIM
-    left = [g[r].reshape(n, cols) for g in grads for r in range(g.shape[0])]
-    out[...] = mm(jnp.concatenate(left, axis=1), sheet[...].reshape(rows * cols, width), NN).T
-
-
-def weight_part(me, sheet, grads, shards, after):
-    rows, cols, width = sheet.shape
-    columns = grads[0].shape[1] * HEAD_DIM
     if shards == 1:
-        kernel, outs, scratch = whole_weight_kernel, [like((width, columns), F32)], ()
+        kernel, outs, scratch = whole_weight_kernel, [like((width, count), F32)], ()
     else:
-        half = (shards // 2, width // shards, columns)
+        half = (shards // 2, width // shards, count)
         kernel, outs = weight_kernel, [like(half, F32), like(half)]
         scratch = (pltpu.VMEM((shards,) + half[1:], F32),)
     return in_vmem(
-        kernel,
+        functools.partial(kernel, first),
         "weight_part",
         outs,
         me,
         sheet,
-        *grads,
+        grads,
         scalars=1,
         after=after,
         scratch=scratch,
         limit=24,
-        flops=2 * rows * cols * width * columns,
-    )
-
-
-def last_kernel(keep, got, out):
-    total = keep[0] + got[0].astype(F32)
+        flops=2 * rows * cols * width * count,
+    )
+
+
+def last_kernel(*refs):
+    *terms, out = refs
+    total = [terms[i][0] + terms[i + 1][0].astype(F32) for i in range(0, len(terms), 2)]
+    total = jnp.concatenate(total, axis=-1)
     local = out.shape[-1]
     for index in range(out.shape[0]):
         out[index] = total[:, index * local : (index + 1) * local]
 
 
-def last_sum(keep, got, local, after):
-    shape = (keep.shape[2] // local, keep.shape[1], local)
-    return in_vmem(last_kernel, "last_sum", (like(shape, F32),), keep, got, after=after)[0]
+def last_sum(halves, local, after):
+    terms = [a for half in halves for a in half]
+    columns = sum(keep.shape[2] for keep, _ in halves)
+    shape = (columns // local, terms[0].shape[1], local)
+    return in_vmem(last_kernel, "last_sum", (like(shape, F32),), *terms, after=after)[0]
 
 
 def body(sheet, w_query, w_key, w_value, cotangent, lengths):
@@ -400,11 +482,21 @@
     direct = n_rows <= 8
     shards = n_rows if direct else 1
     row_bits = [1 << b for b in range(n_rows.bit_length() - 1)]
-    chunks = [row_dev // 8, row_dev // 4, row_dev // 4, 3 * row_dev // 8]
+    chunk = row_dev // 4
 
     me = jnp.stack([lax.axis_index("rows"), lax.axis_index("heads")]).astype(jnp.int32)
     wq, wk, wv = w_query.T, w_key.T, w_value.T
     cot = jnp.swapaxes(cotangent, 1, 2)
+
+    fars = range(2, n_heads, 2)
+    groups = [list(range(core, n_heads, 2)) for core in range(2)]
+    wqa, wka, wva, cota = [
+        lax.all_gather(a, "heads", axis_index_groups=groups) for a in (wq, wk, wv, cot)
+    ]
+    side = lax.shift_right_logical(lax.axis_index("heads").astype(jnp.int32), 1)
+    take = lambda a, f: lax.dynamic_index_in_dim(a, side ^ (f // 2), 0, keepdims=False)
+    far_weights = [[take(w, f) for w in (wqa, wka, wva)] for f in fars]
+    far_cot = [take(cota, f) for f in fars]
 
     qk, held, *logits = query_key(lengths, me, sheet, wq, wk, shards)
     dprob = value_dprob(lengths, me, held, wv, cot, logits[-1:], shards)
@@ -419,34 +511,31 @@
     else:
         logits, dprob = lax.psum((logits, dprob), "rows")
         probs, dscore = softmax_back(logits, dprob, scale)
-
-    grads, adds, last = [], [], []
-    first = 0
-    for chunk in chunks:
-        after = adds[-2:-1]
-        keep, give, grad = backward(first, chunk, lengths, probs, dscore, qk, cot, weights, after)
-        grads.append(grad)
-        bit = 1
-        while bit * 2 < n_heads:
-            give, keep = add_split(keep, flip(give, "heads", bit))
-            bit *= 2
-        adds.append(keep)
-        last.append((keep, flip(give, "heads", bit), first))
-        first += chunk
-
-    arrived = [got for _, got, _ in last]
-    parts = weight_part(me, held, grads, shards, arrived[:1])
+    far_dscore = [flip(dscore, "heads", f) for f in fars]
+    far_probs = [flip(probs, "heads", f) for f in fars]
+
+    grads = own_gradients(lengths, probs, dscore, qk, cot)
+    half = 3 * local // 2
+    parts = [weight_part(me, held, grads, first, half, shards, ()) for first in (0, half)]
+    ready = [parts[1][-1]]
     if direct:
-        parts = halve(*parts, "rows", row_bits, [arrived[1:2], arrived[2:3]])
-        weight_grad = last_sum(*parts, local, arrived[3:])
-        weight_grad = jnp.swapaxes(weight_grad, 0, 1)
+        parts = [halve(*part, "rows", row_bits) for part in parts]
+        weight_grad = jnp.swapaxes(last_sum(parts, local, ()), 0, 1)
     else:
-        weight_grad = lax.psum_scatter(parts[0], "rows", scatter_dimension=0, tiled=True)
+        part = jnp.concatenate([p[0] for p in parts], axis=1)
+        weight_grad = lax.psum_scatter(part, "rows", scatter_dimension=0, tiled=True)
         weight_grad = weight_grad.reshape(width // n_rows, 3, local)
 
+    far = []
+    for index, (fq, fk, fv) in enumerate(far_weights):
+        far_qk = far_query_key(lengths, held, fq, fk, ready)
+        far_natural = turn(me, fq, fk, fv, n_heads, ready)
+        far.append((far_probs[index], far_dscore[index], far_qk, far_cot[index], far_natural))
+    own = own_input(grads, weights, ready)
     out = None
-    for keep, got, first in last:
-        out = finish(keep, got, first, row_dev, out)
+    for first in range(0, row_dev, chunk):
+        keep, give = far_input(first, chunk, lengths, own, far)
+        out = finish(keep, flip(give, "heads", 1), first, row_dev, out)
     return (jnp.swapaxes(out, 1, 2), weight_grad)
 
 

time: 113 us -> 175 us (1.55)
  blocking collectives: 0 us -> 43.9 us
  Pallas kernels: 30.3 us -> 48.6 us
  waiting for transfers between devices: 43.7 us -> 28.9 us
  between operations: 0.81 us -> 14.3 us
  local copies, waits for them, and re-layouts: 5.41 us -> 10.7 us
  starting transfers between devices: 32.4 us -> 28.2 us
    all_gather x0 -> x3, blocking collectives: none -> 43.9 us  [body(): lax.all_gather(a, 'heads', axis_index_groups=groups)]
    pallas_call x21 -> x24, Pallas kernels: 26.6 us -> 45.2 us  [in_vmem(): pl.pallas_call(run, in_specs=[SMEM] * scalars + [HBM] * streamed + [VMEM]...]
    ppermute x23 -> x24, waiting for transfers between devices: 43.7 us -> 28.3 us  [flip(): return lax.ppermute(values, axis, [(s, s ^ bit) for s in range(n)])]
    ppermute x23 -> x24, starting transfers between devices: 32.4 us -> 28.2 us  [flip(): return lax.ppermute(values, axis, [(s, s ^ bit) for s in range(n)])]
    unnamed x21 -> x43, local copies, waits for them, and re-layouts: 5.4 us -> 8.92 us
  transfers between devices with their start and end apart: 23 -> 25, of which waited for: 16 -> 11; matrix products, arithmetic and copies ran while one was open for 0% -> 1% of each run, Pallas kernels for 19% -> 27%
where the time goes in v6:
time: 175 us
  Pallas kernels  48.6 us (28%)
  blocking collectives  43.9 us (25%)
  waiting for transfers between devices  28.9 us (17%)
  starting transfers between devices  28.2 us (16%)
  between operations  14.3 us (8%)
  local copies, waits for them, and re-layouts  10.7 us (6%)
    pallas_call x24, Pallas kernels, in_vmem(): pl.pallas_call(run, in_specs=[SMEM] * scalars + [HBM] * streamed + [VMEM]...  45.2 us
    all_gather x3, blocking collectives, body(): lax.all_gather(a, 'heads', axis_index_groups=groups)  43.9 us
    ppermute x24, waiting for transfers between devices, flip(): return lax.ppermute(values, axis, [(s, s ^ bit) for s in range(n)])  28.3 us
    ppermute x24, starting transfers between devices, flip(): return lax.ppermute(values, axis, [(s, s ^ bit) for s in range(n)])  28.2 us
    unnamed x43, local copies, waits for them, and re-layouts  8.92 us
  transfers between devices with their start and end apart: 25, of which 11 were waited for; matrix products, arithmetic and copies ran while one was open for 1% of the time, Pallas kernels for 27%

profile of v6, /device:TPU:0, one launch (start us, length us, event | category | flops | bytes accessed | tf_op | source)
XLA Modules:
  0.0 174.7 jit_solution(67972480387230637)
XLA Ops:
  8.6 8.7 %query_key.1 = (bf16[16,6,64,256]{3,2,1,0:T(8,128)(2,1)S(1)}, bf16[16,256,768]{2,1,0:T(8,128)(2,1)}, f32[4,3,32,256]{3,2,1,0:T(8,128)S(1)}, bf16[4,3,32,256]{3,2,1,0:T(8,128)(2,1)}) custom-call(s32[16]{0:T(128)S(1)} %copy-done.15, s32[2]{0:T(128)S(1)} %pad_add_fusion.refs_1_.refs_0_, bf16[16,256,768]{2,1,0:T(8,128)(2,1)} %refs_2_.1, ...), custom_call_target="tpu_custom_call" | custom-call | flops 2818572288 | bytes 16711716 | tf_op jit(solution)/shard_map/query_key/pallas_call | solution.py:56
  17.3 3.0 %collective-permute-start = (bf16[4,3,32,256]{3,2,1,0:T(8,128)(2,1)}, bf16[4,3,32,256]{3,2,1,0:T(8,128)(2,1)S(1)}, u32[]{:S(2)}, u32[]{:S(2)}) collective-permute-start(bf16[4,3,32,256]{3,2,1,0:T(8,128)(2,1)} %get-tuple-element.41.refs_5_), channel_id=1, source_target_pairs={{0,4},{4,0},{8,12},{12,8},{16,20},{20,16},{24,28},{28,24},{1,5},{5... | collective-permute-start | bytes 589832 | tf_op jit(solution)/shard_map/ppermute | solution.py:27
  20.3 3.3 %copy-done = bf16[16,256,768]{2,1,0:T(8,128)(2,1)S(1)} copy-done((bf16[16,256,768]{2,1,0:T(8,128)(2,1)S(1)}, bf16[16,256,768]{2,1,0:T(8,128)(2,1)}, u32[]{:S(2)}) %copy-start) | copy-done | bytes 6291480
  23.6 4.2 %value_dprob.1 = (f32[4,3,32,256]{3,2,1,0:T(8,128)S(1)}, bf16[4,3,32,256]{3,2,1,0:T(8,128)(2,1)}) custom-call(s32[16]{0:T(128)S(1)} %copy-done.15, s32[2]{0:T(128)S(1)} %pad_add_fusion.refs_1_.refs_0_, bf16[16,256,768]{2,1,0:T(8,128)(2,1)S(1)} %copy-done, bf16[192,768]{1,0:T(8,128)(2,1)S(1)} %bitcast.25, bf16[16,192,256]{2,1,0:T(8,128)(2,1)S(1)} %bitcast.23, ...), custom_call_target="tpu_custom_call" | custom-call | flops 1610612736 | bytes 8552484 | tf_op jit(solution)/shard_map/value_dprob/pallas_call | solution.py:56
  28.9 16.5 %all-gather.1 = bf16[384,768]{1,0:T(8,128)(2,1)} all-gather(bf16[192,768]{1,0:T(8,128)(2,1)S(1)} %bitcast.32), channel_id=3, replica_groups={{0,2},{1,3},{4,6},{5,7},{8,10},{9,11},{12,14},{13,15},{16,18},{17,19},{..., dimensions={0}, use_global_device_ids=true | all-gather | bytes 884736 | tf_op jit(solution)/shard_map/all_gather | solution.py:494
  45.3 16.2 %all-gather = bf16[384,768]{1,0:T(8,128)(2,1)S(1)} all-gather(bf16[192,768]{1,0:T(8,128)(2,1)S(1)} %bitcast.29), channel_id=2, replica_groups={{0,2},{1,3},{4,6},{5,7},{8,10},{9,11},{12,14},{13,15},{16,18},{17,19},{..., dimensions={0}, use_global_device_ids=true | all-gather | bytes 884736 | tf_op jit(solution)/shard_map/all_gather | solution.py:494
  64.7 11.2 %all-gather.3 = bf16[384,768]{1,0:T(8,128)(2,1)S(1)} all-gather(bf16[192,768]{1,0:T(8,128)(2,1)S(1)} %bitcast.26), channel_id=5, replica_groups={{0,2},{1,3},{4,6},{5,7},{8,10},{9,11},{12,14},{13,15},{16,18},{17,19},{..., dimensions={0}, use_global_device_ids=true | all-gather | bytes 884736 | tf_op jit(solution)/shard_map/all_gather | solution.py:494
  76.0 2.5 %collective-permute-start.5 = (bf16[1,3,32,256]{3,2,1,0:T(8,128)(2,1)S(1)}, bf16[1,3,32,256]{3,2,1,0:T(8,128)(2,1)S(1)}, u32[]{:S(2)}, u32[]{:S(2)}) collective-permute-start(bf16[1,3,32,256]{3,2,1,0:T(8,128)(2,1)S(1)} %get-tuple-element.52), channel_id=1, source_target_pairs={{0,16},{4,20},{8,24},{12,28},{16,0},{20,4},{24,8},{28,12},{1,17},{... | collective-permute-start | bytes 147464 | tf_op jit(solution)/shard_map/ppermute | solution.py:27
  81.4 2.1 %collective-permute-done.2.refs_1_ = bf16[1,3,32,256]{3,2,1,0:T(8,128)(2,1)S(1)} collective-permute-done((bf16[1,3,32,256]{3,2,1,0:T(8,128)(2,1)S(1)}, bf16[1,3,32,256]{3,2,1,0:T(8,128)(2,1)S(1)}, u32[]{:S(2)}, u32[]{:S(2)}) %collective-permute-start.2) | collective-permute-done | bytes 49184 | tf_op jit(solution)/shard_map/ppermute | solution.py:27
  84.4 2.5 %collective-permute-start.6 = (bf16[1,3,32,256]{3,2,1,0:T(8,128)(2,1)S(1)}, bf16[1,3,32,256]{3,2,1,0:T(8,128)(2,1)S(1)}, u32[]{:S(2)}, u32[]{:S(2)}) collective-permute-start(bf16[1,3,32,256]{3,2,1,0:T(8,128)(2,1)S(1)} %get-tuple-element.53), channel_id=1, source_target_pairs={{0,16},{4,20},{8,24},{12,28},{16,0},{20,4},{24,8},{28,12},{1,17},{... | collective-permute-start | bytes 147464 | tf_op jit(solution)/shard_map/ppermute | solution.py:27
  97.2 2.7 %collective-permute-done.11.refs_4_ = bf16[4,3,32,256]{3,2,1,0:T(8,128)(2,1)S(1)} collective-permute-done((bf16[4,3,32,256]{3,2,1,0:T(8,128)(2,1)S(1)}, bf16[4,3,32,256]{3,2,1,0:T(8,128)(2,1)S(1)}, u32[]{:S(2)}, u32[]{:S(2)}) %collective-permute-start.11) | collective-permute-done | bytes 196640 | tf_op jit(solution)/shard_map/ppermute | solution.py:27
  105.5 2.7 %own_gradients.1.refs_2_.refs_0_ = bf16[16,9,64,256]{3,2,1,0:T(8,128)(2,1)S(1)} custom-call(s32[16]{0:T(128)S(1)} %copy-done.16, bf16[8,3,32,256]{3,2,1,0:T(8,128)(2,1)} %get-tuple-element.55.refs_1_, bf16[8,3,32,256]{3,2,1,0:T(8,128)(2,1)} %get-tuple-element.56.refs_2_, bf16[16,6,64,256]{3,2,1,0:T(8,128)(2,1)S(1)} %copy-done.7, ...), custom_call_target="tpu_custom_call" | custom-call | flops 1207959552 | bytes 10223648 | tf_op jit(solution)/shard_map/own_gradients/pallas_call | solution.py:56
  108.2 3.5 %weight_part.2 = (f32[4,96,288]{2,1,0:T(8,128)S(1)}, bf16[4,96,288]{2,1,0:T(8,128)(2,1)}) custom-call(s32[2]{0:T(128)S(1)} %pad_add_fusion.refs_1_.refs_0_, bf16[16,256,768]{2,1,0:T(8,128)(2,1)S(1)} %bitcast.21, bf16[16,9,64,256]{3,2,1,0:T(8,128)(2,1)S(1)} %own_gradients.1.refs_2_.refs_0_), custom_call_target="tpu_custom_call" | custom-call | flops 1811939328 | bytes 11452420 | tf_op jit(solution)/shard_map/weight_part/pallas_call | solution.py:56
  114.3 3.5 %weight_part.3 = (f32[4,96,288]{2,1,0:T(8,128)S(1)}, bf16[4,96,288]{2,1,0:T(8,128)(2,1)}) custom-call(s32[2]{0:T(128)S(1)} %pad_add_fusion.refs_1_.refs_0_, bf16[16,256,768]{2,1,0:T(8,128)(2,1)S(1)} %bitcast.21, bf16[16,9,64,256]{3,2,1,0:T(8,128)(2,1)S(1)} %own_gradients.1.refs_2_.refs_0_), custom_call_target="tpu_custom_call" | custom-call | flops 1811939328 | bytes 11452420 | tf_op jit(solution)/shard_map/weight_part/pallas_call | solution.py:56
  118.1 2.6 %own_input.1.refs_1_ = bf16[2,16,192,256]{3,2,1,0:T(8,128)(2,1)S(1)} custom-call(bf16[16,9,64,256]{3,2,1,0:T(8,128)(2,1)S(1)} %own_gradients.1.refs_2_.refs_0_, bf16[2,192,576]{2,1,0:T(8,128)(2,1)S(1)} %turn.2.refs_1_, bf16[4,96,288]{2,1,0:T(8,128)(2,1)} %get-tuple-element.58.refs_2_.refs_4_), custom_call_target="tpu_custom_call" | custom-call | flops 1811939328 | bytes 8306688 | tf_op jit(solution)/shard_map/own_input/pallas_call | solution.py:56
  122.6 3.2 %far_query_key.1.refs_4_ = bf16[16,6,64,256]{3,2,1,0:T(8,128)(2,1)S(1)} custom-call(s32[16]{0:T(128)S(1)} %copy-done.16, bf16[16,256,768]{2,1,0:T(8,128)(2,1)S(1)} %bitcast.21, bf16[192,768]{1,0:T(8,128)(2,1)S(1)} %dynamic-slice_bitcast_fusion.3.refs_2_.refs_1_, bf16[192,768]{1,0:T(8,128)(2,1)S(1)} %dynamic-slice_bitcast_fusion.2.refs_3_.refs_2_, ...), custom_call_target="tpu_custom_call" | custom-call | flops 2415919104 | bytes 10027040 | tf_op jit(solution)/shard_map/far_query_key/pallas_call | solution.py:56
  130.8 2.2 %far_input.7 = (bf16[4,192,256]{2,1,0:T(8,128)(2,1)S(1)}, bf16[4,192,256]{2,1,0:T(8,128)(2,1)S(1)}) custom-call(s32[16]{0:T(128)S(1)} %copy-done.16, bf16[2,16,192,256]{3,2,1,0:T(8,128)(2,1)S(1)} %own_input.1.refs_1_, bf16[8,3,32,256]{3,2,1,0:T(8,128)(2,1)S(1)} %collective-permute-done.12.refs_2_, bf16[8,3,32,256]{3,2,1,0:T(8,128)(2,1)} %collective-permute-done.13.refs_3_, ...), custom_call_target="tpu_custom_call" | custom-call | flops 754974720 | bytes 9879584 | tf_op jit(solution)/shard_map/far_input/pallas_call | solution.py:56
  133.0 2.4 %far_input.6 = (bf16[4,192,256]{2,1,0:T(8,128)(2,1)S(1)}, bf16[4,192,256]{2,1,0:T(8,128)(2,1)S(1)}) custom-call(s32[16]{0:T(128)S(1)} %copy-done.16, bf16[2,16,192,256]{3,2,1,0:T(8,128)(2,1)S(1)} %own_input.1.refs_1_, bf16[8,3,32,256]{3,2,1,0:T(8,128)(2,1)S(1)} %collective-permute-done.12.refs_2_, bf16[8,3,32,256]{3,2,1,0:T(8,128)(2,1)} %collective-permute-done.13.refs_3_, ...), custom_call_target="tpu_custom_call" | custom-call | flops 754974720 | bytes 9879584 | tf_op jit(solution)/shard_map/far_input/pallas_call | solution.py:56
  136.0 2.2 %far_input.5 = (bf16[4,192,256]{2,1,0:T(8,128)(2,1)S(1)}, bf16[4,192,256]{2,1,0:T(8,128)(2,1)S(1)}) custom-call(s32[16]{0:T(128)S(1)} %copy-done.16, bf16[2,16,192,256]{3,2,1,0:T(8,128)(2,1)S(1)} %own_input.1.refs_1_, bf16[8,3,32,256]{3,2,1,0:T(8,128)(2,1)S(1)} %collective-permute-done.12.refs_2_, bf16[8,3,32,256]{3,2,1,0:T(8,128)(2,1)} %collective-permute-done.13.refs_3_, ...), custom_call_target="tpu_custom_call" | custom-call | flops 754974720 | bytes 9879584 | tf_op jit(solution)/shard_map/far_input/pallas_call | solution.py:56
  138.3 2.2 %far_input.4 = (bf16[4,192,256]{2,1,0:T(8,128)(2,1)S(1)}, bf16[4,192,256]{2,1,0:T(8,128)(2,1)S(1)}) custom-call(s32[16]{0:T(128)S(1)} %copy-done.16, bf16[2,16,192,256]{3,2,1,0:T(8,128)(2,1)S(1)} %own_input.1.refs_1_, bf16[8,3,32,256]{3,2,1,0:T(8,128)(2,1)S(1)} %collective-permute-done.12.refs_2_, bf16[8,3,32,256]{3,2,1,0:T(8,128)(2,1)} %collective-permute-done.13.refs_3_, ...), custom_call_target="tpu_custom_call" | custom-call | flops 754974720 | bytes 9879584 | tf_op jit(solution)/shard_map/far_input/pallas_call | solution.py:56
  144.5 3.4 %collective-permute-done.22.refs_1_ = bf16[2,96,288]{2,1,0:T(8,128)(2,1)S(1)} collective-permute-done((bf16[2,96,288]{2,1,0:T(8,128)(2,1)S(1)}, bf16[2,96,288]{2,1,0:T(8,128)(2,1)S(1)}, u32[]{:S(2)}, u32[]{:S(2)}) %collective-permute-start.22) | collective-permute-done | bytes 110624 | tf_op jit(solution)/shard_map/ppermute | solution.py:27
  149.4 3.7 %collective-permute-done.19.refs_1_ = bf16[2,96,288]{2,1,0:T(8,128)(2,1)S(1)} collective-permute-done((bf16[2,96,288]{2,1,0:T(8,128)(2,1)S(1)}, bf16[2,96,288]{2,1,0:T(8,128)(2,1)S(1)}, u32[]{:S(2)}, u32[]{:S(2)}) %collective-permute-start.19) | collective-permute-done | bytes 110624 | tf_op jit(solution)/shard_map/ppermute | solution.py:27
  154.0 4.4 %collective-permute-done.23.refs_3_ = bf16[1,96,288]{2,1,0:T(8,128)(2,1)S(1)} collective-permute-done((bf16[1,96,288]{2,1,0:T(8,128)(2,1)S(1)}, bf16[1,96,288]{2,1,0:T(8,128)(2,1)S(1)}, u32[]{:S(2)}, u32[]{:S(2)}) %collective-permute-start.23) | collective-permute-done | bytes 55328 | tf_op jit(solution)/shard_map/ppermute | solution.py:27
  159.2 4.4 %collective-permute-done.20.refs_1_ = bf16[1,96,288]{2,1,0:T(8,128)(2,1)S(1)} collective-permute-done((bf16[1,96,288]{2,1,0:T(8,128)(2,1)S(1)}, bf16[1,96,288]{2,1,0:T(8,128)(2,1)S(1)}, u32[]{:S(2)}, u32[]{:S(2)}) %collective-permute-start.20) | collective-permute-done | bytes 55328 | tf_op jit(solution)/shard_map/ppermute | solution.py:27
  (111 shorter events, 47.2 us)
Async XLA Ops:
  7.2 120.2 %all-gather.6.cloned.1.call-start = ((), (), s32[]{:S(2)}) async-start(), calls=%async_computation | async-start | bytes 4718592 | tf_op jit(solution)/shard_map/all_gather | solution.py:494
  17.3 46.9 %collective-permute-start = (bf16[4,3,32,256]{3,2,1,0:T(8,128)(2,1)}, bf16[4,3,32,256]{3,2,1,0:T(8,128)(2,1)S(1)}, u32[]{:S(2)}, u32[]{:S(2)}) collective-permute-start(bf16[4,3,32,256]{3,2,1,0:T(8,128)(2,1)} %get-tuple-element.41.refs_5_), channel_id=1, source_target_pairs={{0,4},{4,0},{8,12},{12,8},{16,20},{20,16},{24,28},{28,24},{1,5},{5... | collective-permute-start | bytes 589832 | tf_op jit(solution)/shard_map/ppermute | solution.py:27
  27.8 33.8 %collective-permute-start.3 = (bf16[4,3,32,256]{3,2,1,0:T(8,128)(2,1)}, bf16[4,3,32,256]{3,2,1,0:T(8,128)(2,1)}, u32[]{:S(2)}, u32[]{:S(2)}) collective-permute-start(bf16[4,3,32,256]{3,2,1,0:T(8,128)(2,1)} %get-tuple-element.48.refs_4_), channel_id=1, source_target_pairs={{0,4},{4,0},{8,12},{12,8},{16,20},{20,16},{24,28},{28,24},{1,5},{5... | collective-permute-start | bytes 589832 | tf_op jit(solution)/shard_map/ppermute | solution.py:27
  62.5 13.4 %collective-permute-start.4 = (bf16[2,3,32,256]{3,2,1,0:T(8,128)(2,1)S(1)}, bf16[2,3,32,256]{3,2,1,0:T(8,128)(2,1)S(1)}, u32[]{:S(2)}, u32[]{:S(2)}) collective-permute-start(bf16[2,3,32,256]{3,2,1,0:T(8,128)(2,1)S(1)} %get-tuple-element.50), channel_id=1, source_target_pairs={{0,8},{4,12},{8,0},{12,4},{16,24},{20,28},{24,16},{28,20},{1,9},{5... | collective-permute-start | bytes 294920 | tf_op jit(solution)/shard_map/ppermute | solution.py:27
  64.3 14.1 %collective-permute-start.1 = (bf16[2,3,32,256]{3,2,1,0:T(8,128)(2,1)S(1)}, bf16[2,3,32,256]{3,2,1,0:T(8,128)(2,1)S(1)}, u32[]{:S(2)}, u32[]{:S(2)}) collective-permute-start(bf16[2,3,32,256]{3,2,1,0:T(8,128)(2,1)S(1)} %get-tuple-element.43), channel_id=1, source_target_pairs={{0,8},{4,12},{8,0},{12,4},{16,24},{20,28},{24,16},{28,20},{1,9},{5... | collective-permute-start | bytes 294920 | tf_op jit(solution)/shard_map/ppermute | solution.py:27
  76.0 5.4 %collective-permute-start.5 = (bf16[1,3,32,256]{3,2,1,0:T(8,128)(2,1)S(1)}, bf16[1,3,32,256]{3,2,1,0:T(8,128)(2,1)S(1)}, u32[]{:S(2)}, u32[]{:S(2)}) collective-permute-start(bf16[1,3,32,256]{3,2,1,0:T(8,128)(2,1)S(1)} %get-tuple-element.52), channel_id=1, source_target_pairs={{0,16},{4,20},{8,24},{12,28},{16,0},{20,4},{24,8},{28,12},{1,17},{... | collective-permute-start | bytes 147464 | tf_op jit(solution)/shard_map/ppermute | solution.py:27
  78.5 5.1 %collective-permute-start.2 = (bf16[1,3,32,256]{3,2,1,0:T(8,128)(2,1)S(1)}, bf16[1,3,32,256]{3,2,1,0:T(8,128)(2,1)S(1)}, u32[]{:S(2)}, u32[]{:S(2)}) collective-permute-start(bf16[1,3,32,256]{3,2,1,0:T(8,128)(2,1)S(1)} %get-tuple-element.45), channel_id=1, source_target_pairs={{0,16},{4,20},{8,24},{12,28},{16,0},{20,4},{24,8},{28,12},{1,17},{... | collective-permute-start | bytes 147464 | tf_op jit(solution)/shard_map/ppermute | solution.py:27
  83.8 5.1 %collective-permute-start.9 = (bf16[1,3,32,256]{3,2,1,0:T(8,128)(2,1)S(1)}, bf16[1,3,32,256]{3,2,1,0:T(8,128)(2,1)S(1)}, u32[]{:S(2)}, u32[]{:S(2)}) collective-permute-start(bf16[1,3,32,256]{3,2,1,0:T(8,128)(2,1)S(1)} %get-tuple-element.54), channel_id=1, source_target_pairs={{0,16},{4,20},{8,24},{12,28},{16,0},{20,4},{24,8},{28,12},{1,17},{... | collective-permute-start | bytes 147464 | tf_op jit(solution)/shard_map/ppermute | solution.py:27
  84.4 6.5 %collective-permute-start.6 = (bf16[1,3,32,256]{3,2,1,0:T(8,128)(2,1)S(1)}, bf16[1,3,32,256]{3,2,1,0:T(8,128)(2,1)S(1)}, u32[]{:S(2)}, u32[]{:S(2)}) collective-permute-start(bf16[1,3,32,256]{3,2,1,0:T(8,128)(2,1)S(1)} %get-tuple-element.53), channel_id=1, source_target_pairs={{0,16},{4,20},{8,24},{12,28},{16,0},{20,4},{24,8},{28,12},{1,17},{... | collective-permute-start | bytes 147464 | tf_op jit(solution)/shard_map/ppermute | solution.py:27
  90.9 4.7 %collective-permute-start.7 = (bf16[2,3,32,256]{3,2,1,0:T(8,128)(2,1)S(1)}, bf16[2,3,32,256]{3,2,1,0:T(8,128)(2,1)S(1)}, u32[]{:S(2)}, u32[]{:S(2)}) collective-permute-start(bf16[2,3,32,256]{3,2,1,0:T(8,128)(2,1)S(1)} %pad_maximum_fusion), channel_id=1, source_target_pairs={{0,8},{4,12},{8,0},{12,4},{16,24},{20,28},{24,16},{28,20},{1,9},{5... | collective-permute-start | bytes 294920 | tf_op jit(solution)/shard_map/ppermute | solution.py:27
  93.6 6.3 %collective-permute-start.11 = (bf16[4,3,32,256]{3,2,1,0:T(8,128)(2,1)S(1)}, bf16[4,3,32,256]{3,2,1,0:T(8,128)(2,1)S(1)}, u32[]{:S(2)}, u32[]{:S(2)}) collective-permute-start(bf16[4,3,32,256]{3,2,1,0:T(8,128)(2,1)S(1)} %constant_dynamic-update-slice_fusion.3.refs_3_), channel_id=1, source_target_pairs={{0,4},{4,0},{8,12},{12,8},{16,20},{20,16},{24,28},{28,24},{1,5},{5... | collective-permute-start | bytes 589832 | tf_op jit(solution)/shard_map/ppermute | solution.py:27
  95.6 6.4 %collective-permute-start.8 = (bf16[4,3,32,256]{3,2,1,0:T(8,128)(2,1)S(1)}, bf16[4,3,32,256]{3,2,1,0:T(8,128)(2,1)S(1)}, u32[]{:S(2)}, u32[]{:S(2)}) collective-permute-start(bf16[4,3,32,256]{3,2,1,0:T(8,128)(2,1)S(1)} %constant_dynamic-update-slice_fusion.refs_1_), channel_id=1, source_target_pairs={{0,4},{4,0},{8,12},{12,8},{16,20},{20,16},{24,28},{28,24},{1,5},{5... | collective-permute-start | bytes 589832 | tf_op jit(solution)/shard_map/ppermute | solution.py:27
  103.5 25.6 %collective-permute-start.12 = (bf16[8,3,32,256]{3,2,1,0:T(8,128)(2,1)}, bf16[8,3,32,256]{3,2,1,0:T(8,128)(2,1)S(1)}, u32[]{:S(2)}, u32[]{:S(2)}) collective-permute-start(bf16[8,3,32,256]{3,2,1,0:T(8,128)(2,1)} %get-tuple-element.55.refs_1_), channel_id=1, source_target_pairs={{0,2},{1,3},{2,0},{3,1},{4,6},{5,7},{6,4},{7,5},{8,10},{9,11},{10,... | collective-permute-start | bytes 1179656 | tf_op jit(solution)/shard_map/ppermute | solution.py:27
  104.0 25.1 %collective-permute-start.13 = (bf16[8,3,32,256]{3,2,1,0:T(8,128)(2,1)}, bf16[8,3,32,256]{3,2,1,0:T(8,128)(2,1)}, u32[]{:S(2)}, u32[]{:S(2)}) collective-permute-start(bf16[8,3,32,256]{3,2,1,0:T(8,128)(2,1)} %get-tuple-element.56.refs_2_), channel_id=1, source_target_pairs={{0,2},{1,3},{2,0},{3,1},{4,6},{5,7},{6,4},{7,5},{8,10},{9,11},{10,... | collective-permute-start | bytes 1179656 | tf_op jit(solution)/shard_map/ppermute | solution.py:27
  112.6 28.0 %collective-permute-start.21 = (bf16[4,96,288]{2,1,0:T(8,128)(2,1)}, bf16[4,96,288]{2,1,0:T(8,128)(2,1)}, u32[]{:S(2)}, u32[]{:S(2)}) collective-permute-start(bf16[4,96,288]{2,1,0:T(8,128)(2,1)} %get-tuple-element.58.refs_2_.refs_4_), channel_id=1, source_target_pairs={{0,4},{4,0},{8,12},{12,8},{16,20},{20,16},{24,28},{28,24},{1,5},{5... | collective-permute-start | bytes 663560 | tf_op jit(solution)/shard_map/ppermute | solution.py:27
  117.8 24.2 %collective-permute-start.18 = (bf16[4,96,288]{2,1,0:T(8,128)(2,1)}, bf16[4,96,288]{2,1,0:T(8,128)(2,1)}, u32[]{:S(2)}, u32[]{:S(2)}) collective-permute-start(bf16[4,96,288]{2,1,0:T(8,128)(2,1)} %get-tuple-element.68), channel_id=1, source_target_pairs={{0,4},{4,0},{8,12},{12,8},{16,20},{20,16},{24,28},{28,24},{1,5},{5... | collective-permute-start | bytes 663560 | tf_op jit(solution)/shard_map/ppermute | solution.py:27
  133.0 31.6 %collective-permute-start.17 = (bf16[4,192,256]{2,1,0:T(8,128)(2,1)S(1)}, bf16[4,192,256]{2,1,0:T(8,128)(2,1)S(1)}, u32[]{:S(2)}, u32[]{:S(2)}) collective-permute-start(bf16[4,192,256]{2,1,0:T(8,128)(2,1)S(1)} %get-tuple-element.66), channel_id=1, source_target_pairs={{0,1},{1,0},{2,3},{3,2},{4,5},{5,4},{6,7},{7,6},{8,9},{9,8},{10,11... | collective-permute-start | bytes 1179656 | tf_op jit(solution)/shard_map/ppermute | solution.py:27
  135.5 29.9 %collective-permute-start.16 = (bf16[4,192,256]{2,1,0:T(8,128)(2,1)S(1)}, bf16[4,192,256]{2,1,0:T(8,128)(2,1)S(1)}, u32[]{:S(2)}, u32[]{:S(2)}) collective-permute-start(bf16[4,192,256]{2,1,0:T(8,128)(2,1)S(1)} %get-tuple-element.64), channel_id=1, source_target_pairs={{0,1},{1,0},{2,3},{3,2},{4,5},{5,4},{6,7},{7,6},{8,9},{9,8},{10,11... | collective-permute-start | bytes 1179656 | tf_op jit(solution)/shard_map/ppermute | solution.py:27
  138.2 28.0 %collective-permute-start.15 = (bf16[4,192,256]{2,1,0:T(8,128)(2,1)S(1)}, bf16[4,192,256]{2,1,0:T(8,128)(2,1)S(1)}, u32[]{:S(2)}, u32[]{:S(2)}) collective-permute-start(bf16[4,192,256]{2,1,0:T(8,128)(2,1)S(1)} %get-tuple-element.62), channel_id=1, source_target_pairs={{0,1},{1,0},{2,3},{3,2},{4,5},{5,4},{6,7},{7,6},{8,9},{9,8},{10,11... | collective-permute-start | bytes 1179656 | tf_op jit(solution)/shard_map/ppermute | solution.py:27
  140.6 26.5 %collective-permute-start.14 = (bf16[4,192,256]{2,1,0:T(8,128)(2,1)S(1)}, bf16[4,192,256]{2,1,0:T(8,128)(2,1)S(1)}, u32[]{:S(2)}, u32[]{:S(2)}) collective-permute-start(bf16[4,192,256]{2,1,0:T(8,128)(2,1)S(1)} %get-tuple-element.60), channel_id=1, source_target_pairs={{0,1},{1,0},{2,3},{3,2},{4,5},{5,4},{6,7},{7,6},{8,9},{9,8},{10,11... | collective-permute-start | bytes 1179656 | tf_op jit(solution)/shard_map/ppermute | solution.py:27
  142.1 5.9 %collective-permute-start.22 = (bf16[2,96,288]{2,1,0:T(8,128)(2,1)S(1)}, bf16[2,96,288]{2,1,0:T(8,128)(2,1)S(1)}, u32[]{:S(2)}, u32[]{:S(2)}) collective-permute-start(bf16[2,96,288]{2,1,0:T(8,128)(2,1)S(1)} %get-tuple-element.75), channel_id=1, source_target_pairs={{0,8},{4,12},{8,0},{12,4},{16,24},{20,28},{24,16},{28,20},{1,9},{5... | collective-permute-start | bytes 331784 | tf_op jit(solution)/shard_map/ppermute | solution.py:27
  148.0 5.1 %collective-permute-start.19 = (bf16[2,96,288]{2,1,0:T(8,128)(2,1)S(1)}, bf16[2,96,288]{2,1,0:T(8,128)(2,1)S(1)}, u32[]{:S(2)}, u32[]{:S(2)}) collective-permute-start(bf16[2,96,288]{2,1,0:T(8,128)(2,1)S(1)} %get-tuple-element.70), channel_id=1, source_target_pairs={{0,8},{4,12},{8,0},{12,4},{16,24},{20,28},{24,16},{28,20},{1,9},{5... | collective-permute-start | bytes 331784 | tf_op jit(solution)/shard_map/ppermute | solution.py:27
  153.1 5.3 %collective-permute-start.23 = (bf16[1,96,288]{2,1,0:T(8,128)(2,1)S(1)}, bf16[1,96,288]{2,1,0:T(8,128)(2,1)S(1)}, u32[]{:S(2)}, u32[]{:S(2)}) collective-permute-start(bf16[1,96,288]{2,1,0:T(8,128)(2,1)S(1)} %get-tuple-element.77), channel_id=1, source_target_pairs={{0,16},{4,20},{8,24},{12,28},{16,0},{20,4},{24,8},{28,12},{1,17},{... | collective-permute-start | bytes 165896 | tf_op jit(solution)/shard_map/ppermute | solution.py:27
  158.4 5.3 %collective-permute-start.20 = (bf16[1,96,288]{2,1,0:T(8,128)(2,1)S(1)}, bf16[1,96,288]{2,1,0:T(8,128)(2,1)S(1)}, u32[]{:S(2)}, u32[]{:S(2)}) collective-permute-start(bf16[1,96,288]{2,1,0:T(8,128)(2,1)S(1)} %get-tuple-element.72), channel_id=1, source_target_pairs={{0,16},{4,20},{8,24},{12,28},{16,0},{20,4},{24,8},{28,12},{1,17},{... | collective-permute-start | bytes 165896 | tf_op jit(solution)/shard_map/ppermute | solution.py:27
  (21 other events, 193.8 us)
Sparse Core Ops, SparseCore 0:
  9.5 63.2 all-gather.5

commit v7 on v6

--- a/solution.py
+++ b/solution.py
@@ -77,6 +77,8 @@
 
 
 BLOCK = 4
+STEP = 2
+AHEAD = 4
 
 
 def query_key_kernel(lengths, me, sheet, wq, wk, qk, held, *rest):
@@ -88,24 +90,28 @@
         pltpu.make_async_copy(wq, wt.at[:local], sems.at[0]),
         pltpu.make_async_copy(wk, wt.at[local:], sems.at[1]),
     ]
-    for index, first in enumerate(range(0, rows, BLOCK)):
-        some = pl.ds(first, BLOCK)
-        copies.append(pltpu.make_async_copy(sheet.at[some], held.at[some], sems.at[2 + index]))
-    for copy in copies:
+    for first in range(0, rows, STEP):
+        some = pl.ds(first, STEP)
+        copies.append(pltpu.make_async_copy(sheet.at[some], held.at[some], sems.at[len(copies)]))
+    for copy in copies[:AHEAD]:
         copy.start()
     copies[0].wait()
     copies[1].wait()
     flat = (BLOCK * HEAD_DIM, cols)
-    for index, first in enumerate(range(0, rows, BLOCK)):
-        copies[2 + index].wait()
+    for first in range(0, rows, BLOCK):
         for r in range(first, first + BLOCK):
+            if r % STEP == 0:
+                at = 2 + r // STEP
+                copies[at].wait()
+                for later in copies[at + AHEAD - 2 : at + AHEAD - 1]:
+                    later.start()
             value = (mm(wt[...], held[r], NT) * lane_mask(lengths[r], cols)).astype(BF16)
             qk[r] = value.reshape(2 * heads, HEAD_DIM, cols)
         some = pl.ds(first, BLOCK)
         for h in range(heads):
             term = mm(qk[some, h].reshape(flat), qk[some, heads + h].reshape(flat), TN)
             term = term.reshape(acc.shape[1:])
-            acc[h] = term if index == 0 else acc[h] + term
+            acc[h] = term if first == 0 else acc[h] + term
     put_shards(me[0], acc, outs)
 
 
@@ -127,9 +133,9 @@
         scratch=(
             pltpu.VMEM((2 * local, width), BF16),
             pltpu.VMEM((heads, shards, cols // shards, cols), F32),
-            pltpu.SemaphoreType.DMA((2 + rows // BLOCK,)),
+            pltpu.SemaphoreType.DMA((2 + rows // STEP,)),
         ),
-        limit=46,
+        limit=14,
         flops=2 * rows * cols * local * (2 * width + cols),
     )
 
@@ -199,31 +205,94 @@
     )[0]
 
 
-def far_query_key_kernel(lengths, sheet, wq, wk, qk):
-    rows, cols, _ = sheet.shape
-    local = wq.shape[0]
+def stage_kernel(*refs):
+    cot, *weights, out, sems = refs
+    rows, _, cols = cot.shape
+    copies = [pltpu.make_async_copy(cot, out.at[pl.ds(0, rows)], sems.at[0])]
+    for weight in weights:
+        for first in range(0, weight.shape[1], cols):
+            at = rows + len(copies) - 1
+            piece = weight.at[:, pl.ds(first, cols)]
+            copies.append(pltpu.make_async_copy(piece, out.at[at], sems.at[len(copies)]))
+    for copy in copies:
+        copy.start()
+    for copy in copies:
+        copy.wait()
+
+
+def stage(cot, weights):
+    rows, local, cols = cot.shape
+    pieces = len(weights) * weights[0].shape[1] // cols
+    held = [place(a, True) for a in (cot, *weights)]
+    return pl.pallas_call(
+        stage_kernel,
+        in_specs=[HBM] * len(held),
+        out_specs=HBM,
+        out_shape=like((rows + pieces, local, cols)),
+        scratch_shapes=[pltpu.SemaphoreType.DMA((1 + pieces,))],
+        cost_estimate=cost(0, 4 * cot.size),
+        name="stage",
+    )(*held)
+
+
+def far_prepare_kernel(far, lengths, me, gathered, sheet, qk, natural, cot, w, turned, sems):
+    rows, cols, width = sheet.shape
+    count, local, _ = w.shape
+    devices, share, _ = turned.shape
     heads = local // HEAD_DIM
-    both = jnp.concatenate([wq[...], wk[...]], axis=0)
+    pos = lax.shift_right_logical(me[1], 1) ^ (far // 2)
+    copies = []
+    for index in range(count):
+        for first in range(0, width, cols):
+            at = rows + len(copies)
+            copies.append(
+                pltpu.make_async_copy(
+                    gathered.at[pos, at], w.at[index, :, pl.ds(first, cols)], sems.at[len(copies)]
+                )
+            )
+    copies.append(pltpu.make_async_copy(gathered.at[pos, pl.ds(0, rows)], cot, sems.at[len(copies)]))
+    for copy in copies:
+        copy.start()
+    for copy in copies[:-1]:
+        copy.wait()
+    both = w[:2].reshape(2 * local, width)
     for r in range(rows):
         value = (mm(both, sheet[r], NT) * lane_mask(lengths[r], cols)).astype(BF16)
         qk[r] = value.reshape(2 * heads, HEAD_DIM, cols)
-
-
-def far_query_key(lengths, sheet, wq, wk, after):
+    for index in range(count):
+        turned[:, :, index * local : (index + 1) * local] = w[index].T.reshape(devices, share, local)
+    for j in range(natural.shape[0]):
+        natural[j] = turned[me[1] ^ j]
+    copies[-1].wait()
+
+
+def far_prepare(far, lengths, me, gathered, sheet, devices, after):
     rows, cols, width = sheet.shape
-    local = wq.shape[0]
-    return in_vmem(
-        far_query_key_kernel,
-        "far_query_key",
-        (like((rows, 2 * local // HEAD_DIM, HEAD_DIM, cols)),),
+    local = gathered.shape[2]
+    share = width // devices
+    return in_vmem(
+        functools.partial(far_prepare_kernel, far),
+        "far_prepare",
+        (
+            like((rows, 2 * local // HEAD_DIM, HEAD_DIM, cols)),
+            like((2, share, 3 * local)),
+            like((rows, local, cols)),
+        ),
         lengths,
+        me,
+        gathered,
         sheet,
-        wq,
-        wk,
-        scalars=1,
+        scalars=2,
+        streamed=1,
         after=after,
+        scratch=(
+            pltpu.VMEM((3, local, width), BF16),
+            pltpu.VMEM((devices, share, 3 * local), BF16),
+            pltpu.SemaphoreType.DMA((3 * width // cols + 1,)),
+        ),
+        limit=14,
         flops=4 * rows * cols * local * width,
-    )[0]
+    )
 
 
 def part_shapes(shards, heads, cols):
@@ -374,7 +443,7 @@
         give[r] = total[r][1].astype(give.dtype)
 
 
-def far_input(first, count, lengths, own, far):
+def far_input(first, count, lengths, own, far, after):
     _, rows, share, cols = own.shape
     columns = far[0][-1].shape[-1]
     out = like((count, share, cols))
@@ -386,6 +455,7 @@
         own,
         *[a for one in far for a in one],
         scalars=1,
+        after=after,
         scratch=(pltpu.VMEM((count, columns // HEAD_DIM, HEAD_DIM, cols), BF16),),
         limit=16,
         flops=2 * len(far) * count * cols * columns * (cols + 2 * share),
@@ -415,45 +485,50 @@
     )(keep, got, *extra)
 
 
-def weight_product(sheet, grads, first, count):
+def weight_product(sheet, grads):
     rows, cols, width = sheet.shape
     columns = grads.shape[1] * HEAD_DIM
-    left = [grads[r].reshape(columns, cols)[first : first + count] for r in range(rows)]
+    left = [grads[r].reshape(columns, cols) for r in range(rows)]
     return mm(jnp.concatenate(left, axis=1), sheet[...].reshape(rows * cols, width), NN).T
 
 
-def weight_kernel(first, me, sheet, grads, keep, give, turned):
-    total = weight_product(sheet, grads, first, turned.shape[-1])
-    turned[...] = total.reshape(turned.shape)
+def weight_kernel(me, sheet, grads, *rest):
+    outs, turned = rest[:-1], rest[-1]
+    turned[...] = weight_product(sheet, grads).reshape(turned.shape)
     for j in range(turned.shape[0]):
-        out = (keep, give)[j % 2]
-        out[j // 2] = turned[me[0] ^ j].astype(out.dtype)
-
-
-def whole_weight_kernel(first, me, sheet, grads, out):
-    out[...] = weight_product(sheet, grads, first, out.shape[-1])
-
-
-def weight_part(me, sheet, grads, first, count, shards, after):
+        first = 0
+        for keep, give in zip(outs[::2], outs[1::2]):
+            out = (keep, give)[j % 2]
+            last = first + out.shape[-1]
+            out[j // 2] = turned[me[0] ^ j, :, first:last].astype(out.dtype)
+            first = last
+
+
+def whole_weight_kernel(me, sheet, grads, out):
+    out[...] = weight_product(sheet, grads)
+
+
+def weight_part(me, sheet, grads, cuts, shards):
     rows, cols, width = sheet.shape
+    columns = grads.shape[1] * HEAD_DIM
     if shards == 1:
-        kernel, outs, scratch = whole_weight_kernel, [like((width, count), F32)], ()
+        kernel, outs, scratch = whole_weight_kernel, [like((width, columns), F32)], ()
     else:
-        half = (shards // 2, width // shards, count)
-        kernel, outs = weight_kernel, [like(half, F32), like(half)]
-        scratch = (pltpu.VMEM((shards,) + half[1:], F32),)
-    return in_vmem(
-        functools.partial(kernel, first),
+        halves = [(shards // 2, width // shards, cut) for cut in cuts]
+        kernel = weight_kernel
+        outs = [o for half in halves for o in (like(half, F32), like(half))]
+        scratch = (pltpu.VMEM((shards, width // shards, columns), F32),)
+    return in_vmem(
+        kernel,
         "weight_part",
         outs,
         me,
         sheet,
         grads,
         scalars=1,
-        after=after,
         scratch=scratch,
-        limit=24,
-        flops=2 * rows * cols * width * count,
+        limit=18,
+        flops=2 * rows * cols * width * columns,
     )
 
 
@@ -490,13 +565,7 @@
 
     fars = range(2, n_heads, 2)
     groups = [list(range(core, n_heads, 2)) for core in range(2)]
-    wqa, wka, wva, cota = [
-        lax.all_gather(a, "heads", axis_index_groups=groups) for a in (wq, wk, wv, cot)
-    ]
-    side = lax.shift_right_logical(lax.axis_index("heads").astype(jnp.int32), 1)
-    take = lambda a, f: lax.dynamic_index_in_dim(a, side ^ (f // 2), 0, keepdims=False)
-    far_weights = [[take(w, f) for w in (wqa, wka, wva)] for f in fars]
-    far_cot = [take(cota, f) for f in fars]
+    gathered = lax.all_gather(stage(cot, (wq, wk, wv)), "heads", axis_index_groups=groups)
 
     qk, held, *logits = query_key(lengths, me, sheet, wq, wk, shards)
     dprob = value_dprob(lengths, me, held, wv, cot, logits[-1:], shards)
@@ -515,27 +584,36 @@
     far_probs = [flip(probs, "heads", f) for f in fars]
 
     grads = own_gradients(lengths, probs, dscore, qk, cot)
-    half = 3 * local // 2
-    parts = [weight_part(me, held, grads, first, half, shards, ()) for first in (0, half)]
-    ready = [parts[1][-1]]
+    cut = 3 * local // 256 * 128
+    cuts = (cut, 3 * local - cut)
+    parts = weight_part(me, held, grads, cuts, shards)
+    ready = [parts[-1]]
+    far = []
+    for index, f in enumerate(fars):
+        far_qk, far_natural, far_cot = far_prepare(f, lengths, me, gathered, held, n_heads, ready)
+        far.append((far_probs[index], far_dscore[index], far_qk, far_cot, far_natural))
+        ready = [far_qk]
+    own = own_input(grads, weights, ready + far_dscore)
+    ready = [own] + far_probs
+    steps = []
     if direct:
-        parts = [halve(*part, "rows", row_bits) for part in parts]
-        weight_grad = jnp.swapaxes(last_sum(parts, local, ()), 0, 1)
+        parts = [tuple(parts[:2]), tuple(parts[2:])]
+        for bit in row_bits[:-1]:
+            parts = [add_split(keep, flip(give, "rows", bit), ready)[::-1] for keep, give in parts]
+            steps.append([keep for keep, _ in parts])
+            ready = ()
+        parts = [(keep, flip(give, "rows", row_bits[-1])) for keep, give in parts]
     else:
-        part = jnp.concatenate([p[0] for p in parts], axis=1)
-        weight_grad = lax.psum_scatter(part, "rows", scatter_dimension=0, tiled=True)
+        weight_grad = lax.psum_scatter(parts[0], "rows", scatter_dimension=0, tiled=True)
         weight_grad = weight_grad.reshape(width // n_rows, 3, local)
 
-    far = []
-    for index, (fq, fk, fv) in enumerate(far_weights):
-        far_qk = far_query_key(lengths, held, fq, fk, ready)
-        far_natural = turn(me, fq, fk, fv, n_heads, ready)
-        far.append((far_probs[index], far_dscore[index], far_qk, far_cot[index], far_natural))
-    own = own_input(grads, weights, ready)
     out = None
-    for first in range(0, row_dev, chunk):
-        keep, give = far_input(first, chunk, lengths, own, far)
+    for index, first in enumerate(range(0, row_dev, chunk)):
+        after = steps[index // 2] if index // 2 < len(steps) else ()
+        keep, give = far_input(first, chunk, lengths, own, far, after)
         out = finish(keep, flip(give, "heads", 1), first, row_dev, out)
+    if direct:
+        weight_grad = jnp.swapaxes(last_sum(parts, local, [out]), 0, 1)
     return (jnp.swapaxes(out, 1, 2), weight_grad)
 
 

time: 175 us -> 206 us (1.18)
  Pallas kernels: 48.6 us -> 114 us
  blocking collectives: 43.9 us -> 0 us
  waiting for transfers between devices: 28.9 us -> 39.2 us
  local copies, waits for them, and re-layouts: 10.7 us -> 4.26 us
  starting transfers between devices: 28.2 us -> 33.8 us
    pallas_call x0 -> x1, Pallas kernels: none -> 75.6 us  [stage(): pl.pallas_call(stage_kernel, in_specs=[HBM] * len(held), out_specs=HBM, o...]
    all_gather x3 -> x0, blocking collectives: 43.9 us -> none  [body(): lax.all_gather(a, 'heads', axis_index_groups=groups)]
    all_gather x1, waiting for transfers between devices: 0.01 us -> 19 us  [body(): lax.all_gather(stage(cot, (wq, wk, wv)), 'heads', axis_index_groups=groups)]
    pallas_call x24 -> x22, Pallas kernels: 45.2 us -> 35.4 us  [in_vmem(): pl.pallas_call(run, in_specs=[SMEM] * scalars + [HBM] * streamed + [VMEM]...]
    ppermute x24, waiting for transfers between devices: 28.3 us -> 20.2 us  [flip(): return lax.ppermute(values, axis, [(s, s ^ bit) for s in range(n)])]
    ppermute x24, starting transfers between devices: 28.2 us -> 33.8 us  [flip(): return lax.ppermute(values, axis, [(s, s ^ bit) for s in range(n)])]
    unnamed x43 -> x23, local copies, waits for them, and re-layouts: 8.92 us -> 4.25 us
  transfers between devices with their start and end apart: 25 -> 25, of which waited for: 11 -> 12; matrix products, arithmetic and copies ran while one was open for 1% -> 0% of each run, Pallas kernels for 27% -> 18%
where the time goes in v7:
time: 206 us
  Pallas kernels  114 us (55%)
  waiting for transfers between devices  39.2 us (19%)
  starting transfers between devices  33.8 us (16%)
  between operations  14.3 us (7%)
  local copies, waits for them, and re-layouts  4.26 us (2%)
    pallas_call x1, Pallas kernels, stage(): pl.pallas_call(stage_kernel, in_specs=[HBM] * len(held), out_specs=HBM, o...  75.6 us
    pallas_call x22, Pallas kernels, in_vmem(): pl.pallas_call(run, in_specs=[SMEM] * scalars + [HBM] * streamed + [VMEM]...  35.4 us
    ppermute x24, starting transfers between devices, flip(): return lax.ppermute(values, axis, [(s, s ^ bit) for s in range(n)])  33.8 us
    ppermute x24, waiting for transfers between devices, flip(): return lax.ppermute(values, axis, [(s, s ^ bit) for s in range(n)])  20.2 us
    all_gather x1, waiting for transfers between devices, body(): lax.all_gather(stage(cot, (wq, wk, wv)), 'heads', axis_index_groups=groups)  19 us
    unnamed x23, local copies, waits for them, and re-layouts  4.25 us
  transfers between devices with their start and end apart: 25, of which 12 were waited for; matrix products, arithmetic and copies ran while one was open for 0% of the time, Pallas kernels for 18%

profile of v7, /device:TPU:0, one launch (start us, length us, event | category | flops | bytes accessed | tf_op | source)
XLA Modules:
  0.0 206.1 jit_solution(12154191797743130897)
XLA Ops:
  7.2 75.6 %stage.1 = bf16[25,192,256]{2,1,0:T(8,128)(2,1)} custom-call(bf16[16,192,256]{2,1,0:T(8,128)(2,1)} %bitcast.10, bf16[192,768]{1,0:T(8,128)(2,1)} %bitcast.16, bf16[192,768]{1,0:T(8,128)(2,1)} %bitcast.19, bf16[192,768]{1,0:T(8,128)(2,1)} %bitcast.13), custom_call_target="tpu_custom_call" | custom-call | bytes 3145728 | tf_op jit(solution)/shard_map/stage/pallas_call | solution.py:227
  83.0 6.9 %query_key.1 = (bf16[16,6,64,256]{3,2,1,0:T(8,128)(2,1)S(1)}, bf16[16,256,768]{2,1,0:T(8,128)(2,1)S(1)}, f32[4,3,32,256]{3,2,1,0:T(8,128)S(1)}, bf16[4,3,32,256]{3,2,1,0:T(8,128)(2,1)S(1)}) custom-call(s32[16]{0:T(128)S(1)} %copy-done.9, s32[2]{0:T(128)S(1)} %pad_add_fusion.refs_1_.refs_0_, bf16[16,256,768]{2,1,0:T(8,128)(2,1)} %refs_2_.1, ...), custom_call_target="tpu_custom_call" | custom-call | flops 2818572288 | bytes 16711716 | tf_op jit(solution)/shard_map/query_key/pallas_call | solution.py:56
  90.0 3.5 %value_dprob.1 = (f32[4,3,32,256]{3,2,1,0:T(8,128)S(1)}, bf16[4,3,32,256]{3,2,1,0:T(8,128)(2,1)S(1)}) custom-call(s32[16]{0:T(128)S(1)} %copy-done.9, s32[2]{0:T(128)S(1)} %pad_add_fusion.refs_1_.refs_0_, bf16[16,256,768]{2,1,0:T(8,128)(2,1)S(1)} %get-tuple-element.49.refs_2_.refs_1_.refs_3_, bf16[192,768]{1,0:T(8,128)(2,1)S(1)} %bitcast.14, ...), custom_call_target="tpu_custom_call" | custom-call | flops 1610612736 | bytes 8552484 | tf_op jit(solution)/shard_map/value_dprob/pallas_call | solution.py:56
  93.5 3.0 %collective-permute-start.3 = (bf16[4,3,32,256]{3,2,1,0:T(8,128)(2,1)S(1)}, bf16[4,3,32,256]{3,2,1,0:T(8,128)(2,1)S(1)}, u32[]{:S(2)}, u32[]{:S(2)}) collective-permute-start(bf16[4,3,32,256]{3,2,1,0:T(8,128)(2,1)S(1)} %get-tuple-element.51.refs_4_), channel_id=1, source_target_pairs={{0,4},{4,0},{8,12},{12,8},{16,20},{20,16},{24,28},{28,24},{1,5},{5... | collective-permute-start | bytes 589832 | tf_op jit(solution)/shard_map/ppermute | solution.py:27
  96.6 5.7 %collective-permute-done.3.refs_1_ = bf16[4,3,32,256]{3,2,1,0:T(8,128)(2,1)S(1)} collective-permute-done((bf16[4,3,32,256]{3,2,1,0:T(8,128)(2,1)S(1)}, bf16[4,3,32,256]{3,2,1,0:T(8,128)(2,1)S(1)}, u32[]{:S(2)}, u32[]{:S(2)}) %collective-permute-start.3) | collective-permute-done | bytes 196640 | tf_op jit(solution)/shard_map/ppermute | solution.py:27
  102.3 2.2 %collective-permute-start.4 = (bf16[2,3,32,256]{3,2,1,0:T(8,128)(2,1)S(1)}, bf16[2,3,32,256]{3,2,1,0:T(8,128)(2,1)S(1)}, u32[]{:S(2)}, u32[]{:S(2)}) collective-permute-start(bf16[2,3,32,256]{3,2,1,0:T(8,128)(2,1)S(1)} %get-tuple-element.53), channel_id=1, source_target_pairs={{0,8},{4,12},{8,0},{12,4},{16,24},{20,28},{24,16},{28,20},{1,9},{5... | collective-permute-start | bytes 294920 | tf_op jit(solution)/shard_map/ppermute | solution.py:27
  105.7 1.9 collective-permute-start.1
  107.6 2.7 %collective-permute-start.5 = (bf16[1,3,32,256]{3,2,1,0:T(8,128)(2,1)S(1)}, bf16[1,3,32,256]{3,2,1,0:T(8,128)(2,1)S(1)}, u32[]{:S(2)}, u32[]{:S(2)}) collective-permute-start(bf16[1,3,32,256]{3,2,1,0:T(8,128)(2,1)S(1)} %get-tuple-element.55), channel_id=1, source_target_pairs={{0,16},{4,20},{8,24},{12,28},{16,0},{20,4},{24,8},{28,12},{1,17},{... | collective-permute-start | bytes 147464 | tf_op jit(solution)/shard_map/ppermute | solution.py:27
  110.9 2.4 %collective-permute-start.2 = (bf16[1,3,32,256]{3,2,1,0:T(8,128)(2,1)S(1)}, bf16[1,3,32,256]{3,2,1,0:T(8,128)(2,1)S(1)}, u32[]{:S(2)}, u32[]{:S(2)}) collective-permute-start(bf16[1,3,32,256]{3,2,1,0:T(8,128)(2,1)S(1)} %get-tuple-element.48), channel_id=1, source_target_pairs={{0,16},{4,20},{8,24},{12,28},{16,0},{20,4},{24,8},{28,12},{1,17},{... | collective-permute-start | bytes 147464 | tf_op jit(solution)/shard_map/ppermute | solution.py:27
  113.3 2.7 %collective-permute-done.2.refs_1_ = bf16[1,3,32,256]{3,2,1,0:T(8,128)(2,1)S(1)} collective-permute-done((bf16[1,3,32,256]{3,2,1,0:T(8,128)(2,1)S(1)}, bf16[1,3,32,256]{3,2,1,0:T(8,128)(2,1)S(1)}, u32[]{:S(2)}, u32[]{:S(2)}) %collective-permute-start.2) | collective-permute-done | bytes 49184 | tf_op jit(solution)/shard_map/ppermute | solution.py:27
  116.2 2.4 %collective-permute-start.9 = (bf16[1,3,32,256]{3,2,1,0:T(8,128)(2,1)S(1)}, bf16[1,3,32,256]{3,2,1,0:T(8,128)(2,1)S(1)}, u32[]{:S(2)}, u32[]{:S(2)}) collective-permute-start(bf16[1,3,32,256]{3,2,1,0:T(8,128)(2,1)S(1)} %get-tuple-element.57), channel_id=1, source_target_pairs={{0,16},{4,20},{8,24},{12,28},{16,0},{20,4},{24,8},{28,12},{1,17},{... | collective-permute-start | bytes 147464 | tf_op jit(solution)/shard_map/ppermute | solution.py:27
  119.3 2.0 collective-permute-done.9
  123.8 2.5 %collective-permute-start.7 = (bf16[2,3,32,256]{3,2,1,0:T(8,128)(2,1)S(1)}, bf16[2,3,32,256]{3,2,1,0:T(8,128)(2,1)S(1)}, u32[]{:S(2)}, u32[]{:S(2)}) collective-permute-start(bf16[2,3,32,256]{3,2,1,0:T(8,128)(2,1)S(1)} %pad_maximum_fusion), channel_id=1, source_target_pairs={{0,8},{4,12},{8,0},{12,4},{16,24},{20,28},{24,16},{28,20},{1,9},{5... | collective-permute-start | bytes 294920 | tf_op jit(solution)/shard_map/ppermute | solution.py:27
  126.3 2.0 collective-permute-start.11
  132.0 2.6 %collective-permute-done.8.refs_2_ = bf16[4,3,32,256]{3,2,1,0:T(8,128)(2,1)S(1)} collective-permute-done((bf16[4,3,32,256]{3,2,1,0:T(8,128)(2,1)S(1)}, bf16[4,3,32,256]{3,2,1,0:T(8,128)(2,1)S(1)}, u32[]{:S(2)}, u32[]{:S(2)}) %collective-permute-start.8) | collective-permute-done | bytes 196640 | tf_op jit(solution)/shard_map/ppermute | solution.py:27
  135.2 2.1 %collective-permute-start.12 = (bf16[8,3,32,256]{3,2,1,0:T(8,128)(2,1)S(1)}, bf16[8,3,32,256]{3,2,1,0:T(8,128)(2,1)S(1)}, u32[]{:S(2)}, u32[]{:S(2)}) collective-permute-start(bf16[8,3,32,256]{3,2,1,0:T(8,128)(2,1)S(1)} %get-tuple-element.59.refs_2_), channel_id=1, source_target_pairs={{0,2},{1,3},{2,0},{3,1},{4,6},{5,7},{6,4},{7,5},{8,10},{9,11},{10,... | collective-permute-start | bytes 1179656 | tf_op jit(solution)/shard_map/ppermute | solution.py:27
  137.4 1.9 own_gradients.1.refs_2_.refs_0_
  139.4 5.5 %weight_part.1 = (f32[4,96,256]{2,1,0:T(8,128)S(1)}, bf16[4,96,256]{2,1,0:T(8,128)(2,1)}, f32[4,96,320]{2,1,0:T(8,128)S(1)}, bf16[4,96,320]{2,1,0:T(8,128)(2,1)}) custom-call(s32[2]{0:T(128)S(1)} %pad_add_fusion.refs_1_.refs_0_, bf16[16,256,768]{2,1,0:T(8,128)(2,1)S(1)} %get-tuple-element.49.refs_2_.refs_1_.refs_3_, ...), custom_call_target="tpu_custom_call" | custom-call | flops 3623878656 | bytes 11894788 | tf_op jit(solution)/shard_map/weight_part/pallas_call | solution.py:56
  146.9 19.0 %all-gather.3.cloned.1.call-done = bf16[50,192,256]{2,1,0:T(8,128)(2,1)} async-done(((bf16[25,192,256]{2,1,0:T(8,128)(2,1)}), bf16[50,192,256]{2,1,0:T(8,128)(2,1)}) %all-gather.3.cloned.1.call-update) | async-done | bytes 4915216 | tf_op jit(solution)/shard_map/all_gather | solution.py:568
  165.9 2.8 %copy-done.2 = bf16[16,256,768]{2,1,0:T(8,128)(2,1)S(1)} copy-done((bf16[16,256,768]{2,1,0:T(8,128)(2,1)S(1)}, bf16[16,256,768]{2,1,0:T(8,128)(2,1)}, u32[]{:S(2)}) %copy-start.2) | copy-done | bytes 6291480
  168.6 5.0 %far_prepare.1 = (bf16[16,6,64,256]{3,2,1,0:T(8,128)(2,1)S(1)}, bf16[2,192,576]{2,1,0:T(8,128)(2,1)S(1)}, bf16[16,192,256]{2,1,0:T(8,128)(2,1)S(1)}) custom-call(s32[16]{0:T(128)S(1)} %copy-done.9, s32[2]{0:T(128)S(1)} %pad_add_fusion.refs_1_.refs_0_, bf16[2,25,192,256]{3,2,1,0:T(8,128)(2,1)} %bitcast.22, bf16[16,256,768]{2,1,0:T(8,128)(2,1)S(1)} %copy-done.2, ...), custom_call_target="tpu_custom_call" | custom-call | flops 2415919104 | bytes 16367652 | tf_op jit(solution)/shard_map/far_prepare/pallas_call | solution.py:56
  173.7 2.6 %own_input.1.refs_2_.refs_1_ = bf16[2,16,192,256]{3,2,1,0:T(8,128)(2,1)S(1)} custom-call(bf16[16,9,64,256]{3,2,1,0:T(8,128)(2,1)S(1)} %copy-done.4, bf16[2,192,576]{2,1,0:T(8,128)(2,1)S(1)} %turn.1.refs_1_, bf16[16,6,64,256]{3,2,1,0:T(8,128)(2,1)S(1)} %get-tuple-element.62.refs_2_.refs_4_, bf16[8,3,32,256]{3,2,1,0:T(8,128)(2,1)S(1)} %collective-permute-done.12.refs_3_), custom_call_target="tpu_custom_call" | custom-call | flops 1811939328 | bytes 8306688 | tf_op jit(solution)/shard_map/own_input/pallas_call | solution.py:56
  188.1 2.7 %collective-permute-start.23 = (bf16[1,96,320]{2,1,0:T(8,128)(2,1)S(1)}, bf16[1,96,320]{2,1,0:T(8,128)(2,1)S(1)}, u32[]{:S(2)}, u32[]{:S(2)}) collective-permute-start(bf16[1,96,320]{2,1,0:T(8,128)(2,1)S(1)} %get-tuple-element.83), channel_id=1, source_target_pairs={{0,16},{4,20},{8,24},{12,28},{16,0},{20,4},{24,8},{28,12},{1,17},{... | collective-permute-start | bytes 184328 | tf_op jit(solution)/shard_map/ppermute | solution.py:27
  194.4 2.6 %collective-permute-done.22.refs_1_ = bf16[1,96,256]{2,1,0:T(8,128)(2,1)S(1)} collective-permute-done((bf16[1,96,256]{2,1,0:T(8,128)(2,1)S(1)}, bf16[1,96,256]{2,1,0:T(8,128)(2,1)S(1)}, u32[]{:S(2)}, u32[]{:S(2)}) %collective-permute-start.22) | collective-permute-done | bytes 49184 | tf_op jit(solution)/shard_map/ppermute | solution.py:27
  (82 shorter events, 29.4 us)
Async XLA Ops:
  7.2 158.7 %all-gather.3.cloned.1.call-start = ((), (), s32[]{:S(2)}) async-start(), calls=%async_computation | async-start | bytes 7372800 | tf_op jit(solution)/shard_map/all_gather | solution.py:568
  93.5 8.7 %collective-permute-start.3 = (bf16[4,3,32,256]{3,2,1,0:T(8,128)(2,1)S(1)}, bf16[4,3,32,256]{3,2,1,0:T(8,128)(2,1)S(1)}, u32[]{:S(2)}, u32[]{:S(2)}) collective-permute-start(bf16[4,3,32,256]{3,2,1,0:T(8,128)(2,1)S(1)} %get-tuple-element.51.refs_4_), channel_id=1, source_target_pairs={{0,4},{4,0},{8,12},{12,8},{16,20},{20,16},{24,28},{28,24},{1,5},{5... | collective-permute-start | bytes 589832 | tf_op jit(solution)/shard_map/ppermute | solution.py:27
  96.5 9.1 %collective-permute-start = (bf16[4,3,32,256]{3,2,1,0:T(8,128)(2,1)S(1)}, bf16[4,3,32,256]{3,2,1,0:T(8,128)(2,1)S(1)}, u32[]{:S(2)}, u32[]{:S(2)}) collective-permute-start(bf16[4,3,32,256]{3,2,1,0:T(8,128)(2,1)S(1)} %get-tuple-element.44.refs_5_), channel_id=1, source_target_pairs={{0,4},{4,0},{8,12},{12,8},{16,20},{20,16},{24,28},{28,24},{1,5},{5... | collective-permute-start | bytes 589832 | tf_op jit(solution)/shard_map/ppermute | solution.py:27
  102.3 5.3 %collective-permute-start.4 = (bf16[2,3,32,256]{3,2,1,0:T(8,128)(2,1)S(1)}, bf16[2,3,32,256]{3,2,1,0:T(8,128)(2,1)S(1)}, u32[]{:S(2)}, u32[]{:S(2)}) collective-permute-start(bf16[2,3,32,256]{3,2,1,0:T(8,128)(2,1)S(1)} %get-tuple-element.53), channel_id=1, source_target_pairs={{0,8},{4,12},{8,0},{12,4},{16,24},{20,28},{24,16},{28,20},{1,9},{5... | collective-permute-start | bytes 294920 | tf_op jit(solution)/shard_map/ppermute | solution.py:27
  105.7 5.2 %collective-permute-start.1 = (bf16[2,3,32,256]{3,2,1,0:T(8,128)(2,1)S(1)}, bf16[2,3,32,256]{3,2,1,0:T(8,128)(2,1)S(1)}, u32[]{:S(2)}, u32[]{:S(2)}) collective-permute-start(bf16[2,3,32,256]{3,2,1,0:T(8,128)(2,1)S(1)} %get-tuple-element.46), channel_id=1, source_target_pairs={{0,8},{4,12},{8,0},{12,4},{16,24},{20,28},{24,16},{28,20},{1,9},{5... | collective-permute-start | bytes 294920 | tf_op jit(solution)/shard_map/ppermute | solution.py:27
  107.6 5.7 %collective-permute-start.5 = (bf16[1,3,32,256]{3,2,1,0:T(8,128)(2,1)S(1)}, bf16[1,3,32,256]{3,2,1,0:T(8,128)(2,1)S(1)}, u32[]{:S(2)}, u32[]{:S(2)}) collective-permute-start(bf16[1,3,32,256]{3,2,1,0:T(8,128)(2,1)S(1)} %get-tuple-element.55), channel_id=1, source_target_pairs={{0,16},{4,20},{8,24},{12,28},{16,0},{20,4},{24,8},{28,12},{1,17},{... | collective-permute-start | bytes 147464 | tf_op jit(solution)/shard_map/ppermute | solution.py:27
  110.9 5.1 %collective-permute-start.2 = (bf16[1,3,32,256]{3,2,1,0:T(8,128)(2,1)S(1)}, bf16[1,3,32,256]{3,2,1,0:T(8,128)(2,1)S(1)}, u32[]{:S(2)}, u32[]{:S(2)}) collective-permute-start(bf16[1,3,32,256]{3,2,1,0:T(8,128)(2,1)S(1)} %get-tuple-element.48), channel_id=1, source_target_pairs={{0,16},{4,20},{8,24},{12,28},{16,0},{20,4},{24,8},{28,12},{1,17},{... | collective-permute-start | bytes 147464 | tf_op jit(solution)/shard_map/ppermute | solution.py:27
  116.2 5.1 %collective-permute-start.9 = (bf16[1,3,32,256]{3,2,1,0:T(8,128)(2,1)S(1)}, bf16[1,3,32,256]{3,2,1,0:T(8,128)(2,1)S(1)}, u32[]{:S(2)}, u32[]{:S(2)}) collective-permute-start(bf16[1,3,32,256]{3,2,1,0:T(8,128)(2,1)S(1)} %get-tuple-element.57), channel_id=1, source_target_pairs={{0,16},{4,20},{8,24},{12,28},{16,0},{20,4},{24,8},{28,12},{1,17},{... | collective-permute-start | bytes 147464 | tf_op jit(solution)/shard_map/ppermute | solution.py:27
  118.7 5.1 %collective-permute-start.6 = (bf16[1,3,32,256]{3,2,1,0:T(8,128)(2,1)S(1)}, bf16[1,3,32,256]{3,2,1,0:T(8,128)(2,1)S(1)}, u32[]{:S(2)}, u32[]{:S(2)}) collective-permute-start(bf16[1,3,32,256]{3,2,1,0:T(8,128)(2,1)S(1)} %get-tuple-element.56), channel_id=1, source_target_pairs={{0,16},{4,20},{8,24},{12,28},{16,0},{20,4},{24,8},{28,12},{1,17},{... | collective-permute-start | bytes 147464 | tf_op jit(solution)/shard_map/ppermute | solution.py:27
  123.8 5.1 %collective-permute-start.7 = (bf16[2,3,32,256]{3,2,1,0:T(8,128)(2,1)S(1)}, bf16[2,3,32,256]{3,2,1,0:T(8,128)(2,1)S(1)}, u32[]{:S(2)}, u32[]{:S(2)}) collective-permute-start(bf16[2,3,32,256]{3,2,1,0:T(8,128)(2,1)S(1)} %pad_maximum_fusion), channel_id=1, source_target_pairs={{0,8},{4,12},{8,0},{12,4},{16,24},{20,28},{24,16},{28,20},{1,9},{5... | collective-permute-start | bytes 294920 | tf_op jit(solution)/shard_map/ppermute | solution.py:27
  126.3 5.7 %collective-permute-start.11 = (bf16[4,3,32,256]{3,2,1,0:T(8,128)(2,1)S(1)}, bf16[4,3,32,256]{3,2,1,0:T(8,128)(2,1)S(1)}, u32[]{:S(2)}, u32[]{:S(2)}) collective-permute-start(bf16[4,3,32,256]{3,2,1,0:T(8,128)(2,1)S(1)} %constant_dynamic-update-slice_fusion.3.refs_3_), channel_id=1, source_target_pairs={{0,4},{4,0},{8,12},{12,8},{16,20},{20,16},{24,28},{28,24},{1,5},{5... | collective-permute-start | bytes 589832 | tf_op jit(solution)/shard_map/ppermute | solution.py:27
  128.9 5.7 %collective-permute-start.8 = (bf16[4,3,32,256]{3,2,1,0:T(8,128)(2,1)S(1)}, bf16[4,3,32,256]{3,2,1,0:T(8,128)(2,1)S(1)}, u32[]{:S(2)}, u32[]{:S(2)}) collective-permute-start(bf16[4,3,32,256]{3,2,1,0:T(8,128)(2,1)S(1)} %constant_dynamic-update-slice_fusion.refs_1_), channel_id=1, source_target_pairs={{0,4},{4,0},{8,12},{12,8},{16,20},{20,16},{24,28},{28,24},{1,5},{5... | collective-permute-start | bytes 589832 | tf_op jit(solution)/shard_map/ppermute | solution.py:27
  135.2 38.5 %collective-permute-start.12 = (bf16[8,3,32,256]{3,2,1,0:T(8,128)(2,1)S(1)}, bf16[8,3,32,256]{3,2,1,0:T(8,128)(2,1)S(1)}, u32[]{:S(2)}, u32[]{:S(2)}) collective-permute-start(bf16[8,3,32,256]{3,2,1,0:T(8,128)(2,1)S(1)} %get-tuple-element.59.refs_2_), channel_id=1, source_target_pairs={{0,2},{1,3},{2,0},{3,1},{4,6},{5,7},{6,4},{7,5},{8,10},{9,11},{10,... | collective-permute-start | bytes 1179656 | tf_op jit(solution)/shard_map/ppermute | solution.py:27
  137.3 39.0 %collective-permute-start.13 = (bf16[8,3,32,256]{3,2,1,0:T(8,128)(2,1)S(1)}, bf16[8,3,32,256]{3,2,1,0:T(8,128)(2,1)S(1)}, u32[]{:S(2)}, u32[]{:S(2)}) collective-permute-start(bf16[8,3,32,256]{3,2,1,0:T(8,128)(2,1)S(1)} %get-tuple-element.58.refs_1_), channel_id=1, source_target_pairs={{0,2},{1,3},{2,0},{3,1},{4,6},{5,7},{6,4},{7,5},{8,10},{9,11},{10,... | collective-permute-start | bytes 1179656 | tf_op jit(solution)/shard_map/ppermute | solution.py:27
  144.9 31.5 %collective-permute-start.16 = (bf16[4,96,320]{2,1,0:T(8,128)(2,1)}, bf16[4,96,320]{2,1,0:T(8,128)(2,1)S(1)}, u32[]{:S(2)}, u32[]{:S(2)}) collective-permute-start(bf16[4,96,320]{2,1,0:T(8,128)(2,1)} %get-tuple-element.61.refs_4_), channel_id=1, source_target_pairs={{0,4},{4,0},{8,12},{12,8},{16,20},{20,16},{24,28},{28,24},{1,5},{5... | collective-permute-start | bytes 737288 | tf_op jit(solution)/shard_map/ppermute | solution.py:27
  146.3 31.5 %collective-permute-start.14 = (bf16[4,96,256]{2,1,0:T(8,128)(2,1)}, bf16[4,96,256]{2,1,0:T(8,128)(2,1)S(1)}, u32[]{:S(2)}, u32[]{:S(2)}) collective-permute-start(bf16[4,96,256]{2,1,0:T(8,128)(2,1)} %get-tuple-element.66), channel_id=1, source_target_pairs={{0,4},{4,0},{8,12},{12,8},{16,20},{20,16},{24,28},{28,24},{1,5},{5... | collective-permute-start | bytes 589832 | tf_op jit(solution)/shard_map/ppermute | solution.py:27
  176.4 7.6 %collective-permute-start.17 = (bf16[2,96,320]{2,1,0:T(8,128)(2,1)S(1)}, bf16[2,96,320]{2,1,0:T(8,128)(2,1)S(1)}, u32[]{:S(2)}, u32[]{:S(2)}) collective-permute-start(bf16[2,96,320]{2,1,0:T(8,128)(2,1)S(1)} %get-tuple-element.72), channel_id=1, source_target_pairs={{0,8},{4,12},{8,0},{12,4},{16,24},{20,28},{24,16},{28,20},{1,9},{5... | collective-permute-start | bytes 368648 | tf_op jit(solution)/shard_map/ppermute | solution.py:27
  177.8 6.1 %collective-permute-start.15 = (bf16[2,96,256]{2,1,0:T(8,128)(2,1)S(1)}, bf16[2,96,256]{2,1,0:T(8,128)(2,1)S(1)}, u32[]{:S(2)}, u32[]{:S(2)}) collective-permute-start(bf16[2,96,256]{2,1,0:T(8,128)(2,1)S(1)} %get-tuple-element.68), channel_id=1, source_target_pairs={{0,8},{4,12},{8,0},{12,4},{16,24},{20,28},{24,16},{28,20},{1,9},{5... | collective-permute-start | bytes 294920 | tf_op jit(solution)/shard_map/ppermute | solution.py:27
  180.3 10.5 %collective-permute-start.21 = (bf16[4,192,256]{2,1,0:T(8,128)(2,1)S(1)}, bf16[4,192,256]{2,1,0:T(8,128)(2,1)S(1)}, u32[]{:S(2)}, u32[]{:S(2)}) collective-permute-start(bf16[4,192,256]{2,1,0:T(8,128)(2,1)S(1)} %get-tuple-element.81), channel_id=1, source_target_pairs={{0,1},{1,0},{2,3},{3,2},{4,5},{5,4},{6,7},{7,6},{8,9},{9,8},{10,11... | collective-permute-start | bytes 1179656 | tf_op jit(solution)/shard_map/ppermute | solution.py:27
  182.1 9.8 %collective-permute-start.20 = (bf16[4,192,256]{2,1,0:T(8,128)(2,1)S(1)}, bf16[4,192,256]{2,1,0:T(8,128)(2,1)S(1)}, u32[]{:S(2)}, u32[]{:S(2)}) collective-permute-start(bf16[4,192,256]{2,1,0:T(8,128)(2,1)S(1)} %get-tuple-element.79), channel_id=1, source_target_pairs={{0,1},{1,0},{2,3},{3,2},{4,5},{5,4},{6,7},{7,6},{8,9},{9,8},{10,11... | collective-permute-start | bytes 1179656 | tf_op jit(solution)/shard_map/ppermute | solution.py:27
  185.8 7.0 %collective-permute-start.19 = (bf16[4,192,256]{2,1,0:T(8,128)(2,1)S(1)}, bf16[4,192,256]{2,1,0:T(8,128)(2,1)S(1)}, u32[]{:S(2)}, u32[]{:S(2)}) collective-permute-start(bf16[4,192,256]{2,1,0:T(8,128)(2,1)S(1)} %get-tuple-element.77), channel_id=1, source_target_pairs={{0,1},{1,0},{2,3},{3,2},{4,5},{5,4},{6,7},{7,6},{8,9},{9,8},{10,11... | collective-permute-start | bytes 1179656 | tf_op jit(solution)/shard_map/ppermute | solution.py:27
  187.6 6.0 %collective-permute-start.18 = (bf16[4,192,256]{2,1,0:T(8,128)(2,1)S(1)}, bf16[4,192,256]{2,1,0:T(8,128)(2,1)S(1)}, u32[]{:S(2)}, u32[]{:S(2)}) collective-permute-start(bf16[4,192,256]{2,1,0:T(8,128)(2,1)S(1)} %get-tuple-element.75), channel_id=1, source_target_pairs={{0,1},{1,0},{2,3},{3,2},{4,5},{5,4},{6,7},{7,6},{8,9},{9,8},{10,11... | collective-permute-start | bytes 1179656 | tf_op jit(solution)/shard_map/ppermute | solution.py:27
  188.1 8.9 %collective-permute-start.23 = (bf16[1,96,320]{2,1,0:T(8,128)(2,1)S(1)}, bf16[1,96,320]{2,1,0:T(8,128)(2,1)S(1)}, u32[]{:S(2)}, u32[]{:S(2)}) collective-permute-start(bf16[1,96,320]{2,1,0:T(8,128)(2,1)S(1)} %get-tuple-element.83), channel_id=1, source_target_pairs={{0,16},{4,20},{8,24},{12,28},{16,0},{20,4},{24,8},{28,12},{1,17},{... | collective-permute-start | bytes 184328 | tf_op jit(solution)/shard_map/ppermute | solution.py:27
  190.8 6.2 %collective-permute-start.22 = (bf16[1,96,256]{2,1,0:T(8,128)(2,1)S(1)}, bf16[1,96,256]{2,1,0:T(8,128)(2,1)S(1)}, u32[]{:S(2)}, u32[]{:S(2)}) collective-permute-start(bf16[1,96,256]{2,1,0:T(8,128)(2,1)S(1)} %get-tuple-element.82), channel_id=1, source_target_pairs={{0,16},{4,20},{8,24},{12,28},{16,0},{20,4},{24,8},{28,12},{1,17},{... | collective-permute-start | bytes 147464 | tf_op jit(solution)/shard_map/ppermute | solution.py:27
  (11 other events, 232.7 us)
Sparse Core Ops, SparseCore 0:
  83.0 82.7 all-gather.2

commit v8 on v7

--- a/solution.py
+++ b/solution.py
@@ -15,11 +15,16 @@
 
 NN = (((1,), (0,)), ((), ()))
 NT = (((1,), (1,)), ((), ()))
-TN = (((0,), (0,)), ((), ()))
 
 
 def mm(a, b, dims):
     return lax.dot_general(a, b, dims, preferred_element_type=F32)
+
+
+def turned(a):
+    n = a.shape[1]
+    same = lax.broadcasted_iota(jnp.int32, (n, n), 0) == lax.broadcasted_iota(jnp.int32, (n, n), 1)
+    return mm(same.astype(a.dtype), a, NT).astype(a.dtype)
 
 
 def flip(values, axis, bit):
@@ -69,11 +74,14 @@
     return (lax.broadcasted_iota(jnp.int32, (1, cols), 1) < length).astype(F32)
 
 
-def put_shards(me, acc, outs):
-    shards = acc.shape[1]
-    for j in range(shards):
-        out = outs[j % len(outs)]
-        out[j // len(outs)] = acc[:, me ^ j].astype(out.dtype)
+def reorder(bits):
+    return [sum(bit for b, bit in enumerate(bits) if t >> b & 1) for t in range(1 << len(bits))]
+
+
+def put_shards(me, acc, bits, outs):
+    for t, j in enumerate(reorder(bits)):
+        out = outs[t % len(outs)]
+        out[t // len(outs)] = acc[:, me ^ j].astype(out.dtype)
 
 
 BLOCK = 4
@@ -81,7 +89,7 @@
 AHEAD = 4
 
 
-def query_key_kernel(lengths, me, sheet, wq, wk, qk, held, *rest):
+def query_key_kernel(bits, lengths, me, sheet, wq, wk, qk, held, *rest):
     outs, (wt, acc, sems) = rest[:-3], rest[-3:]
     rows, cols, _ = sheet.shape
     local = wq.shape[0]
@@ -109,18 +117,19 @@
             qk[r] = value.reshape(2 * heads, HEAD_DIM, cols)
         some = pl.ds(first, BLOCK)
         for h in range(heads):
-            term = mm(qk[some, h].reshape(flat), qk[some, heads + h].reshape(flat), TN)
+            term = mm(turned(qk[some, h].reshape(flat)), qk[some, heads + h].reshape(flat), NN)
             term = term.reshape(acc.shape[1:])
             acc[h] = term if first == 0 else acc[h] + term
-    put_shards(me[0], acc, outs)
-
-
-def query_key(lengths, me, sheet, wq, wk, shards):
+    put_shards(me[0], acc, bits, outs)
+
+
+def query_key(lengths, me, sheet, wq, wk, bits):
     rows, cols, width = sheet.shape
+    shards = 1 << len(bits)
     local = wq.shape[0]
     heads = local // HEAD_DIM
     return in_vmem(
-        query_key_kernel,
+        functools.partial(query_key_kernel, bits),
         "query_key",
         [like((rows, 2 * heads, HEAD_DIM, cols)), like(sheet.shape)] + part_shapes(shards, heads, cols),
         lengths,
@@ -140,7 +149,7 @@
     )
 
 
-def value_kernel(lengths, me, sheet, wv, cot, *rest):
+def value_kernel(bits, lengths, me, sheet, wv, cot, *rest):
     outs, acc = rest[:-1], rest[-1]
     rows, cols, _ = sheet.shape
     local = wv.shape[0]
@@ -154,17 +163,18 @@
         for h in range(heads):
             left = cot[pl.ds(first, BLOCK), h * HEAD_DIM : (h + 1) * HEAD_DIM].reshape(flat)
             right = jnp.concatenate([v[h] for v in values], axis=0)
-            term = mm(left, right, TN).reshape(acc.shape[1:])
+            term = mm(turned(left), right, NN).reshape(acc.shape[1:])
             acc[h] = term if first == 0 else acc[h] + term
-    put_shards(me[0], acc, outs)
-
-
-def value_dprob(lengths, me, sheet, wv, cot, after, shards):
+    put_shards(me[0], acc, bits, outs)
+
+
+def value_dprob(lengths, me, sheet, wv, cot, after, bits):
     rows, cols, width = sheet.shape
+    shards = 1 << len(bits)
     local = wv.shape[0]
     heads = local // HEAD_DIM
     return in_vmem(
-        value_kernel,
+        functools.partial(value_kernel, bits),
         "value_dprob",
         part_shapes(shards, heads, cols),
         lengths,
@@ -176,16 +186,16 @@
         after=after,
         scratch=(pltpu.VMEM((heads, shards, cols // shards, cols), F32),),
         limit=16,
-        flops=2 * rows * cols * local * (width + cols),
-    )
-
-
-def turn_kernel(me, wq, wk, wv, natural, turned):
+        flops=4 * rows * cols * local * (width + cols),
+    )
+
+
+def turn_kernel(me, wq, wk, wv, natural, full):
     local = wq.shape[0]
     for index, weight in enumerate((wq, wk, wv)):
-        turned[:, :, index * local : (index + 1) * local] = weight[...].T.reshape(turned.shape[:2] + (local,))
+        full[:, :, index * local : (index + 1) * local] = weight[...].T.reshape(full.shape[:2] + (local,))
     for j in range(natural.shape[0]):
-        natural[j] = turned[me[1] ^ j]
+        natural[j] = full[me[1] ^ j]
 
 
 def turn(me, wq, wk, wv, devices, after):
@@ -205,94 +215,30 @@
     )[0]
 
 
-def stage_kernel(*refs):
-    cot, *weights, out, sems = refs
-    rows, _, cols = cot.shape
-    copies = [pltpu.make_async_copy(cot, out.at[pl.ds(0, rows)], sems.at[0])]
-    for weight in weights:
-        for first in range(0, weight.shape[1], cols):
-            at = rows + len(copies) - 1
-            piece = weight.at[:, pl.ds(first, cols)]
-            copies.append(pltpu.make_async_copy(piece, out.at[at], sems.at[len(copies)]))
-    for copy in copies:
-        copy.start()
-    for copy in copies:
-        copy.wait()
-
-
-def stage(cot, weights):
-    rows, local, cols = cot.shape
-    pieces = len(weights) * weights[0].shape[1] // cols
-    held = [place(a, True) for a in (cot, *weights)]
-    return pl.pallas_call(
-        stage_kernel,
-        in_specs=[HBM] * len(held),
-        out_specs=HBM,
-        out_shape=like((rows + pieces, local, cols)),
-        scratch_shapes=[pltpu.SemaphoreType.DMA((1 + pieces,))],
-        cost_estimate=cost(0, 4 * cot.size),
-        name="stage",
-    )(*held)
-
-
-def far_prepare_kernel(far, lengths, me, gathered, sheet, qk, natural, cot, w, turned, sems):
-    rows, cols, width = sheet.shape
-    count, local, _ = w.shape
-    devices, share, _ = turned.shape
-    heads = local // HEAD_DIM
-    pos = lax.shift_right_logical(me[1], 1) ^ (far // 2)
-    copies = []
-    for index in range(count):
-        for first in range(0, width, cols):
-            at = rows + len(copies)
-            copies.append(
-                pltpu.make_async_copy(
-                    gathered.at[pos, at], w.at[index, :, pl.ds(first, cols)], sems.at[len(copies)]
-                )
-            )
-    copies.append(pltpu.make_async_copy(gathered.at[pos, pl.ds(0, rows)], cot, sems.at[len(copies)]))
-    for copy in copies:
-        copy.start()
-    for copy in copies[:-1]:
-        copy.wait()
-    both = w[:2].reshape(2 * local, width)
-    for r in range(rows):
-        value = (mm(both, sheet[r], NT) * lane_mask(lengths[r], cols)).astype(BF16)
-        qk[r] = value.reshape(2 * heads, HEAD_DIM, cols)
-    for index in range(count):
-        turned[:, :, index * local : (index + 1) * local] = w[index].T.reshape(devices, share, local)
-    for j in range(natural.shape[0]):
-        natural[j] = turned[me[1] ^ j]
-    copies[-1].wait()
-
-
-def far_prepare(far, lengths, me, gathered, sheet, devices, after):
-    rows, cols, width = sheet.shape
-    local = gathered.shape[2]
-    share = width // devices
-    return in_vmem(
-        functools.partial(far_prepare_kernel, far),
-        "far_prepare",
-        (
-            like((rows, 2 * local // HEAD_DIM, HEAD_DIM, cols)),
-            like((2, share, 3 * local)),
-            like((rows, local, cols)),
-        ),
+def far_query_key_kernel(first, lengths, sheet, wq, wk, qk):
+    local, _ = wq.shape
+    cols = sheet.shape[1]
+    both = jnp.concatenate([wq[...], wk[...]], axis=0)
+    for r in range(qk.shape[0]):
+        value = (mm(both, sheet[first + r], NT) * lane_mask(lengths[first + r], cols)).astype(BF16)
+        qk[r] = value.reshape(2 * local // HEAD_DIM, HEAD_DIM, cols)
+
+
+def far_query_key(first, count, lengths, sheet, wq, wk, after):
+    _, cols, width = sheet.shape
+    local = wq.shape[0]
+    return in_vmem(
+        functools.partial(far_query_key_kernel, first),
+        "far_query_key",
+        (like((count, 2 * local // HEAD_DIM, HEAD_DIM, cols)),),
         lengths,
-        me,
-        gathered,
         sheet,
-        scalars=2,
-        streamed=1,
+        wq,
+        wk,
+        scalars=1,
         after=after,
-        scratch=(
-            pltpu.VMEM((3, local, width), BF16),
-            pltpu.VMEM((devices, share, 3 * local), BF16),
-            pltpu.SemaphoreType.DMA((3 * width // cols + 1,)),
-        ),
-        limit=14,
-        flops=4 * rows * cols * local * width,
-    )
+        flops=4 * count * cols * local * width,
+    )[0]
 
 
 def part_shapes(shards, heads, cols):
@@ -334,10 +280,10 @@
     dscore_out[0] = (scale * probs * (dprob - inner)).astype(BF16)
 
 
-def softmax_back(logits, dprob, scale):
+def softmax_back(logits, dprob, scale, after=()):
     out = like(logits[0].shape)
     return in_vmem(
-        functools.partial(softmax_kernel, scale), "softmax_back", (out, out), *logits, *dprob, limit=16
+        functools.partial(softmax_kernel, scale), "softmax_back", (out, out), *logits, *dprob, limit=16, after=after
     )
 
 
@@ -352,39 +298,37 @@
 
 def assemble_kernel(orders, me, *refs):
     pieces, outs = refs[:-2], refs[-2:]
-    per = len(orders)
-    for kind, out in enumerate(outs):
-        for piece, order in zip(pieces[kind * per : (kind + 1) * per], orders):
-            for t, j in enumerate(order):
-                out[me[0] ^ j] = piece[t]
-
-
-def assemble(me, probs, dscore, orders, shards):
+    for piece, (kind, order) in zip(pieces, orders):
+        for t, j in enumerate(order):
+            outs[kind][me[0] ^ j] = piece[t]
+
+
+def assemble(me, probs, dscore, orders, shards, after):
     out = like((shards,) + probs[0].shape[1:])
     return in_vmem(
-        functools.partial(assemble_kernel, orders), "assemble", (out, out), me, *probs, *dscore, scalars=1
-    )
-
-
-def gradients(lengths, first, count, probs, dscore, qk, cot, grads):
+        functools.partial(assemble_kernel, [(k, o) for k, both in enumerate(orders) for o in both]), "assemble", (out, out), me, *probs, *dscore, scalars=1, after=after
+    )
+
+
+def gradients(lengths, first, at, count, probs, dscore, qk, cot, grads):
     cols = qk.shape[-1]
     heads = qk.shape[1] // 2
-    rows = pl.ds(first, count)
+    rows, held = pl.ds(first, count), pl.ds(at, count)
     flat = (count * HEAD_DIM, cols)
     split = (count, HEAD_DIM, cols)
     masks = jnp.stack([lane_mask(lengths[first + r], cols) for r in range(count)])
     for h in range(heads):
         p, ds = [ref[:, h].reshape(cols, cols) for ref in (probs, dscore)]
         g = cot[rows, h * HEAD_DIM : (h + 1) * HEAD_DIM].reshape(flat)
-        dq = mm(qk[rows, heads + h].reshape(flat), ds, NT)
-        dk = mm(qk[rows, h].reshape(flat), ds, NN)
+        dq = mm(qk[held, heads + h].reshape(flat), ds, NT)
+        dk = mm(qk[held, h].reshape(flat), ds, NN)
         dv = mm(g, p, NN)
         for index, value in enumerate((dq, dk, dv)):
             grads[:, index * heads + h] = (value.reshape(split) * masks).astype(BF16)
 
 
 def own_gradients_kernel(lengths, probs, dscore, qk, cot, grads):
-    gradients(lengths, 0, qk.shape[0], probs, dscore, qk, cot, grads)
+    gradients(lengths, 0, 0, qk.shape[0], probs, dscore, qk, cot, grads)
 
 
 def own_gradients(lengths, probs, dscore, qk, cot):
@@ -399,7 +343,7 @@
         qk,
         cot,
         scalars=1,
-        limit=24,
+        limit=14,
         flops=3 * rows * two * HEAD_DIM * cols * cols,
     )[0]
 
@@ -426,13 +370,13 @@
     )[0]
 
 
-def far_input_kernel(first, lengths, own, *refs):
+def far_input_kernel(first, at, lengths, own, *refs):
     *refs, keep, give, grads = refs
     count, share, cols = keep.shape
     total = [own[:, first + r].astype(F32) for r in range(count)]
     for i in range(0, len(refs), 5):
         probs, dscore, qk, cot, weights = refs[i : i + 5]
-        gradients(lengths, first, count, probs, dscore, qk, cot, grads)
+        gradients(lengths, first, at, count, probs, dscore, qk, cot, grads)
         near, _, columns = weights.shape
         left = weights[...].reshape(near * share, columns)
         for r in range(count):
@@ -443,12 +387,12 @@
         give[r] = total[r][1].astype(give.dtype)
 
 
-def far_input(first, count, lengths, own, far, after):
+def far_input(first, at, count, lengths, own, far, after):
     _, rows, share, cols = own.shape
     columns = far[0][-1].shape[-1]
     out = like((count, share, cols))
     return in_vmem(
-        functools.partial(far_input_kernel, first),
+        functools.partial(far_input_kernel, first, at),
         "far_input",
         (out, out),
         lengths,
@@ -493,14 +437,14 @@
 
 
 def weight_kernel(me, sheet, grads, *rest):
-    outs, turned = rest[:-1], rest[-1]
-    turned[...] = weight_product(sheet, grads).reshape(turned.shape)
-    for j in range(turned.shape[0]):
+    outs, full = rest[:-1], rest[-1]
+    full[...] = weight_product(sheet, grads).reshape(full.shape)
+    for j in range(full.shape[0]):
         first = 0
         for keep, give in zip(outs[::2], outs[1::2]):
             out = (keep, give)[j % 2]
             last = first + out.shape[-1]
-            out[j // 2] = turned[me[0] ^ j, :, first:last].astype(out.dtype)
+            out[j // 2] = full[me[0] ^ j, :, first:last].astype(out.dtype)
             first = last
 
 
@@ -564,19 +508,28 @@
     cot = jnp.swapaxes(cotangent, 1, 2)
 
     fars = range(2, n_heads, 2)
-    groups = [list(range(core, n_heads, 2)) for core in range(2)]
-    gathered = lax.all_gather(stage(cot, (wq, wk, wv)), "heads", axis_index_groups=groups)
-
-    qk, held, *logits = query_key(lengths, me, sheet, wq, wk, shards)
-    dprob = value_dprob(lengths, me, held, wv, cot, logits[-1:], shards)
+    far_cot = [flip(cot, "heads", f) for f in fars]
+    far_weights = [[flip(w, "heads", f) for w in (wq, wk, wv)] for f in fars]
+    fq, fk, fv = [[w[i] for w in far_weights] for i in range(3)]
+
+    up = row_bits if direct else []
+    turn_about = up[1:] + up[:1]
+    qk, held, *logits = query_key(lengths, me, sheet, wq, wk, up)
+    dprob = value_dprob(lengths, me, held, wv, cot, logits[-1:], turn_about)
     weights = turn(me, wq, wk, wv, n_heads, dprob[-1:])
+    far_qk, far_natural = [], []
+    for w in far_weights:
+        parts = [far_query_key(r, row_dev // 2, lengths, held, w[0], w[1], ()) for r in (0, row_dev // 2)]
+        far_qk.append(parts)
+        far_natural.append(turn(me, *w, n_heads, ()))
+    before = [a for two in far_qk for a in two] + far_natural + [weights]
     if direct:
-        logits = halve(*logits, "rows", row_bits)
-        dprob = halve(*dprob, "rows", row_bits)
-        probs_own, dscore_own = softmax_back(logits, dprob, scale)
-        probs, orders = double(probs_own, "rows", row_bits[::-1])
-        dscore, _ = double(dscore_own, "rows", row_bits[::-1])
-        probs, dscore = assemble(me, probs, dscore, orders, shards)
+        logits = halve(*logits, "rows", up)
+        dprob = halve(*dprob, "rows", turn_about)
+        probs_own, dscore_own = softmax_back(logits, dprob, scale, far_cot)
+        probs, probs_order = double(probs_own, "rows", up[::-1])
+        dscore, dscore_order = double(dscore_own, "rows", turn_about[::-1])
+        probs, dscore = assemble(me, probs, dscore, (probs_order, dscore_order), shards, [weights] + far_natural)
     else:
         logits, dprob = lax.psum((logits, dprob), "rows")
         probs, dscore = softmax_back(logits, dprob, scale)
@@ -587,13 +540,7 @@
     cut = 3 * local // 256 * 128
     cuts = (cut, 3 * local - cut)
     parts = weight_part(me, held, grads, cuts, shards)
-    ready = [parts[-1]]
-    far = []
-    for index, f in enumerate(fars):
-        far_qk, far_natural, far_cot = far_prepare(f, lengths, me, gathered, held, n_heads, ready)
-        far.append((far_probs[index], far_dscore[index], far_qk, far_cot, far_natural))
-        ready = [far_qk]
-    own = own_input(grads, weights, ready + far_dscore)
+    own = own_input(grads, weights, [parts[-1]] + far_dscore)
     ready = [own] + far_probs
     steps = []
     if direct:
@@ -608,12 +555,19 @@
         weight_grad = weight_grad.reshape(width // n_rows, 3, local)
 
     out = None
+    got = []
     for index, first in enumerate(range(0, row_dev, chunk)):
         after = steps[index // 2] if index // 2 < len(steps) else ()
-        keep, give = far_input(first, chunk, lengths, own, far, after)
-        out = finish(keep, flip(give, "heads", 1), first, row_dev, out)
+        which, at = divmod(first, row_dev // 2)
+        far = [
+            (far_probs[i], far_dscore[i], far_qk[i][which], far_cot[i], far_natural[i])
+            for i in range(len(fars))
+        ]
+        keep, give = far_input(first, at, chunk, lengths, own, far, after)
+        got.append(flip(give, "heads", 1))
+        out = finish(keep, got[-1], first, row_dev, out)
     if direct:
-        weight_grad = jnp.swapaxes(last_sum(parts, local, [out]), 0, 1)
+        weight_grad = jnp.swapaxes(last_sum(parts, local, got[-2:]), 0, 1)
     return (jnp.swapaxes(out, 1, 2), weight_grad)
 
 

time: 206 us -> 104 us (0.50)
  Pallas kernels: 114 us -> 39.1 us
  waiting for transfers between devices: 39.2 us -> 24.5 us
  between operations: 14.3 us -> 0.89 us
  starting transfers between devices: 33.8 us -> 38.5 us
  local copies, waits for them, and re-layouts: 4.26 us -> 0.71 us
    pallas_call x1 -> x0, Pallas kernels: 75.6 us -> none  [stage(): pl.pallas_call(stage_kernel, in_specs=[HBM] * len(held), out_specs=HBM, o...]
    all_gather x1 -> x0, waiting for transfers between devices: 19 us -> none  [body(): lax.all_gather(stage(cot, (wq, wk, wv)), 'heads', axis_index_groups=groups)]
    ppermute x24 -> x28, starting transfers between devices: 33.8 us -> 38.5 us  [flip(): return lax.ppermute(values, axis, [(s, s ^ bit) for s in range(n)])]
    ppermute x24 -> x28, waiting for transfers between devices: 20.2 us -> 24.5 us  [flip(): return lax.ppermute(values, axis, [(s, s ^ bit) for s in range(n)])]
    unnamed x23 -> x15, local copies, waits for them, and re-layouts: 4.25 us -> 0.69 us
    pallas_call x22 -> x24, Pallas kernels: 35.4 us -> 35.8 us  [in_vmem(): pl.pallas_call(run, in_specs=[SMEM] * scalars + [HBM] * streamed + [VMEM]...]
  transfers between devices with their start and end apart: 25 -> 28, of which waited for: 12 -> 9; matrix products, arithmetic and copies ran while one was open for 0% -> 0% of each run, Pallas kernels for 18% -> 36%
where the time goes in v8:
time: 104 us
  Pallas kernels  39.1 us (38%)
  starting transfers between devices  38.5 us (37%)
  waiting for transfers between devices  24.5 us (24%)
    ppermute x28, starting transfers between devices, flip(): return lax.ppermute(values, axis, [(s, s ^ bit) for s in range(n)])  38.5 us
    pallas_call x24, Pallas kernels, in_vmem(): pl.pallas_call(run, in_specs=[SMEM] * scalars + [HBM] * streamed + [VMEM]...  35.8 us
    ppermute x28, waiting for transfers between devices, flip(): return lax.ppermute(values, axis, [(s, s ^ bit) for s in range(n)])  24.5 us
    pallas_call x4, Pallas kernels, finish(): pl.pallas_call(finish_kernel, grid=(count // block,), in_specs=[spec, spe...  3.36 us
  transfers between devices with their start and end apart: 28, of which 9 were waited for; matrix products, arithmetic and copies ran while one was open for 0% of the time, Pallas kernels for 36%

profile of v8, /device:TPU:0, one launch (start us, length us, event | category | flops | bytes accessed | tf_op | source)
XLA Modules:
  0.0 103.8 jit_solution(11287106936893986109)
XLA Ops:
  0.6 3.0 %collective-permute-start.6 = (bf16[16,192,256]{2,1,0:T(8,128)(2,1)}, bf16[16,192,256]{2,1,0:T(8,128)(2,1)S(1)}, u32[]{:S(2)}, u32[]{:S(2)}) collective-permute-start(bf16[16,192,256]{2,1,0:T(8,128)(2,1)} %bitcast.8), channel_id=1, source_target_pairs={{0,2},{1,3},{2,0},{3,1},{4,6},{5,7},{6,4},{7,5},{8,10},{9,11},{10,... | collective-permute-start | bytes 4718600 | tf_op jit(solution)/shard_map/ppermute | solution.py:32
  4.4 7.6 %query_key.1 = (bf16[16,6,64,256]{3,2,1,0:T(8,128)(2,1)S(1)}, bf16[16,256,768]{2,1,0:T(8,128)(2,1)S(1)}, f32[4,3,32,256]{3,2,1,0:T(8,128)S(1)}, bf16[4,3,32,256]{3,2,1,0:T(8,128)(2,1)S(1)}) custom-call(s32[16]{0:T(128)S(1)} %copy-done.4, s32[2]{0:T(128)S(1)} %pad_add_fusion.refs_1_.refs_0_, bf16[16,256,768]{2,1,0:T(8,128)(2,1)} %refs_2_.1, ...), custom_call_target="tpu_custom_call" | custom-call | flops 2818572288 | bytes 16711716 | tf_op jit(solution)/shard_map/query_key/pallas_call | solution.py:61
  13.5 4.0 %value_dprob.1 = (f32[4,3,32,256]{3,2,1,0:T(8,128)S(1)}, bf16[4,3,32,256]{3,2,1,0:T(8,128)(2,1)S(1)}) custom-call(s32[16]{0:T(128)S(1)} %copy-done.5, s32[2]{0:T(128)S(1)} %pad_add_fusion.refs_1_.refs_0_, bf16[16,256,768]{2,1,0:T(8,128)(2,1)S(1)} %get-tuple-element.46.refs_2_.refs_1_, bf16[192,768]{1,0:T(8,128)(2,1)S(1)} %bitcast.17, ...), custom_call_target="tpu_custom_call" | custom-call | flops 3221225472 | bytes 8552484 | tf_op jit(solution)/shard_map/value_dprob/pallas_call | solution.py:61
  20.1 4.7 %collective-permute-done.3.refs_1_ = bf16[4,3,32,256]{3,2,1,0:T(8,128)(2,1)S(1)} collective-permute-done((bf16[4,3,32,256]{3,2,1,0:T(8,128)(2,1)S(1)}, bf16[4,3,32,256]{3,2,1,0:T(8,128)(2,1)S(1)}, u32[]{:S(2)}, u32[]{:S(2)}) %collective-permute-start.3) | collective-permute-done | bytes 196640 | tf_op jit(solution)/shard_map/ppermute | solution.py:32
  24.8 2.7 %collective-permute-start.4 = (bf16[2,3,32,256]{3,2,1,0:T(8,128)(2,1)S(1)}, bf16[2,3,32,256]{3,2,1,0:T(8,128)(2,1)S(1)}, u32[]{:S(2)}, u32[]{:S(2)}) collective-permute-start(bf16[2,3,32,256]{3,2,1,0:T(8,128)(2,1)S(1)} %get-tuple-element.50), channel_id=1, source_target_pairs={{0,16},{4,20},{8,24},{12,28},{16,0},{20,4},{24,8},{28,12},{1,17},{... | collective-permute-start | bytes 294920 | tf_op jit(solution)/shard_map/ppermute | solution.py:32
  27.5 2.0 %collective-permute-start.2 = (bf16[1,3,32,256]{3,2,1,0:T(8,128)(2,1)S(1)}, bf16[1,3,32,256]{3,2,1,0:T(8,128)(2,1)S(1)}, u32[]{:S(2)}, u32[]{:S(2)}) collective-permute-start(bf16[1,3,32,256]{3,2,1,0:T(8,128)(2,1)S(1)} %get-tuple-element.45), channel_id=1, source_target_pairs={{0,16},{4,20},{8,24},{12,28},{16,0},{20,4},{24,8},{28,12},{1,17},{... | collective-permute-start | bytes 147464 | tf_op jit(solution)/shard_map/ppermute | solution.py:32
  29.5 2.2 %collective-permute-done.4.refs_1_ = bf16[2,3,32,256]{3,2,1,0:T(8,128)(2,1)S(1)} collective-permute-done((bf16[2,3,32,256]{3,2,1,0:T(8,128)(2,1)S(1)}, bf16[2,3,32,256]{3,2,1,0:T(8,128)(2,1)S(1)}, u32[]{:S(2)}, u32[]{:S(2)}) %collective-permute-start.4) | collective-permute-done | bytes 98336 | tf_op jit(solution)/shard_map/ppermute | solution.py:32
  35.9 3.2 %collective-permute-done.6.refs_4_.refs_5_ = bf16[16,192,256]{2,1,0:T(8,128)(2,1)S(1)} collective-permute-done((bf16[16,192,256]{2,1,0:T(8,128)(2,1)}, bf16[16,192,256]{2,1,0:T(8,128)(2,1)S(1)}, u32[]{:S(2)}, u32[]{:S(2)}) %collective-permute-start.6) | collective-permute-done | bytes 1572896 | tf_op jit(solution)/shard_map/ppermute | solution.py:32
  39.4 3.2 %collective-permute-start.7 = (bf16[1,3,32,256]{3,2,1,0:T(8,128)(2,1)S(1)}, bf16[1,3,32,256]{3,2,1,0:T(8,128)(2,1)S(1)}, u32[]{:S(2)}, u32[]{:S(2)}) collective-permute-start(bf16[1,3,32,256]{3,2,1,0:T(8,128)(2,1)S(1)} %get-tuple-element.53), channel_id=1, source_target_pairs={{0,16},{4,20},{8,24},{12,28},{16,0},{20,4},{24,8},{28,12},{1,17},{... | collective-permute-start | bytes 147464 | tf_op jit(solution)/shard_map/ppermute | solution.py:32
  44.7 1.9 %collective-permute-start.8 = (bf16[2,3,32,256]{3,2,1,0:T(8,128)(2,1)S(1)}, bf16[2,3,32,256]{3,2,1,0:T(8,128)(2,1)S(1)}, u32[]{:S(2)}, u32[]{:S(2)}) collective-permute-start(bf16[2,3,32,256]{3,2,1,0:T(8,128)(2,1)S(1)} %pad_maximum_fusion), channel_id=1, source_target_pairs={{0,8},{4,12},{8,0},{12,4},{16,24},{20,28},{24,16},{28,20},{1,9},{5... | collective-permute-start | bytes 294920 | tf_op jit(solution)/shard_map/ppermute | solution.py:32
  46.7 3.2 %collective-permute-start.11 = (bf16[2,3,32,256]{3,2,1,0:T(8,128)(2,1)S(1)}, bf16[2,3,32,256]{3,2,1,0:T(8,128)(2,1)S(1)}, u32[]{:S(2)}, u32[]{:S(2)}) collective-permute-start(bf16[2,3,32,256]{3,2,1,0:T(8,128)(2,1)S(1)} %pad_maximum_fusion.1), channel_id=1, source_target_pairs={{0,16},{4,20},{8,24},{12,28},{16,0},{20,4},{24,8},{28,12},{1,17},{... | collective-permute-start | bytes 294920 | tf_op jit(solution)/shard_map/ppermute | solution.py:32
  49.9 3.1 %collective-permute-done.11 = bf16[2,3,32,256]{3,2,1,0:T(8,128)(2,1)S(1)} collective-permute-done((bf16[2,3,32,256]{3,2,1,0:T(8,128)(2,1)S(1)}, bf16[2,3,32,256]{3,2,1,0:T(8,128)(2,1)S(1)}, u32[]{:S(2)}, u32[]{:S(2)}) %collective-permute-start.11) | collective-permute-done | bytes 98336 | tf_op jit(solution)/shard_map/ppermute | solution.py:32
  53.0 1.7 %collective-permute-start.12 = (bf16[4,3,32,256]{3,2,1,0:T(8,128)(2,1)S(1)}, bf16[4,3,32,256]{3,2,1,0:T(8,128)(2,1)S(1)}, u32[]{:S(2)}, u32[]{:S(2)}) collective-permute-start(bf16[4,3,32,256]{3,2,1,0:T(8,128)(2,1)S(1)} %constant_dynamic-update-slice_fusion.3.refs_3_), channel_id=1, source_target_pairs={{0,8},{4,12},{8,0},{12,4},{16,24},{20,28},{24,16},{28,20},{1,9},{5... | collective-permute-start | bytes 589832 | tf_op jit(solution)/shard_map/ppermute | solution.py:32
  58.4 2.0 %far_query_key.3.refs_4_ = bf16[8,6,64,256]{3,2,1,0:T(8,128)(2,1)S(1)} custom-call(s32[16]{0:T(128)S(1)} %copy-done.5, bf16[16,256,768]{2,1,0:T(8,128)(2,1)S(1)} %get-tuple-element.46.refs_2_.refs_1_, bf16[192,768]{1,0:T(8,128)(2,1)S(1)} %collective-permute-done.13.refs_1_.refs_2_, bf16[192,768]{1,0:T(8,128)(2,1)S(1)} %collective-permute-done.14.refs_2_.refs_3_), custom_call_target="tpu_custom_call" | custom-call | flops 1207959552 | bytes 8454176 | tf_op jit(solution)/shard_map/far_query_key/pallas_call | solution.py:61
  63.1 1.9 %own_gradients.1.refs_2_.refs_0_ = bf16[16,9,64,256]{3,2,1,0:T(8,128)(2,1)S(1)} custom-call(s32[16]{0:T(128)S(1)} %copy-done.5, bf16[8,3,32,256]{3,2,1,0:T(8,128)(2,1)S(1)} %get-tuple-element.55.refs_1_, bf16[8,3,32,256]{3,2,1,0:T(8,128)(2,1)S(1)} %get-tuple-element.56.refs_2_, bf16[16,6,64,256]{3,2,1,0:T(8,128)(2,1)S(1)} %get-tuple-element.57.refs_3_, ...), custom_call_target="tpu_custom_call" | custom-call | flops 1207959552 | bytes 10223648 | tf_op jit(solution)/shard_map/own_gradients/pallas_call | solution.py:61
  65.1 4.9 %weight_part.1 = (f32[4,96,256]{2,1,0:T(8,128)S(1)}, bf16[4,96,256]{2,1,0:T(8,128)(2,1)S(1)}, f32[4,96,320]{2,1,0:T(8,128)S(1)}, bf16[4,96,320]{2,1,0:T(8,128)(2,1)S(1)}) custom-call(s32[2]{0:T(128)S(1)} %pad_add_fusion.refs_1_.refs_0_, bf16[16,256,768]{2,1,0:T(8,128)(2,1)S(1)} %get-tuple-element.46.refs_2_.refs_1_, ...), custom_call_target="tpu_custom_call" | custom-call | flops 3623878656 | bytes 11894788 | tf_op jit(solution)/shard_map/weight_part/pallas_call | solution.py:61
  72.1 2.0 %far_query_key.2.refs_4_ = bf16[8,6,64,256]{3,2,1,0:T(8,128)(2,1)S(1)} custom-call(s32[16]{0:T(128)S(1)} %copy-done.5, bf16[16,256,768]{2,1,0:T(8,128)(2,1)S(1)} %get-tuple-element.46.refs_2_.refs_1_, bf16[192,768]{1,0:T(8,128)(2,1)S(1)} %collective-permute-done.13.refs_1_.refs_2_, bf16[192,768]{1,0:T(8,128)(2,1)S(1)} %collective-permute-done.14.refs_2_.refs_3_), custom_call_target="tpu_custom_call" | custom-call | flops 1207959552 | bytes 8454176 | tf_op jit(solution)/shard_map/far_query_key/pallas_call | solution.py:61
  74.0 5.7 %collective-permute-done.16.refs_3_ = bf16[8,3,32,256]{3,2,1,0:T(8,128)(2,1)S(1)} collective-permute-done((bf16[8,3,32,256]{3,2,1,0:T(8,128)(2,1)S(1)}, bf16[8,3,32,256]{3,2,1,0:T(8,128)(2,1)S(1)}, u32[]{:S(2)}, u32[]{:S(2)}) %collective-permute-start.16) | collective-permute-done | bytes 393248 | tf_op jit(solution)/shard_map/ppermute | solution.py:32
  79.7 2.6 %own_input.1.refs_2_.refs_1_ = bf16[2,16,192,256]{3,2,1,0:T(8,128)(2,1)S(1)} custom-call(bf16[16,9,64,256]{3,2,1,0:T(8,128)(2,1)S(1)} %own_gradients.1.refs_2_.refs_0_, bf16[2,192,576]{2,1,0:T(8,128)(2,1)S(1)} %turn.2.refs_5_.refs_1_, bf16[4,96,320]{2,1,0:T(8,128)(2,1)S(1)} %get-tuple-element.58.refs_2_, ...), custom_call_target="tpu_custom_call" | custom-call | flops 1811939328 | bytes 8306688 | tf_op jit(solution)/shard_map/own_input/pallas_call | solution.py:61
  86.4 1.7 %far_input.6 = (bf16[4,192,256]{2,1,0:T(8,128)(2,1)S(1)}, bf16[4,192,256]{2,1,0:T(8,128)(2,1)S(1)}) custom-call(s32[16]{0:T(128)S(1)} %copy-done.5, bf16[2,16,192,256]{3,2,1,0:T(8,128)(2,1)S(1)} %own_input.1.refs_2_.refs_1_, bf16[8,3,32,256]{3,2,1,0:T(8,128)(2,1)S(1)} %collective-permute-done.17.refs_3_.refs_2_, ...), custom_call_target="tpu_custom_call" | custom-call | flops 754974720 | bytes 8306720 | tf_op jit(solution)/shard_map/far_input/pallas_call | solution.py:61
  89.2 1.7 %far_input.5 = (bf16[4,192,256]{2,1,0:T(8,128)(2,1)S(1)}, bf16[4,192,256]{2,1,0:T(8,128)(2,1)S(1)}) custom-call(s32[16]{0:T(128)S(1)} %copy-done.5, bf16[2,16,192,256]{3,2,1,0:T(8,128)(2,1)S(1)} %own_input.1.refs_2_.refs_1_, bf16[8,3,32,256]{3,2,1,0:T(8,128)(2,1)S(1)} %collective-permute-done.17.refs_3_.refs_2_, ...), custom_call_target="tpu_custom_call" | custom-call | flops 754974720 | bytes 8306720 | tf_op jit(solution)/shard_map/far_input/pallas_call | solution.py:61
  91.0 1.7 %far_input.4 = (bf16[4,192,256]{2,1,0:T(8,128)(2,1)S(1)}, bf16[4,192,256]{2,1,0:T(8,128)(2,1)S(1)}) custom-call(s32[16]{0:T(128)S(1)} %copy-done.5, bf16[2,16,192,256]{3,2,1,0:T(8,128)(2,1)S(1)} %own_input.1.refs_2_.refs_1_, bf16[8,3,32,256]{3,2,1,0:T(8,128)(2,1)S(1)} %collective-permute-done.17.refs_3_.refs_2_, ...), custom_call_target="tpu_custom_call" | custom-call | flops 754974720 | bytes 8306720 | tf_op jit(solution)/shard_map/far_input/pallas_call | solution.py:61
  93.3 2.6 %collective-permute-start.27 = (bf16[1,96,320]{2,1,0:T(8,128)(2,1)S(1)}, bf16[1,96,320]{2,1,0:T(8,128)(2,1)S(1)}, u32[]{:S(2)}, u32[]{:S(2)}) collective-permute-start(bf16[1,96,320]{2,1,0:T(8,128)(2,1)S(1)} %get-tuple-element.77), channel_id=1, source_target_pairs={{0,16},{4,20},{8,24},{12,28},{16,0},{20,4},{24,8},{28,12},{1,17},{... | collective-permute-start | bytes 184328 | tf_op jit(solution)/shard_map/ppermute | solution.py:32
  98.7 3.4 %collective-permute-done.26.refs_1_ = bf16[1,96,256]{2,1,0:T(8,128)(2,1)S(1)} collective-permute-done((bf16[1,96,256]{2,1,0:T(8,128)(2,1)S(1)}, bf16[1,96,256]{2,1,0:T(8,128)(2,1)S(1)}, u32[]{:S(2)}, u32[]{:S(2)}) %collective-permute-start.26) | collective-permute-done | bytes 49184 | tf_op jit(solution)/shard_map/ppermute | solution.py:32
  (80 shorter events, 30.4 us)
Async XLA Ops:
  0.6 38.5 %collective-permute-start.6 = (bf16[16,192,256]{2,1,0:T(8,128)(2,1)}, bf16[16,192,256]{2,1,0:T(8,128)(2,1)S(1)}, u32[]{:S(2)}, u32[]{:S(2)}) collective-permute-start(bf16[16,192,256]{2,1,0:T(8,128)(2,1)} %bitcast.8), channel_id=1, source_target_pairs={{0,2},{1,3},{2,0},{3,1},{4,6},{5,7},{6,4},{7,5},{8,10},{9,11},{10,... | collective-permute-start | bytes 4718600 | tf_op jit(solution)/shard_map/ppermute | solution.py:32
  12.0 7.2 %collective-permute-start = (bf16[4,3,32,256]{3,2,1,0:T(8,128)(2,1)S(1)}, bf16[4,3,32,256]{3,2,1,0:T(8,128)(2,1)S(1)}, u32[]{:S(2)}, u32[]{:S(2)}) collective-permute-start(bf16[4,3,32,256]{3,2,1,0:T(8,128)(2,1)S(1)} %get-tuple-element.41.refs_5_), channel_id=1, source_target_pairs={{0,4},{4,0},{8,12},{12,8},{16,20},{20,16},{24,28},{28,24},{1,5},{5... | collective-permute-start | bytes 589832 | tf_op jit(solution)/shard_map/ppermute | solution.py:32
  17.5 7.2 %collective-permute-start.3 = (bf16[4,3,32,256]{3,2,1,0:T(8,128)(2,1)S(1)}, bf16[4,3,32,256]{3,2,1,0:T(8,128)(2,1)S(1)}, u32[]{:S(2)}, u32[]{:S(2)}) collective-permute-start(bf16[4,3,32,256]{3,2,1,0:T(8,128)(2,1)S(1)} %get-tuple-element.48.refs_4_), channel_id=1, source_target_pairs={{0,8},{4,12},{8,0},{12,4},{16,24},{20,28},{24,16},{28,20},{1,9},{5... | collective-permute-start | bytes 589832 | tf_op jit(solution)/shard_map/ppermute | solution.py:32
  19.2 8.3 %collective-permute-start.1 = (bf16[2,3,32,256]{3,2,1,0:T(8,128)(2,1)S(1)}, bf16[2,3,32,256]{3,2,1,0:T(8,128)(2,1)S(1)}, u32[]{:S(2)}, u32[]{:S(2)}) collective-permute-start(bf16[2,3,32,256]{3,2,1,0:T(8,128)(2,1)S(1)} %get-tuple-element.43), channel_id=1, source_target_pairs={{0,8},{4,12},{8,0},{12,4},{16,24},{20,28},{24,16},{28,20},{1,9},{5... | collective-permute-start | bytes 294920 | tf_op jit(solution)/shard_map/ppermute | solution.py:32
  24.8 6.9 %collective-permute-start.4 = (bf16[2,3,32,256]{3,2,1,0:T(8,128)(2,1)S(1)}, bf16[2,3,32,256]{3,2,1,0:T(8,128)(2,1)S(1)}, u32[]{:S(2)}, u32[]{:S(2)}) collective-permute-start(bf16[2,3,32,256]{3,2,1,0:T(8,128)(2,1)S(1)} %get-tuple-element.50), channel_id=1, source_target_pairs={{0,16},{4,20},{8,24},{12,28},{16,0},{20,4},{24,8},{28,12},{1,17},{... | collective-permute-start | bytes 294920 | tf_op jit(solution)/shard_map/ppermute | solution.py:32
  27.5 6.8 %collective-permute-start.2 = (bf16[1,3,32,256]{3,2,1,0:T(8,128)(2,1)S(1)}, bf16[1,3,32,256]{3,2,1,0:T(8,128)(2,1)S(1)}, u32[]{:S(2)}, u32[]{:S(2)}) collective-permute-start(bf16[1,3,32,256]{3,2,1,0:T(8,128)(2,1)S(1)} %get-tuple-element.45), channel_id=1, source_target_pairs={{0,16},{4,20},{8,24},{12,28},{16,0},{20,4},{24,8},{28,12},{1,17},{... | collective-permute-start | bytes 147464 | tf_op jit(solution)/shard_map/ppermute | solution.py:32
  32.3 25.0 %collective-permute-start.13 = (bf16[192,768]{1,0:T(8,128)(2,1)S(1)}, bf16[192,768]{1,0:T(8,128)(2,1)S(1)}, u32[]{:S(2)}, u32[]{:S(2)}) collective-permute-start(bf16[192,768]{1,0:T(8,128)(2,1)S(1)} %bitcast.12), channel_id=1, source_target_pairs={{0,2},{1,3},{2,0},{3,1},{4,6},{5,7},{6,4},{7,5},{8,10},{9,11},{10,... | collective-permute-start | bytes 884744 | tf_op jit(solution)/shard_map/ppermute | solution.py:32
  32.8 24.5 %collective-permute-start.14 = (bf16[192,768]{1,0:T(8,128)(2,1)S(1)}, bf16[192,768]{1,0:T(8,128)(2,1)S(1)}, u32[]{:S(2)}, u32[]{:S(2)}) collective-permute-start(bf16[192,768]{1,0:T(8,128)(2,1)S(1)} %bitcast.15), channel_id=1, source_target_pairs={{0,2},{1,3},{2,0},{3,1},{4,6},{5,7},{6,4},{7,5},{8,10},{9,11},{10,... | collective-permute-start | bytes 884744 | tf_op jit(solution)/shard_map/ppermute | solution.py:32
  34.4 23.0 %collective-permute-start.15 = (bf16[192,768]{1,0:T(8,128)(2,1)S(1)}, bf16[192,768]{1,0:T(8,128)(2,1)S(1)}, u32[]{:S(2)}, u32[]{:S(2)}) collective-permute-start(bf16[192,768]{1,0:T(8,128)(2,1)S(1)} %bitcast.18), channel_id=1, source_target_pairs={{0,2},{1,3},{2,0},{3,1},{4,6},{5,7},{6,4},{7,5},{8,10},{9,11},{10,... | collective-permute-start | bytes 884744 | tf_op jit(solution)/shard_map/ppermute | solution.py:32
  44.7 10.0 %collective-permute-start.8 = (bf16[2,3,32,256]{3,2,1,0:T(8,128)(2,1)S(1)}, bf16[2,3,32,256]{3,2,1,0:T(8,128)(2,1)S(1)}, u32[]{:S(2)}, u32[]{:S(2)}) collective-permute-start(bf16[2,3,32,256]{3,2,1,0:T(8,128)(2,1)S(1)} %pad_maximum_fusion), channel_id=1, source_target_pairs={{0,8},{4,12},{8,0},{12,4},{16,24},{20,28},{24,16},{28,20},{1,9},{5... | collective-permute-start | bytes 294920 | tf_op jit(solution)/shard_map/ppermute | solution.py:32
  46.7 6.3 %collective-permute-start.11 = (bf16[2,3,32,256]{3,2,1,0:T(8,128)(2,1)S(1)}, bf16[2,3,32,256]{3,2,1,0:T(8,128)(2,1)S(1)}, u32[]{:S(2)}, u32[]{:S(2)}) collective-permute-start(bf16[2,3,32,256]{3,2,1,0:T(8,128)(2,1)S(1)} %pad_maximum_fusion.1), channel_id=1, source_target_pairs={{0,16},{4,20},{8,24},{12,28},{16,0},{20,4},{24,8},{28,12},{1,17},{... | collective-permute-start | bytes 294920 | tf_op jit(solution)/shard_map/ppermute | solution.py:32
  53.0 7.4 %collective-permute-start.12 = (bf16[4,3,32,256]{3,2,1,0:T(8,128)(2,1)S(1)}, bf16[4,3,32,256]{3,2,1,0:T(8,128)(2,1)S(1)}, u32[]{:S(2)}, u32[]{:S(2)}) collective-permute-start(bf16[4,3,32,256]{3,2,1,0:T(8,128)(2,1)S(1)} %constant_dynamic-update-slice_fusion.3.refs_3_), channel_id=1, source_target_pairs={{0,8},{4,12},{8,0},{12,4},{16,24},{20,28},{24,16},{28,20},{1,9},{5... | collective-permute-start | bytes 589832 | tf_op jit(solution)/shard_map/ppermute | solution.py:32
  54.7 5.7 %collective-permute-start.9 = (bf16[4,3,32,256]{3,2,1,0:T(8,128)(2,1)S(1)}, bf16[4,3,32,256]{3,2,1,0:T(8,128)(2,1)S(1)}, u32[]{:S(2)}, u32[]{:S(2)}) collective-permute-start(bf16[4,3,32,256]{3,2,1,0:T(8,128)(2,1)S(1)} %constant_dynamic-update-slice_fusion.refs_1_), channel_id=1, source_target_pairs={{0,4},{4,0},{8,12},{12,8},{16,20},{20,16},{24,28},{28,24},{1,5},{5... | collective-permute-start | bytes 589832 | tf_op jit(solution)/shard_map/ppermute | solution.py:32
  61.0 21.3 %collective-permute-start.17 = (bf16[8,3,32,256]{3,2,1,0:T(8,128)(2,1)S(1)}, bf16[8,3,32,256]{3,2,1,0:T(8,128)(2,1)S(1)}, u32[]{:S(2)}, u32[]{:S(2)}) collective-permute-start(bf16[8,3,32,256]{3,2,1,0:T(8,128)(2,1)S(1)} %get-tuple-element.55.refs_1_), channel_id=1, source_target_pairs={{0,2},{1,3},{2,0},{3,1},{4,6},{5,7},{6,4},{7,5},{8,10},{9,11},{10,... | collective-permute-start | bytes 1179656 | tf_op jit(solution)/shard_map/ppermute | solution.py:32
  62.7 17.0 %collective-permute-start.16 = (bf16[8,3,32,256]{3,2,1,0:T(8,128)(2,1)S(1)}, bf16[8,3,32,256]{3,2,1,0:T(8,128)(2,1)S(1)}, u32[]{:S(2)}, u32[]{:S(2)}) collective-permute-start(bf16[8,3,32,256]{3,2,1,0:T(8,128)(2,1)S(1)} %get-tuple-element.56.refs_2_), channel_id=1, source_target_pairs={{0,2},{1,3},{2,0},{3,1},{4,6},{5,7},{6,4},{7,5},{8,10},{9,11},{10,... | collective-permute-start | bytes 1179656 | tf_op jit(solution)/shard_map/ppermute | solution.py:32
  70.0 12.3 %collective-permute-start.18 = (bf16[4,96,256]{2,1,0:T(8,128)(2,1)S(1)}, bf16[4,96,256]{2,1,0:T(8,128)(2,1)S(1)}, u32[]{:S(2)}, u32[]{:S(2)}) collective-permute-start(bf16[4,96,256]{2,1,0:T(8,128)(2,1)S(1)} %get-tuple-element.60), channel_id=1, source_target_pairs={{0,4},{4,0},{8,12},{12,8},{16,20},{20,16},{24,28},{28,24},{1,5},{5... | collective-permute-start | bytes 589832 | tf_op jit(solution)/shard_map/ppermute | solution.py:32
  71.6 12.3 %collective-permute-start.20 = (bf16[4,96,320]{2,1,0:T(8,128)(2,1)S(1)}, bf16[4,96,320]{2,1,0:T(8,128)(2,1)S(1)}, u32[]{:S(2)}, u32[]{:S(2)}) collective-permute-start(bf16[4,96,320]{2,1,0:T(8,128)(2,1)S(1)} %get-tuple-element.58.refs_2_), channel_id=1, source_target_pairs={{0,4},{4,0},{8,12},{12,8},{16,20},{20,16},{24,28},{28,24},{1,5},{5... | collective-permute-start | bytes 737288 | tf_op jit(solution)/shard_map/ppermute | solution.py:32
  82.4 6.3 %collective-permute-start.19 = (bf16[2,96,256]{2,1,0:T(8,128)(2,1)S(1)}, bf16[2,96,256]{2,1,0:T(8,128)(2,1)S(1)}, u32[]{:S(2)}, u32[]{:S(2)}) collective-permute-start(bf16[2,96,256]{2,1,0:T(8,128)(2,1)S(1)} %get-tuple-element.62), channel_id=1, source_target_pairs={{0,8},{4,12},{8,0},{12,4},{16,24},{20,28},{24,16},{28,20},{1,9},{5... | collective-permute-start | bytes 294920 | tf_op jit(solution)/shard_map/ppermute | solution.py:32
  86.3 9.6 %collective-permute-start.25 = (bf16[4,192,256]{2,1,0:T(8,128)(2,1)S(1)}, bf16[4,192,256]{2,1,0:T(8,128)(2,1)S(1)}, u32[]{:S(2)}, u32[]{:S(2)}) collective-permute-start(bf16[4,192,256]{2,1,0:T(8,128)(2,1)S(1)} %get-tuple-element.75), channel_id=1, source_target_pairs={{0,1},{1,0},{2,3},{3,2},{4,5},{5,4},{6,7},{7,6},{8,9},{9,8},{10,11... | collective-permute-start | bytes 1179656 | tf_op jit(solution)/shard_map/ppermute | solution.py:32
  88.1 9.0 %collective-permute-start.24 = (bf16[4,192,256]{2,1,0:T(8,128)(2,1)S(1)}, bf16[4,192,256]{2,1,0:T(8,128)(2,1)S(1)}, u32[]{:S(2)}, u32[]{:S(2)}) collective-permute-start(bf16[4,192,256]{2,1,0:T(8,128)(2,1)S(1)} %get-tuple-element.73), channel_id=1, source_target_pairs={{0,1},{1,0},{2,3},{3,2},{4,5},{5,4},{6,7},{7,6},{8,9},{9,8},{10,11... | collective-permute-start | bytes 1179656 | tf_op jit(solution)/shard_map/ppermute | solution.py:32
  90.9 7.0 %collective-permute-start.23 = (bf16[4,192,256]{2,1,0:T(8,128)(2,1)S(1)}, bf16[4,192,256]{2,1,0:T(8,128)(2,1)S(1)}, u32[]{:S(2)}, u32[]{:S(2)}) collective-permute-start(bf16[4,192,256]{2,1,0:T(8,128)(2,1)S(1)} %get-tuple-element.71), channel_id=1, source_target_pairs={{0,1},{1,0},{2,3},{3,2},{4,5},{5,4},{6,7},{7,6},{8,9},{9,8},{10,11... | collective-permute-start | bytes 1179656 | tf_op jit(solution)/shard_map/ppermute | solution.py:32
  92.7 9.4 %collective-permute-start.22 = (bf16[4,192,256]{2,1,0:T(8,128)(2,1)S(1)}, bf16[4,192,256]{2,1,0:T(8,128)(2,1)S(1)}, u32[]{:S(2)}, u32[]{:S(2)}) collective-permute-start(bf16[4,192,256]{2,1,0:T(8,128)(2,1)S(1)} %get-tuple-element.69), channel_id=1, source_target_pairs={{0,1},{1,0},{2,3},{3,2},{4,5},{5,4},{6,7},{7,6},{8,9},{9,8},{10,11... | collective-permute-start | bytes 1179656 | tf_op jit(solution)/shard_map/ppermute | solution.py:32
  93.3 8.8 %collective-permute-start.27 = (bf16[1,96,320]{2,1,0:T(8,128)(2,1)S(1)}, bf16[1,96,320]{2,1,0:T(8,128)(2,1)S(1)}, u32[]{:S(2)}, u32[]{:S(2)}) collective-permute-start(bf16[1,96,320]{2,1,0:T(8,128)(2,1)S(1)} %get-tuple-element.77), channel_id=1, source_target_pairs={{0,16},{4,20},{8,24},{12,28},{16,0},{20,4},{24,8},{28,12},{1,17},{... | collective-permute-start | bytes 184328 | tf_op jit(solution)/shard_map/ppermute | solution.py:32
  95.9 6.2 %collective-permute-start.26 = (bf16[1,96,256]{2,1,0:T(8,128)(2,1)S(1)}, bf16[1,96,256]{2,1,0:T(8,128)(2,1)S(1)}, u32[]{:S(2)}, u32[]{:S(2)}) collective-permute-start(bf16[1,96,256]{2,1,0:T(8,128)(2,1)S(1)} %get-tuple-element.76), channel_id=1, source_target_pairs={{0,16},{4,20},{8,24},{12,28},{16,0},{20,4},{24,8},{28,12},{1,17},{... | collective-permute-start | bytes 147464 | tf_op jit(solution)/shard_map/ppermute | solution.py:32
  (10 other events, 76.9 us)

commit v9 on v8

--- a/solution.py
+++ b/solution.py
@@ -15,16 +15,11 @@
 
 NN = (((1,), (0,)), ((), ()))
 NT = (((1,), (1,)), ((), ()))
+TN = (((0,), (0,)), ((), ()))
 
 
 def mm(a, b, dims):
     return lax.dot_general(a, b, dims, preferred_element_type=F32)
-
-
-def turned(a):
-    n = a.shape[1]
-    same = lax.broadcasted_iota(jnp.int32, (n, n), 0) == lax.broadcasted_iota(jnp.int32, (n, n), 1)
-    return mm(same.astype(a.dtype), a, NT).astype(a.dtype)
 
 
 def flip(values, axis, bit):
@@ -89,7 +84,7 @@
 AHEAD = 4
 
 
-def query_key_kernel(bits, lengths, me, sheet, wq, wk, qk, held, *rest):
+def query_key_kernel(bits, where, sheet, wq, wk, qk, held, *rest):
     outs, (wt, acc, sems) = rest[:-3], rest[-3:]
     rows, cols, _ = sheet.shape
     local = wq.shape[0]
@@ -113,17 +108,17 @@
                 copies[at].wait()
                 for later in copies[at + AHEAD - 2 : at + AHEAD - 1]:
                     later.start()
-            value = (mm(wt[...], held[r], NT) * lane_mask(lengths[r], cols)).astype(BF16)
+            value = (mm(wt[...], held[r], NT) * lane_mask(where[2 + r], cols)).astype(BF16)
             qk[r] = value.reshape(2 * heads, HEAD_DIM, cols)
         some = pl.ds(first, BLOCK)
         for h in range(heads):
-            term = mm(turned(qk[some, h].reshape(flat)), qk[some, heads + h].reshape(flat), NN)
+            term = mm(qk[some, h].reshape(flat), qk[some, heads + h].reshape(flat), TN)
             term = term.reshape(acc.shape[1:])
             acc[h] = term if first == 0 else acc[h] + term
-    put_shards(me[0], acc, bits, outs)
-
-
-def query_key(lengths, me, sheet, wq, wk, bits):
+    put_shards(where[0], acc, bits, outs)
+
+
+def query_key(where, sheet, wq, wk, bits):
     rows, cols, width = sheet.shape
     shards = 1 << len(bits)
     local = wq.shape[0]
@@ -132,12 +127,11 @@
         functools.partial(query_key_kernel, bits),
         "query_key",
         [like((rows, 2 * heads, HEAD_DIM, cols)), like(sheet.shape)] + part_shapes(shards, heads, cols),
-        lengths,
-        me,
+        where,
         sheet,
         wq,
         wk,
-        scalars=2,
+        scalars=1,
         streamed=3,
         scratch=(
             pltpu.VMEM((2 * local, width), BF16),
@@ -149,7 +143,7 @@
     )
 
 
-def value_kernel(bits, lengths, me, sheet, wv, cot, *rest):
+def value_kernel(bits, where, sheet, wv, cot, *rest):
     outs, acc = rest[:-1], rest[-1]
     rows, cols, _ = sheet.shape
     local = wv.shape[0]
@@ -158,17 +152,17 @@
     for first in range(0, rows, BLOCK):
         values = []
         for r in range(first, first + BLOCK):
-            value = (mm(wv[...], sheet[r], NT) * lane_mask(lengths[r], cols)).astype(BF16)
+            value = (mm(wv[...], sheet[r], NT) * lane_mask(where[2 + r], cols)).astype(BF16)
             values.append(value.reshape(heads, HEAD_DIM, cols))
         for h in range(heads):
             left = cot[pl.ds(first, BLOCK), h * HEAD_DIM : (h + 1) * HEAD_DIM].reshape(flat)
             right = jnp.concatenate([v[h] for v in values], axis=0)
-            term = mm(turned(left), right, NN).reshape(acc.shape[1:])
+            term = mm(left, right, TN).reshape(acc.shape[1:])
             acc[h] = term if first == 0 else acc[h] + term
-    put_shards(me[0], acc, bits, outs)
-
-
-def value_dprob(lengths, me, sheet, wv, cot, after, bits):
+    put_shards(where[0], acc, bits, outs)
+
+
+def value_dprob(where, sheet, wv, cot, after, bits):
     rows, cols, width = sheet.shape
     shards = 1 << len(bits)
     local = wv.shape[0]
@@ -177,12 +171,11 @@
         functools.partial(value_kernel, bits),
         "value_dprob",
         part_shapes(shards, heads, cols),
-        lengths,
-        me,
+        where,
         sheet,
         wv,
         cot,
-        scalars=2,
+        scalars=1,
         after=after,
         scratch=(pltpu.VMEM((heads, shards, cols // shards, cols), F32),),
         limit=16,
@@ -190,22 +183,22 @@
     )
 
 
-def turn_kernel(me, wq, wk, wv, natural, full):
+def turn_kernel(where, wq, wk, wv, natural, full):
     local = wq.shape[0]
     for index, weight in enumerate((wq, wk, wv)):
         full[:, :, index * local : (index + 1) * local] = weight[...].T.reshape(full.shape[:2] + (local,))
     for j in range(natural.shape[0]):
-        natural[j] = full[me[1] ^ j]
-
-
-def turn(me, wq, wk, wv, devices, after):
+        natural[j] = full[where[1] ^ j]
+
+
+def turn(where, wq, wk, wv, devices, after):
     local, width = wq.shape
     shape = (width // devices, 3 * local)
     return in_vmem(
         turn_kernel,
         "turn",
         (like((2,) + shape),),
-        me,
+        where,
         wq,
         wk,
         wv,
@@ -215,23 +208,23 @@
     )[0]
 
 
-def far_query_key_kernel(first, lengths, sheet, wq, wk, qk):
+def far_query_key_kernel(first, where, sheet, wq, wk, qk):
     local, _ = wq.shape
     cols = sheet.shape[1]
     both = jnp.concatenate([wq[...], wk[...]], axis=0)
     for r in range(qk.shape[0]):
-        value = (mm(both, sheet[first + r], NT) * lane_mask(lengths[first + r], cols)).astype(BF16)
+        value = (mm(both, sheet[first + r], NT) * lane_mask(where[2 + first + r], cols)).astype(BF16)
         qk[r] = value.reshape(2 * local // HEAD_DIM, HEAD_DIM, cols)
 
 
-def far_query_key(first, count, lengths, sheet, wq, wk, after):
+def far_query_key(first, count, where, sheet, wq, wk, after):
     _, cols, width = sheet.shape
     local = wq.shape[0]
     return in_vmem(
         functools.partial(far_query_key_kernel, first),
         "far_query_key",
         (like((count, 2 * local // HEAD_DIM, HEAD_DIM, cols)),),
-        lengths,
+        where,
         sheet,
         wq,
         wk,
@@ -287,57 +280,68 @@
     )
 
 
-def double(values, axis, bits):
+def join_kernel(one, other, out):
+    out[: one.shape[0]] = one[...]
+    out[one.shape[0] :] = other[...]
+
+
+def join(one, other, after):
+    shape = (one.shape[0] + other.shape[0],) + one.shape[1:]
+    return in_vmem(join_kernel, "join", (like(shape),), one, other, after=after)[0]
+
+
+def double(values, axis, bits, after=()):
     order = [0]
-    for bit in bits[:-1]:
-        values = jnp.concatenate([values, flip(values, axis, bit)], axis=0)
+    after = list(after) + [()] * len(bits)
+    for bit, waits in zip(bits[:-1], after):
+        values = join(values, flip(values, axis, bit), waits)
         order = order + [j ^ bit for j in order]
     other = flip(values, axis, bits[-1])
     return (values, other), (order, [j ^ bits[-1] for j in order])
 
 
-def assemble_kernel(orders, me, *refs):
+def assemble_kernel(orders, where, *refs):
     pieces, outs = refs[:-2], refs[-2:]
     for piece, (kind, order) in zip(pieces, orders):
         for t, j in enumerate(order):
-            outs[kind][me[0] ^ j] = piece[t]
-
-
-def assemble(me, probs, dscore, orders, shards, after):
+            outs[kind][where[0] ^ j] = piece[t]
+
+
+def assemble(where, probs, dscore, orders, shards, after):
     out = like((shards,) + probs[0].shape[1:])
     return in_vmem(
-        functools.partial(assemble_kernel, [(k, o) for k, both in enumerate(orders) for o in both]), "assemble", (out, out), me, *probs, *dscore, scalars=1, after=after
-    )
-
-
-def gradients(lengths, first, at, count, probs, dscore, qk, cot, grads):
+        functools.partial(assemble_kernel, [(k, o) for k, both in enumerate(orders) for o in both]), "assemble", (out, out), where, *probs, *dscore, scalars=1, after=after
+    )
+
+
+def gradients(where, first, count, probs, dscore, qk, cot, grads):
     cols = qk.shape[-1]
     heads = qk.shape[1] // 2
-    rows, held = pl.ds(first, count), pl.ds(at, count)
+    rows = pl.ds(first, count)
     flat = (count * HEAD_DIM, cols)
     split = (count, HEAD_DIM, cols)
-    masks = jnp.stack([lane_mask(lengths[first + r], cols) for r in range(count)])
+    masks = jnp.stack([lane_mask(where[2 + first + r], cols) for r in range(count)])
     for h in range(heads):
         p, ds = [ref[:, h].reshape(cols, cols) for ref in (probs, dscore)]
         g = cot[rows, h * HEAD_DIM : (h + 1) * HEAD_DIM].reshape(flat)
-        dq = mm(qk[held, heads + h].reshape(flat), ds, NT)
-        dk = mm(qk[held, h].reshape(flat), ds, NN)
+        dq = mm(qk[rows, heads + h].reshape(flat), ds, NT)
+        dk = mm(qk[rows, h].reshape(flat), ds, NN)
         dv = mm(g, p, NN)
         for index, value in enumerate((dq, dk, dv)):
             grads[:, index * heads + h] = (value.reshape(split) * masks).astype(BF16)
 
 
-def own_gradients_kernel(lengths, probs, dscore, qk, cot, grads):
-    gradients(lengths, 0, 0, qk.shape[0], probs, dscore, qk, cot, grads)
-
-
-def own_gradients(lengths, probs, dscore, qk, cot):
+def own_gradients_kernel(where, probs, dscore, qk, cot, grads):
+    gradients(where, 0, qk.shape[0], probs, dscore, qk, cot, grads)
+
+
+def own_gradients(where, probs, dscore, qk, cot):
     rows, two, _, cols = qk.shape
     return in_vmem(
         own_gradients_kernel,
         "own_gradients",
         (like((rows, two // 2 * 3, HEAD_DIM, cols)),),
-        lengths,
+        where,
         probs,
         dscore,
         qk,
@@ -370,13 +374,13 @@
     )[0]
 
 
-def far_input_kernel(first, at, lengths, own, *refs):
+def far_input_kernel(first, where, own, *refs):
     *refs, keep, give, grads = refs
     count, share, cols = keep.shape
     total = [own[:, first + r].astype(F32) for r in range(count)]
     for i in range(0, len(refs), 5):
         probs, dscore, qk, cot, weights = refs[i : i + 5]
-        gradients(lengths, first, at, count, probs, dscore, qk, cot, grads)
+        gradients(where, first, count, probs, dscore, qk, cot, grads)
         near, _, columns = weights.shape
         left = weights[...].reshape(near * share, columns)
         for r in range(count):
@@ -387,15 +391,15 @@
         give[r] = total[r][1].astype(give.dtype)
 
 
-def far_input(first, at, count, lengths, own, far, after):
+def far_input(first, count, where, own, far, after):
     _, rows, share, cols = own.shape
     columns = far[0][-1].shape[-1]
     out = like((count, share, cols))
     return in_vmem(
-        functools.partial(far_input_kernel, first, at),
+        functools.partial(far_input_kernel, first),
         "far_input",
         (out, out),
-        lengths,
+        where,
         own,
         *[a for one in far for a in one],
         scalars=1,
@@ -411,18 +415,18 @@
     out[...] = (keep[...].astype(F32) + got[...].astype(F32)).astype(BF16)
 
 
-def finish(keep, got, first, total_rows, before):
+def finish(keep, got, first, total_rows, before, after):
     count, share, cols = keep.shape
     block = math.gcd(first, count) if first else count
     spec = pl.BlockSpec((block, share, cols), lambda s: (s, 0, 0))
-    extra = [] if before is None else [before]
+    extra = ([] if before is None else [before]) + after
     return pl.pallas_call(
         finish_kernel,
         grid=(count // block,),
         in_specs=[spec, spec] + [ANY] * len(extra),
         out_specs=pl.BlockSpec((block, share, cols), lambda s: (first // block + s, 0, 0)),
         out_shape=like((total_rows, share, cols)),
-        input_output_aliases={2: 0} if extra else {},
+        input_output_aliases={} if before is None else {2: 0},
         compiler_params=pltpu.CompilerParams(vmem_limit_bytes=12 * MIB),
         cost_estimate=cost(keep.size, keep.size * 6),
         name="finish",
@@ -436,7 +440,7 @@
     return mm(jnp.concatenate(left, axis=1), sheet[...].reshape(rows * cols, width), NN).T
 
 
-def weight_kernel(me, sheet, grads, *rest):
+def weight_kernel(where, sheet, grads, *rest):
     outs, full = rest[:-1], rest[-1]
     full[...] = weight_product(sheet, grads).reshape(full.shape)
     for j in range(full.shape[0]):
@@ -444,15 +448,15 @@
         for keep, give in zip(outs[::2], outs[1::2]):
             out = (keep, give)[j % 2]
             last = first + out.shape[-1]
-            out[j // 2] = full[me[0] ^ j, :, first:last].astype(out.dtype)
+            out[j // 2] = full[where[0] ^ j, :, first:last].astype(out.dtype)
             first = last
 
 
-def whole_weight_kernel(me, sheet, grads, out):
+def whole_weight_kernel(where, sheet, grads, out):
     out[...] = weight_product(sheet, grads)
 
 
-def weight_part(me, sheet, grads, cuts, shards):
+def weight_part(where, sheet, grads, cuts, shards):
     rows, cols, width = sheet.shape
     columns = grads.shape[1] * HEAD_DIM
     if shards == 1:
@@ -466,7 +470,7 @@
         kernel,
         "weight_part",
         outs,
-        me,
+        where,
         sheet,
         grads,
         scalars=1,
@@ -504,6 +508,7 @@
     chunk = row_dev // 4
 
     me = jnp.stack([lax.axis_index("rows"), lax.axis_index("heads")]).astype(jnp.int32)
+    where = jnp.concatenate([me, lengths])
     wq, wk, wv = w_query.T, w_key.T, w_value.T
     cot = jnp.swapaxes(cotangent, 1, 2)
 
@@ -514,34 +519,33 @@
 
     up = row_bits if direct else []
     turn_about = up[1:] + up[:1]
-    qk, held, *logits = query_key(lengths, me, sheet, wq, wk, up)
-    dprob = value_dprob(lengths, me, held, wv, cot, logits[-1:], turn_about)
-    weights = turn(me, wq, wk, wv, n_heads, dprob[-1:])
-    far_qk, far_natural = [], []
-    for w in far_weights:
-        parts = [far_query_key(r, row_dev // 2, lengths, held, w[0], w[1], ()) for r in (0, row_dev // 2)]
-        far_qk.append(parts)
-        far_natural.append(turn(me, *w, n_heads, ()))
-    before = [a for two in far_qk for a in two] + far_natural + [weights]
+    qk, held, *logits = query_key(where, sheet, wq, wk, turn_about)
+    dprob = value_dprob(where, held, wv, cot, logits[-1:], up)
+    weights = turn(where, wq, wk, wv, n_heads, dprob[-1:])
     if direct:
-        logits = halve(*logits, "rows", up)
-        dprob = halve(*dprob, "rows", turn_about)
-        probs_own, dscore_own = softmax_back(logits, dprob, scale, far_cot)
-        probs, probs_order = double(probs_own, "rows", up[::-1])
-        dscore, dscore_order = double(dscore_own, "rows", turn_about[::-1])
-        probs, dscore = assemble(me, probs, dscore, (probs_order, dscore_order), shards, [weights] + far_natural)
+        logits = halve(*logits, "rows", turn_about)
+        dprob = halve(*dprob, "rows", up)
+        probs_own, dscore_own = softmax_back(logits, dprob, scale, [weights])
+        probs, probs_order = double(probs_own, "rows", up[::-1], [far_cot])
+        dscore, dscore_order = double(dscore_own, "rows", turn_about[::-1], [far_cot])
+        probs, dscore = assemble(where, probs, dscore, (probs_order, dscore_order), shards, fq + fk + fv)
     else:
         logits, dprob = lax.psum((logits, dprob), "rows")
         probs, dscore = softmax_back(logits, dprob, scale)
     far_dscore = [flip(dscore, "heads", f) for f in fars]
     far_probs = [flip(probs, "heads", f) for f in fars]
 
-    grads = own_gradients(lengths, probs, dscore, qk, cot)
+    grads = own_gradients(where, probs, dscore, qk, cot)
     cut = 3 * local // 256 * 128
     cuts = (cut, 3 * local - cut)
-    parts = weight_part(me, held, grads, cuts, shards)
-    own = own_input(grads, weights, [parts[-1]] + far_dscore)
-    ready = [own] + far_probs
+    parts = weight_part(where, held, grads, cuts, shards)
+    ready = [parts[-1]]
+    far_qk, far_natural = [], []
+    for w in far_weights:
+        far_qk.append(far_query_key(0, row_dev, where, held, w[0], w[1], ready))
+        far_natural.append(turn(where, *w, n_heads, ready))
+    own = own_input(grads, weights, ready)
+    ready = [own] + far_qk + far_natural + far_probs
     steps = []
     if direct:
         parts = [tuple(parts[:2]), tuple(parts[2:])]
@@ -554,20 +558,18 @@
         weight_grad = lax.psum_scatter(parts[0], "rows", scatter_dimension=0, tiled=True)
         weight_grad = weight_grad.reshape(width // n_rows, 3, local)
 
+    sums = []
+    if direct:
+        weight_grad = last_sum(parts, local, ())
+        sums = [weight_grad]
+        weight_grad = jnp.swapaxes(weight_grad, 0, 1)
     out = None
-    got = []
     for index, first in enumerate(range(0, row_dev, chunk)):
         after = steps[index // 2] if index // 2 < len(steps) else ()
-        which, at = divmod(first, row_dev // 2)
-        far = [
-            (far_probs[i], far_dscore[i], far_qk[i][which], far_cot[i], far_natural[i])
-            for i in range(len(fars))
-        ]
-        keep, give = far_input(first, at, chunk, lengths, own, far, after)
-        got.append(flip(give, "heads", 1))
-        out = finish(keep, got[-1], first, row_dev, out)
-    if direct:
-        weight_grad = jnp.swapaxes(last_sum(parts, local, got[-2:]), 0, 1)
+        far = list(zip(far_probs, far_dscore, far_qk, far_cot, far_natural))
+        keep, give = far_input(first, chunk, where, own, far, after)
+        got = flip(give, "heads", 1)
+        out = finish(keep, got, first, row_dev, out, sums if index == 2 else [])
     return (jnp.swapaxes(out, 1, 2), weight_grad)
 
 

time: 104 us -> 104 us (level)
  waiting for transfers between devices: 24.5 us -> 26.9 us
  Pallas kernels: 39.1 us -> 37.3 us
    ppermute x28, waiting for transfers between devices: 24.5 us -> 26.9 us  [flip(): return lax.ppermute(values, axis, [(s, s ^ bit) for s in range(n)])]
    pallas_call x24 -> x27, Pallas kernels: 35.8 us -> 34 us  [in_vmem(): pl.pallas_call(run, in_specs=[SMEM] * scalars + [HBM] * streamed + [VMEM]...]
  transfers between devices with their start and end apart: 28 -> 28, of which waited for: 9 -> 11; matrix products, arithmetic and copies ran while one was open for 0% -> 1% of each run, Pallas kernels for 36% -> 34%
where the time goes in v9:
time: 104 us
  starting transfers between devices  38.3 us (37%)
  Pallas kernels  37.3 us (36%)
  waiting for transfers between devices  26.9 us (26%)
    ppermute x28, starting transfers between devices, flip(): return lax.ppermute(values, axis, [(s, s ^ bit) for s in range(n)])  38.3 us
    pallas_call x27, Pallas kernels, in_vmem(): pl.pallas_call(run, in_specs=[SMEM] * scalars + [HBM] * streamed + [VMEM]...  34 us
    ppermute x28, waiting for transfers between devices, flip(): return lax.ppermute(values, axis, [(s, s ^ bit) for s in range(n)])  26.9 us
    pallas_call x4, Pallas kernels, finish(): pl.pallas_call(finish_kernel, grid=(count // block,), in_specs=[spec, spe...  3.35 us
  transfers between devices with their start and end apart: 28, of which 11 were waited for; matrix products, arithmetic and copies ran while one was open for 1% of the time, Pallas kernels for 34%

profile of v9, /device:TPU:0, one launch (start us, length us, event | category | flops | bytes accessed | tf_op | source)
XLA Modules:
  0.0 104.2 jit_solution(18115654323048776413)
XLA Ops:
  0.6 3.0 %collective-permute-start.7 = (bf16[16,192,256]{2,1,0:T(8,128)(2,1)}, bf16[16,192,256]{2,1,0:T(8,128)(2,1)S(1)}, u32[]{:S(2)}, u32[]{:S(2)}) collective-permute-start(bf16[16,192,256]{2,1,0:T(8,128)(2,1)} %bitcast.8), channel_id=1, source_target_pairs={{0,2},{1,3},{2,0},{3,1},{4,6},{5,7},{6,4},{7,5},{8,10},{9,11},{10,... | collective-permute-start | bytes 4718600 | tf_op jit(solution)/shard_map/ppermute | solution.py:27
  4.4 6.9 %query_key.1 = (bf16[16,6,64,256]{3,2,1,0:T(8,128)(2,1)S(1)}, bf16[16,256,768]{2,1,0:T(8,128)(2,1)S(1)}, f32[4,3,32,256]{3,2,1,0:T(8,128)S(1)}, bf16[4,3,32,256]{3,2,1,0:T(8,128)(2,1)S(1)}) custom-call(s32[18]{0:T(128)S(1)} %pad_add_fusion.refs_0_, bf16[16,256,768]{2,1,0:T(8,128)(2,1)} %refs_1_.1, bf16[192,768]{1,0:T(8,128)(2,1)} %bitcast.12, ...), custom_call_target="tpu_custom_call" | custom-call | flops 2818572288 | bytes 16711716 | tf_op jit(solution)/shard_map/query_key/pallas_call | solution.py:56
  13.0 3.5 %value_dprob.1 = (f32[4,3,32,256]{3,2,1,0:T(8,128)S(1)}, bf16[4,3,32,256]{3,2,1,0:T(8,128)(2,1)S(1)}) custom-call(s32[18]{0:T(128)S(1)} %pad_add_fusion.refs_0_, bf16[16,256,768]{2,1,0:T(8,128)(2,1)S(1)} %get-tuple-element.46.refs_1_, bf16[192,768]{1,0:T(8,128)(2,1)S(1)} %bitcast.18, bf16[16,192,256]{2,1,0:T(8,128)(2,1)S(1)} %bitcast.9, ...), custom_call_target="tpu_custom_call" | custom-call | flops 3221225472 | bytes 8552484 | tf_op jit(solution)/shard_map/value_dprob/pallas_call | solution.py:56
  18.1 2.7 %collective-permute-start.1 = (bf16[2,3,32,256]{3,2,1,0:T(8,128)(2,1)S(1)}, bf16[2,3,32,256]{3,2,1,0:T(8,128)(2,1)S(1)}, u32[]{:S(2)}, u32[]{:S(2)}) collective-permute-start(bf16[2,3,32,256]{3,2,1,0:T(8,128)(2,1)S(1)} %get-tuple-element.43), channel_id=1, source_target_pairs={{0,16},{4,20},{8,24},{12,28},{16,0},{20,4},{24,8},{28,12},{1,17},{... | collective-permute-start | bytes 294920 | tf_op jit(solution)/shard_map/ppermute | solution.py:27
  20.8 1.9 %collective-permute-done.3.refs_1_ = bf16[4,3,32,256]{3,2,1,0:T(8,128)(2,1)S(1)} collective-permute-done((bf16[4,3,32,256]{3,2,1,0:T(8,128)(2,1)S(1)}, bf16[4,3,32,256]{3,2,1,0:T(8,128)(2,1)S(1)}, u32[]{:S(2)}, u32[]{:S(2)}) %collective-permute-start.3) | collective-permute-done | bytes 196640 | tf_op jit(solution)/shard_map/ppermute | solution.py:27
  25.1 2.3 %collective-permute-done.4.refs_1_ = bf16[2,3,32,256]{3,2,1,0:T(8,128)(2,1)S(1)} collective-permute-done((bf16[2,3,32,256]{3,2,1,0:T(8,128)(2,1)S(1)}, bf16[2,3,32,256]{3,2,1,0:T(8,128)(2,1)S(1)}, u32[]{:S(2)}, u32[]{:S(2)}) %collective-permute-start.4) | collective-permute-done | bytes 98336 | tf_op jit(solution)/shard_map/ppermute | solution.py:27
  27.4 2.9 %collective-permute-start.5 = (bf16[1,3,32,256]{3,2,1,0:T(8,128)(2,1)S(1)}, bf16[1,3,32,256]{3,2,1,0:T(8,128)(2,1)S(1)}, u32[]{:S(2)}, u32[]{:S(2)}) collective-permute-start(bf16[1,3,32,256]{3,2,1,0:T(8,128)(2,1)S(1)} %get-tuple-element.52), channel_id=1, source_target_pairs={{0,16},{4,20},{8,24},{12,28},{16,0},{20,4},{24,8},{28,12},{1,17},{... | collective-permute-start | bytes 147464 | tf_op jit(solution)/shard_map/ppermute | solution.py:27
  33.2 2.4 %collective-permute-start.6 = (bf16[1,3,32,256]{3,2,1,0:T(8,128)(2,1)S(1)}, bf16[1,3,32,256]{3,2,1,0:T(8,128)(2,1)S(1)}, u32[]{:S(2)}, u32[]{:S(2)}) collective-permute-start(bf16[1,3,32,256]{3,2,1,0:T(8,128)(2,1)S(1)} %get-tuple-element.53.refs_0_), channel_id=1, source_target_pairs={{0,16},{4,20},{8,24},{12,28},{16,0},{20,4},{24,8},{28,12},{1,17},{... | collective-permute-start | bytes 147464 | tf_op jit(solution)/shard_map/ppermute | solution.py:27
  41.3 2.7 %collective-permute-start.11 = (bf16[2,3,32,256]{3,2,1,0:T(8,128)(2,1)S(1)}, bf16[2,3,32,256]{3,2,1,0:T(8,128)(2,1)S(1)}, u32[]{:S(2)}, u32[]{:S(2)}) collective-permute-start(bf16[2,3,32,256]{3,2,1,0:T(8,128)(2,1)S(1)} %join.6.refs_0_), channel_id=1, source_target_pairs={{0,16},{4,20},{8,24},{12,28},{16,0},{20,4},{24,8},{28,12},{1,17},{... | collective-permute-start | bytes 294920 | tf_op jit(solution)/shard_map/ppermute | solution.py:27
  45.9 2.1 %collective-permute-done.11.refs_1_ = bf16[2,3,32,256]{3,2,1,0:T(8,128)(2,1)S(1)} collective-permute-done((bf16[2,3,32,256]{3,2,1,0:T(8,128)(2,1)S(1)}, bf16[2,3,32,256]{3,2,1,0:T(8,128)(2,1)S(1)}, u32[]{:S(2)}, u32[]{:S(2)}) %collective-permute-start.11) | collective-permute-done | bytes 98336 | tf_op jit(solution)/shard_map/ppermute | solution.py:27
  48.2 5.2 %collective-permute-done.14.refs_6_.refs_3_.refs_2_ = bf16[192,768]{1,0:T(8,128)(2,1)S(1)} collective-permute-done((bf16[192,768]{1,0:T(8,128)(2,1)S(1)}, bf16[192,768]{1,0:T(8,128)(2,1)S(1)}, u32[]{:S(2)}, u32[]{:S(2)}) %collective-permute-start.14) | collective-permute-done | bytes 294944 | tf_op jit(solution)/shard_map/ppermute | solution.py:27
  53.3 3.9 %collective-permute-done.15.refs_7_.refs_3_ = bf16[192,768]{1,0:T(8,128)(2,1)S(1)} collective-permute-done((bf16[192,768]{1,0:T(8,128)(2,1)S(1)}, bf16[192,768]{1,0:T(8,128)(2,1)S(1)}, u32[]{:S(2)}, u32[]{:S(2)}) %collective-permute-start.15) | collective-permute-done | bytes 294944 | tf_op jit(solution)/shard_map/ppermute | solution.py:27
  57.8 1.8 %collective-permute-start.16 = (bf16[8,3,32,256]{3,2,1,0:T(8,128)(2,1)S(1)}, bf16[8,3,32,256]{3,2,1,0:T(8,128)(2,1)S(1)}, u32[]{:S(2)}, u32[]{:S(2)}) collective-permute-start(bf16[8,3,32,256]{3,2,1,0:T(8,128)(2,1)S(1)} %get-tuple-element.55.refs_1_), channel_id=1, source_target_pairs={{0,2},{1,3},{2,0},{3,1},{4,6},{5,7},{6,4},{7,5},{8,10},{9,11},{10,... | collective-permute-start | bytes 1179656 | tf_op jit(solution)/shard_map/ppermute | solution.py:27
  59.9 1.9 %own_gradients.1.refs_2_.refs_0_ = bf16[16,9,64,256]{3,2,1,0:T(8,128)(2,1)S(1)} custom-call(s32[18]{0:T(128)S(1)} %pad_add_fusion.refs_0_, bf16[8,3,32,256]{3,2,1,0:T(8,128)(2,1)S(1)} %get-tuple-element.55.refs_1_, bf16[8,3,32,256]{3,2,1,0:T(8,128)(2,1)S(1)} %get-tuple-element.56.refs_2_, bf16[16,6,64,256]{3,2,1,0:T(8,128)(2,1)S(1)} %get-tuple-element.57.refs_3_, ...), custom_call_target="tpu_custom_call" | custom-call | flops 1207959552 | bytes 10223652 | tf_op jit(solution)/shard_map/own_gradients/pallas_call | solution.py:56
  61.9 4.7 %weight_part.1 = (f32[4,96,256]{2,1,0:T(8,128)S(1)}, bf16[4,96,256]{2,1,0:T(8,128)(2,1)S(1)}, f32[4,96,320]{2,1,0:T(8,128)S(1)}, bf16[4,96,320]{2,1,0:T(8,128)(2,1)S(1)}) custom-call(s32[18]{0:T(128)S(1)} %pad_add_fusion.refs_0_, bf16[16,256,768]{2,1,0:T(8,128)(2,1)S(1)} %get-tuple-element.46.refs_1_, bf16[16,9,64,256]{3,2,1,0:T(8,128)(2,1)S(1)} %own_gradients.1.refs_2_.refs_0_), custom_call_target="tpu_custom_call" | custom-call | flops 3623878656 | bytes 11894820 | tf_op jit(solution)/shard_map/weight_part/pallas_call | solution.py:56
  66.6 1.8 %collective-permute-start.18 = (bf16[4,96,256]{2,1,0:T(8,128)(2,1)S(1)}, bf16[4,96,256]{2,1,0:T(8,128)(2,1)S(1)}, u32[]{:S(2)}, u32[]{:S(2)}) collective-permute-start(bf16[4,96,256]{2,1,0:T(8,128)(2,1)S(1)} %get-tuple-element.60), channel_id=1, source_target_pairs={{0,4},{4,0},{8,12},{12,8},{16,20},{20,16},{24,28},{28,24},{1,5},{5... | collective-permute-start | bytes 589832 | tf_op jit(solution)/shard_map/ppermute | solution.py:27
  68.7 3.3 %far_query_key.1.refs_3_.refs_4_ = bf16[16,6,64,256]{3,2,1,0:T(8,128)(2,1)S(1)} custom-call(s32[18]{0:T(128)S(1)} %pad_add_fusion.refs_0_, bf16[16,256,768]{2,1,0:T(8,128)(2,1)S(1)} %get-tuple-element.46.refs_1_, bf16[192,768]{1,0:T(8,128)(2,1)S(1)} %collective-permute-done.13.refs_5_.refs_2_.refs_1_, ...), custom_call_target="tpu_custom_call" | custom-call | flops 2415919104 | bytes 10027044 | tf_op jit(solution)/shard_map/far_query_key/pallas_call | solution.py:56
  73.1 2.6 %own_input.1.refs_2_.refs_1_ = bf16[2,16,192,256]{3,2,1,0:T(8,128)(2,1)S(1)} custom-call(bf16[16,9,64,256]{3,2,1,0:T(8,128)(2,1)S(1)} %own_gradients.1.refs_2_.refs_0_, bf16[2,192,576]{2,1,0:T(8,128)(2,1)S(1)} %turn.2.refs_4_.refs_1_, bf16[4,96,320]{2,1,0:T(8,128)(2,1)S(1)} %get-tuple-element.58.refs_2_.refs_4_), custom_call_target="tpu_custom_call" | custom-call | flops 1811939328 | bytes 8306688 | tf_op jit(solution)/shard_map/own_input/pallas_call | solution.py:56
  75.8 1.9 %collective-permute-start.19 = (bf16[2,96,256]{2,1,0:T(8,128)(2,1)S(1)}, bf16[2,96,256]{2,1,0:T(8,128)(2,1)S(1)}, u32[]{:S(2)}, u32[]{:S(2)}) collective-permute-start(bf16[2,96,256]{2,1,0:T(8,128)(2,1)S(1)} %get-tuple-element.62), channel_id=1, source_target_pairs={{0,8},{4,12},{8,0},{12,4},{16,24},{20,28},{24,16},{28,20},{1,9},{5... | collective-permute-start | bytes 294920 | tf_op jit(solution)/shard_map/ppermute | solution.py:27
  78.3 1.8 %collective-permute-start.21 = (bf16[2,96,320]{2,1,0:T(8,128)(2,1)S(1)}, bf16[2,96,320]{2,1,0:T(8,128)(2,1)S(1)}, u32[]{:S(2)}, u32[]{:S(2)}) collective-permute-start(bf16[2,96,320]{2,1,0:T(8,128)(2,1)S(1)} %get-tuple-element.66), channel_id=1, source_target_pairs={{0,8},{4,12},{8,0},{12,4},{16,24},{20,28},{24,16},{28,20},{1,9},{5... | collective-permute-start | bytes 368648 | tf_op jit(solution)/shard_map/ppermute | solution.py:27
  88.3 2.6 %collective-permute-start.26 = (bf16[1,96,256]{2,1,0:T(8,128)(2,1)S(1)}, bf16[1,96,256]{2,1,0:T(8,128)(2,1)S(1)}, u32[]{:S(2)}, u32[]{:S(2)}) collective-permute-start(bf16[1,96,256]{2,1,0:T(8,128)(2,1)S(1)} %get-tuple-element.76), channel_id=1, source_target_pairs={{0,16},{4,20},{8,24},{12,28},{16,0},{20,4},{24,8},{28,12},{1,17},{... | collective-permute-start | bytes 147464 | tf_op jit(solution)/shard_map/ppermute | solution.py:27
  90.9 3.1 %collective-permute-done.26.refs_1_ = bf16[1,96,256]{2,1,0:T(8,128)(2,1)S(1)} collective-permute-done((bf16[1,96,256]{2,1,0:T(8,128)(2,1)S(1)}, bf16[1,96,256]{2,1,0:T(8,128)(2,1)S(1)}, u32[]{:S(2)}, u32[]{:S(2)}) %collective-permute-start.26) | collective-permute-done | bytes 49184 | tf_op jit(solution)/shard_map/ppermute | solution.py:27
  94.0 1.9 %collective-permute-start.27 = (bf16[1,96,320]{2,1,0:T(8,128)(2,1)S(1)}, bf16[1,96,320]{2,1,0:T(8,128)(2,1)S(1)}, u32[]{:S(2)}, u32[]{:S(2)}) collective-permute-start(bf16[1,96,320]{2,1,0:T(8,128)(2,1)S(1)} %get-tuple-element.77), channel_id=1, source_target_pairs={{0,16},{4,20},{8,24},{12,28},{16,0},{20,4},{24,8},{28,12},{1,17},{... | collective-permute-start | bytes 184328 | tf_op jit(solution)/shard_map/ppermute | solution.py:27
  95.9 4.1 %collective-permute-done.27.refs_3_ = bf16[1,96,320]{2,1,0:T(8,128)(2,1)S(1)} collective-permute-done((bf16[1,96,320]{2,1,0:T(8,128)(2,1)S(1)}, bf16[1,96,320]{2,1,0:T(8,128)(2,1)S(1)}, u32[]{:S(2)}, u32[]{:S(2)}) %collective-permute-start.27) | collective-permute-done | bytes 61472 | tf_op jit(solution)/shard_map/ppermute | solution.py:27
  (74 shorter events, 32.3 us)
Async XLA Ops:
  0.6 39.0 %collective-permute-start.7 = (bf16[16,192,256]{2,1,0:T(8,128)(2,1)}, bf16[16,192,256]{2,1,0:T(8,128)(2,1)S(1)}, u32[]{:S(2)}, u32[]{:S(2)}) collective-permute-start(bf16[16,192,256]{2,1,0:T(8,128)(2,1)} %bitcast.8), channel_id=1, source_target_pairs={{0,2},{1,3},{2,0},{3,1},{4,6},{5,7},{6,4},{7,5},{8,10},{9,11},{10,... | collective-permute-start | bytes 4718600 | tf_op jit(solution)/shard_map/ppermute | solution.py:27
  11.3 6.7 %collective-permute-start = (bf16[4,3,32,256]{3,2,1,0:T(8,128)(2,1)S(1)}, bf16[4,3,32,256]{3,2,1,0:T(8,128)(2,1)S(1)}, u32[]{:S(2)}, u32[]{:S(2)}) collective-permute-start(bf16[4,3,32,256]{3,2,1,0:T(8,128)(2,1)S(1)} %get-tuple-element.41.refs_4_), channel_id=1, source_target_pairs={{0,8},{4,12},{8,0},{12,4},{16,24},{20,28},{24,16},{28,20},{1,9},{5... | collective-permute-start | bytes 589832 | tf_op jit(solution)/shard_map/ppermute | solution.py:27
  16.5 6.1 %collective-permute-start.3 = (bf16[4,3,32,256]{3,2,1,0:T(8,128)(2,1)S(1)}, bf16[4,3,32,256]{3,2,1,0:T(8,128)(2,1)S(1)}, u32[]{:S(2)}, u32[]{:S(2)}) collective-permute-start(bf16[4,3,32,256]{3,2,1,0:T(8,128)(2,1)S(1)} %get-tuple-element.48.refs_4_), channel_id=1, source_target_pairs={{0,4},{4,0},{8,12},{12,8},{16,20},{20,16},{24,28},{28,24},{1,5},{5... | collective-permute-start | bytes 589832 | tf_op jit(solution)/shard_map/ppermute | solution.py:27
  18.1 6.9 %collective-permute-start.1 = (bf16[2,3,32,256]{3,2,1,0:T(8,128)(2,1)S(1)}, bf16[2,3,32,256]{3,2,1,0:T(8,128)(2,1)S(1)}, u32[]{:S(2)}, u32[]{:S(2)}) collective-permute-start(bf16[2,3,32,256]{3,2,1,0:T(8,128)(2,1)S(1)} %get-tuple-element.43), channel_id=1, source_target_pairs={{0,16},{4,20},{8,24},{12,28},{16,0},{20,4},{24,8},{28,12},{1,17},{... | collective-permute-start | bytes 294920 | tf_op jit(solution)/shard_map/ppermute | solution.py:27
  25.0 6.3 %collective-permute-start.2 = (bf16[1,3,32,256]{3,2,1,0:T(8,128)(2,1)S(1)}, bf16[1,3,32,256]{3,2,1,0:T(8,128)(2,1)S(1)}, u32[]{:S(2)}, u32[]{:S(2)}) collective-permute-start(bf16[1,3,32,256]{3,2,1,0:T(8,128)(2,1)S(1)} %get-tuple-element.45), channel_id=1, source_target_pairs={{0,4},{4,0},{8,12},{12,8},{16,20},{20,16},{24,28},{28,24},{1,5},{5... | collective-permute-start | bytes 147464 | tf_op jit(solution)/shard_map/ppermute | solution.py:27
  33.2 5.9 %collective-permute-start.6 = (bf16[1,3,32,256]{3,2,1,0:T(8,128)(2,1)S(1)}, bf16[1,3,32,256]{3,2,1,0:T(8,128)(2,1)S(1)}, u32[]{:S(2)}, u32[]{:S(2)}) collective-permute-start(bf16[1,3,32,256]{3,2,1,0:T(8,128)(2,1)S(1)} %get-tuple-element.53.refs_0_), channel_id=1, source_target_pairs={{0,16},{4,20},{8,24},{12,28},{16,0},{20,4},{24,8},{28,12},{1,17},{... | collective-permute-start | bytes 147464 | tf_op jit(solution)/shard_map/ppermute | solution.py:27
  35.6 5.7 %collective-permute-start.10 = (bf16[1,3,32,256]{3,2,1,0:T(8,128)(2,1)S(1)}, bf16[1,3,32,256]{3,2,1,0:T(8,128)(2,1)S(1)}, u32[]{:S(2)}, u32[]{:S(2)}) collective-permute-start(bf16[1,3,32,256]{3,2,1,0:T(8,128)(2,1)S(1)} %get-tuple-element.54.refs_0_), channel_id=1, source_target_pairs={{0,4},{4,0},{8,12},{12,8},{16,20},{20,16},{24,28},{28,24},{1,5},{5... | collective-permute-start | bytes 147464 | tf_op jit(solution)/shard_map/ppermute | solution.py:27
  37.1 11.1 %collective-permute-start.13 = (bf16[192,768]{1,0:T(8,128)(2,1)S(1)}, bf16[192,768]{1,0:T(8,128)(2,1)S(1)}, u32[]{:S(2)}, u32[]{:S(2)}) collective-permute-start(bf16[192,768]{1,0:T(8,128)(2,1)S(1)} %bitcast.14), channel_id=1, source_target_pairs={{0,2},{1,3},{2,0},{3,1},{4,6},{5,7},{6,4},{7,5},{8,10},{9,11},{10,... | collective-permute-start | bytes 884744 | tf_op jit(solution)/shard_map/ppermute | solution.py:27
  37.6 15.7 %collective-permute-start.14 = (bf16[192,768]{1,0:T(8,128)(2,1)S(1)}, bf16[192,768]{1,0:T(8,128)(2,1)S(1)}, u32[]{:S(2)}, u32[]{:S(2)}) collective-permute-start(bf16[192,768]{1,0:T(8,128)(2,1)S(1)} %bitcast.17), channel_id=1, source_target_pairs={{0,2},{1,3},{2,0},{3,1},{4,6},{5,7},{6,4},{7,5},{8,10},{9,11},{10,... | collective-permute-start | bytes 884744 | tf_op jit(solution)/shard_map/ppermute | solution.py:27
  39.1 18.1 %collective-permute-start.15 = (bf16[192,768]{1,0:T(8,128)(2,1)S(1)}, bf16[192,768]{1,0:T(8,128)(2,1)S(1)}, u32[]{:S(2)}, u32[]{:S(2)}) collective-permute-start(bf16[192,768]{1,0:T(8,128)(2,1)S(1)} %bitcast.20), channel_id=1, source_target_pairs={{0,2},{1,3},{2,0},{3,1},{4,6},{5,7},{6,4},{7,5},{8,10},{9,11},{10,... | collective-permute-start | bytes 884744 | tf_op jit(solution)/shard_map/ppermute | solution.py:27
  41.3 6.7 %collective-permute-start.11 = (bf16[2,3,32,256]{3,2,1,0:T(8,128)(2,1)S(1)}, bf16[2,3,32,256]{3,2,1,0:T(8,128)(2,1)S(1)}, u32[]{:S(2)}, u32[]{:S(2)}) collective-permute-start(bf16[2,3,32,256]{3,2,1,0:T(8,128)(2,1)S(1)} %join.6.refs_0_), channel_id=1, source_target_pairs={{0,16},{4,20},{8,24},{12,28},{16,0},{20,4},{24,8},{28,12},{1,17},{... | collective-permute-start | bytes 294920 | tf_op jit(solution)/shard_map/ppermute | solution.py:27
  44.4 12.8 %collective-permute-start.9 = (bf16[4,3,32,256]{3,2,1,0:T(8,128)(2,1)S(1)}, bf16[4,3,32,256]{3,2,1,0:T(8,128)(2,1)S(1)}, u32[]{:S(2)}, u32[]{:S(2)}) collective-permute-start(bf16[4,3,32,256]{3,2,1,0:T(8,128)(2,1)S(1)} %join.5.refs_1_), channel_id=1, source_target_pairs={{0,4},{4,0},{8,12},{12,8},{16,20},{20,16},{24,28},{28,24},{1,5},{5... | collective-permute-start | bytes 589832 | tf_op jit(solution)/shard_map/ppermute | solution.py:27
  48.1 9.2 %collective-permute-start.12 = (bf16[4,3,32,256]{3,2,1,0:T(8,128)(2,1)S(1)}, bf16[4,3,32,256]{3,2,1,0:T(8,128)(2,1)S(1)}, u32[]{:S(2)}, u32[]{:S(2)}) collective-permute-start(bf16[4,3,32,256]{3,2,1,0:T(8,128)(2,1)S(1)} %join.7.refs_3_), channel_id=1, source_target_pairs={{0,8},{4,12},{8,0},{12,4},{16,24},{20,28},{24,16},{28,20},{1,9},{5... | collective-permute-start | bytes 589832 | tf_op jit(solution)/shard_map/ppermute | solution.py:27
  57.8 17.9 %collective-permute-start.16 = (bf16[8,3,32,256]{3,2,1,0:T(8,128)(2,1)S(1)}, bf16[8,3,32,256]{3,2,1,0:T(8,128)(2,1)S(1)}, u32[]{:S(2)}, u32[]{:S(2)}) collective-permute-start(bf16[8,3,32,256]{3,2,1,0:T(8,128)(2,1)S(1)} %get-tuple-element.55.refs_1_), channel_id=1, source_target_pairs={{0,2},{1,3},{2,0},{3,1},{4,6},{5,7},{6,4},{7,5},{8,10},{9,11},{10,... | collective-permute-start | bytes 1179656 | tf_op jit(solution)/shard_map/ppermute | solution.py:27
  59.6 20.5 %collective-permute-start.17 = (bf16[8,3,32,256]{3,2,1,0:T(8,128)(2,1)S(1)}, bf16[8,3,32,256]{3,2,1,0:T(8,128)(2,1)S(1)}, u32[]{:S(2)}, u32[]{:S(2)}) collective-permute-start(bf16[8,3,32,256]{3,2,1,0:T(8,128)(2,1)S(1)} %get-tuple-element.56.refs_2_), channel_id=1, source_target_pairs={{0,2},{1,3},{2,0},{3,1},{4,6},{5,7},{6,4},{7,5},{8,10},{9,11},{10,... | collective-permute-start | bytes 1179656 | tf_op jit(solution)/shard_map/ppermute | solution.py:27
  66.6 9.1 %collective-permute-start.18 = (bf16[4,96,256]{2,1,0:T(8,128)(2,1)S(1)}, bf16[4,96,256]{2,1,0:T(8,128)(2,1)S(1)}, u32[]{:S(2)}, u32[]{:S(2)}) collective-permute-start(bf16[4,96,256]{2,1,0:T(8,128)(2,1)S(1)} %get-tuple-element.60), channel_id=1, source_target_pairs={{0,4},{4,0},{8,12},{12,8},{16,20},{20,16},{24,28},{28,24},{1,5},{5... | collective-permute-start | bytes 589832 | tf_op jit(solution)/shard_map/ppermute | solution.py:27
  68.4 9.9 %collective-permute-start.20 = (bf16[4,96,320]{2,1,0:T(8,128)(2,1)S(1)}, bf16[4,96,320]{2,1,0:T(8,128)(2,1)S(1)}, u32[]{:S(2)}, u32[]{:S(2)}) collective-permute-start(bf16[4,96,320]{2,1,0:T(8,128)(2,1)S(1)} %get-tuple-element.58.refs_2_.refs_4_), channel_id=1, source_target_pairs={{0,4},{4,0},{8,12},{12,8},{16,20},{20,16},{24,28},{28,24},{1,5},{5... | collective-permute-start | bytes 737288 | tf_op jit(solution)/shard_map/ppermute | solution.py:27
  75.8 8.4 %collective-permute-start.19 = (bf16[2,96,256]{2,1,0:T(8,128)(2,1)S(1)}, bf16[2,96,256]{2,1,0:T(8,128)(2,1)S(1)}, u32[]{:S(2)}, u32[]{:S(2)}) collective-permute-start(bf16[2,96,256]{2,1,0:T(8,128)(2,1)S(1)} %get-tuple-element.62), channel_id=1, source_target_pairs={{0,8},{4,12},{8,0},{12,4},{16,24},{20,28},{24,16},{28,20},{1,9},{5... | collective-permute-start | bytes 294920 | tf_op jit(solution)/shard_map/ppermute | solution.py:27
  78.3 5.9 %collective-permute-start.21 = (bf16[2,96,320]{2,1,0:T(8,128)(2,1)S(1)}, bf16[2,96,320]{2,1,0:T(8,128)(2,1)S(1)}, u32[]{:S(2)}, u32[]{:S(2)}) collective-permute-start(bf16[2,96,320]{2,1,0:T(8,128)(2,1)S(1)} %get-tuple-element.66), channel_id=1, source_target_pairs={{0,8},{4,12},{8,0},{12,4},{16,24},{20,28},{24,16},{28,20},{1,9},{5... | collective-permute-start | bytes 368648 | tf_op jit(solution)/shard_map/ppermute | solution.py:27
  81.8 19.0 %collective-permute-start.25 = (bf16[4,192,256]{2,1,0:T(8,128)(2,1)S(1)}, bf16[4,192,256]{2,1,0:T(8,128)(2,1)S(1)}, u32[]{:S(2)}, u32[]{:S(2)}) collective-permute-start(bf16[4,192,256]{2,1,0:T(8,128)(2,1)S(1)} %get-tuple-element.75), channel_id=1, source_target_pairs={{0,1},{1,0},{2,3},{3,2},{4,5},{5,4},{6,7},{7,6},{8,9},{9,8},{10,11... | collective-permute-start | bytes 1179656 | tf_op jit(solution)/shard_map/ppermute | solution.py:27
  83.6 18.1 %collective-permute-start.24 = (bf16[4,192,256]{2,1,0:T(8,128)(2,1)S(1)}, bf16[4,192,256]{2,1,0:T(8,128)(2,1)S(1)}, u32[]{:S(2)}, u32[]{:S(2)}) collective-permute-start(bf16[4,192,256]{2,1,0:T(8,128)(2,1)S(1)} %get-tuple-element.73), channel_id=1, source_target_pairs={{0,1},{1,0},{2,3},{3,2},{4,5},{5,4},{6,7},{7,6},{8,9},{9,8},{10,11... | collective-permute-start | bytes 1179656 | tf_op jit(solution)/shard_map/ppermute | solution.py:27
  86.0 16.6 %collective-permute-start.23 = (bf16[4,192,256]{2,1,0:T(8,128)(2,1)S(1)}, bf16[4,192,256]{2,1,0:T(8,128)(2,1)S(1)}, u32[]{:S(2)}, u32[]{:S(2)}) collective-permute-start(bf16[4,192,256]{2,1,0:T(8,128)(2,1)S(1)} %get-tuple-element.71), channel_id=1, source_target_pairs={{0,1},{1,0},{2,3},{3,2},{4,5},{5,4},{6,7},{7,6},{8,9},{9,8},{10,11... | collective-permute-start | bytes 1179656 | tf_op jit(solution)/shard_map/ppermute | solution.py:27
  87.8 15.6 %collective-permute-start.22 = (bf16[4,192,256]{2,1,0:T(8,128)(2,1)S(1)}, bf16[4,192,256]{2,1,0:T(8,128)(2,1)S(1)}, u32[]{:S(2)}, u32[]{:S(2)}) collective-permute-start(bf16[4,192,256]{2,1,0:T(8,128)(2,1)S(1)} %get-tuple-element.69), channel_id=1, source_target_pairs={{0,1},{1,0},{2,3},{3,2},{4,5},{5,4},{6,7},{7,6},{8,9},{9,8},{10,11... | collective-permute-start | bytes 1179656 | tf_op jit(solution)/shard_map/ppermute | solution.py:27
  94.0 6.0 %collective-permute-start.27 = (bf16[1,96,320]{2,1,0:T(8,128)(2,1)S(1)}, bf16[1,96,320]{2,1,0:T(8,128)(2,1)S(1)}, u32[]{:S(2)}, u32[]{:S(2)}) collective-permute-start(bf16[1,96,320]{2,1,0:T(8,128)(2,1)S(1)} %get-tuple-element.77), channel_id=1, source_target_pairs={{0,16},{4,20},{8,24},{12,28},{16,0},{20,4},{24,8},{28,12},{1,17},{... | collective-permute-start | bytes 184328 | tf_op jit(solution)/shard_map/ppermute | solution.py:27
  (9 other events, 74.0 us)

commit v10 on v9

--- a/solution.py
+++ b/solution.py
@@ -143,11 +143,18 @@
     )
 
 
-def value_kernel(bits, where, sheet, wv, cot, *rest):
-    outs, acc = rest[:-1], rest[-1]
-    rows, cols, _ = sheet.shape
+def value_kernel(bits, fars, where, sheet, wv, cot, *rest):
+    outs, halves, acc = rest[: -1 - len(fars)], rest[-1 - len(fars) : -1], rest[-1]
+    rows, cols, width = sheet.shape
     local = wv.shape[0]
     heads = local // HEAD_DIM
+    for far, half in zip(fars, halves):
+        near = half.shape[1]
+        side = lax.shift_right_logical(where[1], 1) ^ (far // 2)
+        for s in range(width // near):
+            @pl.when(side == s)
+            def _():
+                half[...] = wv[:, s * near : (s + 1) * near]
     flat = (BLOCK * HEAD_DIM, cols)
     for first in range(0, rows, BLOCK):
         values = []
@@ -162,15 +169,15 @@
     put_shards(where[0], acc, bits, outs)
 
 
-def value_dprob(where, sheet, wv, cot, after, bits):
+def value_dprob(where, sheet, wv, cot, after, bits, fars, devices):
     rows, cols, width = sheet.shape
     shards = 1 << len(bits)
     local = wv.shape[0]
     heads = local // HEAD_DIM
     return in_vmem(
-        functools.partial(value_kernel, bits),
+        functools.partial(value_kernel, bits, fars),
         "value_dprob",
-        part_shapes(shards, heads, cols),
+        part_shapes(shards, heads, cols) + [like((local, 2 * width // devices))] * len(fars),
         where,
         sheet,
         wv,
@@ -183,28 +190,30 @@
     )
 
 
-def turn_kernel(where, wq, wk, wv, natural, full):
+def turn_kernel(where, wq, wk, wv, natural, *full):
+    near, share, columns = natural.shape
     local = wq.shape[0]
-    for index, weight in enumerate((wq, wk, wv)):
-        full[:, :, index * local : (index + 1) * local] = weight[...].T.reshape(full.shape[:2] + (local,))
-    for j in range(natural.shape[0]):
-        natural[j] = full[where[1] ^ j]
+    for index, (weight, held) in enumerate(zip((wq, wk, wv), full)):
+        held[...] = weight[...].T.reshape(held.shape)
+        mine = where[1] & (held.shape[0] - 1)
+        for j in range(near):
+            natural[j, :, index * local : (index + 1) * local] = held[mine ^ j]
 
 
 def turn(where, wq, wk, wv, devices, after):
     local, width = wq.shape
-    shape = (width // devices, 3 * local)
+    share = width // devices
     return in_vmem(
         turn_kernel,
         "turn",
-        (like((2,) + shape),),
+        (like((2, share, 3 * local)),),
         where,
         wq,
         wk,
         wv,
         scalars=1,
         after=after,
-        scratch=(pltpu.VMEM((devices,) + shape, BF16),),
+        scratch=[pltpu.VMEM((w.shape[1] // share, share, local), BF16) for w in (wq, wk, wv)],
     )[0]
 
 
@@ -331,15 +340,15 @@
             grads[:, index * heads + h] = (value.reshape(split) * masks).astype(BF16)
 
 
-def own_gradients_kernel(where, probs, dscore, qk, cot, grads):
+def gradients_kernel(where, probs, dscore, qk, cot, grads):
     gradients(where, 0, qk.shape[0], probs, dscore, qk, cot, grads)
 
 
-def own_gradients(where, probs, dscore, qk, cot):
+def all_gradients(where, probs, dscore, qk, cot, name, after):
     rows, two, _, cols = qk.shape
     return in_vmem(
-        own_gradients_kernel,
-        "own_gradients",
+        gradients_kernel,
+        name,
         (like((rows, two // 2 * 3, HEAD_DIM, cols)),),
         where,
         probs,
@@ -347,6 +356,7 @@
         qk,
         cot,
         scalars=1,
+        after=after,
         limit=14,
         flops=3 * rows * two * HEAD_DIM * cols * cols,
     )[0]
@@ -374,63 +384,66 @@
     )[0]
 
 
-def far_input_kernel(first, where, own, *refs):
-    *refs, keep, give, grads = refs
+def far_input_kernel(first, own, *refs):
+    *refs, keep, give = refs
     count, share, cols = keep.shape
-    total = [own[:, first + r].astype(F32) for r in range(count)]
-    for i in range(0, len(refs), 5):
-        probs, dscore, qk, cot, weights = refs[i : i + 5]
-        gradients(where, first, count, probs, dscore, qk, cot, grads)
-        near, _, columns = weights.shape
-        left = weights[...].reshape(near * share, columns)
-        for r in range(count):
-            part = mm(left, grads[r].reshape(columns, cols), NN).astype(BF16)
-            total[r] = total[r] + part.reshape(near, share, cols).astype(F32)
     for r in range(count):
-        keep[r] = total[r][0].astype(keep.dtype)
-        give[r] = total[r][1].astype(give.dtype)
-
-
-def far_input(first, count, where, own, far, after):
+        total = own[:, first + r].astype(F32)
+        for i in range(0, len(refs), 2):
+            grads, weights = refs[i : i + 2]
+            near, _, columns = weights.shape
+            left = weights[...].reshape(near * share, columns)
+            part = mm(left, grads[first + r].reshape(columns, cols), NN).astype(BF16)
+            total = total + part.reshape(near, share, cols).astype(F32)
+        keep[r] = total[0].astype(keep.dtype)
+        give[r] = total[1].astype(give.dtype)
+
+
+def far_input(first, count, own, far, after):
     _, rows, share, cols = own.shape
-    columns = far[0][-1].shape[-1]
+    columns = far[0][1].shape[-1]
     out = like((count, share, cols))
     return in_vmem(
         functools.partial(far_input_kernel, first),
         "far_input",
         (out, out),
-        where,
         own,
         *[a for one in far for a in one],
-        scalars=1,
         after=after,
-        scratch=(pltpu.VMEM((count, columns // HEAD_DIM, HEAD_DIM, cols), BF16),),
-        limit=16,
-        flops=2 * len(far) * count * cols * columns * (cols + 2 * share),
-    )
-
-
-def finish_kernel(keep, got, *rest):
-    out = rest[-1]
-    out[...] = (keep[...].astype(F32) + got[...].astype(F32)).astype(BF16)
-
-
-def finish(keep, got, first, total_rows, before, after):
-    count, share, cols = keep.shape
-    block = math.gcd(first, count) if first else count
-    spec = pl.BlockSpec((block, share, cols), lambda s: (s, 0, 0))
-    extra = ([] if before is None else [before]) + after
+        limit=14,
+        flops=4 * len(far) * count * cols * columns * share,
+    )
+
+
+def finish_kernel(*refs):
+    *terms, out, total, sems = refs
+    copies = []
+    first = 0
+    for index in range(0, len(terms), 2):
+        keep, got = terms[index : index + 2]
+        some = pl.ds(first, keep.shape[0])
+        total[some] = (keep[...].astype(F32) + got[...].astype(F32)).astype(BF16)
+        copies.append(pltpu.make_async_copy(total.at[some], out.at[some], sems.at[index // 2]))
+        copies[-1].start()
+        first += keep.shape[0]
+    for copy in copies:
+        copy.wait()
+
+
+def finish(chunks):
+    _, share, cols = chunks[0][0].shape
+    rows = sum(keep.shape[0] for keep, _ in chunks)
+    terms = [a for chunk in chunks for a in chunk]
     return pl.pallas_call(
         finish_kernel,
-        grid=(count // block,),
-        in_specs=[spec, spec] + [ANY] * len(extra),
-        out_specs=pl.BlockSpec((block, share, cols), lambda s: (first // block + s, 0, 0)),
-        out_shape=like((total_rows, share, cols)),
-        input_output_aliases={} if before is None else {2: 0},
+        in_specs=[VMEM] * len(terms),
+        out_specs=HBM,
+        out_shape=like((rows, share, cols)),
+        scratch_shapes=[pltpu.VMEM((rows, share, cols), BF16), pltpu.SemaphoreType.DMA((len(chunks),))],
         compiler_params=pltpu.CompilerParams(vmem_limit_bytes=12 * MIB),
-        cost_estimate=cost(keep.size, keep.size * 6),
+        cost_estimate=cost(rows * share * cols, 6 * rows * share * cols),
         name="finish",
-    )(keep, got, *extra)
+    )(*terms)
 
 
 def weight_product(sheet, grads):
@@ -514,13 +527,14 @@
 
     fars = range(2, n_heads, 2)
     far_cot = [flip(cot, "heads", f) for f in fars]
-    far_weights = [[flip(w, "heads", f) for w in (wq, wk, wv)] for f in fars]
-    fq, fk, fv = [[w[i] for w in far_weights] for i in range(3)]
+    fq, fk = [[flip(w, "heads", f) for f in fars] for w in (wq, wk)]
 
     up = row_bits if direct else []
     turn_about = up[1:] + up[:1]
     qk, held, *logits = query_key(where, sheet, wq, wk, turn_about)
-    dprob = value_dprob(where, held, wv, cot, logits[-1:], up)
+    *dprob, = value_dprob(where, held, wv, cot, logits[-1:], up, fars, n_heads)
+    dprob, halves = dprob[: -len(fars)], dprob[-len(fars) :]
+    fv = [flip(half, "heads", f) for half, f in zip(halves, fars)]
     weights = turn(where, wq, wk, wv, n_heads, dprob[-1:])
     if direct:
         logits = halve(*logits, "rows", turn_about)
@@ -535,42 +549,39 @@
     far_dscore = [flip(dscore, "heads", f) for f in fars]
     far_probs = [flip(probs, "heads", f) for f in fars]
 
-    grads = own_gradients(where, probs, dscore, qk, cot)
-    cut = 3 * local // 256 * 128
-    cuts = (cut, 3 * local - cut)
-    parts = weight_part(where, held, grads, cuts, shards)
+    grads = all_gradients(where, probs, dscore, qk, cot, "own_gradients", ())
+    parts = weight_part(where, held, grads, (3 * local,), shards)
     ready = [parts[-1]]
     far_qk, far_natural = [], []
-    for w in far_weights:
+    for w in zip(fq, fk, fv):
         far_qk.append(far_query_key(0, row_dev, where, held, w[0], w[1], ready))
         far_natural.append(turn(where, *w, n_heads, ready))
     own = own_input(grads, weights, ready)
-    ready = [own] + far_qk + far_natural + far_probs
-    steps = []
+    ready = [own] + far_qk + far_natural + far_probs + far_dscore
+    steps = [[], []]
     if direct:
-        parts = [tuple(parts[:2]), tuple(parts[2:])]
+        keep, give = parts
+        steps = []
         for bit in row_bits[:-1]:
-            parts = [add_split(keep, flip(give, "rows", bit), ready)[::-1] for keep, give in parts]
-            steps.append([keep for keep, _ in parts])
+            give, keep = add_split(keep, flip(give, "rows", bit), ready)
+            steps.append([keep])
             ready = ()
-        parts = [(keep, flip(give, "rows", row_bits[-1])) for keep, give in parts]
+        sums = last_sum([(keep, flip(give, "rows", row_bits[-1]))], local, ())
+        weight_grad = jnp.swapaxes(sums, 0, 1)
     else:
         weight_grad = lax.psum_scatter(parts[0], "rows", scatter_dimension=0, tiled=True)
         weight_grad = weight_grad.reshape(width // n_rows, 3, local)
 
-    sums = []
-    if direct:
-        weight_grad = last_sum(parts, local, ())
-        sums = [weight_grad]
-        weight_grad = jnp.swapaxes(weight_grad, 0, 1)
-    out = None
+    far_grads = [
+        all_gradients(where, *args, "far_gradients", steps[0])
+        for args in zip(far_probs, far_dscore, far_qk, far_cot)
+    ]
+    chunks = []
     for index, first in enumerate(range(0, row_dev, chunk)):
-        after = steps[index // 2] if index // 2 < len(steps) else ()
-        far = list(zip(far_probs, far_dscore, far_qk, far_cot, far_natural))
-        keep, give = far_input(first, chunk, where, own, far, after)
-        got = flip(give, "heads", 1)
-        out = finish(keep, got, first, row_dev, out, sums if index == 2 else [])
-    return (jnp.swapaxes(out, 1, 2), weight_grad)
+        after = steps[-1] if index >= 2 else ()
+        keep, give = far_input(first, chunk, own, list(zip(far_grads, far_natural)), after)
+        chunks.append((keep, flip(give, "heads", 1)))
+    return (jnp.swapaxes(finish(chunks), 1, 2), weight_grad)
 
 
 def solution(mesh):

time: 104 us -> 101 us (0.971)
  Pallas kernels: 37.3 us -> 33.7 us
  waiting for transfers between devices: 26.9 us -> 29.7 us
  starting transfers between devices: 38.3 us -> 35.8 us
    ppermute x28 -> x25, waiting for transfers between devices: 26.9 us -> 29.7 us  [flip(): return lax.ppermute(values, axis, [(s, s ^ bit) for s in range(n)])]
    ppermute x28 -> x25, starting transfers between devices: 38.3 us -> 35.8 us  [flip(): return lax.ppermute(values, axis, [(s, s ^ bit) for s in range(n)])]
    pallas_call x4 -> x1, Pallas kernels: 3.35 us -> 1.26 us  [finish(): pl.pallas_call(finish_kernel, in_specs=[VMEM] * len(terms), out_specs=HBM...]
    pallas_call x27 -> x26, Pallas kernels: 34 us -> 32.4 us  [in_vmem(): pl.pallas_call(run, in_specs=[SMEM] * scalars + [HBM] * streamed + [VMEM]...]
  transfers between devices with their start and end apart: 28 -> 25, of which waited for: 11 -> 11; matrix products, arithmetic and copies ran while one was open for 1% -> 1% of each run, Pallas kernels for 34% -> 25%
where the time goes in v10:
time: 101 us
  starting transfers between devices  35.8 us (35%)
  Pallas kernels  33.7 us (33%)
  waiting for transfers between devices  29.7 us (29%)
  between operations  1.04 us (1%)
    ppermute x25, starting transfers between devices, flip(): return lax.ppermute(values, axis, [(s, s ^ bit) for s in range(n)])  35.8 us
    pallas_call x26, Pallas kernels, in_vmem(): pl.pallas_call(run, in_specs=[SMEM] * scalars + [HBM] * streamed + [VMEM]...  32.4 us
    ppermute x25, waiting for transfers between devices, flip(): return lax.ppermute(values, axis, [(s, s ^ bit) for s in range(n)])  29.7 us
  transfers between devices with their start and end apart: 25, of which 11 were waited for; matrix products, arithmetic and copies ran while one was open for 1% of the time, Pallas kernels for 25%

profile of v10, /device:TPU:0, one launch (start us, length us, event | category | flops | bytes accessed | tf_op | source)
XLA Modules:
  0.0 100.9 jit_solution(18068219852579941728)
XLA Ops:
  0.6 3.0 %collective-permute-start.7 = (bf16[16,192,256]{2,1,0:T(8,128)(2,1)}, bf16[16,192,256]{2,1,0:T(8,128)(2,1)S(1)}, u32[]{:S(2)}, u32[]{:S(2)}) collective-permute-start(bf16[16,192,256]{2,1,0:T(8,128)(2,1)} %bitcast.8), channel_id=1, source_target_pairs={{0,2},{1,3},{2,0},{3,1},{4,6},{5,7},{6,4},{7,5},{8,10},{9,11},{10,... | collective-permute-start | bytes 4718600 | tf_op jit(solution)/shard_map/ppermute | solution.py:27
  4.4 6.9 %query_key.1 = (bf16[16,6,64,256]{3,2,1,0:T(8,128)(2,1)S(1)}, bf16[16,256,768]{2,1,0:T(8,128)(2,1)S(1)}, f32[4,3,32,256]{3,2,1,0:T(8,128)S(1)}, bf16[4,3,32,256]{3,2,1,0:T(8,128)(2,1)S(1)}) custom-call(s32[18]{0:T(128)S(1)} %pad_add_fusion.refs_0_, bf16[16,256,768]{2,1,0:T(8,128)(2,1)} %refs_1_.1, bf16[192,768]{1,0:T(8,128)(2,1)} %bitcast.13, ...), custom_call_target="tpu_custom_call" | custom-call | flops 2818572288 | bytes 16711716 | tf_op jit(solution)/shard_map/query_key/pallas_call | solution.py:56
  13.0 3.7 %value_dprob.1 = (f32[4,3,32,256]{3,2,1,0:T(8,128)S(1)}, bf16[4,3,32,256]{3,2,1,0:T(8,128)(2,1)S(1)}, bf16[192,384]{1,0:T(8,128)(2,1)S(1)}) custom-call(s32[18]{0:T(128)S(1)} %pad_add_fusion.refs_0_, bf16[16,256,768]{2,1,0:T(8,128)(2,1)S(1)} %get-tuple-element.41.refs_1_, bf16[192,768]{1,0:T(8,128)(2,1)S(1)} %bitcast.11, bf16[16,192,256]{2,1,0:T(8,128)(2,1)S(1)} %bitcast.9, ...), custom_call_target="tpu_custom_call" | custom-call | flops 3221225472 | bytes 8699940 | tf_op jit(solution)/shard_map/value_dprob/pallas_call | solution.py:56
  18.3 2.7 %collective-permute-start.1 = (bf16[2,3,32,256]{3,2,1,0:T(8,128)(2,1)S(1)}, bf16[2,3,32,256]{3,2,1,0:T(8,128)(2,1)S(1)}, u32[]{:S(2)}, u32[]{:S(2)}) collective-permute-start(bf16[2,3,32,256]{3,2,1,0:T(8,128)(2,1)S(1)} %get-tuple-element.38), channel_id=1, source_target_pairs={{0,16},{4,20},{8,24},{12,28},{16,0},{20,4},{24,8},{28,12},{1,17},{... | collective-permute-start | bytes 294920 | tf_op jit(solution)/shard_map/ppermute | solution.py:27
  21.0 1.9 %collective-permute-done.3.refs_1_ = bf16[4,3,32,256]{3,2,1,0:T(8,128)(2,1)S(1)} collective-permute-done((bf16[4,3,32,256]{3,2,1,0:T(8,128)(2,1)S(1)}, bf16[4,3,32,256]{3,2,1,0:T(8,128)(2,1)S(1)}, u32[]{:S(2)}, u32[]{:S(2)}) %collective-permute-start.3) | collective-permute-done | bytes 196640 | tf_op jit(solution)/shard_map/ppermute | solution.py:27
  23.4 1.8 %collective-permute-done.1.refs_1_ = bf16[2,3,32,256]{3,2,1,0:T(8,128)(2,1)S(1)} collective-permute-done((bf16[2,3,32,256]{3,2,1,0:T(8,128)(2,1)S(1)}, bf16[2,3,32,256]{3,2,1,0:T(8,128)(2,1)S(1)}, u32[]{:S(2)}, u32[]{:S(2)}) %collective-permute-start.1) | collective-permute-done | bytes 98336 | tf_op jit(solution)/shard_map/ppermute | solution.py:27
  25.3 2.3 %collective-permute-done.4.refs_1_ = bf16[2,3,32,256]{3,2,1,0:T(8,128)(2,1)S(1)} collective-permute-done((bf16[2,3,32,256]{3,2,1,0:T(8,128)(2,1)S(1)}, bf16[2,3,32,256]{3,2,1,0:T(8,128)(2,1)S(1)}, u32[]{:S(2)}, u32[]{:S(2)}) %collective-permute-start.4) | collective-permute-done | bytes 98336 | tf_op jit(solution)/shard_map/ppermute | solution.py:27
  27.6 2.8 %collective-permute-start.5 = (bf16[1,3,32,256]{3,2,1,0:T(8,128)(2,1)S(1)}, bf16[1,3,32,256]{3,2,1,0:T(8,128)(2,1)S(1)}, u32[]{:S(2)}, u32[]{:S(2)}) collective-permute-start(bf16[1,3,32,256]{3,2,1,0:T(8,128)(2,1)S(1)} %get-tuple-element.47), channel_id=1, source_target_pairs={{0,16},{4,20},{8,24},{12,28},{16,0},{20,4},{24,8},{28,12},{1,17},{... | collective-permute-start | bytes 147464 | tf_op jit(solution)/shard_map/ppermute | solution.py:27
  33.4 2.4 %collective-permute-start.6 = (bf16[1,3,32,256]{3,2,1,0:T(8,128)(2,1)S(1)}, bf16[1,3,32,256]{3,2,1,0:T(8,128)(2,1)S(1)}, u32[]{:S(2)}, u32[]{:S(2)}) collective-permute-start(bf16[1,3,32,256]{3,2,1,0:T(8,128)(2,1)S(1)} %get-tuple-element.48.refs_0_), channel_id=1, source_target_pairs={{0,16},{4,20},{8,24},{12,28},{16,0},{20,4},{24,8},{28,12},{1,17},{... | collective-permute-start | bytes 147464 | tf_op jit(solution)/shard_map/ppermute | solution.py:27
  39.4 1.9 %collective-permute-start.8 = (bf16[2,3,32,256]{3,2,1,0:T(8,128)(2,1)S(1)}, bf16[2,3,32,256]{3,2,1,0:T(8,128)(2,1)S(1)}, u32[]{:S(2)}, u32[]{:S(2)}) collective-permute-start(bf16[2,3,32,256]{3,2,1,0:T(8,128)(2,1)S(1)} %join.4.refs_0_), channel_id=1, source_target_pairs={{0,8},{4,12},{8,0},{12,4},{16,24},{20,28},{24,16},{28,20},{1,9},{5... | collective-permute-start | bytes 294920 | tf_op jit(solution)/shard_map/ppermute | solution.py:27
  41.3 2.7 %collective-permute-start.11 = (bf16[2,3,32,256]{3,2,1,0:T(8,128)(2,1)S(1)}, bf16[2,3,32,256]{3,2,1,0:T(8,128)(2,1)S(1)}, u32[]{:S(2)}, u32[]{:S(2)}) collective-permute-start(bf16[2,3,32,256]{3,2,1,0:T(8,128)(2,1)S(1)} %join.6.refs_0_), channel_id=1, source_target_pairs={{0,16},{4,20},{8,24},{12,28},{16,0},{20,4},{24,8},{28,12},{1,17},{... | collective-permute-start | bytes 294920 | tf_op jit(solution)/shard_map/ppermute | solution.py:27
  45.9 2.1 %collective-permute-done.11.refs_1_ = bf16[2,3,32,256]{3,2,1,0:T(8,128)(2,1)S(1)} collective-permute-done((bf16[2,3,32,256]{3,2,1,0:T(8,128)(2,1)S(1)}, bf16[2,3,32,256]{3,2,1,0:T(8,128)(2,1)S(1)}, u32[]{:S(2)}, u32[]{:S(2)}) %collective-permute-start.11) | collective-permute-done | bytes 98336 | tf_op jit(solution)/shard_map/ppermute | solution.py:27
  49.7 4.3 %collective-permute-done.15.refs_7_.refs_3_ = bf16[192,384]{1,0:T(8,128)(2,1)S(1)} collective-permute-done((bf16[192,384]{1,0:T(8,128)(2,1)S(1)}, bf16[192,384]{1,0:T(8,128)(2,1)S(1)}, u32[]{:S(2)}, u32[]{:S(2)}) %collective-permute-start.15) | collective-permute-done | bytes 147488 | tf_op jit(solution)/shard_map/ppermute | solution.py:27
  54.7 1.9 %own_gradients.1.refs_2_.refs_0_ = bf16[16,9,64,256]{3,2,1,0:T(8,128)(2,1)S(1)} custom-call(s32[18]{0:T(128)S(1)} %pad_add_fusion.refs_0_, bf16[8,3,32,256]{3,2,1,0:T(8,128)(2,1)S(1)} %get-tuple-element.51.refs_1_, bf16[8,3,32,256]{3,2,1,0:T(8,128)(2,1)S(1)} %get-tuple-element.52.refs_2_, bf16[16,6,64,256]{3,2,1,0:T(8,128)(2,1)S(1)} %get-tuple-element.53.refs_3_, ...), custom_call_target="tpu_custom_call" | custom-call | flops 1207959552 | bytes 10223652 | tf_op jit(solution)/shard_map/own_gradients/pallas_call | solution.py:56
  56.6 4.7 %weight_part.1 = (f32[4,96,576]{2,1,0:T(8,128)S(1)}, bf16[4,96,576]{2,1,0:T(8,128)(2,1)S(1)}) custom-call(s32[18]{0:T(128)S(1)} %pad_add_fusion.refs_0_, bf16[16,256,768]{2,1,0:T(8,128)(2,1)S(1)} %get-tuple-element.41.refs_1_, bf16[16,9,64,256]{3,2,1,0:T(8,128)(2,1)S(1)} %own_gradients.1.refs_2_.refs_0_), custom_call_target="tpu_custom_call" | custom-call | flops 3623878656 | bytes 11894820 | tf_op jit(solution)/shard_map/weight_part/pallas_call | solution.py:56
  61.4 1.8 %collective-permute-start.18 = (bf16[4,96,576]{2,1,0:T(8,128)(2,1)S(1)}, bf16[4,96,576]{2,1,0:T(8,128)(2,1)S(1)}, u32[]{:S(2)}, u32[]{:S(2)}) collective-permute-start(bf16[4,96,576]{2,1,0:T(8,128)(2,1)S(1)} %get-tuple-element.54.refs_2_.refs_4_), channel_id=1, source_target_pairs={{0,4},{4,0},{8,12},{12,8},{16,20},{20,16},{24,28},{28,24},{1,5},{5... | collective-permute-start | bytes 1327112 | tf_op jit(solution)/shard_map/ppermute | solution.py:27
  66.2 2.6 %own_input.1.refs_2_.refs_0_ = bf16[2,16,192,256]{3,2,1,0:T(8,128)(2,1)S(1)} custom-call(bf16[16,9,64,256]{3,2,1,0:T(8,128)(2,1)S(1)} %own_gradients.1.refs_2_.refs_0_, bf16[2,192,576]{2,1,0:T(8,128)(2,1)S(1)} %turn.2.refs_4_.refs_1_, bf16[4,96,576]{2,1,0:T(8,128)(2,1)S(1)} %get-tuple-element.54.refs_2_.refs_4_), custom_call_target="tpu_custom_call" | custom-call | flops 1811939328 | bytes 8306688 | tf_op jit(solution)/shard_map/own_input/pallas_call | solution.py:56
  68.8 3.4 %far_query_key.1.refs_3_ = bf16[16,6,64,256]{3,2,1,0:T(8,128)(2,1)S(1)} custom-call(s32[18]{0:T(128)S(1)} %pad_add_fusion.refs_0_, bf16[16,256,768]{2,1,0:T(8,128)(2,1)S(1)} %get-tuple-element.41.refs_1_, bf16[192,768]{1,0:T(8,128)(2,1)S(1)} %collective-permute-done.13.refs_5_.refs_2_.refs_1_, ...), custom_call_target="tpu_custom_call" | custom-call | flops 2415919104 | bytes 10027044 | tf_op jit(solution)/shard_map/far_query_key/pallas_call | solution.py:56
  72.2 3.0 %collective-permute-done.16.refs_5_.refs_1_ = bf16[8,3,32,256]{3,2,1,0:T(8,128)(2,1)S(1)} collective-permute-done((bf16[8,3,32,256]{3,2,1,0:T(8,128)(2,1)S(1)}, bf16[8,3,32,256]{3,2,1,0:T(8,128)(2,1)S(1)}, u32[]{:S(2)}, u32[]{:S(2)}) %collective-permute-start.16) | collective-permute-done | bytes 393248 | tf_op jit(solution)/shard_map/ppermute | solution.py:27
  75.2 5.9 %collective-permute-done.17.refs_6_.refs_2_ = bf16[8,3,32,256]{3,2,1,0:T(8,128)(2,1)S(1)} collective-permute-done((bf16[8,3,32,256]{3,2,1,0:T(8,128)(2,1)S(1)}, bf16[8,3,32,256]{3,2,1,0:T(8,128)(2,1)S(1)}, u32[]{:S(2)}, u32[]{:S(2)}) %collective-permute-start.17) | collective-permute-done | bytes 393248 | tf_op jit(solution)/shard_map/ppermute | solution.py:27
  81.2 1.9 %collective-permute-start.21 = (bf16[2,96,576]{2,1,0:T(8,128)(2,1)S(1)}, bf16[2,96,576]{2,1,0:T(8,128)(2,1)S(1)}, u32[]{:S(2)}, u32[]{:S(2)}) collective-permute-start(bf16[2,96,576]{2,1,0:T(8,128)(2,1)S(1)} %get-tuple-element.61), channel_id=1, source_target_pairs={{0,8},{4,12},{8,0},{12,4},{16,24},{20,28},{24,16},{28,20},{1,9},{5... | collective-permute-start | bytes 663560 | tf_op jit(solution)/shard_map/ppermute | solution.py:27
  83.0 1.9 %far_gradients.1.refs_1_ = bf16[16,9,64,256]{3,2,1,0:T(8,128)(2,1)S(1)} custom-call(s32[18]{0:T(128)S(1)} %pad_add_fusion.refs_0_, bf16[8,3,32,256]{3,2,1,0:T(8,128)(2,1)S(1)} %collective-permute-done.16.refs_5_.refs_1_, bf16[8,3,32,256]{3,2,1,0:T(8,128)(2,1)S(1)} %collective-permute-done.17.refs_6_.refs_2_, ...), custom_call_target="tpu_custom_call" | custom-call | flops 1207959552 | bytes 10223652 | tf_op jit(solution)/shard_map/far_gradients/pallas_call | solution.py:56
  89.6 2.8 %collective-permute-start.24 = (bf16[1,96,576]{2,1,0:T(8,128)(2,1)S(1)}, bf16[1,96,576]{2,1,0:T(8,128)(2,1)S(1)}, u32[]{:S(2)}, u32[]{:S(2)}) collective-permute-start(bf16[1,96,576]{2,1,0:T(8,128)(2,1)S(1)} %get-tuple-element.67), channel_id=1, source_target_pairs={{0,16},{4,20},{8,24},{12,28},{16,0},{20,4},{24,8},{28,12},{1,17},{... | collective-permute-start | bytes 331784 | tf_op jit(solution)/shard_map/ppermute | solution.py:27
  92.4 6.2 %collective-permute-done.24.refs_1_ = bf16[1,96,576]{2,1,0:T(8,128)(2,1)S(1)} collective-permute-done((bf16[1,96,576]{2,1,0:T(8,128)(2,1)S(1)}, bf16[1,96,576]{2,1,0:T(8,128)(2,1)S(1)}, u32[]{:S(2)}, u32[]{:S(2)}) %collective-permute-start.24) | collective-permute-done | bytes 110624 | tf_op jit(solution)/shard_map/ppermute | solution.py:27
  (62 shorter events, 25.3 us)
Async XLA Ops:
  0.6 38.7 %collective-permute-start.7 = (bf16[16,192,256]{2,1,0:T(8,128)(2,1)}, bf16[16,192,256]{2,1,0:T(8,128)(2,1)S(1)}, u32[]{:S(2)}, u32[]{:S(2)}) collective-permute-start(bf16[16,192,256]{2,1,0:T(8,128)(2,1)} %bitcast.8), channel_id=1, source_target_pairs={{0,2},{1,3},{2,0},{3,1},{4,6},{5,7},{6,4},{7,5},{8,10},{9,11},{10,... | collective-permute-start | bytes 4718600 | tf_op jit(solution)/shard_map/ppermute | solution.py:27
  11.3 6.9 %collective-permute-start = (bf16[4,3,32,256]{3,2,1,0:T(8,128)(2,1)S(1)}, bf16[4,3,32,256]{3,2,1,0:T(8,128)(2,1)S(1)}, u32[]{:S(2)}, u32[]{:S(2)}) collective-permute-start(bf16[4,3,32,256]{3,2,1,0:T(8,128)(2,1)S(1)} %get-tuple-element.36.refs_4_), channel_id=1, source_target_pairs={{0,8},{4,12},{8,0},{12,4},{16,24},{20,28},{24,16},{28,20},{1,9},{5... | collective-permute-start | bytes 589832 | tf_op jit(solution)/shard_map/ppermute | solution.py:27
  16.7 6.1 %collective-permute-start.3 = (bf16[4,3,32,256]{3,2,1,0:T(8,128)(2,1)S(1)}, bf16[4,3,32,256]{3,2,1,0:T(8,128)(2,1)S(1)}, u32[]{:S(2)}, u32[]{:S(2)}) collective-permute-start(bf16[4,3,32,256]{3,2,1,0:T(8,128)(2,1)S(1)} %get-tuple-element.43.refs_4_), channel_id=1, source_target_pairs={{0,4},{4,0},{8,12},{12,8},{16,20},{20,16},{24,28},{28,24},{1,5},{5... | collective-permute-start | bytes 589832 | tf_op jit(solution)/shard_map/ppermute | solution.py:27
  18.3 6.9 %collective-permute-start.1 = (bf16[2,3,32,256]{3,2,1,0:T(8,128)(2,1)S(1)}, bf16[2,3,32,256]{3,2,1,0:T(8,128)(2,1)S(1)}, u32[]{:S(2)}, u32[]{:S(2)}) collective-permute-start(bf16[2,3,32,256]{3,2,1,0:T(8,128)(2,1)S(1)} %get-tuple-element.38), channel_id=1, source_target_pairs={{0,16},{4,20},{8,24},{12,28},{16,0},{20,4},{24,8},{28,12},{1,17},{... | collective-permute-start | bytes 294920 | tf_op jit(solution)/shard_map/ppermute | solution.py:27
  25.2 6.3 %collective-permute-start.2 = (bf16[1,3,32,256]{3,2,1,0:T(8,128)(2,1)S(1)}, bf16[1,3,32,256]{3,2,1,0:T(8,128)(2,1)S(1)}, u32[]{:S(2)}, u32[]{:S(2)}) collective-permute-start(bf16[1,3,32,256]{3,2,1,0:T(8,128)(2,1)S(1)} %get-tuple-element.40), channel_id=1, source_target_pairs={{0,4},{4,0},{8,12},{12,8},{16,20},{20,16},{24,28},{28,24},{1,5},{5... | collective-permute-start | bytes 147464 | tf_op jit(solution)/shard_map/ppermute | solution.py:27
  27.6 5.5 %collective-permute-start.5 = (bf16[1,3,32,256]{3,2,1,0:T(8,128)(2,1)S(1)}, bf16[1,3,32,256]{3,2,1,0:T(8,128)(2,1)S(1)}, u32[]{:S(2)}, u32[]{:S(2)}) collective-permute-start(bf16[1,3,32,256]{3,2,1,0:T(8,128)(2,1)S(1)} %get-tuple-element.47), channel_id=1, source_target_pairs={{0,16},{4,20},{8,24},{12,28},{16,0},{20,4},{24,8},{28,12},{1,17},{... | collective-permute-start | bytes 147464 | tf_op jit(solution)/shard_map/ppermute | solution.py:27
  33.4 6.0 %collective-permute-start.6 = (bf16[1,3,32,256]{3,2,1,0:T(8,128)(2,1)S(1)}, bf16[1,3,32,256]{3,2,1,0:T(8,128)(2,1)S(1)}, u32[]{:S(2)}, u32[]{:S(2)}) collective-permute-start(bf16[1,3,32,256]{3,2,1,0:T(8,128)(2,1)S(1)} %get-tuple-element.48.refs_0_), channel_id=1, source_target_pairs={{0,16},{4,20},{8,24},{12,28},{16,0},{20,4},{24,8},{28,12},{1,17},{... | collective-permute-start | bytes 147464 | tf_op jit(solution)/shard_map/ppermute | solution.py:27
  35.8 5.5 %collective-permute-start.10 = (bf16[1,3,32,256]{3,2,1,0:T(8,128)(2,1)S(1)}, bf16[1,3,32,256]{3,2,1,0:T(8,128)(2,1)S(1)}, u32[]{:S(2)}, u32[]{:S(2)}) collective-permute-start(bf16[1,3,32,256]{3,2,1,0:T(8,128)(2,1)S(1)} %get-tuple-element.49.refs_0_), channel_id=1, source_target_pairs={{0,4},{4,0},{8,12},{12,8},{16,20},{20,16},{24,28},{28,24},{1,5},{5... | collective-permute-start | bytes 147464 | tf_op jit(solution)/shard_map/ppermute | solution.py:27
  37.3 16.7 %collective-permute-start.13 = (bf16[192,768]{1,0:T(8,128)(2,1)S(1)}, bf16[192,768]{1,0:T(8,128)(2,1)S(1)}, u32[]{:S(2)}, u32[]{:S(2)}) collective-permute-start(bf16[192,768]{1,0:T(8,128)(2,1)S(1)} %bitcast.15), channel_id=1, source_target_pairs={{0,2},{1,3},{2,0},{3,1},{4,6},{5,7},{6,4},{7,5},{8,10},{9,11},{10,... | collective-permute-start | bytes 884744 | tf_op jit(solution)/shard_map/ppermute | solution.py:27
  37.9 16.2 %collective-permute-start.14 = (bf16[192,768]{1,0:T(8,128)(2,1)S(1)}, bf16[192,768]{1,0:T(8,128)(2,1)S(1)}, u32[]{:S(2)}, u32[]{:S(2)}) collective-permute-start(bf16[192,768]{1,0:T(8,128)(2,1)S(1)} %bitcast.18), channel_id=1, source_target_pairs={{0,2},{1,3},{2,0},{3,1},{4,6},{5,7},{6,4},{7,5},{8,10},{9,11},{10,... | collective-permute-start | bytes 884744 | tf_op jit(solution)/shard_map/ppermute | solution.py:27
  39.4 5.0 %collective-permute-start.8 = (bf16[2,3,32,256]{3,2,1,0:T(8,128)(2,1)S(1)}, bf16[2,3,32,256]{3,2,1,0:T(8,128)(2,1)S(1)}, u32[]{:S(2)}, u32[]{:S(2)}) collective-permute-start(bf16[2,3,32,256]{3,2,1,0:T(8,128)(2,1)S(1)} %join.4.refs_0_), channel_id=1, source_target_pairs={{0,8},{4,12},{8,0},{12,4},{16,24},{20,28},{24,16},{28,20},{1,9},{5... | collective-permute-start | bytes 294920 | tf_op jit(solution)/shard_map/ppermute | solution.py:27
  41.3 6.7 %collective-permute-start.11 = (bf16[2,3,32,256]{3,2,1,0:T(8,128)(2,1)S(1)}, bf16[2,3,32,256]{3,2,1,0:T(8,128)(2,1)S(1)}, u32[]{:S(2)}, u32[]{:S(2)}) collective-permute-start(bf16[2,3,32,256]{3,2,1,0:T(8,128)(2,1)S(1)} %join.6.refs_0_), channel_id=1, source_target_pairs={{0,16},{4,20},{8,24},{12,28},{16,0},{20,4},{24,8},{28,12},{1,17},{... | collective-permute-start | bytes 294920 | tf_op jit(solution)/shard_map/ppermute | solution.py:27
  44.4 9.7 %collective-permute-start.9 = (bf16[4,3,32,256]{3,2,1,0:T(8,128)(2,1)S(1)}, bf16[4,3,32,256]{3,2,1,0:T(8,128)(2,1)S(1)}, u32[]{:S(2)}, u32[]{:S(2)}) collective-permute-start(bf16[4,3,32,256]{3,2,1,0:T(8,128)(2,1)S(1)} %join.5.refs_1_), channel_id=1, source_target_pairs={{0,4},{4,0},{8,12},{12,8},{16,20},{20,16},{24,28},{28,24},{1,5},{5... | collective-permute-start | bytes 589832 | tf_op jit(solution)/shard_map/ppermute | solution.py:27
  48.1 6.0 %collective-permute-start.12 = (bf16[4,3,32,256]{3,2,1,0:T(8,128)(2,1)S(1)}, bf16[4,3,32,256]{3,2,1,0:T(8,128)(2,1)S(1)}, u32[]{:S(2)}, u32[]{:S(2)}) collective-permute-start(bf16[4,3,32,256]{3,2,1,0:T(8,128)(2,1)S(1)} %join.7.refs_3_), channel_id=1, source_target_pairs={{0,8},{4,12},{8,0},{12,4},{16,24},{20,28},{24,16},{28,20},{1,9},{5... | collective-permute-start | bytes 589832 | tf_op jit(solution)/shard_map/ppermute | solution.py:27
  48.2 5.9 %collective-permute-start.15 = (bf16[192,384]{1,0:T(8,128)(2,1)S(1)}, bf16[192,384]{1,0:T(8,128)(2,1)S(1)}, u32[]{:S(2)}, u32[]{:S(2)}) collective-permute-start(bf16[192,384]{1,0:T(8,128)(2,1)S(1)} %get-tuple-element.50), channel_id=1, source_target_pairs={{0,2},{1,3},{2,0},{3,1},{4,6},{5,7},{6,4},{7,5},{8,10},{9,11},{10,... | collective-permute-start | bytes 442376 | tf_op jit(solution)/shard_map/ppermute | solution.py:27
  61.4 19.7 %collective-permute-start.18 = (bf16[4,96,576]{2,1,0:T(8,128)(2,1)S(1)}, bf16[4,96,576]{2,1,0:T(8,128)(2,1)S(1)}, u32[]{:S(2)}, u32[]{:S(2)}) collective-permute-start(bf16[4,96,576]{2,1,0:T(8,128)(2,1)S(1)} %get-tuple-element.54.refs_2_.refs_4_), channel_id=1, source_target_pairs={{0,4},{4,0},{8,12},{12,8},{16,20},{20,16},{24,28},{28,24},{1,5},{5... | collective-permute-start | bytes 1327112 | tf_op jit(solution)/shard_map/ppermute | solution.py:27
  63.2 12.1 %collective-permute-start.16 = (bf16[8,3,32,256]{3,2,1,0:T(8,128)(2,1)S(1)}, bf16[8,3,32,256]{3,2,1,0:T(8,128)(2,1)S(1)}, u32[]{:S(2)}, u32[]{:S(2)}) collective-permute-start(bf16[8,3,32,256]{3,2,1,0:T(8,128)(2,1)S(1)} %get-tuple-element.51.refs_1_), channel_id=1, source_target_pairs={{0,2},{1,3},{2,0},{3,1},{4,6},{5,7},{6,4},{7,5},{8,10},{9,11},{10,... | collective-permute-start | bytes 1179656 | tf_op jit(solution)/shard_map/ppermute | solution.py:27
  64.7 16.4 %collective-permute-start.17 = (bf16[8,3,32,256]{3,2,1,0:T(8,128)(2,1)S(1)}, bf16[8,3,32,256]{3,2,1,0:T(8,128)(2,1)S(1)}, u32[]{:S(2)}, u32[]{:S(2)}) collective-permute-start(bf16[8,3,32,256]{3,2,1,0:T(8,128)(2,1)S(1)} %get-tuple-element.52.refs_2_), channel_id=1, source_target_pairs={{0,2},{1,3},{2,0},{3,1},{4,6},{5,7},{6,4},{7,5},{8,10},{9,11},{10,... | collective-permute-start | bytes 1179656 | tf_op jit(solution)/shard_map/ppermute | solution.py:27
  81.2 6.3 %collective-permute-start.21 = (bf16[2,96,576]{2,1,0:T(8,128)(2,1)S(1)}, bf16[2,96,576]{2,1,0:T(8,128)(2,1)S(1)}, u32[]{:S(2)}, u32[]{:S(2)}) collective-permute-start(bf16[2,96,576]{2,1,0:T(8,128)(2,1)S(1)} %get-tuple-element.61), channel_id=1, source_target_pairs={{0,8},{4,12},{8,0},{12,4},{16,24},{20,28},{24,16},{28,20},{1,9},{5... | collective-permute-start | bytes 663560 | tf_op jit(solution)/shard_map/ppermute | solution.py:27
  85.8 13.7 %collective-permute-start.20 = (bf16[4,192,256]{2,1,0:T(8,128)(2,1)S(1)}, bf16[4,192,256]{2,1,0:T(8,128)(2,1)S(1)}, u32[]{:S(2)}, u32[]{:S(2)}) collective-permute-start(bf16[4,192,256]{2,1,0:T(8,128)(2,1)S(1)} %get-tuple-element.60), channel_id=1, source_target_pairs={{0,1},{1,0},{2,3},{3,2},{4,5},{5,4},{6,7},{7,6},{8,9},{9,8},{10,11... | collective-permute-start | bytes 1179656 | tf_op jit(solution)/shard_map/ppermute | solution.py:27
  86.6 12.8 %collective-permute-start.19 = (bf16[4,192,256]{2,1,0:T(8,128)(2,1)S(1)}, bf16[4,192,256]{2,1,0:T(8,128)(2,1)S(1)}, u32[]{:S(2)}, u32[]{:S(2)}) collective-permute-start(bf16[4,192,256]{2,1,0:T(8,128)(2,1)S(1)} %get-tuple-element.58), channel_id=1, source_target_pairs={{0,1},{1,0},{2,3},{3,2},{4,5},{5,4},{6,7},{7,6},{8,9},{9,8},{10,11... | collective-permute-start | bytes 1179656 | tf_op jit(solution)/shard_map/ppermute | solution.py:27
  89.1 10.4 %collective-permute-start.23 = (bf16[4,192,256]{2,1,0:T(8,128)(2,1)S(1)}, bf16[4,192,256]{2,1,0:T(8,128)(2,1)S(1)}, u32[]{:S(2)}, u32[]{:S(2)}) collective-permute-start(bf16[4,192,256]{2,1,0:T(8,128)(2,1)S(1)} %get-tuple-element.66), channel_id=1, source_target_pairs={{0,1},{1,0},{2,3},{3,2},{4,5},{5,4},{6,7},{7,6},{8,9},{9,8},{10,11... | collective-permute-start | bytes 1179656 | tf_op jit(solution)/shard_map/ppermute | solution.py:27
  89.1 10.3 %collective-permute-start.22 = (bf16[4,192,256]{2,1,0:T(8,128)(2,1)S(1)}, bf16[4,192,256]{2,1,0:T(8,128)(2,1)S(1)}, u32[]{:S(2)}, u32[]{:S(2)}) collective-permute-start(bf16[4,192,256]{2,1,0:T(8,128)(2,1)S(1)} %get-tuple-element.64), channel_id=1, source_target_pairs={{0,1},{1,0},{2,3},{3,2},{4,5},{5,4},{6,7},{7,6},{8,9},{9,8},{10,11... | collective-permute-start | bytes 1179656 | tf_op jit(solution)/shard_map/ppermute | solution.py:27
  89.6 9.0 %collective-permute-start.24 = (bf16[1,96,576]{2,1,0:T(8,128)(2,1)S(1)}, bf16[1,96,576]{2,1,0:T(8,128)(2,1)S(1)}, u32[]{:S(2)}, u32[]{:S(2)}) collective-permute-start(bf16[1,96,576]{2,1,0:T(8,128)(2,1)S(1)} %get-tuple-element.67), channel_id=1, source_target_pairs={{0,16},{4,20},{8,24},{12,28},{16,0},{20,4},{24,8},{28,12},{1,17},{... | collective-permute-start | bytes 331784 | tf_op jit(solution)/shard_map/ppermute | solution.py:27
  (5 other events, 56.8 us)

commit v11 on v10

--- a/solution.py
+++ b/solution.py
@@ -45,7 +45,7 @@
     return pltpu.with_memory_space_constraint(a, pltpu.HBM) if stays else a
 
 
-def in_vmem(kernel, name, out, *operands, scalars=0, streamed=0, after=(), scratch=(), limit=12, flops=0):
+def in_vmem(kernel, name, out, *operands, scalars=0, streamed=0, after=(), scratch=(), limit=12, flops=0, hidden=True):
     many = len(after)
 
     def run(*refs):
@@ -60,7 +60,7 @@
         out_shape=list(out),
         scratch_shapes=list(scratch),
         compiler_params=pltpu.CompilerParams(vmem_limit_bytes=limit * MIB),
-        cost_estimate=cost(flops, moved),
+        cost_estimate=cost(flops, moved) if hidden else cost(0, 0),
         name=name,
     )(*[place(a, scalars <= i < scalars + streamed) for i, a in enumerate(operands)], *after)
 
@@ -213,6 +213,7 @@
         wv,
         scalars=1,
         after=after,
+        hidden=False,
         scratch=[pltpu.VMEM((w.shape[1] // share, share, local), BF16) for w in (wq, wk, wv)],
     )[0]
 
@@ -239,7 +240,7 @@
         wk,
         scalars=1,
         after=after,
-        flops=4 * count * cols * local * width,
+        hidden=False,
     )[0]
 
 
@@ -323,32 +324,40 @@
     )
 
 
-def gradients(where, first, count, probs, dscore, qk, cot, grads):
-    cols = qk.shape[-1]
+def masked(where, value, first, count):
+    cols = value.shape[-1]
+    masks = jnp.stack([lane_mask(where[2 + first + r], cols) for r in range(count)])
+    return (value.reshape(count, HEAD_DIM, cols) * masks).astype(BF16)
+
+
+def query_key_gradients(where, dscore, qk, grads):
+    rows, two, _, cols = qk.shape
+    flat = (rows * HEAD_DIM, cols)
+    heads = two // 2
+    for h in range(heads):
+        ds = dscore[:, h].reshape(cols, cols)
+        grads[:, h] = masked(where, mm(qk[:, heads + h].reshape(flat), ds, NT), 0, rows)
+        grads[:, heads + h] = masked(where, mm(qk[:, h].reshape(flat), ds, NN), 0, rows)
+
+
+def value_gradient(where, probs, cot, h, first, count):
+    cols = cot.shape[-1]
+    g = cot[pl.ds(first, count), h * HEAD_DIM : (h + 1) * HEAD_DIM].reshape(count * HEAD_DIM, cols)
+    return masked(where, mm(g, probs[:, h].reshape(cols, cols), NN), first, count)
+
+
+def own_gradients_kernel(where, probs, dscore, qk, cot, grads):
     heads = qk.shape[1] // 2
-    rows = pl.ds(first, count)
-    flat = (count * HEAD_DIM, cols)
-    split = (count, HEAD_DIM, cols)
-    masks = jnp.stack([lane_mask(where[2 + first + r], cols) for r in range(count)])
+    query_key_gradients(where, dscore, qk, grads)
     for h in range(heads):
-        p, ds = [ref[:, h].reshape(cols, cols) for ref in (probs, dscore)]
-        g = cot[rows, h * HEAD_DIM : (h + 1) * HEAD_DIM].reshape(flat)
-        dq = mm(qk[rows, heads + h].reshape(flat), ds, NT)
-        dk = mm(qk[rows, h].reshape(flat), ds, NN)
-        dv = mm(g, p, NN)
-        for index, value in enumerate((dq, dk, dv)):
-            grads[:, index * heads + h] = (value.reshape(split) * masks).astype(BF16)
-
-
-def gradients_kernel(where, probs, dscore, qk, cot, grads):
-    gradients(where, 0, qk.shape[0], probs, dscore, qk, cot, grads)
-
-
-def all_gradients(where, probs, dscore, qk, cot, name, after):
+        grads[:, 2 * heads + h] = value_gradient(where, probs, cot, h, 0, cot.shape[0])
+
+
+def own_gradients(where, probs, dscore, qk, cot):
     rows, two, _, cols = qk.shape
     return in_vmem(
-        gradients_kernel,
-        name,
+        own_gradients_kernel,
+        "own_gradients",
         (like((rows, two // 2 * 3, HEAD_DIM, cols)),),
         where,
         probs,
@@ -356,63 +365,89 @@
         qk,
         cot,
         scalars=1,
-        after=after,
         limit=14,
         flops=3 * rows * two * HEAD_DIM * cols * cols,
     )[0]
 
 
-def own_input_kernel(grads, weights, out):
+def near_input_kernel(where, own, weights, *refs):
+    *refs, out, grads = refs
     near, share, columns = weights.shape
+    rows, _, _, cols = own.shape
     left = weights[...].reshape(near * share, columns)
-    for r in range(grads.shape[0]):
-        part = mm(left, grads[r].reshape(columns, grads.shape[-1]), NN).astype(BF16)
-        out[:, r] = part.reshape(near, share, grads.shape[-1])
-
-
-def own_input(grads, weights, after):
+    for r in range(rows):
+        part = mm(left, own[r].reshape(columns, cols), NN).astype(BF16).astype(F32)
+        out[:, r] = part.reshape(near, share, cols)
+    for i in range(0, len(refs), 3):
+        dscore, qk, far = refs[i : i + 3]
+        query_key_gradients(where, dscore, qk, grads)
+        some = grads.shape[1] * HEAD_DIM
+        left = far[:, :, :some].reshape(near * share, some)
+        for r in range(rows):
+            part = mm(left, grads[r].reshape(some, cols), NN)
+            out[:, r] = out[:, r] + part.reshape(near, share, cols)
+
+
+def near_input(where, grads, weights, far):
     rows, cols = grads.shape[0], grads.shape[-1]
     near, share, columns = weights.shape
     return in_vmem(
-        own_input_kernel,
-        "own_input",
-        (like((near, rows, share, cols)),),
+        near_input_kernel,
+        "near_input",
+        (like((near, rows, share, cols), F32),),
+        where,
         grads,
         weights,
-        after=after,
-        flops=2 * rows * cols * near * share * columns,
+        *[a for one in far for a in one],
+        scalars=1,
+        scratch=(pltpu.VMEM((rows,) + far[0][1].shape[1:], BF16),),
+        limit=14,
+        hidden=False,
     )[0]
 
 
-def far_input_kernel(first, own, *refs):
+def far_input_kernel(first, where, near, *refs):
     *refs, keep, give = refs
     count, share, cols = keep.shape
+    heads = refs[0].shape[1]
+    local = heads * HEAD_DIM
+    grads = []
+    for i in range(0, len(refs), 3):
+        probs, cot, _ = refs[i : i + 3]
+        grads.append([value_gradient(where, probs, cot, h, first, count) for h in range(heads)])
     for r in range(count):
-        total = own[:, first + r].astype(F32)
-        for i in range(0, len(refs), 2):
-            grads, weights = refs[i : i + 2]
-            near, _, columns = weights.shape
-            left = weights[...].reshape(near * share, columns)
-            part = mm(left, grads[first + r].reshape(columns, cols), NN).astype(BF16)
-            total = total + part.reshape(near, share, cols).astype(F32)
+        total = near[:, first + r]
+        for i, dv in zip(range(0, len(refs), 3), grads):
+            weights = refs[i + 2]
+            left = weights[:, :, 2 * local :].reshape(2 * share, local)
+            right = jnp.concatenate([one[r] for one in dv], axis=0)
+            total = total + mm(left, right, NN).reshape(2, share, cols)
         keep[r] = total[0].astype(keep.dtype)
         give[r] = total[1].astype(give.dtype)
 
 
-def far_input(first, count, own, far, after):
-    _, rows, share, cols = own.shape
-    columns = far[0][1].shape[-1]
+def far_input(first, count, where, near, far):
+    _, rows, share, cols = near.shape
     out = like((count, share, cols))
     return in_vmem(
         functools.partial(far_input_kernel, first),
         "far_input",
         (out, out),
-        own,
+        where,
+        near,
         *[a for one in far for a in one],
-        after=after,
+        scalars=1,
         limit=14,
-        flops=4 * len(far) * count * cols * columns * share,
+        hidden=False,
     )
+
+
+def hold_kernel(values, out):
+    out[...] = values[...]
+
+
+def hold(values, after):
+    return in_vmem(hold_kernel, "hold", (like(values.shape),), values, after=after, hidden=False)[0]
 
 
 def finish_kernel(*refs):
@@ -469,7 +504,7 @@
     out[...] = weight_product(sheet, grads)
 
 
-def weight_part(where, sheet, grads, cuts, shards):
+def weight_part(where, sheet, grads, cuts, shards, after):
     rows, cols, width = sheet.shape
     columns = grads.shape[1] * HEAD_DIM
     if shards == 1:
@@ -487,26 +522,40 @@
         sheet,
         grads,
         scalars=1,
+        after=after,
         scratch=scratch,
         limit=18,
         flops=2 * rows * cols * width * columns,
     )
 
 
-def last_kernel(*refs):
-    *terms, out = refs
-    total = [terms[i][0] + terms[i + 1][0].astype(F32) for i in range(0, len(terms), 2)]
-    total = jnp.concatenate(total, axis=-1)
+def add_apart_kernel(where, keep, got, own, give):
+    mine = lax.shift_right_logical(where[0], 1)
+    for t in range(keep.shape[0]):
+        total = keep[t] + got[t].astype(F32)
+        if t == 0:
+            own[...] = total
+        give[mine ^ t] = total.astype(give.dtype)
+
+
+def add_apart(where, keep, got, after):
+    outs = (like(keep.shape[1:], F32), like(keep.shape))
+    return in_vmem(add_apart_kernel, "add_apart", outs, where, keep, got, scalars=1, after=after, hidden=False)
+
+
+def last_kernel(where, own, got, out):
+    mine = lax.shift_right_logical(where[0], 1)
+    total = own[...]
+    for t in range(1, got.shape[0]):
+        total = total + got[mine ^ t].astype(F32)
     local = out.shape[-1]
     for index in range(out.shape[0]):
         out[index] = total[:, index * local : (index + 1) * local]
 
 
-def last_sum(halves, local, after):
-    terms = [a for half in halves for a in half]
-    columns = sum(keep.shape[2] for keep, _ in halves)
-    shape = (columns // local, terms[0].shape[1], local)
-    return in_vmem(last_kernel, "last_sum", (like(shape, F32),), *terms, after=after)[0]
+def last_sum(where, own, got, local):
+    shape = (own.shape[1] // local, own.shape[0], local)
+    return in_vmem(last_kernel, "last_sum", (like(shape, F32),), where, own, got, scalars=1, hidden=False)[0]
 
 
 def body(sheet, w_query, w_key, w_value, cotangent, lengths):
@@ -542,44 +591,34 @@
         probs_own, dscore_own = softmax_back(logits, dprob, scale, [weights])
         probs, probs_order = double(probs_own, "rows", up[::-1], [far_cot])
         dscore, dscore_order = double(dscore_own, "rows", turn_about[::-1], [far_cot])
-        probs, dscore = assemble(where, probs, dscore, (probs_order, dscore_order), shards, fq + fk + fv)
+        probs, dscore = assemble(where, probs, dscore, (probs_order, dscore_order), shards, fq + fk)
     else:
         logits, dprob = lax.psum((logits, dprob), "rows")
         probs, dscore = softmax_back(logits, dprob, scale)
     far_dscore = [flip(dscore, "heads", f) for f in fars]
+    grads = own_gradients(where, probs, dscore, qk, cot)
+    parts = weight_part(where, held, grads, (3 * local,), shards, fv)
+    probs = hold(probs, [parts[-1]] + far_dscore)
     far_probs = [flip(probs, "heads", f) for f in fars]
-
-    grads = all_gradients(where, probs, dscore, qk, cot, "own_gradients", ())
-    parts = weight_part(where, held, grads, (3 * local,), shards)
-    ready = [parts[-1]]
     far_qk, far_natural = [], []
     for w in zip(fq, fk, fv):
-        far_qk.append(far_query_key(0, row_dev, where, held, w[0], w[1], ready))
-        far_natural.append(turn(where, *w, n_heads, ready))
-    own = own_input(grads, weights, ready)
-    ready = [own] + far_qk + far_natural + far_probs + far_dscore
-    steps = [[], []]
+        far_qk.append(far_query_key(0, row_dev, where, held, w[0], w[1], [probs]))
+        far_natural.append(turn(where, *w, n_heads, [probs]))
+    near = near_input(where, grads, weights, list(zip(far_dscore, far_qk, far_natural)))
     if direct:
         keep, give = parts
-        steps = []
-        for bit in row_bits[:-1]:
-            give, keep = add_split(keep, flip(give, "rows", bit), ready)
-            steps.append([keep])
-            ready = ()
-        sums = last_sum([(keep, flip(give, "rows", row_bits[-1]))], local, ())
-        weight_grad = jnp.swapaxes(sums, 0, 1)
+        own, give = add_apart(where, keep, flip(give, "rows", 1), [near])
+        lines = [list(range(first, n_rows, 2)) for first in range(2)]
+        got = lax.all_to_all(give, "rows", 0, 0, axis_index_groups=lines)
+        weight_grad = last_sum(where, own, got, local)
+        weight_grad = jnp.swapaxes(weight_grad, 0, 1)
     else:
         weight_grad = lax.psum_scatter(parts[0], "rows", scatter_dimension=0, tiled=True)
         weight_grad = weight_grad.reshape(width // n_rows, 3, local)
 
-    far_grads = [
-        all_gradients(where, *args, "far_gradients", steps[0])
-        for args in zip(far_probs, far_dscore, far_qk, far_cot)
-    ]
     chunks = []
-    for index, first in enumerate(range(0, row_dev, chunk)):
-        after = steps[-1] if index >= 2 else ()
-        keep, give = far_input(first, chunk, own, list(zip(far_grads, far_natural)), after)
+    for first in range(0, row_dev, chunk):
+        keep, give = far_input(first, chunk, where, near, list(zip(far_probs, far_cot, far_natural)))
         chunks.append((keep, flip(give, "heads", 1)))
     return (jnp.swapaxes(finish(chunks), 1, 2), weight_grad)
 

time: 101 us -> 105 us (1.040)
  waiting for transfers between devices: 29.7 us -> 14.1 us
  local copies, waits for them, and re-layouts: 0.01 us -> 11.7 us
  Pallas kernels: 33.7 us -> 41.5 us
    ppermute x25 -> x23, waiting for transfers between devices: 29.7 us -> 14.1 us  [flip(): return lax.ppermute(values, axis, [(s, s ^ bit) for s in range(n)])]
    unnamed x8 -> x30, local copies, waits for them, and re-layouts: 0.01 us -> 11.7 us
    pallas_call x26 -> x25, Pallas kernels: 32.4 us -> 39 us  [in_vmem(): pl.pallas_call(run, in_specs=[SMEM] * scalars + [HBM] * streamed + [VMEM]...]
    ppermute x25 -> x23, starting transfers between devices: 35.8 us -> 31.1 us  [flip(): return lax.ppermute(values, axis, [(s, s ^ bit) for s in range(n)])]
    all_to_all x0 -> x1, starting transfers between devices: none -> 4.17 us  [body(): got = lax.all_to_all(give, 'rows', 0, 0, axis_index_groups=lines)]
    pallas_call x1, Pallas kernels: 1.26 us -> 2.49 us  [finish(): pl.pallas_call(finish_kernel, in_specs=[VMEM] * len(terms), out_specs=HBM...]
  transfers between devices with their start and end apart: 25 -> 24, of which waited for: 11 -> 8; matrix products, arithmetic and copies ran while one was open for 1% -> 1% of each run, Pallas kernels for 25% -> 37%
where the time goes in v11:
time: 105 us; the launch traced here: 104 us
  Pallas kernels  41.5 us (40%)
  starting transfers between devices  35.2 us (34%)
  waiting for transfers between devices  14.1 us (13%)
  local copies, waits for them, and re-layouts  11.7 us (11%)
    pallas_call x25, Pallas kernels, in_vmem(): pl.pallas_call(run, in_specs=[SMEM] * scalars + [HBM] * streamed + [VMEM]...  39 us
    ppermute x23, starting transfers between devices, flip(): return lax.ppermute(values, axis, [(s, s ^ bit) for s in range(n)])  31.1 us
    ppermute x23, waiting for transfers between devices, flip(): return lax.ppermute(values, axis, [(s, s ^ bit) for s in range(n)])  14.1 us
    unnamed x30, local copies, waits for them, and re-layouts  11.7 us
    all_to_all x1, starting transfers between devices, body(): got = lax.all_to_all(give, 'rows', 0, 0, axis_index_groups=lines)  4.17 us
    pallas_call x1, Pallas kernels, finish(): pl.pallas_call(finish_kernel, in_specs=[VMEM] * len(terms), out_specs=HBM...  2.49 us
  transfers between devices with their start and end apart: 24, of which 8 were waited for; matrix products, arithmetic and copies ran while one was open for 1% of the time, Pallas kernels for 37%

profile of v11, /device:TPU:0, one launch (start us, length us, event | category | flops | bytes accessed | tf_op | source)
XLA Modules:
  0.0 104.3 jit_solution(7808383291844960275)
XLA Ops:
  0.6 3.0 %collective-permute-start.7 = (bf16[16,192,256]{2,1,0:T(8,128)(2,1)}, bf16[16,192,256]{2,1,0:T(8,128)(2,1)S(1)}, u32[]{:S(2)}, u32[]{:S(2)}) collective-permute-start(bf16[16,192,256]{2,1,0:T(8,128)(2,1)} %bitcast.8), channel_id=1, source_target_pairs={{0,2},{1,3},{2,0},{3,1},{4,6},{5,7},{6,4},{7,5},{8,10},{9,11},{10,... | collective-permute-start | bytes 4718600 | tf_op jit(solution)/shard_map/ppermute | solution.py:27
  4.4 6.9 %query_key.1 = (bf16[16,6,64,256]{3,2,1,0:T(8,128)(2,1)S(1)}, bf16[16,256,768]{2,1,0:T(8,128)(2,1)S(1)}, f32[4,3,32,256]{3,2,1,0:T(8,128)S(1)}, bf16[4,3,32,256]{3,2,1,0:T(8,128)(2,1)S(1)}) custom-call(s32[18]{0:T(128)S(1)} %pad_add_fusion.refs_0_, bf16[16,256,768]{2,1,0:T(8,128)(2,1)} %refs_1_.1, bf16[192,768]{1,0:T(8,128)(2,1)} %bitcast.13, ...), custom_call_target="tpu_custom_call" | custom-call | flops 2818572288 | bytes 16711716 | tf_op jit(solution)/shard_map/query_key/pallas_call | solution.py:56
  13.0 3.7 %value_dprob.1 = (f32[4,3,32,256]{3,2,1,0:T(8,128)S(1)}, bf16[4,3,32,256]{3,2,1,0:T(8,128)(2,1)S(1)}, bf16[192,384]{1,0:T(8,128)(2,1)S(1)}) custom-call(s32[18]{0:T(128)S(1)} %pad_add_fusion.refs_0_, bf16[16,256,768]{2,1,0:T(8,128)(2,1)S(1)} %get-tuple-element.39.refs_1_, bf16[192,768]{1,0:T(8,128)(2,1)S(1)} %bitcast.11, bf16[16,192,256]{2,1,0:T(8,128)(2,1)S(1)} %bitcast.9, ...), custom_call_target="tpu_custom_call" | custom-call | flops 3221225472 | bytes 8699940 | tf_op jit(solution)/shard_map/value_dprob/pallas_call | solution.py:56
  18.3 2.7 %collective-permute-start.1 = (bf16[2,3,32,256]{3,2,1,0:T(8,128)(2,1)S(1)}, bf16[2,3,32,256]{3,2,1,0:T(8,128)(2,1)S(1)}, u32[]{:S(2)}, u32[]{:S(2)}) collective-permute-start(bf16[2,3,32,256]{3,2,1,0:T(8,128)(2,1)S(1)} %get-tuple-element.36), channel_id=1, source_target_pairs={{0,16},{4,20},{8,24},{12,28},{16,0},{20,4},{24,8},{28,12},{1,17},{... | collective-permute-start | bytes 294920 | tf_op jit(solution)/shard_map/ppermute | solution.py:27
  21.0 1.9 %collective-permute-done.3.refs_1_ = bf16[4,3,32,256]{3,2,1,0:T(8,128)(2,1)S(1)} collective-permute-done((bf16[4,3,32,256]{3,2,1,0:T(8,128)(2,1)S(1)}, bf16[4,3,32,256]{3,2,1,0:T(8,128)(2,1)S(1)}, u32[]{:S(2)}, u32[]{:S(2)}) %collective-permute-start.3) | collective-permute-done | bytes 196640 | tf_op jit(solution)/shard_map/ppermute | solution.py:27
  25.3 2.3 %collective-permute-done.4.refs_1_ = bf16[2,3,32,256]{3,2,1,0:T(8,128)(2,1)S(1)} collective-permute-done((bf16[2,3,32,256]{3,2,1,0:T(8,128)(2,1)S(1)}, bf16[2,3,32,256]{3,2,1,0:T(8,128)(2,1)S(1)}, u32[]{:S(2)}, u32[]{:S(2)}) %collective-permute-start.4) | collective-permute-done | bytes 98336 | tf_op jit(solution)/shard_map/ppermute | solution.py:27
  27.6 2.9 %collective-permute-start.5 = (bf16[1,3,32,256]{3,2,1,0:T(8,128)(2,1)S(1)}, bf16[1,3,32,256]{3,2,1,0:T(8,128)(2,1)S(1)}, u32[]{:S(2)}, u32[]{:S(2)}) collective-permute-start(bf16[1,3,32,256]{3,2,1,0:T(8,128)(2,1)S(1)} %get-tuple-element.45), channel_id=1, source_target_pairs={{0,16},{4,20},{8,24},{12,28},{16,0},{20,4},{24,8},{28,12},{1,17},{... | collective-permute-start | bytes 147464 | tf_op jit(solution)/shard_map/ppermute | solution.py:27
  33.4 2.5 %collective-permute-start.6 = (bf16[1,3,32,256]{3,2,1,0:T(8,128)(2,1)S(1)}, bf16[1,3,32,256]{3,2,1,0:T(8,128)(2,1)S(1)}, u32[]{:S(2)}, u32[]{:S(2)}) collective-permute-start(bf16[1,3,32,256]{3,2,1,0:T(8,128)(2,1)S(1)} %get-tuple-element.46.refs_0_), channel_id=1, source_target_pairs={{0,16},{4,20},{8,24},{12,28},{16,0},{20,4},{24,8},{28,12},{1,17},{... | collective-permute-start | bytes 147464 | tf_op jit(solution)/shard_map/ppermute | solution.py:27
  39.4 1.9 %collective-permute-start.8 = (bf16[2,3,32,256]{3,2,1,0:T(8,128)(2,1)S(1)}, bf16[2,3,32,256]{3,2,1,0:T(8,128)(2,1)S(1)}, u32[]{:S(2)}, u32[]{:S(2)}) collective-permute-start(bf16[2,3,32,256]{3,2,1,0:T(8,128)(2,1)S(1)} %join.4.refs_0_), channel_id=1, source_target_pairs={{0,8},{4,12},{8,0},{12,4},{16,24},{20,28},{24,16},{28,20},{1,9},{5... | collective-permute-start | bytes 294920 | tf_op jit(solution)/shard_map/ppermute | solution.py:27
  41.3 2.7 %collective-permute-start.11 = (bf16[2,3,32,256]{3,2,1,0:T(8,128)(2,1)S(1)}, bf16[2,3,32,256]{3,2,1,0:T(8,128)(2,1)S(1)}, u32[]{:S(2)}, u32[]{:S(2)}) collective-permute-start(bf16[2,3,32,256]{3,2,1,0:T(8,128)(2,1)S(1)} %join.6.refs_0_), channel_id=1, source_target_pairs={{0,16},{4,20},{8,24},{12,28},{16,0},{20,4},{24,8},{28,12},{1,17},{... | collective-permute-start | bytes 294920 | tf_op jit(solution)/shard_map/ppermute | solution.py:27
  45.9 2.1 %collective-permute-done.11.refs_1_ = bf16[2,3,32,256]{3,2,1,0:T(8,128)(2,1)S(1)} collective-permute-done((bf16[2,3,32,256]{3,2,1,0:T(8,128)(2,1)S(1)}, bf16[2,3,32,256]{3,2,1,0:T(8,128)(2,1)S(1)}, u32[]{:S(2)}, u32[]{:S(2)}) %collective-permute-start.11) | collective-permute-done | bytes 98336 | tf_op jit(solution)/shard_map/ppermute | solution.py:27
  49.7 2.8 %collective-permute-done.14.refs_6_.refs_3_.refs_2_ = bf16[192,768]{1,0:T(8,128)(2,1)S(1)} collective-permute-done((bf16[192,768]{1,0:T(8,128)(2,1)S(1)}, bf16[192,768]{1,0:T(8,128)(2,1)S(1)}, u32[]{:S(2)}, u32[]{:S(2)}) %collective-permute-start.14) | collective-permute-done | bytes 294944 | tf_op jit(solution)/shard_map/ppermute | solution.py:27
  56.0 1.9 %own_gradients.1.refs_2_.refs_1_ = bf16[16,9,64,256]{3,2,1,0:T(8,128)(2,1)S(1)} custom-call(s32[18]{0:T(128)S(1)} %pad_add_fusion.refs_0_, bf16[8,3,32,256]{3,2,1,0:T(8,128)(2,1)S(1)} %get-tuple-element.48.refs_1_.refs_0_, bf16[8,3,32,256]{3,2,1,0:T(8,128)(2,1)S(1)} %get-tuple-element.49.refs_2_, bf16[16,6,64,256]{3,2,1,0:T(8,128)(2,1)S(1)} %get-tuple-element.50.refs_3_, ...), custom_call_target="tpu_custom_call" | custom-call | flops 1207959552 | bytes 10223652 | tf_op jit(solution)/shard_map/own_gradients/pallas_call | solution.py:56
  57.9 4.7 %weight_part.1 = (f32[4,96,576]{2,1,0:T(8,128)S(1)}, bf16[4,96,576]{2,1,0:T(8,128)(2,1)S(1)}) custom-call(s32[18]{0:T(128)S(1)} %pad_add_fusion.refs_0_, bf16[16,256,768]{2,1,0:T(8,128)(2,1)S(1)} %get-tuple-element.39.refs_1_, bf16[16,9,64,256]{3,2,1,0:T(8,128)(2,1)S(1)} %own_gradients.1.refs_2_.refs_1_, bf16[192,384]{1,0:T(8,128)(2,1)S(1)} %collective-permute-done.16.refs_3_), custom_call_target="tpu_custom_call" | custom-call | flops 3623878656 | bytes 11894820 | tf_op jit(solution)/shard_map/weight_part/pallas_call | solution.py:56
  65.0 3.2 %far_query_key.1.refs_4_ = bf16[16,6,64,256]{3,2,1,0:T(8,128)(2,1)S(1)} custom-call(s32[18]{0:T(128)S(1)} %pad_add_fusion.refs_0_, bf16[16,256,768]{2,1,0:T(8,128)(2,1)S(1)} %get-tuple-element.39.refs_1_, bf16[192,768]{1,0:T(8,128)(2,1)S(1)} %collective-permute-done.13.refs_5_.refs_2_.refs_1_, ...), custom_call_target="tpu_custom_call" | custom-call | tf_op jit(solution)/shard_map/far_query_key/pallas_call | solution.py:56
  69.2 5.9 %near_input.1.refs_1_.refs_3_ = f32[2,16,192,256]{3,2,1,0:T(8,128)S(1)} custom-call(s32[18]{0:T(128)S(1)} %pad_add_fusion.refs_0_, bf16[16,9,64,256]{3,2,1,0:T(8,128)(2,1)S(1)} %own_gradients.1.refs_2_.refs_1_, bf16[2,192,576]{2,1,0:T(8,128)(2,1)S(1)} %turn.2.refs_4_.refs_2_, bf16[8,3,32,256]{3,2,1,0:T(8,128)(2,1)S(1)} %collective-permute-done.15.refs_2_.refs_3_, ...), custom_call_target="tpu_custom_call" | custom-call | tf_op jit(solution)/shard_map/near_input/pallas_call | solution.py:56
  75.8 2.0 %copy-done = f32[2,16,192,256]{3,2,1,0:T(8,128)} copy-done((f32[2,16,192,256]{3,2,1,0:T(8,128)}, f32[2,16,192,256]{3,2,1,0:T(8,128)S(1)}, u32[]{:S(2)}) %copy-start) | copy-done | bytes 6291480
  79.3 4.2 %all-to-all-start = ((bf16[4,96,576]{2,1,0:T(8,128)(2,1)}), bf16[4,96,576]{2,1,0:T(8,128)(2,1)S(1)}, u32[]{:S(2)}, u32[]{:S(2)}) async-start(bf16[4,96,576]{2,1,0:T(8,128)(2,1)} %copy-done.3), calls=%async_computation | async-start | bytes 983040 | tf_op jit(solution)/shard_map/all_to_all | solution.py:612
  83.5 2.8 %copy-done.1 = f32[2,16,192,256]{3,2,1,0:T(8,128)S(1)} copy-done((f32[2,16,192,256]{3,2,1,0:T(8,128)S(1)}, f32[2,16,192,256]{3,2,1,0:T(8,128)}, u32[]{:S(2)}) %copy-start.1) | copy-done | bytes 6291480
  86.3 1.9 %far_input.7 = (bf16[4,192,256]{2,1,0:T(8,128)(2,1)S(1)}, bf16[4,192,256]{2,1,0:T(8,128)(2,1)}) custom-call(s32[18]{0:T(128)S(1)} %pad_add_fusion.refs_0_, f32[2,16,192,256]{3,2,1,0:T(8,128)S(1)} %copy-done.1, bf16[8,3,32,256]{3,2,1,0:T(8,128)(2,1)S(1)} %collective-permute-done.17.refs_2_, bf16[16,192,256]{2,1,0:T(8,128)(2,1)S(1)} %collective-permute-done.7.refs_2_.refs_3_, ...), custom_call_target="tpu_custom_call" | custom-call | tf_op jit(solution)/shard_map/far_input/pallas_call | solution.py:56
  88.2 1.9 %far_input.6 = (bf16[4,192,256]{2,1,0:T(8,128)(2,1)S(1)}, bf16[4,192,256]{2,1,0:T(8,128)(2,1)}) custom-call(s32[18]{0:T(128)S(1)} %pad_add_fusion.refs_0_, f32[2,16,192,256]{3,2,1,0:T(8,128)S(1)} %copy-done.1, bf16[8,3,32,256]{3,2,1,0:T(8,128)(2,1)S(1)} %collective-permute-done.17.refs_2_, bf16[16,192,256]{2,1,0:T(8,128)(2,1)S(1)} %collective-permute-done.7.refs_2_.refs_3_, ...), custom_call_target="tpu_custom_call" | custom-call | tf_op jit(solution)/shard_map/far_input/pallas_call | solution.py:56
  90.5 1.9 %far_input.5 = (bf16[4,192,256]{2,1,0:T(8,128)(2,1)S(1)}, bf16[4,192,256]{2,1,0:T(8,128)(2,1)}) custom-call(s32[18]{0:T(128)S(1)} %pad_add_fusion.refs_0_, f32[2,16,192,256]{3,2,1,0:T(8,128)S(1)} %copy-done.1, bf16[8,3,32,256]{3,2,1,0:T(8,128)(2,1)S(1)} %collective-permute-done.17.refs_2_, bf16[16,192,256]{2,1,0:T(8,128)(2,1)S(1)} %collective-permute-done.7.refs_2_.refs_3_, ...), custom_call_target="tpu_custom_call" | custom-call | tf_op jit(solution)/shard_map/far_input/pallas_call | solution.py:56
  93.2 1.9 %far_input.4 = (bf16[4,192,256]{2,1,0:T(8,128)(2,1)S(1)}, bf16[4,192,256]{2,1,0:T(8,128)(2,1)}) custom-call(s32[18]{0:T(128)S(1)} %pad_add_fusion.refs_0_, f32[2,16,192,256]{3,2,1,0:T(8,128)S(1)} %copy-done.1, bf16[8,3,32,256]{3,2,1,0:T(8,128)(2,1)S(1)} %collective-permute-done.17.refs_2_, bf16[16,192,256]{2,1,0:T(8,128)(2,1)S(1)} %collective-permute-done.7.refs_2_.refs_3_, ...), custom_call_target="tpu_custom_call" | custom-call | tf_op jit(solution)/shard_map/far_input/pallas_call | solution.py:56
  101.7 2.5 %finish.1 = bf16[16,192,256]{2,1,0:T(8,128)(2,1)} custom-call(bf16[4,192,256]{2,1,0:T(8,128)(2,1)S(1)} %copy-done.9, bf16[4,192,256]{2,1,0:T(8,128)(2,1)S(1)} %collective-permute-done.18.refs_1_, bf16[4,192,256]{2,1,0:T(8,128)(2,1)S(1)} %copy-done.7, bf16[4,192,256]{2,1,0:T(8,128)(2,1)} %collective-permute-done.19.refs_3_, ...), custom_call_target="tpu_custom_call" | custom-call | flops 786432 | bytes 4718592 | tf_op jit(solution)/shard_map/finish/pallas_call | solution.py:472
  (81 shorter events, 33.3 us)
Async XLA Ops:
  0.6 38.7 %collective-permute-start.7 = (bf16[16,192,256]{2,1,0:T(8,128)(2,1)}, bf16[16,192,256]{2,1,0:T(8,128)(2,1)S(1)}, u32[]{:S(2)}, u32[]{:S(2)}) collective-permute-start(bf16[16,192,256]{2,1,0:T(8,128)(2,1)} %bitcast.8), channel_id=1, source_target_pairs={{0,2},{1,3},{2,0},{3,1},{4,6},{5,7},{6,4},{7,5},{8,10},{9,11},{10,... | collective-permute-start | bytes 4718600 | tf_op jit(solution)/shard_map/ppermute | solution.py:27
  11.3 6.9 %collective-permute-start = (bf16[4,3,32,256]{3,2,1,0:T(8,128)(2,1)S(1)}, bf16[4,3,32,256]{3,2,1,0:T(8,128)(2,1)S(1)}, u32[]{:S(2)}, u32[]{:S(2)}) collective-permute-start(bf16[4,3,32,256]{3,2,1,0:T(8,128)(2,1)S(1)} %get-tuple-element.34.refs_4_), channel_id=1, source_target_pairs={{0,8},{4,12},{8,0},{12,4},{16,24},{20,28},{24,16},{28,20},{1,9},{5... | collective-permute-start | bytes 589832 | tf_op jit(solution)/shard_map/ppermute | solution.py:27
  16.7 6.1 %collective-permute-start.3 = (bf16[4,3,32,256]{3,2,1,0:T(8,128)(2,1)S(1)}, bf16[4,3,32,256]{3,2,1,0:T(8,128)(2,1)S(1)}, u32[]{:S(2)}, u32[]{:S(2)}) collective-permute-start(bf16[4,3,32,256]{3,2,1,0:T(8,128)(2,1)S(1)} %get-tuple-element.41.refs_4_), channel_id=1, source_target_pairs={{0,4},{4,0},{8,12},{12,8},{16,20},{20,16},{24,28},{28,24},{1,5},{5... | collective-permute-start | bytes 589832 | tf_op jit(solution)/shard_map/ppermute | solution.py:27
  18.3 6.9 %collective-permute-start.1 = (bf16[2,3,32,256]{3,2,1,0:T(8,128)(2,1)S(1)}, bf16[2,3,32,256]{3,2,1,0:T(8,128)(2,1)S(1)}, u32[]{:S(2)}, u32[]{:S(2)}) collective-permute-start(bf16[2,3,32,256]{3,2,1,0:T(8,128)(2,1)S(1)} %get-tuple-element.36), channel_id=1, source_target_pairs={{0,16},{4,20},{8,24},{12,28},{16,0},{20,4},{24,8},{28,12},{1,17},{... | collective-permute-start | bytes 294920 | tf_op jit(solution)/shard_map/ppermute | solution.py:27
  22.9 4.7 %collective-permute-start.4 = (bf16[2,3,32,256]{3,2,1,0:T(8,128)(2,1)S(1)}, bf16[2,3,32,256]{3,2,1,0:T(8,128)(2,1)S(1)}, u32[]{:S(2)}, u32[]{:S(2)}) collective-permute-start(bf16[2,3,32,256]{3,2,1,0:T(8,128)(2,1)S(1)} %get-tuple-element.43), channel_id=1, source_target_pairs={{0,8},{4,12},{8,0},{12,4},{16,24},{20,28},{24,16},{28,20},{1,9},{5... | collective-permute-start | bytes 294920 | tf_op jit(solution)/shard_map/ppermute | solution.py:27
  25.2 6.3 %collective-permute-start.2 = (bf16[1,3,32,256]{3,2,1,0:T(8,128)(2,1)S(1)}, bf16[1,3,32,256]{3,2,1,0:T(8,128)(2,1)S(1)}, u32[]{:S(2)}, u32[]{:S(2)}) collective-permute-start(bf16[1,3,32,256]{3,2,1,0:T(8,128)(2,1)S(1)} %get-tuple-element.38), channel_id=1, source_target_pairs={{0,4},{4,0},{8,12},{12,8},{16,20},{20,16},{24,28},{28,24},{1,5},{5... | collective-permute-start | bytes 147464 | tf_op jit(solution)/shard_map/ppermute | solution.py:27
  27.6 5.5 %collective-permute-start.5 = (bf16[1,3,32,256]{3,2,1,0:T(8,128)(2,1)S(1)}, bf16[1,3,32,256]{3,2,1,0:T(8,128)(2,1)S(1)}, u32[]{:S(2)}, u32[]{:S(2)}) collective-permute-start(bf16[1,3,32,256]{3,2,1,0:T(8,128)(2,1)S(1)} %get-tuple-element.45), channel_id=1, source_target_pairs={{0,16},{4,20},{8,24},{12,28},{16,0},{20,4},{24,8},{28,12},{1,17},{... | collective-permute-start | bytes 147464 | tf_op jit(solution)/shard_map/ppermute | solution.py:27
  33.4 6.0 %collective-permute-start.6 = (bf16[1,3,32,256]{3,2,1,0:T(8,128)(2,1)S(1)}, bf16[1,3,32,256]{3,2,1,0:T(8,128)(2,1)S(1)}, u32[]{:S(2)}, u32[]{:S(2)}) collective-permute-start(bf16[1,3,32,256]{3,2,1,0:T(8,128)(2,1)S(1)} %get-tuple-element.46.refs_0_), channel_id=1, source_target_pairs={{0,16},{4,20},{8,24},{12,28},{16,0},{20,4},{24,8},{28,12},{1,17},{... | collective-permute-start | bytes 147464 | tf_op jit(solution)/shard_map/ppermute | solution.py:27
  35.8 5.5 %collective-permute-start.10 = (bf16[1,3,32,256]{3,2,1,0:T(8,128)(2,1)S(1)}, bf16[1,3,32,256]{3,2,1,0:T(8,128)(2,1)S(1)}, u32[]{:S(2)}, u32[]{:S(2)}) collective-permute-start(bf16[1,3,32,256]{3,2,1,0:T(8,128)(2,1)S(1)} %get-tuple-element.47.refs_0_), channel_id=1, source_target_pairs={{0,4},{4,0},{8,12},{12,8},{16,20},{20,16},{24,28},{28,24},{1,5},{5... | collective-permute-start | bytes 147464 | tf_op jit(solution)/shard_map/ppermute | solution.py:27
  37.3 12.4 %collective-permute-start.13 = (bf16[192,768]{1,0:T(8,128)(2,1)S(1)}, bf16[192,768]{1,0:T(8,128)(2,1)S(1)}, u32[]{:S(2)}, u32[]{:S(2)}) collective-permute-start(bf16[192,768]{1,0:T(8,128)(2,1)S(1)} %bitcast.15), channel_id=1, source_target_pairs={{0,2},{1,3},{2,0},{3,1},{4,6},{5,7},{6,4},{7,5},{8,10},{9,11},{10,... | collective-permute-start | bytes 884744 | tf_op jit(solution)/shard_map/ppermute | solution.py:27
  37.8 14.6 %collective-permute-start.14 = (bf16[192,768]{1,0:T(8,128)(2,1)S(1)}, bf16[192,768]{1,0:T(8,128)(2,1)S(1)}, u32[]{:S(2)}, u32[]{:S(2)}) collective-permute-start(bf16[192,768]{1,0:T(8,128)(2,1)S(1)} %bitcast.18), channel_id=1, source_target_pairs={{0,2},{1,3},{2,0},{3,1},{4,6},{5,7},{6,4},{7,5},{8,10},{9,11},{10,... | collective-permute-start | bytes 884744 | tf_op jit(solution)/shard_map/ppermute | solution.py:27
  39.4 5.0 %collective-permute-start.8 = (bf16[2,3,32,256]{3,2,1,0:T(8,128)(2,1)S(1)}, bf16[2,3,32,256]{3,2,1,0:T(8,128)(2,1)S(1)}, u32[]{:S(2)}, u32[]{:S(2)}) collective-permute-start(bf16[2,3,32,256]{3,2,1,0:T(8,128)(2,1)S(1)} %join.4.refs_0_), channel_id=1, source_target_pairs={{0,8},{4,12},{8,0},{12,4},{16,24},{20,28},{24,16},{28,20},{1,9},{5... | collective-permute-start | bytes 294920 | tf_op jit(solution)/shard_map/ppermute | solution.py:27
  41.3 6.7 %collective-permute-start.11 = (bf16[2,3,32,256]{3,2,1,0:T(8,128)(2,1)S(1)}, bf16[2,3,32,256]{3,2,1,0:T(8,128)(2,1)S(1)}, u32[]{:S(2)}, u32[]{:S(2)}) collective-permute-start(bf16[2,3,32,256]{3,2,1,0:T(8,128)(2,1)S(1)} %join.6.refs_0_), channel_id=1, source_target_pairs={{0,16},{4,20},{8,24},{12,28},{16,0},{20,4},{24,8},{28,12},{1,17},{... | collective-permute-start | bytes 294920 | tf_op jit(solution)/shard_map/ppermute | solution.py:27
  44.4 8.1 %collective-permute-start.9 = (bf16[4,3,32,256]{3,2,1,0:T(8,128)(2,1)S(1)}, bf16[4,3,32,256]{3,2,1,0:T(8,128)(2,1)S(1)}, u32[]{:S(2)}, u32[]{:S(2)}) collective-permute-start(bf16[4,3,32,256]{3,2,1,0:T(8,128)(2,1)S(1)} %join.5.refs_1_), channel_id=1, source_target_pairs={{0,4},{4,0},{8,12},{12,8},{16,20},{20,16},{24,28},{28,24},{1,5},{5... | collective-permute-start | bytes 589832 | tf_op jit(solution)/shard_map/ppermute | solution.py:27
  48.1 5.7 %collective-permute-start.12 = (bf16[4,3,32,256]{3,2,1,0:T(8,128)(2,1)S(1)}, bf16[4,3,32,256]{3,2,1,0:T(8,128)(2,1)S(1)}, u32[]{:S(2)}, u32[]{:S(2)}) collective-permute-start(bf16[4,3,32,256]{3,2,1,0:T(8,128)(2,1)S(1)} %join.7.refs_3_), channel_id=1, source_target_pairs={{0,8},{4,12},{8,0},{12,4},{16,24},{20,28},{24,16},{28,20},{1,9},{5... | collective-permute-start | bytes 589832 | tf_op jit(solution)/shard_map/ppermute | solution.py:27
  48.2 9.8 %collective-permute-start.16 = (bf16[192,384]{1,0:T(8,128)(2,1)S(1)}, bf16[192,384]{1,0:T(8,128)(2,1)S(1)}, u32[]{:S(2)}, u32[]{:S(2)}) collective-permute-start(bf16[192,384]{1,0:T(8,128)(2,1)S(1)} %get-tuple-element.51), channel_id=1, source_target_pairs={{0,2},{1,3},{2,0},{3,1},{4,6},{5,7},{6,4},{7,5},{8,10},{9,11},{10,... | collective-permute-start | bytes 442376 | tf_op jit(solution)/shard_map/ppermute | solution.py:27
  54.4 9.8 %collective-permute-start.15 = (bf16[8,3,32,256]{3,2,1,0:T(8,128)(2,1)S(1)}, bf16[8,3,32,256]{3,2,1,0:T(8,128)(2,1)S(1)}, u32[]{:S(2)}, u32[]{:S(2)}) collective-permute-start(bf16[8,3,32,256]{3,2,1,0:T(8,128)(2,1)S(1)} %get-tuple-element.49.refs_2_), channel_id=1, source_target_pairs={{0,2},{1,3},{2,0},{3,1},{4,6},{5,7},{6,4},{7,5},{8,10},{9,11},{10,... | collective-permute-start | bytes 1179656 | tf_op jit(solution)/shard_map/ppermute | solution.py:27
  62.7 12.5 %collective-permute-start.22 = (bf16[4,96,576]{2,1,0:T(8,128)(2,1)S(1)}, bf16[4,96,576]{2,1,0:T(8,128)(2,1)S(1)}, u32[]{:S(2)}, u32[]{:S(2)}) collective-permute-start(bf16[4,96,576]{2,1,0:T(8,128)(2,1)S(1)} %get-tuple-element.52.refs_1_), channel_id=1, source_target_pairs={{0,4},{4,0},{8,12},{12,8},{16,20},{20,16},{24,28},{28,24},{1,5},{5... | collective-permute-start | bytes 1327112 | tf_op jit(solution)/shard_map/ppermute | solution.py:27
  64.3 19.3 %collective-permute-start.17 = (bf16[8,3,32,256]{3,2,1,0:T(8,128)(2,1)S(1)}, bf16[8,3,32,256]{3,2,1,0:T(8,128)(2,1)S(1)}, u32[]{:S(2)}, u32[]{:S(2)}) collective-permute-start(bf16[8,3,32,256]{3,2,1,0:T(8,128)(2,1)S(1)} %hold.1.refs_4_), channel_id=1, source_target_pairs={{0,2},{1,3},{2,0},{3,1},{4,6},{5,7},{6,4},{7,5},{8,10},{9,11},{10,... | collective-permute-start | bytes 1179656 | tf_op jit(solution)/shard_map/ppermute | solution.py:27
  79.3 17.0 %all-to-all-start = ((bf16[4,96,576]{2,1,0:T(8,128)(2,1)}), bf16[4,96,576]{2,1,0:T(8,128)(2,1)S(1)}, u32[]{:S(2)}, u32[]{:S(2)}) async-start(bf16[4,96,576]{2,1,0:T(8,128)(2,1)} %copy-done.3), calls=%async_computation | async-start | bytes 983040 | tf_op jit(solution)/shard_map/all_to_all | solution.py:612
  88.2 10.5 %collective-permute-start.21 = (bf16[4,192,256]{2,1,0:T(8,128)(2,1)}, bf16[4,192,256]{2,1,0:T(8,128)(2,1)}, u32[]{:S(2)}, u32[]{:S(2)}) collective-permute-start(bf16[4,192,256]{2,1,0:T(8,128)(2,1)} %get-tuple-element.60), channel_id=1, source_target_pairs={{0,1},{1,0},{2,3},{3,2},{4,5},{5,4},{6,7},{7,6},{8,9},{9,8},{10,11... | collective-permute-start | bytes 1179656 | tf_op jit(solution)/shard_map/ppermute | solution.py:27
  90.0 8.6 %collective-permute-start.20 = (bf16[4,192,256]{2,1,0:T(8,128)(2,1)}, bf16[4,192,256]{2,1,0:T(8,128)(2,1)}, u32[]{:S(2)}, u32[]{:S(2)}) collective-permute-start(bf16[4,192,256]{2,1,0:T(8,128)(2,1)} %get-tuple-element.58), channel_id=1, source_target_pairs={{0,1},{1,0},{2,3},{3,2},{4,5},{5,4},{6,7},{7,6},{8,9},{9,8},{10,11... | collective-permute-start | bytes 1179656 | tf_op jit(solution)/shard_map/ppermute | solution.py:27
  93.2 5.5 %collective-permute-start.19 = (bf16[4,192,256]{2,1,0:T(8,128)(2,1)}, bf16[4,192,256]{2,1,0:T(8,128)(2,1)}, u32[]{:S(2)}, u32[]{:S(2)}) collective-permute-start(bf16[4,192,256]{2,1,0:T(8,128)(2,1)} %get-tuple-element.56), channel_id=1, source_target_pairs={{0,1},{1,0},{2,3},{3,2},{4,5},{5,4},{6,7},{7,6},{8,9},{9,8},{10,11... | collective-permute-start | bytes 1179656 | tf_op jit(solution)/shard_map/ppermute | solution.py:27
  95.8 2.8 %collective-permute-start.18 = (bf16[4,192,256]{2,1,0:T(8,128)(2,1)}, bf16[4,192,256]{2,1,0:T(8,128)(2,1)S(1)}, u32[]{:S(2)}, u32[]{:S(2)}) collective-permute-start(bf16[4,192,256]{2,1,0:T(8,128)(2,1)} %get-tuple-element.54), channel_id=1, source_target_pairs={{0,1},{1,0},{2,3},{3,2},{4,5},{5,4},{6,7},{7,6},{8,9},{9,8},{10,11... | collective-permute-start | bytes 1179656 | tf_op jit(solution)/shard_map/ppermute | solution.py:27
  (15 other events, 67.0 us)

commit v12 on v11

--- a/solution.py
+++ b/solution.py
@@ -45,7 +45,7 @@
     return pltpu.with_memory_space_constraint(a, pltpu.HBM) if stays else a
 
 
-def in_vmem(kernel, name, out, *operands, scalars=0, streamed=0, after=(), scratch=(), limit=12, flops=0, hidden=True):
+def in_vmem(kernel, name, out, *operands, scalars=0, streamed=0, after=(), scratch=(), limit=12, flops=0):
     many = len(after)
 
     def run(*refs):
@@ -60,7 +60,7 @@
         out_shape=list(out),
         scratch_shapes=list(scratch),
         compiler_params=pltpu.CompilerParams(vmem_limit_bytes=limit * MIB),
-        cost_estimate=cost(flops, moved) if hidden else cost(0, 0),
+        cost_estimate=cost(flops, moved),
         name=name,
     )(*[place(a, scalars <= i < scalars + streamed) for i, a in enumerate(operands)], *after)
 
@@ -213,7 +213,6 @@
         wv,
         scalars=1,
         after=after,
-        hidden=False,
         scratch=[pltpu.VMEM((w.shape[1] // share, share, local), BF16) for w in (wq, wk, wv)],
     )[0]
 
@@ -240,7 +239,6 @@
         wk,
         scalars=1,
         after=after,
-        hidden=False,
     )[0]
 
 
@@ -370,67 +368,65 @@
     )[0]
 
 
-def near_input_kernel(where, own, weights, *refs):
-    *refs, out, grads = refs
+def near_input_kernel(fars, where, own, weights, *refs):
+    far, outs, grads = refs[: 3 * fars], refs[3 * fars : -1], refs[-1]
     near, share, columns = weights.shape
     rows, _, _, cols = own.shape
-    left = weights[...].reshape(near * share, columns)
+    count = rows // len(outs)
+    some = grads.shape[2] * HEAD_DIM
+    for i in range(fars):
+        query_key_gradients(where, *far[3 * i : 3 * i + 2], grads.at[i])
     for r in range(rows):
-        part = mm(left, own[r].reshape(columns, cols), NN).astype(BF16).astype(F32)
-        out[:, r] = part.reshape(near, share, cols)
-    for i in range(0, len(refs), 3):
-        dscore, qk, far = refs[i : i + 3]
-        query_key_gradients(where, dscore, qk, grads)
-        some = grads.shape[1] * HEAD_DIM
-        left = far[:, :, :some].reshape(near * share, some)
-        for r in range(rows):
-            part = mm(left, grads[r].reshape(some, cols), NN)
-            out[:, r] = out[:, r] + part.reshape(near, share, cols)
-
-
-def near_input(where, grads, weights, far):
+        left = weights[...].reshape(near * share, columns)
+        total = mm(left, own[r].reshape(columns, cols), NN)
+        for i in range(fars):
+            left = far[3 * i + 2][:, :, :some].reshape(near * share, some)
+            total = total + mm(left, grads[i, r].reshape(some, cols), NN)
+        outs[r // count][:, r % count] = total.astype(BF16).reshape(near, share, cols)
+
+
+def near_input(where, grads, weights, far, chunk):
     rows, cols = grads.shape[0], grads.shape[-1]
     near, share, columns = weights.shape
     return in_vmem(
-        near_input_kernel,
+        functools.partial(near_input_kernel, len(far)),
         "near_input",
-        (like((near, rows, share, cols), F32),),
+        [like((near, chunk, share, cols))] * (rows // chunk),
         where,
         grads,
         weights,
         *[a for one in far for a in one],
         scalars=1,
-        scratch=(pltpu.VMEM((rows,) + far[0][1].shape[1:], BF16),),
+        scratch=(pltpu.VMEM((len(far), rows) + far[0][1].shape[1:], BF16),),
         limit=14,
-        hidden=False,
-    )[0]
-
-
-def far_input_kernel(first, where, near, *refs):
-    *refs, keep, give = refs
+        flops=2 * rows * cols * near * share * columns * (1 + len(far)),
+    )
+
+
+def far_input_kernel(first, fars, where, near, *refs):
+    far, keep, give = refs[: 3 * fars], refs[-2], refs[-1]
     count, share, cols = keep.shape
-    heads = refs[0].shape[1]
+    heads = far[0].shape[1]
     local = heads * HEAD_DIM
     grads = []
-    for i in range(0, len(refs), 3):
-        probs, cot, _ = refs[i : i + 3]
+    for i in range(fars):
+        probs, cot, _ = far[3 * i : 3 * i + 3]
         grads.append([value_gradient(where, probs, cot, h, first, count) for h in range(heads)])
     for r in range(count):
-        total = near[:, first + r]
-        for i, dv in zip(range(0, len(refs), 3), grads):
-            weights = refs[i + 2]
-            left = weights[:, :, 2 * local :].reshape(2 * share, local)
+        total = near[:, r].astype(F32)
+        for i, dv in enumerate(grads):
+            left = far[3 * i + 2][:, :, 2 * local :].reshape(2 * share, local)
             right = jnp.concatenate([one[r] for one in dv], axis=0)
             total = total + mm(left, right, NN).reshape(2, share, cols)
         keep[r] = total[0].astype(keep.dtype)
         give[r] = total[1].astype(give.dtype)
 
 
-def far_input(first, count, where, near, far):
-    _, rows, share, cols = near.shape
+def far_input(first, where, near, far):
+    _, count, share, cols = near.shape
     out = like((count, share, cols))
     return in_vmem(
-        functools.partial(far_input_kernel, first),
+        functools.partial(far_input_kernel, first, len(far)),
         "far_input",
         (out, out),
         where,
@@ -438,7 +434,6 @@
         *[a for one in far for a in one],
         scalars=1,
         limit=14,
-        hidden=False,
     )
 
 
@@ -447,7 +442,7 @@
 
 
 def hold(values, after):
-    return in_vmem(hold_kernel, "hold", (like(values.shape),), values, after=after, hidden=False)[0]
+    return in_vmem(hold_kernel, "hold", (like(values.shape),), values, after=after)[0]
 
 
 def finish_kernel(*refs):
@@ -540,7 +535,7 @@
 
 def add_apart(where, keep, got, after):
     outs = (like(keep.shape[1:], F32), like(keep.shape))
-    return in_vmem(add_apart_kernel, "add_apart", outs, where, keep, got, scalars=1, after=after, hidden=False)
+    return in_vmem(add_apart_kernel, "add_apart", outs, where, keep, got, scalars=1, after=after)
 
 
 def last_kernel(where, own, got, out):
@@ -555,7 +550,7 @@
 
 def last_sum(where, own, got, local):
     shape = (own.shape[1] // local, own.shape[0], local)
-    return in_vmem(last_kernel, "last_sum", (like(shape, F32),), where, own, got, scalars=1, hidden=False)[0]
+    return in_vmem(last_kernel, "last_sum", (like(shape, F32),), where, own, got, scalars=1)[0]
 
 
 def body(sheet, w_query, w_key, w_value, cotangent, lengths):
@@ -604,10 +599,10 @@
     for w in zip(fq, fk, fv):
         far_qk.append(far_query_key(0, row_dev, where, held, w[0], w[1], [probs]))
         far_natural.append(turn(where, *w, n_heads, [probs]))
-    near = near_input(where, grads, weights, list(zip(far_dscore, far_qk, far_natural)))
+    near = near_input(where, grads, weights, list(zip(far_dscore, far_qk, far_natural)), chunk)
     if direct:
         keep, give = parts
-        own, give = add_apart(where, keep, flip(give, "rows", 1), [near])
+        own, give = add_apart(where, keep, flip(give, "rows", 1), near[-1:])
         lines = [list(range(first, n_rows, 2)) for first in range(2)]
         got = lax.all_to_all(give, "rows", 0, 0, axis_index_groups=lines)
         weight_grad = last_sum(where, own, got, local)
@@ -617,8 +612,8 @@
         weight_grad = weight_grad.reshape(width // n_rows, 3, local)
 
     chunks = []
-    for first in range(0, row_dev, chunk):
-        keep, give = far_input(first, chunk, where, near, list(zip(far_probs, far_cot, far_natural)))
+    for index, part in enumerate(near):
+        keep, give = far_input(index * chunk, where, part, list(zip(far_probs, far_cot, far_natural)))
         chunks.append((keep, flip(give, "heads", 1)))
     return (jnp.swapaxes(finish(chunks), 1, 2), weight_grad)
 

time: 105 us -> 104 us (level)
  local copies, waits for them, and re-layouts: 11.7 us -> 9.68 us
    unnamed x30 -> x42, local copies, waits for them, and re-layouts: 11.7 us -> 9.68 us
  transfers between devices with their start and end apart: 24 -> 24, of which waited for: 8 -> 9; matrix products, arithmetic and copies ran while one was open for 1% -> 1% of each run, Pallas kernels for 37% -> 38%
where the time goes in v12:
time: 104 us; the launch traced here: 103 us
  Pallas kernels  41.5 us (40%)
  starting transfers between devices  35.2 us (34%)
  waiting for transfers between devices  15.1 us (15%)
  local copies, waits for them, and re-layouts  9.68 us (9%)
    pallas_call x25, Pallas kernels, in_vmem(): pl.pallas_call(run, in_specs=[SMEM] * scalars + [HBM] * streamed + [VMEM]...  39 us
    ppermute x23, starting transfers between devices, flip(): return lax.ppermute(values, axis, [(s, s ^ bit) for s in range(n)])  31.1 us
    ppermute x23, waiting for transfers between devices, flip(): return lax.ppermute(values, axis, [(s, s ^ bit) for s in range(n)])  14.1 us
    unnamed x42, local copies, waits for them, and re-layouts  9.68 us
    all_to_all x1, starting transfers between devices, body(): got = lax.all_to_all(give, 'rows', 0, 0, axis_index_groups=lines)  4.17 us
    pallas_call x1, Pallas kernels, finish(): pl.pallas_call(finish_kernel, in_specs=[VMEM] * len(terms), out_specs=HBM...  2.49 us
  transfers between devices with their start and end apart: 24, of which 9 were waited for; matrix products, arithmetic and copies ran while one was open for 1% of the time, Pallas kernels for 38%

profile of v12, /device:TPU:0, one launch (start us, length us, event | category | flops | bytes accessed | tf_op | source)
XLA Modules:
  0.0 103.2 jit_solution(7729854900152716358)
XLA Ops:
  0.6 3.0 %collective-permute-start.7 = (bf16[16,192,256]{2,1,0:T(8,128)(2,1)}, bf16[16,192,256]{2,1,0:T(8,128)(2,1)S(1)}, u32[]{:S(2)}, u32[]{:S(2)}) collective-permute-start(bf16[16,192,256]{2,1,0:T(8,128)(2,1)} %bitcast.8), channel_id=1, source_target_pairs={{0,2},{1,3},{2,0},{3,1},{4,6},{5,7},{6,4},{7,5},{8,10},{9,11},{10,... | collective-permute-start | bytes 4718600 | tf_op jit(solution)/shard_map/ppermute | solution.py:27
  4.4 6.9 %query_key.1 = (bf16[16,6,64,256]{3,2,1,0:T(8,128)(2,1)S(1)}, bf16[16,256,768]{2,1,0:T(8,128)(2,1)S(1)}, f32[4,3,32,256]{3,2,1,0:T(8,128)S(1)}, bf16[4,3,32,256]{3,2,1,0:T(8,128)(2,1)S(1)}) custom-call(s32[18]{0:T(128)S(1)} %pad_add_fusion.refs_0_, bf16[16,256,768]{2,1,0:T(8,128)(2,1)} %refs_1_.1, bf16[192,768]{1,0:T(8,128)(2,1)} %bitcast.13, ...), custom_call_target="tpu_custom_call" | custom-call | flops 2818572288 | bytes 16711716 | tf_op jit(solution)/shard_map/query_key/pallas_call | solution.py:56
  11.3 1.6 %collective-permute-start = (bf16[4,3,32,256]{3,2,1,0:T(8,128)(2,1)S(1)}, bf16[4,3,32,256]{3,2,1,0:T(8,128)(2,1)S(1)}, u32[]{:S(2)}, u32[]{:S(2)}) collective-permute-start(bf16[4,3,32,256]{3,2,1,0:T(8,128)(2,1)S(1)} %get-tuple-element.38.refs_4_), channel_id=1, source_target_pairs={{0,8},{4,12},{8,0},{12,4},{16,24},{20,28},{24,16},{28,20},{1,9},{5... | collective-permute-start | bytes 589832 | tf_op jit(solution)/shard_map/ppermute | solution.py:27
  13.0 3.7 %value_dprob.1 = (f32[4,3,32,256]{3,2,1,0:T(8,128)S(1)}, bf16[4,3,32,256]{3,2,1,0:T(8,128)(2,1)S(1)}, bf16[192,384]{1,0:T(8,128)(2,1)S(1)}) custom-call(s32[18]{0:T(128)S(1)} %pad_add_fusion.refs_0_, bf16[16,256,768]{2,1,0:T(8,128)(2,1)S(1)} %get-tuple-element.43.refs_1_, bf16[192,768]{1,0:T(8,128)(2,1)S(1)} %bitcast.11, bf16[16,192,256]{2,1,0:T(8,128)(2,1)S(1)} %bitcast.9, ...), custom_call_target="tpu_custom_call" | custom-call | flops 3221225472 | bytes 8699940 | tf_op jit(solution)/shard_map/value_dprob/pallas_call | solution.py:56
  18.3 2.7 %collective-permute-start.1 = (bf16[2,3,32,256]{3,2,1,0:T(8,128)(2,1)S(1)}, bf16[2,3,32,256]{3,2,1,0:T(8,128)(2,1)S(1)}, u32[]{:S(2)}, u32[]{:S(2)}) collective-permute-start(bf16[2,3,32,256]{3,2,1,0:T(8,128)(2,1)S(1)} %get-tuple-element.40), channel_id=1, source_target_pairs={{0,16},{4,20},{8,24},{12,28},{16,0},{20,4},{24,8},{28,12},{1,17},{... | collective-permute-start | bytes 294920 | tf_op jit(solution)/shard_map/ppermute | solution.py:27
  21.0 1.9 %collective-permute-done.3.refs_1_ = bf16[4,3,32,256]{3,2,1,0:T(8,128)(2,1)S(1)} collective-permute-done((bf16[4,3,32,256]{3,2,1,0:T(8,128)(2,1)S(1)}, bf16[4,3,32,256]{3,2,1,0:T(8,128)(2,1)S(1)}, u32[]{:S(2)}, u32[]{:S(2)}) %collective-permute-start.3) | collective-permute-done | bytes 196640 | tf_op jit(solution)/shard_map/ppermute | solution.py:27
  23.4 1.8 %collective-permute-done.1.refs_1_ = bf16[2,3,32,256]{3,2,1,0:T(8,128)(2,1)S(1)} collective-permute-done((bf16[2,3,32,256]{3,2,1,0:T(8,128)(2,1)S(1)}, bf16[2,3,32,256]{3,2,1,0:T(8,128)(2,1)S(1)}, u32[]{:S(2)}, u32[]{:S(2)}) %collective-permute-start.1) | collective-permute-done | bytes 98336 | tf_op jit(solution)/shard_map/ppermute | solution.py:27
  25.3 2.3 %collective-permute-done.4.refs_1_ = bf16[2,3,32,256]{3,2,1,0:T(8,128)(2,1)S(1)} collective-permute-done((bf16[2,3,32,256]{3,2,1,0:T(8,128)(2,1)S(1)}, bf16[2,3,32,256]{3,2,1,0:T(8,128)(2,1)S(1)}, u32[]{:S(2)}, u32[]{:S(2)}) %collective-permute-start.4) | collective-permute-done | bytes 98336 | tf_op jit(solution)/shard_map/ppermute | solution.py:27
  27.6 2.9 %collective-permute-start.5 = (bf16[1,3,32,256]{3,2,1,0:T(8,128)(2,1)S(1)}, bf16[1,3,32,256]{3,2,1,0:T(8,128)(2,1)S(1)}, u32[]{:S(2)}, u32[]{:S(2)}) collective-permute-start(bf16[1,3,32,256]{3,2,1,0:T(8,128)(2,1)S(1)} %get-tuple-element.49), channel_id=1, source_target_pairs={{0,16},{4,20},{8,24},{12,28},{16,0},{20,4},{24,8},{28,12},{1,17},{... | collective-permute-start | bytes 147464 | tf_op jit(solution)/shard_map/ppermute | solution.py:27
  33.4 2.5 %collective-permute-start.6 = (bf16[1,3,32,256]{3,2,1,0:T(8,128)(2,1)S(1)}, bf16[1,3,32,256]{3,2,1,0:T(8,128)(2,1)S(1)}, u32[]{:S(2)}, u32[]{:S(2)}) collective-permute-start(bf16[1,3,32,256]{3,2,1,0:T(8,128)(2,1)S(1)} %get-tuple-element.50.refs_0_), channel_id=1, source_target_pairs={{0,16},{4,20},{8,24},{12,28},{16,0},{20,4},{24,8},{28,12},{1,17},{... | collective-permute-start | bytes 147464 | tf_op jit(solution)/shard_map/ppermute | solution.py:27
  39.4 1.9 %collective-permute-start.8 = (bf16[2,3,32,256]{3,2,1,0:T(8,128)(2,1)S(1)}, bf16[2,3,32,256]{3,2,1,0:T(8,128)(2,1)S(1)}, u32[]{:S(2)}, u32[]{:S(2)}) collective-permute-start(bf16[2,3,32,256]{3,2,1,0:T(8,128)(2,1)S(1)} %join.4.refs_0_), channel_id=1, source_target_pairs={{0,8},{4,12},{8,0},{12,4},{16,24},{20,28},{24,16},{28,20},{1,9},{5... | collective-permute-start | bytes 294920 | tf_op jit(solution)/shard_map/ppermute | solution.py:27
  41.3 2.7 %collective-permute-start.11 = (bf16[2,3,32,256]{3,2,1,0:T(8,128)(2,1)S(1)}, bf16[2,3,32,256]{3,2,1,0:T(8,128)(2,1)S(1)}, u32[]{:S(2)}, u32[]{:S(2)}) collective-permute-start(bf16[2,3,32,256]{3,2,1,0:T(8,128)(2,1)S(1)} %join.6.refs_0_), channel_id=1, source_target_pairs={{0,16},{4,20},{8,24},{12,28},{16,0},{20,4},{24,8},{28,12},{1,17},{... | collective-permute-start | bytes 294920 | tf_op jit(solution)/shard_map/ppermute | solution.py:27
  45.9 2.1 %collective-permute-done.11.refs_1_ = bf16[2,3,32,256]{3,2,1,0:T(8,128)(2,1)S(1)} collective-permute-done((bf16[2,3,32,256]{3,2,1,0:T(8,128)(2,1)S(1)}, bf16[2,3,32,256]{3,2,1,0:T(8,128)(2,1)S(1)}, u32[]{:S(2)}, u32[]{:S(2)}) %collective-permute-start.11) | collective-permute-done | bytes 98336 | tf_op jit(solution)/shard_map/ppermute | solution.py:27
  49.7 2.8 %collective-permute-done.14.refs_6_.refs_3_.refs_2_ = bf16[192,768]{1,0:T(8,128)(2,1)S(1)} collective-permute-done((bf16[192,768]{1,0:T(8,128)(2,1)S(1)}, bf16[192,768]{1,0:T(8,128)(2,1)S(1)}, u32[]{:S(2)}, u32[]{:S(2)}) %collective-permute-start.14) | collective-permute-done | bytes 294944 | tf_op jit(solution)/shard_map/ppermute | solution.py:27
  56.0 1.9 %own_gradients.1.refs_2_.refs_1_ = bf16[16,9,64,256]{3,2,1,0:T(8,128)(2,1)S(1)} custom-call(s32[18]{0:T(128)S(1)} %pad_add_fusion.refs_0_, bf16[8,3,32,256]{3,2,1,0:T(8,128)(2,1)S(1)} %get-tuple-element.52.refs_1_.refs_0_, bf16[8,3,32,256]{3,2,1,0:T(8,128)(2,1)S(1)} %get-tuple-element.53.refs_2_, bf16[16,6,64,256]{3,2,1,0:T(8,128)(2,1)S(1)} %get-tuple-element.54.refs_3_, ...), custom_call_target="tpu_custom_call" | custom-call | flops 1207959552 | bytes 10223652 | tf_op jit(solution)/shard_map/own_gradients/pallas_call | solution.py:56
  57.9 4.7 %weight_part.1 = (f32[4,96,576]{2,1,0:T(8,128)S(1)}, bf16[4,96,576]{2,1,0:T(8,128)(2,1)S(1)}) custom-call(s32[18]{0:T(128)S(1)} %pad_add_fusion.refs_0_, bf16[16,256,768]{2,1,0:T(8,128)(2,1)S(1)} %get-tuple-element.43.refs_1_, bf16[16,9,64,256]{3,2,1,0:T(8,128)(2,1)S(1)} %own_gradients.1.refs_2_.refs_1_, bf16[192,384]{1,0:T(8,128)(2,1)S(1)} %collective-permute-done.16.refs_3_), custom_call_target="tpu_custom_call" | custom-call | flops 3623878656 | bytes 11894820 | tf_op jit(solution)/shard_map/weight_part/pallas_call | solution.py:56
  65.0 3.2 %far_query_key.1.refs_4_ = bf16[16,6,64,256]{3,2,1,0:T(8,128)(2,1)S(1)} custom-call(s32[18]{0:T(128)S(1)} %pad_add_fusion.refs_0_, bf16[16,256,768]{2,1,0:T(8,128)(2,1)S(1)} %get-tuple-element.43.refs_1_, bf16[192,768]{1,0:T(8,128)(2,1)S(1)} %collective-permute-done.13.refs_5_.refs_2_.refs_1_, ...), custom_call_target="tpu_custom_call" | custom-call | bytes 10027044 | tf_op jit(solution)/shard_map/far_query_key/pallas_call | solution.py:56
  69.2 5.9 %near_input.1 = (bf16[2,4,192,256]{3,2,1,0:T(8,128)(2,1)S(1)}, bf16[2,4,192,256]{3,2,1,0:T(8,128)(2,1)S(1)}, bf16[2,4,192,256]{3,2,1,0:T(8,128)(2,1)S(1)}, bf16[2,4,192,256]{3,2,1,0:T(8,128)(2,1)S(1)}) custom-call(s32[18]{0:T(128)S(1)} %pad_add_fusion.refs_0_, bf16[16,9,64,256]{3,2,1,0:T(8,128)(2,1)S(1)} %own_gradients.1.refs_2_.refs_1_, ...), custom_call_target="tpu_custom_call" | custom-call | flops 3623878656 | bytes 12288036 | tf_op jit(solution)/shard_map/near_input/pallas_call | solution.py:56
  79.5 4.2 %all-to-all-start = ((bf16[4,96,576]{2,1,0:T(8,128)(2,1)}), bf16[4,96,576]{2,1,0:T(8,128)(2,1)S(1)}, u32[]{:S(2)}, u32[]{:S(2)}) async-start(bf16[4,96,576]{2,1,0:T(8,128)(2,1)} %copy-done.9), calls=%async_computation | async-start | bytes 983040 | tf_op jit(solution)/shard_map/all_to_all | solution.py:607
  84.9 1.9 %far_input.4 = (bf16[4,192,256]{2,1,0:T(8,128)(2,1)S(1)}, bf16[4,192,256]{2,1,0:T(8,128)(2,1)}) custom-call(s32[18]{0:T(128)S(1)} %pad_add_fusion.refs_0_, bf16[2,4,192,256]{3,2,1,0:T(8,128)(2,1)S(1)} %copy-done.8, bf16[8,3,32,256]{3,2,1,0:T(8,128)(2,1)S(1)} %collective-permute-done.17.refs_2_, ...), custom_call_target="tpu_custom_call" | custom-call | bytes 3981348 | tf_op jit(solution)/shard_map/far_input/pallas_call | solution.py:56
  86.8 1.9 %far_input.7 = (bf16[4,192,256]{2,1,0:T(8,128)(2,1)S(1)}, bf16[4,192,256]{2,1,0:T(8,128)(2,1)}) custom-call(s32[18]{0:T(128)S(1)} %pad_add_fusion.refs_0_, bf16[2,4,192,256]{3,2,1,0:T(8,128)(2,1)S(1)} %copy-done.1, bf16[8,3,32,256]{3,2,1,0:T(8,128)(2,1)S(1)} %collective-permute-done.17.refs_2_, ...), custom_call_target="tpu_custom_call" | custom-call | bytes 3981348 | tf_op jit(solution)/shard_map/far_input/pallas_call | solution.py:56
  89.2 1.9 %far_input.5 = (bf16[4,192,256]{2,1,0:T(8,128)(2,1)S(1)}, bf16[4,192,256]{2,1,0:T(8,128)(2,1)}) custom-call(s32[18]{0:T(128)S(1)} %pad_add_fusion.refs_0_, bf16[2,4,192,256]{3,2,1,0:T(8,128)(2,1)S(1)} %copy-done.6, bf16[8,3,32,256]{3,2,1,0:T(8,128)(2,1)S(1)} %collective-permute-done.17.refs_2_, ...), custom_call_target="tpu_custom_call" | custom-call | bytes 3981348 | tf_op jit(solution)/shard_map/far_input/pallas_call | solution.py:56
  91.0 1.9 %far_input.6 = (bf16[4,192,256]{2,1,0:T(8,128)(2,1)S(1)}, bf16[4,192,256]{2,1,0:T(8,128)(2,1)}) custom-call(s32[18]{0:T(128)S(1)} %pad_add_fusion.refs_0_, bf16[2,4,192,256]{3,2,1,0:T(8,128)(2,1)S(1)} %copy-done.4, bf16[8,3,32,256]{3,2,1,0:T(8,128)(2,1)S(1)} %collective-permute-done.17.refs_2_, ...), custom_call_target="tpu_custom_call" | custom-call | bytes 3981348 | tf_op jit(solution)/shard_map/far_input/pallas_call | solution.py:56
  100.5 2.5 %finish.1 = bf16[16,192,256]{2,1,0:T(8,128)(2,1)} custom-call(bf16[4,192,256]{2,1,0:T(8,128)(2,1)S(1)} %get-tuple-element.58.refs_0_, bf16[4,192,256]{2,1,0:T(8,128)(2,1)} %collective-permute-done.18.refs_1_, bf16[4,192,256]{2,1,0:T(8,128)(2,1)S(1)} %copy-done.13, bf16[4,192,256]{2,1,0:T(8,128)(2,1)} %collective-permute-done.19.refs_3_, ...), custom_call_target="tpu_custom_call" | custom-call | flops 786432 | bytes 4718592 | tf_op jit(solution)/shard_map/finish/pallas_call | solution.py:467
  (93 shorter events, 33.6 us)
Async XLA Ops:
  0.6 38.7 %collective-permute-start.7 = (bf16[16,192,256]{2,1,0:T(8,128)(2,1)}, bf16[16,192,256]{2,1,0:T(8,128)(2,1)S(1)}, u32[]{:S(2)}, u32[]{:S(2)}) collective-permute-start(bf16[16,192,256]{2,1,0:T(8,128)(2,1)} %bitcast.8), channel_id=1, source_target_pairs={{0,2},{1,3},{2,0},{3,1},{4,6},{5,7},{6,4},{7,5},{8,10},{9,11},{10,... | collective-permute-start | bytes 4718600 | tf_op jit(solution)/shard_map/ppermute | solution.py:27
  11.3 6.9 %collective-permute-start = (bf16[4,3,32,256]{3,2,1,0:T(8,128)(2,1)S(1)}, bf16[4,3,32,256]{3,2,1,0:T(8,128)(2,1)S(1)}, u32[]{:S(2)}, u32[]{:S(2)}) collective-permute-start(bf16[4,3,32,256]{3,2,1,0:T(8,128)(2,1)S(1)} %get-tuple-element.38.refs_4_), channel_id=1, source_target_pairs={{0,8},{4,12},{8,0},{12,4},{16,24},{20,28},{24,16},{28,20},{1,9},{5... | collective-permute-start | bytes 589832 | tf_op jit(solution)/shard_map/ppermute | solution.py:27
  16.7 6.1 %collective-permute-start.3 = (bf16[4,3,32,256]{3,2,1,0:T(8,128)(2,1)S(1)}, bf16[4,3,32,256]{3,2,1,0:T(8,128)(2,1)S(1)}, u32[]{:S(2)}, u32[]{:S(2)}) collective-permute-start(bf16[4,3,32,256]{3,2,1,0:T(8,128)(2,1)S(1)} %get-tuple-element.45.refs_4_), channel_id=1, source_target_pairs={{0,4},{4,0},{8,12},{12,8},{16,20},{20,16},{24,28},{28,24},{1,5},{5... | collective-permute-start | bytes 589832 | tf_op jit(solution)/shard_map/ppermute | solution.py:27
  18.3 6.9 %collective-permute-start.1 = (bf16[2,3,32,256]{3,2,1,0:T(8,128)(2,1)S(1)}, bf16[2,3,32,256]{3,2,1,0:T(8,128)(2,1)S(1)}, u32[]{:S(2)}, u32[]{:S(2)}) collective-permute-start(bf16[2,3,32,256]{3,2,1,0:T(8,128)(2,1)S(1)} %get-tuple-element.40), channel_id=1, source_target_pairs={{0,16},{4,20},{8,24},{12,28},{16,0},{20,4},{24,8},{28,12},{1,17},{... | collective-permute-start | bytes 294920 | tf_op jit(solution)/shard_map/ppermute | solution.py:27
  22.9 4.7 %collective-permute-start.4 = (bf16[2,3,32,256]{3,2,1,0:T(8,128)(2,1)S(1)}, bf16[2,3,32,256]{3,2,1,0:T(8,128)(2,1)S(1)}, u32[]{:S(2)}, u32[]{:S(2)}) collective-permute-start(bf16[2,3,32,256]{3,2,1,0:T(8,128)(2,1)S(1)} %get-tuple-element.47), channel_id=1, source_target_pairs={{0,8},{4,12},{8,0},{12,4},{16,24},{20,28},{24,16},{28,20},{1,9},{5... | collective-permute-start | bytes 294920 | tf_op jit(solution)/shard_map/ppermute | solution.py:27
  25.2 6.3 %collective-permute-start.2 = (bf16[1,3,32,256]{3,2,1,0:T(8,128)(2,1)S(1)}, bf16[1,3,32,256]{3,2,1,0:T(8,128)(2,1)S(1)}, u32[]{:S(2)}, u32[]{:S(2)}) collective-permute-start(bf16[1,3,32,256]{3,2,1,0:T(8,128)(2,1)S(1)} %get-tuple-element.42), channel_id=1, source_target_pairs={{0,4},{4,0},{8,12},{12,8},{16,20},{20,16},{24,28},{28,24},{1,5},{5... | collective-permute-start | bytes 147464 | tf_op jit(solution)/shard_map/ppermute | solution.py:27
  27.6 5.5 %collective-permute-start.5 = (bf16[1,3,32,256]{3,2,1,0:T(8,128)(2,1)S(1)}, bf16[1,3,32,256]{3,2,1,0:T(8,128)(2,1)S(1)}, u32[]{:S(2)}, u32[]{:S(2)}) collective-permute-start(bf16[1,3,32,256]{3,2,1,0:T(8,128)(2,1)S(1)} %get-tuple-element.49), channel_id=1, source_target_pairs={{0,16},{4,20},{8,24},{12,28},{16,0},{20,4},{24,8},{28,12},{1,17},{... | collective-permute-start | bytes 147464 | tf_op jit(solution)/shard_map/ppermute | solution.py:27
  33.4 6.0 %collective-permute-start.6 = (bf16[1,3,32,256]{3,2,1,0:T(8,128)(2,1)S(1)}, bf16[1,3,32,256]{3,2,1,0:T(8,128)(2,1)S(1)}, u32[]{:S(2)}, u32[]{:S(2)}) collective-permute-start(bf16[1,3,32,256]{3,2,1,0:T(8,128)(2,1)S(1)} %get-tuple-element.50.refs_0_), channel_id=1, source_target_pairs={{0,16},{4,20},{8,24},{12,28},{16,0},{20,4},{24,8},{28,12},{1,17},{... | collective-permute-start | bytes 147464 | tf_op jit(solution)/shard_map/ppermute | solution.py:27
  35.8 5.5 %collective-permute-start.10 = (bf16[1,3,32,256]{3,2,1,0:T(8,128)(2,1)S(1)}, bf16[1,3,32,256]{3,2,1,0:T(8,128)(2,1)S(1)}, u32[]{:S(2)}, u32[]{:S(2)}) collective-permute-start(bf16[1,3,32,256]{3,2,1,0:T(8,128)(2,1)S(1)} %get-tuple-element.51.refs_0_), channel_id=1, source_target_pairs={{0,4},{4,0},{8,12},{12,8},{16,20},{20,16},{24,28},{28,24},{1,5},{5... | collective-permute-start | bytes 147464 | tf_op jit(solution)/shard_map/ppermute | solution.py:27
  37.3 12.4 %collective-permute-start.13 = (bf16[192,768]{1,0:T(8,128)(2,1)S(1)}, bf16[192,768]{1,0:T(8,128)(2,1)S(1)}, u32[]{:S(2)}, u32[]{:S(2)}) collective-permute-start(bf16[192,768]{1,0:T(8,128)(2,1)S(1)} %bitcast.15), channel_id=1, source_target_pairs={{0,2},{1,3},{2,0},{3,1},{4,6},{5,7},{6,4},{7,5},{8,10},{9,11},{10,... | collective-permute-start | bytes 884744 | tf_op jit(solution)/shard_map/ppermute | solution.py:27
  37.8 14.6 %collective-permute-start.14 = (bf16[192,768]{1,0:T(8,128)(2,1)S(1)}, bf16[192,768]{1,0:T(8,128)(2,1)S(1)}, u32[]{:S(2)}, u32[]{:S(2)}) collective-permute-start(bf16[192,768]{1,0:T(8,128)(2,1)S(1)} %bitcast.18), channel_id=1, source_target_pairs={{0,2},{1,3},{2,0},{3,1},{4,6},{5,7},{6,4},{7,5},{8,10},{9,11},{10,... | collective-permute-start | bytes 884744 | tf_op jit(solution)/shard_map/ppermute | solution.py:27
  39.4 5.0 %collective-permute-start.8 = (bf16[2,3,32,256]{3,2,1,0:T(8,128)(2,1)S(1)}, bf16[2,3,32,256]{3,2,1,0:T(8,128)(2,1)S(1)}, u32[]{:S(2)}, u32[]{:S(2)}) collective-permute-start(bf16[2,3,32,256]{3,2,1,0:T(8,128)(2,1)S(1)} %join.4.refs_0_), channel_id=1, source_target_pairs={{0,8},{4,12},{8,0},{12,4},{16,24},{20,28},{24,16},{28,20},{1,9},{5... | collective-permute-start | bytes 294920 | tf_op jit(solution)/shard_map/ppermute | solution.py:27
  41.3 6.7 %collective-permute-start.11 = (bf16[2,3,32,256]{3,2,1,0:T(8,128)(2,1)S(1)}, bf16[2,3,32,256]{3,2,1,0:T(8,128)(2,1)S(1)}, u32[]{:S(2)}, u32[]{:S(2)}) collective-permute-start(bf16[2,3,32,256]{3,2,1,0:T(8,128)(2,1)S(1)} %join.6.refs_0_), channel_id=1, source_target_pairs={{0,16},{4,20},{8,24},{12,28},{16,0},{20,4},{24,8},{28,12},{1,17},{... | collective-permute-start | bytes 294920 | tf_op jit(solution)/shard_map/ppermute | solution.py:27
  44.4 8.1 %collective-permute-start.9 = (bf16[4,3,32,256]{3,2,1,0:T(8,128)(2,1)S(1)}, bf16[4,3,32,256]{3,2,1,0:T(8,128)(2,1)S(1)}, u32[]{:S(2)}, u32[]{:S(2)}) collective-permute-start(bf16[4,3,32,256]{3,2,1,0:T(8,128)(2,1)S(1)} %join.5.refs_1_), channel_id=1, source_target_pairs={{0,4},{4,0},{8,12},{12,8},{16,20},{20,16},{24,28},{28,24},{1,5},{5... | collective-permute-start | bytes 589832 | tf_op jit(solution)/shard_map/ppermute | solution.py:27
  48.1 5.7 %collective-permute-start.12 = (bf16[4,3,32,256]{3,2,1,0:T(8,128)(2,1)S(1)}, bf16[4,3,32,256]{3,2,1,0:T(8,128)(2,1)S(1)}, u32[]{:S(2)}, u32[]{:S(2)}) collective-permute-start(bf16[4,3,32,256]{3,2,1,0:T(8,128)(2,1)S(1)} %join.7.refs_3_), channel_id=1, source_target_pairs={{0,8},{4,12},{8,0},{12,4},{16,24},{20,28},{24,16},{28,20},{1,9},{5... | collective-permute-start | bytes 589832 | tf_op jit(solution)/shard_map/ppermute | solution.py:27
  48.2 9.8 %collective-permute-start.16 = (bf16[192,384]{1,0:T(8,128)(2,1)S(1)}, bf16[192,384]{1,0:T(8,128)(2,1)S(1)}, u32[]{:S(2)}, u32[]{:S(2)}) collective-permute-start(bf16[192,384]{1,0:T(8,128)(2,1)S(1)} %get-tuple-element.55), channel_id=1, source_target_pairs={{0,2},{1,3},{2,0},{3,1},{4,6},{5,7},{6,4},{7,5},{8,10},{9,11},{10,... | collective-permute-start | bytes 442376 | tf_op jit(solution)/shard_map/ppermute | solution.py:27
  54.4 9.8 %collective-permute-start.15 = (bf16[8,3,32,256]{3,2,1,0:T(8,128)(2,1)S(1)}, bf16[8,3,32,256]{3,2,1,0:T(8,128)(2,1)S(1)}, u32[]{:S(2)}, u32[]{:S(2)}) collective-permute-start(bf16[8,3,32,256]{3,2,1,0:T(8,128)(2,1)S(1)} %get-tuple-element.53.refs_2_), channel_id=1, source_target_pairs={{0,2},{1,3},{2,0},{3,1},{4,6},{5,7},{6,4},{7,5},{8,10},{9,11},{10,... | collective-permute-start | bytes 1179656 | tf_op jit(solution)/shard_map/ppermute | solution.py:27
  62.7 13.3 %collective-permute-start.22 = (bf16[4,96,576]{2,1,0:T(8,128)(2,1)S(1)}, bf16[4,96,576]{2,1,0:T(8,128)(2,1)S(1)}, u32[]{:S(2)}, u32[]{:S(2)}) collective-permute-start(bf16[4,96,576]{2,1,0:T(8,128)(2,1)S(1)} %get-tuple-element.56.refs_1_), channel_id=1, source_target_pairs={{0,4},{4,0},{8,12},{12,8},{16,20},{20,16},{24,28},{28,24},{1,5},{5... | collective-permute-start | bytes 1327112 | tf_op jit(solution)/shard_map/ppermute | solution.py:27
  64.3 19.4 %collective-permute-start.17 = (bf16[8,3,32,256]{3,2,1,0:T(8,128)(2,1)S(1)}, bf16[8,3,32,256]{3,2,1,0:T(8,128)(2,1)S(1)}, u32[]{:S(2)}, u32[]{:S(2)}) collective-permute-start(bf16[8,3,32,256]{3,2,1,0:T(8,128)(2,1)S(1)} %hold.1.refs_4_), channel_id=1, source_target_pairs={{0,2},{1,3},{2,0},{3,1},{4,6},{5,7},{6,4},{7,5},{8,10},{9,11},{10,... | collective-permute-start | bytes 1179656 | tf_op jit(solution)/shard_map/ppermute | solution.py:27
  79.5 15.7 %all-to-all-start = ((bf16[4,96,576]{2,1,0:T(8,128)(2,1)}), bf16[4,96,576]{2,1,0:T(8,128)(2,1)S(1)}, u32[]{:S(2)}, u32[]{:S(2)}) async-start(bf16[4,96,576]{2,1,0:T(8,128)(2,1)} %copy-done.9), calls=%async_computation | async-start | bytes 983040 | tf_op jit(solution)/shard_map/all_to_all | solution.py:607
  86.8 10.7 %collective-permute-start.18 = (bf16[4,192,256]{2,1,0:T(8,128)(2,1)}, bf16[4,192,256]{2,1,0:T(8,128)(2,1)}, u32[]{:S(2)}, u32[]{:S(2)}) collective-permute-start(bf16[4,192,256]{2,1,0:T(8,128)(2,1)} %get-tuple-element.59), channel_id=1, source_target_pairs={{0,1},{1,0},{2,3},{3,2},{4,5},{5,4},{6,7},{7,6},{8,9},{9,8},{10,11... | collective-permute-start | bytes 1179656 | tf_op jit(solution)/shard_map/ppermute | solution.py:27
  88.7 8.9 %collective-permute-start.21 = (bf16[4,192,256]{2,1,0:T(8,128)(2,1)}, bf16[4,192,256]{2,1,0:T(8,128)(2,1)}, u32[]{:S(2)}, u32[]{:S(2)}) collective-permute-start(bf16[4,192,256]{2,1,0:T(8,128)(2,1)} %get-tuple-element.68), channel_id=1, source_target_pairs={{0,1},{1,0},{2,3},{3,2},{4,5},{5,4},{6,7},{7,6},{8,9},{9,8},{10,11... | collective-permute-start | bytes 1179656 | tf_op jit(solution)/shard_map/ppermute | solution.py:27
  91.0 6.5 %collective-permute-start.19 = (bf16[4,192,256]{2,1,0:T(8,128)(2,1)}, bf16[4,192,256]{2,1,0:T(8,128)(2,1)}, u32[]{:S(2)}, u32[]{:S(2)}) collective-permute-start(bf16[4,192,256]{2,1,0:T(8,128)(2,1)} %get-tuple-element.62), channel_id=1, source_target_pairs={{0,1},{1,0},{2,3},{3,2},{4,5},{5,4},{6,7},{7,6},{8,9},{9,8},{10,11... | collective-permute-start | bytes 1179656 | tf_op jit(solution)/shard_map/ppermute | solution.py:27
  93.7 3.8 %collective-permute-start.20 = (bf16[4,192,256]{2,1,0:T(8,128)(2,1)}, bf16[4,192,256]{2,1,0:T(8,128)(2,1)S(1)}, u32[]{:S(2)}, u32[]{:S(2)}) collective-permute-start(bf16[4,192,256]{2,1,0:T(8,128)(2,1)} %get-tuple-element.65), channel_id=1, source_target_pairs={{0,1},{1,0},{2,3},{3,2},{4,5},{5,4},{6,7},{7,6},{8,9},{9,8},{10,11... | collective-permute-start | bytes 1179656 | tf_op jit(solution)/shard_map/ppermute | solution.py:27
  (21 other events, 82.0 us)

commit v13 on v12

--- a/solution.py
+++ b/solution.py
@@ -329,13 +329,18 @@
 
 
 def query_key_gradients(where, dscore, qk, grads):
-    rows, two, _, cols = qk.shape
-    flat = (rows * HEAD_DIM, cols)
-    heads = two // 2
-    for h in range(heads):
-        ds = dscore[:, h].reshape(cols, cols)
-        grads[:, h] = masked(where, mm(qk[:, heads + h].reshape(flat), ds, NT), 0, rows)
-        grads[:, heads + h] = masked(where, mm(qk[:, h].reshape(flat), ds, NN), 0, rows)
+    first = 0
+    heads = qk[0].shape[1] // 2
+    cols = qk[0].shape[-1]
+    for part in qk:
+        count = part.shape[0]
+        flat = (count * HEAD_DIM, cols)
+        some = pl.ds(first, count)
+        for h in range(heads):
+            ds = dscore[:, h].reshape(cols, cols)
+            grads[some, h] = masked(where, mm(part[:, heads + h].reshape(flat), ds, NT), first, count)
+            grads[some, heads + h] = masked(where, mm(part[:, h].reshape(flat), ds, NN), first, count)
+        first += count
 
 
 def value_gradient(where, probs, cot, h, first, count):
@@ -346,7 +351,7 @@
 
 def own_gradients_kernel(where, probs, dscore, qk, cot, grads):
     heads = qk.shape[1] // 2
-    query_key_gradients(where, dscore, qk, grads)
+    query_key_gradients(where, dscore, [qk], grads)
     for h in range(heads):
         grads[:, 2 * heads + h] = value_gradient(where, probs, cot, h, 0, cot.shape[0])
 
@@ -368,19 +373,21 @@
     )[0]
 
 
-def near_input_kernel(fars, where, own, weights, *refs):
-    far, outs, grads = refs[: 3 * fars], refs[3 * fars : -1], refs[-1]
+def near_input_kernel(fars, pieces, where, own, weights, *refs):
+    each = 2 + pieces
+    far, outs, grads = refs[: each * fars], refs[each * fars : -1], refs[-1]
     near, share, columns = weights.shape
     rows, _, _, cols = own.shape
     count = rows // len(outs)
     some = grads.shape[2] * HEAD_DIM
-    for i in range(fars):
-        query_key_gradients(where, *far[3 * i : 3 * i + 2], grads.at[i])
+    far = [far[i * each : (i + 1) * each] for i in range(fars)]
+    for i, (dscore, _, *qk) in enumerate(far):
+        query_key_gradients(where, dscore, qk, grads.at[i])
     for r in range(rows):
         left = weights[...].reshape(near * share, columns)
         total = mm(left, own[r].reshape(columns, cols), NN)
-        for i in range(fars):
-            left = far[3 * i + 2][:, :, :some].reshape(near * share, some)
+        for i, (_, natural, *_) in enumerate(far):
+            left = natural[:, :, :some].reshape(near * share, some)
             total = total + mm(left, grads[i, r].reshape(some, cols), NN)
         outs[r // count][:, r % count] = total.astype(BF16).reshape(near, share, cols)
 
@@ -388,16 +395,18 @@
 def near_input(where, grads, weights, far, chunk):
     rows, cols = grads.shape[0], grads.shape[-1]
     near, share, columns = weights.shape
-    return in_vmem(
-        functools.partial(near_input_kernel, len(far)),
+    pieces = len(far[0][1])
+    heads = far[0][1][0].shape[1]
+    return in_vmem(
+        functools.partial(near_input_kernel, len(far), pieces),
         "near_input",
         [like((near, chunk, share, cols))] * (rows // chunk),
         where,
         grads,
         weights,
-        *[a for one in far for a in one],
-        scalars=1,
-        scratch=(pltpu.VMEM((len(far), rows) + far[0][1].shape[1:], BF16),),
+        *[a for dscore, qk, natural in far for a in (dscore, natural, *qk)],
+        scalars=1,
+        scratch=(pltpu.VMEM((len(far), rows, heads, HEAD_DIM, cols), BF16),),
         limit=14,
         flops=2 * rows * cols * near * share * columns * (1 + len(far)),
     )
@@ -422,7 +431,7 @@
         give[r] = total[1].astype(give.dtype)
 
 
-def far_input(first, where, near, far):
+def far_input(first, where, near, far, after):
     _, count, share, cols = near.shape
     out = like((count, share, cols))
     return in_vmem(
@@ -433,6 +442,7 @@
         near,
         *[a for one in far for a in one],
         scalars=1,
+        after=after,
         limit=14,
     )
 
@@ -524,33 +534,16 @@
     )
 
 
-def add_apart_kernel(where, keep, got, own, give):
-    mine = lax.shift_right_logical(where[0], 1)
-    for t in range(keep.shape[0]):
-        total = keep[t] + got[t].astype(F32)
-        if t == 0:
-            own[...] = total
-        give[mine ^ t] = total.astype(give.dtype)
-
-
-def add_apart(where, keep, got, after):
-    outs = (like(keep.shape[1:], F32), like(keep.shape))
-    return in_vmem(add_apart_kernel, "add_apart", outs, where, keep, got, scalars=1, after=after)
-
-
-def last_kernel(where, own, got, out):
-    mine = lax.shift_right_logical(where[0], 1)
-    total = own[...]
-    for t in range(1, got.shape[0]):
-        total = total + got[mine ^ t].astype(F32)
+def last_kernel(keep, got, out):
+    total = keep[0] + got[0].astype(F32)
     local = out.shape[-1]
     for index in range(out.shape[0]):
         out[index] = total[:, index * local : (index + 1) * local]
 
 
-def last_sum(where, own, got, local):
-    shape = (own.shape[1] // local, own.shape[0], local)
-    return in_vmem(last_kernel, "last_sum", (like(shape, F32),), where, own, got, scalars=1)[0]
+def last_sum(keep, got, local):
+    shape = (keep.shape[2] // local, keep.shape[1], local)
+    return in_vmem(last_kernel, "last_sum", (like(shape, F32),), keep, got)[0]
 
 
 def body(sheet, w_query, w_key, w_value, cotangent, lengths):
@@ -580,13 +573,18 @@
     dprob, halves = dprob[: -len(fars)], dprob[-len(fars) :]
     fv = [flip(half, "heads", f) for half, f in zip(halves, fars)]
     weights = turn(where, wq, wk, wv, n_heads, dprob[-1:])
+    piece = row_dev // 4
+    far_qk = [
+        [far_query_key(r, piece, where, held, w[0], w[1], ()) for r in range(0, row_dev, piece)]
+        for w in zip(fq, fk)
+    ]
     if direct:
         logits = halve(*logits, "rows", turn_about)
         dprob = halve(*dprob, "rows", up)
-        probs_own, dscore_own = softmax_back(logits, dprob, scale, [weights])
-        probs, probs_order = double(probs_own, "rows", up[::-1], [far_cot])
-        dscore, dscore_order = double(dscore_own, "rows", turn_about[::-1], [far_cot])
-        probs, dscore = assemble(where, probs, dscore, (probs_order, dscore_order), shards, fq + fk)
+        probs_own, dscore_own = softmax_back(logits, dprob, scale, [weights] + fq + fk)
+        probs, probs_order = double(probs_own, "rows", up[::-1])
+        dscore, dscore_order = double(dscore_own, "rows", turn_about[::-1])
+        probs, dscore = assemble(where, probs, dscore, (probs_order, dscore_order), shards, sum(far_qk, far_cot))
     else:
         logits, dprob = lax.psum((logits, dprob), "rows")
         probs, dscore = softmax_back(logits, dprob, scale)
@@ -595,25 +593,26 @@
     parts = weight_part(where, held, grads, (3 * local,), shards, fv)
     probs = hold(probs, [parts[-1]] + far_dscore)
     far_probs = [flip(probs, "heads", f) for f in fars]
-    far_qk, far_natural = [], []
-    for w in zip(fq, fk, fv):
-        far_qk.append(far_query_key(0, row_dev, where, held, w[0], w[1], [probs]))
-        far_natural.append(turn(where, *w, n_heads, [probs]))
+    far_natural = [turn(where, *w, n_heads, [probs]) for w in zip(fq, fk, fv)]
     near = near_input(where, grads, weights, list(zip(far_dscore, far_qk, far_natural)), chunk)
+    ready = near[-1:]
+    steps = []
     if direct:
         keep, give = parts
-        own, give = add_apart(where, keep, flip(give, "rows", 1), near[-1:])
-        lines = [list(range(first, n_rows, 2)) for first in range(2)]
-        got = lax.all_to_all(give, "rows", 0, 0, axis_index_groups=lines)
-        weight_grad = last_sum(where, own, got, local)
+        for bit in row_bits[:-1]:
+            give, keep = add_split(keep, flip(give, "rows", bit), ready)
+            ready = ()
+            steps.append([keep])
+        weight_grad = last_sum(keep, flip(give, "rows", row_bits[-1]), local)
         weight_grad = jnp.swapaxes(weight_grad, 0, 1)
     else:
         weight_grad = lax.psum_scatter(parts[0], "rows", scatter_dimension=0, tiled=True)
         weight_grad = weight_grad.reshape(width // n_rows, 3, local)
-
     chunks = []
     for index, part in enumerate(near):
-        keep, give = far_input(index * chunk, where, part, list(zip(far_probs, far_cot, far_natural)))
+        far = list(zip(far_probs, far_cot, far_natural))
+        after = steps[index // 2] if index // 2 < len(steps) else ()
+        keep, give = far_input(index * chunk, where, part, far, after)
         chunks.append((keep, flip(give, "heads", 1)))
     return (jnp.swapaxes(finish(chunks), 1, 2), weight_grad)
 

time: 104 us -> 114 us (1.096)
  waiting for transfers between devices: 15.1 us -> 36.4 us
  local copies, waits for them, and re-layouts: 9.68 us -> 0.02 us
  Pallas kernels: 41.5 us -> 38.4 us
  starting transfers between devices: 35.2 us -> 37 us
    ppermute x23 -> x25, waiting for transfers between devices: 14.1 us -> 36.4 us  [flip(): return lax.ppermute(values, axis, [(s, s ^ bit) for s in range(n)])]
    unnamed x42 -> x8, local copies, waits for them, and re-layouts: 9.68 us -> 0.02 us
    ppermute x23 -> x25, starting transfers between devices: 31.1 us -> 37 us  [flip(): return lax.ppermute(values, axis, [(s, s ^ bit) for s in range(n)])]
    all_to_all x1 -> x0, starting transfers between devices: 4.17 us -> none  [body(): got = lax.all_to_all(give, 'rows', 0, 0, axis_index_groups=lines)]
    pallas_call x25 -> x29, Pallas kernels: 39 us -> 37.1 us  [in_vmem(): pl.pallas_call(run, in_specs=[SMEM] * scalars + [HBM] * streamed + [VMEM]...]
    pallas_call x1, Pallas kernels: 2.49 us -> 1.27 us  [finish(): pl.pallas_call(finish_kernel, in_specs=[VMEM] * len(terms), out_specs=HBM...]
  transfers between devices with their start and end apart: 24 -> 25, of which waited for: 9 -> 12; matrix products, arithmetic and copies ran while one was open for 1% -> 1% of each run, Pallas kernels for 38% -> 32%
where the time goes in v13:
time: 114 us
  Pallas kernels  38.4 us (34%)
  starting transfers between devices  37 us (32%)
  waiting for transfers between devices  36.4 us (32%)
    pallas_call x29, Pallas kernels, in_vmem(): pl.pallas_call(run, in_specs=[SMEM] * scalars + [HBM] * streamed + [VMEM]...  37.1 us
    ppermute x25, starting transfers between devices, flip(): return lax.ppermute(values, axis, [(s, s ^ bit) for s in range(n)])  37 us
    ppermute x25, waiting for transfers between devices, flip(): return lax.ppermute(values, axis, [(s, s ^ bit) for s in range(n)])  36.4 us
  transfers between devices with their start and end apart: 25, of which 12 were waited for; matrix products, arithmetic and copies ran while one was open for 1% of the time, Pallas kernels for 32%

profile of v13, /device:TPU:0, one launch (start us, length us, event | category | flops | bytes accessed | tf_op | source)
XLA Modules:
  0.0 113.7 jit_solution(2596411928238251390)
XLA Ops:
  0.6 3.0 %collective-permute-start.14 = (bf16[16,192,256]{2,1,0:T(8,128)(2,1)}, bf16[16,192,256]{2,1,0:T(8,128)(2,1)S(1)}, u32[]{:S(2)}, u32[]{:S(2)}) collective-permute-start(bf16[16,192,256]{2,1,0:T(8,128)(2,1)} %bitcast.8), channel_id=1, source_target_pairs={{0,2},{1,3},{2,0},{3,1},{4,6},{5,7},{6,4},{7,5},{8,10},{9,11},{10,... | collective-permute-start | bytes 4718600 | tf_op jit(solution)/shard_map/ppermute | solution.py:27
  4.4 6.9 %query_key.1 = (bf16[16,6,64,256]{3,2,1,0:T(8,128)(2,1)S(1)}, bf16[16,256,768]{2,1,0:T(8,128)(2,1)S(1)}, f32[4,3,32,256]{3,2,1,0:T(8,128)S(1)}, bf16[4,3,32,256]{3,2,1,0:T(8,128)(2,1)S(1)}) custom-call(s32[18]{0:T(128)S(1)} %pad_add_fusion.refs_0_, bf16[16,256,768]{2,1,0:T(8,128)(2,1)} %refs_1_.1, bf16[192,768]{1,0:T(8,128)(2,1)} %bitcast.13, ...), custom_call_target="tpu_custom_call" | custom-call | flops 2818572288 | bytes 16711716 | tf_op jit(solution)/shard_map/query_key/pallas_call | solution.py:56
  11.4 3.7 %value_dprob.1 = (f32[4,3,32,256]{3,2,1,0:T(8,128)S(1)}, bf16[4,3,32,256]{3,2,1,0:T(8,128)(2,1)S(1)}, bf16[192,384]{1,0:T(8,128)(2,1)S(1)}) custom-call(s32[18]{0:T(128)S(1)} %pad_add_fusion.refs_0_, bf16[16,256,768]{2,1,0:T(8,128)(2,1)S(1)} %get-tuple-element.45.refs_1_, bf16[192,768]{1,0:T(8,128)(2,1)S(1)} %bitcast.11, bf16[16,192,256]{2,1,0:T(8,128)(2,1)S(1)} %bitcast.9, ...), custom_call_target="tpu_custom_call" | custom-call | flops 3221225472 | bytes 8699940 | tf_op jit(solution)/shard_map/value_dprob/pallas_call | solution.py:56
  16.7 1.6 %collective-permute-start = (bf16[4,3,32,256]{3,2,1,0:T(8,128)(2,1)S(1)}, bf16[4,3,32,256]{3,2,1,0:T(8,128)(2,1)S(1)}, u32[]{:S(2)}, u32[]{:S(2)}) collective-permute-start(bf16[4,3,32,256]{3,2,1,0:T(8,128)(2,1)S(1)} %get-tuple-element.40.refs_4_), channel_id=1, source_target_pairs={{0,8},{4,12},{8,0},{12,4},{16,24},{20,28},{24,16},{28,20},{1,9},{5... | collective-permute-start | bytes 589832 | tf_op jit(solution)/shard_map/ppermute | solution.py:27
  21.6 1.7 %collective-permute-start.4 = (bf16[2,3,32,256]{3,2,1,0:T(8,128)(2,1)S(1)}, bf16[2,3,32,256]{3,2,1,0:T(8,128)(2,1)S(1)}, u32[]{:S(2)}, u32[]{:S(2)}) collective-permute-start(bf16[2,3,32,256]{3,2,1,0:T(8,128)(2,1)S(1)} %get-tuple-element.49), channel_id=1, source_target_pairs={{0,8},{4,12},{8,0},{12,4},{16,24},{20,28},{24,16},{28,20},{1,9},{5... | collective-permute-start | bytes 294920 | tf_op jit(solution)/shard_map/ppermute | solution.py:27
  23.3 2.6 %collective-permute-start.1 = (bf16[2,3,32,256]{3,2,1,0:T(8,128)(2,1)S(1)}, bf16[2,3,32,256]{3,2,1,0:T(8,128)(2,1)S(1)}, u32[]{:S(2)}, u32[]{:S(2)}) collective-permute-start(bf16[2,3,32,256]{3,2,1,0:T(8,128)(2,1)S(1)} %get-tuple-element.42), channel_id=1, source_target_pairs={{0,16},{4,20},{8,24},{12,28},{16,0},{20,4},{24,8},{28,12},{1,17},{... | collective-permute-start | bytes 294920 | tf_op jit(solution)/shard_map/ppermute | solution.py:27
  27.1 1.8 %collective-permute-start.5 = (bf16[1,3,32,256]{3,2,1,0:T(8,128)(2,1)S(1)}, bf16[1,3,32,256]{3,2,1,0:T(8,128)(2,1)S(1)}, u32[]{:S(2)}, u32[]{:S(2)}) collective-permute-start(bf16[1,3,32,256]{3,2,1,0:T(8,128)(2,1)S(1)} %get-tuple-element.51), channel_id=1, source_target_pairs={{0,16},{4,20},{8,24},{12,28},{16,0},{20,4},{24,8},{28,12},{1,17},{... | collective-permute-start | bytes 147464 | tf_op jit(solution)/shard_map/ppermute | solution.py:27
  28.9 1.8 %collective-permute-done.1.refs_1_ = bf16[2,3,32,256]{3,2,1,0:T(8,128)(2,1)S(1)} collective-permute-done((bf16[2,3,32,256]{3,2,1,0:T(8,128)(2,1)S(1)}, bf16[2,3,32,256]{3,2,1,0:T(8,128)(2,1)S(1)}, u32[]{:S(2)}, u32[]{:S(2)}) %collective-permute-start.1) | collective-permute-done | bytes 98336 | tf_op jit(solution)/shard_map/ppermute | solution.py:27
  33.4 12.0 %collective-permute-done.6.refs_5_.refs_2_.refs_1_ = bf16[192,768]{1,0:T(8,128)(2,1)S(1)} collective-permute-done((bf16[192,768]{1,0:T(8,128)(2,1)S(1)}, bf16[192,768]{1,0:T(8,128)(2,1)S(1)}, u32[]{:S(2)}, u32[]{:S(2)}) %collective-permute-start.6) | collective-permute-done | bytes 294944 | tf_op jit(solution)/shard_map/ppermute | solution.py:27
  45.4 5.5 %collective-permute-done.7.refs_6_.refs_3_.refs_2_ = bf16[192,768]{1,0:T(8,128)(2,1)S(1)} collective-permute-done((bf16[192,768]{1,0:T(8,128)(2,1)S(1)}, bf16[192,768]{1,0:T(8,128)(2,1)S(1)}, u32[]{:S(2)}, u32[]{:S(2)}) %collective-permute-start.7) | collective-permute-done | bytes 294944 | tf_op jit(solution)/shard_map/ppermute | solution.py:27
  51.2 1.8 %collective-permute-start.11 = (bf16[1,3,32,256]{3,2,1,0:T(8,128)(2,1)S(1)}, bf16[1,3,32,256]{3,2,1,0:T(8,128)(2,1)S(1)}, u32[]{:S(2)}, u32[]{:S(2)}) collective-permute-start(bf16[1,3,32,256]{3,2,1,0:T(8,128)(2,1)S(1)} %get-tuple-element.53.refs_0_), channel_id=1, source_target_pairs={{0,4},{4,0},{8,12},{12,8},{16,20},{20,16},{24,28},{28,24},{1,5},{5... | collective-permute-start | bytes 147464 | tf_op jit(solution)/shard_map/ppermute | solution.py:27
  53.0 2.6 %collective-permute-start.8 = (bf16[1,3,32,256]{3,2,1,0:T(8,128)(2,1)S(1)}, bf16[1,3,32,256]{3,2,1,0:T(8,128)(2,1)S(1)}, u32[]{:S(2)}, u32[]{:S(2)}) collective-permute-start(bf16[1,3,32,256]{3,2,1,0:T(8,128)(2,1)S(1)} %get-tuple-element.52.refs_0_), channel_id=1, source_target_pairs={{0,16},{4,20},{8,24},{12,28},{16,0},{20,4},{24,8},{28,12},{1,17},{... | collective-permute-start | bytes 147464 | tf_op jit(solution)/shard_map/ppermute | solution.py:27
  55.6 2.7 %collective-permute-start.12 = (bf16[2,3,32,256]{3,2,1,0:T(8,128)(2,1)S(1)}, bf16[2,3,32,256]{3,2,1,0:T(8,128)(2,1)S(1)}, u32[]{:S(2)}, u32[]{:S(2)}) collective-permute-start(bf16[2,3,32,256]{3,2,1,0:T(8,128)(2,1)S(1)} %join.6.refs_0_), channel_id=1, source_target_pairs={{0,16},{4,20},{8,24},{12,28},{16,0},{20,4},{24,8},{28,12},{1,17},{... | collective-permute-start | bytes 294920 | tf_op jit(solution)/shard_map/ppermute | solution.py:27
  58.4 1.9 %collective-permute-start.9 = (bf16[2,3,32,256]{3,2,1,0:T(8,128)(2,1)S(1)}, bf16[2,3,32,256]{3,2,1,0:T(8,128)(2,1)S(1)}, u32[]{:S(2)}, u32[]{:S(2)}) collective-permute-start(bf16[2,3,32,256]{3,2,1,0:T(8,128)(2,1)S(1)} %join.4.refs_0_), channel_id=1, source_target_pairs={{0,8},{4,12},{8,0},{12,4},{16,24},{20,28},{24,16},{28,20},{1,9},{5... | collective-permute-start | bytes 294920 | tf_op jit(solution)/shard_map/ppermute | solution.py:27
  60.3 2.5 %collective-permute-done.12.refs_1_ = bf16[2,3,32,256]{3,2,1,0:T(8,128)(2,1)S(1)} collective-permute-done((bf16[2,3,32,256]{3,2,1,0:T(8,128)(2,1)S(1)}, bf16[2,3,32,256]{3,2,1,0:T(8,128)(2,1)S(1)}, u32[]{:S(2)}, u32[]{:S(2)}) %collective-permute-start.12) | collective-permute-done | bytes 98336 | tf_op jit(solution)/shard_map/ppermute | solution.py:27
  63.3 1.9 %collective-permute-start.10 = (bf16[4,3,32,256]{3,2,1,0:T(8,128)(2,1)S(1)}, bf16[4,3,32,256]{3,2,1,0:T(8,128)(2,1)S(1)}, u32[]{:S(2)}, u32[]{:S(2)}) collective-permute-start(bf16[4,3,32,256]{3,2,1,0:T(8,128)(2,1)S(1)} %join.5.refs_1_), channel_id=1, source_target_pairs={{0,4},{4,0},{8,12},{12,8},{16,20},{20,16},{24,28},{28,24},{1,5},{5... | collective-permute-start | bytes 589832 | tf_op jit(solution)/shard_map/ppermute | solution.py:27
  65.2 1.6 %collective-permute-start.16 = (bf16[192,384]{1,0:T(8,128)(2,1)S(1)}, bf16[192,384]{1,0:T(8,128)(2,1)S(1)}, u32[]{:S(2)}, u32[]{:S(2)}) collective-permute-start(bf16[192,384]{1,0:T(8,128)(2,1)S(1)} %get-tuple-element.57), channel_id=1, source_target_pairs={{0,2},{1,3},{2,0},{3,1},{4,6},{5,7},{6,4},{7,5},{8,10},{9,11},{10,... | collective-permute-start | bytes 442376 | tf_op jit(solution)/shard_map/ppermute | solution.py:27
  73.4 1.9 %own_gradients.1.refs_2_.refs_1_ = bf16[16,9,64,256]{3,2,1,0:T(8,128)(2,1)S(1)} custom-call(s32[18]{0:T(128)S(1)} %pad_add_fusion.refs_0_, bf16[8,3,32,256]{3,2,1,0:T(8,128)(2,1)S(1)} %get-tuple-element.54.refs_1_.refs_0_, bf16[8,3,32,256]{3,2,1,0:T(8,128)(2,1)S(1)} %get-tuple-element.55.refs_2_, bf16[16,6,64,256]{3,2,1,0:T(8,128)(2,1)S(1)} %get-tuple-element.56.refs_3_, ...), custom_call_target="tpu_custom_call" | custom-call | flops 1207959552 | bytes 10223652 | tf_op jit(solution)/shard_map/own_gradients/pallas_call | solution.py:56
  75.3 4.7 %weight_part.1 = (f32[4,96,576]{2,1,0:T(8,128)S(1)}, bf16[4,96,576]{2,1,0:T(8,128)(2,1)S(1)}) custom-call(s32[18]{0:T(128)S(1)} %pad_add_fusion.refs_0_, bf16[16,256,768]{2,1,0:T(8,128)(2,1)S(1)} %get-tuple-element.45.refs_1_, bf16[16,9,64,256]{3,2,1,0:T(8,128)(2,1)S(1)} %own_gradients.1.refs_2_.refs_1_, bf16[192,384]{1,0:T(8,128)(2,1)S(1)} %collective-permute-done.16.refs_3_), custom_call_target="tpu_custom_call" | custom-call | flops 3623878656 | bytes 11894820 | tf_op jit(solution)/shard_map/weight_part/pallas_call | solution.py:56
  82.9 5.9 %near_input.1 = (bf16[2,4,192,256]{3,2,1,0:T(8,128)(2,1)S(1)}, bf16[2,4,192,256]{3,2,1,0:T(8,128)(2,1)S(1)}, bf16[2,4,192,256]{3,2,1,0:T(8,128)(2,1)S(1)}, bf16[2,4,192,256]{3,2,1,0:T(8,128)(2,1)S(1)}) custom-call(s32[18]{0:T(128)S(1)} %pad_add_fusion.refs_0_, bf16[16,9,64,256]{3,2,1,0:T(8,128)(2,1)S(1)} %own_gradients.1.refs_2_.refs_1_, ...), custom_call_target="tpu_custom_call" | custom-call | flops 3623878656 | bytes 12288036 | tf_op jit(solution)/shard_map/near_input/pallas_call | solution.py:56
  89.1 2.3 %collective-permute-start.21 = (bf16[2,96,576]{2,1,0:T(8,128)(2,1)S(1)}, bf16[2,96,576]{2,1,0:T(8,128)(2,1)S(1)}, u32[]{:S(2)}, u32[]{:S(2)}) collective-permute-start(bf16[2,96,576]{2,1,0:T(8,128)(2,1)S(1)} %get-tuple-element.69), channel_id=1, source_target_pairs={{0,8},{4,12},{8,0},{12,4},{16,24},{20,28},{24,16},{28,20},{1,9},{5... | collective-permute-start | bytes 663560 | tf_op jit(solution)/shard_map/ppermute | solution.py:27
  91.4 4.2 %collective-permute-done.21.refs_1_ = bf16[2,96,576]{2,1,0:T(8,128)(2,1)S(1)} collective-permute-done((bf16[2,96,576]{2,1,0:T(8,128)(2,1)S(1)}, bf16[2,96,576]{2,1,0:T(8,128)(2,1)S(1)}, u32[]{:S(2)}, u32[]{:S(2)}) %collective-permute-start.21) | collective-permute-done | bytes 221216 | tf_op jit(solution)/shard_map/ppermute | solution.py:27
  101.5 3.7 %collective-permute-start.24 = (bf16[1,96,576]{2,1,0:T(8,128)(2,1)S(1)}, bf16[1,96,576]{2,1,0:T(8,128)(2,1)S(1)}, u32[]{:S(2)}, u32[]{:S(2)}) collective-permute-start(bf16[1,96,576]{2,1,0:T(8,128)(2,1)S(1)} %get-tuple-element.75), channel_id=1, source_target_pairs={{0,16},{4,20},{8,24},{12,28},{16,0},{20,4},{24,8},{28,12},{1,17},{... | collective-permute-start | bytes 331784 | tf_op jit(solution)/shard_map/ppermute | solution.py:27
  105.2 6.2 %collective-permute-done.24.refs_1_ = bf16[1,96,576]{2,1,0:T(8,128)(2,1)S(1)} collective-permute-done((bf16[1,96,576]{2,1,0:T(8,128)(2,1)S(1)}, bf16[1,96,576]{2,1,0:T(8,128)(2,1)S(1)}, u32[]{:S(2)}, u32[]{:S(2)}) %collective-permute-start.24) | collective-permute-done | bytes 110624 | tf_op jit(solution)/shard_map/ppermute | solution.py:27
  (65 shorter events, 28.0 us)
Async XLA Ops:
  0.6 71.6 %collective-permute-start.14 = (bf16[16,192,256]{2,1,0:T(8,128)(2,1)}, bf16[16,192,256]{2,1,0:T(8,128)(2,1)S(1)}, u32[]{:S(2)}, u32[]{:S(2)}) collective-permute-start(bf16[16,192,256]{2,1,0:T(8,128)(2,1)} %bitcast.8), channel_id=1, source_target_pairs={{0,2},{1,3},{2,0},{3,1},{4,6},{5,7},{6,4},{7,5},{8,10},{9,11},{10,... | collective-permute-start | bytes 4718600 | tf_op jit(solution)/shard_map/ppermute | solution.py:27
  15.1 6.4 %collective-permute-start.3 = (bf16[4,3,32,256]{3,2,1,0:T(8,128)(2,1)S(1)}, bf16[4,3,32,256]{3,2,1,0:T(8,128)(2,1)S(1)}, u32[]{:S(2)}, u32[]{:S(2)}) collective-permute-start(bf16[4,3,32,256]{3,2,1,0:T(8,128)(2,1)S(1)} %get-tuple-element.47.refs_4_), channel_id=1, source_target_pairs={{0,4},{4,0},{8,12},{12,8},{16,20},{20,16},{24,28},{28,24},{1,5},{5... | collective-permute-start | bytes 589832 | tf_op jit(solution)/shard_map/ppermute | solution.py:27
  16.7 6.6 %collective-permute-start = (bf16[4,3,32,256]{3,2,1,0:T(8,128)(2,1)S(1)}, bf16[4,3,32,256]{3,2,1,0:T(8,128)(2,1)S(1)}, u32[]{:S(2)}, u32[]{:S(2)}) collective-permute-start(bf16[4,3,32,256]{3,2,1,0:T(8,128)(2,1)S(1)} %get-tuple-element.40.refs_4_), channel_id=1, source_target_pairs={{0,8},{4,12},{8,0},{12,4},{16,24},{20,28},{24,16},{28,20},{1,9},{5... | collective-permute-start | bytes 589832 | tf_op jit(solution)/shard_map/ppermute | solution.py:27
  18.2 27.2 %collective-permute-start.6 = (bf16[192,768]{1,0:T(8,128)(2,1)S(1)}, bf16[192,768]{1,0:T(8,128)(2,1)S(1)}, u32[]{:S(2)}, u32[]{:S(2)}) collective-permute-start(bf16[192,768]{1,0:T(8,128)(2,1)S(1)} %bitcast.14), channel_id=1, source_target_pairs={{0,2},{1,3},{2,0},{3,1},{4,6},{5,7},{6,4},{7,5},{8,10},{9,11},{10,... | collective-permute-start | bytes 884744 | tf_op jit(solution)/shard_map/ppermute | solution.py:27
  18.8 32.1 %collective-permute-start.7 = (bf16[192,768]{1,0:T(8,128)(2,1)S(1)}, bf16[192,768]{1,0:T(8,128)(2,1)S(1)}, u32[]{:S(2)}, u32[]{:S(2)}) collective-permute-start(bf16[192,768]{1,0:T(8,128)(2,1)S(1)} %bitcast.17), channel_id=1, source_target_pairs={{0,2},{1,3},{2,0},{3,1},{4,6},{5,7},{6,4},{7,5},{8,10},{9,11},{10,... | collective-permute-start | bytes 884744 | tf_op jit(solution)/shard_map/ppermute | solution.py:27
  21.6 5.5 %collective-permute-start.4 = (bf16[2,3,32,256]{3,2,1,0:T(8,128)(2,1)S(1)}, bf16[2,3,32,256]{3,2,1,0:T(8,128)(2,1)S(1)}, u32[]{:S(2)}, u32[]{:S(2)}) collective-permute-start(bf16[2,3,32,256]{3,2,1,0:T(8,128)(2,1)S(1)} %get-tuple-element.49), channel_id=1, source_target_pairs={{0,8},{4,12},{8,0},{12,4},{16,24},{20,28},{24,16},{28,20},{1,9},{5... | collective-permute-start | bytes 294920 | tf_op jit(solution)/shard_map/ppermute | solution.py:27
  23.3 7.5 %collective-permute-start.1 = (bf16[2,3,32,256]{3,2,1,0:T(8,128)(2,1)S(1)}, bf16[2,3,32,256]{3,2,1,0:T(8,128)(2,1)S(1)}, u32[]{:S(2)}, u32[]{:S(2)}) collective-permute-start(bf16[2,3,32,256]{3,2,1,0:T(8,128)(2,1)S(1)} %get-tuple-element.42), channel_id=1, source_target_pairs={{0,16},{4,20},{8,24},{12,28},{16,0},{20,4},{24,8},{28,12},{1,17},{... | collective-permute-start | bytes 294920 | tf_op jit(solution)/shard_map/ppermute | solution.py:27
  27.1 23.8 %collective-permute-start.5 = (bf16[1,3,32,256]{3,2,1,0:T(8,128)(2,1)S(1)}, bf16[1,3,32,256]{3,2,1,0:T(8,128)(2,1)S(1)}, u32[]{:S(2)}, u32[]{:S(2)}) collective-permute-start(bf16[1,3,32,256]{3,2,1,0:T(8,128)(2,1)S(1)} %get-tuple-element.51), channel_id=1, source_target_pairs={{0,16},{4,20},{8,24},{12,28},{16,0},{20,4},{24,8},{28,12},{1,17},{... | collective-permute-start | bytes 147464 | tf_op jit(solution)/shard_map/ppermute | solution.py:27
  30.8 20.1 %collective-permute-start.2 = (bf16[1,3,32,256]{3,2,1,0:T(8,128)(2,1)S(1)}, bf16[1,3,32,256]{3,2,1,0:T(8,128)(2,1)S(1)}, u32[]{:S(2)}, u32[]{:S(2)}) collective-permute-start(bf16[1,3,32,256]{3,2,1,0:T(8,128)(2,1)S(1)} %get-tuple-element.44), channel_id=1, source_target_pairs={{0,4},{4,0},{8,12},{12,8},{16,20},{20,16},{24,28},{28,24},{1,5},{5... | collective-permute-start | bytes 147464 | tf_op jit(solution)/shard_map/ppermute | solution.py:27
  53.0 5.4 %collective-permute-start.8 = (bf16[1,3,32,256]{3,2,1,0:T(8,128)(2,1)S(1)}, bf16[1,3,32,256]{3,2,1,0:T(8,128)(2,1)S(1)}, u32[]{:S(2)}, u32[]{:S(2)}) collective-permute-start(bf16[1,3,32,256]{3,2,1,0:T(8,128)(2,1)S(1)} %get-tuple-element.52.refs_0_), channel_id=1, source_target_pairs={{0,16},{4,20},{8,24},{12,28},{16,0},{20,4},{24,8},{28,12},{1,17},{... | collective-permute-start | bytes 147464 | tf_op jit(solution)/shard_map/ppermute | solution.py:27
  55.6 7.2 %collective-permute-start.12 = (bf16[2,3,32,256]{3,2,1,0:T(8,128)(2,1)S(1)}, bf16[2,3,32,256]{3,2,1,0:T(8,128)(2,1)S(1)}, u32[]{:S(2)}, u32[]{:S(2)}) collective-permute-start(bf16[2,3,32,256]{3,2,1,0:T(8,128)(2,1)S(1)} %join.6.refs_0_), channel_id=1, source_target_pairs={{0,16},{4,20},{8,24},{12,28},{16,0},{20,4},{24,8},{28,12},{1,17},{... | collective-permute-start | bytes 294920 | tf_op jit(solution)/shard_map/ppermute | solution.py:27
  58.4 4.9 %collective-permute-start.9 = (bf16[2,3,32,256]{3,2,1,0:T(8,128)(2,1)S(1)}, bf16[2,3,32,256]{3,2,1,0:T(8,128)(2,1)S(1)}, u32[]{:S(2)}, u32[]{:S(2)}) collective-permute-start(bf16[2,3,32,256]{3,2,1,0:T(8,128)(2,1)S(1)} %join.4.refs_0_), channel_id=1, source_target_pairs={{0,8},{4,12},{8,0},{12,4},{16,24},{20,28},{24,16},{28,20},{1,9},{5... | collective-permute-start | bytes 294920 | tf_op jit(solution)/shard_map/ppermute | solution.py:27
  62.8 9.4 %collective-permute-start.13 = (bf16[4,3,32,256]{3,2,1,0:T(8,128)(2,1)S(1)}, bf16[4,3,32,256]{3,2,1,0:T(8,128)(2,1)S(1)}, u32[]{:S(2)}, u32[]{:S(2)}) collective-permute-start(bf16[4,3,32,256]{3,2,1,0:T(8,128)(2,1)S(1)} %join.7.refs_3_), channel_id=1, source_target_pairs={{0,8},{4,12},{8,0},{12,4},{16,24},{20,28},{24,16},{28,20},{1,9},{5... | collective-permute-start | bytes 589832 | tf_op jit(solution)/shard_map/ppermute | solution.py:27
  63.3 8.9 %collective-permute-start.10 = (bf16[4,3,32,256]{3,2,1,0:T(8,128)(2,1)S(1)}, bf16[4,3,32,256]{3,2,1,0:T(8,128)(2,1)S(1)}, u32[]{:S(2)}, u32[]{:S(2)}) collective-permute-start(bf16[4,3,32,256]{3,2,1,0:T(8,128)(2,1)S(1)} %join.5.refs_1_), channel_id=1, source_target_pairs={{0,4},{4,0},{8,12},{12,8},{16,20},{20,16},{24,28},{28,24},{1,5},{5... | collective-permute-start | bytes 589832 | tf_op jit(solution)/shard_map/ppermute | solution.py:27
  65.2 10.1 %collective-permute-start.16 = (bf16[192,384]{1,0:T(8,128)(2,1)S(1)}, bf16[192,384]{1,0:T(8,128)(2,1)S(1)}, u32[]{:S(2)}, u32[]{:S(2)}) collective-permute-start(bf16[192,384]{1,0:T(8,128)(2,1)S(1)} %get-tuple-element.57), channel_id=1, source_target_pairs={{0,2},{1,3},{2,0},{3,1},{4,6},{5,7},{6,4},{7,5},{8,10},{9,11},{10,... | collective-permute-start | bytes 442376 | tf_op jit(solution)/shard_map/ppermute | solution.py:27
  72.9 8.7 %collective-permute-start.15 = (bf16[8,3,32,256]{3,2,1,0:T(8,128)(2,1)S(1)}, bf16[8,3,32,256]{3,2,1,0:T(8,128)(2,1)S(1)}, u32[]{:S(2)}, u32[]{:S(2)}) collective-permute-start(bf16[8,3,32,256]{3,2,1,0:T(8,128)(2,1)S(1)} %get-tuple-element.55.refs_2_), channel_id=1, source_target_pairs={{0,2},{1,3},{2,0},{3,1},{4,6},{5,7},{6,4},{7,5},{8,10},{9,11},{10,... | collective-permute-start | bytes 1179656 | tf_op jit(solution)/shard_map/ppermute | solution.py:27
  80.1 9.0 %collective-permute-start.18 = (bf16[4,96,576]{2,1,0:T(8,128)(2,1)S(1)}, bf16[4,96,576]{2,1,0:T(8,128)(2,1)S(1)}, u32[]{:S(2)}, u32[]{:S(2)}) collective-permute-start(bf16[4,96,576]{2,1,0:T(8,128)(2,1)S(1)} %get-tuple-element.58.refs_1_), channel_id=1, source_target_pairs={{0,4},{4,0},{8,12},{12,8},{16,20},{20,16},{24,28},{28,24},{1,5},{5... | collective-permute-start | bytes 1327112 | tf_op jit(solution)/shard_map/ppermute | solution.py:27
  81.6 14.1 %collective-permute-start.17 = (bf16[8,3,32,256]{3,2,1,0:T(8,128)(2,1)S(1)}, bf16[8,3,32,256]{3,2,1,0:T(8,128)(2,1)S(1)}, u32[]{:S(2)}, u32[]{:S(2)}) collective-permute-start(bf16[8,3,32,256]{3,2,1,0:T(8,128)(2,1)S(1)} %hold.1.refs_4_), channel_id=1, source_target_pairs={{0,2},{1,3},{2,0},{3,1},{4,6},{5,7},{6,4},{7,5},{8,10},{9,11},{10,... | collective-permute-start | bytes 1179656 | tf_op jit(solution)/shard_map/ppermute | solution.py:27
  89.1 6.5 %collective-permute-start.21 = (bf16[2,96,576]{2,1,0:T(8,128)(2,1)S(1)}, bf16[2,96,576]{2,1,0:T(8,128)(2,1)S(1)}, u32[]{:S(2)}, u32[]{:S(2)}) collective-permute-start(bf16[2,96,576]{2,1,0:T(8,128)(2,1)S(1)} %get-tuple-element.69), channel_id=1, source_target_pairs={{0,8},{4,12},{8,0},{12,4},{16,24},{20,28},{24,16},{28,20},{1,9},{5... | collective-permute-start | bytes 663560 | tf_op jit(solution)/shard_map/ppermute | solution.py:27
  96.8 15.4 %collective-permute-start.23 = (bf16[4,192,256]{2,1,0:T(8,128)(2,1)S(1)}, bf16[4,192,256]{2,1,0:T(8,128)(2,1)S(1)}, u32[]{:S(2)}, u32[]{:S(2)}) collective-permute-start(bf16[4,192,256]{2,1,0:T(8,128)(2,1)S(1)} %get-tuple-element.74), channel_id=1, source_target_pairs={{0,1},{1,0},{2,3},{3,2},{4,5},{5,4},{6,7},{7,6},{8,9},{9,8},{10,11... | collective-permute-start | bytes 1179656 | tf_op jit(solution)/shard_map/ppermute | solution.py:27
  98.0 14.2 %collective-permute-start.22 = (bf16[4,192,256]{2,1,0:T(8,128)(2,1)S(1)}, bf16[4,192,256]{2,1,0:T(8,128)(2,1)S(1)}, u32[]{:S(2)}, u32[]{:S(2)}) collective-permute-start(bf16[4,192,256]{2,1,0:T(8,128)(2,1)S(1)} %get-tuple-element.72), channel_id=1, source_target_pairs={{0,1},{1,0},{2,3},{3,2},{4,5},{5,4},{6,7},{7,6},{8,9},{9,8},{10,11... | collective-permute-start | bytes 1179656 | tf_op jit(solution)/shard_map/ppermute | solution.py:27
  99.7 12.5 %collective-permute-start.20 = (bf16[4,192,256]{2,1,0:T(8,128)(2,1)S(1)}, bf16[4,192,256]{2,1,0:T(8,128)(2,1)S(1)}, u32[]{:S(2)}, u32[]{:S(2)}) collective-permute-start(bf16[4,192,256]{2,1,0:T(8,128)(2,1)S(1)} %get-tuple-element.67), channel_id=1, source_target_pairs={{0,1},{1,0},{2,3},{3,2},{4,5},{5,4},{6,7},{7,6},{8,9},{9,8},{10,11... | collective-permute-start | bytes 1179656 | tf_op jit(solution)/shard_map/ppermute | solution.py:27
  100.9 11.3 %collective-permute-start.19 = (bf16[4,192,256]{2,1,0:T(8,128)(2,1)S(1)}, bf16[4,192,256]{2,1,0:T(8,128)(2,1)S(1)}, u32[]{:S(2)}, u32[]{:S(2)}) collective-permute-start(bf16[4,192,256]{2,1,0:T(8,128)(2,1)S(1)} %get-tuple-element.64), channel_id=1, source_target_pairs={{0,1},{1,0},{2,3},{3,2},{4,5},{5,4},{6,7},{7,6},{8,9},{9,8},{10,11... | collective-permute-start | bytes 1179656 | tf_op jit(solution)/shard_map/ppermute | solution.py:27
  101.5 9.9 %collective-permute-start.24 = (bf16[1,96,576]{2,1,0:T(8,128)(2,1)S(1)}, bf16[1,96,576]{2,1,0:T(8,128)(2,1)S(1)}, u32[]{:S(2)}, u32[]{:S(2)}) collective-permute-start(bf16[1,96,576]{2,1,0:T(8,128)(2,1)S(1)} %get-tuple-element.75), channel_id=1, source_target_pairs={{0,16},{4,20},{8,24},{12,28},{16,0},{20,4},{24,8},{28,12},{1,17},{... | collective-permute-start | bytes 331784 | tf_op jit(solution)/shard_map/ppermute | solution.py:27
  (5 other events, 32.5 us)

commit v14 on v10

--- a/solution.py
+++ b/solution.py
@@ -84,20 +84,29 @@
 AHEAD = 4
 
 
-def query_key_kernel(bits, where, sheet, wq, wk, qk, held, *rest):
-    outs, (wt, acc, sems) = rest[:-3], rest[-3:]
-    rows, cols, _ = sheet.shape
+def query_key_kernel(bits, fars, where, sheet, wq, wk, wv, qk, held, *rest):
+    outs, staged, (wt, acc, sems) = rest[: -3 - len(fars)], rest[-3 - len(fars) : -3], rest[-3:]
+    rows, cols, width = sheet.shape
     local = wq.shape[0]
     heads = local // HEAD_DIM
-    copies = [
-        pltpu.make_async_copy(wq, wt.at[:local], sems.at[0]),
-        pltpu.make_async_copy(wk, wt.at[local:], sems.at[1]),
-    ]
+    copies = []
+
+    def copy(source, target):
+        copies.append(pltpu.make_async_copy(source, target, sems.at[len(copies)]))
+
+    copy(wq, wt.at[:local])
+    copy(wk, wt.at[local:])
     for first in range(0, rows, STEP):
         some = pl.ds(first, STEP)
-        copies.append(pltpu.make_async_copy(sheet.at[some], held.at[some], sems.at[len(copies)]))
-    for copy in copies[:AHEAD]:
-        copy.start()
+        copy(sheet.at[some], held.at[some])
+    for far, out in zip(fars, staged):
+        near = out.shape[1] - width
+        side = lax.shift_right_logical(where[1], 1) ^ (far // 2)
+        some = pl.ds(pl.multiple_of(side * near, 128), near)
+        copy(wk, out.at[:, pl.ds(0, width)])
+        copy(wv.at[:, some], out.at[:, pl.ds(width, near)])
+    for one in copies[:AHEAD]:
+        one.start()
     copies[0].wait()
     copies[1].wait()
     flat = (BLOCK * HEAD_DIM, cols)
@@ -106,7 +115,8 @@
             if r % STEP == 0:
                 at = 2 + r // STEP
                 copies[at].wait()
-                for later in copies[at + AHEAD - 2 : at + AHEAD - 1]:
+                last = at + AHEAD - 1 if r + STEP < rows else len(copies)
+                for later in copies[at + AHEAD - 2 : last]:
                     later.start()
             value = (mm(wt[...], held[r], NT) * lane_mask(where[2 + r], cols)).astype(BF16)
             qk[r] = value.reshape(2 * heads, HEAD_DIM, cols)
@@ -116,45 +126,45 @@
             term = term.reshape(acc.shape[1:])
             acc[h] = term if first == 0 else acc[h] + term
     put_shards(where[0], acc, bits, outs)
-
-
-def query_key(where, sheet, wq, wk, bits):
+    started = 2 + rows // STEP
+    for one in copies[started:]:
+        one.wait()
+
+
+def query_key(where, sheet, wq, wk, wv, bits, fars, devices):
     rows, cols, width = sheet.shape
     shards = 1 << len(bits)
     local = wq.shape[0]
     heads = local // HEAD_DIM
     return in_vmem(
-        functools.partial(query_key_kernel, bits),
+        functools.partial(query_key_kernel, bits, fars),
         "query_key",
-        [like((rows, 2 * heads, HEAD_DIM, cols)), like(sheet.shape)] + part_shapes(shards, heads, cols),
+        [like((rows, 2 * heads, HEAD_DIM, cols)), like(sheet.shape)]
+        + part_shapes(shards, heads, cols)
+        + [like((local, width + 2 * width // devices))] * len(fars),
         where,
         sheet,
         wq,
         wk,
+        wv,
         scalars=1,
-        streamed=3,
+        streamed=4,
         scratch=(
             pltpu.VMEM((2 * local, width), BF16),
             pltpu.VMEM((heads, shards, cols // shards, cols), F32),
-            pltpu.SemaphoreType.DMA((2 + rows // STEP,)),
+            pltpu.SemaphoreType.DMA((2 + rows // STEP + 2 * len(fars),)),
         ),
         limit=14,
         flops=2 * rows * cols * local * (2 * width + cols),
     )
 
 
-def value_kernel(bits, fars, where, sheet, wv, cot, *rest):
-    outs, halves, acc = rest[: -1 - len(fars)], rest[-1 - len(fars) : -1], rest[-1]
+def value_kernel(bits, where, sheet, wv, cot, *rest):
+    *outs, copied, acc = rest
+    copied[...] = cot[...]
     rows, cols, width = sheet.shape
     local = wv.shape[0]
     heads = local // HEAD_DIM
-    for far, half in zip(fars, halves):
-        near = half.shape[1]
-        side = lax.shift_right_logical(where[1], 1) ^ (far // 2)
-        for s in range(width // near):
-            @pl.when(side == s)
-            def _():
-                half[...] = wv[:, s * near : (s + 1) * near]
     flat = (BLOCK * HEAD_DIM, cols)
     for first in range(0, rows, BLOCK):
         values = []
@@ -169,15 +179,15 @@
     put_shards(where[0], acc, bits, outs)
 
 
-def value_dprob(where, sheet, wv, cot, after, bits, fars, devices):
+def value_dprob(where, sheet, wv, cot, after, bits):
     rows, cols, width = sheet.shape
     shards = 1 << len(bits)
     local = wv.shape[0]
     heads = local // HEAD_DIM
     return in_vmem(
-        functools.partial(value_kernel, bits, fars),
+        functools.partial(value_kernel, bits),
         "value_dprob",
-        part_shapes(shards, heads, cols) + [like((local, 2 * width // devices))] * len(fars),
+        part_shapes(shards, heads, cols) + [like(cot.shape)],
         where,
         sheet,
         wv,
@@ -186,60 +196,63 @@
         after=after,
         scratch=(pltpu.VMEM((heads, shards, cols // shards, cols), F32),),
         limit=16,
-        flops=4 * rows * cols * local * (width + cols),
+        flops=16 * rows * cols * local * (width + cols),
     )
 
 
-def turn_kernel(where, wq, wk, wv, natural, *full):
+def turn_kernel(where, wq, *rest):
+    *others, natural, query, key, value = rest
     near, share, columns = natural.shape
-    local = wq.shape[0]
-    for index, (weight, held) in enumerate(zip((wq, wk, wv), full)):
-        held[...] = weight[...].T.reshape(held.shape)
+    local, width = wq.shape
+    wk = others[0][:, :width]
+    wv = others[1][...] if len(others) == 2 else others[0][:, width:]
+    for index, (weight, held) in enumerate(((wq[...], query), (wk, key), (wv, value))):
+        held[...] = weight.T.reshape(held.shape)
         mine = where[1] & (held.shape[0] - 1)
         for j in range(near):
             natural[j, :, index * local : (index + 1) * local] = held[mine ^ j]
 
 
-def turn(where, wq, wk, wv, devices, after):
+def turn(where, wq, others, devices, after):
     local, width = wq.shape
     share = width // devices
+    counts = (devices, devices, devices if len(others) == 2 else 2)
     return in_vmem(
         turn_kernel,
         "turn",
         (like((2, share, 3 * local)),),
         where,
         wq,
-        wk,
-        wv,
+        *others,
         scalars=1,
         after=after,
-        scratch=[pltpu.VMEM((w.shape[1] // share, share, local), BF16) for w in (wq, wk, wv)],
+        scratch=[pltpu.VMEM((count, share, local), BF16) for count in counts],
     )[0]
 
 
-def far_query_key_kernel(first, where, sheet, wq, wk, qk):
-    local, _ = wq.shape
-    cols = sheet.shape[1]
-    both = jnp.concatenate([wq[...], wk[...]], axis=0)
-    for r in range(qk.shape[0]):
-        value = (mm(both, sheet[first + r], NT) * lane_mask(where[2 + first + r], cols)).astype(BF16)
+def far_query_key_kernel(where, sheet, wq, staged, qk):
+    local = staged.shape[0]
+    rows, cols, width = sheet.shape
+    both = jnp.concatenate([wq[...], staged[:, :width]], axis=0)
+    for r in range(rows):
+        value = (mm(both, sheet[r], NT) * lane_mask(where[2 + r], cols)).astype(BF16)
         qk[r] = value.reshape(2 * local // HEAD_DIM, HEAD_DIM, cols)
 
 
-def far_query_key(first, count, where, sheet, wq, wk, after):
-    _, cols, width = sheet.shape
-    local = wq.shape[0]
-    return in_vmem(
-        functools.partial(far_query_key_kernel, first),
+def far_query_key(where, sheet, wq, staged, after):
+    rows, cols, width = sheet.shape
+    local = staged.shape[0]
+    return in_vmem(
+        far_query_key_kernel,
         "far_query_key",
-        (like((count, 2 * local // HEAD_DIM, HEAD_DIM, cols)),),
+        (like((rows, 2 * local // HEAD_DIM, HEAD_DIM, cols)),),
         where,
         sheet,
         wq,
-        wk,
+        staged,
         scalars=1,
         after=after,
-        flops=4 * count * cols * local * width,
+        flops=4 * rows * cols * local * width,
     )[0]
 
 
@@ -310,20 +323,28 @@
 
 
 def assemble_kernel(orders, where, *refs):
-    pieces, outs = refs[:-2], refs[-2:]
+    *pieces, out = refs
     for piece, (kind, order) in zip(pieces, orders):
         for t, j in enumerate(order):
-            outs[kind][where[0] ^ j] = piece[t]
+            out[kind, where[0] ^ j] = piece[t]
 
 
 def assemble(where, probs, dscore, orders, shards, after):
-    out = like((shards,) + probs[0].shape[1:])
-    return in_vmem(
-        functools.partial(assemble_kernel, [(k, o) for k, both in enumerate(orders) for o in both]), "assemble", (out, out), where, *probs, *dscore, scalars=1, after=after
-    )
-
-
-def gradients(where, first, count, probs, dscore, qk, cot, grads):
+    orders = [(kind, order) for kind, both in enumerate(orders) for order in both]
+    out = like((2, shards) + probs[0].shape[1:])
+    return in_vmem(
+        functools.partial(assemble_kernel, orders),
+        "assemble",
+        (out,),
+        where,
+        *probs,
+        *dscore,
+        scalars=1,
+        after=after,
+    )[0]
+
+
+def gradients(where, first, count, scores, qk, cot, grads):
     cols = qk.shape[-1]
     heads = qk.shape[1] // 2
     rows = pl.ds(first, count)
@@ -331,7 +352,7 @@
     split = (count, HEAD_DIM, cols)
     masks = jnp.stack([lane_mask(where[2 + first + r], cols) for r in range(count)])
     for h in range(heads):
-        p, ds = [ref[:, h].reshape(cols, cols) for ref in (probs, dscore)]
+        p, ds = [scores[kind, :, h].reshape(cols, cols) for kind in range(2)]
         g = cot[rows, h * HEAD_DIM : (h + 1) * HEAD_DIM].reshape(flat)
         dq = mm(qk[rows, heads + h].reshape(flat), ds, NT)
         dk = mm(qk[rows, h].reshape(flat), ds, NN)
@@ -340,19 +361,18 @@
             grads[:, index * heads + h] = (value.reshape(split) * masks).astype(BF16)
 
 
-def gradients_kernel(where, probs, dscore, qk, cot, grads):
-    gradients(where, 0, qk.shape[0], probs, dscore, qk, cot, grads)
-
-
-def all_gradients(where, probs, dscore, qk, cot, name, after):
+def gradients_kernel(where, scores, qk, cot, grads):
+    gradients(where, 0, qk.shape[0], scores, qk, cot, grads)
+
+
+def all_gradients(where, scores, qk, cot, name, after):
     rows, two, _, cols = qk.shape
     return in_vmem(
         gradients_kernel,
         name,
         (like((rows, two // 2 * 3, HEAD_DIM, cols)),),
         where,
-        probs,
-        dscore,
+        scores,
         qk,
         cot,
         scalars=1,
@@ -469,7 +489,7 @@
     out[...] = weight_product(sheet, grads)
 
 
-def weight_part(where, sheet, grads, cuts, shards):
+def weight_part(where, sheet, grads, cuts, shards, after):
     rows, cols, width = sheet.shape
     columns = grads.shape[1] * HEAD_DIM
     if shards == 1:
@@ -487,6 +507,7 @@
         sheet,
         grads,
         scalars=1,
+        after=after,
         scratch=scratch,
         limit=18,
         flops=2 * rows * cols * width * columns,
@@ -526,38 +547,33 @@
     cot = jnp.swapaxes(cotangent, 1, 2)
 
     fars = range(2, n_heads, 2)
-    far_cot = [flip(cot, "heads", f) for f in fars]
-    fq, fk = [[flip(w, "heads", f) for f in fars] for w in (wq, wk)]
-
+    far_wq = [flip(wq, "heads", f) for f in fars]
     up = row_bits if direct else []
     turn_about = up[1:] + up[:1]
-    qk, held, *logits = query_key(where, sheet, wq, wk, turn_about)
-    *dprob, = value_dprob(where, held, wv, cot, logits[-1:], up, fars, n_heads)
-    dprob, halves = dprob[: -len(fars)], dprob[-len(fars) :]
-    fv = [flip(half, "heads", f) for half, f in zip(halves, fars)]
-    weights = turn(where, wq, wk, wv, n_heads, dprob[-1:])
+    qk, held, *logits = query_key(where, sheet, wq, wk, wv, turn_about, fars, n_heads)
+    logits, staged = logits[: -len(fars)], logits[-len(fars) :]
+    far_staged = [flip(a, "heads", f) for a, f in zip(staged, fars)]
+    *dprob, copied = value_dprob(where, held, wv, cot, logits[-1:] + far_wq, up)
+    far_cot = [flip(copied, "heads", f) for f in fars]
+    weights = turn(where, wq, [wk, wv], n_heads, dprob[-1:])
     if direct:
         logits = halve(*logits, "rows", turn_about)
-        dprob = halve(*dprob, "rows", up)
-        probs_own, dscore_own = softmax_back(logits, dprob, scale, [weights])
-        probs, probs_order = double(probs_own, "rows", up[::-1], [far_cot])
-        dscore, dscore_order = double(dscore_own, "rows", turn_about[::-1], [far_cot])
-        probs, dscore = assemble(where, probs, dscore, (probs_order, dscore_order), shards, fq + fk + fv)
+        dprob = halve(*dprob, "rows", up, [far_staged])
+        probs, dscore = softmax_back(logits, dprob, scale, [weights] + far_staged)
+        probs, probs_order = double(probs, "rows", up[::-1])
+        dscore, dscore_order = double(dscore, "rows", turn_about[::-1])
+        scores = assemble(where, probs, dscore, (probs_order, dscore_order), shards, ())
     else:
         logits, dprob = lax.psum((logits, dprob), "rows")
-        probs, dscore = softmax_back(logits, dprob, scale)
-    far_dscore = [flip(dscore, "heads", f) for f in fars]
-    far_probs = [flip(probs, "heads", f) for f in fars]
-
-    grads = all_gradients(where, probs, dscore, qk, cot, "own_gradients", ())
-    parts = weight_part(where, held, grads, (3 * local,), shards)
+        scores = jnp.stack(softmax_back(logits, dprob, scale))
+    far_scores = [flip(scores, "heads", f) for f in fars]
+    grads = all_gradients(where, scores, qk, cot, "own_gradients", ())
+    parts = weight_part(where, held, grads, (3 * local,), shards, ())
     ready = [parts[-1]]
-    far_qk, far_natural = [], []
-    for w in zip(fq, fk, fv):
-        far_qk.append(far_query_key(0, row_dev, where, held, w[0], w[1], ready))
-        far_natural.append(turn(where, *w, n_heads, ready))
+    far_qk = [far_query_key(where, held, *w, ready + far_cot) for w in zip(far_wq, far_staged)]
+    far_natural = [turn(where, w, [other], n_heads, ready) for w, other in zip(far_wq, far_staged)]
     own = own_input(grads, weights, ready)
-    ready = [own] + far_qk + far_natural + far_probs + far_dscore
+    ready = [own] + far_qk + far_natural + far_scores
     steps = [[], []]
     if direct:
         keep, give = parts
@@ -574,7 +590,7 @@
 
     far_grads = [
         all_gradients(where, *args, "far_gradients", steps[0])
-        for args in zip(far_probs, far_dscore, far_qk, far_cot)
+        for args in zip(far_scores, far_qk, far_cot)
     ]
     chunks = []
     for index, first in enumerate(range(0, row_dev, chunk)):

time: 101 us -> 93.7 us (0.928)
  waiting for transfers between devices: 29.7 us -> 21.9 us
    ppermute x25 -> x23, waiting for transfers between devices: 29.7 us -> 21.9 us  [flip(): return lax.ppermute(values, axis, [(s, s ^ bit) for s in range(n)])]
    ppermute x25 -> x23, starting transfers between devices: 35.8 us -> 36 us  [flip(): return lax.ppermute(values, axis, [(s, s ^ bit) for s in range(n)])]
  transfers between devices with their start and end apart: 25 -> 23, of which waited for: 11 -> 12; matrix products, arithmetic and copies ran while one was open for 1% -> 1% of each run, Pallas kernels for 25% -> 35%
where the time goes in v14:
time: 93.7 us; the launch traced here: 93.4 us
  starting transfers between devices  36 us (38%)
  Pallas kernels  33.8 us (36%)
  waiting for transfers between devices  21.9 us (23%)
  between operations  1.03 us (1%)
    ppermute x23, starting transfers between devices, flip(): return lax.ppermute(values, axis, [(s, s ^ bit) for s in range(n)])  36 us
    pallas_call x26, Pallas kernels, in_vmem(): pl.pallas_call(run, in_specs=[SMEM] * scalars + [HBM] * streamed + [VMEM]...  32.5 us
    ppermute x23, waiting for transfers between devices, flip(): return lax.ppermute(values, axis, [(s, s ^ bit) for s in range(n)])  21.9 us
  transfers between devices with their start and end apart: 23, of which 12 were waited for; matrix products, arithmetic and copies ran while one was open for 1% of the time, Pallas kernels for 35%

profile of v14, /device:TPU:0, one launch (start us, length us, event | category | flops | bytes accessed | tf_op | source)
XLA Modules:
  0.0 93.4 jit_solution(5621874742854179777)
XLA Ops:
  0.6 3.0 %collective-permute-start.3 = (bf16[192,768]{1,0:T(8,128)(2,1)}, bf16[192,768]{1,0:T(8,128)(2,1)S(1)}, u32[]{:S(2)}, u32[]{:S(2)}) collective-permute-start(bf16[192,768]{1,0:T(8,128)(2,1)} %bitcast.10), channel_id=1, source_target_pairs={{0,2},{1,3},{2,0},{3,1},{4,6},{5,7},{6,4},{7,5},{8,10},{9,11},{10,... | collective-permute-start | bytes 884744 | tf_op jit(solution)/shard_map/ppermute | solution.py:27
  4.4 7.1 %query_key.1 = (bf16[16,6,64,256]{3,2,1,0:T(8,128)(2,1)S(1)}, bf16[16,256,768]{2,1,0:T(8,128)(2,1)S(1)}, f32[4,3,32,256]{3,2,1,0:T(8,128)S(1)}, bf16[4,3,32,256]{3,2,1,0:T(8,128)(2,1)S(1)}, bf16[192,1152]{1,0:T(8,128)(2,1)S(1)}) custom-call(s32[18]{0:T(128)S(1)} %pad_add_fusion.refs_0_, bf16[16,256,768]{2,1,0:T(8,128)(2,1)} %refs_1_.1, ...), custom_call_target="tpu_custom_call" | custom-call | flops 2818572288 | bytes 17448996 | tf_op jit(solution)/shard_map/query_key/pallas_call | solution.py:56
  11.7 3.6 %value_dprob.1 = (f32[4,3,32,256]{3,2,1,0:T(8,128)S(1)}, bf16[4,3,32,256]{3,2,1,0:T(8,128)(2,1)S(1)}, bf16[16,192,256]{2,1,0:T(8,128)(2,1)S(1)}) custom-call(s32[18]{0:T(128)S(1)} %pad_add_fusion.refs_0_, bf16[16,256,768]{2,1,0:T(8,128)(2,1)S(1)} %get-tuple-element.40.refs_1_, bf16[192,768]{1,0:T(8,128)(2,1)S(1)} %bitcast.16, ...), custom_call_target="tpu_custom_call" | custom-call | flops 12884901888 | bytes 10125348 | tf_op jit(solution)/shard_map/value_dprob/pallas_call | solution.py:56
  15.3 2.1 %collective-permute-start.15 = (bf16[16,192,256]{2,1,0:T(8,128)(2,1)S(1)}, bf16[16,192,256]{2,1,0:T(8,128)(2,1)S(1)}, u32[]{:S(2)}, u32[]{:S(2)}) collective-permute-start(bf16[16,192,256]{2,1,0:T(8,128)(2,1)S(1)} %get-tuple-element.52), channel_id=1, source_target_pairs={{0,2},{1,3},{2,0},{3,1},{4,6},{5,7},{6,4},{7,5},{8,10},{9,11},{10,... | collective-permute-start | bytes 4718600 | tf_op jit(solution)/shard_map/ppermute | solution.py:27
  20.4 2.7 %collective-permute-done.refs_1_ = bf16[4,3,32,256]{3,2,1,0:T(8,128)(2,1)S(1)} collective-permute-done((bf16[4,3,32,256]{3,2,1,0:T(8,128)(2,1)S(1)}, bf16[4,3,32,256]{3,2,1,0:T(8,128)(2,1)S(1)}, u32[]{:S(2)}, u32[]{:S(2)}) %collective-permute-start) | collective-permute-done | bytes 196640 | tf_op jit(solution)/shard_map/ppermute | solution.py:27
  23.2 2.7 %collective-permute-start.1 = (bf16[2,3,32,256]{3,2,1,0:T(8,128)(2,1)S(1)}, bf16[2,3,32,256]{3,2,1,0:T(8,128)(2,1)S(1)}, u32[]{:S(2)}, u32[]{:S(2)}) collective-permute-start(bf16[2,3,32,256]{3,2,1,0:T(8,128)(2,1)S(1)} %get-tuple-element.37), channel_id=1, source_target_pairs={{0,16},{4,20},{8,24},{12,28},{16,0},{20,4},{24,8},{28,12},{1,17},{... | collective-permute-start | bytes 294920 | tf_op jit(solution)/shard_map/ppermute | solution.py:27
  25.9 1.6 %collective-permute-start.6 = (bf16[2,3,32,256]{3,2,1,0:T(8,128)(2,1)S(1)}, bf16[2,3,32,256]{3,2,1,0:T(8,128)(2,1)S(1)}, u32[]{:S(2)}, u32[]{:S(2)}) collective-permute-start(bf16[2,3,32,256]{3,2,1,0:T(8,128)(2,1)S(1)} %get-tuple-element.45), channel_id=1, source_target_pairs={{0,8},{4,12},{8,0},{12,4},{16,24},{20,28},{24,16},{28,20},{1,9},{5... | collective-permute-start | bytes 294920 | tf_op jit(solution)/shard_map/ppermute | solution.py:27
  30.6 2.5 %collective-permute-start.7 = (bf16[1,3,32,256]{3,2,1,0:T(8,128)(2,1)S(1)}, bf16[1,3,32,256]{3,2,1,0:T(8,128)(2,1)S(1)}, u32[]{:S(2)}, u32[]{:S(2)}) collective-permute-start(bf16[1,3,32,256]{3,2,1,0:T(8,128)(2,1)S(1)} %get-tuple-element.47), channel_id=1, source_target_pairs={{0,16},{4,20},{8,24},{12,28},{16,0},{20,4},{24,8},{28,12},{1,17},{... | collective-permute-start | bytes 147464 | tf_op jit(solution)/shard_map/ppermute | solution.py:27
  34.2 1.8 %collective-permute-done.7.refs_3_ = bf16[1,3,32,256]{3,2,1,0:T(8,128)(2,1)S(1)} collective-permute-done((bf16[1,3,32,256]{3,2,1,0:T(8,128)(2,1)S(1)}, bf16[1,3,32,256]{3,2,1,0:T(8,128)(2,1)S(1)}, u32[]{:S(2)}, u32[]{:S(2)}) %collective-permute-start.7) | collective-permute-done | bytes 49184 | tf_op jit(solution)/shard_map/ppermute | solution.py:27
  36.3 2.5 %collective-permute-start.8 = (bf16[1,3,32,256]{3,2,1,0:T(8,128)(2,1)S(1)}, bf16[1,3,32,256]{3,2,1,0:T(8,128)(2,1)S(1)}, u32[]{:S(2)}, u32[]{:S(2)}) collective-permute-start(bf16[1,3,32,256]{3,2,1,0:T(8,128)(2,1)S(1)} %get-tuple-element.48.refs_0_), channel_id=1, source_target_pairs={{0,16},{4,20},{8,24},{12,28},{16,0},{20,4},{24,8},{28,12},{1,17},{... | collective-permute-start | bytes 147464 | tf_op jit(solution)/shard_map/ppermute | solution.py:27
  39.2 2.2 %collective-permute-done.8.refs_1_ = bf16[1,3,32,256]{3,2,1,0:T(8,128)(2,1)S(1)} collective-permute-done((bf16[1,3,32,256]{3,2,1,0:T(8,128)(2,1)S(1)}, bf16[1,3,32,256]{3,2,1,0:T(8,128)(2,1)S(1)}, u32[]{:S(2)}, u32[]{:S(2)}) %collective-permute-start.8) | collective-permute-done | bytes 49184 | tf_op jit(solution)/shard_map/ppermute | solution.py:27
  41.4 3.0 %collective-permute-start.9 = (bf16[2,3,32,256]{3,2,1,0:T(8,128)(2,1)S(1)}, bf16[2,3,32,256]{3,2,1,0:T(8,128)(2,1)S(1)}, u32[]{:S(2)}, u32[]{:S(2)}) collective-permute-start(bf16[2,3,32,256]{3,2,1,0:T(8,128)(2,1)S(1)} %join.4.refs_0_), channel_id=1, source_target_pairs={{0,8},{4,12},{8,0},{12,4},{16,24},{20,28},{24,16},{28,20},{1,9},{5... | collective-permute-start | bytes 294920 | tf_op jit(solution)/shard_map/ppermute | solution.py:27
  44.4 3.5 %collective-permute-start.12 = (bf16[2,3,32,256]{3,2,1,0:T(8,128)(2,1)S(1)}, bf16[2,3,32,256]{3,2,1,0:T(8,128)(2,1)S(1)}, u32[]{:S(2)}, u32[]{:S(2)}) collective-permute-start(bf16[2,3,32,256]{3,2,1,0:T(8,128)(2,1)S(1)} %join.6.refs_0_), channel_id=1, source_target_pairs={{0,16},{4,20},{8,24},{12,28},{16,0},{20,4},{24,8},{28,12},{1,17},{... | collective-permute-start | bytes 294920 | tf_op jit(solution)/shard_map/ppermute | solution.py:27
  48.7 1.8 %collective-permute-done.12.refs_1_ = bf16[2,3,32,256]{3,2,1,0:T(8,128)(2,1)S(1)} collective-permute-done((bf16[2,3,32,256]{3,2,1,0:T(8,128)(2,1)S(1)}, bf16[2,3,32,256]{3,2,1,0:T(8,128)(2,1)S(1)}, u32[]{:S(2)}, u32[]{:S(2)}) %collective-permute-start.12) | collective-permute-done | bytes 98336 | tf_op jit(solution)/shard_map/ppermute | solution.py:27
  50.6 2.5 %collective-permute-start.13 = (bf16[4,3,32,256]{3,2,1,0:T(8,128)(2,1)S(1)}, bf16[4,3,32,256]{3,2,1,0:T(8,128)(2,1)S(1)}, u32[]{:S(2)}, u32[]{:S(2)}) collective-permute-start(bf16[4,3,32,256]{3,2,1,0:T(8,128)(2,1)S(1)} %join.7.refs_3_), channel_id=1, source_target_pairs={{0,8},{4,12},{8,0},{12,4},{16,24},{20,28},{24,16},{28,20},{1,9},{5... | collective-permute-start | bytes 589832 | tf_op jit(solution)/shard_map/ppermute | solution.py:27
  53.7 3.0 %collective-permute-done.13.refs_4_ = bf16[4,3,32,256]{3,2,1,0:T(8,128)(2,1)S(1)} collective-permute-done((bf16[4,3,32,256]{3,2,1,0:T(8,128)(2,1)S(1)}, bf16[4,3,32,256]{3,2,1,0:T(8,128)(2,1)S(1)}, u32[]{:S(2)}, u32[]{:S(2)}) %collective-permute-start.13) | collective-permute-done | bytes 196640 | tf_op jit(solution)/shard_map/ppermute | solution.py:27
  57.8 1.9 %own_gradients.1.refs_2_.refs_0_ = bf16[16,9,64,256]{3,2,1,0:T(8,128)(2,1)S(1)} custom-call(s32[18]{0:T(128)S(1)} %pad_add_fusion.refs_0_, bf16[2,8,3,32,256]{4,3,2,1,0:T(8,128)(2,1)S(1)} %assemble.1.refs_1_, bf16[16,6,64,256]{3,2,1,0:T(8,128)(2,1)S(1)} %get-tuple-element.50.refs_2_, bf16[16,192,256]{2,1,0:T(8,128)(2,1)S(1)} %bitcast.9), custom_call_target="tpu_custom_call" | custom-call | flops 1207959552 | bytes 10223652 | tf_op jit(solution)/shard_map/own_gradients/pallas_call | solution.py:56
  59.8 4.7 %weight_part.1 = (f32[4,96,576]{2,1,0:T(8,128)S(1)}, bf16[4,96,576]{2,1,0:T(8,128)(2,1)S(1)}) custom-call(s32[18]{0:T(128)S(1)} %pad_add_fusion.refs_0_, bf16[16,256,768]{2,1,0:T(8,128)(2,1)S(1)} %get-tuple-element.40.refs_1_, bf16[16,9,64,256]{3,2,1,0:T(8,128)(2,1)S(1)} %own_gradients.1.refs_2_.refs_0_), custom_call_target="tpu_custom_call" | custom-call | flops 3623878656 | bytes 11894820 | tf_op jit(solution)/shard_map/weight_part/pallas_call | solution.py:56
  66.2 2.8 %own_input.1.refs_2_.refs_0_ = bf16[2,16,192,256]{3,2,1,0:T(8,128)(2,1)S(1)} custom-call(bf16[16,9,64,256]{3,2,1,0:T(8,128)(2,1)S(1)} %own_gradients.1.refs_2_.refs_0_, bf16[2,192,576]{2,1,0:T(8,128)(2,1)S(1)} %turn.2.refs_4_.refs_1_, bf16[4,96,576]{2,1,0:T(8,128)(2,1)S(1)} %get-tuple-element.51.refs_2_.refs_4_.refs_3_), custom_call_target="tpu_custom_call" | custom-call | flops 1811939328 | bytes 8306688 | tf_op jit(solution)/shard_map/own_input/pallas_call | solution.py:56
  69.1 3.2 %far_query_key.1.refs_3_.refs_2_ = bf16[16,6,64,256]{3,2,1,0:T(8,128)(2,1)S(1)} custom-call(s32[18]{0:T(128)S(1)} %pad_add_fusion.refs_0_, bf16[16,256,768]{2,1,0:T(8,128)(2,1)S(1)} %get-tuple-element.40.refs_1_, bf16[192,768]{1,0:T(8,128)(2,1)S(1)} %collective-permute-done.3.refs_5_.refs_2_.refs_1_, ...), custom_call_target="tpu_custom_call" | custom-call | flops 2415919104 | bytes 10174500 | tf_op jit(solution)/shard_map/far_query_key/pallas_call | solution.py:56
  73.9 1.7 %collective-permute-start.19 = (bf16[2,96,576]{2,1,0:T(8,128)(2,1)S(1)}, bf16[2,96,576]{2,1,0:T(8,128)(2,1)S(1)}, u32[]{:S(2)}, u32[]{:S(2)}) collective-permute-start(bf16[2,96,576]{2,1,0:T(8,128)(2,1)S(1)} %get-tuple-element.59), channel_id=1, source_target_pairs={{0,8},{4,12},{8,0},{12,4},{16,24},{20,28},{24,16},{28,20},{1,9},{5... | collective-permute-start | bytes 663560 | tf_op jit(solution)/shard_map/ppermute | solution.py:27
  75.6 1.9 %far_gradients.1.refs_1_ = bf16[16,9,64,256]{3,2,1,0:T(8,128)(2,1)S(1)} custom-call(s32[18]{0:T(128)S(1)} %pad_add_fusion.refs_0_, bf16[2,8,3,32,256]{4,3,2,1,0:T(8,128)(2,1)S(1)} %collective-permute-done.14.refs_5_.refs_1_, bf16[16,6,64,256]{3,2,1,0:T(8,128)(2,1)S(1)} %far_query_key.1.refs_3_.refs_2_, ...), custom_call_target="tpu_custom_call" | custom-call | flops 1207959552 | bytes 10223652 | tf_op jit(solution)/shard_map/far_gradients/pallas_call | solution.py:56
  82.3 2.6 %collective-permute-start.22 = (bf16[1,96,576]{2,1,0:T(8,128)(2,1)S(1)}, bf16[1,96,576]{2,1,0:T(8,128)(2,1)S(1)}, u32[]{:S(2)}, u32[]{:S(2)}) collective-permute-start(bf16[1,96,576]{2,1,0:T(8,128)(2,1)S(1)} %get-tuple-element.65), channel_id=1, source_target_pairs={{0,16},{4,20},{8,24},{12,28},{16,0},{20,4},{24,8},{28,12},{1,17},{... | collective-permute-start | bytes 331784 | tf_op jit(solution)/shard_map/ppermute | solution.py:27
  84.9 6.2 %collective-permute-done.22.refs_1_ = bf16[1,96,576]{2,1,0:T(8,128)(2,1)S(1)} collective-permute-done((bf16[1,96,576]{2,1,0:T(8,128)(2,1)S(1)}, bf16[1,96,576]{2,1,0:T(8,128)(2,1)S(1)}, u32[]{:S(2)}, u32[]{:S(2)}) %collective-permute-start.22) | collective-permute-done | bytes 110624 | tf_op jit(solution)/shard_map/ppermute | solution.py:27
  (58 shorter events, 21.5 us)
Async XLA Ops:
  0.6 11.0 %collective-permute-start.3 = (bf16[192,768]{1,0:T(8,128)(2,1)}, bf16[192,768]{1,0:T(8,128)(2,1)S(1)}, u32[]{:S(2)}, u32[]{:S(2)}) collective-permute-start(bf16[192,768]{1,0:T(8,128)(2,1)} %bitcast.10), channel_id=1, source_target_pairs={{0,2},{1,3},{2,0},{3,1},{4,6},{5,7},{6,4},{7,5},{8,10},{9,11},{10,... | collective-permute-start | bytes 884744 | tf_op jit(solution)/shard_map/ppermute | solution.py:27
  11.5 14.3 %collective-permute-start.5 = (bf16[192,1152]{1,0:T(8,128)(2,1)S(1)}, bf16[192,1152]{1,0:T(8,128)(2,1)S(1)}, u32[]{:S(2)}, u32[]{:S(2)}) collective-permute-start(bf16[192,1152]{1,0:T(8,128)(2,1)S(1)} %get-tuple-element.43), channel_id=1, source_target_pairs={{0,2},{1,3},{2,0},{3,1},{4,6},{5,7},{6,4},{7,5},{8,10},{9,11},{10,... | collective-permute-start | bytes 1327112 | tf_op jit(solution)/shard_map/ppermute | solution.py:27
  11.6 21.5 %copy-start.1 = (bf16[768,192]{0,1:T(8,128)(2,1)S(1)}, bf16[768,192]{0,1:T(8,128)(2,1)}, u32[]{:S(2)}) copy-start(bf16[768,192]{0,1:T(8,128)(2,1)} %param.7) | copy-start | bytes 884740
  15.3 53.8 %collective-permute-start.15 = (bf16[16,192,256]{2,1,0:T(8,128)(2,1)S(1)}, bf16[16,192,256]{2,1,0:T(8,128)(2,1)S(1)}, u32[]{:S(2)}, u32[]{:S(2)}) collective-permute-start(bf16[16,192,256]{2,1,0:T(8,128)(2,1)S(1)} %get-tuple-element.52), channel_id=1, source_target_pairs={{0,2},{1,3},{2,0},{3,1},{4,6},{5,7},{6,4},{7,5},{8,10},{9,11},{10,... | collective-permute-start | bytes 4718600 | tf_op jit(solution)/shard_map/ppermute | solution.py:27
  17.3 5.8 %collective-permute-start = (bf16[4,3,32,256]{3,2,1,0:T(8,128)(2,1)S(1)}, bf16[4,3,32,256]{3,2,1,0:T(8,128)(2,1)S(1)}, u32[]{:S(2)}, u32[]{:S(2)}) collective-permute-start(bf16[4,3,32,256]{3,2,1,0:T(8,128)(2,1)S(1)} %get-tuple-element.35.refs_4_), channel_id=1, source_target_pairs={{0,8},{4,12},{8,0},{12,4},{16,24},{20,28},{24,16},{28,20},{1,9},{5... | collective-permute-start | bytes 589832 | tf_op jit(solution)/shard_map/ppermute | solution.py:27
  18.9 6.9 %collective-permute-start.4 = (bf16[4,3,32,256]{3,2,1,0:T(8,128)(2,1)S(1)}, bf16[4,3,32,256]{3,2,1,0:T(8,128)(2,1)S(1)}, u32[]{:S(2)}, u32[]{:S(2)}) collective-permute-start(bf16[4,3,32,256]{3,2,1,0:T(8,128)(2,1)S(1)} %get-tuple-element.42.refs_4_), channel_id=1, source_target_pairs={{0,4},{4,0},{8,12},{12,8},{16,20},{20,16},{24,28},{28,24},{1,5},{5... | collective-permute-start | bytes 589832 | tf_op jit(solution)/shard_map/ppermute | solution.py:27
  23.2 5.6 %collective-permute-start.1 = (bf16[2,3,32,256]{3,2,1,0:T(8,128)(2,1)S(1)}, bf16[2,3,32,256]{3,2,1,0:T(8,128)(2,1)S(1)}, u32[]{:S(2)}, u32[]{:S(2)}) collective-permute-start(bf16[2,3,32,256]{3,2,1,0:T(8,128)(2,1)S(1)} %get-tuple-element.37), channel_id=1, source_target_pairs={{0,16},{4,20},{8,24},{12,28},{16,0},{20,4},{24,8},{28,12},{1,17},{... | collective-permute-start | bytes 294920 | tf_op jit(solution)/shard_map/ppermute | solution.py:27
  25.9 4.7 %collective-permute-start.6 = (bf16[2,3,32,256]{3,2,1,0:T(8,128)(2,1)S(1)}, bf16[2,3,32,256]{3,2,1,0:T(8,128)(2,1)S(1)}, u32[]{:S(2)}, u32[]{:S(2)}) collective-permute-start(bf16[2,3,32,256]{3,2,1,0:T(8,128)(2,1)S(1)} %get-tuple-element.45), channel_id=1, source_target_pairs={{0,8},{4,12},{8,0},{12,4},{16,24},{20,28},{24,16},{28,20},{1,9},{5... | collective-permute-start | bytes 294920 | tf_op jit(solution)/shard_map/ppermute | solution.py:27
  28.8 5.4 %collective-permute-start.2 = (bf16[1,3,32,256]{3,2,1,0:T(8,128)(2,1)S(1)}, bf16[1,3,32,256]{3,2,1,0:T(8,128)(2,1)S(1)}, u32[]{:S(2)}, u32[]{:S(2)}) collective-permute-start(bf16[1,3,32,256]{3,2,1,0:T(8,128)(2,1)S(1)} %get-tuple-element.39), channel_id=1, source_target_pairs={{0,4},{4,0},{8,12},{12,8},{16,20},{20,16},{24,28},{28,24},{1,5},{5... | collective-permute-start | bytes 147464 | tf_op jit(solution)/shard_map/ppermute | solution.py:27
  30.6 5.4 %collective-permute-start.7 = (bf16[1,3,32,256]{3,2,1,0:T(8,128)(2,1)S(1)}, bf16[1,3,32,256]{3,2,1,0:T(8,128)(2,1)S(1)}, u32[]{:S(2)}, u32[]{:S(2)}) collective-permute-start(bf16[1,3,32,256]{3,2,1,0:T(8,128)(2,1)S(1)} %get-tuple-element.47), channel_id=1, source_target_pairs={{0,16},{4,20},{8,24},{12,28},{16,0},{20,4},{24,8},{28,12},{1,17},{... | collective-permute-start | bytes 147464 | tf_op jit(solution)/shard_map/ppermute | solution.py:27
  36.3 5.1 %collective-permute-start.8 = (bf16[1,3,32,256]{3,2,1,0:T(8,128)(2,1)S(1)}, bf16[1,3,32,256]{3,2,1,0:T(8,128)(2,1)S(1)}, u32[]{:S(2)}, u32[]{:S(2)}) collective-permute-start(bf16[1,3,32,256]{3,2,1,0:T(8,128)(2,1)S(1)} %get-tuple-element.48.refs_0_), channel_id=1, source_target_pairs={{0,16},{4,20},{8,24},{12,28},{16,0},{20,4},{24,8},{28,12},{1,17},{... | collective-permute-start | bytes 147464 | tf_op jit(solution)/shard_map/ppermute | solution.py:27
  38.8 5.6 %collective-permute-start.11 = (bf16[1,3,32,256]{3,2,1,0:T(8,128)(2,1)S(1)}, bf16[1,3,32,256]{3,2,1,0:T(8,128)(2,1)S(1)}, u32[]{:S(2)}, u32[]{:S(2)}) collective-permute-start(bf16[1,3,32,256]{3,2,1,0:T(8,128)(2,1)S(1)} %get-tuple-element.49.refs_0_), channel_id=1, source_target_pairs={{0,4},{4,0},{8,12},{12,8},{16,20},{20,16},{24,28},{28,24},{1,5},{5... | collective-permute-start | bytes 147464 | tf_op jit(solution)/shard_map/ppermute | solution.py:27
  41.4 6.6 %collective-permute-start.9 = (bf16[2,3,32,256]{3,2,1,0:T(8,128)(2,1)S(1)}, bf16[2,3,32,256]{3,2,1,0:T(8,128)(2,1)S(1)}, u32[]{:S(2)}, u32[]{:S(2)}) collective-permute-start(bf16[2,3,32,256]{3,2,1,0:T(8,128)(2,1)S(1)} %join.4.refs_0_), channel_id=1, source_target_pairs={{0,8},{4,12},{8,0},{12,4},{16,24},{20,28},{24,16},{28,20},{1,9},{5... | collective-permute-start | bytes 294920 | tf_op jit(solution)/shard_map/ppermute | solution.py:27
  44.4 6.1 %collective-permute-start.12 = (bf16[2,3,32,256]{3,2,1,0:T(8,128)(2,1)S(1)}, bf16[2,3,32,256]{3,2,1,0:T(8,128)(2,1)S(1)}, u32[]{:S(2)}, u32[]{:S(2)}) collective-permute-start(bf16[2,3,32,256]{3,2,1,0:T(8,128)(2,1)S(1)} %join.6.refs_0_), channel_id=1, source_target_pairs={{0,16},{4,20},{8,24},{12,28},{16,0},{20,4},{24,8},{28,12},{1,17},{... | collective-permute-start | bytes 294920 | tf_op jit(solution)/shard_map/ppermute | solution.py:27
  48.0 5.7 %collective-permute-start.10 = (bf16[4,3,32,256]{3,2,1,0:T(8,128)(2,1)S(1)}, bf16[4,3,32,256]{3,2,1,0:T(8,128)(2,1)S(1)}, u32[]{:S(2)}, u32[]{:S(2)}) collective-permute-start(bf16[4,3,32,256]{3,2,1,0:T(8,128)(2,1)S(1)} %join.5.refs_1_), channel_id=1, source_target_pairs={{0,4},{4,0},{8,12},{12,8},{16,20},{20,16},{24,28},{28,24},{1,5},{5... | collective-permute-start | bytes 589832 | tf_op jit(solution)/shard_map/ppermute | solution.py:27
  50.6 6.1 %collective-permute-start.13 = (bf16[4,3,32,256]{3,2,1,0:T(8,128)(2,1)S(1)}, bf16[4,3,32,256]{3,2,1,0:T(8,128)(2,1)S(1)}, u32[]{:S(2)}, u32[]{:S(2)}) collective-permute-start(bf16[4,3,32,256]{3,2,1,0:T(8,128)(2,1)S(1)} %join.7.refs_3_), channel_id=1, source_target_pairs={{0,8},{4,12},{8,0},{12,4},{16,24},{20,28},{24,16},{28,20},{1,9},{5... | collective-permute-start | bytes 589832 | tf_op jit(solution)/shard_map/ppermute | solution.py:27
  57.3 16.5 %collective-permute-start.14 = (bf16[2,8,3,32,256]{4,3,2,1,0:T(8,128)(2,1)S(1)}, bf16[2,8,3,32,256]{4,3,2,1,0:T(8,128)(2,1)S(1)}, u32[]{:S(2)}, u32[]{:S(2)}) collective-permute-start(bf16[2,8,3,32,256]{4,3,2,1,0:T(8,128)(2,1)S(1)} %assemble.1.refs_1_), channel_id=1, source_target_pairs={{0,2},{1,3},{2,0},{3,1},{4,6},{5,7},{6,4},{7,5},{8,10},{9,11},{10,... | collective-permute-start | bytes 2359304 | tf_op jit(solution)/shard_map/ppermute | solution.py:27
  64.5 8.9 %collective-permute-start.16 = (bf16[4,96,576]{2,1,0:T(8,128)(2,1)S(1)}, bf16[4,96,576]{2,1,0:T(8,128)(2,1)S(1)}, u32[]{:S(2)}, u32[]{:S(2)}) collective-permute-start(bf16[4,96,576]{2,1,0:T(8,128)(2,1)S(1)} %get-tuple-element.51.refs_2_.refs_4_.refs_3_), channel_id=1, source_target_pairs={{0,4},{4,0},{8,12},{12,8},{16,20},{20,16},{24,28},{28,24},{1,5},{5... | collective-permute-start | bytes 1327112 | tf_op jit(solution)/shard_map/ppermute | solution.py:27
  73.9 6.3 %collective-permute-start.19 = (bf16[2,96,576]{2,1,0:T(8,128)(2,1)S(1)}, bf16[2,96,576]{2,1,0:T(8,128)(2,1)S(1)}, u32[]{:S(2)}, u32[]{:S(2)}) collective-permute-start(bf16[2,96,576]{2,1,0:T(8,128)(2,1)S(1)} %get-tuple-element.59), channel_id=1, source_target_pairs={{0,8},{4,12},{8,0},{12,4},{16,24},{20,28},{24,16},{28,20},{1,9},{5... | collective-permute-start | bytes 663560 | tf_op jit(solution)/shard_map/ppermute | solution.py:27
  78.3 13.7 %collective-permute-start.18 = (bf16[4,192,256]{2,1,0:T(8,128)(2,1)S(1)}, bf16[4,192,256]{2,1,0:T(8,128)(2,1)S(1)}, u32[]{:S(2)}, u32[]{:S(2)}) collective-permute-start(bf16[4,192,256]{2,1,0:T(8,128)(2,1)S(1)} %get-tuple-element.58), channel_id=1, source_target_pairs={{0,1},{1,0},{2,3},{3,2},{4,5},{5,4},{6,7},{7,6},{8,9},{9,8},{10,11... | collective-permute-start | bytes 1179656 | tf_op jit(solution)/shard_map/ppermute | solution.py:27
  79.2 12.8 %collective-permute-start.17 = (bf16[4,192,256]{2,1,0:T(8,128)(2,1)S(1)}, bf16[4,192,256]{2,1,0:T(8,128)(2,1)S(1)}, u32[]{:S(2)}, u32[]{:S(2)}) collective-permute-start(bf16[4,192,256]{2,1,0:T(8,128)(2,1)S(1)} %get-tuple-element.56), channel_id=1, source_target_pairs={{0,1},{1,0},{2,3},{3,2},{4,5},{5,4},{6,7},{7,6},{8,9},{9,8},{10,11... | collective-permute-start | bytes 1179656 | tf_op jit(solution)/shard_map/ppermute | solution.py:27
  81.8 10.2 %collective-permute-start.21 = (bf16[4,192,256]{2,1,0:T(8,128)(2,1)S(1)}, bf16[4,192,256]{2,1,0:T(8,128)(2,1)S(1)}, u32[]{:S(2)}, u32[]{:S(2)}) collective-permute-start(bf16[4,192,256]{2,1,0:T(8,128)(2,1)S(1)} %get-tuple-element.64), channel_id=1, source_target_pairs={{0,1},{1,0},{2,3},{3,2},{4,5},{5,4},{6,7},{7,6},{8,9},{9,8},{10,11... | collective-permute-start | bytes 1179656 | tf_op jit(solution)/shard_map/ppermute | solution.py:27
  81.9 10.2 %collective-permute-start.20 = (bf16[4,192,256]{2,1,0:T(8,128)(2,1)S(1)}, bf16[4,192,256]{2,1,0:T(8,128)(2,1)S(1)}, u32[]{:S(2)}, u32[]{:S(2)}) collective-permute-start(bf16[4,192,256]{2,1,0:T(8,128)(2,1)S(1)} %get-tuple-element.62), channel_id=1, source_target_pairs={{0,1},{1,0},{2,3},{3,2},{4,5},{5,4},{6,7},{7,6},{8,9},{9,8},{10,11... | collective-permute-start | bytes 1179656 | tf_op jit(solution)/shard_map/ppermute | solution.py:27
  82.3 8.8 %collective-permute-start.22 = (bf16[1,96,576]{2,1,0:T(8,128)(2,1)S(1)}, bf16[1,96,576]{2,1,0:T(8,128)(2,1)S(1)}, u32[]{:S(2)}, u32[]{:S(2)}) collective-permute-start(bf16[1,96,576]{2,1,0:T(8,128)(2,1)S(1)} %get-tuple-element.65), channel_id=1, source_target_pairs={{0,16},{4,20},{8,24},{12,28},{16,0},{20,4},{24,8},{28,12},{1,17},{... | collective-permute-start | bytes 331784 | tf_op jit(solution)/shard_map/ppermute | solution.py:27
  (3 other events, 35.9 us)

commit v15 on v14

--- a/solution.py
+++ b/solution.py
@@ -160,8 +160,7 @@
 
 
 def value_kernel(bits, where, sheet, wv, cot, *rest):
-    *outs, copied, acc = rest
-    copied[...] = cot[...]
+    outs, acc = rest[:-1], rest[-1]
     rows, cols, width = sheet.shape
     local = wv.shape[0]
     heads = local // HEAD_DIM
@@ -187,7 +186,7 @@
     return in_vmem(
         functools.partial(value_kernel, bits),
         "value_dprob",
-        part_shapes(shards, heads, cols) + [like(cot.shape)],
+        part_shapes(shards, heads, cols),
         where,
         sheet,
         wv,
@@ -261,6 +260,14 @@
         return [like((1, heads, cols, cols), F32)]
     half = (shards // 2, heads, cols // shards, cols)
     return [like(half, F32), like(half)]
+
+
+def hold_kernel(values, out):
+    out[...] = values[...]
+
+
+def hold(values, after):
+    return in_vmem(hold_kernel, "hold", (like(values.shape),), values, after=after)[0]
 
 
 def add_split_kernel(keep, got, give_out, keep_out):
@@ -514,20 +521,16 @@
     )
 
 
-def last_kernel(*refs):
-    *terms, out = refs
-    total = [terms[i][0] + terms[i + 1][0].astype(F32) for i in range(0, len(terms), 2)]
-    total = jnp.concatenate(total, axis=-1)
+def last_kernel(_, keep, got, out):
+    total = keep[0] + got[0].astype(F32)
     local = out.shape[-1]
     for index in range(out.shape[0]):
         out[index] = total[:, index * local : (index + 1) * local]
 
 
-def last_sum(halves, local, after):
-    terms = [a for half in halves for a in half]
-    columns = sum(keep.shape[2] for keep, _ in halves)
-    shape = (columns // local, terms[0].shape[1], local)
-    return in_vmem(last_kernel, "last_sum", (like(shape, F32),), *terms, after=after)[0]
+def last_sum(before, keep, got, local):
+    shape = (keep.shape[2] // local, keep.shape[1], local)
+    return in_vmem(last_kernel, "last_sum", (like(shape, F32),), before, keep, got, streamed=1)[0]
 
 
 def body(sheet, w_query, w_key, w_value, cotangent, lengths):
@@ -553,19 +556,22 @@
     qk, held, *logits = query_key(where, sheet, wq, wk, wv, turn_about, fars, n_heads)
     logits, staged = logits[: -len(fars)], logits[-len(fars) :]
     far_staged = [flip(a, "heads", f) for a, f in zip(staged, fars)]
-    *dprob, copied = value_dprob(where, held, wv, cot, logits[-1:] + far_wq, up)
-    far_cot = [flip(copied, "heads", f) for f in fars]
+    dprob = value_dprob(where, held, wv, cot, logits[-1:] + far_wq, up)
     weights = turn(where, wq, [wk, wv], n_heads, dprob[-1:])
     if direct:
-        logits = halve(*logits, "rows", turn_about)
+        give, keep = add_split(logits[0], flip(logits[1], "rows", turn_about[0]), dprob[1:])
+        later = [give]
+        logits = halve(keep, give, "rows", turn_about[1:])
         dprob = halve(*dprob, "rows", up, [far_staged])
         probs, dscore = softmax_back(logits, dprob, scale, [weights] + far_staged)
         probs, probs_order = double(probs, "rows", up[::-1])
         dscore, dscore_order = double(dscore, "rows", turn_about[::-1])
         scores = assemble(where, probs, dscore, (probs_order, dscore_order), shards, ())
     else:
+        later = [weights]
         logits, dprob = lax.psum((logits, dprob), "rows")
         scores = jnp.stack(softmax_back(logits, dprob, scale))
+    far_cot = [flip(hold(cot, later), "heads", f) for f in fars]
     far_scores = [flip(scores, "heads", f) for f in fars]
     grads = all_gradients(where, scores, qk, cot, "own_gradients", ())
     parts = weight_part(where, held, grads, (3 * local,), shards, ())
@@ -582,8 +588,7 @@
             give, keep = add_split(keep, flip(give, "rows", bit), ready)
             steps.append([keep])
             ready = ()
-        sums = last_sum([(keep, flip(give, "rows", row_bits[-1]))], local, ())
-        weight_grad = jnp.swapaxes(sums, 0, 1)
+        last = keep, flip(give, "rows", row_bits[-1])
     else:
         weight_grad = lax.psum_scatter(parts[0], "rows", scatter_dimension=0, tiled=True)
         weight_grad = weight_grad.reshape(width // n_rows, 3, local)
@@ -597,7 +602,10 @@
         after = steps[-1] if index >= 2 else ()
         keep, give = far_input(first, chunk, own, list(zip(far_grads, far_natural)), after)
         chunks.append((keep, flip(give, "heads", 1)))
-    return (jnp.swapaxes(finish(chunks), 1, 2), weight_grad)
+    out = finish(chunks)
+    if direct:
+        weight_grad = jnp.swapaxes(last_sum(out, *last, local), 0, 1)
+    return (jnp.swapaxes(out, 1, 2), weight_grad)
 
 
 def solution(mesh):

time: 93.7 us -> 93.4 us (level)
  starting transfers between devices: 36 us -> 27.5 us
  waiting for transfers between devices: 21.9 us -> 30.2 us
    ppermute x23, starting transfers between devices: 36 us -> 27.5 us  [flip(): return lax.ppermute(values, axis, [(s, s ^ bit) for s in range(n)])]
    ppermute x23, waiting for transfers between devices: 21.9 us -> 30.2 us  [flip(): return lax.ppermute(values, axis, [(s, s ^ bit) for s in range(n)])]
    pallas_call x26 -> x27, Pallas kernels: 32.5 us -> 32.5 us  [in_vmem(): pl.pallas_call(run, in_specs=[SMEM] * scalars + [HBM] * streamed + [VMEM]...]
  transfers between devices with their start and end apart: 23 -> 23, of which waited for: 12 -> 13; matrix products, arithmetic and copies ran while one was open for 1% -> 1% of each run, Pallas kernels for 35% -> 35%
where the time goes in v15:
time: 93.4 us; the launch traced here: 93.2 us
  Pallas kernels  33.8 us (36%)
  waiting for transfers between devices  30.2 us (32%)
  starting transfers between devices  27.5 us (29%)
    pallas_call x27, Pallas kernels, in_vmem(): pl.pallas_call(run, in_specs=[SMEM] * scalars + [HBM] * streamed + [VMEM]...  32.5 us
    ppermute x23, waiting for transfers between devices, flip(): return lax.ppermute(values, axis, [(s, s ^ bit) for s in range(n)])  30.2 us
    ppermute x23, starting transfers between devices, flip(): return lax.ppermute(values, axis, [(s, s ^ bit) for s in range(n)])  27.5 us
  transfers between devices with their start and end apart: 23, of which 13 were waited for; matrix products, arithmetic and copies ran while one was open for 1% of the time, Pallas kernels for 35%

profile of v15, /device:TPU:0, one launch (start us, length us, event | category | flops | bytes accessed | tf_op | source)
XLA Modules:
  0.0 93.2 jit_solution(8180649202820732814)
XLA Ops:
  0.6 3.0 %collective-permute-start.1 = (bf16[192,768]{1,0:T(8,128)(2,1)}, bf16[192,768]{1,0:T(8,128)(2,1)S(1)}, u32[]{:S(2)}, u32[]{:S(2)}) collective-permute-start(bf16[192,768]{1,0:T(8,128)(2,1)} %bitcast.11), channel_id=1, source_target_pairs={{0,2},{1,3},{2,0},{3,1},{4,6},{5,7},{6,4},{7,5},{8,10},{9,11},{10,... | collective-permute-start | bytes 884744 | tf_op jit(solution)/shard_map/ppermute | solution.py:27
  4.4 7.1 %query_key.1 = (bf16[16,6,64,256]{3,2,1,0:T(8,128)(2,1)S(1)}, bf16[16,256,768]{2,1,0:T(8,128)(2,1)S(1)}, f32[4,3,32,256]{3,2,1,0:T(8,128)S(1)}, bf16[4,3,32,256]{3,2,1,0:T(8,128)(2,1)S(1)}, bf16[192,1152]{1,0:T(8,128)(2,1)S(1)}) custom-call(s32[18]{0:T(128)S(1)} %pad_add_fusion.refs_0_, bf16[16,256,768]{2,1,0:T(8,128)(2,1)} %refs_1_.1, ...), custom_call_target="tpu_custom_call" | custom-call | flops 2818572288 | bytes 17448996 | tf_op jit(solution)/shard_map/query_key/pallas_call | solution.py:56
  11.5 1.6 %collective-permute-start = (bf16[4,3,32,256]{3,2,1,0:T(8,128)(2,1)S(1)}, bf16[4,3,32,256]{3,2,1,0:T(8,128)(2,1)S(1)}, u32[]{:S(2)}, u32[]{:S(2)}) collective-permute-start(bf16[4,3,32,256]{3,2,1,0:T(8,128)(2,1)S(1)} %get-tuple-element.34.refs_4_), channel_id=1, source_target_pairs={{0,8},{4,12},{8,0},{12,4},{16,24},{20,28},{24,16},{28,20},{1,9},{5... | collective-permute-start | bytes 589832 | tf_op jit(solution)/shard_map/ppermute | solution.py:27
  13.7 3.5 %value_dprob.1 = (f32[4,3,32,256]{3,2,1,0:T(8,128)S(1)}, bf16[4,3,32,256]{3,2,1,0:T(8,128)(2,1)S(1)}) custom-call(s32[18]{0:T(128)S(1)} %pad_add_fusion.refs_0_, bf16[16,256,768]{2,1,0:T(8,128)(2,1)S(1)} %get-tuple-element.35.refs_1_, bf16[192,768]{1,0:T(8,128)(2,1)S(1)} %bitcast.17, bf16[16,192,256]{2,1,0:T(8,128)(2,1)S(1)} %bitcast.8, ...), custom_call_target="tpu_custom_call" | custom-call | flops 12884901888 | bytes 8552484 | tf_op jit(solution)/shard_map/value_dprob/pallas_call | solution.py:56
  20.5 2.6 %collective-permute-start.2 = (bf16[2,3,32,256]{3,2,1,0:T(8,128)(2,1)S(1)}, bf16[2,3,32,256]{3,2,1,0:T(8,128)(2,1)S(1)}, u32[]{:S(2)}, u32[]{:S(2)}) collective-permute-start(bf16[2,3,32,256]{3,2,1,0:T(8,128)(2,1)S(1)} %get-tuple-element.38.refs_1_), channel_id=1, source_target_pairs={{0,16},{4,20},{8,24},{12,28},{16,0},{20,4},{24,8},{28,12},{1,17},{... | collective-permute-start | bytes 294920 | tf_op jit(solution)/shard_map/ppermute | solution.py:27
  23.1 3.2 %collective-permute-done.5.refs_2_.refs_5_.refs_3_ = bf16[192,1152]{1,0:T(8,128)(2,1)S(1)} collective-permute-done((bf16[192,1152]{1,0:T(8,128)(2,1)S(1)}, bf16[192,1152]{1,0:T(8,128)(2,1)S(1)}, u32[]{:S(2)}, u32[]{:S(2)}) %collective-permute-start.5) | collective-permute-done | bytes 442400 | tf_op jit(solution)/shard_map/ppermute | solution.py:27
  28.4 3.1 %collective-permute-done.6.refs_1_ = bf16[2,3,32,256]{3,2,1,0:T(8,128)(2,1)S(1)} collective-permute-done((bf16[2,3,32,256]{3,2,1,0:T(8,128)(2,1)S(1)}, bf16[2,3,32,256]{3,2,1,0:T(8,128)(2,1)S(1)}, u32[]{:S(2)}, u32[]{:S(2)}) %collective-permute-start.6) | collective-permute-done | bytes 98336 | tf_op jit(solution)/shard_map/ppermute | solution.py:27
  31.6 2.1 %collective-permute-start.7 = (bf16[1,3,32,256]{3,2,1,0:T(8,128)(2,1)S(1)}, bf16[1,3,32,256]{3,2,1,0:T(8,128)(2,1)S(1)}, u32[]{:S(2)}, u32[]{:S(2)}) collective-permute-start(bf16[1,3,32,256]{3,2,1,0:T(8,128)(2,1)S(1)} %get-tuple-element.46), channel_id=1, source_target_pairs={{0,16},{4,20},{8,24},{12,28},{16,0},{20,4},{24,8},{28,12},{1,17},{... | collective-permute-start | bytes 147464 | tf_op jit(solution)/shard_map/ppermute | solution.py:27
  34.8 2.3 %collective-permute-done.7.refs_3_ = bf16[1,3,32,256]{3,2,1,0:T(8,128)(2,1)S(1)} collective-permute-done((bf16[1,3,32,256]{3,2,1,0:T(8,128)(2,1)S(1)}, bf16[1,3,32,256]{3,2,1,0:T(8,128)(2,1)S(1)}, u32[]{:S(2)}, u32[]{:S(2)}) %collective-permute-start.7) | collective-permute-done | bytes 49184 | tf_op jit(solution)/shard_map/ppermute | solution.py:27
  37.3 1.7 %collective-permute-start.8 = (bf16[1,3,32,256]{3,2,1,0:T(8,128)(2,1)S(1)}, bf16[1,3,32,256]{3,2,1,0:T(8,128)(2,1)S(1)}, u32[]{:S(2)}, u32[]{:S(2)}) collective-permute-start(bf16[1,3,32,256]{3,2,1,0:T(8,128)(2,1)S(1)} %get-tuple-element.47.refs_0_), channel_id=1, source_target_pairs={{0,16},{4,20},{8,24},{12,28},{16,0},{20,4},{24,8},{28,12},{1,17},{... | collective-permute-start | bytes 147464 | tf_op jit(solution)/shard_map/ppermute | solution.py:27
  40.5 3.9 %collective-permute-done.8.refs_1_ = bf16[1,3,32,256]{3,2,1,0:T(8,128)(2,1)S(1)} collective-permute-done((bf16[1,3,32,256]{3,2,1,0:T(8,128)(2,1)S(1)}, bf16[1,3,32,256]{3,2,1,0:T(8,128)(2,1)S(1)}, u32[]{:S(2)}, u32[]{:S(2)}) %collective-permute-start.8) | collective-permute-done | bytes 49184 | tf_op jit(solution)/shard_map/ppermute | solution.py:27
  44.5 3.2 %collective-permute-start.12 = (bf16[2,3,32,256]{3,2,1,0:T(8,128)(2,1)S(1)}, bf16[2,3,32,256]{3,2,1,0:T(8,128)(2,1)S(1)}, u32[]{:S(2)}, u32[]{:S(2)}) collective-permute-start(bf16[2,3,32,256]{3,2,1,0:T(8,128)(2,1)S(1)} %join.6.refs_0_), channel_id=1, source_target_pairs={{0,16},{4,20},{8,24},{12,28},{16,0},{20,4},{24,8},{28,12},{1,17},{... | collective-permute-start | bytes 294920 | tf_op jit(solution)/shard_map/ppermute | solution.py:27
  47.7 3.5 %collective-permute-done.9.refs_1_ = bf16[2,3,32,256]{3,2,1,0:T(8,128)(2,1)S(1)} collective-permute-done((bf16[2,3,32,256]{3,2,1,0:T(8,128)(2,1)S(1)}, bf16[2,3,32,256]{3,2,1,0:T(8,128)(2,1)S(1)}, u32[]{:S(2)}, u32[]{:S(2)}) %collective-permute-start.9) | collective-permute-done | bytes 98336 | tf_op jit(solution)/shard_map/ppermute | solution.py:27
  51.2 1.7 %collective-permute-start.10 = (bf16[4,3,32,256]{3,2,1,0:T(8,128)(2,1)S(1)}, bf16[4,3,32,256]{3,2,1,0:T(8,128)(2,1)S(1)}, u32[]{:S(2)}, u32[]{:S(2)}) collective-permute-start(bf16[4,3,32,256]{3,2,1,0:T(8,128)(2,1)S(1)} %join.5.refs_1_), channel_id=1, source_target_pairs={{0,4},{4,0},{8,12},{12,8},{16,20},{20,16},{24,28},{28,24},{1,5},{5... | collective-permute-start | bytes 589832 | tf_op jit(solution)/shard_map/ppermute | solution.py:27
  53.0 3.9 %collective-permute-done.10.refs_2_ = bf16[4,3,32,256]{3,2,1,0:T(8,128)(2,1)S(1)} collective-permute-done((bf16[4,3,32,256]{3,2,1,0:T(8,128)(2,1)S(1)}, bf16[4,3,32,256]{3,2,1,0:T(8,128)(2,1)S(1)}, u32[]{:S(2)}, u32[]{:S(2)}) %collective-permute-start.10) | collective-permute-done | bytes 196640 | tf_op jit(solution)/shard_map/ppermute | solution.py:27
  56.9 1.8 %collective-permute-done.13.refs_4_ = bf16[4,3,32,256]{3,2,1,0:T(8,128)(2,1)S(1)} collective-permute-done((bf16[4,3,32,256]{3,2,1,0:T(8,128)(2,1)S(1)}, bf16[4,3,32,256]{3,2,1,0:T(8,128)(2,1)S(1)}, u32[]{:S(2)}, u32[]{:S(2)}) %collective-permute-start.13) | collective-permute-done | bytes 196640 | tf_op jit(solution)/shard_map/ppermute | solution.py:27
  59.3 1.9 %own_gradients.1.refs_2_.refs_0_ = bf16[16,9,64,256]{3,2,1,0:T(8,128)(2,1)S(1)} custom-call(s32[18]{0:T(128)S(1)} %pad_add_fusion.refs_0_, bf16[2,8,3,32,256]{4,3,2,1,0:T(8,128)(2,1)S(1)} %assemble.1.refs_1_, bf16[16,6,64,256]{3,2,1,0:T(8,128)(2,1)S(1)} %get-tuple-element.49.refs_2_, bf16[16,192,256]{2,1,0:T(8,128)(2,1)S(1)} %bitcast.10), custom_call_target="tpu_custom_call" | custom-call | flops 1207959552 | bytes 10223652 | tf_op jit(solution)/shard_map/own_gradients/pallas_call | solution.py:56
  61.3 4.7 %weight_part.1 = (f32[4,96,576]{2,1,0:T(8,128)S(1)}, bf16[4,96,576]{2,1,0:T(8,128)(2,1)S(1)}) custom-call(s32[18]{0:T(128)S(1)} %pad_add_fusion.refs_0_, bf16[16,256,768]{2,1,0:T(8,128)(2,1)S(1)} %get-tuple-element.35.refs_1_, bf16[16,9,64,256]{3,2,1,0:T(8,128)(2,1)S(1)} %own_gradients.1.refs_2_.refs_0_), custom_call_target="tpu_custom_call" | custom-call | flops 3623878656 | bytes 11894820 | tf_op jit(solution)/shard_map/weight_part/pallas_call | solution.py:56
  67.8 2.8 %own_input.1.refs_2_.refs_0_ = bf16[2,16,192,256]{3,2,1,0:T(8,128)(2,1)S(1)} custom-call(bf16[16,9,64,256]{3,2,1,0:T(8,128)(2,1)S(1)} %own_gradients.1.refs_2_.refs_0_, bf16[2,192,576]{2,1,0:T(8,128)(2,1)S(1)} %turn.2.refs_4_.refs_1_, bf16[4,96,576]{2,1,0:T(8,128)(2,1)S(1)} %get-tuple-element.50.refs_2_.refs_4_.refs_3_), custom_call_target="tpu_custom_call" | custom-call | flops 1811939328 | bytes 8306688 | tf_op jit(solution)/shard_map/own_input/pallas_call | solution.py:56
  70.7 3.2 %far_query_key.1.refs_3_.refs_2_ = bf16[16,6,64,256]{3,2,1,0:T(8,128)(2,1)S(1)} custom-call(s32[18]{0:T(128)S(1)} %pad_add_fusion.refs_0_, bf16[16,256,768]{2,1,0:T(8,128)(2,1)S(1)} %get-tuple-element.35.refs_1_, bf16[192,768]{1,0:T(8,128)(2,1)S(1)} %collective-permute-done.1.refs_5_.refs_2_.refs_1_, ...), custom_call_target="tpu_custom_call" | custom-call | flops 2415919104 | bytes 10174500 | tf_op jit(solution)/shard_map/far_query_key/pallas_call | solution.py:56
  75.7 1.9 %far_gradients.1.refs_1_ = bf16[16,9,64,256]{3,2,1,0:T(8,128)(2,1)S(1)} custom-call(s32[18]{0:T(128)S(1)} %pad_add_fusion.refs_0_, bf16[2,8,3,32,256]{4,3,2,1,0:T(8,128)(2,1)S(1)} %collective-permute-done.14.refs_5_.refs_1_, bf16[16,6,64,256]{3,2,1,0:T(8,128)(2,1)S(1)} %far_query_key.1.refs_3_.refs_2_, ...), custom_call_target="tpu_custom_call" | custom-call | flops 1207959552 | bytes 10223652 | tf_op jit(solution)/shard_map/far_gradients/pallas_call | solution.py:56
  79.8 1.6 %collective-permute-done.19.refs_1_ = bf16[2,96,576]{2,1,0:T(8,128)(2,1)S(1)} collective-permute-done((bf16[2,96,576]{2,1,0:T(8,128)(2,1)S(1)}, bf16[2,96,576]{2,1,0:T(8,128)(2,1)S(1)}, u32[]{:S(2)}, u32[]{:S(2)}) %collective-permute-start.19) | collective-permute-done | bytes 221216 | tf_op jit(solution)/shard_map/ppermute | solution.py:27
  83.6 2.6 %collective-permute-start.22 = (bf16[1,96,576]{2,1,0:T(8,128)(2,1)S(1)}, bf16[1,96,576]{2,1,0:T(8,128)(2,1)S(1)}, u32[]{:S(2)}, u32[]{:S(2)}) collective-permute-start(bf16[1,96,576]{2,1,0:T(8,128)(2,1)S(1)} %get-tuple-element.63), channel_id=1, source_target_pairs={{0,16},{4,20},{8,24},{12,28},{16,0},{20,4},{24,8},{28,12},{1,17},{... | collective-permute-start | bytes 331784 | tf_op jit(solution)/shard_map/ppermute | solution.py:27
  87.5 4.8 %collective-permute-done.22.refs_2_ = bf16[1,96,576]{2,1,0:T(8,128)(2,1)S(1)} collective-permute-done((bf16[1,96,576]{2,1,0:T(8,128)(2,1)S(1)}, bf16[1,96,576]{2,1,0:T(8,128)(2,1)S(1)}, u32[]{:S(2)}, u32[]{:S(2)}) %collective-permute-start.22) | collective-permute-done | bytes 110624 | tf_op jit(solution)/shard_map/ppermute | solution.py:27
  (59 shorter events, 20.4 us)
Async XLA Ops:
  0.6 13.0 %collective-permute-start.1 = (bf16[192,768]{1,0:T(8,128)(2,1)}, bf16[192,768]{1,0:T(8,128)(2,1)S(1)}, u32[]{:S(2)}, u32[]{:S(2)}) collective-permute-start(bf16[192,768]{1,0:T(8,128)(2,1)} %bitcast.11), channel_id=1, source_target_pairs={{0,2},{1,3},{2,0},{3,1},{4,6},{5,7},{6,4},{7,5},{8,10},{9,11},{10,... | collective-permute-start | bytes 884744 | tf_op jit(solution)/shard_map/ppermute | solution.py:27
  11.5 6.4 %collective-permute-start = (bf16[4,3,32,256]{3,2,1,0:T(8,128)(2,1)S(1)}, bf16[4,3,32,256]{3,2,1,0:T(8,128)(2,1)S(1)}, u32[]{:S(2)}, u32[]{:S(2)}) collective-permute-start(bf16[4,3,32,256]{3,2,1,0:T(8,128)(2,1)S(1)} %get-tuple-element.34.refs_4_), channel_id=1, source_target_pairs={{0,8},{4,12},{8,0},{12,4},{16,24},{20,28},{24,16},{28,20},{1,9},{5... | collective-permute-start | bytes 589832 | tf_op jit(solution)/shard_map/ppermute | solution.py:27
  13.2 13.1 %collective-permute-start.5 = (bf16[192,1152]{1,0:T(8,128)(2,1)S(1)}, bf16[192,1152]{1,0:T(8,128)(2,1)S(1)}, u32[]{:S(2)}, u32[]{:S(2)}) collective-permute-start(bf16[192,1152]{1,0:T(8,128)(2,1)S(1)} %get-tuple-element.42), channel_id=1, source_target_pairs={{0,2},{1,3},{2,0},{3,1},{4,6},{5,7},{6,4},{7,5},{8,10},{9,11},{10,... | collective-permute-start | bytes 1327112 | tf_op jit(solution)/shard_map/ppermute | solution.py:27
  17.2 16.5 %copy-start.1 = (bf16[768,192]{0,1:T(8,128)(2,1)S(1)}, bf16[768,192]{0,1:T(8,128)(2,1)}, u32[]{:S(2)}) copy-start(bf16[768,192]{0,1:T(8,128)(2,1)} %param.7) | copy-start | bytes 884740
  18.1 52.5 %collective-permute-start.15 = (bf16[16,192,256]{2,1,0:T(8,128)(2,1)S(1)}, bf16[16,192,256]{2,1,0:T(8,128)(2,1)S(1)}, u32[]{:S(2)}, u32[]{:S(2)}) collective-permute-start(bf16[16,192,256]{2,1,0:T(8,128)(2,1)S(1)} %hold.1), channel_id=1, source_target_pairs={{0,2},{1,3},{2,0},{3,1},{4,6},{5,7},{6,4},{7,5},{8,10},{9,11},{10,... | collective-permute-start | bytes 4718600 | tf_op jit(solution)/shard_map/ppermute | solution.py:27
  19.0 7.3 %collective-permute-start.4 = (bf16[4,3,32,256]{3,2,1,0:T(8,128)(2,1)S(1)}, bf16[4,3,32,256]{3,2,1,0:T(8,128)(2,1)S(1)}, u32[]{:S(2)}, u32[]{:S(2)}) collective-permute-start(bf16[4,3,32,256]{3,2,1,0:T(8,128)(2,1)S(1)} %get-tuple-element.36.refs_2_.refs_4_), channel_id=1, source_target_pairs={{0,4},{4,0},{8,12},{12,8},{16,20},{20,16},{24,28},{28,24},{1,5},{5... | collective-permute-start | bytes 589832 | tf_op jit(solution)/shard_map/ppermute | solution.py:27
  20.5 6.6 %collective-permute-start.2 = (bf16[2,3,32,256]{3,2,1,0:T(8,128)(2,1)S(1)}, bf16[2,3,32,256]{3,2,1,0:T(8,128)(2,1)S(1)}, u32[]{:S(2)}, u32[]{:S(2)}) collective-permute-start(bf16[2,3,32,256]{3,2,1,0:T(8,128)(2,1)S(1)} %get-tuple-element.38.refs_1_), channel_id=1, source_target_pairs={{0,16},{4,20},{8,24},{12,28},{16,0},{20,4},{24,8},{28,12},{1,17},{... | collective-permute-start | bytes 294920 | tf_op jit(solution)/shard_map/ppermute | solution.py:27
  26.3 5.2 %collective-permute-start.6 = (bf16[2,3,32,256]{3,2,1,0:T(8,128)(2,1)S(1)}, bf16[2,3,32,256]{3,2,1,0:T(8,128)(2,1)S(1)}, u32[]{:S(2)}, u32[]{:S(2)}) collective-permute-start(bf16[2,3,32,256]{3,2,1,0:T(8,128)(2,1)S(1)} %get-tuple-element.44), channel_id=1, source_target_pairs={{0,8},{4,12},{8,0},{12,4},{16,24},{20,28},{24,16},{28,20},{1,9},{5... | collective-permute-start | bytes 294920 | tf_op jit(solution)/shard_map/ppermute | solution.py:27
  27.1 7.7 %collective-permute-start.3 = (bf16[1,3,32,256]{3,2,1,0:T(8,128)(2,1)S(1)}, bf16[1,3,32,256]{3,2,1,0:T(8,128)(2,1)S(1)}, u32[]{:S(2)}, u32[]{:S(2)}) collective-permute-start(bf16[1,3,32,256]{3,2,1,0:T(8,128)(2,1)S(1)} %get-tuple-element.40), channel_id=1, source_target_pairs={{0,4},{4,0},{8,12},{12,8},{16,20},{20,16},{24,28},{28,24},{1,5},{5... | collective-permute-start | bytes 147464 | tf_op jit(solution)/shard_map/ppermute | solution.py:27
  31.6 5.5 %collective-permute-start.7 = (bf16[1,3,32,256]{3,2,1,0:T(8,128)(2,1)S(1)}, bf16[1,3,32,256]{3,2,1,0:T(8,128)(2,1)S(1)}, u32[]{:S(2)}, u32[]{:S(2)}) collective-permute-start(bf16[1,3,32,256]{3,2,1,0:T(8,128)(2,1)S(1)} %get-tuple-element.46), channel_id=1, source_target_pairs={{0,16},{4,20},{8,24},{12,28},{16,0},{20,4},{24,8},{28,12},{1,17},{... | collective-permute-start | bytes 147464 | tf_op jit(solution)/shard_map/ppermute | solution.py:27
  37.3 7.1 %collective-permute-start.8 = (bf16[1,3,32,256]{3,2,1,0:T(8,128)(2,1)S(1)}, bf16[1,3,32,256]{3,2,1,0:T(8,128)(2,1)S(1)}, u32[]{:S(2)}, u32[]{:S(2)}) collective-permute-start(bf16[1,3,32,256]{3,2,1,0:T(8,128)(2,1)S(1)} %get-tuple-element.47.refs_0_), channel_id=1, source_target_pairs={{0,16},{4,20},{8,24},{12,28},{16,0},{20,4},{24,8},{28,12},{1,17},{... | collective-permute-start | bytes 147464 | tf_op jit(solution)/shard_map/ppermute | solution.py:27
  39.0 5.4 %collective-permute-start.11 = (bf16[1,3,32,256]{3,2,1,0:T(8,128)(2,1)S(1)}, bf16[1,3,32,256]{3,2,1,0:T(8,128)(2,1)S(1)}, u32[]{:S(2)}, u32[]{:S(2)}) collective-permute-start(bf16[1,3,32,256]{3,2,1,0:T(8,128)(2,1)S(1)} %get-tuple-element.48.refs_0_), channel_id=1, source_target_pairs={{0,4},{4,0},{8,12},{12,8},{16,20},{20,16},{24,28},{28,24},{1,5},{5... | collective-permute-start | bytes 147464 | tf_op jit(solution)/shard_map/ppermute | solution.py:27
  44.4 6.8 %collective-permute-start.9 = (bf16[2,3,32,256]{3,2,1,0:T(8,128)(2,1)S(1)}, bf16[2,3,32,256]{3,2,1,0:T(8,128)(2,1)S(1)}, u32[]{:S(2)}, u32[]{:S(2)}) collective-permute-start(bf16[2,3,32,256]{3,2,1,0:T(8,128)(2,1)S(1)} %join.4.refs_0_), channel_id=1, source_target_pairs={{0,8},{4,12},{8,0},{12,4},{16,24},{20,28},{24,16},{28,20},{1,9},{5... | collective-permute-start | bytes 294920 | tf_op jit(solution)/shard_map/ppermute | solution.py:27
  44.5 8.4 %collective-permute-start.12 = (bf16[2,3,32,256]{3,2,1,0:T(8,128)(2,1)S(1)}, bf16[2,3,32,256]{3,2,1,0:T(8,128)(2,1)S(1)}, u32[]{:S(2)}, u32[]{:S(2)}) collective-permute-start(bf16[2,3,32,256]{3,2,1,0:T(8,128)(2,1)S(1)} %join.6.refs_0_), channel_id=1, source_target_pairs={{0,16},{4,20},{8,24},{12,28},{16,0},{20,4},{24,8},{28,12},{1,17},{... | collective-permute-start | bytes 294920 | tf_op jit(solution)/shard_map/ppermute | solution.py:27
  51.2 5.7 %collective-permute-start.10 = (bf16[4,3,32,256]{3,2,1,0:T(8,128)(2,1)S(1)}, bf16[4,3,32,256]{3,2,1,0:T(8,128)(2,1)S(1)}, u32[]{:S(2)}, u32[]{:S(2)}) collective-permute-start(bf16[4,3,32,256]{3,2,1,0:T(8,128)(2,1)S(1)} %join.5.refs_1_), channel_id=1, source_target_pairs={{0,4},{4,0},{8,12},{12,8},{16,20},{20,16},{24,28},{28,24},{1,5},{5... | collective-permute-start | bytes 589832 | tf_op jit(solution)/shard_map/ppermute | solution.py:27
  52.9 5.7 %collective-permute-start.13 = (bf16[4,3,32,256]{3,2,1,0:T(8,128)(2,1)S(1)}, bf16[4,3,32,256]{3,2,1,0:T(8,128)(2,1)S(1)}, u32[]{:S(2)}, u32[]{:S(2)}) collective-permute-start(bf16[4,3,32,256]{3,2,1,0:T(8,128)(2,1)S(1)} %join.7.refs_3_), channel_id=1, source_target_pairs={{0,8},{4,12},{8,0},{12,4},{16,24},{20,28},{24,16},{28,20},{1,9},{5... | collective-permute-start | bytes 589832 | tf_op jit(solution)/shard_map/ppermute | solution.py:27
  59.3 15.8 %collective-permute-start.14 = (bf16[2,8,3,32,256]{4,3,2,1,0:T(8,128)(2,1)S(1)}, bf16[2,8,3,32,256]{4,3,2,1,0:T(8,128)(2,1)S(1)}, u32[]{:S(2)}, u32[]{:S(2)}) collective-permute-start(bf16[2,8,3,32,256]{4,3,2,1,0:T(8,128)(2,1)S(1)} %assemble.1.refs_1_), channel_id=1, source_target_pairs={{0,2},{1,3},{2,0},{3,1},{4,6},{5,7},{6,4},{7,5},{8,10},{9,11},{10,... | collective-permute-start | bytes 2359304 | tf_op jit(solution)/shard_map/ppermute | solution.py:27
  66.0 8.9 %collective-permute-start.16 = (bf16[4,96,576]{2,1,0:T(8,128)(2,1)S(1)}, bf16[4,96,576]{2,1,0:T(8,128)(2,1)S(1)}, u32[]{:S(2)}, u32[]{:S(2)}) collective-permute-start(bf16[4,96,576]{2,1,0:T(8,128)(2,1)S(1)} %get-tuple-element.50.refs_2_.refs_4_.refs_3_), channel_id=1, source_target_pairs={{0,4},{4,0},{8,12},{12,8},{16,20},{20,16},{24,28},{28,24},{1,5},{5... | collective-permute-start | bytes 1327112 | tf_op jit(solution)/shard_map/ppermute | solution.py:27
  75.2 6.3 %collective-permute-start.19 = (bf16[2,96,576]{2,1,0:T(8,128)(2,1)S(1)}, bf16[2,96,576]{2,1,0:T(8,128)(2,1)S(1)}, u32[]{:S(2)}, u32[]{:S(2)}) collective-permute-start(bf16[2,96,576]{2,1,0:T(8,128)(2,1)S(1)} %get-tuple-element.57), channel_id=1, source_target_pairs={{0,8},{4,12},{8,0},{12,4},{16,24},{20,28},{24,16},{28,20},{1,9},{5... | collective-permute-start | bytes 663560 | tf_op jit(solution)/shard_map/ppermute | solution.py:27
  78.4 7.8 %collective-permute-start.17 = (bf16[4,192,256]{2,1,0:T(8,128)(2,1)S(1)}, bf16[4,192,256]{2,1,0:T(8,128)(2,1)S(1)}, u32[]{:S(2)}, u32[]{:S(2)}) collective-permute-start(bf16[4,192,256]{2,1,0:T(8,128)(2,1)S(1)} %get-tuple-element.54), channel_id=1, source_target_pairs={{0,1},{1,0},{2,3},{3,2},{4,5},{5,4},{6,7},{7,6},{8,9},{9,8},{10,11... | collective-permute-start | bytes 1179656 | tf_op jit(solution)/shard_map/ppermute | solution.py:27
  79.3 6.9 %collective-permute-start.18 = (bf16[4,192,256]{2,1,0:T(8,128)(2,1)S(1)}, bf16[4,192,256]{2,1,0:T(8,128)(2,1)S(1)}, u32[]{:S(2)}, u32[]{:S(2)}) collective-permute-start(bf16[4,192,256]{2,1,0:T(8,128)(2,1)S(1)} %get-tuple-element.56), channel_id=1, source_target_pairs={{0,1},{1,0},{2,3},{3,2},{4,5},{5,4},{6,7},{7,6},{8,9},{9,8},{10,11... | collective-permute-start | bytes 1179656 | tf_op jit(solution)/shard_map/ppermute | solution.py:27
  83.0 3.2 %collective-permute-start.20 = (bf16[4,192,256]{2,1,0:T(8,128)(2,1)S(1)}, bf16[4,192,256]{2,1,0:T(8,128)(2,1)S(1)}, u32[]{:S(2)}, u32[]{:S(2)}) collective-permute-start(bf16[4,192,256]{2,1,0:T(8,128)(2,1)S(1)} %get-tuple-element.60), channel_id=1, source_target_pairs={{0,1},{1,0},{2,3},{3,2},{4,5},{5,4},{6,7},{7,6},{8,9},{9,8},{10,11... | collective-permute-start | bytes 1179656 | tf_op jit(solution)/shard_map/ppermute | solution.py:27
  83.1 3.1 %collective-permute-start.21 = (bf16[4,192,256]{2,1,0:T(8,128)(2,1)S(1)}, bf16[4,192,256]{2,1,0:T(8,128)(2,1)S(1)}, u32[]{:S(2)}, u32[]{:S(2)}) collective-permute-start(bf16[4,192,256]{2,1,0:T(8,128)(2,1)S(1)} %get-tuple-element.62), channel_id=1, source_target_pairs={{0,1},{1,0},{2,3},{3,2},{4,5},{5,4},{6,7},{7,6},{8,9},{9,8},{10,11... | collective-permute-start | bytes 1179656 | tf_op jit(solution)/shard_map/ppermute | solution.py:27
  83.6 8.7 %collective-permute-start.22 = (bf16[1,96,576]{2,1,0:T(8,128)(2,1)S(1)}, bf16[1,96,576]{2,1,0:T(8,128)(2,1)S(1)}, u32[]{:S(2)}, u32[]{:S(2)}) collective-permute-start(bf16[1,96,576]{2,1,0:T(8,128)(2,1)S(1)} %get-tuple-element.63), channel_id=1, source_target_pairs={{0,16},{4,20},{8,24},{12,28},{16,0},{20,4},{24,8},{28,12},{1,17},{... | collective-permute-start | bytes 331784 | tf_op jit(solution)/shard_map/ppermute | solution.py:27
  (3 other events, 35.0 us)

commit v16 on v15

--- a/solution.py
+++ b/solution.py
@@ -81,11 +81,11 @@
 
 BLOCK = 4
 STEP = 2
-AHEAD = 4
-
-
-def query_key_kernel(bits, fars, where, sheet, wq, wk, wv, qk, held, *rest):
-    outs, staged, (wt, acc, sems) = rest[: -3 - len(fars)], rest[-3 - len(fars) : -3], rest[-3:]
+AHEAD = 6
+
+
+def query_key_kernel(bits, fars, me, lengths, sheet, wq, wk, wv, qk, held, seen, *rest):
+    outs, staged, (wt, acc, number, sems) = rest[: -4 - len(fars)], rest[-4 - len(fars) : -4], rest[-4:]
     rows, cols, width = sheet.shape
     local = wq.shape[0]
     heads = local // HEAD_DIM
@@ -94,6 +94,8 @@
     def copy(source, target):
         copies.append(pltpu.make_async_copy(source, target, sems.at[len(copies)]))
 
+    copy(lengths, number)
+    copy(lengths, seen)
     copy(wq, wt.at[:local])
     copy(wk, wt.at[local:])
     for first in range(0, rows, STEP):
@@ -101,37 +103,37 @@
         copy(sheet.at[some], held.at[some])
     for far, out in zip(fars, staged):
         near = out.shape[1] - width
-        side = lax.shift_right_logical(where[1], 1) ^ (far // 2)
+        side = lax.shift_right_logical(me[1], 1) ^ (far // 2)
         some = pl.ds(pl.multiple_of(side * near, 128), near)
         copy(wk, out.at[:, pl.ds(0, width)])
         copy(wv.at[:, some], out.at[:, pl.ds(width, near)])
     for one in copies[:AHEAD]:
         one.start()
-    copies[0].wait()
-    copies[1].wait()
+    for one in copies[:4]:
+        one.wait()
     flat = (BLOCK * HEAD_DIM, cols)
     for first in range(0, rows, BLOCK):
         for r in range(first, first + BLOCK):
             if r % STEP == 0:
-                at = 2 + r // STEP
+                at = 4 + r // STEP
                 copies[at].wait()
-                last = at + AHEAD - 1 if r + STEP < rows else len(copies)
-                for later in copies[at + AHEAD - 2 : last]:
+                last = at + AHEAD - 3 if r + STEP < rows else len(copies)
+                for later in copies[at + AHEAD - 4 : last]:
                     later.start()
-            value = (mm(wt[...], held[r], NT) * lane_mask(where[2 + r], cols)).astype(BF16)
+            value = (mm(wt[...], held[r], NT) * lane_mask(number[0, r], cols)).astype(BF16)
             qk[r] = value.reshape(2 * heads, HEAD_DIM, cols)
         some = pl.ds(first, BLOCK)
         for h in range(heads):
             term = mm(qk[some, h].reshape(flat), qk[some, heads + h].reshape(flat), TN)
             term = term.reshape(acc.shape[1:])
             acc[h] = term if first == 0 else acc[h] + term
-    put_shards(where[0], acc, bits, outs)
-    started = 2 + rows // STEP
+    put_shards(me[0], acc, bits, outs)
+    started = 4 + rows // STEP
     for one in copies[started:]:
         one.wait()
 
 
-def query_key(where, sheet, wq, wk, wv, bits, fars, devices):
+def query_key(me, lengths, sheet, wq, wk, wv, bits, fars, devices):
     rows, cols, width = sheet.shape
     shards = 1 << len(bits)
     local = wq.shape[0]
@@ -139,20 +141,22 @@
     return in_vmem(
         functools.partial(query_key_kernel, bits, fars),
         "query_key",
-        [like((rows, 2 * heads, HEAD_DIM, cols)), like(sheet.shape)]
+        [like((rows, 2 * heads, HEAD_DIM, cols)), like(sheet.shape), like(lengths.shape, jnp.int32)]
         + part_shapes(shards, heads, cols)
         + [like((local, width + 2 * width // devices))] * len(fars),
-        where,
+        me,
+        lengths,
         sheet,
         wq,
         wk,
         wv,
         scalars=1,
-        streamed=4,
+        streamed=5,
         scratch=(
             pltpu.VMEM((2 * local, width), BF16),
             pltpu.VMEM((heads, shards, cols // shards, cols), F32),
-            pltpu.SemaphoreType.DMA((2 + rows // STEP + 2 * len(fars),)),
+            pltpu.SMEM(lengths.shape, jnp.int32),
+            pltpu.SemaphoreType.DMA((4 + rows // STEP + 2 * len(fars),)),
         ),
         limit=14,
         flops=2 * rows * cols * local * (2 * width + cols),
@@ -542,10 +546,9 @@
     direct = n_rows <= 8
     shards = n_rows if direct else 1
     row_bits = [1 << b for b in range(n_rows.bit_length() - 1)]
-    chunk = row_dev // 4
+    chunk = row_dev // 2
 
     me = jnp.stack([lax.axis_index("rows"), lax.axis_index("heads")]).astype(jnp.int32)
-    where = jnp.concatenate([me, lengths])
     wq, wk, wv = w_query.T, w_key.T, w_value.T
     cot = jnp.swapaxes(cotangent, 1, 2)
 
@@ -553,7 +556,9 @@
     far_wq = [flip(wq, "heads", f) for f in fars]
     up = row_bits if direct else []
     turn_about = up[1:] + up[:1]
-    qk, held, *logits = query_key(where, sheet, wq, wk, wv, turn_about, fars, n_heads)
+    parts = query_key(me, lengths.reshape(1, row_dev), sheet, wq, wk, wv, turn_about, fars, n_heads)
+    qk, held, seen, *logits = parts
+    where = jnp.concatenate([me, seen.reshape(row_dev)])
     logits, staged = logits[: -len(fars)], logits[-len(fars) :]
     far_staged = [flip(a, "heads", f) for a, f in zip(staged, fars)]
     dprob = value_dprob(where, held, wv, cot, logits[-1:] + far_wq, up)
@@ -599,7 +604,7 @@
     ]
     chunks = []
     for index, first in enumerate(range(0, row_dev, chunk)):
-        after = steps[-1] if index >= 2 else ()
+        after = steps[-1] if index else ()
         keep, give = far_input(first, chunk, own, list(zip(far_grads, far_natural)), after)
         chunks.append((keep, flip(give, "heads", 1)))
     out = finish(chunks)

time: 93.4 us -> 92.6 us (level)
    ppermute x23 -> x21, starting transfers between devices: 27.5 us -> 26.8 us  [flip(): return lax.ppermute(values, axis, [(s, s ^ bit) for s in range(n)])]
    ppermute x23 -> x21, waiting for transfers between devices: 30.2 us -> 30.9 us  [flip(): return lax.ppermute(values, axis, [(s, s ^ bit) for s in range(n)])]
    pallas_call x27 -> x25, Pallas kernels: 32.5 us -> 32.3 us  [in_vmem(): pl.pallas_call(run, in_specs=[SMEM] * scalars + [HBM] * streamed + [VMEM]...]
  transfers between devices with their start and end apart: 23 -> 21, of which waited for: 13 -> 13; matrix products, arithmetic and copies ran while one was open for 1% -> 0% of each run, Pallas kernels for 35% -> 35%
where the time goes in v16:
time: 92.6 us; the launch traced here: 92.3 us
  Pallas kernels  33.6 us (36%)
  waiting for transfers between devices  30.9 us (33%)
  starting transfers between devices  26.8 us (29%)
    pallas_call x25, Pallas kernels, in_vmem(): pl.pallas_call(run, in_specs=[SMEM] * scalars + [HBM] * streamed + [VMEM]...  32.3 us
    ppermute x21, waiting for transfers between devices, flip(): return lax.ppermute(values, axis, [(s, s ^ bit) for s in range(n)])  30.9 us
    ppermute x21, starting transfers between devices, flip(): return lax.ppermute(values, axis, [(s, s ^ bit) for s in range(n)])  26.8 us
  transfers between devices with their start and end apart: 21, of which 13 were waited for; matrix products, arithmetic and copies ran while one was open for 0% of the time, Pallas kernels for 35%

profile of v16, /device:TPU:0, one launch (start us, length us, event | category | flops | bytes accessed | tf_op | source)
XLA Modules:
  0.0 92.3 jit_solution(15116614885959604163)
XLA Ops:
  0.6 3.0 %collective-permute-start.1 = (bf16[192,768]{1,0:T(8,128)(2,1)}, bf16[192,768]{1,0:T(8,128)(2,1)S(1)}, u32[]{:S(2)}, u32[]{:S(2)}) collective-permute-start(bf16[192,768]{1,0:T(8,128)(2,1)} %bitcast.13), channel_id=1, source_target_pairs={{0,2},{1,3},{2,0},{3,1},{4,6},{5,7},{6,4},{7,5},{8,10},{9,11},{10,... | collective-permute-start | bytes 884744 | tf_op jit(solution)/shard_map/ppermute | solution.py:27
  3.7 7.2 %query_key.1 = (bf16[16,6,64,256]{3,2,1,0:T(8,128)(2,1)S(1)}, bf16[16,256,768]{2,1,0:T(8,128)(2,1)S(1)}, s32[1,16]{1,0:T(1,128)S(1)}, f32[4,3,32,256]{3,2,1,0:T(...) custom-call(s32[2]{0:T(128)S(1)} %pad_add_fusion.refs_0_, s32[1,16]{1,0:T(1,128)} %bitcast.24, ...), custom_call_target="tpu_custom_call" | custom-call | flops 2818572288 | bytes 17449028 | tf_op jit(solution)/shard_map/query_key/pallas_call | solution.py:56
  10.9 1.6 %collective-permute-start = (bf16[4,3,32,256]{3,2,1,0:T(8,128)(2,1)S(1)}, bf16[4,3,32,256]{3,2,1,0:T(8,128)(2,1)S(1)}, u32[]{:S(2)}, u32[]{:S(2)}) collective-permute-start(bf16[4,3,32,256]{3,2,1,0:T(8,128)(2,1)S(1)} %get-tuple-element.32.refs_4_), channel_id=1, source_target_pairs={{0,8},{4,12},{8,0},{12,4},{16,24},{20,28},{24,16},{28,20},{1,9},{5... | collective-permute-start | bytes 589832 | tf_op jit(solution)/shard_map/ppermute | solution.py:27
  13.1 3.5 %value_dprob.1 = (f32[4,3,32,256]{3,2,1,0:T(8,128)S(1)}, bf16[4,3,32,256]{3,2,1,0:T(8,128)(2,1)S(1)}) custom-call(s32[18]{0:T(128)S(1)} %pad_add_fusion.1.refs_0_, bf16[16,256,768]{2,1,0:T(8,128)(2,1)S(1)} %get-tuple-element.33.refs_1_, bf16[192,768]{1,0:T(8,128)(2,1)S(1)} %bitcast.19, bf16[16,192,256]{2,1,0:T(8,128)(2,1)S(1)} %bitcast.10, ...), custom_call_target="tpu_custom_call" | custom-call | flops 12884901888 | bytes 8552484 | tf_op jit(solution)/shard_map/value_dprob/pallas_call | solution.py:56
  19.9 2.6 %collective-permute-start.2 = (bf16[2,3,32,256]{3,2,1,0:T(8,128)(2,1)S(1)}, bf16[2,3,32,256]{3,2,1,0:T(8,128)(2,1)S(1)}, u32[]{:S(2)}, u32[]{:S(2)}) collective-permute-start(bf16[2,3,32,256]{3,2,1,0:T(8,128)(2,1)S(1)} %get-tuple-element.36.refs_1_), channel_id=1, source_target_pairs={{0,16},{4,20},{8,24},{12,28},{16,0},{20,4},{24,8},{28,12},{1,17},{... | collective-permute-start | bytes 294920 | tf_op jit(solution)/shard_map/ppermute | solution.py:27
  22.5 3.1 %collective-permute-done.5.refs_2_.refs_5_.refs_3_ = bf16[192,1152]{1,0:T(8,128)(2,1)S(1)} collective-permute-done((bf16[192,1152]{1,0:T(8,128)(2,1)S(1)}, bf16[192,1152]{1,0:T(8,128)(2,1)S(1)}, u32[]{:S(2)}, u32[]{:S(2)}) %collective-permute-start.5) | collective-permute-done | bytes 442400 | tf_op jit(solution)/shard_map/ppermute | solution.py:27
  27.8 3.1 %collective-permute-done.6.refs_1_ = bf16[2,3,32,256]{3,2,1,0:T(8,128)(2,1)S(1)} collective-permute-done((bf16[2,3,32,256]{3,2,1,0:T(8,128)(2,1)S(1)}, bf16[2,3,32,256]{3,2,1,0:T(8,128)(2,1)S(1)}, u32[]{:S(2)}, u32[]{:S(2)}) %collective-permute-start.6) | collective-permute-done | bytes 98336 | tf_op jit(solution)/shard_map/ppermute | solution.py:27
  30.9 2.1 %collective-permute-start.7 = (bf16[1,3,32,256]{3,2,1,0:T(8,128)(2,1)S(1)}, bf16[1,3,32,256]{3,2,1,0:T(8,128)(2,1)S(1)}, u32[]{:S(2)}, u32[]{:S(2)}) collective-permute-start(bf16[1,3,32,256]{3,2,1,0:T(8,128)(2,1)S(1)} %get-tuple-element.44), channel_id=1, source_target_pairs={{0,16},{4,20},{8,24},{12,28},{16,0},{20,4},{24,8},{28,12},{1,17},{... | collective-permute-start | bytes 147464 | tf_op jit(solution)/shard_map/ppermute | solution.py:27
  34.1 2.3 %collective-permute-done.7.refs_3_ = bf16[1,3,32,256]{3,2,1,0:T(8,128)(2,1)S(1)} collective-permute-done((bf16[1,3,32,256]{3,2,1,0:T(8,128)(2,1)S(1)}, bf16[1,3,32,256]{3,2,1,0:T(8,128)(2,1)S(1)}, u32[]{:S(2)}, u32[]{:S(2)}) %collective-permute-start.7) | collective-permute-done | bytes 49184 | tf_op jit(solution)/shard_map/ppermute | solution.py:27
  36.7 1.7 %collective-permute-start.8 = (bf16[1,3,32,256]{3,2,1,0:T(8,128)(2,1)S(1)}, bf16[1,3,32,256]{3,2,1,0:T(8,128)(2,1)S(1)}, u32[]{:S(2)}, u32[]{:S(2)}) collective-permute-start(bf16[1,3,32,256]{3,2,1,0:T(8,128)(2,1)S(1)} %get-tuple-element.45.refs_0_), channel_id=1, source_target_pairs={{0,16},{4,20},{8,24},{12,28},{16,0},{20,4},{24,8},{28,12},{1,17},{... | collective-permute-start | bytes 147464 | tf_op jit(solution)/shard_map/ppermute | solution.py:27
  39.9 3.9 %collective-permute-done.8.refs_1_ = bf16[1,3,32,256]{3,2,1,0:T(8,128)(2,1)S(1)} collective-permute-done((bf16[1,3,32,256]{3,2,1,0:T(8,128)(2,1)S(1)}, bf16[1,3,32,256]{3,2,1,0:T(8,128)(2,1)S(1)}, u32[]{:S(2)}, u32[]{:S(2)}) %collective-permute-start.8) | collective-permute-done | bytes 49184 | tf_op jit(solution)/shard_map/ppermute | solution.py:27
  43.9 3.2 %collective-permute-start.12 = (bf16[2,3,32,256]{3,2,1,0:T(8,128)(2,1)S(1)}, bf16[2,3,32,256]{3,2,1,0:T(8,128)(2,1)S(1)}, u32[]{:S(2)}, u32[]{:S(2)}) collective-permute-start(bf16[2,3,32,256]{3,2,1,0:T(8,128)(2,1)S(1)} %join.6.refs_0_), channel_id=1, source_target_pairs={{0,16},{4,20},{8,24},{12,28},{16,0},{20,4},{24,8},{28,12},{1,17},{... | collective-permute-start | bytes 294920 | tf_op jit(solution)/shard_map/ppermute | solution.py:27
  47.0 3.5 %collective-permute-done.9.refs_1_ = bf16[2,3,32,256]{3,2,1,0:T(8,128)(2,1)S(1)} collective-permute-done((bf16[2,3,32,256]{3,2,1,0:T(8,128)(2,1)S(1)}, bf16[2,3,32,256]{3,2,1,0:T(8,128)(2,1)S(1)}, u32[]{:S(2)}, u32[]{:S(2)}) %collective-permute-start.9) | collective-permute-done | bytes 98336 | tf_op jit(solution)/shard_map/ppermute | solution.py:27
  50.5 1.7 %collective-permute-start.10 = (bf16[4,3,32,256]{3,2,1,0:T(8,128)(2,1)S(1)}, bf16[4,3,32,256]{3,2,1,0:T(8,128)(2,1)S(1)}, u32[]{:S(2)}, u32[]{:S(2)}) collective-permute-start(bf16[4,3,32,256]{3,2,1,0:T(8,128)(2,1)S(1)} %join.5.refs_1_), channel_id=1, source_target_pairs={{0,4},{4,0},{8,12},{12,8},{16,20},{20,16},{24,28},{28,24},{1,5},{5... | collective-permute-start | bytes 589832 | tf_op jit(solution)/shard_map/ppermute | solution.py:27
  52.4 3.9 %collective-permute-done.10.refs_2_ = bf16[4,3,32,256]{3,2,1,0:T(8,128)(2,1)S(1)} collective-permute-done((bf16[4,3,32,256]{3,2,1,0:T(8,128)(2,1)S(1)}, bf16[4,3,32,256]{3,2,1,0:T(8,128)(2,1)S(1)}, u32[]{:S(2)}, u32[]{:S(2)}) %collective-permute-start.10) | collective-permute-done | bytes 196640 | tf_op jit(solution)/shard_map/ppermute | solution.py:27
  56.3 1.8 %collective-permute-done.13.refs_4_ = bf16[4,3,32,256]{3,2,1,0:T(8,128)(2,1)S(1)} collective-permute-done((bf16[4,3,32,256]{3,2,1,0:T(8,128)(2,1)S(1)}, bf16[4,3,32,256]{3,2,1,0:T(8,128)(2,1)S(1)}, u32[]{:S(2)}, u32[]{:S(2)}) %collective-permute-start.13) | collective-permute-done | bytes 196640 | tf_op jit(solution)/shard_map/ppermute | solution.py:27
  58.7 1.9 %own_gradients.1.refs_2_.refs_0_ = bf16[16,9,64,256]{3,2,1,0:T(8,128)(2,1)S(1)} custom-call(s32[18]{0:T(128)S(1)} %pad_add_fusion.1.refs_0_, bf16[2,8,3,32,256]{4,3,2,1,0:T(8,128)(2,1)S(1)} %assemble.1.refs_1_, bf16[16,6,64,256]{3,2,1,0:T(8,128)(2,1)S(1)} %get-tuple-element.47.refs_2_, bf16[16,192,256]{2,1,0:T(8,128)(2,1)S(1)} %bitcast.12), custom_call_target="tpu_custom_call" | custom-call | flops 1207959552 | bytes 10223652 | tf_op jit(solution)/shard_map/own_gradients/pallas_call | solution.py:56
  60.7 4.7 %weight_part.1 = (f32[4,96,576]{2,1,0:T(8,128)S(1)}, bf16[4,96,576]{2,1,0:T(8,128)(2,1)S(1)}) custom-call(s32[18]{0:T(128)S(1)} %pad_add_fusion.1.refs_0_, bf16[16,256,768]{2,1,0:T(8,128)(2,1)S(1)} %get-tuple-element.33.refs_1_, bf16[16,9,64,256]{3,2,1,0:T(8,128)(2,1)S(1)} %own_gradients.1.refs_2_.refs_0_), custom_call_target="tpu_custom_call" | custom-call | flops 3623878656 | bytes 11894820 | tf_op jit(solution)/shard_map/weight_part/pallas_call | solution.py:56
  67.4 2.8 %own_input.1.refs_2_.refs_0_ = bf16[2,16,192,256]{3,2,1,0:T(8,128)(2,1)S(1)} custom-call(bf16[16,9,64,256]{3,2,1,0:T(8,128)(2,1)S(1)} %own_gradients.1.refs_2_.refs_0_, bf16[2,192,576]{2,1,0:T(8,128)(2,1)S(1)} %turn.2.refs_4_.refs_1_, bf16[4,96,576]{2,1,0:T(8,128)(2,1)S(1)} %get-tuple-element.48.refs_2_.refs_4_.refs_3_), custom_call_target="tpu_custom_call" | custom-call | flops 1811939328 | bytes 8306688 | tf_op jit(solution)/shard_map/own_input/pallas_call | solution.py:56
  70.2 3.2 %far_query_key.1.refs_3_.refs_2_ = bf16[16,6,64,256]{3,2,1,0:T(8,128)(2,1)S(1)} custom-call(s32[18]{0:T(128)S(1)} %pad_add_fusion.1.refs_0_, bf16[16,256,768]{2,1,0:T(8,128)(2,1)S(1)} %get-tuple-element.33.refs_1_, bf16[192,768]{1,0:T(8,128)(2,1)S(1)} %collective-permute-done.1.refs_5_.refs_2_.refs_1_, ...), custom_call_target="tpu_custom_call" | custom-call | flops 2415919104 | bytes 10174500 | tf_op jit(solution)/shard_map/far_query_key/pallas_call | solution.py:56
  75.1 1.9 %far_gradients.1.refs_1_ = bf16[16,9,64,256]{3,2,1,0:T(8,128)(2,1)S(1)} custom-call(s32[18]{0:T(128)S(1)} %pad_add_fusion.1.refs_0_, bf16[2,8,3,32,256]{4,3,2,1,0:T(8,128)(2,1)S(1)} %collective-permute-done.14.refs_5_.refs_1_, bf16[16,6,64,256]{3,2,1,0:T(8,128)(2,1)S(1)} %far_query_key.1.refs_3_.refs_2_, ...), custom_call_target="tpu_custom_call" | custom-call | flops 1207959552 | bytes 10223652 | tf_op jit(solution)/shard_map/far_gradients/pallas_call | solution.py:56
  78.5 2.3 %collective-permute-done.18.refs_1_ = bf16[2,96,576]{2,1,0:T(8,128)(2,1)S(1)} collective-permute-done((bf16[2,96,576]{2,1,0:T(8,128)(2,1)S(1)}, bf16[2,96,576]{2,1,0:T(8,128)(2,1)S(1)}, u32[]{:S(2)}, u32[]{:S(2)}) %collective-permute-start.18) | collective-permute-done | bytes 221216 | tf_op jit(solution)/shard_map/ppermute | solution.py:27
  82.4 2.6 %collective-permute-start.20 = (bf16[1,96,576]{2,1,0:T(8,128)(2,1)S(1)}, bf16[1,96,576]{2,1,0:T(8,128)(2,1)S(1)}, u32[]{:S(2)}, u32[]{:S(2)}) collective-permute-start(bf16[1,96,576]{2,1,0:T(8,128)(2,1)S(1)} %get-tuple-element.57), channel_id=1, source_target_pairs={{0,16},{4,20},{8,24},{12,28},{16,0},{20,4},{24,8},{28,12},{1,17},{... | collective-permute-start | bytes 331784 | tf_op jit(solution)/shard_map/ppermute | solution.py:27
  86.4 5.2 %collective-permute-done.20.refs_2_ = bf16[1,96,576]{2,1,0:T(8,128)(2,1)S(1)} collective-permute-done((bf16[1,96,576]{2,1,0:T(8,128)(2,1)S(1)}, bf16[1,96,576]{2,1,0:T(8,128)(2,1)S(1)}, u32[]{:S(2)}, u32[]{:S(2)}) %collective-permute-start.20) | collective-permute-done | bytes 110624 | tf_op jit(solution)/shard_map/ppermute | solution.py:27
  (54 shorter events, 18.5 us)
Async XLA Ops:
  0.6 12.5 %collective-permute-start.1 = (bf16[192,768]{1,0:T(8,128)(2,1)}, bf16[192,768]{1,0:T(8,128)(2,1)S(1)}, u32[]{:S(2)}, u32[]{:S(2)}) collective-permute-start(bf16[192,768]{1,0:T(8,128)(2,1)} %bitcast.13), channel_id=1, source_target_pairs={{0,2},{1,3},{2,0},{3,1},{4,6},{5,7},{6,4},{7,5},{8,10},{9,11},{10,... | collective-permute-start | bytes 884744 | tf_op jit(solution)/shard_map/ppermute | solution.py:27
  3.7 9.4 %copy-start.3 = (bf16[768,192]{0,1:T(8,128)(2,1)S(1)}, bf16[768,192]{0,1:T(8,128)(2,1)}, u32[]{:S(2)}) copy-start(bf16[768,192]{0,1:T(8,128)(2,1)} %param.9) | copy-start | bytes 884740
  10.9 6.4 %collective-permute-start = (bf16[4,3,32,256]{3,2,1,0:T(8,128)(2,1)S(1)}, bf16[4,3,32,256]{3,2,1,0:T(8,128)(2,1)S(1)}, u32[]{:S(2)}, u32[]{:S(2)}) collective-permute-start(bf16[4,3,32,256]{3,2,1,0:T(8,128)(2,1)S(1)} %get-tuple-element.32.refs_4_), channel_id=1, source_target_pairs={{0,8},{4,12},{8,0},{12,4},{16,24},{20,28},{24,16},{28,20},{1,9},{5... | collective-permute-start | bytes 589832 | tf_op jit(solution)/shard_map/ppermute | solution.py:27
  12.5 13.1 %collective-permute-start.5 = (bf16[192,1152]{1,0:T(8,128)(2,1)S(1)}, bf16[192,1152]{1,0:T(8,128)(2,1)S(1)}, u32[]{:S(2)}, u32[]{:S(2)}) collective-permute-start(bf16[192,1152]{1,0:T(8,128)(2,1)S(1)} %get-tuple-element.40), channel_id=1, source_target_pairs={{0,2},{1,3},{2,0},{3,1},{4,6},{5,7},{6,4},{7,5},{8,10},{9,11},{10,... | collective-permute-start | bytes 1327112 | tf_op jit(solution)/shard_map/ppermute | solution.py:27
  16.7 16.4 %copy-start.1 = (bf16[768,192]{0,1:T(8,128)(2,1)S(1)}, bf16[768,192]{0,1:T(8,128)(2,1)}, u32[]{:S(2)}) copy-start(bf16[768,192]{0,1:T(8,128)(2,1)} %param.7) | copy-start | bytes 884740
  16.7 16.4 %copy-start.2 = (bf16[768,192]{0,1:T(8,128)(2,1)S(1)}, bf16[768,192]{0,1:T(8,128)(2,1)}, u32[]{:S(2)}) copy-start(bf16[768,192]{0,1:T(8,128)(2,1)} %param.8) | copy-start | bytes 884740
  17.5 52.8 %collective-permute-start.15 = (bf16[16,192,256]{2,1,0:T(8,128)(2,1)S(1)}, bf16[16,192,256]{2,1,0:T(8,128)(2,1)S(1)}, u32[]{:S(2)}, u32[]{:S(2)}) collective-permute-start(bf16[16,192,256]{2,1,0:T(8,128)(2,1)S(1)} %hold.1), channel_id=1, source_target_pairs={{0,2},{1,3},{2,0},{3,1},{4,6},{5,7},{6,4},{7,5},{8,10},{9,11},{10,... | collective-permute-start | bytes 4718600 | tf_op jit(solution)/shard_map/ppermute | solution.py:27
  18.4 7.2 %collective-permute-start.4 = (bf16[4,3,32,256]{3,2,1,0:T(8,128)(2,1)S(1)}, bf16[4,3,32,256]{3,2,1,0:T(8,128)(2,1)S(1)}, u32[]{:S(2)}, u32[]{:S(2)}) collective-permute-start(bf16[4,3,32,256]{3,2,1,0:T(8,128)(2,1)S(1)} %get-tuple-element.34.refs_2_.refs_4_), channel_id=1, source_target_pairs={{0,4},{4,0},{8,12},{12,8},{16,20},{20,16},{24,28},{28,24},{1,5},{5... | collective-permute-start | bytes 589832 | tf_op jit(solution)/shard_map/ppermute | solution.py:27
  19.9 6.6 %collective-permute-start.2 = (bf16[2,3,32,256]{3,2,1,0:T(8,128)(2,1)S(1)}, bf16[2,3,32,256]{3,2,1,0:T(8,128)(2,1)S(1)}, u32[]{:S(2)}, u32[]{:S(2)}) collective-permute-start(bf16[2,3,32,256]{3,2,1,0:T(8,128)(2,1)S(1)} %get-tuple-element.36.refs_1_), channel_id=1, source_target_pairs={{0,16},{4,20},{8,24},{12,28},{16,0},{20,4},{24,8},{28,12},{1,17},{... | collective-permute-start | bytes 294920 | tf_op jit(solution)/shard_map/ppermute | solution.py:27
  25.7 5.2 %collective-permute-start.6 = (bf16[2,3,32,256]{3,2,1,0:T(8,128)(2,1)S(1)}, bf16[2,3,32,256]{3,2,1,0:T(8,128)(2,1)S(1)}, u32[]{:S(2)}, u32[]{:S(2)}) collective-permute-start(bf16[2,3,32,256]{3,2,1,0:T(8,128)(2,1)S(1)} %get-tuple-element.42), channel_id=1, source_target_pairs={{0,8},{4,12},{8,0},{12,4},{16,24},{20,28},{24,16},{28,20},{1,9},{5... | collective-permute-start | bytes 294920 | tf_op jit(solution)/shard_map/ppermute | solution.py:27
  26.5 7.6 %collective-permute-start.3 = (bf16[1,3,32,256]{3,2,1,0:T(8,128)(2,1)S(1)}, bf16[1,3,32,256]{3,2,1,0:T(8,128)(2,1)S(1)}, u32[]{:S(2)}, u32[]{:S(2)}) collective-permute-start(bf16[1,3,32,256]{3,2,1,0:T(8,128)(2,1)S(1)} %get-tuple-element.38), channel_id=1, source_target_pairs={{0,4},{4,0},{8,12},{12,8},{16,20},{20,16},{24,28},{28,24},{1,5},{5... | collective-permute-start | bytes 147464 | tf_op jit(solution)/shard_map/ppermute | solution.py:27
  30.9 5.5 %collective-permute-start.7 = (bf16[1,3,32,256]{3,2,1,0:T(8,128)(2,1)S(1)}, bf16[1,3,32,256]{3,2,1,0:T(8,128)(2,1)S(1)}, u32[]{:S(2)}, u32[]{:S(2)}) collective-permute-start(bf16[1,3,32,256]{3,2,1,0:T(8,128)(2,1)S(1)} %get-tuple-element.44), channel_id=1, source_target_pairs={{0,16},{4,20},{8,24},{12,28},{16,0},{20,4},{24,8},{28,12},{1,17},{... | collective-permute-start | bytes 147464 | tf_op jit(solution)/shard_map/ppermute | solution.py:27
  36.7 7.1 %collective-permute-start.8 = (bf16[1,3,32,256]{3,2,1,0:T(8,128)(2,1)S(1)}, bf16[1,3,32,256]{3,2,1,0:T(8,128)(2,1)S(1)}, u32[]{:S(2)}, u32[]{:S(2)}) collective-permute-start(bf16[1,3,32,256]{3,2,1,0:T(8,128)(2,1)S(1)} %get-tuple-element.45.refs_0_), channel_id=1, source_target_pairs={{0,16},{4,20},{8,24},{12,28},{16,0},{20,4},{24,8},{28,12},{1,17},{... | collective-permute-start | bytes 147464 | tf_op jit(solution)/shard_map/ppermute | solution.py:27
  38.4 5.5 %collective-permute-start.11 = (bf16[1,3,32,256]{3,2,1,0:T(8,128)(2,1)S(1)}, bf16[1,3,32,256]{3,2,1,0:T(8,128)(2,1)S(1)}, u32[]{:S(2)}, u32[]{:S(2)}) collective-permute-start(bf16[1,3,32,256]{3,2,1,0:T(8,128)(2,1)S(1)} %get-tuple-element.46.refs_0_), channel_id=1, source_target_pairs={{0,4},{4,0},{8,12},{12,8},{16,20},{20,16},{24,28},{28,24},{1,5},{5... | collective-permute-start | bytes 147464 | tf_op jit(solution)/shard_map/ppermute | solution.py:27
  43.7 6.8 %collective-permute-start.9 = (bf16[2,3,32,256]{3,2,1,0:T(8,128)(2,1)S(1)}, bf16[2,3,32,256]{3,2,1,0:T(8,128)(2,1)S(1)}, u32[]{:S(2)}, u32[]{:S(2)}) collective-permute-start(bf16[2,3,32,256]{3,2,1,0:T(8,128)(2,1)S(1)} %join.4.refs_0_), channel_id=1, source_target_pairs={{0,8},{4,12},{8,0},{12,4},{16,24},{20,28},{24,16},{28,20},{1,9},{5... | collective-permute-start | bytes 294920 | tf_op jit(solution)/shard_map/ppermute | solution.py:27
  43.9 8.4 %collective-permute-start.12 = (bf16[2,3,32,256]{3,2,1,0:T(8,128)(2,1)S(1)}, bf16[2,3,32,256]{3,2,1,0:T(8,128)(2,1)S(1)}, u32[]{:S(2)}, u32[]{:S(2)}) collective-permute-start(bf16[2,3,32,256]{3,2,1,0:T(8,128)(2,1)S(1)} %join.6.refs_0_), channel_id=1, source_target_pairs={{0,16},{4,20},{8,24},{12,28},{16,0},{20,4},{24,8},{28,12},{1,17},{... | collective-permute-start | bytes 294920 | tf_op jit(solution)/shard_map/ppermute | solution.py:27
  50.5 5.7 %collective-permute-start.10 = (bf16[4,3,32,256]{3,2,1,0:T(8,128)(2,1)S(1)}, bf16[4,3,32,256]{3,2,1,0:T(8,128)(2,1)S(1)}, u32[]{:S(2)}, u32[]{:S(2)}) collective-permute-start(bf16[4,3,32,256]{3,2,1,0:T(8,128)(2,1)S(1)} %join.5.refs_1_), channel_id=1, source_target_pairs={{0,4},{4,0},{8,12},{12,8},{16,20},{20,16},{24,28},{28,24},{1,5},{5... | collective-permute-start | bytes 589832 | tf_op jit(solution)/shard_map/ppermute | solution.py:27
  52.3 5.7 %collective-permute-start.13 = (bf16[4,3,32,256]{3,2,1,0:T(8,128)(2,1)S(1)}, bf16[4,3,32,256]{3,2,1,0:T(8,128)(2,1)S(1)}, u32[]{:S(2)}, u32[]{:S(2)}) collective-permute-start(bf16[4,3,32,256]{3,2,1,0:T(8,128)(2,1)S(1)} %join.7.refs_3_), channel_id=1, source_target_pairs={{0,8},{4,12},{8,0},{12,4},{16,24},{20,28},{24,16},{28,20},{1,9},{5... | collective-permute-start | bytes 589832 | tf_op jit(solution)/shard_map/ppermute | solution.py:27
  58.6 15.8 %collective-permute-start.14 = (bf16[2,8,3,32,256]{4,3,2,1,0:T(8,128)(2,1)S(1)}, bf16[2,8,3,32,256]{4,3,2,1,0:T(8,128)(2,1)S(1)}, u32[]{:S(2)}, u32[]{:S(2)}) collective-permute-start(bf16[2,8,3,32,256]{4,3,2,1,0:T(8,128)(2,1)S(1)} %assemble.1.refs_1_), channel_id=1, source_target_pairs={{0,2},{1,3},{2,0},{3,1},{4,6},{5,7},{6,4},{7,5},{8,10},{9,11},{10,... | collective-permute-start | bytes 2359304 | tf_op jit(solution)/shard_map/ppermute | solution.py:27
  65.4 8.9 %collective-permute-start.16 = (bf16[4,96,576]{2,1,0:T(8,128)(2,1)S(1)}, bf16[4,96,576]{2,1,0:T(8,128)(2,1)S(1)}, u32[]{:S(2)}, u32[]{:S(2)}) collective-permute-start(bf16[4,96,576]{2,1,0:T(8,128)(2,1)S(1)} %get-tuple-element.48.refs_2_.refs_4_.refs_3_), channel_id=1, source_target_pairs={{0,4},{4,0},{8,12},{12,8},{16,20},{20,16},{24,28},{28,24},{1,5},{5... | collective-permute-start | bytes 1327112 | tf_op jit(solution)/shard_map/ppermute | solution.py:27
  74.6 6.3 %collective-permute-start.18 = (bf16[2,96,576]{2,1,0:T(8,128)(2,1)S(1)}, bf16[2,96,576]{2,1,0:T(8,128)(2,1)S(1)}, u32[]{:S(2)}, u32[]{:S(2)}) collective-permute-start(bf16[2,96,576]{2,1,0:T(8,128)(2,1)S(1)} %get-tuple-element.53), channel_id=1, source_target_pairs={{0,8},{4,12},{8,0},{12,4},{16,24},{20,28},{24,16},{28,20},{1,9},{5... | collective-permute-start | bytes 663560 | tf_op jit(solution)/shard_map/ppermute | solution.py:27
  78.4 6.6 %collective-permute-start.17 = (bf16[8,192,256]{2,1,0:T(8,128)(2,1)S(1)}, bf16[8,192,256]{2,1,0:T(8,128)(2,1)S(1)}, u32[]{:S(2)}, u32[]{:S(2)}) collective-permute-start(bf16[8,192,256]{2,1,0:T(8,128)(2,1)S(1)} %get-tuple-element.52), channel_id=1, source_target_pairs={{0,1},{1,0},{2,3},{3,2},{4,5},{5,4},{6,7},{7,6},{8,9},{9,8},{10,11... | collective-permute-start | bytes 2359304 | tf_op jit(solution)/shard_map/ppermute | solution.py:27
  82.3 2.7 %collective-permute-start.19 = (bf16[8,192,256]{2,1,0:T(8,128)(2,1)S(1)}, bf16[8,192,256]{2,1,0:T(8,128)(2,1)S(1)}, u32[]{:S(2)}, u32[]{:S(2)}) collective-permute-start(bf16[8,192,256]{2,1,0:T(8,128)(2,1)S(1)} %get-tuple-element.56), channel_id=1, source_target_pairs={{0,1},{1,0},{2,3},{3,2},{4,5},{5,4},{6,7},{7,6},{8,9},{9,8},{10,11... | collective-permute-start | bytes 2359304 | tf_op jit(solution)/shard_map/ppermute | solution.py:27
  82.4 9.2 %collective-permute-start.20 = (bf16[1,96,576]{2,1,0:T(8,128)(2,1)S(1)}, bf16[1,96,576]{2,1,0:T(8,128)(2,1)S(1)}, u32[]{:S(2)}, u32[]{:S(2)}) collective-permute-start(bf16[1,96,576]{2,1,0:T(8,128)(2,1)S(1)} %get-tuple-element.57), channel_id=1, source_target_pairs={{0,16},{4,20},{8,24},{12,28},{16,0},{20,4},{24,8},{28,12},{1,17},{... | collective-permute-start | bytes 331784 | tf_op jit(solution)/shard_map/ppermute | solution.py:27
  (1 other events, 9.4 us)

commit v17 on v16

--- a/solution.py
+++ b/solution.py
@@ -84,8 +84,8 @@
 AHEAD = 6
 
 
-def query_key_kernel(bits, fars, me, lengths, sheet, wq, wk, wv, qk, held, seen, *rest):
-    outs, staged, (wt, acc, number, sems) = rest[: -4 - len(fars)], rest[-4 - len(fars) : -4], rest[-4:]
+def query_key_kernel(bits, me, lengths, sheet, wq, wk, qk, held, seen, *rest):
+    outs, (wt, acc, number, sems) = rest[:-4], rest[-4:]
     rows, cols, width = sheet.shape
     local = wq.shape[0]
     heads = local // HEAD_DIM
@@ -101,12 +101,6 @@
     for first in range(0, rows, STEP):
         some = pl.ds(first, STEP)
         copy(sheet.at[some], held.at[some])
-    for far, out in zip(fars, staged):
-        near = out.shape[1] - width
-        side = lax.shift_right_logical(me[1], 1) ^ (far // 2)
-        some = pl.ds(pl.multiple_of(side * near, 128), near)
-        copy(wk, out.at[:, pl.ds(0, width)])
-        copy(wv.at[:, some], out.at[:, pl.ds(width, near)])
     for one in copies[:AHEAD]:
         one.start()
     for one in copies[:4]:
@@ -117,8 +111,7 @@
             if r % STEP == 0:
                 at = 4 + r // STEP
                 copies[at].wait()
-                last = at + AHEAD - 3 if r + STEP < rows else len(copies)
-                for later in copies[at + AHEAD - 4 : last]:
+                for later in copies[at + AHEAD - 4 : at + AHEAD - 3]:
                     later.start()
             value = (mm(wt[...], held[r], NT) * lane_mask(number[0, r], cols)).astype(BF16)
             qk[r] = value.reshape(2 * heads, HEAD_DIM, cols)
@@ -128,44 +121,46 @@
             term = term.reshape(acc.shape[1:])
             acc[h] = term if first == 0 else acc[h] + term
     put_shards(me[0], acc, bits, outs)
-    started = 4 + rows // STEP
-    for one in copies[started:]:
-        one.wait()
-
-
-def query_key(me, lengths, sheet, wq, wk, wv, bits, fars, devices):
+
+
+def query_key(me, lengths, sheet, wq, wk, bits):
     rows, cols, width = sheet.shape
     shards = 1 << len(bits)
     local = wq.shape[0]
     heads = local // HEAD_DIM
     return in_vmem(
-        functools.partial(query_key_kernel, bits, fars),
+        functools.partial(query_key_kernel, bits),
         "query_key",
         [like((rows, 2 * heads, HEAD_DIM, cols)), like(sheet.shape), like(lengths.shape, jnp.int32)]
-        + part_shapes(shards, heads, cols)
-        + [like((local, width + 2 * width // devices))] * len(fars),
+        + part_shapes(shards, heads, cols),
         me,
         lengths,
         sheet,
         wq,
         wk,
-        wv,
         scalars=1,
-        streamed=5,
+        streamed=4,
         scratch=(
             pltpu.VMEM((2 * local, width), BF16),
             pltpu.VMEM((heads, shards, cols // shards, cols), F32),
             pltpu.SMEM(lengths.shape, jnp.int32),
-            pltpu.SemaphoreType.DMA((4 + rows // STEP + 2 * len(fars),)),
+            pltpu.SemaphoreType.DMA((4 + rows // STEP,)),
         ),
         limit=14,
         flops=2 * rows * cols * local * (2 * width + cols),
     )
 
 
-def value_kernel(bits, where, sheet, wv, cot, *rest):
-    outs, acc = rest[:-1], rest[-1]
+def value_kernel(bits, fars, where, sheet, wv, cot, *rest):
+    outs, halves, acc = rest[: -1 - len(fars)], rest[-1 - len(fars) : -1], rest[-1]
     rows, cols, width = sheet.shape
+    for far, half in zip(fars, halves):
+        near = half.shape[1]
+        side = lax.shift_right_logical(where[1], 1) ^ (far // 2)
+        for s in range(width // near):
+            @pl.when(side == s)
+            def _():
+                half[...] = wv[:, s * near : (s + 1) * near]
     local = wv.shape[0]
     heads = local // HEAD_DIM
     flat = (BLOCK * HEAD_DIM, cols)
@@ -182,15 +177,15 @@
     put_shards(where[0], acc, bits, outs)
 
 
-def value_dprob(where, sheet, wv, cot, after, bits):
+def value_dprob(where, sheet, wv, cot, after, bits, fars, devices):
     rows, cols, width = sheet.shape
     shards = 1 << len(bits)
     local = wv.shape[0]
     heads = local // HEAD_DIM
     return in_vmem(
-        functools.partial(value_kernel, bits),
+        functools.partial(value_kernel, bits, fars),
         "value_dprob",
-        part_shapes(shards, heads, cols),
+        part_shapes(shards, heads, cols) + [like((local, 2 * width // devices))] * len(fars),
         where,
         sheet,
         wv,
@@ -203,48 +198,45 @@
     )
 
 
-def turn_kernel(where, wq, *rest):
-    *others, natural, query, key, value = rest
+def turn_kernel(where, wq, wk, wv, natural, *full):
     near, share, columns = natural.shape
-    local, width = wq.shape
-    wk = others[0][:, :width]
-    wv = others[1][...] if len(others) == 2 else others[0][:, width:]
-    for index, (weight, held) in enumerate(((wq[...], query), (wk, key), (wv, value))):
-        held[...] = weight.T.reshape(held.shape)
+    local = wq.shape[0]
+    for index, (weight, held) in enumerate(zip((wq, wk, wv), full)):
+        held[...] = weight[...].T.reshape(held.shape)
         mine = where[1] & (held.shape[0] - 1)
         for j in range(near):
             natural[j, :, index * local : (index + 1) * local] = held[mine ^ j]
 
 
-def turn(where, wq, others, devices, after):
+def turn(where, wq, wk, wv, devices, after):
     local, width = wq.shape
     share = width // devices
-    counts = (devices, devices, devices if len(others) == 2 else 2)
     return in_vmem(
         turn_kernel,
         "turn",
         (like((2, share, 3 * local)),),
         where,
         wq,
-        *others,
+        wk,
+        wv,
         scalars=1,
         after=after,
-        scratch=[pltpu.VMEM((count, share, local), BF16) for count in counts],
+        scratch=[pltpu.VMEM((w.shape[1] // share, share, local), BF16) for w in (wq, wk, wv)],
     )[0]
 
 
-def far_query_key_kernel(where, sheet, wq, staged, qk):
-    local = staged.shape[0]
-    rows, cols, width = sheet.shape
-    both = jnp.concatenate([wq[...], staged[:, :width]], axis=0)
+def far_query_key_kernel(where, sheet, wq, wk, qk):
+    local = wq.shape[0]
+    rows, cols, _ = sheet.shape
+    both = jnp.concatenate([wq[...], wk[...]], axis=0)
     for r in range(rows):
         value = (mm(both, sheet[r], NT) * lane_mask(where[2 + r], cols)).astype(BF16)
         qk[r] = value.reshape(2 * local // HEAD_DIM, HEAD_DIM, cols)
 
 
-def far_query_key(where, sheet, wq, staged, after):
+def far_query_key(where, sheet, wq, wk, after):
     rows, cols, width = sheet.shape
-    local = staged.shape[0]
+    local = wq.shape[0]
     return in_vmem(
         far_query_key_kernel,
         "far_query_key",
@@ -252,7 +244,7 @@
         where,
         sheet,
         wq,
-        staged,
+        wk,
         scalars=1,
         after=after,
         flops=4 * rows * cols * local * width,
@@ -553,36 +545,32 @@
     cot = jnp.swapaxes(cotangent, 1, 2)
 
     fars = range(2, n_heads, 2)
-    far_wq = [flip(wq, "heads", f) for f in fars]
+    far_cot = [flip(cot, "heads", f) for f in fars]
+    fq, fk = [[flip(w, "heads", f) for f in fars] for w in (wq, wk)]
     up = row_bits if direct else []
     turn_about = up[1:] + up[:1]
-    parts = query_key(me, lengths.reshape(1, row_dev), sheet, wq, wk, wv, turn_about, fars, n_heads)
-    qk, held, seen, *logits = parts
+    qk, held, seen, *logits = query_key(me, lengths.reshape(1, row_dev), sheet, wq, wk, turn_about)
     where = jnp.concatenate([me, seen.reshape(row_dev)])
-    logits, staged = logits[: -len(fars)], logits[-len(fars) :]
-    far_staged = [flip(a, "heads", f) for a, f in zip(staged, fars)]
-    dprob = value_dprob(where, held, wv, cot, logits[-1:] + far_wq, up)
-    weights = turn(where, wq, [wk, wv], n_heads, dprob[-1:])
+    dprob = value_dprob(where, held, wv, cot, logits[-1:], up, fars, n_heads)
+    dprob, halves = dprob[: -len(fars)], dprob[-len(fars) :]
+    fv = [flip(half, "heads", f) for half, f in zip(halves, fars)]
+    weights = turn(where, wq, wk, wv, n_heads, dprob[-1:])
     if direct:
-        give, keep = add_split(logits[0], flip(logits[1], "rows", turn_about[0]), dprob[1:])
-        later = [give]
-        logits = halve(keep, give, "rows", turn_about[1:])
-        dprob = halve(*dprob, "rows", up, [far_staged])
-        probs, dscore = softmax_back(logits, dprob, scale, [weights] + far_staged)
-        probs, probs_order = double(probs, "rows", up[::-1])
+        logits = halve(*logits, "rows", turn_about)
+        dprob = halve(*dprob, "rows", up)
+        probs, dscore = softmax_back(logits, dprob, scale, [weights])
+        probs, probs_order = double(probs, "rows", up[::-1], [far_cot, fv])
         dscore, dscore_order = double(dscore, "rows", turn_about[::-1])
-        scores = assemble(where, probs, dscore, (probs_order, dscore_order), shards, ())
+        scores = assemble(where, probs, dscore, (probs_order, dscore_order), shards, fq)
     else:
-        later = [weights]
         logits, dprob = lax.psum((logits, dprob), "rows")
         scores = jnp.stack(softmax_back(logits, dprob, scale))
-    far_cot = [flip(hold(cot, later), "heads", f) for f in fars]
     far_scores = [flip(scores, "heads", f) for f in fars]
     grads = all_gradients(where, scores, qk, cot, "own_gradients", ())
-    parts = weight_part(where, held, grads, (3 * local,), shards, ())
+    parts = weight_part(where, held, grads, (3 * local,), shards, fk)
     ready = [parts[-1]]
-    far_qk = [far_query_key(where, held, *w, ready + far_cot) for w in zip(far_wq, far_staged)]
-    far_natural = [turn(where, w, [other], n_heads, ready) for w, other in zip(far_wq, far_staged)]
+    far_qk = [far_query_key(where, held, *w, ready) for w in zip(fq, fk)]
+    far_natural = [turn(where, *w, n_heads, ready) for w in zip(fq, fk, fv)]
     own = own_input(grads, weights, ready)
     ready = [own] + far_qk + far_natural + far_scores
     steps = [[], []]

time: 92.6 us -> 89.8 us (0.970)
  waiting for transfers between devices: 30.9 us -> 23.6 us
  starting transfers between devices: 26.8 us -> 31.5 us
    ppermute x21 -> x22, waiting for transfers between devices: 30.9 us -> 23.6 us  [flip(): return lax.ppermute(values, axis, [(s, s ^ bit) for s in range(n)])]
    ppermute x21 -> x22, starting transfers between devices: 26.8 us -> 31.5 us  [flip(): return lax.ppermute(values, axis, [(s, s ^ bit) for s in range(n)])]
    pallas_call x25 -> x24, Pallas kernels: 32.3 us -> 32.2 us  [in_vmem(): pl.pallas_call(run, in_specs=[SMEM] * scalars + [HBM] * streamed + [VMEM]...]
  transfers between devices with their start and end apart: 21 -> 22, of which waited for: 13 -> 14; matrix products, arithmetic and copies ran while one was open for 0% -> 0% of each run, Pallas kernels for 35% -> 36%
where the time goes in v17:
time: 89.8 us; the launch traced here: 89.6 us
  Pallas kernels  33.5 us (37%)
  starting transfers between devices  31.5 us (35%)
  waiting for transfers between devices  23.6 us (26%)
    pallas_call x24, Pallas kernels, in_vmem(): pl.pallas_call(run, in_specs=[SMEM] * scalars + [HBM] * streamed + [VMEM]...  32.2 us
    ppermute x22, starting transfers between devices, flip(): return lax.ppermute(values, axis, [(s, s ^ bit) for s in range(n)])  31.5 us
    ppermute x22, waiting for transfers between devices, flip(): return lax.ppermute(values, axis, [(s, s ^ bit) for s in range(n)])  23.6 us
  transfers between devices with their start and end apart: 22, of which 14 were waited for; matrix products, arithmetic and copies ran while one was open for 0% of the time, Pallas kernels for 36%

profile of v17, /device:TPU:0, one launch (start us, length us, event | category | flops | bytes accessed | tf_op | source)
XLA Modules:
  0.0 89.6 jit_solution(4730558604463809245)
XLA Ops:
  0.6 3.0 %collective-permute-start.7 = (bf16[16,192,256]{2,1,0:T(8,128)(2,1)}, bf16[16,192,256]{2,1,0:T(8,128)(2,1)S(1)}, u32[]{:S(2)}, u32[]{:S(2)}) collective-permute-start(bf16[16,192,256]{2,1,0:T(8,128)(2,1)} %bitcast.10), channel_id=1, source_target_pairs={{0,2},{1,3},{2,0},{3,1},{4,6},{5,7},{6,4},{7,5},{8,10},{9,11},{10,... | collective-permute-start | bytes 4718600 | tf_op jit(solution)/shard_map/ppermute | solution.py:27
  3.7 7.0 %query_key.1 = (bf16[16,6,64,256]{3,2,1,0:T(8,128)(2,1)S(1)}, bf16[16,256,768]{2,1,0:T(8,128)(2,1)S(1)}, s32[1,16]{1,0:T(1,128)S(1)}, f32[4,3,32,256]{3,2,1,0:T(8,128)S(1)}, bf16[4,3,32,256]{3,2,1,0:T(8,128)(2,1)S(1)}) custom-call(s32[2]{0:T(128)S(1)} %pad_add_fusion.refs_0_, s32[1,16]{1,0:T(1,128)} %bitcast.24, bf16[16,256,768]{2,1,0:T(8,128)(2,1)} %refs_2_.1, ...), custom_call_target="tpu_custom_call" | custom-call | flops 2818572288 | bytes 16711748 | tf_op jit(solution)/shard_map/query_key/pallas_call | solution.py:56
  10.7 1.6 %collective-permute-start = (bf16[4,3,32,256]{3,2,1,0:T(8,128)(2,1)S(1)}, bf16[4,3,32,256]{3,2,1,0:T(8,128)(2,1)S(1)}, u32[]{:S(2)}, u32[]{:S(2)}) collective-permute-start(bf16[4,3,32,256]{3,2,1,0:T(8,128)(2,1)S(1)} %get-tuple-element.32.refs_4_), channel_id=1, source_target_pairs={{0,8},{4,12},{8,0},{12,4},{16,24},{20,28},{24,16},{28,20},{1,9},{5... | collective-permute-start | bytes 589832 | tf_op jit(solution)/shard_map/ppermute | solution.py:27
  12.5 3.7 %value_dprob.1 = (f32[4,3,32,256]{3,2,1,0:T(8,128)S(1)}, bf16[4,3,32,256]{3,2,1,0:T(8,128)(2,1)S(1)}, bf16[192,384]{1,0:T(8,128)(2,1)S(1)}) custom-call(s32[18]{0:T(128)S(1)} %pad_add_fusion.1.refs_0_, bf16[16,256,768]{2,1,0:T(8,128)(2,1)S(1)} %get-tuple-element.37.refs_1_, bf16[192,768]{1,0:T(8,128)(2,1)S(1)} %bitcast.13, ...), custom_call_target="tpu_custom_call" | custom-call | flops 12884901888 | bytes 8699940 | tf_op jit(solution)/shard_map/value_dprob/pallas_call | solution.py:56
  17.8 2.7 %collective-permute-start.1 = (bf16[2,3,32,256]{3,2,1,0:T(8,128)(2,1)S(1)}, bf16[2,3,32,256]{3,2,1,0:T(8,128)(2,1)S(1)}, u32[]{:S(2)}, u32[]{:S(2)}) collective-permute-start(bf16[2,3,32,256]{3,2,1,0:T(8,128)(2,1)S(1)} %get-tuple-element.34), channel_id=1, source_target_pairs={{0,16},{4,20},{8,24},{12,28},{16,0},{20,4},{24,8},{28,12},{1,17},{... | collective-permute-start | bytes 294920 | tf_op jit(solution)/shard_map/ppermute | solution.py:27
  20.5 1.9 %collective-permute-done.3.refs_1_ = bf16[4,3,32,256]{3,2,1,0:T(8,128)(2,1)S(1)} collective-permute-done((bf16[4,3,32,256]{3,2,1,0:T(8,128)(2,1)S(1)}, bf16[4,3,32,256]{3,2,1,0:T(8,128)(2,1)S(1)}, u32[]{:S(2)}, u32[]{:S(2)}) %collective-permute-start.3) | collective-permute-done | bytes 196640 | tf_op jit(solution)/shard_map/ppermute | solution.py:27
  22.9 1.8 %collective-permute-done.1.refs_1_ = bf16[2,3,32,256]{3,2,1,0:T(8,128)(2,1)S(1)} collective-permute-done((bf16[2,3,32,256]{3,2,1,0:T(8,128)(2,1)S(1)}, bf16[2,3,32,256]{3,2,1,0:T(8,128)(2,1)S(1)}, u32[]{:S(2)}, u32[]{:S(2)}) %collective-permute-start.1) | collective-permute-done | bytes 98336 | tf_op jit(solution)/shard_map/ppermute | solution.py:27
  24.8 2.3 %collective-permute-done.4.refs_1_ = bf16[2,3,32,256]{3,2,1,0:T(8,128)(2,1)S(1)} collective-permute-done((bf16[2,3,32,256]{3,2,1,0:T(8,128)(2,1)S(1)}, bf16[2,3,32,256]{3,2,1,0:T(8,128)(2,1)S(1)}, u32[]{:S(2)}, u32[]{:S(2)}) %collective-permute-start.4) | collective-permute-done | bytes 98336 | tf_op jit(solution)/shard_map/ppermute | solution.py:27
  27.1 2.8 %collective-permute-start.5 = (bf16[1,3,32,256]{3,2,1,0:T(8,128)(2,1)S(1)}, bf16[1,3,32,256]{3,2,1,0:T(8,128)(2,1)S(1)}, u32[]{:S(2)}, u32[]{:S(2)}) collective-permute-start(bf16[1,3,32,256]{3,2,1,0:T(8,128)(2,1)S(1)} %get-tuple-element.43), channel_id=1, source_target_pairs={{0,16},{4,20},{8,24},{12,28},{16,0},{20,4},{24,8},{28,12},{1,17},{... | collective-permute-start | bytes 147464 | tf_op jit(solution)/shard_map/ppermute | solution.py:27
  31.0 1.6 %collective-permute-done.5.refs_3_ = bf16[1,3,32,256]{3,2,1,0:T(8,128)(2,1)S(1)} collective-permute-done((bf16[1,3,32,256]{3,2,1,0:T(8,128)(2,1)S(1)}, bf16[1,3,32,256]{3,2,1,0:T(8,128)(2,1)S(1)}, u32[]{:S(2)}, u32[]{:S(2)}) %collective-permute-start.5) | collective-permute-done | bytes 49184 | tf_op jit(solution)/shard_map/ppermute | solution.py:27
  34.4 2.4 %collective-permute-start.6 = (bf16[1,3,32,256]{3,2,1,0:T(8,128)(2,1)S(1)}, bf16[1,3,32,256]{3,2,1,0:T(8,128)(2,1)S(1)}, u32[]{:S(2)}, u32[]{:S(2)}) collective-permute-start(bf16[1,3,32,256]{3,2,1,0:T(8,128)(2,1)S(1)} %get-tuple-element.44.refs_0_), channel_id=1, source_target_pairs={{0,16},{4,20},{8,24},{12,28},{16,0},{20,4},{24,8},{28,12},{1,17},{... | collective-permute-start | bytes 147464 | tf_op jit(solution)/shard_map/ppermute | solution.py:27
  37.3 2.1 %collective-permute-start.12 = (bf16[2,3,32,256]{3,2,1,0:T(8,128)(2,1)S(1)}, bf16[2,3,32,256]{3,2,1,0:T(8,128)(2,1)S(1)}, u32[]{:S(2)}, u32[]{:S(2)}) collective-permute-start(bf16[2,3,32,256]{3,2,1,0:T(8,128)(2,1)S(1)} %join.6.refs_0_), channel_id=1, source_target_pairs={{0,16},{4,20},{8,24},{12,28},{16,0},{20,4},{24,8},{28,12},{1,17},{... | collective-permute-start | bytes 294920 | tf_op jit(solution)/shard_map/ppermute | solution.py:27
  43.8 2.0 %collective-permute-done.8.refs_1_ = bf16[2,3,32,256]{3,2,1,0:T(8,128)(2,1)S(1)} collective-permute-done((bf16[2,3,32,256]{3,2,1,0:T(8,128)(2,1)S(1)}, bf16[2,3,32,256]{3,2,1,0:T(8,128)(2,1)S(1)}, u32[]{:S(2)}, u32[]{:S(2)}) %collective-permute-start.8) | collective-permute-done | bytes 98336 | tf_op jit(solution)/shard_map/ppermute | solution.py:27
  46.9 1.6 %collective-permute-start.15 = (bf16[192,768]{1,0:T(8,128)(2,1)S(1)}, bf16[192,768]{1,0:T(8,128)(2,1)S(1)}, u32[]{:S(2)}, u32[]{:S(2)}) collective-permute-start(bf16[192,768]{1,0:T(8,128)(2,1)S(1)} %bitcast.20), channel_id=1, source_target_pairs={{0,2},{1,3},{2,0},{3,1},{4,6},{5,7},{6,4},{7,5},{8,10},{9,11},{10,... | collective-permute-start | bytes 884744 | tf_op jit(solution)/shard_map/ppermute | solution.py:27
  48.5 2.7 %collective-permute-done.14.refs_5_.refs_2_.refs_1_ = bf16[192,768]{1,0:T(8,128)(2,1)S(1)} collective-permute-done((bf16[192,768]{1,0:T(8,128)(2,1)S(1)}, bf16[192,768]{1,0:T(8,128)(2,1)S(1)}, u32[]{:S(2)}, u32[]{:S(2)}) %collective-permute-start.14) | collective-permute-done | bytes 294944 | tf_op jit(solution)/shard_map/ppermute | solution.py:27
  52.2 1.6 %collective-permute-start.16 = (bf16[2,8,3,32,256]{4,3,2,1,0:T(8,128)(2,1)S(1)}, bf16[2,8,3,32,256]{4,3,2,1,0:T(8,128)(2,1)S(1)}, u32[]{:S(2)}, u32[]{:S(2)}) collective-permute-start(bf16[2,8,3,32,256]{4,3,2,1,0:T(8,128)(2,1)S(1)} %assemble.1.refs_1_), channel_id=1, source_target_pairs={{0,2},{1,3},{2,0},{3,1},{4,6},{5,7},{6,4},{7,5},{8,10},{9,11},{10,... | collective-permute-start | bytes 2359304 | tf_op jit(solution)/shard_map/ppermute | solution.py:27
  53.7 1.9 %own_gradients.1.refs_2_.refs_0_ = bf16[16,9,64,256]{3,2,1,0:T(8,128)(2,1)S(1)} custom-call(s32[18]{0:T(128)S(1)} %pad_add_fusion.1.refs_0_, bf16[2,8,3,32,256]{4,3,2,1,0:T(8,128)(2,1)S(1)} %assemble.1.refs_1_, bf16[16,6,64,256]{3,2,1,0:T(8,128)(2,1)S(1)} %get-tuple-element.47.refs_2_, bf16[16,192,256]{2,1,0:T(8,128)(2,1)S(1)} %bitcast.12), custom_call_target="tpu_custom_call" | custom-call | flops 1207959552 | bytes 10223652 | tf_op jit(solution)/shard_map/own_gradients/pallas_call | solution.py:56
  55.7 1.9 %collective-permute-done.15.refs_3_.refs_2_ = bf16[192,768]{1,0:T(8,128)(2,1)S(1)} collective-permute-done((bf16[192,768]{1,0:T(8,128)(2,1)S(1)}, bf16[192,768]{1,0:T(8,128)(2,1)S(1)}, u32[]{:S(2)}, u32[]{:S(2)}) %collective-permute-start.15) | collective-permute-done | bytes 294944 | tf_op jit(solution)/shard_map/ppermute | solution.py:27
  57.6 4.7 %weight_part.1 = (f32[4,96,576]{2,1,0:T(8,128)S(1)}, bf16[4,96,576]{2,1,0:T(8,128)(2,1)S(1)}) custom-call(s32[18]{0:T(128)S(1)} %pad_add_fusion.1.refs_0_, bf16[16,256,768]{2,1,0:T(8,128)(2,1)S(1)} %get-tuple-element.37.refs_1_, bf16[16,9,64,256]{3,2,1,0:T(8,128)(2,1)S(1)} %own_gradients.1.refs_2_.refs_0_, ...), custom_call_target="tpu_custom_call" | custom-call | flops 3623878656 | bytes 11894820 | tf_op jit(solution)/shard_map/weight_part/pallas_call | solution.py:56
  64.8 2.6 %own_input.1.refs_2_.refs_0_ = bf16[2,16,192,256]{3,2,1,0:T(8,128)(2,1)S(1)} custom-call(bf16[16,9,64,256]{3,2,1,0:T(8,128)(2,1)S(1)} %own_gradients.1.refs_2_.refs_0_, bf16[2,192,576]{2,1,0:T(8,128)(2,1)S(1)} %turn.2.refs_4_.refs_1_, bf16[4,96,576]{2,1,0:T(8,128)(2,1)S(1)} %get-tuple-element.48.refs_2_.refs_4_), custom_call_target="tpu_custom_call" | custom-call | flops 1811939328 | bytes 8306688 | tf_op jit(solution)/shard_map/own_input/pallas_call | solution.py:56
  67.5 3.2 %far_query_key.1.refs_3_.refs_2_ = bf16[16,6,64,256]{3,2,1,0:T(8,128)(2,1)S(1)} custom-call(s32[18]{0:T(128)S(1)} %pad_add_fusion.1.refs_0_, bf16[16,256,768]{2,1,0:T(8,128)(2,1)S(1)} %get-tuple-element.37.refs_1_, bf16[192,768]{1,0:T(8,128)(2,1)S(1)} %collective-permute-done.14.refs_5_.refs_2_.refs_1_, ...), custom_call_target="tpu_custom_call" | custom-call | flops 2415919104 | bytes 10027044 | tf_op jit(solution)/shard_map/far_query_key/pallas_call | solution.py:56
  73.1 1.9 %far_gradients.1.refs_1_ = bf16[16,9,64,256]{3,2,1,0:T(8,128)(2,1)S(1)} custom-call(s32[18]{0:T(128)S(1)} %pad_add_fusion.1.refs_0_, bf16[2,8,3,32,256]{4,3,2,1,0:T(8,128)(2,1)S(1)} %collective-permute-done.16.refs_5_.refs_1_, bf16[16,6,64,256]{3,2,1,0:T(8,128)(2,1)S(1)} %far_query_key.1.refs_3_.refs_2_, ...), custom_call_target="tpu_custom_call" | custom-call | flops 1207959552 | bytes 10223652 | tf_op jit(solution)/shard_map/far_gradients/pallas_call | solution.py:56
  79.6 2.4 %collective-permute-start.21 = (bf16[1,96,576]{2,1,0:T(8,128)(2,1)S(1)}, bf16[1,96,576]{2,1,0:T(8,128)(2,1)S(1)}, u32[]{:S(2)}, u32[]{:S(2)}) collective-permute-start(bf16[1,96,576]{2,1,0:T(8,128)(2,1)S(1)} %get-tuple-element.57), channel_id=1, source_target_pairs={{0,16},{4,20},{8,24},{12,28},{16,0},{20,4},{24,8},{28,12},{1,17},{... | collective-permute-start | bytes 331784 | tf_op jit(solution)/shard_map/ppermute | solution.py:27
  83.3 5.5 %collective-permute-done.21.refs_2_ = bf16[1,96,576]{2,1,0:T(8,128)(2,1)S(1)} collective-permute-done((bf16[1,96,576]{2,1,0:T(8,128)(2,1)S(1)}, bf16[1,96,576]{2,1,0:T(8,128)(2,1)S(1)}, u32[]{:S(2)}, u32[]{:S(2)}) %collective-permute-start.21) | collective-permute-done | bytes 110624 | tf_op jit(solution)/shard_map/ppermute | solution.py:27
  (55 shorter events, 23.9 us)
Async XLA Ops:
  0.6 39.4 %collective-permute-start.7 = (bf16[16,192,256]{2,1,0:T(8,128)(2,1)}, bf16[16,192,256]{2,1,0:T(8,128)(2,1)S(1)}, u32[]{:S(2)}, u32[]{:S(2)}) collective-permute-start(bf16[16,192,256]{2,1,0:T(8,128)(2,1)} %bitcast.10), channel_id=1, source_target_pairs={{0,2},{1,3},{2,0},{3,1},{4,6},{5,7},{6,4},{7,5},{8,10},{9,11},{10,... | collective-permute-start | bytes 4718600 | tf_op jit(solution)/shard_map/ppermute | solution.py:27
  10.7 7.0 %collective-permute-start = (bf16[4,3,32,256]{3,2,1,0:T(8,128)(2,1)S(1)}, bf16[4,3,32,256]{3,2,1,0:T(8,128)(2,1)S(1)}, u32[]{:S(2)}, u32[]{:S(2)}) collective-permute-start(bf16[4,3,32,256]{3,2,1,0:T(8,128)(2,1)S(1)} %get-tuple-element.32.refs_4_), channel_id=1, source_target_pairs={{0,8},{4,12},{8,0},{12,4},{16,24},{20,28},{24,16},{28,20},{1,9},{5... | collective-permute-start | bytes 589832 | tf_op jit(solution)/shard_map/ppermute | solution.py:27
  12.4 17.5 %copy-start.2 = (bf16[768,192]{0,1:T(8,128)(2,1)S(1)}, bf16[768,192]{0,1:T(8,128)(2,1)}, u32[]{:S(2)}) copy-start(bf16[768,192]{0,1:T(8,128)(2,1)} %param.7) | copy-start | bytes 884740
  12.4 17.5 %copy-start.3 = (bf16[768,192]{0,1:T(8,128)(2,1)S(1)}, bf16[768,192]{0,1:T(8,128)(2,1)}, u32[]{:S(2)}) copy-start(bf16[768,192]{0,1:T(8,128)(2,1)} %param.8) | copy-start | bytes 884740
  16.2 6.1 %collective-permute-start.3 = (bf16[4,3,32,256]{3,2,1,0:T(8,128)(2,1)S(1)}, bf16[4,3,32,256]{3,2,1,0:T(8,128)(2,1)S(1)}, u32[]{:S(2)}, u32[]{:S(2)}) collective-permute-start(bf16[4,3,32,256]{3,2,1,0:T(8,128)(2,1)S(1)} %get-tuple-element.39.refs_4_), channel_id=1, source_target_pairs={{0,4},{4,0},{8,12},{12,8},{16,20},{20,16},{24,28},{28,24},{1,5},{5... | collective-permute-start | bytes 589832 | tf_op jit(solution)/shard_map/ppermute | solution.py:27
  17.8 6.9 %collective-permute-start.1 = (bf16[2,3,32,256]{3,2,1,0:T(8,128)(2,1)S(1)}, bf16[2,3,32,256]{3,2,1,0:T(8,128)(2,1)S(1)}, u32[]{:S(2)}, u32[]{:S(2)}) collective-permute-start(bf16[2,3,32,256]{3,2,1,0:T(8,128)(2,1)S(1)} %get-tuple-element.34), channel_id=1, source_target_pairs={{0,16},{4,20},{8,24},{12,28},{16,0},{20,4},{24,8},{28,12},{1,17},{... | collective-permute-start | bytes 294920 | tf_op jit(solution)/shard_map/ppermute | solution.py:27
  22.4 4.7 %collective-permute-start.4 = (bf16[2,3,32,256]{3,2,1,0:T(8,128)(2,1)S(1)}, bf16[2,3,32,256]{3,2,1,0:T(8,128)(2,1)S(1)}, u32[]{:S(2)}, u32[]{:S(2)}) collective-permute-start(bf16[2,3,32,256]{3,2,1,0:T(8,128)(2,1)S(1)} %get-tuple-element.41), channel_id=1, source_target_pairs={{0,8},{4,12},{8,0},{12,4},{16,24},{20,28},{24,16},{28,20},{1,9},{5... | collective-permute-start | bytes 294920 | tf_op jit(solution)/shard_map/ppermute | solution.py:27
  24.7 6.3 %collective-permute-start.2 = (bf16[1,3,32,256]{3,2,1,0:T(8,128)(2,1)S(1)}, bf16[1,3,32,256]{3,2,1,0:T(8,128)(2,1)S(1)}, u32[]{:S(2)}, u32[]{:S(2)}) collective-permute-start(bf16[1,3,32,256]{3,2,1,0:T(8,128)(2,1)S(1)} %get-tuple-element.36), channel_id=1, source_target_pairs={{0,4},{4,0},{8,12},{12,8},{16,20},{20,16},{24,28},{28,24},{1,5},{5... | collective-permute-start | bytes 147464 | tf_op jit(solution)/shard_map/ppermute | solution.py:27
  27.1 5.5 %collective-permute-start.5 = (bf16[1,3,32,256]{3,2,1,0:T(8,128)(2,1)S(1)}, bf16[1,3,32,256]{3,2,1,0:T(8,128)(2,1)S(1)}, u32[]{:S(2)}, u32[]{:S(2)}) collective-permute-start(bf16[1,3,32,256]{3,2,1,0:T(8,128)(2,1)S(1)} %get-tuple-element.43), channel_id=1, source_target_pairs={{0,16},{4,20},{8,24},{12,28},{16,0},{20,4},{24,8},{28,12},{1,17},{... | collective-permute-start | bytes 147464 | tf_op jit(solution)/shard_map/ppermute | solution.py:27
  32.8 4.4 %collective-permute-start.11 = (bf16[1,3,32,256]{3,2,1,0:T(8,128)(2,1)S(1)}, bf16[1,3,32,256]{3,2,1,0:T(8,128)(2,1)S(1)}, u32[]{:S(2)}, u32[]{:S(2)}) collective-permute-start(bf16[1,3,32,256]{3,2,1,0:T(8,128)(2,1)S(1)} %get-tuple-element.46.refs_0_), channel_id=1, source_target_pairs={{0,4},{4,0},{8,12},{12,8},{16,20},{20,16},{24,28},{28,24},{1,5},{5... | collective-permute-start | bytes 147464 | tf_op jit(solution)/shard_map/ppermute | solution.py:27
  34.4 5.6 %collective-permute-start.6 = (bf16[1,3,32,256]{3,2,1,0:T(8,128)(2,1)S(1)}, bf16[1,3,32,256]{3,2,1,0:T(8,128)(2,1)S(1)}, u32[]{:S(2)}, u32[]{:S(2)}) collective-permute-start(bf16[1,3,32,256]{3,2,1,0:T(8,128)(2,1)S(1)} %get-tuple-element.44.refs_0_), channel_id=1, source_target_pairs={{0,16},{4,20},{8,24},{12,28},{16,0},{20,4},{24,8},{28,12},{1,17},{... | collective-permute-start | bytes 147464 | tf_op jit(solution)/shard_map/ppermute | solution.py:27
  36.8 7.0 %collective-permute-start.9 = (bf16[192,384]{1,0:T(8,128)(2,1)S(1)}, bf16[192,384]{1,0:T(8,128)(2,1)S(1)}, u32[]{:S(2)}, u32[]{:S(2)}) collective-permute-start(bf16[192,384]{1,0:T(8,128)(2,1)S(1)} %get-tuple-element.45), channel_id=1, source_target_pairs={{0,2},{1,3},{2,0},{3,1},{4,6},{5,7},{6,4},{7,5},{8,10},{9,11},{10,... | collective-permute-start | bytes 442376 | tf_op jit(solution)/shard_map/ppermute | solution.py:27
  37.3 6.4 %collective-permute-start.12 = (bf16[2,3,32,256]{3,2,1,0:T(8,128)(2,1)S(1)}, bf16[2,3,32,256]{3,2,1,0:T(8,128)(2,1)S(1)}, u32[]{:S(2)}, u32[]{:S(2)}) collective-permute-start(bf16[2,3,32,256]{3,2,1,0:T(8,128)(2,1)S(1)} %join.6.refs_0_), channel_id=1, source_target_pairs={{0,16},{4,20},{8,24},{12,28},{16,0},{20,4},{24,8},{28,12},{1,17},{... | collective-permute-start | bytes 294920 | tf_op jit(solution)/shard_map/ppermute | solution.py:27
  40.0 5.8 %collective-permute-start.8 = (bf16[2,3,32,256]{3,2,1,0:T(8,128)(2,1)S(1)}, bf16[2,3,32,256]{3,2,1,0:T(8,128)(2,1)S(1)}, u32[]{:S(2)}, u32[]{:S(2)}) collective-permute-start(bf16[2,3,32,256]{3,2,1,0:T(8,128)(2,1)S(1)} %join.4.refs_0_), channel_id=1, source_target_pairs={{0,8},{4,12},{8,0},{12,4},{16,24},{20,28},{24,16},{28,20},{1,9},{5... | collective-permute-start | bytes 294920 | tf_op jit(solution)/shard_map/ppermute | solution.py:27
  41.3 9.9 %collective-permute-start.14 = (bf16[192,768]{1,0:T(8,128)(2,1)S(1)}, bf16[192,768]{1,0:T(8,128)(2,1)S(1)}, u32[]{:S(2)}, u32[]{:S(2)}) collective-permute-start(bf16[192,768]{1,0:T(8,128)(2,1)S(1)} %bitcast.17), channel_id=1, source_target_pairs={{0,2},{1,3},{2,0},{3,1},{4,6},{5,7},{6,4},{7,5},{8,10},{9,11},{10,... | collective-permute-start | bytes 884744 | tf_op jit(solution)/shard_map/ppermute | solution.py:27
  43.7 7.5 %collective-permute-start.13 = (bf16[4,3,32,256]{3,2,1,0:T(8,128)(2,1)S(1)}, bf16[4,3,32,256]{3,2,1,0:T(8,128)(2,1)S(1)}, u32[]{:S(2)}, u32[]{:S(2)}) collective-permute-start(bf16[4,3,32,256]{3,2,1,0:T(8,128)(2,1)S(1)} %join.7.refs_3_), channel_id=1, source_target_pairs={{0,8},{4,12},{8,0},{12,4},{16,24},{20,28},{24,16},{28,20},{1,9},{5... | collective-permute-start | bytes 589832 | tf_op jit(solution)/shard_map/ppermute | solution.py:27
  45.8 5.7 %collective-permute-start.10 = (bf16[4,3,32,256]{3,2,1,0:T(8,128)(2,1)S(1)}, bf16[4,3,32,256]{3,2,1,0:T(8,128)(2,1)S(1)}, u32[]{:S(2)}, u32[]{:S(2)}) collective-permute-start(bf16[4,3,32,256]{3,2,1,0:T(8,128)(2,1)S(1)} %join.5.refs_1_), channel_id=1, source_target_pairs={{0,4},{4,0},{8,12},{12,8},{16,20},{20,16},{24,28},{28,24},{1,5},{5... | collective-permute-start | bytes 589832 | tf_op jit(solution)/shard_map/ppermute | solution.py:27
  46.9 10.6 %collective-permute-start.15 = (bf16[192,768]{1,0:T(8,128)(2,1)S(1)}, bf16[192,768]{1,0:T(8,128)(2,1)S(1)}, u32[]{:S(2)}, u32[]{:S(2)}) collective-permute-start(bf16[192,768]{1,0:T(8,128)(2,1)S(1)} %bitcast.20), channel_id=1, source_target_pairs={{0,2},{1,3},{2,0},{3,1},{4,6},{5,7},{6,4},{7,5},{8,10},{9,11},{10,... | collective-permute-start | bytes 884744 | tf_op jit(solution)/shard_map/ppermute | solution.py:27
  52.2 19.3 %collective-permute-start.16 = (bf16[2,8,3,32,256]{4,3,2,1,0:T(8,128)(2,1)S(1)}, bf16[2,8,3,32,256]{4,3,2,1,0:T(8,128)(2,1)S(1)}, u32[]{:S(2)}, u32[]{:S(2)}) collective-permute-start(bf16[2,8,3,32,256]{4,3,2,1,0:T(8,128)(2,1)S(1)} %assemble.1.refs_1_), channel_id=1, source_target_pairs={{0,2},{1,3},{2,0},{3,1},{4,6},{5,7},{6,4},{7,5},{8,10},{9,11},{10,... | collective-permute-start | bytes 2359304 | tf_op jit(solution)/shard_map/ppermute | solution.py:27
  62.3 8.9 %collective-permute-start.17 = (bf16[4,96,576]{2,1,0:T(8,128)(2,1)S(1)}, bf16[4,96,576]{2,1,0:T(8,128)(2,1)S(1)}, u32[]{:S(2)}, u32[]{:S(2)}) collective-permute-start(bf16[4,96,576]{2,1,0:T(8,128)(2,1)S(1)} %get-tuple-element.48.refs_2_.refs_4_), channel_id=1, source_target_pairs={{0,4},{4,0},{8,12},{12,8},{16,20},{20,16},{24,28},{28,24},{1,5},{5... | collective-permute-start | bytes 1327112 | tf_op jit(solution)/shard_map/ppermute | solution.py:27
  71.8 6.3 %collective-permute-start.19 = (bf16[2,96,576]{2,1,0:T(8,128)(2,1)S(1)}, bf16[2,96,576]{2,1,0:T(8,128)(2,1)S(1)}, u32[]{:S(2)}, u32[]{:S(2)}) collective-permute-start(bf16[2,96,576]{2,1,0:T(8,128)(2,1)S(1)} %get-tuple-element.53), channel_id=1, source_target_pairs={{0,8},{4,12},{8,0},{12,4},{16,24},{20,28},{24,16},{28,20},{1,9},{5... | collective-permute-start | bytes 663560 | tf_op jit(solution)/shard_map/ppermute | solution.py:27
  76.5 5.5 %collective-permute-start.18 = (bf16[8,192,256]{2,1,0:T(8,128)(2,1)S(1)}, bf16[8,192,256]{2,1,0:T(8,128)(2,1)S(1)}, u32[]{:S(2)}, u32[]{:S(2)}) collective-permute-start(bf16[8,192,256]{2,1,0:T(8,128)(2,1)S(1)} %get-tuple-element.52), channel_id=1, source_target_pairs={{0,1},{1,0},{2,3},{3,2},{4,5},{5,4},{6,7},{7,6},{8,9},{9,8},{10,11... | collective-permute-start | bytes 2359304 | tf_op jit(solution)/shard_map/ppermute | solution.py:27
  79.5 2.5 %collective-permute-start.20 = (bf16[8,192,256]{2,1,0:T(8,128)(2,1)S(1)}, bf16[8,192,256]{2,1,0:T(8,128)(2,1)S(1)}, u32[]{:S(2)}, u32[]{:S(2)}) collective-permute-start(bf16[8,192,256]{2,1,0:T(8,128)(2,1)S(1)} %get-tuple-element.56), channel_id=1, source_target_pairs={{0,1},{1,0},{2,3},{3,2},{4,5},{5,4},{6,7},{7,6},{8,9},{9,8},{10,11... | collective-permute-start | bytes 2359304 | tf_op jit(solution)/shard_map/ppermute | solution.py:27
  79.6 9.3 %collective-permute-start.21 = (bf16[1,96,576]{2,1,0:T(8,128)(2,1)S(1)}, bf16[1,96,576]{2,1,0:T(8,128)(2,1)S(1)}, u32[]{:S(2)}, u32[]{:S(2)}) collective-permute-start(bf16[1,96,576]{2,1,0:T(8,128)(2,1)S(1)} %get-tuple-element.57), channel_id=1, source_target_pairs={{0,16},{4,20},{8,24},{12,28},{16,0},{20,4},{24,8},{28,12},{1,17},{... | collective-permute-start | bytes 331784 | tf_op jit(solution)/shard_map/ppermute | solution.py:27
  (2 other events, 17.4 us)

commit v18 on v17

--- a/solution.py
+++ b/solution.py
@@ -559,7 +559,7 @@
         logits = halve(*logits, "rows", turn_about)
         dprob = halve(*dprob, "rows", up)
         probs, dscore = softmax_back(logits, dprob, scale, [weights])
-        probs, probs_order = double(probs, "rows", up[::-1], [far_cot, fv])
+        probs, probs_order = double(probs, "rows", up[::-1], [far_cot])
         dscore, dscore_order = double(dscore, "rows", turn_about[::-1])
         scores = assemble(where, probs, dscore, (probs_order, dscore_order), shards, fq)
     else:
@@ -567,29 +567,32 @@
         scores = jnp.stack(softmax_back(logits, dprob, scale))
     far_scores = [flip(scores, "heads", f) for f in fars]
     grads = all_gradients(where, scores, qk, cot, "own_gradients", ())
-    parts = weight_part(where, held, grads, (3 * local,), shards, fk)
+    parts = weight_part(where, held, grads, (3 * local,), shards, fv)
     ready = [parts[-1]]
     far_qk = [far_query_key(where, held, *w, ready) for w in zip(fq, fk)]
     far_natural = [turn(where, *w, n_heads, ready) for w in zip(fq, fk, fv)]
     own = own_input(grads, weights, ready)
-    ready = [own] + far_qk + far_natural + far_scores
-    steps = [[], []]
+    ready = [own] + far_qk + far_natural
+    far_grads = []
+
+    def far_gradients(after):
+        for args in zip(far_scores, far_qk, far_cot):
+            far_grads.append(all_gradients(where, *args, "far_gradients", after))
+        return far_grads
+
+    steps = [[]]
     if direct:
         keep, give = parts
-        steps = []
         for bit in row_bits[:-1]:
             give, keep = add_split(keep, flip(give, "rows", bit), ready)
             steps.append([keep])
-            ready = ()
+            ready = far_grads or far_gradients(steps[-1])
         last = keep, flip(give, "rows", row_bits[-1])
     else:
         weight_grad = lax.psum_scatter(parts[0], "rows", scatter_dimension=0, tiled=True)
         weight_grad = weight_grad.reshape(width // n_rows, 3, local)
-
-    far_grads = [
-        all_gradients(where, *args, "far_gradients", steps[0])
-        for args in zip(far_scores, far_qk, far_cot)
-    ]
+    if not far_grads:
+        far_gradients(steps[-1])
     chunks = []
     for index, first in enumerate(range(0, row_dev, chunk)):
         after = steps[-1] if index else ()

time: 89.8 us -> 96.3 us (1.072)
  waiting for transfers between devices: 23.6 us -> 28.1 us
  starting transfers between devices: 31.5 us -> 33.5 us
    ppermute x22, waiting for transfers between devices: 23.6 us -> 28.1 us  [flip(): return lax.ppermute(values, axis, [(s, s ^ bit) for s in range(n)])]
    ppermute x22, starting transfers between devices: 31.5 us -> 33.5 us  [flip(): return lax.ppermute(values, axis, [(s, s ^ bit) for s in range(n)])]
  transfers between devices with their start and end apart: 22 -> 22, of which waited for: 14 -> 12; matrix products, arithmetic and copies ran while one was open for 0% -> 0% of each run, Pallas kernels for 36% -> 27%
where the time goes in v18:
time: 96.3 us; the launch traced here: 96.1 us
  Pallas kernels  33.5 us (35%)
  starting transfers between devices  33.5 us (35%)
  waiting for transfers between devices  28.1 us (29%)
    ppermute x22, starting transfers between devices, flip(): return lax.ppermute(values, axis, [(s, s ^ bit) for s in range(n)])  33.5 us
    pallas_call x24, Pallas kernels, in_vmem(): pl.pallas_call(run, in_specs=[SMEM] * scalars + [HBM] * streamed + [VMEM]...  32.1 us
    ppermute x22, waiting for transfers between devices, flip(): return lax.ppermute(values, axis, [(s, s ^ bit) for s in range(n)])  28.1 us
  transfers between devices with their start and end apart: 22, of which 12 were waited for; matrix products, arithmetic and copies ran while one was open for 0% of the time, Pallas kernels for 27%

profile of v18, /device:TPU:0, one launch (start us, length us, event | category | flops | bytes accessed | tf_op | source)
XLA Modules:
  0.0 96.1 jit_solution(10319101548382486037)
XLA Ops:
  0.7 7.0 %query_key.1 = (bf16[16,6,64,256]{3,2,1,0:T(8,128)(2,1)S(1)}, bf16[16,256,768]{2,1,0:T(8,128)(2,1)S(1)}, s32[1,16]{1,0:T(1,128)S(1)}, f32[4,3,32,256]{3,2,1,0:T(8,128)S(1)}, bf16[4,3,32,256]{3,2,1,0:T(8,128)(2,1)S(1)}) custom-call(s32[2]{0:T(128)S(1)} %pad_add_fusion.refs_0_, s32[1,16]{1,0:T(1,128)} %bitcast.24, bf16[16,256,768]{2,1,0:T(8,128)(2,1)} %refs_2_.1, ...), custom_call_target="tpu_custom_call" | custom-call | flops 2818572288 | bytes 16711748 | tf_op jit(solution)/shard_map/query_key/pallas_call | solution.py:56
  7.7 3.1 %collective-permute-start = (bf16[4,3,32,256]{3,2,1,0:T(8,128)(2,1)S(1)}, bf16[4,3,32,256]{3,2,1,0:T(8,128)(2,1)S(1)}, u32[]{:S(2)}, u32[]{:S(2)}) collective-permute-start(bf16[4,3,32,256]{3,2,1,0:T(8,128)(2,1)S(1)} %get-tuple-element.32.refs_4_), channel_id=1, source_target_pairs={{0,8},{4,12},{8,0},{12,4},{16,24},{20,28},{24,16},{28,20},{1,9},{5... | collective-permute-start | bytes 589832 | tf_op jit(solution)/shard_map/ppermute | solution.py:27
  12.4 3.7 %value_dprob.1 = (f32[4,3,32,256]{3,2,1,0:T(8,128)S(1)}, bf16[4,3,32,256]{3,2,1,0:T(8,128)(2,1)S(1)}, bf16[192,384]{1,0:T(8,128)(2,1)S(1)}) custom-call(s32[18]{0:T(128)S(1)} %pad_add_fusion.1.refs_0_, bf16[16,256,768]{2,1,0:T(8,128)(2,1)S(1)} %get-tuple-element.37.refs_1_, bf16[192,768]{1,0:T(8,128)(2,1)S(1)} %bitcast.13, ...), custom_call_target="tpu_custom_call" | custom-call | flops 12884901888 | bytes 8699940 | tf_op jit(solution)/shard_map/value_dprob/pallas_call | solution.py:56
  16.1 1.6 %collective-permute-start.3 = (bf16[4,3,32,256]{3,2,1,0:T(8,128)(2,1)S(1)}, bf16[4,3,32,256]{3,2,1,0:T(8,128)(2,1)S(1)}, u32[]{:S(2)}, u32[]{:S(2)}) collective-permute-start(bf16[4,3,32,256]{3,2,1,0:T(8,128)(2,1)S(1)} %get-tuple-element.39.refs_4_), channel_id=1, source_target_pairs={{0,4},{4,0},{8,12},{12,8},{16,20},{20,16},{24,28},{28,24},{1,5},{5... | collective-permute-start | bytes 589832 | tf_op jit(solution)/shard_map/ppermute | solution.py:27
  17.7 2.7 %collective-permute-start.1 = (bf16[2,3,32,256]{3,2,1,0:T(8,128)(2,1)S(1)}, bf16[2,3,32,256]{3,2,1,0:T(8,128)(2,1)S(1)}, u32[]{:S(2)}, u32[]{:S(2)}) collective-permute-start(bf16[2,3,32,256]{3,2,1,0:T(8,128)(2,1)S(1)} %get-tuple-element.34), channel_id=1, source_target_pairs={{0,16},{4,20},{8,24},{12,28},{16,0},{20,4},{24,8},{28,12},{1,17},{... | collective-permute-start | bytes 294920 | tf_op jit(solution)/shard_map/ppermute | solution.py:27
  20.4 1.9 %collective-permute-done.3.refs_1_ = bf16[4,3,32,256]{3,2,1,0:T(8,128)(2,1)S(1)} collective-permute-done((bf16[4,3,32,256]{3,2,1,0:T(8,128)(2,1)S(1)}, bf16[4,3,32,256]{3,2,1,0:T(8,128)(2,1)S(1)}, u32[]{:S(2)}, u32[]{:S(2)}) %collective-permute-start.3) | collective-permute-done | bytes 196640 | tf_op jit(solution)/shard_map/ppermute | solution.py:27
  22.8 1.7 %collective-permute-done.1.refs_1_ = bf16[2,3,32,256]{3,2,1,0:T(8,128)(2,1)S(1)} collective-permute-done((bf16[2,3,32,256]{3,2,1,0:T(8,128)(2,1)S(1)}, bf16[2,3,32,256]{3,2,1,0:T(8,128)(2,1)S(1)}, u32[]{:S(2)}, u32[]{:S(2)}) %collective-permute-start.1) | collective-permute-done | bytes 98336 | tf_op jit(solution)/shard_map/ppermute | solution.py:27
  25.1 1.9 %collective-permute-done.4.refs_1_ = bf16[2,3,32,256]{3,2,1,0:T(8,128)(2,1)S(1)} collective-permute-done((bf16[2,3,32,256]{3,2,1,0:T(8,128)(2,1)S(1)}, bf16[2,3,32,256]{3,2,1,0:T(8,128)(2,1)S(1)}, u32[]{:S(2)}, u32[]{:S(2)}) %collective-permute-start.4) | collective-permute-done | bytes 98336 | tf_op jit(solution)/shard_map/ppermute | solution.py:27
  27.0 2.9 %collective-permute-start.5 = (bf16[1,3,32,256]{3,2,1,0:T(8,128)(2,1)S(1)}, bf16[1,3,32,256]{3,2,1,0:T(8,128)(2,1)S(1)}, u32[]{:S(2)}, u32[]{:S(2)}) collective-permute-start(bf16[1,3,32,256]{3,2,1,0:T(8,128)(2,1)S(1)} %get-tuple-element.43), channel_id=1, source_target_pairs={{0,16},{4,20},{8,24},{12,28},{16,0},{20,4},{24,8},{28,12},{1,17},{... | collective-permute-start | bytes 147464 | tf_op jit(solution)/shard_map/ppermute | solution.py:27
  34.3 3.0 %collective-permute-start.6 = (bf16[1,3,32,256]{3,2,1,0:T(8,128)(2,1)S(1)}, bf16[1,3,32,256]{3,2,1,0:T(8,128)(2,1)S(1)}, u32[]{:S(2)}, u32[]{:S(2)}) collective-permute-start(bf16[1,3,32,256]{3,2,1,0:T(8,128)(2,1)S(1)} %get-tuple-element.44.refs_0_), channel_id=1, source_target_pairs={{0,16},{4,20},{8,24},{12,28},{16,0},{20,4},{24,8},{28,12},{1,17},{... | collective-permute-start | bytes 147464 | tf_op jit(solution)/shard_map/ppermute | solution.py:27
  37.3 2.1 %collective-permute-start.11 = (bf16[2,3,32,256]{3,2,1,0:T(8,128)(2,1)S(1)}, bf16[2,3,32,256]{3,2,1,0:T(8,128)(2,1)S(1)}, u32[]{:S(2)}, u32[]{:S(2)}) collective-permute-start(bf16[2,3,32,256]{3,2,1,0:T(8,128)(2,1)S(1)} %join.6.refs_0_), channel_id=1, source_target_pairs={{0,16},{4,20},{8,24},{12,28},{16,0},{20,4},{24,8},{28,12},{1,17},{... | collective-permute-start | bytes 294920 | tf_op jit(solution)/shard_map/ppermute | solution.py:27
  39.8 6.9 %collective-permute-done.7.refs_2_.refs_3_ = bf16[16,192,256]{2,1,0:T(8,128)(2,1)S(1)} collective-permute-done((bf16[16,192,256]{2,1,0:T(8,128)(2,1)S(1)}, bf16[16,192,256]{2,1,0:T(8,128)(2,1)S(1)}, u32[]{:S(2)}, u32[]{:S(2)}) %collective-permute-start.7) | collective-permute-done | bytes 1572896 | tf_op jit(solution)/shard_map/ppermute | solution.py:27
  47.1 1.6 %collective-permute-start.13 = (bf16[192,768]{1,0:T(8,128)(2,1)S(1)}, bf16[192,768]{1,0:T(8,128)(2,1)S(1)}, u32[]{:S(2)}, u32[]{:S(2)}) collective-permute-start(bf16[192,768]{1,0:T(8,128)(2,1)S(1)} %bitcast.17), channel_id=1, source_target_pairs={{0,2},{1,3},{2,0},{3,1},{4,6},{5,7},{6,4},{7,5},{8,10},{9,11},{10,... | collective-permute-start | bytes 884744 | tf_op jit(solution)/shard_map/ppermute | solution.py:27
  48.7 1.6 %collective-permute-start.12 = (bf16[4,3,32,256]{3,2,1,0:T(8,128)(2,1)S(1)}, bf16[4,3,32,256]{3,2,1,0:T(8,128)(2,1)S(1)}, u32[]{:S(2)}, u32[]{:S(2)}) collective-permute-start(bf16[4,3,32,256]{3,2,1,0:T(8,128)(2,1)S(1)} %join.7.refs_3_), channel_id=1, source_target_pairs={{0,8},{4,12},{8,0},{12,4},{16,24},{20,28},{24,16},{28,20},{1,9},{5... | collective-permute-start | bytes 589832 | tf_op jit(solution)/shard_map/ppermute | solution.py:27
  50.3 2.0 %collective-permute-done.8.refs_1_ = bf16[2,3,32,256]{3,2,1,0:T(8,128)(2,1)S(1)} collective-permute-done((bf16[2,3,32,256]{3,2,1,0:T(8,128)(2,1)S(1)}, bf16[2,3,32,256]{3,2,1,0:T(8,128)(2,1)S(1)}, u32[]{:S(2)}, u32[]{:S(2)}) %collective-permute-start.8) | collective-permute-done | bytes 98336 | tf_op jit(solution)/shard_map/ppermute | solution.py:27
  60.1 1.9 %own_gradients.1.refs_2_.refs_0_ = bf16[16,9,64,256]{3,2,1,0:T(8,128)(2,1)S(1)} custom-call(s32[18]{0:T(128)S(1)} %pad_add_fusion.1.refs_0_, bf16[2,8,3,32,256]{4,3,2,1,0:T(8,128)(2,1)S(1)} %assemble.1.refs_1_, bf16[16,6,64,256]{3,2,1,0:T(8,128)(2,1)S(1)} %get-tuple-element.46.refs_2_, bf16[16,192,256]{2,1,0:T(8,128)(2,1)S(1)} %bitcast.12), custom_call_target="tpu_custom_call" | custom-call | flops 1207959552 | bytes 10223652 | tf_op jit(solution)/shard_map/own_gradients/pallas_call | solution.py:56
  62.0 4.7 %weight_part.1 = (f32[4,96,576]{2,1,0:T(8,128)S(1)}, bf16[4,96,576]{2,1,0:T(8,128)(2,1)S(1)}) custom-call(s32[18]{0:T(128)S(1)} %pad_add_fusion.1.refs_0_, bf16[16,256,768]{2,1,0:T(8,128)(2,1)S(1)} %get-tuple-element.37.refs_1_, bf16[16,9,64,256]{3,2,1,0:T(8,128)(2,1)S(1)} %own_gradients.1.refs_2_.refs_0_, bf16[192,384]{1,0:T(8,128)(2,1)S(1)} %collective-permute-done.14.refs_3_), custom_call_target="tpu_custom_call" | custom-call | flops 3623878656 | bytes 11894820 | tf_op jit(solution)/shard_map/weight_part/pallas_call | solution.py:56
  66.8 1.6 %collective-permute-start.17 = (bf16[4,96,576]{2,1,0:T(8,128)(2,1)S(1)}, bf16[4,96,576]{2,1,0:T(8,128)(2,1)S(1)}, u32[]{:S(2)}, u32[]{:S(2)}) collective-permute-start(bf16[4,96,576]{2,1,0:T(8,128)(2,1)S(1)} %get-tuple-element.48.refs_2_.refs_4_), channel_id=1, source_target_pairs={{0,4},{4,0},{8,12},{12,8},{16,20},{20,16},{24,28},{28,24},{1,5},{5... | collective-permute-start | bytes 1327112 | tf_op jit(solution)/shard_map/ppermute | solution.py:27
  69.4 2.6 %own_input.1.refs_2_.refs_0_ = bf16[2,16,192,256]{3,2,1,0:T(8,128)(2,1)S(1)} custom-call(bf16[16,9,64,256]{3,2,1,0:T(8,128)(2,1)S(1)} %own_gradients.1.refs_2_.refs_0_, bf16[2,192,576]{2,1,0:T(8,128)(2,1)S(1)} %turn.2.refs_4_.refs_1_, bf16[4,96,576]{2,1,0:T(8,128)(2,1)S(1)} %get-tuple-element.48.refs_2_.refs_4_), custom_call_target="tpu_custom_call" | custom-call | flops 1811939328 | bytes 8306688 | tf_op jit(solution)/shard_map/own_input/pallas_call | solution.py:56
  72.0 3.2 %far_query_key.1.refs_3_.refs_2_ = bf16[16,6,64,256]{3,2,1,0:T(8,128)(2,1)S(1)} custom-call(s32[18]{0:T(128)S(1)} %pad_add_fusion.1.refs_0_, bf16[16,256,768]{2,1,0:T(8,128)(2,1)S(1)} %get-tuple-element.37.refs_1_, bf16[192,768]{1,0:T(8,128)(2,1)S(1)} %collective-permute-done.13.refs_5_.refs_2_.refs_1_, ...), custom_call_target="tpu_custom_call" | custom-call | flops 2415919104 | bytes 10027044 | tf_op jit(solution)/shard_map/far_query_key/pallas_call | solution.py:56
  76.8 4.2 %collective-permute-done.15.refs_1_ = bf16[2,8,3,32,256]{4,3,2,1,0:T(8,128)(2,1)S(1)} collective-permute-done((bf16[2,8,3,32,256]{4,3,2,1,0:T(8,128)(2,1)S(1)}, bf16[2,8,3,32,256]{4,3,2,1,0:T(8,128)(2,1)S(1)}, u32[]{:S(2)}, u32[]{:S(2)}) %collective-permute-start.15) | collective-permute-done | bytes 786464 | tf_op jit(solution)/shard_map/ppermute | solution.py:27
  81.0 1.9 %far_gradients.1.refs_1_.refs_2_ = bf16[16,9,64,256]{3,2,1,0:T(8,128)(2,1)S(1)} custom-call(s32[18]{0:T(128)S(1)} %pad_add_fusion.1.refs_0_, bf16[2,8,3,32,256]{4,3,2,1,0:T(8,128)(2,1)S(1)} %collective-permute-done.15.refs_1_, bf16[16,6,64,256]{3,2,1,0:T(8,128)(2,1)S(1)} %far_query_key.1.refs_3_.refs_2_, ...), custom_call_target="tpu_custom_call" | custom-call | flops 1207959552 | bytes 10223652 | tf_op jit(solution)/shard_map/far_gradients/pallas_call | solution.py:56
  86.4 2.4 %collective-permute-start.21 = (bf16[1,96,576]{2,1,0:T(8,128)(2,1)S(1)}, bf16[1,96,576]{2,1,0:T(8,128)(2,1)S(1)}, u32[]{:S(2)}, u32[]{:S(2)}) collective-permute-start(bf16[1,96,576]{2,1,0:T(8,128)(2,1)S(1)} %get-tuple-element.57), channel_id=1, source_target_pairs={{0,16},{4,20},{8,24},{12,28},{16,0},{20,4},{24,8},{28,12},{1,17},{... | collective-permute-start | bytes 331784 | tf_op jit(solution)/shard_map/ppermute | solution.py:27
  90.2 5.1 %collective-permute-done.21.refs_2_ = bf16[1,96,576]{2,1,0:T(8,128)(2,1)S(1)} collective-permute-done((bf16[1,96,576]{2,1,0:T(8,128)(2,1)S(1)}, bf16[1,96,576]{2,1,0:T(8,128)(2,1)S(1)}, u32[]{:S(2)}, u32[]{:S(2)}) %collective-permute-start.21) | collective-permute-done | bytes 110624 | tf_op jit(solution)/shard_map/ppermute | solution.py:27
  (55 shorter events, 24.2 us)
Async XLA Ops:
  7.7 10.0 %collective-permute-start = (bf16[4,3,32,256]{3,2,1,0:T(8,128)(2,1)S(1)}, bf16[4,3,32,256]{3,2,1,0:T(8,128)(2,1)S(1)}, u32[]{:S(2)}, u32[]{:S(2)}) collective-permute-start(bf16[4,3,32,256]{3,2,1,0:T(8,128)(2,1)S(1)} %get-tuple-element.32.refs_4_), channel_id=1, source_target_pairs={{0,8},{4,12},{8,0},{12,4},{16,24},{20,28},{24,16},{28,20},{1,9},{5... | collective-permute-start | bytes 589832 | tf_op jit(solution)/shard_map/ppermute | solution.py:27
  10.8 35.9 %collective-permute-start.7 = (bf16[16,192,256]{2,1,0:T(8,128)(2,1)S(1)}, bf16[16,192,256]{2,1,0:T(8,128)(2,1)S(1)}, u32[]{:S(2)}, u32[]{:S(2)}) collective-permute-start(bf16[16,192,256]{2,1,0:T(8,128)(2,1)S(1)} %bitcast.10), channel_id=1, source_target_pairs={{0,2},{1,3},{2,0},{3,1},{4,6},{5,7},{6,4},{7,5},{8,10},{9,11},{10,... | collective-permute-start | bytes 4718600 | tf_op jit(solution)/shard_map/ppermute | solution.py:27
  12.4 17.5 %copy-start.2 = (bf16[768,192]{0,1:T(8,128)(2,1)S(1)}, bf16[768,192]{0,1:T(8,128)(2,1)}, u32[]{:S(2)}) copy-start(bf16[768,192]{0,1:T(8,128)(2,1)} %param.7) | copy-start | bytes 884740
  12.4 17.5 %copy-start.3 = (bf16[768,192]{0,1:T(8,128)(2,1)S(1)}, bf16[768,192]{0,1:T(8,128)(2,1)}, u32[]{:S(2)}) copy-start(bf16[768,192]{0,1:T(8,128)(2,1)} %param.8) | copy-start | bytes 884740
  16.1 6.1 %collective-permute-start.3 = (bf16[4,3,32,256]{3,2,1,0:T(8,128)(2,1)S(1)}, bf16[4,3,32,256]{3,2,1,0:T(8,128)(2,1)S(1)}, u32[]{:S(2)}, u32[]{:S(2)}) collective-permute-start(bf16[4,3,32,256]{3,2,1,0:T(8,128)(2,1)S(1)} %get-tuple-element.39.refs_4_), channel_id=1, source_target_pairs={{0,4},{4,0},{8,12},{12,8},{16,20},{20,16},{24,28},{28,24},{1,5},{5... | collective-permute-start | bytes 589832 | tf_op jit(solution)/shard_map/ppermute | solution.py:27
  17.7 6.8 %collective-permute-start.1 = (bf16[2,3,32,256]{3,2,1,0:T(8,128)(2,1)S(1)}, bf16[2,3,32,256]{3,2,1,0:T(8,128)(2,1)S(1)}, u32[]{:S(2)}, u32[]{:S(2)}) collective-permute-start(bf16[2,3,32,256]{3,2,1,0:T(8,128)(2,1)S(1)} %get-tuple-element.34), channel_id=1, source_target_pairs={{0,16},{4,20},{8,24},{12,28},{16,0},{20,4},{24,8},{28,12},{1,17},{... | collective-permute-start | bytes 294920 | tf_op jit(solution)/shard_map/ppermute | solution.py:27
  22.3 4.7 %collective-permute-start.4 = (bf16[2,3,32,256]{3,2,1,0:T(8,128)(2,1)S(1)}, bf16[2,3,32,256]{3,2,1,0:T(8,128)(2,1)S(1)}, u32[]{:S(2)}, u32[]{:S(2)}) collective-permute-start(bf16[2,3,32,256]{3,2,1,0:T(8,128)(2,1)S(1)} %get-tuple-element.41), channel_id=1, source_target_pairs={{0,8},{4,12},{8,0},{12,4},{16,24},{20,28},{24,16},{28,20},{1,9},{5... | collective-permute-start | bytes 294920 | tf_op jit(solution)/shard_map/ppermute | solution.py:27
  24.5 6.4 %collective-permute-start.2 = (bf16[1,3,32,256]{3,2,1,0:T(8,128)(2,1)S(1)}, bf16[1,3,32,256]{3,2,1,0:T(8,128)(2,1)S(1)}, u32[]{:S(2)}, u32[]{:S(2)}) collective-permute-start(bf16[1,3,32,256]{3,2,1,0:T(8,128)(2,1)S(1)} %get-tuple-element.36), channel_id=1, source_target_pairs={{0,4},{4,0},{8,12},{12,8},{16,20},{20,16},{24,28},{28,24},{1,5},{5... | collective-permute-start | bytes 147464 | tf_op jit(solution)/shard_map/ppermute | solution.py:27
  27.0 5.5 %collective-permute-start.5 = (bf16[1,3,32,256]{3,2,1,0:T(8,128)(2,1)S(1)}, bf16[1,3,32,256]{3,2,1,0:T(8,128)(2,1)S(1)}, u32[]{:S(2)}, u32[]{:S(2)}) collective-permute-start(bf16[1,3,32,256]{3,2,1,0:T(8,128)(2,1)S(1)} %get-tuple-element.43), channel_id=1, source_target_pairs={{0,16},{4,20},{8,24},{12,28},{16,0},{20,4},{24,8},{28,12},{1,17},{... | collective-permute-start | bytes 147464 | tf_op jit(solution)/shard_map/ppermute | solution.py:27
  32.8 4.5 %collective-permute-start.10 = (bf16[1,3,32,256]{3,2,1,0:T(8,128)(2,1)S(1)}, bf16[1,3,32,256]{3,2,1,0:T(8,128)(2,1)S(1)}, u32[]{:S(2)}, u32[]{:S(2)}) collective-permute-start(bf16[1,3,32,256]{3,2,1,0:T(8,128)(2,1)S(1)} %get-tuple-element.45.refs_0_), channel_id=1, source_target_pairs={{0,4},{4,0},{8,12},{12,8},{16,20},{20,16},{24,28},{28,24},{1,5},{5... | collective-permute-start | bytes 147464 | tf_op jit(solution)/shard_map/ppermute | solution.py:27
  34.3 5.4 %collective-permute-start.6 = (bf16[1,3,32,256]{3,2,1,0:T(8,128)(2,1)S(1)}, bf16[1,3,32,256]{3,2,1,0:T(8,128)(2,1)S(1)}, u32[]{:S(2)}, u32[]{:S(2)}) collective-permute-start(bf16[1,3,32,256]{3,2,1,0:T(8,128)(2,1)S(1)} %get-tuple-element.44.refs_0_), channel_id=1, source_target_pairs={{0,16},{4,20},{8,24},{12,28},{16,0},{20,4},{24,8},{28,12},{1,17},{... | collective-permute-start | bytes 147464 | tf_op jit(solution)/shard_map/ppermute | solution.py:27
  37.3 11.4 %collective-permute-start.11 = (bf16[2,3,32,256]{3,2,1,0:T(8,128)(2,1)S(1)}, bf16[2,3,32,256]{3,2,1,0:T(8,128)(2,1)S(1)}, u32[]{:S(2)}, u32[]{:S(2)}) collective-permute-start(bf16[2,3,32,256]{3,2,1,0:T(8,128)(2,1)S(1)} %join.6.refs_0_), channel_id=1, source_target_pairs={{0,16},{4,20},{8,24},{12,28},{16,0},{20,4},{24,8},{28,12},{1,17},{... | collective-permute-start | bytes 294920 | tf_op jit(solution)/shard_map/ppermute | solution.py:27
  46.6 5.7 %collective-permute-start.8 = (bf16[2,3,32,256]{3,2,1,0:T(8,128)(2,1)S(1)}, bf16[2,3,32,256]{3,2,1,0:T(8,128)(2,1)S(1)}, u32[]{:S(2)}, u32[]{:S(2)}) collective-permute-start(bf16[2,3,32,256]{3,2,1,0:T(8,128)(2,1)S(1)} %join.4.refs_0_), channel_id=1, source_target_pairs={{0,8},{4,12},{8,0},{12,4},{16,24},{20,28},{24,16},{28,20},{1,9},{5... | collective-permute-start | bytes 294920 | tf_op jit(solution)/shard_map/ppermute | solution.py:27
  47.1 9.5 %collective-permute-start.13 = (bf16[192,768]{1,0:T(8,128)(2,1)S(1)}, bf16[192,768]{1,0:T(8,128)(2,1)S(1)}, u32[]{:S(2)}, u32[]{:S(2)}) collective-permute-start(bf16[192,768]{1,0:T(8,128)(2,1)S(1)} %bitcast.17), channel_id=1, source_target_pairs={{0,2},{1,3},{2,0},{3,1},{4,6},{5,7},{6,4},{7,5},{8,10},{9,11},{10,... | collective-permute-start | bytes 884744 | tf_op jit(solution)/shard_map/ppermute | solution.py:27
  48.7 7.9 %collective-permute-start.12 = (bf16[4,3,32,256]{3,2,1,0:T(8,128)(2,1)S(1)}, bf16[4,3,32,256]{3,2,1,0:T(8,128)(2,1)S(1)}, u32[]{:S(2)}, u32[]{:S(2)}) collective-permute-start(bf16[4,3,32,256]{3,2,1,0:T(8,128)(2,1)S(1)} %join.7.refs_3_), channel_id=1, source_target_pairs={{0,8},{4,12},{8,0},{12,4},{16,24},{20,28},{24,16},{28,20},{1,9},{5... | collective-permute-start | bytes 589832 | tf_op jit(solution)/shard_map/ppermute | solution.py:27
  52.4 5.7 %collective-permute-start.9 = (bf16[4,3,32,256]{3,2,1,0:T(8,128)(2,1)S(1)}, bf16[4,3,32,256]{3,2,1,0:T(8,128)(2,1)S(1)}, u32[]{:S(2)}, u32[]{:S(2)}) collective-permute-start(bf16[4,3,32,256]{3,2,1,0:T(8,128)(2,1)S(1)} %join.5.refs_1_), channel_id=1, source_target_pairs={{0,4},{4,0},{8,12},{12,8},{16,20},{20,16},{24,28},{28,24},{1,5},{5... | collective-permute-start | bytes 589832 | tf_op jit(solution)/shard_map/ppermute | solution.py:27
  53.9 8.1 %collective-permute-start.14 = (bf16[192,384]{1,0:T(8,128)(2,1)S(1)}, bf16[192,384]{1,0:T(8,128)(2,1)S(1)}, u32[]{:S(2)}, u32[]{:S(2)}) collective-permute-start(bf16[192,384]{1,0:T(8,128)(2,1)S(1)} %get-tuple-element.47), channel_id=1, source_target_pairs={{0,2},{1,3},{2,0},{3,1},{4,6},{5,7},{6,4},{7,5},{8,10},{9,11},{10,... | collective-permute-start | bytes 442376 | tf_op jit(solution)/shard_map/ppermute | solution.py:27
  55.3 13.1 %collective-permute-start.16 = (bf16[192,768]{1,0:T(8,128)(2,1)S(1)}, bf16[192,768]{1,0:T(8,128)(2,1)S(1)}, u32[]{:S(2)}, u32[]{:S(2)}) collective-permute-start(bf16[192,768]{1,0:T(8,128)(2,1)S(1)} %bitcast.20), channel_id=1, source_target_pairs={{0,2},{1,3},{2,0},{3,1},{4,6},{5,7},{6,4},{7,5},{8,10},{9,11},{10,... | collective-permute-start | bytes 884744 | tf_op jit(solution)/shard_map/ppermute | solution.py:27
  58.7 22.3 %collective-permute-start.15 = (bf16[2,8,3,32,256]{4,3,2,1,0:T(8,128)(2,1)S(1)}, bf16[2,8,3,32,256]{4,3,2,1,0:T(8,128)(2,1)S(1)}, u32[]{:S(2)}, u32[]{:S(2)}) collective-permute-start(bf16[2,8,3,32,256]{4,3,2,1,0:T(8,128)(2,1)S(1)} %assemble.1.refs_1_), channel_id=1, source_target_pairs={{0,2},{1,3},{2,0},{3,1},{4,6},{5,7},{6,4},{7,5},{8,10},{9,11},{10,... | collective-permute-start | bytes 2359304 | tf_op jit(solution)/shard_map/ppermute | solution.py:27
  66.8 8.9 %collective-permute-start.17 = (bf16[4,96,576]{2,1,0:T(8,128)(2,1)S(1)}, bf16[4,96,576]{2,1,0:T(8,128)(2,1)S(1)}, u32[]{:S(2)}, u32[]{:S(2)}) collective-permute-start(bf16[4,96,576]{2,1,0:T(8,128)(2,1)S(1)} %get-tuple-element.48.refs_2_.refs_4_), channel_id=1, source_target_pairs={{0,4},{4,0},{8,12},{12,8},{16,20},{20,16},{24,28},{28,24},{1,5},{5... | collective-permute-start | bytes 1327112 | tf_op jit(solution)/shard_map/ppermute | solution.py:27
  76.0 8.4 %collective-permute-start.19 = (bf16[2,96,576]{2,1,0:T(8,128)(2,1)S(1)}, bf16[2,96,576]{2,1,0:T(8,128)(2,1)S(1)}, u32[]{:S(2)}, u32[]{:S(2)}) collective-permute-start(bf16[2,96,576]{2,1,0:T(8,128)(2,1)S(1)} %get-tuple-element.53), channel_id=1, source_target_pairs={{0,8},{4,12},{8,0},{12,4},{16,24},{20,28},{24,16},{28,20},{1,9},{5... | collective-permute-start | bytes 663560 | tf_op jit(solution)/shard_map/ppermute | solution.py:27
  84.3 4.5 %collective-permute-start.18 = (bf16[8,192,256]{2,1,0:T(8,128)(2,1)S(1)}, bf16[8,192,256]{2,1,0:T(8,128)(2,1)S(1)}, u32[]{:S(2)}, u32[]{:S(2)}) collective-permute-start(bf16[8,192,256]{2,1,0:T(8,128)(2,1)S(1)} %get-tuple-element.52), channel_id=1, source_target_pairs={{0,1},{1,0},{2,3},{3,2},{4,5},{5,4},{6,7},{7,6},{8,9},{9,8},{10,11... | collective-permute-start | bytes 2359304 | tf_op jit(solution)/shard_map/ppermute | solution.py:27
  85.9 2.9 %collective-permute-start.20 = (bf16[8,192,256]{2,1,0:T(8,128)(2,1)S(1)}, bf16[8,192,256]{2,1,0:T(8,128)(2,1)S(1)}, u32[]{:S(2)}, u32[]{:S(2)}) collective-permute-start(bf16[8,192,256]{2,1,0:T(8,128)(2,1)S(1)} %get-tuple-element.56), channel_id=1, source_target_pairs={{0,1},{1,0},{2,3},{3,2},{4,5},{5,4},{6,7},{7,6},{8,9},{9,8},{10,11... | collective-permute-start | bytes 2359304 | tf_op jit(solution)/shard_map/ppermute | solution.py:27
  86.4 8.8 %collective-permute-start.21 = (bf16[1,96,576]{2,1,0:T(8,128)(2,1)S(1)}, bf16[1,96,576]{2,1,0:T(8,128)(2,1)S(1)}, u32[]{:S(2)}, u32[]{:S(2)}) collective-permute-start(bf16[1,96,576]{2,1,0:T(8,128)(2,1)S(1)} %get-tuple-element.57), channel_id=1, source_target_pairs={{0,16},{4,20},{8,24},{12,28},{16,0},{20,4},{24,8},{28,12},{1,17},{... | collective-permute-start | bytes 331784 | tf_op jit(solution)/shard_map/ppermute | solution.py:27
  (2 other events, 21.7 us)

commit v19 on v18

--- a/solution.py
+++ b/solution.py
@@ -147,7 +147,7 @@
             pltpu.SemaphoreType.DMA((4 + rows // STEP,)),
         ),
         limit=14,
-        flops=2 * rows * cols * local * (2 * width + cols),
+        flops=rows * cols * local * (2 * width + cols) // 2,
     )
 
 
@@ -194,7 +194,7 @@
         after=after,
         scratch=(pltpu.VMEM((heads, shards, cols // shards, cols), F32),),
         limit=16,
-        flops=16 * rows * cols * local * (width + cols),
+        flops=4 * rows * cols * local * (width + cols),
     )
 
 

time: 96.3 us -> 89.4 us (0.928)
  starting transfers between devices: 33.5 us -> 29.9 us
  waiting for transfers between devices: 28.1 us -> 24.8 us
    ppermute x22, starting transfers between devices: 33.5 us -> 29.9 us  [flip(): return lax.ppermute(values, axis, [(s, s ^ bit) for s in range(n)])]
    ppermute x22, waiting for transfers between devices: 28.1 us -> 24.8 us  [flip(): return lax.ppermute(values, axis, [(s, s ^ bit) for s in range(n)])]
  transfers between devices with their start and end apart: 22 -> 22, of which waited for: 12 -> 13; matrix products, arithmetic and copies ran while one was open for 0% -> 0% of each run, Pallas kernels for 27% -> 37%
where the time goes in v19:
time: 89.4 us; the launch traced here: 89.2 us
  Pallas kernels  33.5 us (37%)
  starting transfers between devices  29.9 us (33%)
  waiting for transfers between devices  24.8 us (28%)
    pallas_call x24, Pallas kernels, in_vmem(): pl.pallas_call(run, in_specs=[SMEM] * scalars + [HBM] * streamed + [VMEM]...  32.1 us
    ppermute x22, starting transfers between devices, flip(): return lax.ppermute(values, axis, [(s, s ^ bit) for s in range(n)])  29.9 us
    ppermute x22, waiting for transfers between devices, flip(): return lax.ppermute(values, axis, [(s, s ^ bit) for s in range(n)])  24.8 us
  transfers between devices with their start and end apart: 22, of which 13 were waited for; matrix products, arithmetic and copies ran while one was open for 0% of the time, Pallas kernels for 37%

profile of v19, /device:TPU:0, one launch (start us, length us, event | category | flops | bytes accessed | tf_op | source)
XLA Modules:
  0.0 89.2 jit_solution(5061407744122386640)
XLA Ops:
  0.6 3.0 %collective-permute-start.7 = (bf16[16,192,256]{2,1,0:T(8,128)(2,1)}, bf16[16,192,256]{2,1,0:T(8,128)(2,1)S(1)}, u32[]{:S(2)}, u32[]{:S(2)}) collective-permute-start(bf16[16,192,256]{2,1,0:T(8,128)(2,1)} %bitcast.10), channel_id=1, source_target_pairs={{0,2},{1,3},{2,0},{3,1},{4,6},{5,7},{6,4},{7,5},{8,10},{9,11},{10,... | collective-permute-start | bytes 4718600 | tf_op jit(solution)/shard_map/ppermute | solution.py:27
  3.7 7.0 %query_key.1 = (bf16[16,6,64,256]{3,2,1,0:T(8,128)(2,1)S(1)}, bf16[16,256,768]{2,1,0:T(8,128)(2,1)S(1)}, s32[1,16]{1,0:T(1,128)S(1)}, f32[4,3,32,256]{3,2,1,0:T(8,128)S(1)}, bf16[4,3,32,256]{3,2,1,0:T(8,128)(2,1)S(1)}) custom-call(s32[2]{0:T(128)S(1)} %pad_add_fusion.refs_0_, s32[1,16]{1,0:T(1,128)} %bitcast.24, bf16[16,256,768]{2,1,0:T(8,128)(2,1)} %refs_2_.1, ...), custom_call_target="tpu_custom_call" | custom-call | flops 704643072 | bytes 16711748 | tf_op jit(solution)/shard_map/query_key/pallas_call | solution.py:56
  10.7 1.6 %collective-permute-start = (bf16[4,3,32,256]{3,2,1,0:T(8,128)(2,1)S(1)}, bf16[4,3,32,256]{3,2,1,0:T(8,128)(2,1)S(1)}, u32[]{:S(2)}, u32[]{:S(2)}) collective-permute-start(bf16[4,3,32,256]{3,2,1,0:T(8,128)(2,1)S(1)} %get-tuple-element.32.refs_4_), channel_id=1, source_target_pairs={{0,8},{4,12},{8,0},{12,4},{16,24},{20,28},{24,16},{28,20},{1,9},{5... | collective-permute-start | bytes 589832 | tf_op jit(solution)/shard_map/ppermute | solution.py:27
  12.5 3.7 %value_dprob.1 = (f32[4,3,32,256]{3,2,1,0:T(8,128)S(1)}, bf16[4,3,32,256]{3,2,1,0:T(8,128)(2,1)S(1)}, bf16[192,384]{1,0:T(8,128)(2,1)S(1)}) custom-call(s32[18]{0:T(128)S(1)} %pad_add_fusion.1.refs_0_, bf16[16,256,768]{2,1,0:T(8,128)(2,1)S(1)} %get-tuple-element.37.refs_1_, bf16[192,768]{1,0:T(8,128)(2,1)S(1)} %bitcast.19, ...), custom_call_target="tpu_custom_call" | custom-call | flops 3221225472 | bytes 8699940 | tf_op jit(solution)/shard_map/value_dprob/pallas_call | solution.py:56
  16.2 1.6 %collective-permute-start.3 = (bf16[4,3,32,256]{3,2,1,0:T(8,128)(2,1)S(1)}, bf16[4,3,32,256]{3,2,1,0:T(8,128)(2,1)S(1)}, u32[]{:S(2)}, u32[]{:S(2)}) collective-permute-start(bf16[4,3,32,256]{3,2,1,0:T(8,128)(2,1)S(1)} %get-tuple-element.39.refs_4_), channel_id=1, source_target_pairs={{0,4},{4,0},{8,12},{12,8},{16,20},{20,16},{24,28},{28,24},{1,5},{5... | collective-permute-start | bytes 589832 | tf_op jit(solution)/shard_map/ppermute | solution.py:27
  17.8 2.7 %collective-permute-start.1 = (bf16[2,3,32,256]{3,2,1,0:T(8,128)(2,1)S(1)}, bf16[2,3,32,256]{3,2,1,0:T(8,128)(2,1)S(1)}, u32[]{:S(2)}, u32[]{:S(2)}) collective-permute-start(bf16[2,3,32,256]{3,2,1,0:T(8,128)(2,1)S(1)} %get-tuple-element.34), channel_id=1, source_target_pairs={{0,16},{4,20},{8,24},{12,28},{16,0},{20,4},{24,8},{28,12},{1,17},{... | collective-permute-start | bytes 294920 | tf_op jit(solution)/shard_map/ppermute | solution.py:27
  20.4 1.9 %collective-permute-done.3.refs_1_ = bf16[4,3,32,256]{3,2,1,0:T(8,128)(2,1)S(1)} collective-permute-done((bf16[4,3,32,256]{3,2,1,0:T(8,128)(2,1)S(1)}, bf16[4,3,32,256]{3,2,1,0:T(8,128)(2,1)S(1)}, u32[]{:S(2)}, u32[]{:S(2)}) %collective-permute-start.3) | collective-permute-done | bytes 196640 | tf_op jit(solution)/shard_map/ppermute | solution.py:27
  22.9 1.8 %collective-permute-done.1.refs_1_ = bf16[2,3,32,256]{3,2,1,0:T(8,128)(2,1)S(1)} collective-permute-done((bf16[2,3,32,256]{3,2,1,0:T(8,128)(2,1)S(1)}, bf16[2,3,32,256]{3,2,1,0:T(8,128)(2,1)S(1)}, u32[]{:S(2)}, u32[]{:S(2)}) %collective-permute-start.1) | collective-permute-done | bytes 98336 | tf_op jit(solution)/shard_map/ppermute | solution.py:27
  24.8 2.3 %collective-permute-done.4.refs_1_ = bf16[2,3,32,256]{3,2,1,0:T(8,128)(2,1)S(1)} collective-permute-done((bf16[2,3,32,256]{3,2,1,0:T(8,128)(2,1)S(1)}, bf16[2,3,32,256]{3,2,1,0:T(8,128)(2,1)S(1)}, u32[]{:S(2)}, u32[]{:S(2)}) %collective-permute-start.4) | collective-permute-done | bytes 98336 | tf_op jit(solution)/shard_map/ppermute | solution.py:27
  27.1 2.8 %collective-permute-start.5 = (bf16[1,3,32,256]{3,2,1,0:T(8,128)(2,1)S(1)}, bf16[1,3,32,256]{3,2,1,0:T(8,128)(2,1)S(1)}, u32[]{:S(2)}, u32[]{:S(2)}) collective-permute-start(bf16[1,3,32,256]{3,2,1,0:T(8,128)(2,1)S(1)} %get-tuple-element.43), channel_id=1, source_target_pairs={{0,16},{4,20},{8,24},{12,28},{16,0},{20,4},{24,8},{28,12},{1,17},{... | collective-permute-start | bytes 147464 | tf_op jit(solution)/shard_map/ppermute | solution.py:27
  31.0 1.6 %collective-permute-done.5.refs_3_ = bf16[1,3,32,256]{3,2,1,0:T(8,128)(2,1)S(1)} collective-permute-done((bf16[1,3,32,256]{3,2,1,0:T(8,128)(2,1)S(1)}, bf16[1,3,32,256]{3,2,1,0:T(8,128)(2,1)S(1)}, u32[]{:S(2)}, u32[]{:S(2)}) %collective-permute-start.5) | collective-permute-done | bytes 49184 | tf_op jit(solution)/shard_map/ppermute | solution.py:27
  32.8 1.6 %collective-permute-start.10 = (bf16[1,3,32,256]{3,2,1,0:T(8,128)(2,1)S(1)}, bf16[1,3,32,256]{3,2,1,0:T(8,128)(2,1)S(1)}, u32[]{:S(2)}, u32[]{:S(2)}) collective-permute-start(bf16[1,3,32,256]{3,2,1,0:T(8,128)(2,1)S(1)} %get-tuple-element.45.refs_0_), channel_id=1, source_target_pairs={{0,4},{4,0},{8,12},{12,8},{16,20},{20,16},{24,28},{28,24},{1,5},{5... | collective-permute-start | bytes 147464 | tf_op jit(solution)/shard_map/ppermute | solution.py:27
  34.4 2.4 %collective-permute-start.6 = (bf16[1,3,32,256]{3,2,1,0:T(8,128)(2,1)S(1)}, bf16[1,3,32,256]{3,2,1,0:T(8,128)(2,1)S(1)}, u32[]{:S(2)}, u32[]{:S(2)}) collective-permute-start(bf16[1,3,32,256]{3,2,1,0:T(8,128)(2,1)S(1)} %get-tuple-element.44.refs_0_), channel_id=1, source_target_pairs={{0,16},{4,20},{8,24},{12,28},{16,0},{20,4},{24,8},{28,12},{1,17},{... | collective-permute-start | bytes 147464 | tf_op jit(solution)/shard_map/ppermute | solution.py:27
  37.0 2.4 %collective-permute-start.11 = (bf16[2,3,32,256]{3,2,1,0:T(8,128)(2,1)S(1)}, bf16[2,3,32,256]{3,2,1,0:T(8,128)(2,1)S(1)}, u32[]{:S(2)}, u32[]{:S(2)}) collective-permute-start(bf16[2,3,32,256]{3,2,1,0:T(8,128)(2,1)S(1)} %join.6.refs_0_), channel_id=1, source_target_pairs={{0,16},{4,20},{8,24},{12,28},{16,0},{20,4},{24,8},{28,12},{1,17},{... | collective-permute-start | bytes 294920 | tf_op jit(solution)/shard_map/ppermute | solution.py:27
  43.3 2.4 %collective-permute-done.8.refs_1_ = bf16[2,3,32,256]{3,2,1,0:T(8,128)(2,1)S(1)} collective-permute-done((bf16[2,3,32,256]{3,2,1,0:T(8,128)(2,1)S(1)}, bf16[2,3,32,256]{3,2,1,0:T(8,128)(2,1)S(1)}, u32[]{:S(2)}, u32[]{:S(2)}) %collective-permute-start.8) | collective-permute-done | bytes 98336 | tf_op jit(solution)/shard_map/ppermute | solution.py:27
  52.7 1.9 %own_gradients.1.refs_2_.refs_0_ = bf16[16,9,64,256]{3,2,1,0:T(8,128)(2,1)S(1)} custom-call(s32[18]{0:T(128)S(1)} %pad_add_fusion.1.refs_0_, bf16[2,8,3,32,256]{4,3,2,1,0:T(8,128)(2,1)S(1)} %assemble.1.refs_1_, bf16[16,6,64,256]{3,2,1,0:T(8,128)(2,1)S(1)} %get-tuple-element.46.refs_2_, bf16[16,192,256]{2,1,0:T(8,128)(2,1)S(1)} %bitcast.12), custom_call_target="tpu_custom_call" | custom-call | flops 1207959552 | bytes 10223652 | tf_op jit(solution)/shard_map/own_gradients/pallas_call | solution.py:56
  54.7 4.7 %weight_part.1 = (f32[4,96,576]{2,1,0:T(8,128)S(1)}, bf16[4,96,576]{2,1,0:T(8,128)(2,1)S(1)}) custom-call(s32[18]{0:T(128)S(1)} %pad_add_fusion.1.refs_0_, bf16[16,256,768]{2,1,0:T(8,128)(2,1)S(1)} %get-tuple-element.37.refs_1_, bf16[16,9,64,256]{3,2,1,0:T(8,128)(2,1)S(1)} %own_gradients.1.refs_2_.refs_0_, bf16[192,384]{1,0:T(8,128)(2,1)S(1)} %collective-permute-done.14.refs_3_), custom_call_target="tpu_custom_call" | custom-call | flops 3623878656 | bytes 11894820 | tf_op jit(solution)/shard_map/weight_part/pallas_call | solution.py:56
  61.5 2.6 %own_input.1.refs_2_.refs_0_ = bf16[2,16,192,256]{3,2,1,0:T(8,128)(2,1)S(1)} custom-call(bf16[16,9,64,256]{3,2,1,0:T(8,128)(2,1)S(1)} %own_gradients.1.refs_2_.refs_0_, bf16[2,192,576]{2,1,0:T(8,128)(2,1)S(1)} %turn.2.refs_4_.refs_1_, bf16[4,96,576]{2,1,0:T(8,128)(2,1)S(1)} %get-tuple-element.48.refs_2_.refs_4_), custom_call_target="tpu_custom_call" | custom-call | flops 1811939328 | bytes 8306688 | tf_op jit(solution)/shard_map/own_input/pallas_call | solution.py:56
  64.2 3.2 %far_query_key.1.refs_3_.refs_2_ = bf16[16,6,64,256]{3,2,1,0:T(8,128)(2,1)S(1)} custom-call(s32[18]{0:T(128)S(1)} %pad_add_fusion.1.refs_0_, bf16[16,256,768]{2,1,0:T(8,128)(2,1)S(1)} %get-tuple-element.37.refs_1_, bf16[192,768]{1,0:T(8,128)(2,1)S(1)} %collective-permute-done.13.refs_5_.refs_2_.refs_1_, ...), custom_call_target="tpu_custom_call" | custom-call | flops 2415919104 | bytes 10027044 | tf_op jit(solution)/shard_map/far_query_key/pallas_call | solution.py:56
  67.4 1.6 %collective-permute-done.17.refs_1_ = bf16[4,96,576]{2,1,0:T(8,128)(2,1)S(1)} collective-permute-done((bf16[4,96,576]{2,1,0:T(8,128)(2,1)S(1)}, bf16[4,96,576]{2,1,0:T(8,128)(2,1)S(1)}, u32[]{:S(2)}, u32[]{:S(2)}) %collective-permute-start.17) | collective-permute-done | bytes 442400 | tf_op jit(solution)/shard_map/ppermute | solution.py:27
  70.6 3.5 %collective-permute-done.15.refs_1_ = bf16[2,8,3,32,256]{4,3,2,1,0:T(8,128)(2,1)S(1)} collective-permute-done((bf16[2,8,3,32,256]{4,3,2,1,0:T(8,128)(2,1)S(1)}, bf16[2,8,3,32,256]{4,3,2,1,0:T(8,128)(2,1)S(1)}, u32[]{:S(2)}, u32[]{:S(2)}) %collective-permute-start.15) | collective-permute-done | bytes 786464 | tf_op jit(solution)/shard_map/ppermute | solution.py:27
  74.1 1.9 %far_gradients.1.refs_1_.refs_2_ = bf16[16,9,64,256]{3,2,1,0:T(8,128)(2,1)S(1)} custom-call(s32[18]{0:T(128)S(1)} %pad_add_fusion.1.refs_0_, bf16[2,8,3,32,256]{4,3,2,1,0:T(8,128)(2,1)S(1)} %collective-permute-done.15.refs_1_, bf16[16,6,64,256]{3,2,1,0:T(8,128)(2,1)S(1)} %far_query_key.1.refs_3_.refs_2_, ...), custom_call_target="tpu_custom_call" | custom-call | flops 1207959552 | bytes 10223652 | tf_op jit(solution)/shard_map/far_gradients/pallas_call | solution.py:56
  79.5 2.6 %collective-permute-start.21 = (bf16[1,96,576]{2,1,0:T(8,128)(2,1)S(1)}, bf16[1,96,576]{2,1,0:T(8,128)(2,1)S(1)}, u32[]{:S(2)}, u32[]{:S(2)}) collective-permute-start(bf16[1,96,576]{2,1,0:T(8,128)(2,1)S(1)} %get-tuple-element.57), channel_id=1, source_target_pairs={{0,16},{4,20},{8,24},{12,28},{16,0},{20,4},{24,8},{28,12},{1,17},{... | collective-permute-start | bytes 331784 | tf_op jit(solution)/shard_map/ppermute | solution.py:27
  83.5 4.9 %collective-permute-done.21.refs_2_ = bf16[1,96,576]{2,1,0:T(8,128)(2,1)S(1)} collective-permute-done((bf16[1,96,576]{2,1,0:T(8,128)(2,1)S(1)}, bf16[1,96,576]{2,1,0:T(8,128)(2,1)S(1)}, u32[]{:S(2)}, u32[]{:S(2)}) %collective-permute-start.21) | collective-permute-done | bytes 110624 | tf_op jit(solution)/shard_map/ppermute | solution.py:27
  (55 shorter events, 22.6 us)
Async XLA Ops:
  0.6 39.4 %collective-permute-start.7 = (bf16[16,192,256]{2,1,0:T(8,128)(2,1)}, bf16[16,192,256]{2,1,0:T(8,128)(2,1)S(1)}, u32[]{:S(2)}, u32[]{:S(2)}) collective-permute-start(bf16[16,192,256]{2,1,0:T(8,128)(2,1)} %bitcast.10), channel_id=1, source_target_pairs={{0,2},{1,3},{2,0},{3,1},{4,6},{5,7},{6,4},{7,5},{8,10},{9,11},{10,... | collective-permute-start | bytes 4718600 | tf_op jit(solution)/shard_map/ppermute | solution.py:27
  10.7 7.0 %collective-permute-start = (bf16[4,3,32,256]{3,2,1,0:T(8,128)(2,1)S(1)}, bf16[4,3,32,256]{3,2,1,0:T(8,128)(2,1)S(1)}, u32[]{:S(2)}, u32[]{:S(2)}) collective-permute-start(bf16[4,3,32,256]{3,2,1,0:T(8,128)(2,1)S(1)} %get-tuple-element.32.refs_4_), channel_id=1, source_target_pairs={{0,8},{4,12},{8,0},{12,4},{16,24},{20,28},{24,16},{28,20},{1,9},{5... | collective-permute-start | bytes 589832 | tf_op jit(solution)/shard_map/ppermute | solution.py:27
  12.4 17.5 %copy-start.1 = (bf16[768,192]{0,1:T(8,128)(2,1)S(1)}, bf16[768,192]{0,1:T(8,128)(2,1)}, u32[]{:S(2)}) copy-start(bf16[768,192]{0,1:T(8,128)(2,1)} %param.7) | copy-start | bytes 884740
  12.4 17.5 %copy-start.2 = (bf16[768,192]{0,1:T(8,128)(2,1)S(1)}, bf16[768,192]{0,1:T(8,128)(2,1)}, u32[]{:S(2)}) copy-start(bf16[768,192]{0,1:T(8,128)(2,1)} %param.8) | copy-start | bytes 884740
  16.2 6.2 %collective-permute-start.3 = (bf16[4,3,32,256]{3,2,1,0:T(8,128)(2,1)S(1)}, bf16[4,3,32,256]{3,2,1,0:T(8,128)(2,1)S(1)}, u32[]{:S(2)}, u32[]{:S(2)}) collective-permute-start(bf16[4,3,32,256]{3,2,1,0:T(8,128)(2,1)S(1)} %get-tuple-element.39.refs_4_), channel_id=1, source_target_pairs={{0,4},{4,0},{8,12},{12,8},{16,20},{20,16},{24,28},{28,24},{1,5},{5... | collective-permute-start | bytes 589832 | tf_op jit(solution)/shard_map/ppermute | solution.py:27
  17.8 6.9 %collective-permute-start.1 = (bf16[2,3,32,256]{3,2,1,0:T(8,128)(2,1)S(1)}, bf16[2,3,32,256]{3,2,1,0:T(8,128)(2,1)S(1)}, u32[]{:S(2)}, u32[]{:S(2)}) collective-permute-start(bf16[2,3,32,256]{3,2,1,0:T(8,128)(2,1)S(1)} %get-tuple-element.34), channel_id=1, source_target_pairs={{0,16},{4,20},{8,24},{12,28},{16,0},{20,4},{24,8},{28,12},{1,17},{... | collective-permute-start | bytes 294920 | tf_op jit(solution)/shard_map/ppermute | solution.py:27
  22.4 4.7 %collective-permute-start.4 = (bf16[2,3,32,256]{3,2,1,0:T(8,128)(2,1)S(1)}, bf16[2,3,32,256]{3,2,1,0:T(8,128)(2,1)S(1)}, u32[]{:S(2)}, u32[]{:S(2)}) collective-permute-start(bf16[2,3,32,256]{3,2,1,0:T(8,128)(2,1)S(1)} %get-tuple-element.41), channel_id=1, source_target_pairs={{0,8},{4,12},{8,0},{12,4},{16,24},{20,28},{24,16},{28,20},{1,9},{5... | collective-permute-start | bytes 294920 | tf_op jit(solution)/shard_map/ppermute | solution.py:27
  24.7 6.3 %collective-permute-start.2 = (bf16[1,3,32,256]{3,2,1,0:T(8,128)(2,1)S(1)}, bf16[1,3,32,256]{3,2,1,0:T(8,128)(2,1)S(1)}, u32[]{:S(2)}, u32[]{:S(2)}) collective-permute-start(bf16[1,3,32,256]{3,2,1,0:T(8,128)(2,1)S(1)} %get-tuple-element.36), channel_id=1, source_target_pairs={{0,4},{4,0},{8,12},{12,8},{16,20},{20,16},{24,28},{28,24},{1,5},{5... | collective-permute-start | bytes 147464 | tf_op jit(solution)/shard_map/ppermute | solution.py:27
  27.1 5.5 %collective-permute-start.5 = (bf16[1,3,32,256]{3,2,1,0:T(8,128)(2,1)S(1)}, bf16[1,3,32,256]{3,2,1,0:T(8,128)(2,1)S(1)}, u32[]{:S(2)}, u32[]{:S(2)}) collective-permute-start(bf16[1,3,32,256]{3,2,1,0:T(8,128)(2,1)S(1)} %get-tuple-element.43), channel_id=1, source_target_pairs={{0,16},{4,20},{8,24},{12,28},{16,0},{20,4},{24,8},{28,12},{1,17},{... | collective-permute-start | bytes 147464 | tf_op jit(solution)/shard_map/ppermute | solution.py:27
  32.8 4.2 %collective-permute-start.10 = (bf16[1,3,32,256]{3,2,1,0:T(8,128)(2,1)S(1)}, bf16[1,3,32,256]{3,2,1,0:T(8,128)(2,1)S(1)}, u32[]{:S(2)}, u32[]{:S(2)}) collective-permute-start(bf16[1,3,32,256]{3,2,1,0:T(8,128)(2,1)S(1)} %get-tuple-element.45.refs_0_), channel_id=1, source_target_pairs={{0,4},{4,0},{8,12},{12,8},{16,20},{20,16},{24,28},{28,24},{1,5},{5... | collective-permute-start | bytes 147464 | tf_op jit(solution)/shard_map/ppermute | solution.py:27
  34.4 5.6 %collective-permute-start.6 = (bf16[1,3,32,256]{3,2,1,0:T(8,128)(2,1)S(1)}, bf16[1,3,32,256]{3,2,1,0:T(8,128)(2,1)S(1)}, u32[]{:S(2)}, u32[]{:S(2)}) collective-permute-start(bf16[1,3,32,256]{3,2,1,0:T(8,128)(2,1)S(1)} %get-tuple-element.44.refs_0_), channel_id=1, source_target_pairs={{0,16},{4,20},{8,24},{12,28},{16,0},{20,4},{24,8},{28,12},{1,17},{... | collective-permute-start | bytes 147464 | tf_op jit(solution)/shard_map/ppermute | solution.py:27
  37.0 6.2 %collective-permute-start.11 = (bf16[2,3,32,256]{3,2,1,0:T(8,128)(2,1)S(1)}, bf16[2,3,32,256]{3,2,1,0:T(8,128)(2,1)S(1)}, u32[]{:S(2)}, u32[]{:S(2)}) collective-permute-start(bf16[2,3,32,256]{3,2,1,0:T(8,128)(2,1)S(1)} %join.6.refs_0_), channel_id=1, source_target_pairs={{0,16},{4,20},{8,24},{12,28},{16,0},{20,4},{24,8},{28,12},{1,17},{... | collective-permute-start | bytes 294920 | tf_op jit(solution)/shard_map/ppermute | solution.py:27
  40.0 5.7 %collective-permute-start.8 = (bf16[2,3,32,256]{3,2,1,0:T(8,128)(2,1)S(1)}, bf16[2,3,32,256]{3,2,1,0:T(8,128)(2,1)S(1)}, u32[]{:S(2)}, u32[]{:S(2)}) collective-permute-start(bf16[2,3,32,256]{3,2,1,0:T(8,128)(2,1)S(1)} %join.4.refs_0_), channel_id=1, source_target_pairs={{0,8},{4,12},{8,0},{12,4},{16,24},{20,28},{24,16},{28,20},{1,9},{5... | collective-permute-start | bytes 294920 | tf_op jit(solution)/shard_map/ppermute | solution.py:27
  40.1 10.0 %collective-permute-start.13 = (bf16[192,768]{1,0:T(8,128)(2,1)S(1)}, bf16[192,768]{1,0:T(8,128)(2,1)S(1)}, u32[]{:S(2)}, u32[]{:S(2)}) collective-permute-start(bf16[192,768]{1,0:T(8,128)(2,1)S(1)} %bitcast.15), channel_id=1, source_target_pairs={{0,2},{1,3},{2,0},{3,1},{4,6},{5,7},{6,4},{7,5},{8,10},{9,11},{10,... | collective-permute-start | bytes 884744 | tf_op jit(solution)/shard_map/ppermute | solution.py:27
  43.2 6.9 %collective-permute-start.12 = (bf16[4,3,32,256]{3,2,1,0:T(8,128)(2,1)S(1)}, bf16[4,3,32,256]{3,2,1,0:T(8,128)(2,1)S(1)}, u32[]{:S(2)}, u32[]{:S(2)}) collective-permute-start(bf16[4,3,32,256]{3,2,1,0:T(8,128)(2,1)S(1)} %join.7.refs_3_), channel_id=1, source_target_pairs={{0,8},{4,12},{8,0},{12,4},{16,24},{20,28},{24,16},{28,20},{1,9},{5... | collective-permute-start | bytes 589832 | tf_op jit(solution)/shard_map/ppermute | solution.py:27
  45.7 5.7 %collective-permute-start.9 = (bf16[4,3,32,256]{3,2,1,0:T(8,128)(2,1)S(1)}, bf16[4,3,32,256]{3,2,1,0:T(8,128)(2,1)S(1)}, u32[]{:S(2)}, u32[]{:S(2)}) collective-permute-start(bf16[4,3,32,256]{3,2,1,0:T(8,128)(2,1)S(1)} %join.5.refs_1_), channel_id=1, source_target_pairs={{0,4},{4,0},{8,12},{12,8},{16,20},{20,16},{24,28},{28,24},{1,5},{5... | collective-permute-start | bytes 589832 | tf_op jit(solution)/shard_map/ppermute | solution.py:27
  46.9 7.8 %collective-permute-start.14 = (bf16[192,384]{1,0:T(8,128)(2,1)S(1)}, bf16[192,384]{1,0:T(8,128)(2,1)S(1)}, u32[]{:S(2)}, u32[]{:S(2)}) collective-permute-start(bf16[192,384]{1,0:T(8,128)(2,1)S(1)} %get-tuple-element.47), channel_id=1, source_target_pairs={{0,2},{1,3},{2,0},{3,1},{4,6},{5,7},{6,4},{7,5},{8,10},{9,11},{10,... | collective-permute-start | bytes 442376 | tf_op jit(solution)/shard_map/ppermute | solution.py:27
  47.4 13.1 %collective-permute-start.16 = (bf16[192,768]{1,0:T(8,128)(2,1)S(1)}, bf16[192,768]{1,0:T(8,128)(2,1)S(1)}, u32[]{:S(2)}, u32[]{:S(2)}) collective-permute-start(bf16[192,768]{1,0:T(8,128)(2,1)S(1)} %bitcast.18), channel_id=1, source_target_pairs={{0,2},{1,3},{2,0},{3,1},{4,6},{5,7},{6,4},{7,5},{8,10},{9,11},{10,... | collective-permute-start | bytes 884744 | tf_op jit(solution)/shard_map/ppermute | solution.py:27
  52.1 22.0 %collective-permute-start.15 = (bf16[2,8,3,32,256]{4,3,2,1,0:T(8,128)(2,1)S(1)}, bf16[2,8,3,32,256]{4,3,2,1,0:T(8,128)(2,1)S(1)}, u32[]{:S(2)}, u32[]{:S(2)}) collective-permute-start(bf16[2,8,3,32,256]{4,3,2,1,0:T(8,128)(2,1)S(1)} %assemble.1.refs_1_), channel_id=1, source_target_pairs={{0,2},{1,3},{2,0},{3,1},{4,6},{5,7},{6,4},{7,5},{8,10},{9,11},{10,... | collective-permute-start | bytes 2359304 | tf_op jit(solution)/shard_map/ppermute | solution.py:27
  59.4 9.5 %collective-permute-start.17 = (bf16[4,96,576]{2,1,0:T(8,128)(2,1)S(1)}, bf16[4,96,576]{2,1,0:T(8,128)(2,1)S(1)}, u32[]{:S(2)}, u32[]{:S(2)}) collective-permute-start(bf16[4,96,576]{2,1,0:T(8,128)(2,1)S(1)} %get-tuple-element.48.refs_2_.refs_4_), channel_id=1, source_target_pairs={{0,4},{4,0},{8,12},{12,8},{16,20},{20,16},{24,28},{28,24},{1,5},{5... | collective-permute-start | bytes 1327112 | tf_op jit(solution)/shard_map/ppermute | solution.py:27
  69.2 8.3 %collective-permute-start.19 = (bf16[2,96,576]{2,1,0:T(8,128)(2,1)S(1)}, bf16[2,96,576]{2,1,0:T(8,128)(2,1)S(1)}, u32[]{:S(2)}, u32[]{:S(2)}) collective-permute-start(bf16[2,96,576]{2,1,0:T(8,128)(2,1)S(1)} %get-tuple-element.53), channel_id=1, source_target_pairs={{0,8},{4,12},{8,0},{12,4},{16,24},{20,28},{24,16},{28,20},{1,9},{5... | collective-permute-start | bytes 663560 | tf_op jit(solution)/shard_map/ppermute | solution.py:27
  77.4 4.7 %collective-permute-start.18 = (bf16[8,192,256]{2,1,0:T(8,128)(2,1)S(1)}, bf16[8,192,256]{2,1,0:T(8,128)(2,1)S(1)}, u32[]{:S(2)}, u32[]{:S(2)}) collective-permute-start(bf16[8,192,256]{2,1,0:T(8,128)(2,1)S(1)} %get-tuple-element.52), channel_id=1, source_target_pairs={{0,1},{1,0},{2,3},{3,2},{4,5},{5,4},{6,7},{7,6},{8,9},{9,8},{10,11... | collective-permute-start | bytes 2359304 | tf_op jit(solution)/shard_map/ppermute | solution.py:27
  79.0 3.1 %collective-permute-start.20 = (bf16[8,192,256]{2,1,0:T(8,128)(2,1)S(1)}, bf16[8,192,256]{2,1,0:T(8,128)(2,1)S(1)}, u32[]{:S(2)}, u32[]{:S(2)}) collective-permute-start(bf16[8,192,256]{2,1,0:T(8,128)(2,1)S(1)} %get-tuple-element.56), channel_id=1, source_target_pairs={{0,1},{1,0},{2,3},{3,2},{4,5},{5,4},{6,7},{7,6},{8,9},{9,8},{10,11... | collective-permute-start | bytes 2359304 | tf_op jit(solution)/shard_map/ppermute | solution.py:27
  79.5 8.8 %collective-permute-start.21 = (bf16[1,96,576]{2,1,0:T(8,128)(2,1)S(1)}, bf16[1,96,576]{2,1,0:T(8,128)(2,1)S(1)}, u32[]{:S(2)}, u32[]{:S(2)}) collective-permute-start(bf16[1,96,576]{2,1,0:T(8,128)(2,1)S(1)} %get-tuple-element.57), channel_id=1, source_target_pairs={{0,16},{4,20},{8,24},{12,28},{16,0},{20,4},{24,8},{28,12},{1,17},{... | collective-permute-start | bytes 331784 | tf_op jit(solution)/shard_map/ppermute | solution.py:27
  (2 other events, 17.4 us)

commit v20 on v19

--- a/solution.py
+++ b/solution.py
@@ -45,7 +45,7 @@
     return pltpu.with_memory_space_constraint(a, pltpu.HBM) if stays else a
 
 
-def in_vmem(kernel, name, out, *operands, scalars=0, streamed=0, after=(), scratch=(), limit=12, flops=0):
+def in_vmem(kernel, name, out, *operands, scalars=0, streamed=0, after=(), scratch=(), limit=12, flops=0, counted=True):
     many = len(after)
 
     def run(*refs):
@@ -60,7 +60,7 @@
         out_shape=list(out),
         scratch_shapes=list(scratch),
         compiler_params=pltpu.CompilerParams(vmem_limit_bytes=limit * MIB),
-        cost_estimate=cost(flops, moved),
+        cost_estimate=cost(flops, moved) if counted else cost(0, 0),
         name=name,
     )(*[place(a, scalars <= i < scalars + streamed) for i, a in enumerate(operands)], *after)
 
@@ -273,15 +273,15 @@
         out[j // 2] = total.astype(out.dtype)
 
 
-def add_split(keep, got, after=()):
+def add_split(keep, got, after=(), flops=0):
     half = (keep.shape[0] // 2,) + keep.shape[1:]
-    return in_vmem(add_split_kernel, "add_split", (like(half), like(half, keep.dtype)), keep, got, after=after)
-
-
-def halve(keep, give, axis, bits, after=()):
+    return in_vmem(add_split_kernel, "add_split", (like(half), like(half, keep.dtype)), keep, got, after=after, flops=flops)
+
+
+def halve(keep, give, axis, bits, after=(), flops=0):
     after = list(after) + [()] * len(bits)
     for bit, waits in zip(bits[:-1], after):
-        give, keep = add_split(keep, flip(give, axis, bit), waits)
+        give, keep = add_split(keep, flip(give, axis, bit), waits, flops)
     return keep, flip(give, axis, bits[-1])
 
 
@@ -368,7 +368,7 @@
     gradients(where, 0, qk.shape[0], scores, qk, cot, grads)
 
 
-def all_gradients(where, scores, qk, cot, name, after):
+def all_gradients(where, scores, qk, cot, name, after, counted=True):
     rows, two, _, cols = qk.shape
     return in_vmem(
         gradients_kernel,
@@ -381,6 +381,7 @@
         scalars=1,
         after=after,
         limit=14,
+        counted=counted,
         flops=3 * rows * two * HEAD_DIM * cols * cols,
     )[0]
 
@@ -434,6 +435,7 @@
         *[a for one in far for a in one],
         after=after,
         limit=14,
+        counted=False,
         flops=4 * len(far) * count * cols * columns * share,
     )
 
@@ -476,24 +478,25 @@
     return mm(jnp.concatenate(left, axis=1), sheet[...].reshape(rows * cols, width), NN).T
 
 
-def weight_kernel(where, sheet, grads, *rest):
+def weight_kernel(bits, where, sheet, grads, *rest):
     outs, full = rest[:-1], rest[-1]
     full[...] = weight_product(sheet, grads).reshape(full.shape)
-    for j in range(full.shape[0]):
+    for t, j in enumerate(reorder(bits)):
         first = 0
         for keep, give in zip(outs[::2], outs[1::2]):
-            out = (keep, give)[j % 2]
+            out = (keep, give)[t % 2]
             last = first + out.shape[-1]
-            out[j // 2] = full[where[0] ^ j, :, first:last].astype(out.dtype)
+            out[t // 2] = full[where[0] ^ j, :, first:last].astype(out.dtype)
             first = last
 
 
-def whole_weight_kernel(where, sheet, grads, out):
+def whole_weight_kernel(_, where, sheet, grads, out):
     out[...] = weight_product(sheet, grads)
 
 
-def weight_part(where, sheet, grads, cuts, shards, after):
+def weight_part(where, sheet, grads, cuts, bits, after):
     rows, cols, width = sheet.shape
+    shards = 1 << len(bits)
     columns = grads.shape[1] * HEAD_DIM
     if shards == 1:
         kernel, outs, scratch = whole_weight_kernel, [like((width, columns), F32)], ()
@@ -503,7 +506,7 @@
         outs = [o for half in halves for o in (like(half, F32), like(half))]
         scratch = (pltpu.VMEM((shards, width // shards, columns), F32),)
     return in_vmem(
-        kernel,
+        functools.partial(kernel, bits),
         "weight_part",
         outs,
         where,
@@ -567,37 +570,31 @@
         scores = jnp.stack(softmax_back(logits, dprob, scale))
     far_scores = [flip(scores, "heads", f) for f in fars]
     grads = all_gradients(where, scores, qk, cot, "own_gradients", ())
-    parts = weight_part(where, held, grads, (3 * local,), shards, fv)
+    weight_bits = up[:1] + up[1:][::-1]
+    parts = weight_part(where, held, grads, (3 * local,), weight_bits, fv)
     ready = [parts[-1]]
     far_qk = [far_query_key(where, held, *w, ready) for w in zip(fq, fk)]
     far_natural = [turn(where, *w, n_heads, ready) for w in zip(fq, fk, fv)]
     own = own_input(grads, weights, ready)
     ready = [own] + far_qk + far_natural
-    far_grads = []
-
-    def far_gradients(after):
-        for args in zip(far_scores, far_qk, far_cot):
-            far_grads.append(all_gradients(where, *args, "far_gradients", after))
-        return far_grads
-
-    steps = [[]]
+    first_sum = []
     if direct:
         keep, give = parts
-        for bit in row_bits[:-1]:
-            give, keep = add_split(keep, flip(give, "rows", bit), ready)
-            steps.append([keep])
-            ready = far_grads or far_gradients(steps[-1])
-        last = keep, flip(give, "rows", row_bits[-1])
+        give, keep = add_split(keep, flip(give, "rows", weight_bits[0]), ready)
+        first_sum = [keep]
     else:
         weight_grad = lax.psum_scatter(parts[0], "rows", scatter_dimension=0, tiled=True)
         weight_grad = weight_grad.reshape(width // n_rows, 3, local)
-    if not far_grads:
-        far_gradients(steps[-1])
+    far_grads = [
+        all_gradients(where, *args, "far_gradients", first_sum, False)
+        for args in zip(far_scores, far_qk, far_cot)
+    ]
     chunks = []
-    for index, first in enumerate(range(0, row_dev, chunk)):
-        after = steps[-1] if index else ()
-        keep, give = far_input(first, chunk, own, list(zip(far_grads, far_natural)), after)
-        chunks.append((keep, flip(give, "heads", 1)))
+    for first in range(0, row_dev, chunk):
+        keep_rows, give_rows = far_input(first, chunk, own, list(zip(far_grads, far_natural)), ())
+        chunks.append((keep_rows, flip(give_rows, "heads", 1)))
+    if direct:
+        last = halve(keep, give, "rows", weight_bits[1:], [[chunks[-1][0]]], 1 << 34)
     out = finish(chunks)
     if direct:
         weight_grad = jnp.swapaxes(last_sum(out, *last, local), 0, 1)

time: 89.4 us -> 85.9 us (0.961)
  waiting for transfers between devices: 24.8 us -> 22.5 us
  starting transfers between devices: 29.9 us -> 28.7 us
    ppermute x22, waiting for transfers between devices: 24.8 us -> 22.5 us  [flip(): return lax.ppermute(values, axis, [(s, s ^ bit) for s in range(n)])]
    ppermute x22, starting transfers between devices: 29.9 us -> 28.7 us  [flip(): return lax.ppermute(values, axis, [(s, s ^ bit) for s in range(n)])]
  transfers between devices with their start and end apart: 22 -> 22, of which waited for: 13 -> 15; matrix products, arithmetic and copies ran while one was open for 0% -> 0% of each run, Pallas kernels for 37% -> 38%
where the time goes in v20:
time: 85.9 us; the launch traced here: 85.7 us
  Pallas kernels  33.5 us (39%)
  starting transfers between devices  28.7 us (33%)
  waiting for transfers between devices  22.5 us (26%)
    pallas_call x24, Pallas kernels, in_vmem(): pl.pallas_call(run, in_specs=[SMEM] * scalars + [HBM] * streamed + [VMEM]...  32.1 us
    ppermute x22, starting transfers between devices, flip(): return lax.ppermute(values, axis, [(s, s ^ bit) for s in range(n)])  28.7 us
    ppermute x22, waiting for transfers between devices, flip(): return lax.ppermute(values, axis, [(s, s ^ bit) for s in range(n)])  22.5 us
  transfers between devices with their start and end apart: 22, of which 15 were waited for; matrix products, arithmetic and copies ran while one was open for 0% of the time, Pallas kernels for 38%

profile of v20, /device:TPU:0, one launch (start us, length us, event | category | flops | bytes accessed | tf_op | source)
XLA Modules:
  0.0 85.7 jit_solution(7662221425117034256)
XLA Ops:
  0.6 3.0 %collective-permute-start.7 = (bf16[16,192,256]{2,1,0:T(8,128)(2,1)}, bf16[16,192,256]{2,1,0:T(8,128)(2,1)S(1)}, u32[]{:S(2)}, u32[]{:S(2)}) collective-permute-start(bf16[16,192,256]{2,1,0:T(8,128)(2,1)} %bitcast.10), channel_id=1, source_target_pairs={{0,2},{1,3},{2,0},{3,1},{4,6},{5,7},{6,4},{7,5},{8,10},{9,11},{10,... | collective-permute-start | bytes 4718600 | tf_op jit(solution)/shard_map/ppermute | solution.py:27
  3.7 7.0 %query_key.1 = (bf16[16,6,64,256]{3,2,1,0:T(8,128)(2,1)S(1)}, bf16[16,256,768]{2,1,0:T(8,128)(2,1)S(1)}, s32[1,16]{1,0:T(1,128)S(1)}, f32[4,3,32,256]{3,2,1,0:T(8,128)S(1)}, bf16[4,3,32,256]{3,2,1,0:T(8,128)(2,1)S(1)}) custom-call(s32[2]{0:T(128)S(1)} %pad_add_fusion.refs_0_, s32[1,16]{1,0:T(1,128)} %bitcast.24, bf16[16,256,768]{2,1,0:T(8,128)(2,1)} %refs_2_.1, ...), custom_call_target="tpu_custom_call" | custom-call | flops 704643072 | bytes 16711748 | tf_op jit(solution)/shard_map/query_key/pallas_call | solution.py:56
  10.7 1.6 %collective-permute-start = (bf16[4,3,32,256]{3,2,1,0:T(8,128)(2,1)S(1)}, bf16[4,3,32,256]{3,2,1,0:T(8,128)(2,1)S(1)}, u32[]{:S(2)}, u32[]{:S(2)}) collective-permute-start(bf16[4,3,32,256]{3,2,1,0:T(8,128)(2,1)S(1)} %get-tuple-element.32.refs_4_), channel_id=1, source_target_pairs={{0,8},{4,12},{8,0},{12,4},{16,24},{20,28},{24,16},{28,20},{1,9},{5... | collective-permute-start | bytes 589832 | tf_op jit(solution)/shard_map/ppermute | solution.py:27
  12.5 3.7 %value_dprob.1 = (f32[4,3,32,256]{3,2,1,0:T(8,128)S(1)}, bf16[4,3,32,256]{3,2,1,0:T(8,128)(2,1)S(1)}, bf16[192,384]{1,0:T(8,128)(2,1)S(1)}) custom-call(s32[18]{0:T(128)S(1)} %pad_add_fusion.1.refs_0_, bf16[16,256,768]{2,1,0:T(8,128)(2,1)S(1)} %get-tuple-element.37.refs_1_, bf16[192,768]{1,0:T(8,128)(2,1)S(1)} %bitcast.19, ...), custom_call_target="tpu_custom_call" | custom-call | flops 3221225472 | bytes 8699940 | tf_op jit(solution)/shard_map/value_dprob/pallas_call | solution.py:56
  16.2 1.6 %collective-permute-start.3 = (bf16[4,3,32,256]{3,2,1,0:T(8,128)(2,1)S(1)}, bf16[4,3,32,256]{3,2,1,0:T(8,128)(2,1)S(1)}, u32[]{:S(2)}, u32[]{:S(2)}) collective-permute-start(bf16[4,3,32,256]{3,2,1,0:T(8,128)(2,1)S(1)} %get-tuple-element.39.refs_4_), channel_id=1, source_target_pairs={{0,4},{4,0},{8,12},{12,8},{16,20},{20,16},{24,28},{28,24},{1,5},{5... | collective-permute-start | bytes 589832 | tf_op jit(solution)/shard_map/ppermute | solution.py:27
  17.8 2.7 %collective-permute-start.1 = (bf16[2,3,32,256]{3,2,1,0:T(8,128)(2,1)S(1)}, bf16[2,3,32,256]{3,2,1,0:T(8,128)(2,1)S(1)}, u32[]{:S(2)}, u32[]{:S(2)}) collective-permute-start(bf16[2,3,32,256]{3,2,1,0:T(8,128)(2,1)S(1)} %get-tuple-element.34), channel_id=1, source_target_pairs={{0,16},{4,20},{8,24},{12,28},{16,0},{20,4},{24,8},{28,12},{1,17},{... | collective-permute-start | bytes 294920 | tf_op jit(solution)/shard_map/ppermute | solution.py:27
  20.5 1.9 %collective-permute-done.3.refs_1_ = bf16[4,3,32,256]{3,2,1,0:T(8,128)(2,1)S(1)} collective-permute-done((bf16[4,3,32,256]{3,2,1,0:T(8,128)(2,1)S(1)}, bf16[4,3,32,256]{3,2,1,0:T(8,128)(2,1)S(1)}, u32[]{:S(2)}, u32[]{:S(2)}) %collective-permute-start.3) | collective-permute-done | bytes 196640 | tf_op jit(solution)/shard_map/ppermute | solution.py:27
  22.9 1.8 %collective-permute-done.1.refs_1_ = bf16[2,3,32,256]{3,2,1,0:T(8,128)(2,1)S(1)} collective-permute-done((bf16[2,3,32,256]{3,2,1,0:T(8,128)(2,1)S(1)}, bf16[2,3,32,256]{3,2,1,0:T(8,128)(2,1)S(1)}, u32[]{:S(2)}, u32[]{:S(2)}) %collective-permute-start.1) | collective-permute-done | bytes 98336 | tf_op jit(solution)/shard_map/ppermute | solution.py:27
  24.8 2.3 %collective-permute-done.4.refs_1_ = bf16[2,3,32,256]{3,2,1,0:T(8,128)(2,1)S(1)} collective-permute-done((bf16[2,3,32,256]{3,2,1,0:T(8,128)(2,1)S(1)}, bf16[2,3,32,256]{3,2,1,0:T(8,128)(2,1)S(1)}, u32[]{:S(2)}, u32[]{:S(2)}) %collective-permute-start.4) | collective-permute-done | bytes 98336 | tf_op jit(solution)/shard_map/ppermute | solution.py:27
  27.1 2.8 %collective-permute-start.5 = (bf16[1,3,32,256]{3,2,1,0:T(8,128)(2,1)S(1)}, bf16[1,3,32,256]{3,2,1,0:T(8,128)(2,1)S(1)}, u32[]{:S(2)}, u32[]{:S(2)}) collective-permute-start(bf16[1,3,32,256]{3,2,1,0:T(8,128)(2,1)S(1)} %get-tuple-element.43), channel_id=1, source_target_pairs={{0,16},{4,20},{8,24},{12,28},{16,0},{20,4},{24,8},{28,12},{1,17},{... | collective-permute-start | bytes 147464 | tf_op jit(solution)/shard_map/ppermute | solution.py:27
  31.0 1.6 %collective-permute-done.5.refs_3_ = bf16[1,3,32,256]{3,2,1,0:T(8,128)(2,1)S(1)} collective-permute-done((bf16[1,3,32,256]{3,2,1,0:T(8,128)(2,1)S(1)}, bf16[1,3,32,256]{3,2,1,0:T(8,128)(2,1)S(1)}, u32[]{:S(2)}, u32[]{:S(2)}) %collective-permute-start.5) | collective-permute-done | bytes 49184 | tf_op jit(solution)/shard_map/ppermute | solution.py:27
  32.8 1.6 %collective-permute-start.10 = (bf16[1,3,32,256]{3,2,1,0:T(8,128)(2,1)S(1)}, bf16[1,3,32,256]{3,2,1,0:T(8,128)(2,1)S(1)}, u32[]{:S(2)}, u32[]{:S(2)}) collective-permute-start(bf16[1,3,32,256]{3,2,1,0:T(8,128)(2,1)S(1)} %get-tuple-element.45.refs_0_), channel_id=1, source_target_pairs={{0,4},{4,0},{8,12},{12,8},{16,20},{20,16},{24,28},{28,24},{1,5},{5... | collective-permute-start | bytes 147464 | tf_op jit(solution)/shard_map/ppermute | solution.py:27
  34.4 2.4 %collective-permute-start.6 = (bf16[1,3,32,256]{3,2,1,0:T(8,128)(2,1)S(1)}, bf16[1,3,32,256]{3,2,1,0:T(8,128)(2,1)S(1)}, u32[]{:S(2)}, u32[]{:S(2)}) collective-permute-start(bf16[1,3,32,256]{3,2,1,0:T(8,128)(2,1)S(1)} %get-tuple-element.44.refs_0_), channel_id=1, source_target_pairs={{0,16},{4,20},{8,24},{12,28},{16,0},{20,4},{24,8},{28,12},{1,17},{... | collective-permute-start | bytes 147464 | tf_op jit(solution)/shard_map/ppermute | solution.py:27
  37.0 2.4 %collective-permute-start.11 = (bf16[2,3,32,256]{3,2,1,0:T(8,128)(2,1)S(1)}, bf16[2,3,32,256]{3,2,1,0:T(8,128)(2,1)S(1)}, u32[]{:S(2)}, u32[]{:S(2)}) collective-permute-start(bf16[2,3,32,256]{3,2,1,0:T(8,128)(2,1)S(1)} %join.6.refs_0_), channel_id=1, source_target_pairs={{0,16},{4,20},{8,24},{12,28},{16,0},{20,4},{24,8},{28,12},{1,17},{... | collective-permute-start | bytes 294920 | tf_op jit(solution)/shard_map/ppermute | solution.py:27
  41.7 1.5 %collective-permute-done.11.refs_1_ = bf16[2,3,32,256]{3,2,1,0:T(8,128)(2,1)S(1)} collective-permute-done((bf16[2,3,32,256]{3,2,1,0:T(8,128)(2,1)S(1)}, bf16[2,3,32,256]{3,2,1,0:T(8,128)(2,1)S(1)}, u32[]{:S(2)}, u32[]{:S(2)}) %collective-permute-start.11) | collective-permute-done | bytes 98336 | tf_op jit(solution)/shard_map/ppermute | solution.py:27
  43.3 2.4 %collective-permute-done.8.refs_1_ = bf16[2,3,32,256]{3,2,1,0:T(8,128)(2,1)S(1)} collective-permute-done((bf16[2,3,32,256]{3,2,1,0:T(8,128)(2,1)S(1)}, bf16[2,3,32,256]{3,2,1,0:T(8,128)(2,1)S(1)}, u32[]{:S(2)}, u32[]{:S(2)}) %collective-permute-start.8) | collective-permute-done | bytes 98336 | tf_op jit(solution)/shard_map/ppermute | solution.py:27
  52.7 1.9 %own_gradients.1.refs_2_.refs_0_ = bf16[16,9,64,256]{3,2,1,0:T(8,128)(2,1)S(1)} custom-call(s32[18]{0:T(128)S(1)} %pad_add_fusion.1.refs_0_, bf16[2,8,3,32,256]{4,3,2,1,0:T(8,128)(2,1)S(1)} %assemble.1.refs_1_, bf16[16,6,64,256]{3,2,1,0:T(8,128)(2,1)S(1)} %get-tuple-element.46.refs_2_, bf16[16,192,256]{2,1,0:T(8,128)(2,1)S(1)} %bitcast.12), custom_call_target="tpu_custom_call" | custom-call | flops 1207959552 | bytes 10223652 | tf_op jit(solution)/shard_map/own_gradients/pallas_call | solution.py:56
  54.7 4.7 %weight_part.1 = (f32[4,96,576]{2,1,0:T(8,128)S(1)}, bf16[4,96,576]{2,1,0:T(8,128)(2,1)S(1)}) custom-call(s32[18]{0:T(128)S(1)} %pad_add_fusion.1.refs_0_, bf16[16,256,768]{2,1,0:T(8,128)(2,1)S(1)} %get-tuple-element.37.refs_1_, bf16[16,9,64,256]{3,2,1,0:T(8,128)(2,1)S(1)} %own_gradients.1.refs_2_.refs_0_, bf16[192,384]{1,0:T(8,128)(2,1)S(1)} %collective-permute-done.14.refs_3_), custom_call_target="tpu_custom_call" | custom-call | flops 3623878656 | bytes 11894820 | tf_op jit(solution)/shard_map/weight_part/pallas_call | solution.py:56
  61.5 2.6 %own_input.1.refs_2_.refs_0_ = bf16[2,16,192,256]{3,2,1,0:T(8,128)(2,1)S(1)} custom-call(bf16[16,9,64,256]{3,2,1,0:T(8,128)(2,1)S(1)} %own_gradients.1.refs_2_.refs_0_, bf16[2,192,576]{2,1,0:T(8,128)(2,1)S(1)} %turn.2.refs_4_.refs_1_, bf16[4,96,576]{2,1,0:T(8,128)(2,1)S(1)} %get-tuple-element.48.refs_2_.refs_4_), custom_call_target="tpu_custom_call" | custom-call | flops 1811939328 | bytes 8306688 | tf_op jit(solution)/shard_map/own_input/pallas_call | solution.py:56
  64.1 3.2 %far_query_key.1.refs_3_.refs_2_ = bf16[16,6,64,256]{3,2,1,0:T(8,128)(2,1)S(1)} custom-call(s32[18]{0:T(128)S(1)} %pad_add_fusion.1.refs_0_, bf16[16,256,768]{2,1,0:T(8,128)(2,1)S(1)} %get-tuple-element.37.refs_1_, bf16[192,768]{1,0:T(8,128)(2,1)S(1)} %collective-permute-done.13.refs_5_.refs_2_.refs_1_, ...), custom_call_target="tpu_custom_call" | custom-call | flops 2415919104 | bytes 10027044 | tf_op jit(solution)/shard_map/far_query_key/pallas_call | solution.py:56
  67.3 1.6 %collective-permute-done.17.refs_1_ = bf16[4,96,576]{2,1,0:T(8,128)(2,1)S(1)} collective-permute-done((bf16[4,96,576]{2,1,0:T(8,128)(2,1)S(1)}, bf16[4,96,576]{2,1,0:T(8,128)(2,1)S(1)}, u32[]{:S(2)}, u32[]{:S(2)}) %collective-permute-start.17) | collective-permute-done | bytes 442400 | tf_op jit(solution)/shard_map/ppermute | solution.py:27
  69.2 1.7 %collective-permute-start.20 = (bf16[2,96,576]{2,1,0:T(8,128)(2,1)S(1)}, bf16[2,96,576]{2,1,0:T(8,128)(2,1)S(1)}, u32[]{:S(2)}, u32[]{:S(2)}) collective-permute-start(bf16[2,96,576]{2,1,0:T(8,128)(2,1)S(1)} %get-tuple-element.55), channel_id=1, source_target_pairs={{0,16},{4,20},{8,24},{12,28},{16,0},{20,4},{24,8},{28,12},{1,17},{... | collective-permute-start | bytes 663560 | tf_op jit(solution)/shard_map/ppermute | solution.py:27
  70.9 3.1 %collective-permute-done.15.refs_1_ = bf16[2,8,3,32,256]{4,3,2,1,0:T(8,128)(2,1)S(1)} collective-permute-done((bf16[2,8,3,32,256]{4,3,2,1,0:T(8,128)(2,1)S(1)}, bf16[2,8,3,32,256]{4,3,2,1,0:T(8,128)(2,1)S(1)}, u32[]{:S(2)}, u32[]{:S(2)}) %collective-permute-start.15) | collective-permute-done | bytes 786464 | tf_op jit(solution)/shard_map/ppermute | solution.py:27
  74.1 1.9 %far_gradients.1.refs_1_ = bf16[16,9,64,256]{3,2,1,0:T(8,128)(2,1)S(1)} custom-call(s32[18]{0:T(128)S(1)} %pad_add_fusion.1.refs_0_, bf16[2,8,3,32,256]{4,3,2,1,0:T(8,128)(2,1)S(1)} %collective-permute-done.15.refs_1_, bf16[16,6,64,256]{3,2,1,0:T(8,128)(2,1)S(1)} %far_query_key.1.refs_3_.refs_2_, ...), custom_call_target="tpu_custom_call" | custom-call | tf_op jit(solution)/shard_map/far_gradients/pallas_call | solution.py:56
  (55 shorter events, 23.8 us)
Async XLA Ops:
  0.6 39.4 %collective-permute-start.7 = (bf16[16,192,256]{2,1,0:T(8,128)(2,1)}, bf16[16,192,256]{2,1,0:T(8,128)(2,1)S(1)}, u32[]{:S(2)}, u32[]{:S(2)}) collective-permute-start(bf16[16,192,256]{2,1,0:T(8,128)(2,1)} %bitcast.10), channel_id=1, source_target_pairs={{0,2},{1,3},{2,0},{3,1},{4,6},{5,7},{6,4},{7,5},{8,10},{9,11},{10,... | collective-permute-start | bytes 4718600 | tf_op jit(solution)/shard_map/ppermute | solution.py:27
  10.7 7.0 %collective-permute-start = (bf16[4,3,32,256]{3,2,1,0:T(8,128)(2,1)S(1)}, bf16[4,3,32,256]{3,2,1,0:T(8,128)(2,1)S(1)}, u32[]{:S(2)}, u32[]{:S(2)}) collective-permute-start(bf16[4,3,32,256]{3,2,1,0:T(8,128)(2,1)S(1)} %get-tuple-element.32.refs_4_), channel_id=1, source_target_pairs={{0,8},{4,12},{8,0},{12,4},{16,24},{20,28},{24,16},{28,20},{1,9},{5... | collective-permute-start | bytes 589832 | tf_op jit(solution)/shard_map/ppermute | solution.py:27
  12.4 17.5 %copy-start.1 = (bf16[768,192]{0,1:T(8,128)(2,1)S(1)}, bf16[768,192]{0,1:T(8,128)(2,1)}, u32[]{:S(2)}) copy-start(bf16[768,192]{0,1:T(8,128)(2,1)} %param.7) | copy-start | bytes 884740
  12.4 17.5 %copy-start.2 = (bf16[768,192]{0,1:T(8,128)(2,1)S(1)}, bf16[768,192]{0,1:T(8,128)(2,1)}, u32[]{:S(2)}) copy-start(bf16[768,192]{0,1:T(8,128)(2,1)} %param.8) | copy-start | bytes 884740
  16.2 6.1 %collective-permute-start.3 = (bf16[4,3,32,256]{3,2,1,0:T(8,128)(2,1)S(1)}, bf16[4,3,32,256]{3,2,1,0:T(8,128)(2,1)S(1)}, u32[]{:S(2)}, u32[]{:S(2)}) collective-permute-start(bf16[4,3,32,256]{3,2,1,0:T(8,128)(2,1)S(1)} %get-tuple-element.39.refs_4_), channel_id=1, source_target_pairs={{0,4},{4,0},{8,12},{12,8},{16,20},{20,16},{24,28},{28,24},{1,5},{5... | collective-permute-start | bytes 589832 | tf_op jit(solution)/shard_map/ppermute | solution.py:27
  17.8 6.9 %collective-permute-start.1 = (bf16[2,3,32,256]{3,2,1,0:T(8,128)(2,1)S(1)}, bf16[2,3,32,256]{3,2,1,0:T(8,128)(2,1)S(1)}, u32[]{:S(2)}, u32[]{:S(2)}) collective-permute-start(bf16[2,3,32,256]{3,2,1,0:T(8,128)(2,1)S(1)} %get-tuple-element.34), channel_id=1, source_target_pairs={{0,16},{4,20},{8,24},{12,28},{16,0},{20,4},{24,8},{28,12},{1,17},{... | collective-permute-start | bytes 294920 | tf_op jit(solution)/shard_map/ppermute | solution.py:27
  22.4 4.7 %collective-permute-start.4 = (bf16[2,3,32,256]{3,2,1,0:T(8,128)(2,1)S(1)}, bf16[2,3,32,256]{3,2,1,0:T(8,128)(2,1)S(1)}, u32[]{:S(2)}, u32[]{:S(2)}) collective-permute-start(bf16[2,3,32,256]{3,2,1,0:T(8,128)(2,1)S(1)} %get-tuple-element.41), channel_id=1, source_target_pairs={{0,8},{4,12},{8,0},{12,4},{16,24},{20,28},{24,16},{28,20},{1,9},{5... | collective-permute-start | bytes 294920 | tf_op jit(solution)/shard_map/ppermute | solution.py:27
  24.7 6.3 %collective-permute-start.2 = (bf16[1,3,32,256]{3,2,1,0:T(8,128)(2,1)S(1)}, bf16[1,3,32,256]{3,2,1,0:T(8,128)(2,1)S(1)}, u32[]{:S(2)}, u32[]{:S(2)}) collective-permute-start(bf16[1,3,32,256]{3,2,1,0:T(8,128)(2,1)S(1)} %get-tuple-element.36), channel_id=1, source_target_pairs={{0,4},{4,0},{8,12},{12,8},{16,20},{20,16},{24,28},{28,24},{1,5},{5... | collective-permute-start | bytes 147464 | tf_op jit(solution)/shard_map/ppermute | solution.py:27
  27.1 5.5 %collective-permute-start.5 = (bf16[1,3,32,256]{3,2,1,0:T(8,128)(2,1)S(1)}, bf16[1,3,32,256]{3,2,1,0:T(8,128)(2,1)S(1)}, u32[]{:S(2)}, u32[]{:S(2)}) collective-permute-start(bf16[1,3,32,256]{3,2,1,0:T(8,128)(2,1)S(1)} %get-tuple-element.43), channel_id=1, source_target_pairs={{0,16},{4,20},{8,24},{12,28},{16,0},{20,4},{24,8},{28,12},{1,17},{... | collective-permute-start | bytes 147464 | tf_op jit(solution)/shard_map/ppermute | solution.py:27
  32.8 4.2 %collective-permute-start.10 = (bf16[1,3,32,256]{3,2,1,0:T(8,128)(2,1)S(1)}, bf16[1,3,32,256]{3,2,1,0:T(8,128)(2,1)S(1)}, u32[]{:S(2)}, u32[]{:S(2)}) collective-permute-start(bf16[1,3,32,256]{3,2,1,0:T(8,128)(2,1)S(1)} %get-tuple-element.45.refs_0_), channel_id=1, source_target_pairs={{0,4},{4,0},{8,12},{12,8},{16,20},{20,16},{24,28},{28,24},{1,5},{5... | collective-permute-start | bytes 147464 | tf_op jit(solution)/shard_map/ppermute | solution.py:27
  34.4 5.6 %collective-permute-start.6 = (bf16[1,3,32,256]{3,2,1,0:T(8,128)(2,1)S(1)}, bf16[1,3,32,256]{3,2,1,0:T(8,128)(2,1)S(1)}, u32[]{:S(2)}, u32[]{:S(2)}) collective-permute-start(bf16[1,3,32,256]{3,2,1,0:T(8,128)(2,1)S(1)} %get-tuple-element.44.refs_0_), channel_id=1, source_target_pairs={{0,16},{4,20},{8,24},{12,28},{16,0},{20,4},{24,8},{28,12},{1,17},{... | collective-permute-start | bytes 147464 | tf_op jit(solution)/shard_map/ppermute | solution.py:27
  37.0 6.2 %collective-permute-start.11 = (bf16[2,3,32,256]{3,2,1,0:T(8,128)(2,1)S(1)}, bf16[2,3,32,256]{3,2,1,0:T(8,128)(2,1)S(1)}, u32[]{:S(2)}, u32[]{:S(2)}) collective-permute-start(bf16[2,3,32,256]{3,2,1,0:T(8,128)(2,1)S(1)} %join.6.refs_0_), channel_id=1, source_target_pairs={{0,16},{4,20},{8,24},{12,28},{16,0},{20,4},{24,8},{28,12},{1,17},{... | collective-permute-start | bytes 294920 | tf_op jit(solution)/shard_map/ppermute | solution.py:27
  40.0 5.7 %collective-permute-start.8 = (bf16[2,3,32,256]{3,2,1,0:T(8,128)(2,1)S(1)}, bf16[2,3,32,256]{3,2,1,0:T(8,128)(2,1)S(1)}, u32[]{:S(2)}, u32[]{:S(2)}) collective-permute-start(bf16[2,3,32,256]{3,2,1,0:T(8,128)(2,1)S(1)} %join.4.refs_0_), channel_id=1, source_target_pairs={{0,8},{4,12},{8,0},{12,4},{16,24},{20,28},{24,16},{28,20},{1,9},{5... | collective-permute-start | bytes 294920 | tf_op jit(solution)/shard_map/ppermute | solution.py:27
  40.1 10.0 %collective-permute-start.13 = (bf16[192,768]{1,0:T(8,128)(2,1)S(1)}, bf16[192,768]{1,0:T(8,128)(2,1)S(1)}, u32[]{:S(2)}, u32[]{:S(2)}) collective-permute-start(bf16[192,768]{1,0:T(8,128)(2,1)S(1)} %bitcast.15), channel_id=1, source_target_pairs={{0,2},{1,3},{2,0},{3,1},{4,6},{5,7},{6,4},{7,5},{8,10},{9,11},{10,... | collective-permute-start | bytes 884744 | tf_op jit(solution)/shard_map/ppermute | solution.py:27
  43.2 6.9 %collective-permute-start.12 = (bf16[4,3,32,256]{3,2,1,0:T(8,128)(2,1)S(1)}, bf16[4,3,32,256]{3,2,1,0:T(8,128)(2,1)S(1)}, u32[]{:S(2)}, u32[]{:S(2)}) collective-permute-start(bf16[4,3,32,256]{3,2,1,0:T(8,128)(2,1)S(1)} %join.7.refs_3_), channel_id=1, source_target_pairs={{0,8},{4,12},{8,0},{12,4},{16,24},{20,28},{24,16},{28,20},{1,9},{5... | collective-permute-start | bytes 589832 | tf_op jit(solution)/shard_map/ppermute | solution.py:27
  45.7 5.7 %collective-permute-start.9 = (bf16[4,3,32,256]{3,2,1,0:T(8,128)(2,1)S(1)}, bf16[4,3,32,256]{3,2,1,0:T(8,128)(2,1)S(1)}, u32[]{:S(2)}, u32[]{:S(2)}) collective-permute-start(bf16[4,3,32,256]{3,2,1,0:T(8,128)(2,1)S(1)} %join.5.refs_1_), channel_id=1, source_target_pairs={{0,4},{4,0},{8,12},{12,8},{16,20},{20,16},{24,28},{28,24},{1,5},{5... | collective-permute-start | bytes 589832 | tf_op jit(solution)/shard_map/ppermute | solution.py:27
  46.9 7.8 %collective-permute-start.14 = (bf16[192,384]{1,0:T(8,128)(2,1)S(1)}, bf16[192,384]{1,0:T(8,128)(2,1)S(1)}, u32[]{:S(2)}, u32[]{:S(2)}) collective-permute-start(bf16[192,384]{1,0:T(8,128)(2,1)S(1)} %get-tuple-element.47), channel_id=1, source_target_pairs={{0,2},{1,3},{2,0},{3,1},{4,6},{5,7},{6,4},{7,5},{8,10},{9,11},{10,... | collective-permute-start | bytes 442376 | tf_op jit(solution)/shard_map/ppermute | solution.py:27
  47.4 13.1 %collective-permute-start.16 = (bf16[192,768]{1,0:T(8,128)(2,1)S(1)}, bf16[192,768]{1,0:T(8,128)(2,1)S(1)}, u32[]{:S(2)}, u32[]{:S(2)}) collective-permute-start(bf16[192,768]{1,0:T(8,128)(2,1)S(1)} %bitcast.18), channel_id=1, source_target_pairs={{0,2},{1,3},{2,0},{3,1},{4,6},{5,7},{6,4},{7,5},{8,10},{9,11},{10,... | collective-permute-start | bytes 884744 | tf_op jit(solution)/shard_map/ppermute | solution.py:27
  52.1 22.0 %collective-permute-start.15 = (bf16[2,8,3,32,256]{4,3,2,1,0:T(8,128)(2,1)S(1)}, bf16[2,8,3,32,256]{4,3,2,1,0:T(8,128)(2,1)S(1)}, u32[]{:S(2)}, u32[]{:S(2)}) collective-permute-start(bf16[2,8,3,32,256]{4,3,2,1,0:T(8,128)(2,1)S(1)} %assemble.1.refs_1_), channel_id=1, source_target_pairs={{0,2},{1,3},{2,0},{3,1},{4,6},{5,7},{6,4},{7,5},{8,10},{9,11},{10,... | collective-permute-start | bytes 2359304 | tf_op jit(solution)/shard_map/ppermute | solution.py:27
  59.4 9.5 %collective-permute-start.17 = (bf16[4,96,576]{2,1,0:T(8,128)(2,1)S(1)}, bf16[4,96,576]{2,1,0:T(8,128)(2,1)S(1)}, u32[]{:S(2)}, u32[]{:S(2)}) collective-permute-start(bf16[4,96,576]{2,1,0:T(8,128)(2,1)S(1)} %get-tuple-element.48.refs_2_.refs_4_), channel_id=1, source_target_pairs={{0,4},{4,0},{8,12},{12,8},{16,20},{20,16},{24,28},{28,24},{1,5},{5... | collective-permute-start | bytes 1327112 | tf_op jit(solution)/shard_map/ppermute | solution.py:27
  69.2 10.2 %collective-permute-start.20 = (bf16[2,96,576]{2,1,0:T(8,128)(2,1)S(1)}, bf16[2,96,576]{2,1,0:T(8,128)(2,1)S(1)}, u32[]{:S(2)}, u32[]{:S(2)}) collective-permute-start(bf16[2,96,576]{2,1,0:T(8,128)(2,1)S(1)} %get-tuple-element.55), channel_id=1, source_target_pairs={{0,16},{4,20},{8,24},{12,28},{16,0},{20,4},{24,8},{28,12},{1,17},{... | collective-permute-start | bytes 663560 | tf_op jit(solution)/shard_map/ppermute | solution.py:27
  78.8 2.4 %collective-permute-start.18 = (bf16[8,192,256]{2,1,0:T(8,128)(2,1)S(1)}, bf16[8,192,256]{2,1,0:T(8,128)(2,1)S(1)}, u32[]{:S(2)}, u32[]{:S(2)}) collective-permute-start(bf16[8,192,256]{2,1,0:T(8,128)(2,1)S(1)} %get-tuple-element.52), channel_id=1, source_target_pairs={{0,1},{1,0},{2,3},{3,2},{4,5},{5,4},{6,7},{7,6},{8,9},{9,8},{10,11... | collective-permute-start | bytes 2359304 | tf_op jit(solution)/shard_map/ppermute | solution.py:27
  78.9 3.4 %collective-permute-start.19 = (bf16[8,192,256]{2,1,0:T(8,128)(2,1)S(1)}, bf16[8,192,256]{2,1,0:T(8,128)(2,1)S(1)}, u32[]{:S(2)}, u32[]{:S(2)}) collective-permute-start(bf16[8,192,256]{2,1,0:T(8,128)(2,1)S(1)} %get-tuple-element.54), channel_id=1, source_target_pairs={{0,1},{1,0},{2,3},{3,2},{4,5},{5,4},{6,7},{7,6},{8,9},{9,8},{10,11... | collective-permute-start | bytes 2359304 | tf_op jit(solution)/shard_map/ppermute | solution.py:27
  79.5 5.4 %collective-permute-start.21 = (bf16[1,96,576]{2,1,0:T(8,128)(2,1)S(1)}, bf16[1,96,576]{2,1,0:T(8,128)(2,1)S(1)}, u32[]{:S(2)}, u32[]{:S(2)}) collective-permute-start(bf16[1,96,576]{2,1,0:T(8,128)(2,1)S(1)} %get-tuple-element.57), channel_id=1, source_target_pairs={{0,8},{4,12},{8,0},{12,4},{16,24},{20,28},{24,16},{28,20},{1,9},{5... | collective-permute-start | bytes 331784 | tf_op jit(solution)/shard_map/ppermute | solution.py:27
  (2 other events, 17.4 us)

commit v21 on v20

--- a/solution.py
+++ b/solution.py
@@ -347,32 +347,81 @@
     )[0]
 
 
-def gradients(where, first, count, scores, qk, cot, grads):
-    cols = qk.shape[-1]
-    heads = qk.shape[1] // 2
-    rows = pl.ds(first, count)
-    flat = (count * HEAD_DIM, cols)
-    split = (count, HEAD_DIM, cols)
-    masks = jnp.stack([lane_mask(where[2 + first + r], cols) for r in range(count)])
+def masked(where, value):
+    rows, cols = value.shape[0] // HEAD_DIM, value.shape[1]
+    masks = jnp.stack([lane_mask(where[2 + r], cols) for r in range(rows)])
+    return (value.reshape(rows, HEAD_DIM, cols) * masks).astype(BF16)
+
+
+def query_key_gradients(where, dscore, qk, grads):
+    rows, two, _, cols = qk.shape
+    heads = two // 2
+    flat = (rows * HEAD_DIM, cols)
     for h in range(heads):
-        p, ds = [scores[kind, :, h].reshape(cols, cols) for kind in range(2)]
-        g = cot[rows, h * HEAD_DIM : (h + 1) * HEAD_DIM].reshape(flat)
-        dq = mm(qk[rows, heads + h].reshape(flat), ds, NT)
-        dk = mm(qk[rows, h].reshape(flat), ds, NN)
-        dv = mm(g, p, NN)
-        for index, value in enumerate((dq, dk, dv)):
-            grads[:, index * heads + h] = (value.reshape(split) * masks).astype(BF16)
-
-
-def gradients_kernel(where, scores, qk, cot, grads):
-    gradients(where, 0, qk.shape[0], scores, qk, cot, grads)
-
-
-def all_gradients(where, scores, qk, cot, name, after, counted=True):
+        ds = dscore[:, h].reshape(cols, cols)
+        grads[:, h] = masked(where, mm(qk[:, heads + h].reshape(flat), ds, NT))
+        grads[:, heads + h] = masked(where, mm(qk[:, h].reshape(flat), ds, NN))
+
+
+def value_gradients(where, probs, cot, first, grads):
+    rows, local, cols = cot.shape
+    for h in range(local // HEAD_DIM):
+        g = cot[:, h * HEAD_DIM : (h + 1) * HEAD_DIM].reshape(rows * HEAD_DIM, cols)
+        grads[:, first + h] = masked(where, mm(g, probs[:, h].reshape(cols, cols), NN))
+
+
+def own_query_key_kernel(orders, where, *refs):
+    *pieces, qk, grads, dscore = refs
+    for piece, order in zip(pieces, orders):
+        for t, j in enumerate(order):
+            dscore[where[0] ^ j] = piece[t]
+    query_key_gradients(where, dscore, qk, grads)
+
+
+def own_query_key(where, pieces, orders, qk, shards):
+    return in_vmem(
+        functools.partial(own_query_key_kernel, orders),
+        "own_query_key",
+        (like(qk.shape),),
+        where,
+        *pieces,
+        qk,
+        scalars=1,
+        scratch=(pltpu.VMEM((shards,) + pieces[0].shape[1:], BF16),),
+        limit=14,
+        flops=2 * qk.size * qk.shape[-1],
+    )[0]
+
+
+def own_value_kernel(where, scores, cot, grads):
+    value_gradients(where, scores.at[0], cot, 0, grads)
+
+
+def own_value(where, scores, cot):
+    rows, local, cols = cot.shape
+    return in_vmem(
+        own_value_kernel,
+        "own_value",
+        (like((rows, local // HEAD_DIM, HEAD_DIM, cols)),),
+        where,
+        scores,
+        cot,
+        scalars=1,
+        limit=14,
+        flops=2 * cot.size * cols,
+    )[0]
+
+
+def far_gradients_kernel(where, scores, qk, cot, grads):
+    query_key_gradients(where, scores.at[1], qk, grads)
+    value_gradients(where, scores.at[0], cot, qk.shape[1], grads)
+
+
+def far_gradients(where, scores, qk, cot, after):
     rows, two, _, cols = qk.shape
     return in_vmem(
-        gradients_kernel,
-        name,
+        far_gradients_kernel,
+        "far_gradients",
         (like((rows, two // 2 * 3, HEAD_DIM, cols)),),
         where,
         scores,
@@ -381,27 +430,31 @@
         scalars=1,
         after=after,
         limit=14,
-        counted=counted,
-        flops=3 * rows * two * HEAD_DIM * cols * cols,
+        counted=False,
     )[0]
 
 
-def own_input_kernel(grads, weights, out):
+def all_rows(grads, r):
+    cols = grads[0].shape[-1]
+    return jnp.concatenate([g[r].reshape(g.shape[1] * HEAD_DIM, cols) for g in grads], axis=0)
+
+
+def own_input_kernel(two, value, weights, out):
     near, share, columns = weights.shape
     left = weights[...].reshape(near * share, columns)
-    for r in range(grads.shape[0]):
-        part = mm(left, grads[r].reshape(columns, grads.shape[-1]), NN).astype(BF16)
-        out[:, r] = part.reshape(near, share, grads.shape[-1])
+    for r in range(two.shape[0]):
+        part = mm(left, all_rows((two, value), r), NN).astype(BF16)
+        out[:, r] = part.reshape(near, share, two.shape[-1])
 
 
 def own_input(grads, weights, after):
-    rows, cols = grads.shape[0], grads.shape[-1]
+    rows, cols = grads[0].shape[0], grads[0].shape[-1]
     near, share, columns = weights.shape
     return in_vmem(
         own_input_kernel,
         "own_input",
         (like((near, rows, share, cols)),),
-        grads,
+        *grads,
         weights,
         after=after,
         flops=2 * rows * cols * near * share * columns,
@@ -473,14 +526,13 @@
 
 def weight_product(sheet, grads):
     rows, cols, width = sheet.shape
-    columns = grads.shape[1] * HEAD_DIM
-    left = [grads[r].reshape(columns, cols) for r in range(rows)]
+    left = [all_rows(grads, r) for r in range(rows)]
     return mm(jnp.concatenate(left, axis=1), sheet[...].reshape(rows * cols, width), NN).T
 
 
-def weight_kernel(bits, where, sheet, grads, *rest):
+def weight_kernel(bits, where, sheet, two, value, *rest):
     outs, full = rest[:-1], rest[-1]
-    full[...] = weight_product(sheet, grads).reshape(full.shape)
+    full[...] = weight_product(sheet, (two, value)).reshape(full.shape)
     for t, j in enumerate(reorder(bits)):
         first = 0
         for keep, give in zip(outs[::2], outs[1::2]):
@@ -490,14 +542,14 @@
             first = last
 
 
-def whole_weight_kernel(_, where, sheet, grads, out):
-    out[...] = weight_product(sheet, grads)
+def whole_weight_kernel(_, where, sheet, two, value, out):
+    out[...] = weight_product(sheet, (two, value))
 
 
 def weight_part(where, sheet, grads, cuts, bits, after):
     rows, cols, width = sheet.shape
     shards = 1 << len(bits)
-    columns = grads.shape[1] * HEAD_DIM
+    columns = sum(g.shape[1] for g in grads) * HEAD_DIM
     if shards == 1:
         kernel, outs, scratch = whole_weight_kernel, [like((width, columns), F32)], ()
     else:
@@ -511,7 +563,7 @@
         outs,
         where,
         sheet,
-        grads,
+        *grads,
         scalars=1,
         after=after,
         scratch=scratch,
@@ -562,14 +614,17 @@
         logits = halve(*logits, "rows", turn_about)
         dprob = halve(*dprob, "rows", up)
         probs, dscore = softmax_back(logits, dprob, scale, [weights])
-        probs, probs_order = double(probs, "rows", up[::-1], [far_cot])
+        probs, probs_order = double(probs, "rows", up[::-1], [far_cot, fq])
         dscore, dscore_order = double(dscore, "rows", turn_about[::-1])
-        scores = assemble(where, probs, dscore, (probs_order, dscore_order), shards, fq)
+        two = own_query_key(where, dscore, dscore_order, qk, shards)
+        scores = assemble(where, probs, dscore, (probs_order, dscore_order), shards, [two])
     else:
         logits, dprob = lax.psum((logits, dprob), "rows")
-        scores = jnp.stack(softmax_back(logits, dprob, scale))
+        probs, dscore = softmax_back(logits, dprob, scale)
+        two = own_query_key(where, [dscore], [[0]], qk, shards)
+        scores = jnp.stack([probs, dscore])
     far_scores = [flip(scores, "heads", f) for f in fars]
-    grads = all_gradients(where, scores, qk, cot, "own_gradients", ())
+    grads = two, own_value(where, scores, cot)
     weight_bits = up[:1] + up[1:][::-1]
     parts = weight_part(where, held, grads, (3 * local,), weight_bits, fv)
     ready = [parts[-1]]
@@ -586,7 +641,7 @@
         weight_grad = lax.psum_scatter(parts[0], "rows", scatter_dimension=0, tiled=True)
         weight_grad = weight_grad.reshape(width // n_rows, 3, local)
     far_grads = [
-        all_gradients(where, *args, "far_gradients", first_sum, False)
+        far_gradients(where, *args, first_sum)
         for args in zip(far_scores, far_qk, far_cot)
     ]
     chunks = []

time: 85.9 us -> 87.1 us (1.014)
  waiting for transfers between devices: 22.5 us -> 23.9 us
  starting transfers between devices: 28.7 us -> 27.8 us
    ppermute x22, waiting for transfers between devices: 22.5 us -> 23.9 us  [flip(): return lax.ppermute(values, axis, [(s, s ^ bit) for s in range(n)])]
    ppermute x22, starting transfers between devices: 28.7 us -> 27.8 us  [flip(): return lax.ppermute(values, axis, [(s, s ^ bit) for s in range(n)])]
    pallas_call x24 -> x25, Pallas kernels: 32.1 us -> 32.9 us  [in_vmem(): pl.pallas_call(run, in_specs=[SMEM] * scalars + [HBM] * streamed + [VMEM]...]
  transfers between devices with their start and end apart: 22 -> 22, of which waited for: 15 -> 16; matrix products, arithmetic and copies ran while one was open for 0% -> 0% of each run, Pallas kernels for 38% -> 38%
where the time goes in v21:
time: 87.1 us; the launch traced here: 86.9 us
  Pallas kernels  34.2 us (39%)
  starting transfers between devices  27.8 us (32%)
  waiting for transfers between devices  23.9 us (27%)
    pallas_call x25, Pallas kernels, in_vmem(): pl.pallas_call(run, in_specs=[SMEM] * scalars + [HBM] * streamed + [VMEM]...  32.9 us
    ppermute x22, starting transfers between devices, flip(): return lax.ppermute(values, axis, [(s, s ^ bit) for s in range(n)])  27.8 us
    ppermute x22, waiting for transfers between devices, flip(): return lax.ppermute(values, axis, [(s, s ^ bit) for s in range(n)])  23.9 us
  transfers between devices with their start and end apart: 22, of which 16 were waited for; matrix products, arithmetic and copies ran while one was open for 0% of the time, Pallas kernels for 38%

profile of v21, /device:TPU:0, one launch (start us, length us, event | category | flops | bytes accessed | tf_op | source)
XLA Modules:
  0.0 86.9 jit_solution(2532244409823479863)
XLA Ops:
  0.6 3.0 %collective-permute-start.10 = (bf16[16,192,256]{2,1,0:T(8,128)(2,1)}, bf16[16,192,256]{2,1,0:T(8,128)(2,1)S(1)}, u32[]{:S(2)}, u32[]{:S(2)}) collective-permute-start(bf16[16,192,256]{2,1,0:T(8,128)(2,1)} %bitcast.10), channel_id=1, source_target_pairs={{0,2},{1,3},{2,0},{3,1},{4,6},{5,7},{6,4},{7,5},{8,10},{9,11},{10,... | collective-permute-start | bytes 4718600 | tf_op jit(solution)/shard_map/ppermute | solution.py:27
  3.7 7.0 %query_key.1 = (bf16[16,6,64,256]{3,2,1,0:T(8,128)(2,1)S(1)}, bf16[16,256,768]{2,1,0:T(8,128)(2,1)S(1)}, s32[1,16]{1,0:T(1,128)S(1)}, f32[4,3,32,256]{3,2,1,0:T(8,128)S(1)}, bf16[4,3,32,256]{3,2,1,0:T(8,128)(2,1)S(1)}) custom-call(s32[2]{0:T(128)S(1)} %pad_add_fusion.refs_0_, s32[1,16]{1,0:T(1,128)} %bitcast.24, bf16[16,256,768]{2,1,0:T(8,128)(2,1)} %refs_2_.1, ...), custom_call_target="tpu_custom_call" | custom-call | flops 704643072 | bytes 16711748 | tf_op jit(solution)/shard_map/query_key/pallas_call | solution.py:56
  10.7 1.6 %collective-permute-start = (bf16[4,3,32,256]{3,2,1,0:T(8,128)(2,1)S(1)}, bf16[4,3,32,256]{3,2,1,0:T(8,128)(2,1)S(1)}, u32[]{:S(2)}, u32[]{:S(2)}) collective-permute-start(bf16[4,3,32,256]{3,2,1,0:T(8,128)(2,1)S(1)} %get-tuple-element.32.refs_4_), channel_id=1, source_target_pairs={{0,8},{4,12},{8,0},{12,4},{16,24},{20,28},{24,16},{28,20},{1,9},{5... | collective-permute-start | bytes 589832 | tf_op jit(solution)/shard_map/ppermute | solution.py:27
  12.5 3.7 %value_dprob.1 = (f32[4,3,32,256]{3,2,1,0:T(8,128)S(1)}, bf16[4,3,32,256]{3,2,1,0:T(8,128)(2,1)S(1)}, bf16[192,384]{1,0:T(8,128)(2,1)S(1)}) custom-call(s32[18]{0:T(128)S(1)} %pad_add_fusion.1.refs_0_, bf16[16,256,768]{2,1,0:T(8,128)(2,1)S(1)} %get-tuple-element.37.refs_1_, bf16[192,768]{1,0:T(8,128)(2,1)S(1)} %bitcast.19, ...), custom_call_target="tpu_custom_call" | custom-call | flops 3221225472 | bytes 8699940 | tf_op jit(solution)/shard_map/value_dprob/pallas_call | solution.py:56
  16.2 1.6 %collective-permute-start.3 = (bf16[4,3,32,256]{3,2,1,0:T(8,128)(2,1)S(1)}, bf16[4,3,32,256]{3,2,1,0:T(8,128)(2,1)S(1)}, u32[]{:S(2)}, u32[]{:S(2)}) collective-permute-start(bf16[4,3,32,256]{3,2,1,0:T(8,128)(2,1)S(1)} %get-tuple-element.39.refs_4_), channel_id=1, source_target_pairs={{0,4},{4,0},{8,12},{12,8},{16,20},{20,16},{24,28},{28,24},{1,5},{5... | collective-permute-start | bytes 589832 | tf_op jit(solution)/shard_map/ppermute | solution.py:27
  17.8 2.7 %collective-permute-start.1 = (bf16[2,3,32,256]{3,2,1,0:T(8,128)(2,1)S(1)}, bf16[2,3,32,256]{3,2,1,0:T(8,128)(2,1)S(1)}, u32[]{:S(2)}, u32[]{:S(2)}) collective-permute-start(bf16[2,3,32,256]{3,2,1,0:T(8,128)(2,1)S(1)} %get-tuple-element.34), channel_id=1, source_target_pairs={{0,16},{4,20},{8,24},{12,28},{16,0},{20,4},{24,8},{28,12},{1,17},{... | collective-permute-start | bytes 294920 | tf_op jit(solution)/shard_map/ppermute | solution.py:27
  20.5 1.9 %collective-permute-done.3.refs_1_ = bf16[4,3,32,256]{3,2,1,0:T(8,128)(2,1)S(1)} collective-permute-done((bf16[4,3,32,256]{3,2,1,0:T(8,128)(2,1)S(1)}, bf16[4,3,32,256]{3,2,1,0:T(8,128)(2,1)S(1)}, u32[]{:S(2)}, u32[]{:S(2)}) %collective-permute-start.3) | collective-permute-done | bytes 196640 | tf_op jit(solution)/shard_map/ppermute | solution.py:27
  25.0 2.1 %collective-permute-done.4.refs_1_ = bf16[2,3,32,256]{3,2,1,0:T(8,128)(2,1)S(1)} collective-permute-done((bf16[2,3,32,256]{3,2,1,0:T(8,128)(2,1)S(1)}, bf16[2,3,32,256]{3,2,1,0:T(8,128)(2,1)S(1)}, u32[]{:S(2)}, u32[]{:S(2)}) %collective-permute-start.4) | collective-permute-done | bytes 98336 | tf_op jit(solution)/shard_map/ppermute | solution.py:27
  27.1 2.8 %collective-permute-start.5 = (bf16[1,3,32,256]{3,2,1,0:T(8,128)(2,1)S(1)}, bf16[1,3,32,256]{3,2,1,0:T(8,128)(2,1)S(1)}, u32[]{:S(2)}, u32[]{:S(2)}) collective-permute-start(bf16[1,3,32,256]{3,2,1,0:T(8,128)(2,1)S(1)} %get-tuple-element.43), channel_id=1, source_target_pairs={{0,16},{4,20},{8,24},{12,28},{16,0},{20,4},{24,8},{28,12},{1,17},{... | collective-permute-start | bytes 147464 | tf_op jit(solution)/shard_map/ppermute | solution.py:27
  31.0 1.6 %collective-permute-done.5.refs_3_ = bf16[1,3,32,256]{3,2,1,0:T(8,128)(2,1)S(1)} collective-permute-done((bf16[1,3,32,256]{3,2,1,0:T(8,128)(2,1)S(1)}, bf16[1,3,32,256]{3,2,1,0:T(8,128)(2,1)S(1)}, u32[]{:S(2)}, u32[]{:S(2)}) %collective-permute-start.5) | collective-permute-done | bytes 49184 | tf_op jit(solution)/shard_map/ppermute | solution.py:27
  32.8 1.6 %collective-permute-start.6 = (bf16[1,3,32,256]{3,2,1,0:T(8,128)(2,1)S(1)}, bf16[1,3,32,256]{3,2,1,0:T(8,128)(2,1)S(1)}, u32[]{:S(2)}, u32[]{:S(2)}) collective-permute-start(bf16[1,3,32,256]{3,2,1,0:T(8,128)(2,1)S(1)} %get-tuple-element.44.refs_0_), channel_id=1, source_target_pairs={{0,4},{4,0},{8,12},{12,8},{16,20},{20,16},{24,28},{28,24},{1,5},{5... | collective-permute-start | bytes 147464 | tf_op jit(solution)/shard_map/ppermute | solution.py:27
  34.4 2.6 %collective-permute-done.6.refs_1_ = bf16[1,3,32,256]{3,2,1,0:T(8,128)(2,1)S(1)} collective-permute-done((bf16[1,3,32,256]{3,2,1,0:T(8,128)(2,1)S(1)}, bf16[1,3,32,256]{3,2,1,0:T(8,128)(2,1)S(1)}, u32[]{:S(2)}, u32[]{:S(2)}) %collective-permute-start.6) | collective-permute-done | bytes 49184 | tf_op jit(solution)/shard_map/ppermute | solution.py:27
  37.0 2.4 %collective-permute-start.7 = (bf16[2,3,32,256]{3,2,1,0:T(8,128)(2,1)S(1)}, bf16[2,3,32,256]{3,2,1,0:T(8,128)(2,1)S(1)}, u32[]{:S(2)}, u32[]{:S(2)}) collective-permute-start(bf16[2,3,32,256]{3,2,1,0:T(8,128)(2,1)S(1)} %join.4.refs_0_), channel_id=1, source_target_pairs={{0,16},{4,20},{8,24},{12,28},{16,0},{20,4},{24,8},{28,12},{1,17},{... | collective-permute-start | bytes 294920 | tf_op jit(solution)/shard_map/ppermute | solution.py:27
  40.0 4.9 %collective-permute-done.9.refs_1_ = bf16[1,3,32,256]{3,2,1,0:T(8,128)(2,1)S(1)} collective-permute-done((bf16[1,3,32,256]{3,2,1,0:T(8,128)(2,1)S(1)}, bf16[1,3,32,256]{3,2,1,0:T(8,128)(2,1)S(1)}, u32[]{:S(2)}, u32[]{:S(2)}) %collective-permute-start.9) | collective-permute-done | bytes 49184 | tf_op jit(solution)/shard_map/ppermute | solution.py:27
  45.2 1.8 %collective-permute-start.8 = (bf16[4,3,32,256]{3,2,1,0:T(8,128)(2,1)S(1)}, bf16[4,3,32,256]{3,2,1,0:T(8,128)(2,1)S(1)}, u32[]{:S(2)}, u32[]{:S(2)}) collective-permute-start(bf16[4,3,32,256]{3,2,1,0:T(8,128)(2,1)S(1)} %join.5.refs_1_.refs_3_), channel_id=1, source_target_pairs={{0,8},{4,12},{8,0},{12,4},{16,24},{20,28},{24,16},{28,20},{1,9},{5... | collective-permute-start | bytes 589832 | tf_op jit(solution)/shard_map/ppermute | solution.py:27
  47.0 2.5 %collective-permute-done.11.refs_1_ = bf16[2,3,32,256]{3,2,1,0:T(8,128)(2,1)S(1)} collective-permute-done((bf16[2,3,32,256]{3,2,1,0:T(8,128)(2,1)S(1)}, bf16[2,3,32,256]{3,2,1,0:T(8,128)(2,1)S(1)}, u32[]{:S(2)}, u32[]{:S(2)}) %collective-permute-start.11) | collective-permute-done | bytes 98336 | tf_op jit(solution)/shard_map/ppermute | solution.py:27
  49.6 1.6 %collective-permute-start.13 = (bf16[4,3,32,256]{3,2,1,0:T(8,128)(2,1)S(1)}, bf16[4,3,32,256]{3,2,1,0:T(8,128)(2,1)S(1)}, u32[]{:S(2)}, u32[]{:S(2)}) collective-permute-start(bf16[4,3,32,256]{3,2,1,0:T(8,128)(2,1)S(1)} %join.7.refs_1_), channel_id=1, source_target_pairs={{0,4},{4,0},{8,12},{12,8},{16,20},{20,16},{24,28},{28,24},{1,5},{5... | collective-permute-start | bytes 589832 | tf_op jit(solution)/shard_map/ppermute | solution.py:27
  53.2 1.6 %own_query_key.1.refs_5_.refs_2_.refs_0_ = bf16[16,6,64,256]{3,2,1,0:T(8,128)(2,1)S(1)} custom-call(s32[18]{0:T(128)S(1)} %pad_add_fusion.1.refs_0_, bf16[4,3,32,256]{3,2,1,0:T(8,128)(2,1)S(1)} %join.5.refs_1_.refs_3_, bf16[4,3,32,256]{3,2,1,0:T(8,128)(2,1)S(1)} %collective-permute-done.8.refs_2_.refs_4_, bf16[16,6,64,256]{3,2,1,0:T(8,128)(2,1)S(1)} %get-tuple-element.45.refs_3_), custom_call_target="tpu_custom_call" | custom-call | flops 805306368 | bytes 6684708 | tf_op jit(solution)/shard_map/own_query_key/pallas_call | solution.py:56
  57.9 4.7 %weight_part.1 = (f32[4,96,576]{2,1,0:T(8,128)S(1)}, bf16[4,96,576]{2,1,0:T(8,128)(2,1)S(1)}) custom-call(s32[18]{0:T(128)S(1)} %pad_add_fusion.1.refs_0_, bf16[16,256,768]{2,1,0:T(8,128)(2,1)S(1)} %get-tuple-element.37.refs_1_, bf16[16,6,64,256]{3,2,1,0:T(8,128)(2,1)S(1)} %own_query_key.1.refs_5_.refs_2_.refs_0_, ...), custom_call_target="tpu_custom_call" | custom-call | flops 3623878656 | bytes 11894820 | tf_op jit(solution)/shard_map/weight_part/pallas_call | solution.py:56
  65.3 2.6 %own_input.1.refs_2_.refs_0_ = bf16[2,16,192,256]{3,2,1,0:T(8,128)(2,1)S(1)} custom-call(bf16[16,6,64,256]{3,2,1,0:T(8,128)(2,1)S(1)} %own_query_key.1.refs_5_.refs_2_.refs_0_, bf16[16,3,64,256]{3,2,1,0:T(8,128)(2,1)S(1)} %own_value.1.refs_3_.refs_1_, bf16[2,192,576]{2,1,0:T(8,128)(2,1)S(1)} %turn.2.refs_4_.refs_2_, ...), custom_call_target="tpu_custom_call" | custom-call | flops 1811939328 | bytes 8306688 | tf_op jit(solution)/shard_map/own_input/pallas_call | solution.py:56
  67.9 3.4 %far_query_key.1.refs_3_.refs_2_ = bf16[16,6,64,256]{3,2,1,0:T(8,128)(2,1)S(1)} custom-call(s32[18]{0:T(128)S(1)} %pad_add_fusion.1.refs_0_, bf16[16,256,768]{2,1,0:T(8,128)(2,1)S(1)} %get-tuple-element.37.refs_1_, bf16[192,768]{1,0:T(8,128)(2,1)S(1)} %collective-permute-done.12.refs_2_.refs_1_, ...), custom_call_target="tpu_custom_call" | custom-call | flops 2415919104 | bytes 10027044 | tf_op jit(solution)/shard_map/far_query_key/pallas_call | solution.py:56
  71.6 2.3 %collective-permute-start.20 = (bf16[2,96,576]{2,1,0:T(8,128)(2,1)S(1)}, bf16[2,96,576]{2,1,0:T(8,128)(2,1)S(1)}, u32[]{:S(2)}, u32[]{:S(2)}) collective-permute-start(bf16[2,96,576]{2,1,0:T(8,128)(2,1)S(1)} %get-tuple-element.55), channel_id=1, source_target_pairs={{0,16},{4,20},{8,24},{12,28},{16,0},{20,4},{24,8},{28,12},{1,17},{... | collective-permute-start | bytes 663560 | tf_op jit(solution)/shard_map/ppermute | solution.py:27
  74.4 1.9 %far_gradients.1.refs_1_ = bf16[16,9,64,256]{3,2,1,0:T(8,128)(2,1)S(1)} custom-call(s32[18]{0:T(128)S(1)} %pad_add_fusion.1.refs_0_, bf16[2,8,3,32,256]{4,3,2,1,0:T(8,128)(2,1)S(1)} %collective-permute-done.15.refs_1_, bf16[16,6,64,256]{3,2,1,0:T(8,128)(2,1)S(1)} %far_query_key.1.refs_3_.refs_2_, ...), custom_call_target="tpu_custom_call" | custom-call | tf_op jit(solution)/shard_map/far_gradients/pallas_call | solution.py:56
  84.0 2.1 %collective-permute-done.21.refs_2_ = bf16[1,96,576]{2,1,0:T(8,128)(2,1)S(1)} collective-permute-done((bf16[1,96,576]{2,1,0:T(8,128)(2,1)S(1)}, bf16[1,96,576]{2,1,0:T(8,128)(2,1)S(1)}, u32[]{:S(2)}, u32[]{:S(2)}) %collective-permute-start.21) | collective-permute-done | bytes 110624 | tf_op jit(solution)/shard_map/ppermute | solution.py:27
  (56 shorter events, 22.2 us)
Async XLA Ops:
  0.6 44.2 %collective-permute-start.10 = (bf16[16,192,256]{2,1,0:T(8,128)(2,1)}, bf16[16,192,256]{2,1,0:T(8,128)(2,1)S(1)}, u32[]{:S(2)}, u32[]{:S(2)}) collective-permute-start(bf16[16,192,256]{2,1,0:T(8,128)(2,1)} %bitcast.10), channel_id=1, source_target_pairs={{0,2},{1,3},{2,0},{3,1},{4,6},{5,7},{6,4},{7,5},{8,10},{9,11},{10,... | collective-permute-start | bytes 4718600 | tf_op jit(solution)/shard_map/ppermute | solution.py:27
  10.7 7.0 %collective-permute-start = (bf16[4,3,32,256]{3,2,1,0:T(8,128)(2,1)S(1)}, bf16[4,3,32,256]{3,2,1,0:T(8,128)(2,1)S(1)}, u32[]{:S(2)}, u32[]{:S(2)}) collective-permute-start(bf16[4,3,32,256]{3,2,1,0:T(8,128)(2,1)S(1)} %get-tuple-element.32.refs_4_), channel_id=1, source_target_pairs={{0,8},{4,12},{8,0},{12,4},{16,24},{20,28},{24,16},{28,20},{1,9},{5... | collective-permute-start | bytes 589832 | tf_op jit(solution)/shard_map/ppermute | solution.py:27
  12.4 10.5 %copy-start.1 = (bf16[768,192]{0,1:T(8,128)(2,1)S(1)}, bf16[768,192]{0,1:T(8,128)(2,1)}, u32[]{:S(2)}) copy-start(bf16[768,192]{0,1:T(8,128)(2,1)} %param.7) | copy-start | bytes 884740
  12.4 17.5 %copy-start.2 = (bf16[768,192]{0,1:T(8,128)(2,1)S(1)}, bf16[768,192]{0,1:T(8,128)(2,1)}, u32[]{:S(2)}) copy-start(bf16[768,192]{0,1:T(8,128)(2,1)} %param.8) | copy-start | bytes 884740
  16.2 6.1 %collective-permute-start.3 = (bf16[4,3,32,256]{3,2,1,0:T(8,128)(2,1)S(1)}, bf16[4,3,32,256]{3,2,1,0:T(8,128)(2,1)S(1)}, u32[]{:S(2)}, u32[]{:S(2)}) collective-permute-start(bf16[4,3,32,256]{3,2,1,0:T(8,128)(2,1)S(1)} %get-tuple-element.39.refs_4_), channel_id=1, source_target_pairs={{0,4},{4,0},{8,12},{12,8},{16,20},{20,16},{24,28},{28,24},{1,5},{5... | collective-permute-start | bytes 589832 | tf_op jit(solution)/shard_map/ppermute | solution.py:27
  17.8 6.9 %collective-permute-start.1 = (bf16[2,3,32,256]{3,2,1,0:T(8,128)(2,1)S(1)}, bf16[2,3,32,256]{3,2,1,0:T(8,128)(2,1)S(1)}, u32[]{:S(2)}, u32[]{:S(2)}) collective-permute-start(bf16[2,3,32,256]{3,2,1,0:T(8,128)(2,1)S(1)} %get-tuple-element.34), channel_id=1, source_target_pairs={{0,16},{4,20},{8,24},{12,28},{16,0},{20,4},{24,8},{28,12},{1,17},{... | collective-permute-start | bytes 294920 | tf_op jit(solution)/shard_map/ppermute | solution.py:27
  22.4 4.7 %collective-permute-start.4 = (bf16[2,3,32,256]{3,2,1,0:T(8,128)(2,1)S(1)}, bf16[2,3,32,256]{3,2,1,0:T(8,128)(2,1)S(1)}, u32[]{:S(2)}, u32[]{:S(2)}) collective-permute-start(bf16[2,3,32,256]{3,2,1,0:T(8,128)(2,1)S(1)} %get-tuple-element.41), channel_id=1, source_target_pairs={{0,8},{4,12},{8,0},{12,4},{16,24},{20,28},{24,16},{28,20},{1,9},{5... | collective-permute-start | bytes 294920 | tf_op jit(solution)/shard_map/ppermute | solution.py:27
  22.9 24.1 %collective-permute-start.12 = (bf16[192,768]{1,0:T(8,128)(2,1)S(1)}, bf16[192,768]{1,0:T(8,128)(2,1)S(1)}, u32[]{:S(2)}, u32[]{:S(2)}) collective-permute-start(bf16[192,768]{1,0:T(8,128)(2,1)S(1)} %bitcast.14), channel_id=1, source_target_pairs={{0,2},{1,3},{2,0},{3,1},{4,6},{5,7},{6,4},{7,5},{8,10},{9,11},{10,... | collective-permute-start | bytes 884744 | tf_op jit(solution)/shard_map/ppermute | solution.py:27
  24.7 6.3 %collective-permute-start.2 = (bf16[1,3,32,256]{3,2,1,0:T(8,128)(2,1)S(1)}, bf16[1,3,32,256]{3,2,1,0:T(8,128)(2,1)S(1)}, u32[]{:S(2)}, u32[]{:S(2)}) collective-permute-start(bf16[1,3,32,256]{3,2,1,0:T(8,128)(2,1)S(1)} %get-tuple-element.36), channel_id=1, source_target_pairs={{0,4},{4,0},{8,12},{12,8},{16,20},{20,16},{24,28},{28,24},{1,5},{5... | collective-permute-start | bytes 147464 | tf_op jit(solution)/shard_map/ppermute | solution.py:27
  27.1 5.5 %collective-permute-start.5 = (bf16[1,3,32,256]{3,2,1,0:T(8,128)(2,1)S(1)}, bf16[1,3,32,256]{3,2,1,0:T(8,128)(2,1)S(1)}, u32[]{:S(2)}, u32[]{:S(2)}) collective-permute-start(bf16[1,3,32,256]{3,2,1,0:T(8,128)(2,1)S(1)} %get-tuple-element.43), channel_id=1, source_target_pairs={{0,16},{4,20},{8,24},{12,28},{16,0},{20,4},{24,8},{28,12},{1,17},{... | collective-permute-start | bytes 147464 | tf_op jit(solution)/shard_map/ppermute | solution.py:27
  32.8 4.2 %collective-permute-start.6 = (bf16[1,3,32,256]{3,2,1,0:T(8,128)(2,1)S(1)}, bf16[1,3,32,256]{3,2,1,0:T(8,128)(2,1)S(1)}, u32[]{:S(2)}, u32[]{:S(2)}) collective-permute-start(bf16[1,3,32,256]{3,2,1,0:T(8,128)(2,1)S(1)} %get-tuple-element.44.refs_0_), channel_id=1, source_target_pairs={{0,4},{4,0},{8,12},{12,8},{16,20},{20,16},{24,28},{28,24},{1,5},{5... | collective-permute-start | bytes 147464 | tf_op jit(solution)/shard_map/ppermute | solution.py:27
  37.0 8.2 %collective-permute-start.7 = (bf16[2,3,32,256]{3,2,1,0:T(8,128)(2,1)S(1)}, bf16[2,3,32,256]{3,2,1,0:T(8,128)(2,1)S(1)}, u32[]{:S(2)}, u32[]{:S(2)}) collective-permute-start(bf16[2,3,32,256]{3,2,1,0:T(8,128)(2,1)S(1)} %join.4.refs_0_), channel_id=1, source_target_pairs={{0,16},{4,20},{8,24},{12,28},{16,0},{20,4},{24,8},{28,12},{1,17},{... | collective-permute-start | bytes 294920 | tf_op jit(solution)/shard_map/ppermute | solution.py:27
  39.4 5.4 %collective-permute-start.9 = (bf16[1,3,32,256]{3,2,1,0:T(8,128)(2,1)S(1)}, bf16[1,3,32,256]{3,2,1,0:T(8,128)(2,1)S(1)}, u32[]{:S(2)}, u32[]{:S(2)}) collective-permute-start(bf16[1,3,32,256]{3,2,1,0:T(8,128)(2,1)S(1)} %get-tuple-element.46.refs_0_), channel_id=1, source_target_pairs={{0,16},{4,20},{8,24},{12,28},{16,0},{20,4},{24,8},{28,12},{1,17},{... | collective-permute-start | bytes 147464 | tf_op jit(solution)/shard_map/ppermute | solution.py:27
  44.9 4.7 %collective-permute-start.11 = (bf16[2,3,32,256]{3,2,1,0:T(8,128)(2,1)S(1)}, bf16[2,3,32,256]{3,2,1,0:T(8,128)(2,1)S(1)}, u32[]{:S(2)}, u32[]{:S(2)}) collective-permute-start(bf16[2,3,32,256]{3,2,1,0:T(8,128)(2,1)S(1)} %join.6.refs_0_), channel_id=1, source_target_pairs={{0,8},{4,12},{8,0},{12,4},{16,24},{20,28},{24,16},{28,20},{1,9},{5... | collective-permute-start | bytes 294920 | tf_op jit(solution)/shard_map/ppermute | solution.py:27
  45.2 8.0 %collective-permute-start.8 = (bf16[4,3,32,256]{3,2,1,0:T(8,128)(2,1)S(1)}, bf16[4,3,32,256]{3,2,1,0:T(8,128)(2,1)S(1)}, u32[]{:S(2)}, u32[]{:S(2)}) collective-permute-start(bf16[4,3,32,256]{3,2,1,0:T(8,128)(2,1)S(1)} %join.5.refs_1_.refs_3_), channel_id=1, source_target_pairs={{0,8},{4,12},{8,0},{12,4},{16,24},{20,28},{24,16},{28,20},{1,9},{5... | collective-permute-start | bytes 589832 | tf_op jit(solution)/shard_map/ppermute | solution.py:27
  49.6 5.7 %collective-permute-start.13 = (bf16[4,3,32,256]{3,2,1,0:T(8,128)(2,1)S(1)}, bf16[4,3,32,256]{3,2,1,0:T(8,128)(2,1)S(1)}, u32[]{:S(2)}, u32[]{:S(2)}) collective-permute-start(bf16[4,3,32,256]{3,2,1,0:T(8,128)(2,1)S(1)} %join.7.refs_1_), channel_id=1, source_target_pairs={{0,4},{4,0},{8,12},{12,8},{16,20},{20,16},{24,28},{28,24},{1,5},{5... | collective-permute-start | bytes 589832 | tf_op jit(solution)/shard_map/ppermute | solution.py:27
  51.1 6.8 %collective-permute-start.14 = (bf16[192,384]{1,0:T(8,128)(2,1)S(1)}, bf16[192,384]{1,0:T(8,128)(2,1)S(1)}, u32[]{:S(2)}, u32[]{:S(2)}) collective-permute-start(bf16[192,384]{1,0:T(8,128)(2,1)S(1)} %get-tuple-element.47), channel_id=1, source_target_pairs={{0,2},{1,3},{2,0},{3,1},{4,6},{5,7},{6,4},{7,5},{8,10},{9,11},{10,... | collective-permute-start | bytes 442376 | tf_op jit(solution)/shard_map/ppermute | solution.py:27
  51.6 12.6 %collective-permute-start.16 = (bf16[192,768]{1,0:T(8,128)(2,1)S(1)}, bf16[192,768]{1,0:T(8,128)(2,1)S(1)}, u32[]{:S(2)}, u32[]{:S(2)}) collective-permute-start(bf16[192,768]{1,0:T(8,128)(2,1)S(1)} %bitcast.18), channel_id=1, source_target_pairs={{0,2},{1,3},{2,0},{3,1},{4,6},{5,7},{6,4},{7,5},{8,10},{9,11},{10,... | collective-permute-start | bytes 884744 | tf_op jit(solution)/shard_map/ppermute | solution.py:27
  55.9 18.5 %collective-permute-start.15 = (bf16[2,8,3,32,256]{4,3,2,1,0:T(8,128)(2,1)S(1)}, bf16[2,8,3,32,256]{4,3,2,1,0:T(8,128)(2,1)S(1)}, u32[]{:S(2)}, u32[]{:S(2)}) collective-permute-start(bf16[2,8,3,32,256]{4,3,2,1,0:T(8,128)(2,1)S(1)} %assemble.1.refs_1_), channel_id=1, source_target_pairs={{0,2},{1,3},{2,0},{3,1},{4,6},{5,7},{6,4},{7,5},{8,10},{9,11},{10,... | collective-permute-start | bytes 2359304 | tf_op jit(solution)/shard_map/ppermute | solution.py:27
  62.7 8.9 %collective-permute-start.17 = (bf16[4,96,576]{2,1,0:T(8,128)(2,1)S(1)}, bf16[4,96,576]{2,1,0:T(8,128)(2,1)S(1)}, u32[]{:S(2)}, u32[]{:S(2)}) collective-permute-start(bf16[4,96,576]{2,1,0:T(8,128)(2,1)S(1)} %get-tuple-element.48.refs_3_.refs_4_), channel_id=1, source_target_pairs={{0,4},{4,0},{8,12},{12,8},{16,20},{20,16},{24,28},{28,24},{1,5},{5... | collective-permute-start | bytes 1327112 | tf_op jit(solution)/shard_map/ppermute | solution.py:27
  71.6 9.5 %collective-permute-start.20 = (bf16[2,96,576]{2,1,0:T(8,128)(2,1)S(1)}, bf16[2,96,576]{2,1,0:T(8,128)(2,1)S(1)}, u32[]{:S(2)}, u32[]{:S(2)}) collective-permute-start(bf16[2,96,576]{2,1,0:T(8,128)(2,1)S(1)} %get-tuple-element.55), channel_id=1, source_target_pairs={{0,16},{4,20},{8,24},{12,28},{16,0},{20,4},{24,8},{28,12},{1,17},{... | collective-permute-start | bytes 663560 | tf_op jit(solution)/shard_map/ppermute | solution.py:27
  79.2 2.4 %collective-permute-start.18 = (bf16[8,192,256]{2,1,0:T(8,128)(2,1)S(1)}, bf16[8,192,256]{2,1,0:T(8,128)(2,1)S(1)}, u32[]{:S(2)}, u32[]{:S(2)}) collective-permute-start(bf16[8,192,256]{2,1,0:T(8,128)(2,1)S(1)} %get-tuple-element.52), channel_id=1, source_target_pairs={{0,1},{1,0},{2,3},{3,2},{4,5},{5,4},{6,7},{7,6},{8,9},{9,8},{10,11... | collective-permute-start | bytes 2359304 | tf_op jit(solution)/shard_map/ppermute | solution.py:27
  79.2 3.4 %collective-permute-start.19 = (bf16[8,192,256]{2,1,0:T(8,128)(2,1)S(1)}, bf16[8,192,256]{2,1,0:T(8,128)(2,1)S(1)}, u32[]{:S(2)}, u32[]{:S(2)}) collective-permute-start(bf16[8,192,256]{2,1,0:T(8,128)(2,1)S(1)} %get-tuple-element.54), channel_id=1, source_target_pairs={{0,1},{1,0},{2,3},{3,2},{4,5},{5,4},{6,7},{7,6},{8,9},{9,8},{10,11... | collective-permute-start | bytes 2359304 | tf_op jit(solution)/shard_map/ppermute | solution.py:27
  81.2 4.9 %collective-permute-start.21 = (bf16[1,96,576]{2,1,0:T(8,128)(2,1)S(1)}, bf16[1,96,576]{2,1,0:T(8,128)(2,1)S(1)}, u32[]{:S(2)}, u32[]{:S(2)}) collective-permute-start(bf16[1,96,576]{2,1,0:T(8,128)(2,1)S(1)} %get-tuple-element.57), channel_id=1, source_target_pairs={{0,8},{4,12},{8,0},{12,4},{16,24},{20,28},{24,16},{28,20},{1,9},{5... | collective-permute-start | bytes 331784 | tf_op jit(solution)/shard_map/ppermute | solution.py:27
  (2 other events, 17.4 us)

commit v22 on v20

--- a/solution.py
+++ b/solution.py
@@ -562,9 +562,9 @@
         logits = halve(*logits, "rows", turn_about)
         dprob = halve(*dprob, "rows", up)
         probs, dscore = softmax_back(logits, dprob, scale, [weights])
-        probs, probs_order = double(probs, "rows", up[::-1], [far_cot])
+        probs, probs_order = double(probs, "rows", up[::-1], [far_cot, fq])
         dscore, dscore_order = double(dscore, "rows", turn_about[::-1])
-        scores = assemble(where, probs, dscore, (probs_order, dscore_order), shards, fq)
+        scores = assemble(where, probs, dscore, (probs_order, dscore_order), shards, ())
     else:
         logits, dprob = lax.psum((logits, dprob), "rows")
         scores = jnp.stack(softmax_back(logits, dprob, scale))

time: 85.9 us -> 87.7 us (1.021)
  starting transfers between devices: 28.7 us -> 31 us
    ppermute x22, starting transfers between devices: 28.7 us -> 31 us  [flip(): return lax.ppermute(values, axis, [(s, s ^ bit) for s in range(n)])]
  transfers between devices with their start and end apart: 22 -> 22, of which waited for: 15 -> 14; matrix products, arithmetic and copies ran while one was open for 0% -> 0% of each run, Pallas kernels for 38% -> 37%
where the time goes in v22:
time: 87.7 us; the launch traced here: 87.5 us
  Pallas kernels  33.5 us (38%)
  starting transfers between devices  31 us (35%)
  waiting for transfers between devices  22 us (25%)
    pallas_call x24, Pallas kernels, in_vmem(): pl.pallas_call(run, in_specs=[SMEM] * scalars + [HBM] * streamed + [VMEM]...  32.1 us
    ppermute x22, starting transfers between devices, flip(): return lax.ppermute(values, axis, [(s, s ^ bit) for s in range(n)])  31 us
    ppermute x22, waiting for transfers between devices, flip(): return lax.ppermute(values, axis, [(s, s ^ bit) for s in range(n)])  22 us
  transfers between devices with their start and end apart: 22, of which 14 were waited for; matrix products, arithmetic and copies ran while one was open for 0% of the time, Pallas kernels for 37%

profile of v22, /device:TPU:0, one launch (start us, length us, event | category | flops | bytes accessed | tf_op | source)
XLA Modules:
  0.0 87.5 jit_solution(1398843223766629918)
XLA Ops:
  0.6 3.0 %collective-permute-start.7 = (bf16[16,192,256]{2,1,0:T(8,128)(2,1)}, bf16[16,192,256]{2,1,0:T(8,128)(2,1)S(1)}, u32[]{:S(2)}, u32[]{:S(2)}) collective-permute-start(bf16[16,192,256]{2,1,0:T(8,128)(2,1)} %bitcast.10), channel_id=1, source_target_pairs={{0,2},{1,3},{2,0},{3,1},{4,6},{5,7},{6,4},{7,5},{8,10},{9,11},{10,... | collective-permute-start | bytes 4718600 | tf_op jit(solution)/shard_map/ppermute | solution.py:27
  3.7 7.0 %query_key.1 = (bf16[16,6,64,256]{3,2,1,0:T(8,128)(2,1)S(1)}, bf16[16,256,768]{2,1,0:T(8,128)(2,1)S(1)}, s32[1,16]{1,0:T(1,128)S(1)}, f32[4,3,32,256]{3,2,1,0:T(8,128)S(1)}, bf16[4,3,32,256]{3,2,1,0:T(8,128)(2,1)S(1)}) custom-call(s32[2]{0:T(128)S(1)} %pad_add_fusion.refs_0_, s32[1,16]{1,0:T(1,128)} %bitcast.24, bf16[16,256,768]{2,1,0:T(8,128)(2,1)} %refs_2_.1, ...), custom_call_target="tpu_custom_call" | custom-call | flops 704643072 | bytes 16711748 | tf_op jit(solution)/shard_map/query_key/pallas_call | solution.py:56
  10.7 1.6 %collective-permute-start = (bf16[4,3,32,256]{3,2,1,0:T(8,128)(2,1)S(1)}, bf16[4,3,32,256]{3,2,1,0:T(8,128)(2,1)S(1)}, u32[]{:S(2)}, u32[]{:S(2)}) collective-permute-start(bf16[4,3,32,256]{3,2,1,0:T(8,128)(2,1)S(1)} %get-tuple-element.32.refs_4_), channel_id=1, source_target_pairs={{0,8},{4,12},{8,0},{12,4},{16,24},{20,28},{24,16},{28,20},{1,9},{5... | collective-permute-start | bytes 589832 | tf_op jit(solution)/shard_map/ppermute | solution.py:27
  12.5 3.7 %value_dprob.1 = (f32[4,3,32,256]{3,2,1,0:T(8,128)S(1)}, bf16[4,3,32,256]{3,2,1,0:T(8,128)(2,1)S(1)}, bf16[192,384]{1,0:T(8,128)(2,1)S(1)}) custom-call(s32[18]{0:T(128)S(1)} %pad_add_fusion.1.refs_0_, bf16[16,256,768]{2,1,0:T(8,128)(2,1)S(1)} %get-tuple-element.37.refs_1_, bf16[192,768]{1,0:T(8,128)(2,1)S(1)} %bitcast.19, ...), custom_call_target="tpu_custom_call" | custom-call | flops 3221225472 | bytes 8699940 | tf_op jit(solution)/shard_map/value_dprob/pallas_call | solution.py:56
  16.2 1.6 %collective-permute-start.3 = (bf16[4,3,32,256]{3,2,1,0:T(8,128)(2,1)S(1)}, bf16[4,3,32,256]{3,2,1,0:T(8,128)(2,1)S(1)}, u32[]{:S(2)}, u32[]{:S(2)}) collective-permute-start(bf16[4,3,32,256]{3,2,1,0:T(8,128)(2,1)S(1)} %get-tuple-element.39.refs_4_), channel_id=1, source_target_pairs={{0,4},{4,0},{8,12},{12,8},{16,20},{20,16},{24,28},{28,24},{1,5},{5... | collective-permute-start | bytes 589832 | tf_op jit(solution)/shard_map/ppermute | solution.py:27
  17.8 2.7 %collective-permute-start.1 = (bf16[2,3,32,256]{3,2,1,0:T(8,128)(2,1)S(1)}, bf16[2,3,32,256]{3,2,1,0:T(8,128)(2,1)S(1)}, u32[]{:S(2)}, u32[]{:S(2)}) collective-permute-start(bf16[2,3,32,256]{3,2,1,0:T(8,128)(2,1)S(1)} %get-tuple-element.34), channel_id=1, source_target_pairs={{0,16},{4,20},{8,24},{12,28},{16,0},{20,4},{24,8},{28,12},{1,17},{... | collective-permute-start | bytes 294920 | tf_op jit(solution)/shard_map/ppermute | solution.py:27
  20.5 1.9 %collective-permute-done.3.refs_1_ = bf16[4,3,32,256]{3,2,1,0:T(8,128)(2,1)S(1)} collective-permute-done((bf16[4,3,32,256]{3,2,1,0:T(8,128)(2,1)S(1)}, bf16[4,3,32,256]{3,2,1,0:T(8,128)(2,1)S(1)}, u32[]{:S(2)}, u32[]{:S(2)}) %collective-permute-start.3) | collective-permute-done | bytes 196640 | tf_op jit(solution)/shard_map/ppermute | solution.py:27
  25.0 2.1 %collective-permute-done.4.refs_1_ = bf16[2,3,32,256]{3,2,1,0:T(8,128)(2,1)S(1)} collective-permute-done((bf16[2,3,32,256]{3,2,1,0:T(8,128)(2,1)S(1)}, bf16[2,3,32,256]{3,2,1,0:T(8,128)(2,1)S(1)}, u32[]{:S(2)}, u32[]{:S(2)}) %collective-permute-start.4) | collective-permute-done | bytes 98336 | tf_op jit(solution)/shard_map/ppermute | solution.py:27
  27.1 2.8 %collective-permute-start.5 = (bf16[1,3,32,256]{3,2,1,0:T(8,128)(2,1)S(1)}, bf16[1,3,32,256]{3,2,1,0:T(8,128)(2,1)S(1)}, u32[]{:S(2)}, u32[]{:S(2)}) collective-permute-start(bf16[1,3,32,256]{3,2,1,0:T(8,128)(2,1)S(1)} %get-tuple-element.43), channel_id=1, source_target_pairs={{0,16},{4,20},{8,24},{12,28},{16,0},{20,4},{24,8},{28,12},{1,17},{... | collective-permute-start | bytes 147464 | tf_op jit(solution)/shard_map/ppermute | solution.py:27
  31.0 1.6 %collective-permute-done.5.refs_3_ = bf16[1,3,32,256]{3,2,1,0:T(8,128)(2,1)S(1)} collective-permute-done((bf16[1,3,32,256]{3,2,1,0:T(8,128)(2,1)S(1)}, bf16[1,3,32,256]{3,2,1,0:T(8,128)(2,1)S(1)}, u32[]{:S(2)}, u32[]{:S(2)}) %collective-permute-start.5) | collective-permute-done | bytes 49184 | tf_op jit(solution)/shard_map/ppermute | solution.py:27
  34.4 2.4 %collective-permute-start.6 = (bf16[1,3,32,256]{3,2,1,0:T(8,128)(2,1)S(1)}, bf16[1,3,32,256]{3,2,1,0:T(8,128)(2,1)S(1)}, u32[]{:S(2)}, u32[]{:S(2)}) collective-permute-start(bf16[1,3,32,256]{3,2,1,0:T(8,128)(2,1)S(1)} %get-tuple-element.44.refs_0_), channel_id=1, source_target_pairs={{0,16},{4,20},{8,24},{12,28},{16,0},{20,4},{24,8},{28,12},{1,17},{... | collective-permute-start | bytes 147464 | tf_op jit(solution)/shard_map/ppermute | solution.py:27
  37.0 2.4 %collective-permute-start.12 = (bf16[2,3,32,256]{3,2,1,0:T(8,128)(2,1)S(1)}, bf16[2,3,32,256]{3,2,1,0:T(8,128)(2,1)S(1)}, u32[]{:S(2)}, u32[]{:S(2)}) collective-permute-start(bf16[2,3,32,256]{3,2,1,0:T(8,128)(2,1)S(1)} %join.6.refs_0_), channel_id=1, source_target_pairs={{0,16},{4,20},{8,24},{12,28},{16,0},{20,4},{24,8},{28,12},{1,17},{... | collective-permute-start | bytes 294920 | tf_op jit(solution)/shard_map/ppermute | solution.py:27
  41.3 1.9 %collective-permute-done.12.refs_1_ = bf16[2,3,32,256]{3,2,1,0:T(8,128)(2,1)S(1)} collective-permute-done((bf16[2,3,32,256]{3,2,1,0:T(8,128)(2,1)S(1)}, bf16[2,3,32,256]{3,2,1,0:T(8,128)(2,1)S(1)}, u32[]{:S(2)}, u32[]{:S(2)}) %collective-permute-start.12) | collective-permute-done | bytes 98336 | tf_op jit(solution)/shard_map/ppermute | solution.py:27
  49.0 2.4 %collective-permute-done.10.refs_2_ = bf16[4,3,32,256]{3,2,1,0:T(8,128)(2,1)S(1)} collective-permute-done((bf16[4,3,32,256]{3,2,1,0:T(8,128)(2,1)S(1)}, bf16[4,3,32,256]{3,2,1,0:T(8,128)(2,1)S(1)}, u32[]{:S(2)}, u32[]{:S(2)}) %collective-permute-start.10) | collective-permute-done | bytes 196640 | tf_op jit(solution)/shard_map/ppermute | solution.py:27
  53.3 1.9 %own_gradients.1.refs_2_.refs_0_ = bf16[16,9,64,256]{3,2,1,0:T(8,128)(2,1)S(1)} custom-call(s32[18]{0:T(128)S(1)} %pad_add_fusion.1.refs_0_, bf16[2,8,3,32,256]{4,3,2,1,0:T(8,128)(2,1)S(1)} %assemble.1.refs_1_, bf16[16,6,64,256]{3,2,1,0:T(8,128)(2,1)S(1)} %get-tuple-element.46.refs_2_, bf16[16,192,256]{2,1,0:T(8,128)(2,1)S(1)} %bitcast.12), custom_call_target="tpu_custom_call" | custom-call | flops 1207959552 | bytes 10223652 | tf_op jit(solution)/shard_map/own_gradients/pallas_call | solution.py:56
  55.3 4.7 %weight_part.1 = (f32[4,96,576]{2,1,0:T(8,128)S(1)}, bf16[4,96,576]{2,1,0:T(8,128)(2,1)S(1)}) custom-call(s32[18]{0:T(128)S(1)} %pad_add_fusion.1.refs_0_, bf16[16,256,768]{2,1,0:T(8,128)(2,1)S(1)} %get-tuple-element.37.refs_1_, bf16[16,9,64,256]{3,2,1,0:T(8,128)(2,1)S(1)} %own_gradients.1.refs_2_.refs_0_, bf16[192,384]{1,0:T(8,128)(2,1)S(1)} %collective-permute-done.14.refs_3_), custom_call_target="tpu_custom_call" | custom-call | flops 3623878656 | bytes 11894820 | tf_op jit(solution)/shard_map/weight_part/pallas_call | solution.py:56
  60.0 1.6 %collective-permute-start.17 = (bf16[4,96,576]{2,1,0:T(8,128)(2,1)S(1)}, bf16[4,96,576]{2,1,0:T(8,128)(2,1)S(1)}, u32[]{:S(2)}, u32[]{:S(2)}) collective-permute-start(bf16[4,96,576]{2,1,0:T(8,128)(2,1)S(1)} %get-tuple-element.48.refs_2_.refs_4_), channel_id=1, source_target_pairs={{0,4},{4,0},{8,12},{12,8},{16,20},{20,16},{24,28},{28,24},{1,5},{5... | collective-permute-start | bytes 1327112 | tf_op jit(solution)/shard_map/ppermute | solution.py:27
  62.6 2.6 %own_input.1.refs_2_.refs_0_ = bf16[2,16,192,256]{3,2,1,0:T(8,128)(2,1)S(1)} custom-call(bf16[16,9,64,256]{3,2,1,0:T(8,128)(2,1)S(1)} %own_gradients.1.refs_2_.refs_0_, bf16[2,192,576]{2,1,0:T(8,128)(2,1)S(1)} %turn.2.refs_4_.refs_1_, bf16[4,96,576]{2,1,0:T(8,128)(2,1)S(1)} %get-tuple-element.48.refs_2_.refs_4_), custom_call_target="tpu_custom_call" | custom-call | flops 1811939328 | bytes 8306688 | tf_op jit(solution)/shard_map/own_input/pallas_call | solution.py:56
  65.2 3.2 %far_query_key.1.refs_3_.refs_2_ = bf16[16,6,64,256]{3,2,1,0:T(8,128)(2,1)S(1)} custom-call(s32[18]{0:T(128)S(1)} %pad_add_fusion.1.refs_0_, bf16[16,256,768]{2,1,0:T(8,128)(2,1)S(1)} %get-tuple-element.37.refs_1_, bf16[192,768]{1,0:T(8,128)(2,1)S(1)} %collective-permute-done.9.refs_2_.refs_1_, bf16[192,768]{1,0:T(8,128)(2,1)S(1)} %collective-permute-done.16.refs_3_.refs_2_, ...), custom_call_target="tpu_custom_call" | custom-call | flops 2415919104 | bytes 10027044 | tf_op jit(solution)/shard_map/far_query_key/pallas_call | solution.py:56
  68.4 1.8 %collective-permute-done.17.refs_1_ = bf16[4,96,576]{2,1,0:T(8,128)(2,1)S(1)} collective-permute-done((bf16[4,96,576]{2,1,0:T(8,128)(2,1)S(1)}, bf16[4,96,576]{2,1,0:T(8,128)(2,1)S(1)}, u32[]{:S(2)}, u32[]{:S(2)}) %collective-permute-start.17) | collective-permute-done | bytes 442400 | tf_op jit(solution)/shard_map/ppermute | solution.py:27
  70.5 3.0 %collective-permute-start.20 = (bf16[2,96,576]{2,1,0:T(8,128)(2,1)S(1)}, bf16[2,96,576]{2,1,0:T(8,128)(2,1)S(1)}, u32[]{:S(2)}, u32[]{:S(2)}) collective-permute-start(bf16[2,96,576]{2,1,0:T(8,128)(2,1)S(1)} %get-tuple-element.55), channel_id=1, source_target_pairs={{0,16},{4,20},{8,24},{12,28},{16,0},{20,4},{24,8},{28,12},{1,17},{... | collective-permute-start | bytes 663560 | tf_op jit(solution)/shard_map/ppermute | solution.py:27
  74.0 1.9 %far_gradients.1.refs_1_ = bf16[16,9,64,256]{3,2,1,0:T(8,128)(2,1)S(1)} custom-call(s32[18]{0:T(128)S(1)} %pad_add_fusion.1.refs_0_, bf16[2,8,3,32,256]{4,3,2,1,0:T(8,128)(2,1)S(1)} %collective-permute-done.15.refs_1_, bf16[16,6,64,256]{3,2,1,0:T(8,128)(2,1)S(1)} %far_query_key.1.refs_3_.refs_2_, ...), custom_call_target="tpu_custom_call" | custom-call | tf_op jit(solution)/shard_map/far_gradients/pallas_call | solution.py:56
  79.4 2.3 %collective-permute-done.20.refs_1_ = bf16[2,96,576]{2,1,0:T(8,128)(2,1)S(1)} collective-permute-done((bf16[2,96,576]{2,1,0:T(8,128)(2,1)S(1)}, bf16[2,96,576]{2,1,0:T(8,128)(2,1)S(1)}, u32[]{:S(2)}, u32[]{:S(2)}) %collective-permute-start.20) | collective-permute-done | bytes 221216 | tf_op jit(solution)/shard_map/ppermute | solution.py:27
  83.9 2.8 %collective-permute-done.21.refs_2_ = bf16[1,96,576]{2,1,0:T(8,128)(2,1)S(1)} collective-permute-done((bf16[1,96,576]{2,1,0:T(8,128)(2,1)S(1)}, bf16[1,96,576]{2,1,0:T(8,128)(2,1)S(1)}, u32[]{:S(2)}, u32[]{:S(2)}) %collective-permute-start.21) | collective-permute-done | bytes 110624 | tf_op jit(solution)/shard_map/ppermute | solution.py:27
  (55 shorter events, 23.7 us)
Async XLA Ops:
  0.6 39.4 %collective-permute-start.7 = (bf16[16,192,256]{2,1,0:T(8,128)(2,1)}, bf16[16,192,256]{2,1,0:T(8,128)(2,1)S(1)}, u32[]{:S(2)}, u32[]{:S(2)}) collective-permute-start(bf16[16,192,256]{2,1,0:T(8,128)(2,1)} %bitcast.10), channel_id=1, source_target_pairs={{0,2},{1,3},{2,0},{3,1},{4,6},{5,7},{6,4},{7,5},{8,10},{9,11},{10,... | collective-permute-start | bytes 4718600 | tf_op jit(solution)/shard_map/ppermute | solution.py:27
  10.7 7.0 %collective-permute-start = (bf16[4,3,32,256]{3,2,1,0:T(8,128)(2,1)S(1)}, bf16[4,3,32,256]{3,2,1,0:T(8,128)(2,1)S(1)}, u32[]{:S(2)}, u32[]{:S(2)}) collective-permute-start(bf16[4,3,32,256]{3,2,1,0:T(8,128)(2,1)S(1)} %get-tuple-element.32.refs_4_), channel_id=1, source_target_pairs={{0,8},{4,12},{8,0},{12,4},{16,24},{20,28},{24,16},{28,20},{1,9},{5... | collective-permute-start | bytes 589832 | tf_op jit(solution)/shard_map/ppermute | solution.py:27
  12.4 10.5 %copy-start.1 = (bf16[768,192]{0,1:T(8,128)(2,1)S(1)}, bf16[768,192]{0,1:T(8,128)(2,1)}, u32[]{:S(2)}) copy-start(bf16[768,192]{0,1:T(8,128)(2,1)} %param.7) | copy-start | bytes 884740
  12.4 17.5 %copy-start.2 = (bf16[768,192]{0,1:T(8,128)(2,1)S(1)}, bf16[768,192]{0,1:T(8,128)(2,1)}, u32[]{:S(2)}) copy-start(bf16[768,192]{0,1:T(8,128)(2,1)} %param.8) | copy-start | bytes 884740
  16.2 6.1 %collective-permute-start.3 = (bf16[4,3,32,256]{3,2,1,0:T(8,128)(2,1)S(1)}, bf16[4,3,32,256]{3,2,1,0:T(8,128)(2,1)S(1)}, u32[]{:S(2)}, u32[]{:S(2)}) collective-permute-start(bf16[4,3,32,256]{3,2,1,0:T(8,128)(2,1)S(1)} %get-tuple-element.39.refs_4_), channel_id=1, source_target_pairs={{0,4},{4,0},{8,12},{12,8},{16,20},{20,16},{24,28},{28,24},{1,5},{5... | collective-permute-start | bytes 589832 | tf_op jit(solution)/shard_map/ppermute | solution.py:27
  17.8 6.9 %collective-permute-start.1 = (bf16[2,3,32,256]{3,2,1,0:T(8,128)(2,1)S(1)}, bf16[2,3,32,256]{3,2,1,0:T(8,128)(2,1)S(1)}, u32[]{:S(2)}, u32[]{:S(2)}) collective-permute-start(bf16[2,3,32,256]{3,2,1,0:T(8,128)(2,1)S(1)} %get-tuple-element.34), channel_id=1, source_target_pairs={{0,16},{4,20},{8,24},{12,28},{16,0},{20,4},{24,8},{28,12},{1,17},{... | collective-permute-start | bytes 294920 | tf_op jit(solution)/shard_map/ppermute | solution.py:27
  22.4 4.7 %collective-permute-start.4 = (bf16[2,3,32,256]{3,2,1,0:T(8,128)(2,1)S(1)}, bf16[2,3,32,256]{3,2,1,0:T(8,128)(2,1)S(1)}, u32[]{:S(2)}, u32[]{:S(2)}) collective-permute-start(bf16[2,3,32,256]{3,2,1,0:T(8,128)(2,1)S(1)} %get-tuple-element.41), channel_id=1, source_target_pairs={{0,8},{4,12},{8,0},{12,4},{16,24},{20,28},{24,16},{28,20},{1,9},{5... | collective-permute-start | bytes 294920 | tf_op jit(solution)/shard_map/ppermute | solution.py:27
  22.9 21.7 %collective-permute-start.9 = (bf16[192,768]{1,0:T(8,128)(2,1)S(1)}, bf16[192,768]{1,0:T(8,128)(2,1)S(1)}, u32[]{:S(2)}, u32[]{:S(2)}) collective-permute-start(bf16[192,768]{1,0:T(8,128)(2,1)S(1)} %bitcast.14), channel_id=1, source_target_pairs={{0,2},{1,3},{2,0},{3,1},{4,6},{5,7},{6,4},{7,5},{8,10},{9,11},{10,... | collective-permute-start | bytes 884744 | tf_op jit(solution)/shard_map/ppermute | solution.py:27
  24.7 6.3 %collective-permute-start.2 = (bf16[1,3,32,256]{3,2,1,0:T(8,128)(2,1)S(1)}, bf16[1,3,32,256]{3,2,1,0:T(8,128)(2,1)S(1)}, u32[]{:S(2)}, u32[]{:S(2)}) collective-permute-start(bf16[1,3,32,256]{3,2,1,0:T(8,128)(2,1)S(1)} %get-tuple-element.36), channel_id=1, source_target_pairs={{0,4},{4,0},{8,12},{12,8},{16,20},{20,16},{24,28},{28,24},{1,5},{5... | collective-permute-start | bytes 147464 | tf_op jit(solution)/shard_map/ppermute | solution.py:27
  27.1 5.5 %collective-permute-start.5 = (bf16[1,3,32,256]{3,2,1,0:T(8,128)(2,1)S(1)}, bf16[1,3,32,256]{3,2,1,0:T(8,128)(2,1)S(1)}, u32[]{:S(2)}, u32[]{:S(2)}) collective-permute-start(bf16[1,3,32,256]{3,2,1,0:T(8,128)(2,1)S(1)} %get-tuple-element.43), channel_id=1, source_target_pairs={{0,16},{4,20},{8,24},{12,28},{16,0},{20,4},{24,8},{28,12},{1,17},{... | collective-permute-start | bytes 147464 | tf_op jit(solution)/shard_map/ppermute | solution.py:27
  32.8 4.2 %collective-permute-start.11 = (bf16[1,3,32,256]{3,2,1,0:T(8,128)(2,1)S(1)}, bf16[1,3,32,256]{3,2,1,0:T(8,128)(2,1)S(1)}, u32[]{:S(2)}, u32[]{:S(2)}) collective-permute-start(bf16[1,3,32,256]{3,2,1,0:T(8,128)(2,1)S(1)} %get-tuple-element.45.refs_0_), channel_id=1, source_target_pairs={{0,4},{4,0},{8,12},{12,8},{16,20},{20,16},{24,28},{28,24},{1,5},{5... | collective-permute-start | bytes 147464 | tf_op jit(solution)/shard_map/ppermute | solution.py:27
  34.4 5.6 %collective-permute-start.6 = (bf16[1,3,32,256]{3,2,1,0:T(8,128)(2,1)S(1)}, bf16[1,3,32,256]{3,2,1,0:T(8,128)(2,1)S(1)}, u32[]{:S(2)}, u32[]{:S(2)}) collective-permute-start(bf16[1,3,32,256]{3,2,1,0:T(8,128)(2,1)S(1)} %get-tuple-element.44.refs_0_), channel_id=1, source_target_pairs={{0,16},{4,20},{8,24},{12,28},{16,0},{20,4},{24,8},{28,12},{1,17},{... | collective-permute-start | bytes 147464 | tf_op jit(solution)/shard_map/ppermute | solution.py:27
  37.0 6.2 %collective-permute-start.12 = (bf16[2,3,32,256]{3,2,1,0:T(8,128)(2,1)S(1)}, bf16[2,3,32,256]{3,2,1,0:T(8,128)(2,1)S(1)}, u32[]{:S(2)}, u32[]{:S(2)}) collective-permute-start(bf16[2,3,32,256]{3,2,1,0:T(8,128)(2,1)S(1)} %join.6.refs_0_), channel_id=1, source_target_pairs={{0,16},{4,20},{8,24},{12,28},{16,0},{20,4},{24,8},{28,12},{1,17},{... | collective-permute-start | bytes 294920 | tf_op jit(solution)/shard_map/ppermute | solution.py:27
  40.0 5.7 %collective-permute-start.8 = (bf16[2,3,32,256]{3,2,1,0:T(8,128)(2,1)S(1)}, bf16[2,3,32,256]{3,2,1,0:T(8,128)(2,1)S(1)}, u32[]{:S(2)}, u32[]{:S(2)}) collective-permute-start(bf16[2,3,32,256]{3,2,1,0:T(8,128)(2,1)S(1)} %join.4.refs_0_), channel_id=1, source_target_pairs={{0,8},{4,12},{8,0},{12,4},{16,24},{20,28},{24,16},{28,20},{1,9},{5... | collective-permute-start | bytes 294920 | tf_op jit(solution)/shard_map/ppermute | solution.py:27
  43.2 5.8 %collective-permute-start.13 = (bf16[4,3,32,256]{3,2,1,0:T(8,128)(2,1)S(1)}, bf16[4,3,32,256]{3,2,1,0:T(8,128)(2,1)S(1)}, u32[]{:S(2)}, u32[]{:S(2)}) collective-permute-start(bf16[4,3,32,256]{3,2,1,0:T(8,128)(2,1)S(1)} %join.7.refs_3_), channel_id=1, source_target_pairs={{0,8},{4,12},{8,0},{12,4},{16,24},{20,28},{24,16},{28,20},{1,9},{5... | collective-permute-start | bytes 589832 | tf_op jit(solution)/shard_map/ppermute | solution.py:27
  45.7 5.7 %collective-permute-start.10 = (bf16[4,3,32,256]{3,2,1,0:T(8,128)(2,1)S(1)}, bf16[4,3,32,256]{3,2,1,0:T(8,128)(2,1)S(1)}, u32[]{:S(2)}, u32[]{:S(2)}) collective-permute-start(bf16[4,3,32,256]{3,2,1,0:T(8,128)(2,1)S(1)} %join.5.refs_1_), channel_id=1, source_target_pairs={{0,4},{4,0},{8,12},{12,8},{16,20},{20,16},{24,28},{28,24},{1,5},{5... | collective-permute-start | bytes 589832 | tf_op jit(solution)/shard_map/ppermute | solution.py:27
  47.0 8.3 %collective-permute-start.14 = (bf16[192,384]{1,0:T(8,128)(2,1)S(1)}, bf16[192,384]{1,0:T(8,128)(2,1)S(1)}, u32[]{:S(2)}, u32[]{:S(2)}) collective-permute-start(bf16[192,384]{1,0:T(8,128)(2,1)S(1)} %get-tuple-element.47), channel_id=1, source_target_pairs={{0,2},{1,3},{2,0},{3,1},{4,6},{5,7},{6,4},{7,5},{8,10},{9,11},{10,... | collective-permute-start | bytes 442376 | tf_op jit(solution)/shard_map/ppermute | solution.py:27
  48.5 13.1 %collective-permute-start.16 = (bf16[192,768]{1,0:T(8,128)(2,1)S(1)}, bf16[192,768]{1,0:T(8,128)(2,1)S(1)}, u32[]{:S(2)}, u32[]{:S(2)}) collective-permute-start(bf16[192,768]{1,0:T(8,128)(2,1)S(1)} %bitcast.18), channel_id=1, source_target_pairs={{0,2},{1,3},{2,0},{3,1},{4,6},{5,7},{6,4},{7,5},{8,10},{9,11},{10,... | collective-permute-start | bytes 884744 | tf_op jit(solution)/shard_map/ppermute | solution.py:27
  52.1 21.9 %collective-permute-start.15 = (bf16[2,8,3,32,256]{4,3,2,1,0:T(8,128)(2,1)S(1)}, bf16[2,8,3,32,256]{4,3,2,1,0:T(8,128)(2,1)S(1)}, u32[]{:S(2)}, u32[]{:S(2)}) collective-permute-start(bf16[2,8,3,32,256]{4,3,2,1,0:T(8,128)(2,1)S(1)} %assemble.1.refs_1_), channel_id=1, source_target_pairs={{0,2},{1,3},{2,0},{3,1},{4,6},{5,7},{6,4},{7,5},{8,10},{9,11},{10,... | collective-permute-start | bytes 2359304 | tf_op jit(solution)/shard_map/ppermute | solution.py:27
  60.0 10.2 %collective-permute-start.17 = (bf16[4,96,576]{2,1,0:T(8,128)(2,1)S(1)}, bf16[4,96,576]{2,1,0:T(8,128)(2,1)S(1)}, u32[]{:S(2)}, u32[]{:S(2)}) collective-permute-start(bf16[4,96,576]{2,1,0:T(8,128)(2,1)S(1)} %get-tuple-element.48.refs_2_.refs_4_), channel_id=1, source_target_pairs={{0,4},{4,0},{8,12},{12,8},{16,20},{20,16},{24,28},{28,24},{1,5},{5... | collective-permute-start | bytes 1327112 | tf_op jit(solution)/shard_map/ppermute | solution.py:27
  70.5 11.2 %collective-permute-start.20 = (bf16[2,96,576]{2,1,0:T(8,128)(2,1)S(1)}, bf16[2,96,576]{2,1,0:T(8,128)(2,1)S(1)}, u32[]{:S(2)}, u32[]{:S(2)}) collective-permute-start(bf16[2,96,576]{2,1,0:T(8,128)(2,1)S(1)} %get-tuple-element.55), channel_id=1, source_target_pairs={{0,16},{4,20},{8,24},{12,28},{16,0},{20,4},{24,8},{28,12},{1,17},{... | collective-permute-start | bytes 663560 | tf_op jit(solution)/shard_map/ppermute | solution.py:27
  78.8 3.7 %collective-permute-start.18 = (bf16[8,192,256]{2,1,0:T(8,128)(2,1)S(1)}, bf16[8,192,256]{2,1,0:T(8,128)(2,1)S(1)}, u32[]{:S(2)}, u32[]{:S(2)}) collective-permute-start(bf16[8,192,256]{2,1,0:T(8,128)(2,1)S(1)} %get-tuple-element.52), channel_id=1, source_target_pairs={{0,1},{1,0},{2,3},{3,2},{4,5},{5,4},{6,7},{7,6},{8,9},{9,8},{10,11... | collective-permute-start | bytes 2359304 | tf_op jit(solution)/shard_map/ppermute | solution.py:27
  78.9 3.7 %collective-permute-start.19 = (bf16[8,192,256]{2,1,0:T(8,128)(2,1)S(1)}, bf16[8,192,256]{2,1,0:T(8,128)(2,1)S(1)}, u32[]{:S(2)}, u32[]{:S(2)}) collective-permute-start(bf16[8,192,256]{2,1,0:T(8,128)(2,1)S(1)} %get-tuple-element.54), channel_id=1, source_target_pairs={{0,1},{1,0},{2,3},{3,2},{4,5},{5,4},{6,7},{7,6},{8,9},{9,8},{10,11... | collective-permute-start | bytes 2359304 | tf_op jit(solution)/shard_map/ppermute | solution.py:27
  81.7 4.9 %collective-permute-start.21 = (bf16[1,96,576]{2,1,0:T(8,128)(2,1)S(1)}, bf16[1,96,576]{2,1,0:T(8,128)(2,1)S(1)}, u32[]{:S(2)}, u32[]{:S(2)}) collective-permute-start(bf16[1,96,576]{2,1,0:T(8,128)(2,1)S(1)} %get-tuple-element.57), channel_id=1, source_target_pairs={{0,8},{4,12},{8,0},{12,4},{16,24},{20,28},{24,16},{28,20},{1,9},{5... | collective-permute-start | bytes 331784 | tf_op jit(solution)/shard_map/ppermute | solution.py:27
  (2 other events, 17.4 us)

commit v23 on v20

--- a/solution.py
+++ b/solution.py
@@ -435,7 +435,6 @@
         *[a for one in far for a in one],
         after=after,
         limit=14,
-        counted=False,
         flops=4 * len(far) * count * cols * columns * share,
     )
 

time: 85.9 us -> 85.9 us (level)
  transfers between devices with their start and end apart: 22 -> 22, of which waited for: 15 -> 14; matrix products, arithmetic and copies ran while one was open for 0% -> 0% of each run, Pallas kernels for 38% -> 38%
where the time goes in v23:
time: 85.9 us; the launch traced here: 85.7 us
  Pallas kernels  33.5 us (39%)
  starting transfers between devices  28.8 us (34%)
  waiting for transfers between devices  22.4 us (26%)
    pallas_call x24, Pallas kernels, in_vmem(): pl.pallas_call(run, in_specs=[SMEM] * scalars + [HBM] * streamed + [VMEM]...  32.1 us
    ppermute x22, starting transfers between devices, flip(): return lax.ppermute(values, axis, [(s, s ^ bit) for s in range(n)])  28.8 us
    ppermute x22, waiting for transfers between devices, flip(): return lax.ppermute(values, axis, [(s, s ^ bit) for s in range(n)])  22.4 us
  transfers between devices with their start and end apart: 22, of which 14 were waited for; matrix products, arithmetic and copies ran while one was open for 0% of the time, Pallas kernels for 38%

profile of v23, /device:TPU:0, one launch (start us, length us, event | category | flops | bytes accessed | tf_op | source)
XLA Modules:
  0.0 85.7 jit_solution(2980983084585224425)
XLA Ops:
  0.6 3.0 %collective-permute-start.7 = (bf16[16,192,256]{2,1,0:T(8,128)(2,1)}, bf16[16,192,256]{2,1,0:T(8,128)(2,1)S(1)}, u32[]{:S(2)}, u32[]{:S(2)}) collective-permute-start(bf16[16,192,256]{2,1,0:T(8,128)(2,1)} %bitcast.10), channel_id=1, source_target_pairs={{0,2},{1,3},{2,0},{3,1},{4,6},{5,7},{6,4},{7,5},{8,10},{9,11},{10,... | collective-permute-start | bytes 4718600 | tf_op jit(solution)/shard_map/ppermute | solution.py:27
  3.7 7.0 %query_key.1 = (bf16[16,6,64,256]{3,2,1,0:T(8,128)(2,1)S(1)}, bf16[16,256,768]{2,1,0:T(8,128)(2,1)S(1)}, s32[1,16]{1,0:T(1,128)S(1)}, f32[4,3,32,256]{3,2,1,0:T(8,128)S(1)}, bf16[4,3,32,256]{3,2,1,0:T(8,128)(2,1)S(1)}) custom-call(s32[2]{0:T(128)S(1)} %pad_add_fusion.refs_0_, s32[1,16]{1,0:T(1,128)} %bitcast.24, bf16[16,256,768]{2,1,0:T(8,128)(2,1)} %refs_2_.1, ...), custom_call_target="tpu_custom_call" | custom-call | flops 704643072 | bytes 16711748 | tf_op jit(solution)/shard_map/query_key/pallas_call | solution.py:56
  10.7 1.6 %collective-permute-start = (bf16[4,3,32,256]{3,2,1,0:T(8,128)(2,1)S(1)}, bf16[4,3,32,256]{3,2,1,0:T(8,128)(2,1)S(1)}, u32[]{:S(2)}, u32[]{:S(2)}) collective-permute-start(bf16[4,3,32,256]{3,2,1,0:T(8,128)(2,1)S(1)} %get-tuple-element.32.refs_4_), channel_id=1, source_target_pairs={{0,8},{4,12},{8,0},{12,4},{16,24},{20,28},{24,16},{28,20},{1,9},{5... | collective-permute-start | bytes 589832 | tf_op jit(solution)/shard_map/ppermute | solution.py:27
  12.5 3.7 %value_dprob.1 = (f32[4,3,32,256]{3,2,1,0:T(8,128)S(1)}, bf16[4,3,32,256]{3,2,1,0:T(8,128)(2,1)S(1)}, bf16[192,384]{1,0:T(8,128)(2,1)S(1)}) custom-call(s32[18]{0:T(128)S(1)} %pad_add_fusion.1.refs_0_, bf16[16,256,768]{2,1,0:T(8,128)(2,1)S(1)} %get-tuple-element.37.refs_1_, bf16[192,768]{1,0:T(8,128)(2,1)S(1)} %bitcast.19, ...), custom_call_target="tpu_custom_call" | custom-call | flops 3221225472 | bytes 8699940 | tf_op jit(solution)/shard_map/value_dprob/pallas_call | solution.py:56
  16.2 1.6 %collective-permute-start.3 = (bf16[4,3,32,256]{3,2,1,0:T(8,128)(2,1)S(1)}, bf16[4,3,32,256]{3,2,1,0:T(8,128)(2,1)S(1)}, u32[]{:S(2)}, u32[]{:S(2)}) collective-permute-start(bf16[4,3,32,256]{3,2,1,0:T(8,128)(2,1)S(1)} %get-tuple-element.39.refs_4_), channel_id=1, source_target_pairs={{0,4},{4,0},{8,12},{12,8},{16,20},{20,16},{24,28},{28,24},{1,5},{5... | collective-permute-start | bytes 589832 | tf_op jit(solution)/shard_map/ppermute | solution.py:27
  17.8 2.7 %collective-permute-start.1 = (bf16[2,3,32,256]{3,2,1,0:T(8,128)(2,1)S(1)}, bf16[2,3,32,256]{3,2,1,0:T(8,128)(2,1)S(1)}, u32[]{:S(2)}, u32[]{:S(2)}) collective-permute-start(bf16[2,3,32,256]{3,2,1,0:T(8,128)(2,1)S(1)} %get-tuple-element.34), channel_id=1, source_target_pairs={{0,16},{4,20},{8,24},{12,28},{16,0},{20,4},{24,8},{28,12},{1,17},{... | collective-permute-start | bytes 294920 | tf_op jit(solution)/shard_map/ppermute | solution.py:27
  20.5 1.9 %collective-permute-done.3.refs_1_ = bf16[4,3,32,256]{3,2,1,0:T(8,128)(2,1)S(1)} collective-permute-done((bf16[4,3,32,256]{3,2,1,0:T(8,128)(2,1)S(1)}, bf16[4,3,32,256]{3,2,1,0:T(8,128)(2,1)S(1)}, u32[]{:S(2)}, u32[]{:S(2)}) %collective-permute-start.3) | collective-permute-done | bytes 196640 | tf_op jit(solution)/shard_map/ppermute | solution.py:27
  22.9 1.8 %collective-permute-done.1.refs_1_ = bf16[2,3,32,256]{3,2,1,0:T(8,128)(2,1)S(1)} collective-permute-done((bf16[2,3,32,256]{3,2,1,0:T(8,128)(2,1)S(1)}, bf16[2,3,32,256]{3,2,1,0:T(8,128)(2,1)S(1)}, u32[]{:S(2)}, u32[]{:S(2)}) %collective-permute-start.1) | collective-permute-done | bytes 98336 | tf_op jit(solution)/shard_map/ppermute | solution.py:27
  24.8 2.3 %collective-permute-done.4.refs_1_ = bf16[2,3,32,256]{3,2,1,0:T(8,128)(2,1)S(1)} collective-permute-done((bf16[2,3,32,256]{3,2,1,0:T(8,128)(2,1)S(1)}, bf16[2,3,32,256]{3,2,1,0:T(8,128)(2,1)S(1)}, u32[]{:S(2)}, u32[]{:S(2)}) %collective-permute-start.4) | collective-permute-done | bytes 98336 | tf_op jit(solution)/shard_map/ppermute | solution.py:27
  27.1 2.8 %collective-permute-start.5 = (bf16[1,3,32,256]{3,2,1,0:T(8,128)(2,1)S(1)}, bf16[1,3,32,256]{3,2,1,0:T(8,128)(2,1)S(1)}, u32[]{:S(2)}, u32[]{:S(2)}) collective-permute-start(bf16[1,3,32,256]{3,2,1,0:T(8,128)(2,1)S(1)} %get-tuple-element.43), channel_id=1, source_target_pairs={{0,16},{4,20},{8,24},{12,28},{16,0},{20,4},{24,8},{28,12},{1,17},{... | collective-permute-start | bytes 147464 | tf_op jit(solution)/shard_map/ppermute | solution.py:27
  31.0 1.6 %collective-permute-done.5.refs_3_ = bf16[1,3,32,256]{3,2,1,0:T(8,128)(2,1)S(1)} collective-permute-done((bf16[1,3,32,256]{3,2,1,0:T(8,128)(2,1)S(1)}, bf16[1,3,32,256]{3,2,1,0:T(8,128)(2,1)S(1)}, u32[]{:S(2)}, u32[]{:S(2)}) %collective-permute-start.5) | collective-permute-done | bytes 49184 | tf_op jit(solution)/shard_map/ppermute | solution.py:27
  32.8 1.6 %collective-permute-start.10 = (bf16[1,3,32,256]{3,2,1,0:T(8,128)(2,1)S(1)}, bf16[1,3,32,256]{3,2,1,0:T(8,128)(2,1)S(1)}, u32[]{:S(2)}, u32[]{:S(2)}) collective-permute-start(bf16[1,3,32,256]{3,2,1,0:T(8,128)(2,1)S(1)} %get-tuple-element.45.refs_0_), channel_id=1, source_target_pairs={{0,4},{4,0},{8,12},{12,8},{16,20},{20,16},{24,28},{28,24},{1,5},{5... | collective-permute-start | bytes 147464 | tf_op jit(solution)/shard_map/ppermute | solution.py:27
  34.4 2.4 %collective-permute-start.6 = (bf16[1,3,32,256]{3,2,1,0:T(8,128)(2,1)S(1)}, bf16[1,3,32,256]{3,2,1,0:T(8,128)(2,1)S(1)}, u32[]{:S(2)}, u32[]{:S(2)}) collective-permute-start(bf16[1,3,32,256]{3,2,1,0:T(8,128)(2,1)S(1)} %get-tuple-element.44.refs_0_), channel_id=1, source_target_pairs={{0,16},{4,20},{8,24},{12,28},{16,0},{20,4},{24,8},{28,12},{1,17},{... | collective-permute-start | bytes 147464 | tf_op jit(solution)/shard_map/ppermute | solution.py:27
  37.0 2.4 %collective-permute-start.11 = (bf16[2,3,32,256]{3,2,1,0:T(8,128)(2,1)S(1)}, bf16[2,3,32,256]{3,2,1,0:T(8,128)(2,1)S(1)}, u32[]{:S(2)}, u32[]{:S(2)}) collective-permute-start(bf16[2,3,32,256]{3,2,1,0:T(8,128)(2,1)S(1)} %join.6.refs_0_), channel_id=1, source_target_pairs={{0,16},{4,20},{8,24},{12,28},{16,0},{20,4},{24,8},{28,12},{1,17},{... | collective-permute-start | bytes 294920 | tf_op jit(solution)/shard_map/ppermute | solution.py:27
  43.3 2.4 %collective-permute-done.8.refs_1_ = bf16[2,3,32,256]{3,2,1,0:T(8,128)(2,1)S(1)} collective-permute-done((bf16[2,3,32,256]{3,2,1,0:T(8,128)(2,1)S(1)}, bf16[2,3,32,256]{3,2,1,0:T(8,128)(2,1)S(1)}, u32[]{:S(2)}, u32[]{:S(2)}) %collective-permute-start.8) | collective-permute-done | bytes 98336 | tf_op jit(solution)/shard_map/ppermute | solution.py:27
  52.7 1.9 %own_gradients.1.refs_2_.refs_0_ = bf16[16,9,64,256]{3,2,1,0:T(8,128)(2,1)S(1)} custom-call(s32[18]{0:T(128)S(1)} %pad_add_fusion.1.refs_0_, bf16[2,8,3,32,256]{4,3,2,1,0:T(8,128)(2,1)S(1)} %assemble.1.refs_1_, bf16[16,6,64,256]{3,2,1,0:T(8,128)(2,1)S(1)} %get-tuple-element.46.refs_2_, bf16[16,192,256]{2,1,0:T(8,128)(2,1)S(1)} %bitcast.12), custom_call_target="tpu_custom_call" | custom-call | flops 1207959552 | bytes 10223652 | tf_op jit(solution)/shard_map/own_gradients/pallas_call | solution.py:56
  54.7 4.7 %weight_part.1 = (f32[4,96,576]{2,1,0:T(8,128)S(1)}, bf16[4,96,576]{2,1,0:T(8,128)(2,1)S(1)}) custom-call(s32[18]{0:T(128)S(1)} %pad_add_fusion.1.refs_0_, bf16[16,256,768]{2,1,0:T(8,128)(2,1)S(1)} %get-tuple-element.37.refs_1_, bf16[16,9,64,256]{3,2,1,0:T(8,128)(2,1)S(1)} %own_gradients.1.refs_2_.refs_0_, bf16[192,384]{1,0:T(8,128)(2,1)S(1)} %collective-permute-done.14.refs_3_), custom_call_target="tpu_custom_call" | custom-call | flops 3623878656 | bytes 11894820 | tf_op jit(solution)/shard_map/weight_part/pallas_call | solution.py:56
  61.5 2.6 %own_input.1.refs_2_.refs_0_ = bf16[2,16,192,256]{3,2,1,0:T(8,128)(2,1)S(1)} custom-call(bf16[16,9,64,256]{3,2,1,0:T(8,128)(2,1)S(1)} %own_gradients.1.refs_2_.refs_0_, bf16[2,192,576]{2,1,0:T(8,128)(2,1)S(1)} %turn.2.refs_4_.refs_1_, bf16[4,96,576]{2,1,0:T(8,128)(2,1)S(1)} %get-tuple-element.48.refs_2_.refs_4_), custom_call_target="tpu_custom_call" | custom-call | flops 1811939328 | bytes 8306688 | tf_op jit(solution)/shard_map/own_input/pallas_call | solution.py:56
  64.1 3.2 %far_query_key.1.refs_3_.refs_2_ = bf16[16,6,64,256]{3,2,1,0:T(8,128)(2,1)S(1)} custom-call(s32[18]{0:T(128)S(1)} %pad_add_fusion.1.refs_0_, bf16[16,256,768]{2,1,0:T(8,128)(2,1)S(1)} %get-tuple-element.37.refs_1_, bf16[192,768]{1,0:T(8,128)(2,1)S(1)} %collective-permute-done.13.refs_5_.refs_2_.refs_1_, ...), custom_call_target="tpu_custom_call" | custom-call | flops 2415919104 | bytes 10027044 | tf_op jit(solution)/shard_map/far_query_key/pallas_call | solution.py:56
  67.3 1.6 %collective-permute-done.17.refs_1_ = bf16[4,96,576]{2,1,0:T(8,128)(2,1)S(1)} collective-permute-done((bf16[4,96,576]{2,1,0:T(8,128)(2,1)S(1)}, bf16[4,96,576]{2,1,0:T(8,128)(2,1)S(1)}, u32[]{:S(2)}, u32[]{:S(2)}) %collective-permute-start.17) | collective-permute-done | bytes 442400 | tf_op jit(solution)/shard_map/ppermute | solution.py:27
  69.2 1.7 %collective-permute-start.20 = (bf16[2,96,576]{2,1,0:T(8,128)(2,1)S(1)}, bf16[2,96,576]{2,1,0:T(8,128)(2,1)S(1)}, u32[]{:S(2)}, u32[]{:S(2)}) collective-permute-start(bf16[2,96,576]{2,1,0:T(8,128)(2,1)S(1)} %get-tuple-element.55), channel_id=1, source_target_pairs={{0,16},{4,20},{8,24},{12,28},{16,0},{20,4},{24,8},{28,12},{1,17},{... | collective-permute-start | bytes 663560 | tf_op jit(solution)/shard_map/ppermute | solution.py:27
  70.9 3.1 %collective-permute-done.15.refs_1_ = bf16[2,8,3,32,256]{4,3,2,1,0:T(8,128)(2,1)S(1)} collective-permute-done((bf16[2,8,3,32,256]{4,3,2,1,0:T(8,128)(2,1)S(1)}, bf16[2,8,3,32,256]{4,3,2,1,0:T(8,128)(2,1)S(1)}, u32[]{:S(2)}, u32[]{:S(2)}) %collective-permute-start.15) | collective-permute-done | bytes 786464 | tf_op jit(solution)/shard_map/ppermute | solution.py:27
  74.1 1.9 %far_gradients.1.refs_1_ = bf16[16,9,64,256]{3,2,1,0:T(8,128)(2,1)S(1)} custom-call(s32[18]{0:T(128)S(1)} %pad_add_fusion.1.refs_0_, bf16[2,8,3,32,256]{4,3,2,1,0:T(8,128)(2,1)S(1)} %collective-permute-done.15.refs_1_, bf16[16,6,64,256]{3,2,1,0:T(8,128)(2,1)S(1)} %far_query_key.1.refs_3_.refs_2_, ...), custom_call_target="tpu_custom_call" | custom-call | tf_op jit(solution)/shard_map/far_gradients/pallas_call | solution.py:56
  82.7 2.1 %collective-permute-done.21.refs_2_ = bf16[1,96,576]{2,1,0:T(8,128)(2,1)S(1)} collective-permute-done((bf16[1,96,576]{2,1,0:T(8,128)(2,1)S(1)}, bf16[1,96,576]{2,1,0:T(8,128)(2,1)S(1)}, u32[]{:S(2)}, u32[]{:S(2)}) %collective-permute-start.21) | collective-permute-done | bytes 110624 | tf_op jit(solution)/shard_map/ppermute | solution.py:27
  (55 shorter events, 23.2 us)
Async XLA Ops:
  0.6 39.4 %collective-permute-start.7 = (bf16[16,192,256]{2,1,0:T(8,128)(2,1)}, bf16[16,192,256]{2,1,0:T(8,128)(2,1)S(1)}, u32[]{:S(2)}, u32[]{:S(2)}) collective-permute-start(bf16[16,192,256]{2,1,0:T(8,128)(2,1)} %bitcast.10), channel_id=1, source_target_pairs={{0,2},{1,3},{2,0},{3,1},{4,6},{5,7},{6,4},{7,5},{8,10},{9,11},{10,... | collective-permute-start | bytes 4718600 | tf_op jit(solution)/shard_map/ppermute | solution.py:27
  10.7 7.0 %collective-permute-start = (bf16[4,3,32,256]{3,2,1,0:T(8,128)(2,1)S(1)}, bf16[4,3,32,256]{3,2,1,0:T(8,128)(2,1)S(1)}, u32[]{:S(2)}, u32[]{:S(2)}) collective-permute-start(bf16[4,3,32,256]{3,2,1,0:T(8,128)(2,1)S(1)} %get-tuple-element.32.refs_4_), channel_id=1, source_target_pairs={{0,8},{4,12},{8,0},{12,4},{16,24},{20,28},{24,16},{28,20},{1,9},{5... | collective-permute-start | bytes 589832 | tf_op jit(solution)/shard_map/ppermute | solution.py:27
  12.4 17.5 %copy-start.1 = (bf16[768,192]{0,1:T(8,128)(2,1)S(1)}, bf16[768,192]{0,1:T(8,128)(2,1)}, u32[]{:S(2)}) copy-start(bf16[768,192]{0,1:T(8,128)(2,1)} %param.7) | copy-start | bytes 884740
  12.4 17.5 %copy-start.2 = (bf16[768,192]{0,1:T(8,128)(2,1)S(1)}, bf16[768,192]{0,1:T(8,128)(2,1)}, u32[]{:S(2)}) copy-start(bf16[768,192]{0,1:T(8,128)(2,1)} %param.8) | copy-start | bytes 884740
  16.2 6.1 %collective-permute-start.3 = (bf16[4,3,32,256]{3,2,1,0:T(8,128)(2,1)S(1)}, bf16[4,3,32,256]{3,2,1,0:T(8,128)(2,1)S(1)}, u32[]{:S(2)}, u32[]{:S(2)}) collective-permute-start(bf16[4,3,32,256]{3,2,1,0:T(8,128)(2,1)S(1)} %get-tuple-element.39.refs_4_), channel_id=1, source_target_pairs={{0,4},{4,0},{8,12},{12,8},{16,20},{20,16},{24,28},{28,24},{1,5},{5... | collective-permute-start | bytes 589832 | tf_op jit(solution)/shard_map/ppermute | solution.py:27
  17.8 6.9 %collective-permute-start.1 = (bf16[2,3,32,256]{3,2,1,0:T(8,128)(2,1)S(1)}, bf16[2,3,32,256]{3,2,1,0:T(8,128)(2,1)S(1)}, u32[]{:S(2)}, u32[]{:S(2)}) collective-permute-start(bf16[2,3,32,256]{3,2,1,0:T(8,128)(2,1)S(1)} %get-tuple-element.34), channel_id=1, source_target_pairs={{0,16},{4,20},{8,24},{12,28},{16,0},{20,4},{24,8},{28,12},{1,17},{... | collective-permute-start | bytes 294920 | tf_op jit(solution)/shard_map/ppermute | solution.py:27
  22.4 4.7 %collective-permute-start.4 = (bf16[2,3,32,256]{3,2,1,0:T(8,128)(2,1)S(1)}, bf16[2,3,32,256]{3,2,1,0:T(8,128)(2,1)S(1)}, u32[]{:S(2)}, u32[]{:S(2)}) collective-permute-start(bf16[2,3,32,256]{3,2,1,0:T(8,128)(2,1)S(1)} %get-tuple-element.41), channel_id=1, source_target_pairs={{0,8},{4,12},{8,0},{12,4},{16,24},{20,28},{24,16},{28,20},{1,9},{5... | collective-permute-start | bytes 294920 | tf_op jit(solution)/shard_map/ppermute | solution.py:27
  24.7 6.3 %collective-permute-start.2 = (bf16[1,3,32,256]{3,2,1,0:T(8,128)(2,1)S(1)}, bf16[1,3,32,256]{3,2,1,0:T(8,128)(2,1)S(1)}, u32[]{:S(2)}, u32[]{:S(2)}) collective-permute-start(bf16[1,3,32,256]{3,2,1,0:T(8,128)(2,1)S(1)} %get-tuple-element.36), channel_id=1, source_target_pairs={{0,4},{4,0},{8,12},{12,8},{16,20},{20,16},{24,28},{28,24},{1,5},{5... | collective-permute-start | bytes 147464 | tf_op jit(solution)/shard_map/ppermute | solution.py:27
  27.1 5.5 %collective-permute-start.5 = (bf16[1,3,32,256]{3,2,1,0:T(8,128)(2,1)S(1)}, bf16[1,3,32,256]{3,2,1,0:T(8,128)(2,1)S(1)}, u32[]{:S(2)}, u32[]{:S(2)}) collective-permute-start(bf16[1,3,32,256]{3,2,1,0:T(8,128)(2,1)S(1)} %get-tuple-element.43), channel_id=1, source_target_pairs={{0,16},{4,20},{8,24},{12,28},{16,0},{20,4},{24,8},{28,12},{1,17},{... | collective-permute-start | bytes 147464 | tf_op jit(solution)/shard_map/ppermute | solution.py:27
  32.8 4.2 %collective-permute-start.10 = (bf16[1,3,32,256]{3,2,1,0:T(8,128)(2,1)S(1)}, bf16[1,3,32,256]{3,2,1,0:T(8,128)(2,1)S(1)}, u32[]{:S(2)}, u32[]{:S(2)}) collective-permute-start(bf16[1,3,32,256]{3,2,1,0:T(8,128)(2,1)S(1)} %get-tuple-element.45.refs_0_), channel_id=1, source_target_pairs={{0,4},{4,0},{8,12},{12,8},{16,20},{20,16},{24,28},{28,24},{1,5},{5... | collective-permute-start | bytes 147464 | tf_op jit(solution)/shard_map/ppermute | solution.py:27
  34.4 5.6 %collective-permute-start.6 = (bf16[1,3,32,256]{3,2,1,0:T(8,128)(2,1)S(1)}, bf16[1,3,32,256]{3,2,1,0:T(8,128)(2,1)S(1)}, u32[]{:S(2)}, u32[]{:S(2)}) collective-permute-start(bf16[1,3,32,256]{3,2,1,0:T(8,128)(2,1)S(1)} %get-tuple-element.44.refs_0_), channel_id=1, source_target_pairs={{0,16},{4,20},{8,24},{12,28},{16,0},{20,4},{24,8},{28,12},{1,17},{... | collective-permute-start | bytes 147464 | tf_op jit(solution)/shard_map/ppermute | solution.py:27
  37.0 6.2 %collective-permute-start.11 = (bf16[2,3,32,256]{3,2,1,0:T(8,128)(2,1)S(1)}, bf16[2,3,32,256]{3,2,1,0:T(8,128)(2,1)S(1)}, u32[]{:S(2)}, u32[]{:S(2)}) collective-permute-start(bf16[2,3,32,256]{3,2,1,0:T(8,128)(2,1)S(1)} %join.6.refs_0_), channel_id=1, source_target_pairs={{0,16},{4,20},{8,24},{12,28},{16,0},{20,4},{24,8},{28,12},{1,17},{... | collective-permute-start | bytes 294920 | tf_op jit(solution)/shard_map/ppermute | solution.py:27
  40.0 5.7 %collective-permute-start.8 = (bf16[2,3,32,256]{3,2,1,0:T(8,128)(2,1)S(1)}, bf16[2,3,32,256]{3,2,1,0:T(8,128)(2,1)S(1)}, u32[]{:S(2)}, u32[]{:S(2)}) collective-permute-start(bf16[2,3,32,256]{3,2,1,0:T(8,128)(2,1)S(1)} %join.4.refs_0_), channel_id=1, source_target_pairs={{0,8},{4,12},{8,0},{12,4},{16,24},{20,28},{24,16},{28,20},{1,9},{5... | collective-permute-start | bytes 294920 | tf_op jit(solution)/shard_map/ppermute | solution.py:27
  40.1 10.0 %collective-permute-start.13 = (bf16[192,768]{1,0:T(8,128)(2,1)S(1)}, bf16[192,768]{1,0:T(8,128)(2,1)S(1)}, u32[]{:S(2)}, u32[]{:S(2)}) collective-permute-start(bf16[192,768]{1,0:T(8,128)(2,1)S(1)} %bitcast.15), channel_id=1, source_target_pairs={{0,2},{1,3},{2,0},{3,1},{4,6},{5,7},{6,4},{7,5},{8,10},{9,11},{10,... | collective-permute-start | bytes 884744 | tf_op jit(solution)/shard_map/ppermute | solution.py:27
  43.2 6.9 %collective-permute-start.12 = (bf16[4,3,32,256]{3,2,1,0:T(8,128)(2,1)S(1)}, bf16[4,3,32,256]{3,2,1,0:T(8,128)(2,1)S(1)}, u32[]{:S(2)}, u32[]{:S(2)}) collective-permute-start(bf16[4,3,32,256]{3,2,1,0:T(8,128)(2,1)S(1)} %join.7.refs_3_), channel_id=1, source_target_pairs={{0,8},{4,12},{8,0},{12,4},{16,24},{20,28},{24,16},{28,20},{1,9},{5... | collective-permute-start | bytes 589832 | tf_op jit(solution)/shard_map/ppermute | solution.py:27
  45.7 5.7 %collective-permute-start.9 = (bf16[4,3,32,256]{3,2,1,0:T(8,128)(2,1)S(1)}, bf16[4,3,32,256]{3,2,1,0:T(8,128)(2,1)S(1)}, u32[]{:S(2)}, u32[]{:S(2)}) collective-permute-start(bf16[4,3,32,256]{3,2,1,0:T(8,128)(2,1)S(1)} %join.5.refs_1_), channel_id=1, source_target_pairs={{0,4},{4,0},{8,12},{12,8},{16,20},{20,16},{24,28},{28,24},{1,5},{5... | collective-permute-start | bytes 589832 | tf_op jit(solution)/shard_map/ppermute | solution.py:27
  46.9 7.8 %collective-permute-start.14 = (bf16[192,384]{1,0:T(8,128)(2,1)S(1)}, bf16[192,384]{1,0:T(8,128)(2,1)S(1)}, u32[]{:S(2)}, u32[]{:S(2)}) collective-permute-start(bf16[192,384]{1,0:T(8,128)(2,1)S(1)} %get-tuple-element.47), channel_id=1, source_target_pairs={{0,2},{1,3},{2,0},{3,1},{4,6},{5,7},{6,4},{7,5},{8,10},{9,11},{10,... | collective-permute-start | bytes 442376 | tf_op jit(solution)/shard_map/ppermute | solution.py:27
  47.4 13.1 %collective-permute-start.16 = (bf16[192,768]{1,0:T(8,128)(2,1)S(1)}, bf16[192,768]{1,0:T(8,128)(2,1)S(1)}, u32[]{:S(2)}, u32[]{:S(2)}) collective-permute-start(bf16[192,768]{1,0:T(8,128)(2,1)S(1)} %bitcast.18), channel_id=1, source_target_pairs={{0,2},{1,3},{2,0},{3,1},{4,6},{5,7},{6,4},{7,5},{8,10},{9,11},{10,... | collective-permute-start | bytes 884744 | tf_op jit(solution)/shard_map/ppermute | solution.py:27
  52.1 22.0 %collective-permute-start.15 = (bf16[2,8,3,32,256]{4,3,2,1,0:T(8,128)(2,1)S(1)}, bf16[2,8,3,32,256]{4,3,2,1,0:T(8,128)(2,1)S(1)}, u32[]{:S(2)}, u32[]{:S(2)}) collective-permute-start(bf16[2,8,3,32,256]{4,3,2,1,0:T(8,128)(2,1)S(1)} %assemble.1.refs_1_), channel_id=1, source_target_pairs={{0,2},{1,3},{2,0},{3,1},{4,6},{5,7},{6,4},{7,5},{8,10},{9,11},{10,... | collective-permute-start | bytes 2359304 | tf_op jit(solution)/shard_map/ppermute | solution.py:27
  59.4 9.5 %collective-permute-start.17 = (bf16[4,96,576]{2,1,0:T(8,128)(2,1)S(1)}, bf16[4,96,576]{2,1,0:T(8,128)(2,1)S(1)}, u32[]{:S(2)}, u32[]{:S(2)}) collective-permute-start(bf16[4,96,576]{2,1,0:T(8,128)(2,1)S(1)} %get-tuple-element.48.refs_2_.refs_4_), channel_id=1, source_target_pairs={{0,4},{4,0},{8,12},{12,8},{16,20},{20,16},{24,28},{28,24},{1,5},{5... | collective-permute-start | bytes 1327112 | tf_op jit(solution)/shard_map/ppermute | solution.py:27
  69.2 10.3 %collective-permute-start.20 = (bf16[2,96,576]{2,1,0:T(8,128)(2,1)S(1)}, bf16[2,96,576]{2,1,0:T(8,128)(2,1)S(1)}, u32[]{:S(2)}, u32[]{:S(2)}) collective-permute-start(bf16[2,96,576]{2,1,0:T(8,128)(2,1)S(1)} %get-tuple-element.55), channel_id=1, source_target_pairs={{0,16},{4,20},{8,24},{12,28},{16,0},{20,4},{24,8},{28,12},{1,17},{... | collective-permute-start | bytes 663560 | tf_op jit(solution)/shard_map/ppermute | solution.py:27
  77.4 3.3 %collective-permute-start.18 = (bf16[8,192,256]{2,1,0:T(8,128)(2,1)S(1)}, bf16[8,192,256]{2,1,0:T(8,128)(2,1)S(1)}, u32[]{:S(2)}, u32[]{:S(2)}) collective-permute-start(bf16[8,192,256]{2,1,0:T(8,128)(2,1)S(1)} %get-tuple-element.52), channel_id=1, source_target_pairs={{0,1},{1,0},{2,3},{3,2},{4,5},{5,4},{6,7},{7,6},{8,9},{9,8},{10,11... | collective-permute-start | bytes 2359304 | tf_op jit(solution)/shard_map/ppermute | solution.py:27
  78.9 2.5 %collective-permute-start.19 = (bf16[8,192,256]{2,1,0:T(8,128)(2,1)S(1)}, bf16[8,192,256]{2,1,0:T(8,128)(2,1)S(1)}, u32[]{:S(2)}, u32[]{:S(2)}) collective-permute-start(bf16[8,192,256]{2,1,0:T(8,128)(2,1)S(1)} %get-tuple-element.54), channel_id=1, source_target_pairs={{0,1},{1,0},{2,3},{3,2},{4,5},{5,4},{6,7},{7,6},{8,9},{9,8},{10,11... | collective-permute-start | bytes 2359304 | tf_op jit(solution)/shard_map/ppermute | solution.py:27
  79.5 5.3 %collective-permute-start.21 = (bf16[1,96,576]{2,1,0:T(8,128)(2,1)S(1)}, bf16[1,96,576]{2,1,0:T(8,128)(2,1)S(1)}, u32[]{:S(2)}, u32[]{:S(2)}) collective-permute-start(bf16[1,96,576]{2,1,0:T(8,128)(2,1)S(1)} %get-tuple-element.57), channel_id=1, source_target_pairs={{0,8},{4,12},{8,0},{12,4},{16,24},{20,28},{24,16},{28,20},{1,9},{5... | collective-permute-start | bytes 331784 | tf_op jit(solution)/shard_map/ppermute | solution.py:27
  (2 other events, 17.4 us)

commit v24 on v23

--- a/solution.py
+++ b/solution.py
@@ -80,8 +80,8 @@
 
 
 BLOCK = 4
-STEP = 2
-AHEAD = 6
+STEP = 1
+AHEAD = 7
 
 
 def query_key_kernel(bits, me, lengths, sheet, wq, wk, qk, held, seen, *rest):

time: 85.9 us -> 88 us (1.024)
  Pallas kernels: 33.5 us -> 36.8 us
  starting transfers between devices: 28.8 us -> 26.2 us
  waiting for transfers between devices: 22.4 us -> 23.9 us
    pallas_call x24, Pallas kernels: 32.1 us -> 35.5 us  [in_vmem(): pl.pallas_call(run, in_specs=[SMEM] * scalars + [HBM] * streamed + [VMEM]...]
    ppermute x22, starting transfers between devices: 28.8 us -> 26.2 us  [flip(): return lax.ppermute(values, axis, [(s, s ^ bit) for s in range(n)])]
    ppermute x22, waiting for transfers between devices: 22.4 us -> 23.9 us  [flip(): return lax.ppermute(values, axis, [(s, s ^ bit) for s in range(n)])]
  transfers between devices with their start and end apart: 22 -> 22, of which waited for: 14 -> 14; matrix products, arithmetic and copies ran while one was open for 0% -> 0% of each run, Pallas kernels for 38% -> 41%
where the time goes in v24:
time: 88 us; the launch traced here: 87.8 us
  Pallas kernels  36.8 us (42%)
  starting transfers between devices  26.2 us (30%)
  waiting for transfers between devices  23.9 us (27%)
    pallas_call x24, Pallas kernels, in_vmem(): pl.pallas_call(run, in_specs=[SMEM] * scalars + [HBM] * streamed + [VMEM]...  35.5 us
    ppermute x22, starting transfers between devices, flip(): return lax.ppermute(values, axis, [(s, s ^ bit) for s in range(n)])  26.2 us
    ppermute x22, waiting for transfers between devices, flip(): return lax.ppermute(values, axis, [(s, s ^ bit) for s in range(n)])  23.9 us
  transfers between devices with their start and end apart: 22, of which 14 were waited for; matrix products, arithmetic and copies ran while one was open for 0% of the time, Pallas kernels for 41%

profile of v24, /device:TPU:0, one launch (start us, length us, event | category | flops | bytes accessed | tf_op | source)
XLA Modules:
  0.0 87.8 jit_solution(11510889254444801208)
XLA Ops:
  0.6 3.0 %collective-permute-start.7 = (bf16[16,192,256]{2,1,0:T(8,128)(2,1)}, bf16[16,192,256]{2,1,0:T(8,128)(2,1)S(1)}, u32[]{:S(2)}, u32[]{:S(2)}) collective-permute-start(bf16[16,192,256]{2,1,0:T(8,128)(2,1)} %bitcast.10), channel_id=1, source_target_pairs={{0,2},{1,3},{2,0},{3,1},{4,6},{5,7},{6,4},{7,5},{8,10},{9,11},{10,... | collective-permute-start | bytes 4718600 | tf_op jit(solution)/shard_map/ppermute | solution.py:27
  3.7 10.3 %query_key.1 = (bf16[16,6,64,256]{3,2,1,0:T(8,128)(2,1)S(1)}, bf16[16,256,768]{2,1,0:T(8,128)(2,1)S(1)}, s32[1,16]{1,0:T(1,128)S(1)}, f32[4,3,32,256]{3,2,1,0:T(8,128)S(1)}, bf16[4,3,32,256]{3,2,1,0:T(8,128)(2,1)S(1)}) custom-call(s32[2]{0:T(128)S(1)} %pad_add_fusion.refs_0_, s32[1,16]{1,0:T(1,128)} %bitcast.24, bf16[16,256,768]{2,1,0:T(8,128)(2,1)} %refs_2_.1, ...), custom_call_target="tpu_custom_call" | custom-call | flops 704643072 | bytes 16711748 | tf_op jit(solution)/shard_map/query_key/pallas_call | solution.py:56
  14.1 1.6 %collective-permute-start = (bf16[4,3,32,256]{3,2,1,0:T(8,128)(2,1)S(1)}, bf16[4,3,32,256]{3,2,1,0:T(8,128)(2,1)S(1)}, u32[]{:S(2)}, u32[]{:S(2)}) collective-permute-start(bf16[4,3,32,256]{3,2,1,0:T(8,128)(2,1)S(1)} %get-tuple-element.32.refs_4_), channel_id=1, source_target_pairs={{0,8},{4,12},{8,0},{12,4},{16,24},{20,28},{24,16},{28,20},{1,9},{5... | collective-permute-start | bytes 589832 | tf_op jit(solution)/shard_map/ppermute | solution.py:27
  15.8 3.7 %value_dprob.1 = (f32[4,3,32,256]{3,2,1,0:T(8,128)S(1)}, bf16[4,3,32,256]{3,2,1,0:T(8,128)(2,1)S(1)}, bf16[192,384]{1,0:T(8,128)(2,1)S(1)}) custom-call(s32[18]{0:T(128)S(1)} %pad_add_fusion.1.refs_0_, bf16[16,256,768]{2,1,0:T(8,128)(2,1)S(1)} %get-tuple-element.37.refs_1_, bf16[192,768]{1,0:T(8,128)(2,1)S(1)} %bitcast.19, ...), custom_call_target="tpu_custom_call" | custom-call | flops 3221225472 | bytes 8699940 | tf_op jit(solution)/shard_map/value_dprob/pallas_call | solution.py:56
  19.5 1.6 %collective-permute-start.3 = (bf16[4,3,32,256]{3,2,1,0:T(8,128)(2,1)S(1)}, bf16[4,3,32,256]{3,2,1,0:T(8,128)(2,1)S(1)}, u32[]{:S(2)}, u32[]{:S(2)}) collective-permute-start(bf16[4,3,32,256]{3,2,1,0:T(8,128)(2,1)S(1)} %get-tuple-element.39.refs_4_), channel_id=1, source_target_pairs={{0,4},{4,0},{8,12},{12,8},{16,20},{20,16},{24,28},{28,24},{1,5},{5... | collective-permute-start | bytes 589832 | tf_op jit(solution)/shard_map/ppermute | solution.py:27
  21.1 2.7 %collective-permute-start.1 = (bf16[2,3,32,256]{3,2,1,0:T(8,128)(2,1)S(1)}, bf16[2,3,32,256]{3,2,1,0:T(8,128)(2,1)S(1)}, u32[]{:S(2)}, u32[]{:S(2)}) collective-permute-start(bf16[2,3,32,256]{3,2,1,0:T(8,128)(2,1)S(1)} %get-tuple-element.34), channel_id=1, source_target_pairs={{0,16},{4,20},{8,24},{12,28},{16,0},{20,4},{24,8},{28,12},{1,17},{... | collective-permute-start | bytes 294920 | tf_op jit(solution)/shard_map/ppermute | solution.py:27
  23.8 1.9 %collective-permute-done.3.refs_1_ = bf16[4,3,32,256]{3,2,1,0:T(8,128)(2,1)S(1)} collective-permute-done((bf16[4,3,32,256]{3,2,1,0:T(8,128)(2,1)S(1)}, bf16[4,3,32,256]{3,2,1,0:T(8,128)(2,1)S(1)}, u32[]{:S(2)}, u32[]{:S(2)}) %collective-permute-start.3) | collective-permute-done | bytes 196640 | tf_op jit(solution)/shard_map/ppermute | solution.py:27
  26.2 1.8 %collective-permute-done.1.refs_1_ = bf16[2,3,32,256]{3,2,1,0:T(8,128)(2,1)S(1)} collective-permute-done((bf16[2,3,32,256]{3,2,1,0:T(8,128)(2,1)S(1)}, bf16[2,3,32,256]{3,2,1,0:T(8,128)(2,1)S(1)}, u32[]{:S(2)}, u32[]{:S(2)}) %collective-permute-start.1) | collective-permute-done | bytes 98336 | tf_op jit(solution)/shard_map/ppermute | solution.py:27
  28.1 2.3 %collective-permute-done.4.refs_1_ = bf16[2,3,32,256]{3,2,1,0:T(8,128)(2,1)S(1)} collective-permute-done((bf16[2,3,32,256]{3,2,1,0:T(8,128)(2,1)S(1)}, bf16[2,3,32,256]{3,2,1,0:T(8,128)(2,1)S(1)}, u32[]{:S(2)}, u32[]{:S(2)}) %collective-permute-start.4) | collective-permute-done | bytes 98336 | tf_op jit(solution)/shard_map/ppermute | solution.py:27
  30.4 2.8 %collective-permute-start.5 = (bf16[1,3,32,256]{3,2,1,0:T(8,128)(2,1)S(1)}, bf16[1,3,32,256]{3,2,1,0:T(8,128)(2,1)S(1)}, u32[]{:S(2)}, u32[]{:S(2)}) collective-permute-start(bf16[1,3,32,256]{3,2,1,0:T(8,128)(2,1)S(1)} %get-tuple-element.43), channel_id=1, source_target_pairs={{0,16},{4,20},{8,24},{12,28},{16,0},{20,4},{24,8},{28,12},{1,17},{... | collective-permute-start | bytes 147464 | tf_op jit(solution)/shard_map/ppermute | solution.py:27
  34.3 1.6 %collective-permute-done.5.refs_3_ = bf16[1,3,32,256]{3,2,1,0:T(8,128)(2,1)S(1)} collective-permute-done((bf16[1,3,32,256]{3,2,1,0:T(8,128)(2,1)S(1)}, bf16[1,3,32,256]{3,2,1,0:T(8,128)(2,1)S(1)}, u32[]{:S(2)}, u32[]{:S(2)}) %collective-permute-start.5) | collective-permute-done | bytes 49184 | tf_op jit(solution)/shard_map/ppermute | solution.py:27
  36.2 1.6 %collective-permute-start.10 = (bf16[1,3,32,256]{3,2,1,0:T(8,128)(2,1)S(1)}, bf16[1,3,32,256]{3,2,1,0:T(8,128)(2,1)S(1)}, u32[]{:S(2)}, u32[]{:S(2)}) collective-permute-start(bf16[1,3,32,256]{3,2,1,0:T(8,128)(2,1)S(1)} %get-tuple-element.45.refs_0_), channel_id=1, source_target_pairs={{0,4},{4,0},{8,12},{12,8},{16,20},{20,16},{24,28},{28,24},{1,5},{5... | collective-permute-start | bytes 147464 | tf_op jit(solution)/shard_map/ppermute | solution.py:27
  37.7 2.4 %collective-permute-start.6 = (bf16[1,3,32,256]{3,2,1,0:T(8,128)(2,1)S(1)}, bf16[1,3,32,256]{3,2,1,0:T(8,128)(2,1)S(1)}, u32[]{:S(2)}, u32[]{:S(2)}) collective-permute-start(bf16[1,3,32,256]{3,2,1,0:T(8,128)(2,1)S(1)} %get-tuple-element.44.refs_0_), channel_id=1, source_target_pairs={{0,16},{4,20},{8,24},{12,28},{16,0},{20,4},{24,8},{28,12},{1,17},{... | collective-permute-start | bytes 147464 | tf_op jit(solution)/shard_map/ppermute | solution.py:27
  40.3 2.4 %collective-permute-start.11 = (bf16[2,3,32,256]{3,2,1,0:T(8,128)(2,1)S(1)}, bf16[2,3,32,256]{3,2,1,0:T(8,128)(2,1)S(1)}, u32[]{:S(2)}, u32[]{:S(2)}) collective-permute-start(bf16[2,3,32,256]{3,2,1,0:T(8,128)(2,1)S(1)} %join.6.refs_0_), channel_id=1, source_target_pairs={{0,16},{4,20},{8,24},{12,28},{16,0},{20,4},{24,8},{28,12},{1,17},{... | collective-permute-start | bytes 294920 | tf_op jit(solution)/shard_map/ppermute | solution.py:27
  44.0 2.5 %collective-permute-done.11.refs_1_ = bf16[2,3,32,256]{3,2,1,0:T(8,128)(2,1)S(1)} collective-permute-done((bf16[2,3,32,256]{3,2,1,0:T(8,128)(2,1)S(1)}, bf16[2,3,32,256]{3,2,1,0:T(8,128)(2,1)S(1)}, u32[]{:S(2)}, u32[]{:S(2)}) %collective-permute-start.11) | collective-permute-done | bytes 98336 | tf_op jit(solution)/shard_map/ppermute | solution.py:27
  46.6 2.4 %collective-permute-done.8.refs_1_ = bf16[2,3,32,256]{3,2,1,0:T(8,128)(2,1)S(1)} collective-permute-done((bf16[2,3,32,256]{3,2,1,0:T(8,128)(2,1)S(1)}, bf16[2,3,32,256]{3,2,1,0:T(8,128)(2,1)S(1)}, u32[]{:S(2)}, u32[]{:S(2)}) %collective-permute-start.8) | collective-permute-done | bytes 98336 | tf_op jit(solution)/shard_map/ppermute | solution.py:27
  50.2 1.6 %collective-permute-start.16 = (bf16[192,768]{1,0:T(8,128)(2,1)S(1)}, bf16[192,768]{1,0:T(8,128)(2,1)S(1)}, u32[]{:S(2)}, u32[]{:S(2)}) collective-permute-start(bf16[192,768]{1,0:T(8,128)(2,1)S(1)} %bitcast.18), channel_id=1, source_target_pairs={{0,2},{1,3},{2,0},{3,1},{4,6},{5,7},{6,4},{7,5},{8,10},{9,11},{10,... | collective-permute-start | bytes 884744 | tf_op jit(solution)/shard_map/ppermute | solution.py:27
  56.0 1.9 %own_gradients.1.refs_2_.refs_0_ = bf16[16,9,64,256]{3,2,1,0:T(8,128)(2,1)S(1)} custom-call(s32[18]{0:T(128)S(1)} %pad_add_fusion.1.refs_0_, bf16[2,8,3,32,256]{4,3,2,1,0:T(8,128)(2,1)S(1)} %assemble.1.refs_1_, bf16[16,6,64,256]{3,2,1,0:T(8,128)(2,1)S(1)} %get-tuple-element.46.refs_2_, bf16[16,192,256]{2,1,0:T(8,128)(2,1)S(1)} %bitcast.12), custom_call_target="tpu_custom_call" | custom-call | flops 1207959552 | bytes 10223652 | tf_op jit(solution)/shard_map/own_gradients/pallas_call | solution.py:56
  57.9 4.7 %weight_part.1 = (f32[4,96,576]{2,1,0:T(8,128)S(1)}, bf16[4,96,576]{2,1,0:T(8,128)(2,1)S(1)}) custom-call(s32[18]{0:T(128)S(1)} %pad_add_fusion.1.refs_0_, bf16[16,256,768]{2,1,0:T(8,128)(2,1)S(1)} %get-tuple-element.37.refs_1_, bf16[16,9,64,256]{3,2,1,0:T(8,128)(2,1)S(1)} %own_gradients.1.refs_2_.refs_0_, bf16[192,384]{1,0:T(8,128)(2,1)S(1)} %collective-permute-done.14.refs_3_), custom_call_target="tpu_custom_call" | custom-call | flops 3623878656 | bytes 11894820 | tf_op jit(solution)/shard_map/weight_part/pallas_call | solution.py:56
  64.3 2.6 %own_input.1.refs_2_.refs_0_ = bf16[2,16,192,256]{3,2,1,0:T(8,128)(2,1)S(1)} custom-call(bf16[16,9,64,256]{3,2,1,0:T(8,128)(2,1)S(1)} %own_gradients.1.refs_2_.refs_0_, bf16[2,192,576]{2,1,0:T(8,128)(2,1)S(1)} %turn.2.refs_4_.refs_1_, bf16[4,96,576]{2,1,0:T(8,128)(2,1)S(1)} %get-tuple-element.48.refs_2_.refs_4_), custom_call_target="tpu_custom_call" | custom-call | flops 1811939328 | bytes 8306688 | tf_op jit(solution)/shard_map/own_input/pallas_call | solution.py:56
  66.9 3.2 %far_query_key.1.refs_3_.refs_2_ = bf16[16,6,64,256]{3,2,1,0:T(8,128)(2,1)S(1)} custom-call(s32[18]{0:T(128)S(1)} %pad_add_fusion.1.refs_0_, bf16[16,256,768]{2,1,0:T(8,128)(2,1)S(1)} %get-tuple-element.37.refs_1_, bf16[192,768]{1,0:T(8,128)(2,1)S(1)} %collective-permute-done.13.refs_5_.refs_2_.refs_1_, ...), custom_call_target="tpu_custom_call" | custom-call | flops 2415919104 | bytes 10027044 | tf_op jit(solution)/shard_map/far_query_key/pallas_call | solution.py:56
  72.8 3.5 %collective-permute-done.15.refs_1_ = bf16[2,8,3,32,256]{4,3,2,1,0:T(8,128)(2,1)S(1)} collective-permute-done((bf16[2,8,3,32,256]{4,3,2,1,0:T(8,128)(2,1)S(1)}, bf16[2,8,3,32,256]{4,3,2,1,0:T(8,128)(2,1)S(1)}, u32[]{:S(2)}, u32[]{:S(2)}) %collective-permute-start.15) | collective-permute-done | bytes 786464 | tf_op jit(solution)/shard_map/ppermute | solution.py:27
  76.2 1.9 %far_gradients.1.refs_1_ = bf16[16,9,64,256]{3,2,1,0:T(8,128)(2,1)S(1)} custom-call(s32[18]{0:T(128)S(1)} %pad_add_fusion.1.refs_0_, bf16[2,8,3,32,256]{4,3,2,1,0:T(8,128)(2,1)S(1)} %collective-permute-done.15.refs_1_, bf16[16,6,64,256]{3,2,1,0:T(8,128)(2,1)S(1)} %far_query_key.1.refs_3_.refs_2_, ...), custom_call_target="tpu_custom_call" | custom-call | tf_op jit(solution)/shard_map/far_gradients/pallas_call | solution.py:56
  84.9 2.1 %collective-permute-done.21.refs_2_ = bf16[1,96,576]{2,1,0:T(8,128)(2,1)S(1)} collective-permute-done((bf16[1,96,576]{2,1,0:T(8,128)(2,1)S(1)}, bf16[1,96,576]{2,1,0:T(8,128)(2,1)S(1)}, u32[]{:S(2)}, u32[]{:S(2)}) %collective-permute-start.21) | collective-permute-done | bytes 110624 | tf_op jit(solution)/shard_map/ppermute | solution.py:27
  (55 shorter events, 20.9 us)
Async XLA Ops:
  0.6 42.7 %collective-permute-start.7 = (bf16[16,192,256]{2,1,0:T(8,128)(2,1)}, bf16[16,192,256]{2,1,0:T(8,128)(2,1)S(1)}, u32[]{:S(2)}, u32[]{:S(2)}) collective-permute-start(bf16[16,192,256]{2,1,0:T(8,128)(2,1)} %bitcast.10), channel_id=1, source_target_pairs={{0,2},{1,3},{2,0},{3,1},{4,6},{5,7},{6,4},{7,5},{8,10},{9,11},{10,... | collective-permute-start | bytes 4718600 | tf_op jit(solution)/shard_map/ppermute | solution.py:27
  14.1 7.0 %collective-permute-start = (bf16[4,3,32,256]{3,2,1,0:T(8,128)(2,1)S(1)}, bf16[4,3,32,256]{3,2,1,0:T(8,128)(2,1)S(1)}, u32[]{:S(2)}, u32[]{:S(2)}) collective-permute-start(bf16[4,3,32,256]{3,2,1,0:T(8,128)(2,1)S(1)} %get-tuple-element.32.refs_4_), channel_id=1, source_target_pairs={{0,8},{4,12},{8,0},{12,4},{16,24},{20,28},{24,16},{28,20},{1,9},{5... | collective-permute-start | bytes 589832 | tf_op jit(solution)/shard_map/ppermute | solution.py:27
  15.8 17.5 %copy-start.1 = (bf16[768,192]{0,1:T(8,128)(2,1)S(1)}, bf16[768,192]{0,1:T(8,128)(2,1)}, u32[]{:S(2)}) copy-start(bf16[768,192]{0,1:T(8,128)(2,1)} %param.7) | copy-start | bytes 884740
  15.8 17.5 %copy-start.2 = (bf16[768,192]{0,1:T(8,128)(2,1)S(1)}, bf16[768,192]{0,1:T(8,128)(2,1)}, u32[]{:S(2)}) copy-start(bf16[768,192]{0,1:T(8,128)(2,1)} %param.8) | copy-start | bytes 884740
  19.5 6.1 %collective-permute-start.3 = (bf16[4,3,32,256]{3,2,1,0:T(8,128)(2,1)S(1)}, bf16[4,3,32,256]{3,2,1,0:T(8,128)(2,1)S(1)}, u32[]{:S(2)}, u32[]{:S(2)}) collective-permute-start(bf16[4,3,32,256]{3,2,1,0:T(8,128)(2,1)S(1)} %get-tuple-element.39.refs_4_), channel_id=1, source_target_pairs={{0,4},{4,0},{8,12},{12,8},{16,20},{20,16},{24,28},{28,24},{1,5},{5... | collective-permute-start | bytes 589832 | tf_op jit(solution)/shard_map/ppermute | solution.py:27
  21.1 6.9 %collective-permute-start.1 = (bf16[2,3,32,256]{3,2,1,0:T(8,128)(2,1)S(1)}, bf16[2,3,32,256]{3,2,1,0:T(8,128)(2,1)S(1)}, u32[]{:S(2)}, u32[]{:S(2)}) collective-permute-start(bf16[2,3,32,256]{3,2,1,0:T(8,128)(2,1)S(1)} %get-tuple-element.34), channel_id=1, source_target_pairs={{0,16},{4,20},{8,24},{12,28},{16,0},{20,4},{24,8},{28,12},{1,17},{... | collective-permute-start | bytes 294920 | tf_op jit(solution)/shard_map/ppermute | solution.py:27
  25.7 4.7 %collective-permute-start.4 = (bf16[2,3,32,256]{3,2,1,0:T(8,128)(2,1)S(1)}, bf16[2,3,32,256]{3,2,1,0:T(8,128)(2,1)S(1)}, u32[]{:S(2)}, u32[]{:S(2)}) collective-permute-start(bf16[2,3,32,256]{3,2,1,0:T(8,128)(2,1)S(1)} %get-tuple-element.41), channel_id=1, source_target_pairs={{0,8},{4,12},{8,0},{12,4},{16,24},{20,28},{24,16},{28,20},{1,9},{5... | collective-permute-start | bytes 294920 | tf_op jit(solution)/shard_map/ppermute | solution.py:27
  28.0 6.3 %collective-permute-start.2 = (bf16[1,3,32,256]{3,2,1,0:T(8,128)(2,1)S(1)}, bf16[1,3,32,256]{3,2,1,0:T(8,128)(2,1)S(1)}, u32[]{:S(2)}, u32[]{:S(2)}) collective-permute-start(bf16[1,3,32,256]{3,2,1,0:T(8,128)(2,1)S(1)} %get-tuple-element.36), channel_id=1, source_target_pairs={{0,4},{4,0},{8,12},{12,8},{16,20},{20,16},{24,28},{28,24},{1,5},{5... | collective-permute-start | bytes 147464 | tf_op jit(solution)/shard_map/ppermute | solution.py:27
  30.4 5.5 %collective-permute-start.5 = (bf16[1,3,32,256]{3,2,1,0:T(8,128)(2,1)S(1)}, bf16[1,3,32,256]{3,2,1,0:T(8,128)(2,1)S(1)}, u32[]{:S(2)}, u32[]{:S(2)}) collective-permute-start(bf16[1,3,32,256]{3,2,1,0:T(8,128)(2,1)S(1)} %get-tuple-element.43), channel_id=1, source_target_pairs={{0,16},{4,20},{8,24},{12,28},{16,0},{20,4},{24,8},{28,12},{1,17},{... | collective-permute-start | bytes 147464 | tf_op jit(solution)/shard_map/ppermute | solution.py:27
  36.2 4.2 %collective-permute-start.10 = (bf16[1,3,32,256]{3,2,1,0:T(8,128)(2,1)S(1)}, bf16[1,3,32,256]{3,2,1,0:T(8,128)(2,1)S(1)}, u32[]{:S(2)}, u32[]{:S(2)}) collective-permute-start(bf16[1,3,32,256]{3,2,1,0:T(8,128)(2,1)S(1)} %get-tuple-element.45.refs_0_), channel_id=1, source_target_pairs={{0,4},{4,0},{8,12},{12,8},{16,20},{20,16},{24,28},{28,24},{1,5},{5... | collective-permute-start | bytes 147464 | tf_op jit(solution)/shard_map/ppermute | solution.py:27
  37.7 5.6 %collective-permute-start.6 = (bf16[1,3,32,256]{3,2,1,0:T(8,128)(2,1)S(1)}, bf16[1,3,32,256]{3,2,1,0:T(8,128)(2,1)S(1)}, u32[]{:S(2)}, u32[]{:S(2)}) collective-permute-start(bf16[1,3,32,256]{3,2,1,0:T(8,128)(2,1)S(1)} %get-tuple-element.44.refs_0_), channel_id=1, source_target_pairs={{0,16},{4,20},{8,24},{12,28},{16,0},{20,4},{24,8},{28,12},{1,17},{... | collective-permute-start | bytes 147464 | tf_op jit(solution)/shard_map/ppermute | solution.py:27
  40.3 6.2 %collective-permute-start.11 = (bf16[2,3,32,256]{3,2,1,0:T(8,128)(2,1)S(1)}, bf16[2,3,32,256]{3,2,1,0:T(8,128)(2,1)S(1)}, u32[]{:S(2)}, u32[]{:S(2)}) collective-permute-start(bf16[2,3,32,256]{3,2,1,0:T(8,128)(2,1)S(1)} %join.6.refs_0_), channel_id=1, source_target_pairs={{0,16},{4,20},{8,24},{12,28},{16,0},{20,4},{24,8},{28,12},{1,17},{... | collective-permute-start | bytes 294920 | tf_op jit(solution)/shard_map/ppermute | solution.py:27
  43.3 5.7 %collective-permute-start.8 = (bf16[2,3,32,256]{3,2,1,0:T(8,128)(2,1)S(1)}, bf16[2,3,32,256]{3,2,1,0:T(8,128)(2,1)S(1)}, u32[]{:S(2)}, u32[]{:S(2)}) collective-permute-start(bf16[2,3,32,256]{3,2,1,0:T(8,128)(2,1)S(1)} %join.4.refs_0_), channel_id=1, source_target_pairs={{0,8},{4,12},{8,0},{12,4},{16,24},{20,28},{24,16},{28,20},{1,9},{5... | collective-permute-start | bytes 294920 | tf_op jit(solution)/shard_map/ppermute | solution.py:27
  43.4 9.9 %collective-permute-start.13 = (bf16[192,768]{1,0:T(8,128)(2,1)S(1)}, bf16[192,768]{1,0:T(8,128)(2,1)S(1)}, u32[]{:S(2)}, u32[]{:S(2)}) collective-permute-start(bf16[192,768]{1,0:T(8,128)(2,1)S(1)} %bitcast.15), channel_id=1, source_target_pairs={{0,2},{1,3},{2,0},{3,1},{4,6},{5,7},{6,4},{7,5},{8,10},{9,11},{10,... | collective-permute-start | bytes 884744 | tf_op jit(solution)/shard_map/ppermute | solution.py:27
  46.5 6.8 %collective-permute-start.12 = (bf16[4,3,32,256]{3,2,1,0:T(8,128)(2,1)S(1)}, bf16[4,3,32,256]{3,2,1,0:T(8,128)(2,1)S(1)}, u32[]{:S(2)}, u32[]{:S(2)}) collective-permute-start(bf16[4,3,32,256]{3,2,1,0:T(8,128)(2,1)S(1)} %join.7.refs_3_), channel_id=1, source_target_pairs={{0,8},{4,12},{8,0},{12,4},{16,24},{20,28},{24,16},{28,20},{1,9},{5... | collective-permute-start | bytes 589832 | tf_op jit(solution)/shard_map/ppermute | solution.py:27
  49.1 5.7 %collective-permute-start.9 = (bf16[4,3,32,256]{3,2,1,0:T(8,128)(2,1)S(1)}, bf16[4,3,32,256]{3,2,1,0:T(8,128)(2,1)S(1)}, u32[]{:S(2)}, u32[]{:S(2)}) collective-permute-start(bf16[4,3,32,256]{3,2,1,0:T(8,128)(2,1)S(1)} %join.5.refs_1_), channel_id=1, source_target_pairs={{0,4},{4,0},{8,12},{12,8},{16,20},{20,16},{24,28},{28,24},{1,5},{5... | collective-permute-start | bytes 589832 | tf_op jit(solution)/shard_map/ppermute | solution.py:27
  49.8 8.1 %collective-permute-start.14 = (bf16[192,384]{1,0:T(8,128)(2,1)S(1)}, bf16[192,384]{1,0:T(8,128)(2,1)S(1)}, u32[]{:S(2)}, u32[]{:S(2)}) collective-permute-start(bf16[192,384]{1,0:T(8,128)(2,1)S(1)} %get-tuple-element.47), channel_id=1, source_target_pairs={{0,2},{1,3},{2,0},{3,1},{4,6},{5,7},{6,4},{7,5},{8,10},{9,11},{10,... | collective-permute-start | bytes 442376 | tf_op jit(solution)/shard_map/ppermute | solution.py:27
  50.2 13.1 %collective-permute-start.16 = (bf16[192,768]{1,0:T(8,128)(2,1)S(1)}, bf16[192,768]{1,0:T(8,128)(2,1)S(1)}, u32[]{:S(2)}, u32[]{:S(2)}) collective-permute-start(bf16[192,768]{1,0:T(8,128)(2,1)S(1)} %bitcast.18), channel_id=1, source_target_pairs={{0,2},{1,3},{2,0},{3,1},{4,6},{5,7},{6,4},{7,5},{8,10},{9,11},{10,... | collective-permute-start | bytes 884744 | tf_op jit(solution)/shard_map/ppermute | solution.py:27
  55.4 20.8 %collective-permute-start.15 = (bf16[2,8,3,32,256]{4,3,2,1,0:T(8,128)(2,1)S(1)}, bf16[2,8,3,32,256]{4,3,2,1,0:T(8,128)(2,1)S(1)}, u32[]{:S(2)}, u32[]{:S(2)}) collective-permute-start(bf16[2,8,3,32,256]{4,3,2,1,0:T(8,128)(2,1)S(1)} %assemble.1.refs_1_), channel_id=1, source_target_pairs={{0,2},{1,3},{2,0},{3,1},{4,6},{5,7},{6,4},{7,5},{8,10},{9,11},{10,... | collective-permute-start | bytes 2359304 | tf_op jit(solution)/shard_map/ppermute | solution.py:27
  62.7 8.9 %collective-permute-start.17 = (bf16[4,96,576]{2,1,0:T(8,128)(2,1)S(1)}, bf16[4,96,576]{2,1,0:T(8,128)(2,1)S(1)}, u32[]{:S(2)}, u32[]{:S(2)}) collective-permute-start(bf16[4,96,576]{2,1,0:T(8,128)(2,1)S(1)} %get-tuple-element.48.refs_2_.refs_4_), channel_id=1, source_target_pairs={{0,4},{4,0},{8,12},{12,8},{16,20},{20,16},{24,28},{28,24},{1,5},{5... | collective-permute-start | bytes 1327112 | tf_op jit(solution)/shard_map/ppermute | solution.py:27
  71.9 9.8 %collective-permute-start.20 = (bf16[2,96,576]{2,1,0:T(8,128)(2,1)S(1)}, bf16[2,96,576]{2,1,0:T(8,128)(2,1)S(1)}, u32[]{:S(2)}, u32[]{:S(2)}) collective-permute-start(bf16[2,96,576]{2,1,0:T(8,128)(2,1)S(1)} %get-tuple-element.55), channel_id=1, source_target_pairs={{0,16},{4,20},{8,24},{12,28},{16,0},{20,4},{24,8},{28,12},{1,17},{... | collective-permute-start | bytes 663560 | tf_op jit(solution)/shard_map/ppermute | solution.py:27
  79.6 3.4 %collective-permute-start.18 = (bf16[8,192,256]{2,1,0:T(8,128)(2,1)S(1)}, bf16[8,192,256]{2,1,0:T(8,128)(2,1)S(1)}, u32[]{:S(2)}, u32[]{:S(2)}) collective-permute-start(bf16[8,192,256]{2,1,0:T(8,128)(2,1)S(1)} %get-tuple-element.52), channel_id=1, source_target_pairs={{0,1},{1,0},{2,3},{3,2},{4,5},{5,4},{6,7},{7,6},{8,9},{9,8},{10,11... | collective-permute-start | bytes 2359304 | tf_op jit(solution)/shard_map/ppermute | solution.py:27
  81.1 2.5 %collective-permute-start.19 = (bf16[8,192,256]{2,1,0:T(8,128)(2,1)S(1)}, bf16[8,192,256]{2,1,0:T(8,128)(2,1)S(1)}, u32[]{:S(2)}, u32[]{:S(2)}) collective-permute-start(bf16[8,192,256]{2,1,0:T(8,128)(2,1)S(1)} %get-tuple-element.54), channel_id=1, source_target_pairs={{0,1},{1,0},{2,3},{3,2},{4,5},{5,4},{6,7},{7,6},{8,9},{9,8},{10,11... | collective-permute-start | bytes 2359304 | tf_op jit(solution)/shard_map/ppermute | solution.py:27
  81.7 5.3 %collective-permute-start.21 = (bf16[1,96,576]{2,1,0:T(8,128)(2,1)S(1)}, bf16[1,96,576]{2,1,0:T(8,128)(2,1)S(1)}, u32[]{:S(2)}, u32[]{:S(2)}) collective-permute-start(bf16[1,96,576]{2,1,0:T(8,128)(2,1)S(1)} %get-tuple-element.57), channel_id=1, source_target_pairs={{0,8},{4,12},{8,0},{12,4},{16,24},{20,28},{24,16},{28,20},{1,9},{5... | collective-permute-start | bytes 331784 | tf_op jit(solution)/shard_map/ppermute | solution.py:27
  (2 other events, 24.1 us)
